TPU v7x, 32 devices: a whole 2x2x4 slice. The times are simulated.
32 devices in a mesh: row: 8 (over y, x, core), col: 4 (over z).
Axes of the slice: x: 2, y: 2, z: 4, core: 2. Of those that a mesh axis runs over, the one named last changes fastest.
Arguments:
- x_dosage: bfloat16 [16384, 2048], P('row', 'col'), may hold values from 0 to 2
- y_dosage: bfloat16 [2048, 8192], P('row', 'col'), may hold values from 0 to 2
- freq: float32 [2048], replicated, may hold values from 0.05 to 0.5
- weight: float32 [2048], replicated, may hold values from 0.5 to 3.47
- sex_rows: int32 [16384], P('row'), may hold values 0 or 1
- sex_cols: int32 [8192], P('col'), may hold values 0 or 1
Outputs:
- relation: bfloat16 [16384, 8192], P('row', 'col')
- inbreeding: float32 [16384], P('row')
All inputs are finite; a program needn't handle non-finite values. No bound on the sum of `sex_rows` or of `sex_cols` on one device may be relied on, other than what follows from the above.
Results may differ from a plain program's by a relative error of at most 0.0057.
Values may be sent and summed in bfloat16 or wider, within the bound.
No kernel may reach another device: no remote copies, remote signals or barrier semaphores. Data moves between devices by JAX's collectives and lax.ppermute only.
A program may use at most 128 MiB of HBM per device.

v0:
```python
import jax
import jax.numpy as jnp
from jax import lax
from jax.sharding import PartitionSpec as P

STEPS = 4


def broadcast(value, axis, source):
    kept = jnp.where(lax.axis_index(axis) == source, value, 0).astype(value.dtype)
    return lax.psum(kept, axis)


def passed_along(block, axis, distance):
    devices = range(lax.axis_size(axis))
    route = [((i - distance) % len(devices), i) for i in devices]
    return lax.ppermute(block, axis, route)


def standardize(dosage, freq, weight, male):
    value = dosage.astype(jnp.float32)
    female_z = weight * (value - 2.0 * freq) / jnp.sqrt(2.0 * freq * (1.0 - freq))
    male_z = weight * (0.5 * value - freq) / jnp.sqrt(freq * (1.0 - freq))
    return jnp.where(male > 0, male_z, female_z).astype(jnp.bfloat16)


def local(x_dosage, y_dosage, freq, weight, sex_rows, sex_cols):
    group_size = y_dosage.shape[0]
    local_vars = x_dosage.shape[1]
    groups_here = local_vars // group_size
    total_vars = freq.shape[0]
    cycle_size = lax.axis_size("row")
    row_place = lax.axis_index("row")
    col_place = lax.axis_index("col")
    x_freq = lax.dynamic_slice_in_dim(freq, col_place * local_vars, local_vars)
    x_weight = lax.dynamic_slice_in_dim(weight, col_place * local_vars, local_vars)
    zx = standardize(x_dosage, x_freq[None, :], x_weight[None, :], sex_rows[:, None])
    y_freq = lax.dynamic_slice_in_dim(freq, row_place * group_size, group_size)
    y_weight = lax.dynamic_slice_in_dim(weight, row_place * group_size, group_size)
    zy = standardize(y_dosage, y_freq[:, None], y_weight[:, None], sex_cols[None, :])
    squares = jnp.sum(jnp.square(zx.astype(jnp.float32)), axis=1)
    squares = lax.psum(squares, "col")
    inbreeding = squares / jnp.float32(total_vars) - 1.0
    total = jnp.zeros((zx.shape[0], zy.shape[1]), jnp.float32)
    current = zy
    for step in range(STEPS):
        group = (row_place + step) % cycle_size
        owner = group // groups_here
        offset = group % groups_here * group_size
        piece = lax.dynamic_slice_in_dim(zx, offset, group_size, 1)
        received = broadcast(piece, "col", owner)
        if step > 0:
            current = passed_along(current, "row", -1)
        total = total + jnp.dot(received, current, preferred_element_type=jnp.float32)
    relation = (total / jnp.sqrt(jnp.float32(STEPS * group_size))).astype(jnp.bfloat16)
    return (relation, inbreeding)


def solution(mesh):
    return jax.shard_map(
        local,
        mesh=mesh,
        in_specs=(P("row", "col"), P("row", "col"), P(), P(), P("row"), P("col")),
        out_specs=(P("row", "col"), P("row")),
        check_vma=False,
    )
```

profile of v0, /device:TPU:0, one launch (start us, length us, event | category | flops | bytes accessed | tf_op | source)
XLA Modules:
  0.0 227.7 jit_solution(7510458820225558471)
XLA Ops:
  7.2 0.0 all-reduce.3.cloned.1.call-start
  7.4 0.7 broadcast_compare_fusion.1
  8.1 0.8 dynamic_slice.24
  8.9 0.8 fusion.14
  9.6 3.1 %multiply_reduce_fusion = (f32[2048]{0:T(1024)S(1)}, bf16[2048,512]{1,0:T(8,128)(2,1)S(1)}) fusion(f32[512]{0:T(512)S(1)} %get-tuple-element.17, f32[512]{0:T(512)S(1)} %get-tuple-element.16, f32[512]{0:T(512)S(1)} %get-tuple-element.10, f32[512]{0:T(512)S(1)} %get-tuple-element.11, bf16[2048,512]{1,0:T(8,128)(2,1)} %param.6, f32[512]{0:T(512)S(1)} %dynamic_slice.24, ...), kind=kLoop, calls=%fused_computation.10 | loop fusion | flops 13629440 | bytes 4214784 | tf_op jit(solution)/shard_map/reduce_sum | solution.py:41
  12.8 2.5 %dynamic-slice_select_fusion = (bf16[2048,256]{1,0:T(8,128)(2,1)}, bf16[2048,256]{1,0:T(8,128)(2,1)}, bf16[2048,256]{1,0:T(8,128)(2,1)}, bf16[2048,256]{1,0:T(8,128)(2,1)}) fusion(bf16[2048,512]{1,0:T(8,128)(2,1)S(1)} %get-tuple-element.7, s32[]{:T(128)S(6)} %select_n.128, pred[]{:T(512)S(6)} %eq.24, s32[]{:T(128)S(6)} %select_n.122, pred[]{:T(512)S(6)} %eq.23, ...), kind=kLoop, calls=%fused_computation.20 | loop fusion | flops 2097152 | bytes 8388628 | tf_op jit(solution)/shard_map/jit(_where)/select_n | solution.py:10
  15.2 0.0 copy-start.4
  15.3 0.0 copy-start.2
  15.3 0.0 all-reduce.3.cloned.1.call-update
  15.3 0.8 dynamic_slice.27
  16.1 0.8 fusion.16
  16.9 0.0 copy-done.4
  16.9 0.0 copy-done.2
  16.9 0.8 fusion.13
  17.8 3.4 %collective-permute-start = (bf16[256,2048]{1,0:T(8,128)(2,1)S(1)}, bf16[256,2048]{1,0:T(8,128)(2,1)S(1)}, u32[]{:S(2)}, u32[]{:S(2)}) collective-permute-start(bf16[256,2048]{1,0:T(8,128)(2,1)S(1)} %fusion.13), channel_id=1, source_target_pairs={{4,0},{8,4},{12,8},{16,12},{20,16},{24,20},{28,24},{0,28},{5,1},{9... | collective-permute-start | bytes 3145736 | tf_op jit(solution)/shard_map/ppermute | solution.py:17
  21.2 12.3 %collective-permute-done = bf16[256,2048]{1,0:T(8,128)(2,1)S(1)} collective-permute-done((bf16[256,2048]{1,0:T(8,128)(2,1)S(1)}, bf16[256,2048]{1,0:T(8,128)(2,1)S(1)}, u32[]{:S(2)}, u32[]{:S(2)}) %collective-permute-start) | collective-permute-done | bytes 1048608 | tf_op jit(solution)/shard_map/ppermute | solution.py:17
  33.5 3.2 %collective-permute-start.1 = (bf16[256,2048]{1,0:T(8,128)(2,1)S(1)}, bf16[256,2048]{1,0:T(8,128)(2,1)S(1)}, u32[]{:S(2)}, u32[]{:S(2)}) collective-permute-start(bf16[256,2048]{1,0:T(8,128)(2,1)S(1)} %collective-permute-done), channel_id=1, source_target_pairs={{4,0},{8,4},{12,8},{16,12},{20,16},{24,20},{28,24},{0,28},{5,1},{9... | collective-permute-start | bytes 3145736 | tf_op jit(solution)/shard_map/ppermute | solution.py:17
  36.7 12.6 %psum.39 = f32[2048]{0:T(1024)S(1)} all-reduce(f32[2048]{0:T(1024)S(1)} %get-tuple-element.6), channel_id=1, replica_groups=mesh['row'=8,'col'=4] {'col'}, use_global_device_ids=true, to_apply=%region_5.6 | all-reduce | flops 2048 | bytes 16384 | tf_op jit(solution)/shard_map/psum | solution.py:42
  49.3 0.6 multiply_add_fusion
  49.9 0.0 collective-permute-done.1
  49.9 2.3 %collective-permute-start.2 = (bf16[256,2048]{1,0:T(8,128)(2,1)S(1)}, bf16[256,2048]{1,0:T(8,128)(2,1)}, u32[]{:S(2)}, u32[]{:S(2)}) collective-permute-start(bf16[256,2048]{1,0:T(8,128)(2,1)S(1)} %collective-permute-done.1), channel_id=1, source_target_pairs={{4,0},{8,4},{12,8},{16,12},{20,16},{24,20},{28,24},{0,28},{5,1},{9... | collective-permute-start | bytes 3145736 | tf_op jit(solution)/shard_map/ppermute | solution.py:17
  52.2 122.5 %all-reduce.3.cloned.1.call-done = (bf16[2048,256]{1,0:T(8,128)(2,1)}, bf16[2048,256]{1,0:T(8,128)(2,1)}, bf16[2048,256]{1,0:T(8,128)(2,1)}, bf16[2048,256]{1,0:T(8,128)(2,1)}) async-done(((bf16[2048,256]{1,0:T(8,128)(2,1)}, bf16[2048,256]{1,0:T(8,128)(2,1)}, bf16[2048,256]{1,0:T(8,128)(2,1)}, bf16[2048,256]{1,0:T(8,128)(2,1)}), (bf16[2048,256]{1,0:T(8,128)(2,1)}, bf16[2048,256]{1,0:T(8,128)(2,1)}, ...) | async-done | bytes 4194320 | tf_op jit(solution)/shard_map/psum | solution.py:11
  174.7 0.0 copy-start.1
  174.7 9.4 %fusion.19 = f32[2048,2048]{1,0:T(8,128)} fusion(bf16[2048,256]{1,0:T(8,128)(2,1)} %get-tuple-element.3, bf16[256,2048]{1,0:T(8,128)(2,1)S(1)} %fusion.13), kind=kOutput, calls=%fused_computation.37 | convolution fusion | flops 2147483648 | bytes 18874368 | tf_op jit(solution)/shard_map/dot_general | solution.py:54
  184.1 0.0 copy-done.1
  184.1 0.0 copy-start
  184.1 8.1 %fusion.21 = f32[2048,2048]{1,0:T(8,128)} fusion(bf16[2048,256]{1,0:T(8,128)(2,1)S(1)} %copy-done.1, bf16[256,2048]{1,0:T(8,128)(2,1)S(1)} %collective-permute-done.1), kind=kOutput, calls=%fused_computation.39 | convolution fusion | flops 2147483648 | bytes 18874368 | tf_op jit(solution)/shard_map/dot_general | solution.py:54
  192.2 0.0 copy-done
  192.2 0.0 copy-start.3
  192.2 8.1 %fusion.20 = f32[2048,2048]{1,0:T(8,128)} fusion(bf16[2048,256]{1,0:T(8,128)(2,1)S(1)} %copy-done, bf16[256,2048]{1,0:T(8,128)(2,1)S(1)} %collective-permute-done), kind=kOutput, calls=%fused_computation.38 | convolution fusion | flops 2147483648 | bytes 18874368 | tf_op jit(solution)/shard_map/dot_general | solution.py:54
  200.2 0.0 collective-permute-done.2
  200.3 0.0 copy-done.3
  200.3 20.6 %multiply_convert_fusion = bf16[2048,2048]{1,0:T(8,128)(2,1)} fusion(f32[2048,2048]{1,0:T(8,128)} %fusion.21, f32[2048,2048]{1,0:T(8,128)} %fusion.19, f32[2048,2048]{1,0:T(8,128)} %fusion.20, bf16[2048,256]{1,0:T(8,128)(2,1)S(1)} %copy-done.3, bf16[256,2048]{1,0:T(8,128)(2,1)} %collective-permute-done.2), kind=kOutput, calls=%fused_computation | convolution fusion | flops 2168455168 | bytes 60817408 | tf_op jit(solution)/shard_map/dot_general | solution.py:54
  (3 shorter events, 0.0 us)
Async XLA Ops:
  7.2 167.5 %all-reduce.3.cloned.1.call-start = ((), (), s32[]{:S(2)}) async-start(), calls=%async_computation | async-start | bytes 8388608 | tf_op jit(solution)/shard_map/psum | solution.py:11
  15.2 1.7 copy-start.4
  15.3 1.7 copy-start.2
  17.8 15.7 %collective-permute-start = (bf16[256,2048]{1,0:T(8,128)(2,1)S(1)}, bf16[256,2048]{1,0:T(8,128)(2,1)S(1)}, u32[]{:S(2)}, u32[]{:S(2)}) collective-permute-start(bf16[256,2048]{1,0:T(8,128)(2,1)S(1)} %fusion.13), channel_id=1, source_target_pairs={{4,0},{8,4},{12,8},{16,12},{20,16},{24,20},{28,24},{0,28},{5,1},{9... | collective-permute-start | bytes 3145736 | tf_op jit(solution)/shard_map/ppermute | solution.py:17
  33.5 16.4 %collective-permute-start.1 = (bf16[256,2048]{1,0:T(8,128)(2,1)S(1)}, bf16[256,2048]{1,0:T(8,128)(2,1)S(1)}, u32[]{:S(2)}, u32[]{:S(2)}) collective-permute-start(bf16[256,2048]{1,0:T(8,128)(2,1)S(1)} %collective-permute-done), channel_id=1, source_target_pairs={{4,0},{8,4},{12,8},{16,12},{20,16},{24,20},{28,24},{0,28},{5,1},{9... | collective-permute-start | bytes 3145736 | tf_op jit(solution)/shard_map/ppermute | solution.py:17
  49.9 150.3 %collective-permute-start.2 = (bf16[256,2048]{1,0:T(8,128)(2,1)S(1)}, bf16[256,2048]{1,0:T(8,128)(2,1)}, u32[]{:S(2)}, u32[]{:S(2)}) collective-permute-start(bf16[256,2048]{1,0:T(8,128)(2,1)S(1)} %collective-permute-done.1), channel_id=1, source_target_pairs={{4,0},{8,4},{12,8},{16,12},{20,16},{24,20},{28,24},{0,28},{5,1},{9... | collective-permute-start | bytes 3145736 | tf_op jit(solution)/shard_map/ppermute | solution.py:17
  174.7 9.4 %copy-start.1 = (bf16[2048,256]{1,0:T(8,128)(2,1)S(1)}, bf16[2048,256]{1,0:T(8,128)(2,1)}, u32[]{:S(2)}) copy-start(bf16[2048,256]{1,0:T(8,128)(2,1)} %get-tuple-element.2) | copy-start | bytes 3145732
  184.1 8.1 %copy-start = (bf16[2048,256]{1,0:T(8,128)(2,1)S(1)}, bf16[2048,256]{1,0:T(8,128)(2,1)}, u32[]{:S(2)}) copy-start(bf16[2048,256]{1,0:T(8,128)(2,1)} %get-tuple-element.4) | copy-start | bytes 3145732
  192.2 8.1 %copy-start.3 = (bf16[2048,256]{1,0:T(8,128)(2,1)S(1)}, bf16[2048,256]{1,0:T(8,128)(2,1)}, u32[]{:S(2)}) copy-start(bf16[2048,256]{1,0:T(8,128)(2,1)} %get-tuple-element.5) | copy-start | bytes 3145732
Sparse Core Ops, SparseCore 0:
  15.4 159.2 all-reduce.2
where the time goes:
time: 228 us
  waiting for transfers between devices  135 us (59%)
  matrix products  46.2 us (20%)
  between operations  14.3 us (6%)
  blocking collectives  12.6 us (6%)
  other arithmetic  9.29 us (4%)
  starting transfers between devices  8.92 us (4%)
    psum x1, waiting for transfers between devices, broadcast(): return lax.psum(kept, axis)  122 us
    dot_general x4, matrix products, local(): jnp.dot(received, current, preferred_element_type=jnp.float32)  46.2 us
    psum x1, blocking collectives, local(): squares = lax.psum(squares, 'col')  12.6 us
    ppermute x3, waiting for transfers between devices, passed_along(): return lax.ppermute(block, axis, route)  12.3 us
    ppermute x3, starting transfers between devices, passed_along(): return lax.ppermute(block, axis, route)  8.89 us
  transfers between devices with their start and end apart: 4, of which 2 were waited for; matrix products, arithmetic and copies ran while one was open for 13% of the time, Pallas kernels for 0%

commit v1 on v0

v1 whole, which is shorter than its diff:
```python
import functools

import jax
import jax.numpy as jnp
import numpy as np
from jax import lax
from jax.experimental import pallas as pl
from jax.experimental.pallas import tpu as pltpu
from jax.sharding import PartitionSpec as P

STEPS = 4
HALVES = 2
DEPTH = 2
TILES = 4
VMEM_LIMIT = 48 * 2**20


class Lane:
    def __init__(self, rows, cols, groups_here, towards_zero):
        self.cols = cols
        self.place = (lambda c: c) if towards_zero else (lambda c: cols - 1 - c)
        self.chunks = []
        for r in range(rows):
            slots = {}
            todo = []
            for half in range(HALVES):
                for s in range(STEPS):
                    p = self.place((r + s) % rows // groups_here)
                    if p > 0:
                        todo.append((half, p, s))
            todo.sort()
            slot = 1
            while todo:
                ready = [k for k in todo if 1 + DEPTH * (k[1] - 1) <= slot]
                if ready:
                    todo.remove(ready[0])
                    slots[slot] = ready[0]
                slot += 1
            self.chunks.append(slots)
        self.rounds = max([max(slots, default=0) for slots in self.chunks])

    def sent(self, r, c, t):
        p = self.place(c)
        key = self.chunks[r].get(t + DEPTH * (p - 1)) if p > 0 else None
        if key is None or key[1] < p:
            return None
        return key

    def pairs(self, t):
        found = []
        for r in range(len(self.chunks)):
            for c in range(self.cols):
                if self.sent(r, c, t) is not None:
                    p = self.place(c) - 1
                    to = p if self.place(0) == 0 else self.cols - 1 - p
                    found.append((r * self.cols + c, r * self.cols + to))
        return found

    def own(self, r, c, t):
        key = self.sent(r, c, t)
        return key if key is not None and key[1] == self.place(c) else None

    def arrival(self, r, c, half, s):
        p = self.place(c)
        for slot, key in self.chunks[r].items():
            if key[0] == half and key[2] == s and key[1] > p:
                return slot - DEPTH * p
        return None


def relay_kernel(at, table, x, held, out, sem):
    half_rows, width = out.shape

    @pl.when(table[at] == 1)
    def _():
        row = pl.multiple_of(table[at + 1] * half_rows, half_rows)
        col = pl.multiple_of(table[at + 2] * width, width)
        copy = pltpu.make_async_copy(x.at[pl.ds(row, half_rows), pl.ds(col, width)], out, sem)
        copy.start()
        copy.wait()


def relay(at, table, x, held):
    return pl.pallas_call(
        functools.partial(relay_kernel, at),
        out_shape=jax.ShapeDtypeStruct(held.shape, held.dtype),
        grid_spec=pltpu.PrefetchScalarGridSpec(
            num_scalar_prefetch=1,
            grid=(1,),
            in_specs=[pl.BlockSpec(memory_space=pl.ANY)] * 2,
            out_specs=pl.BlockSpec(memory_space=pl.ANY),
            scratch_shapes=[pltpu.SemaphoreType.DMA],
        ),
        input_output_aliases={2: 0},
        name="relay",
    )(table, x, held)


def product_kernel(half, at, candidates, scale, n_buffers, table, *refs):
    x, buffers = refs[0], refs[1 : 1 + n_buffers]
    factor, twice, male, zy = refs[1 + n_buffers : 5 + n_buffers]
    out, raw, sems = refs[-3:]
    half_rows = raw.shape[0]
    width = raw.shape[1] // STEPS
    tile_rows = half_rows // TILES
    i = pl.program_id(0)

    def fetch(source, row, col, s):
        for tile in range(TILES):
            pltpu.make_async_copy(
                source.at[pl.ds(row + tile * tile_rows, tile_rows), pl.ds(col, width)],
                raw.at[pl.ds(tile * tile_rows, tile_rows), pl.ds(s * width, width)],
                sems.at[tile, s],
            ).start()

    @pl.when(i == 0)
    def _():
        for s in range(STEPS):
            place = table[at + s]
            for number in candidates[s]:
                if number >= 0:

                    @pl.when(place == number)
                    def _(number=number, s=s):
                        fetch(buffers[number], 0, 0, s)

                else:

                    @pl.when(place < 0)
                    def _(s=s, place=place):
                        col = pl.multiple_of((-1 - place) * width, width)
                        fetch(x, half * half_rows, col, s)

    rows = pl.ds(pl.multiple_of(i * tile_rows, tile_rows), tile_rows)
    for s in range(STEPS):
        part = raw.at[rows, pl.ds(s * width, width)]
        pltpu.make_async_copy(part, part, sems.at[i, s]).wait()
    value = raw[rows, :].astype(jnp.float32) - twice[...]
    zx = (value * factor[...] * male[...]).astype(jnp.bfloat16)
    total = jnp.dot(zx, zy[...], preferred_element_type=jnp.float32)
    out[...] = (total * scale).astype(out.dtype)


def product(half, at, candidates, table, x, buffers, factor, twice, male, zy, before):
    rows, n = x.shape[0], zy.shape[1]
    half_rows = rows // HALVES
    tile_rows = half_rows // TILES
    depth = zy.shape[0]
    scale = float(1.0 / np.sqrt(np.float32(depth)))
    whole = lambda i, table: (0, 0)
    specs = [pl.BlockSpec(memory_space=pl.ANY)] * (1 + len(buffers)) + [
        pl.BlockSpec((1, depth), whole),
        pl.BlockSpec((1, depth), whole),
        pl.BlockSpec((tile_rows, 1), lambda i, table: (half * TILES + i, 0)),
        pl.BlockSpec((depth, n), whole),
    ]
    args = [table, x, *buffers, factor, twice, male, zy]
    aliases = {}
    if before is not None:
        aliases = {len(args): 0}
        specs.append(pl.BlockSpec(memory_space=pl.ANY))
        args.append(before)
    return pl.pallas_call(
        functools.partial(product_kernel, half, at, candidates, scale, len(buffers)),
        out_shape=jax.ShapeDtypeStruct((rows, n), jnp.bfloat16),
        grid_spec=pltpu.PrefetchScalarGridSpec(
            num_scalar_prefetch=1,
            grid=(TILES,),
            in_specs=specs,
            out_specs=pl.BlockSpec((tile_rows, n), lambda i, table: (half * TILES + i, 0)),
            scratch_shapes=[
                pltpu.VMEM((half_rows, depth), jnp.bfloat16),
                pltpu.SemaphoreType.DMA((TILES, STEPS)),
            ],
        ),
        input_output_aliases=aliases,
        compiler_params=pltpu.CompilerParams(vmem_limit_bytes=VMEM_LIMIT),
        cost_estimate=pl.CostEstimate(
            flops=2 * half_rows * depth * n,
            bytes_accessed=2 * (half_rows * depth + depth * n + half_rows * n),
            transcendentals=0,
        ),
        name="product",
    )(*args)


def col_sum(value, cols):
    if cols & (cols - 1):
        return lax.psum(value, "col")
    bit = 1
    while bit < cols:
        value = value + lax.ppermute(value, "col", [(i, i ^ bit) for i in range(cols)])
        bit *= 2
    return value


def local(rows, cols, x, y, freq, weight, sex_rows, sex_cols):
    group_size = y.shape[0]
    local_vars = x.shape[1]
    groups_here = local_vars // group_size
    half_rows = x.shape[0] // HALVES
    lanes = [Lane(rows, cols, groups_here, towards) for towards in (True, False)]

    numbers = np.zeros((rows * cols, 0), np.int32)

    def add(columns):
        nonlocal numbers
        at = numbers.shape[1]
        numbers = np.concatenate([numbers, np.asarray(columns, np.int32)], axis=1)
        return at

    devices = [(r, c) for r in range(rows) for c in range(cols)]
    own_at = {}
    for d, lane in enumerate(lanes):
        for t in range(1, lane.rounds + 1):
            entry = []
            for r, c in devices:
                key = lane.own(r, c, t)
                entry.append((0, 0, 0) if key is None else (1, key[0], (r + key[2]) % rows % groups_here))
            own_at[d, t] = add(entry)
    used = {}
    place_at = {}
    candidates = {}
    for half in range(HALVES):
        arrivals = {
            (r, c, s, d): lane.arrival(r, c, half, s)
            for r, c in devices
            for s in range(STEPS)
            for d, lane in enumerate(lanes)
        }
        used[half] = sorted({(t, d) for (_, _, _, d), t in arrivals.items() if t is not None})
        entry = []
        for r, c in devices:
            places = []
            for s in range(STEPS):
                place = -1 - (r + s) % rows % groups_here
                for d in range(len(lanes)):
                    if arrivals[r, c, s, d] is not None:
                        place = used[half].index((arrivals[r, c, s, d], d))
                places.append(place)
            entry.append(places)
        place_at[half] = add(entry)
        candidates[half] = [sorted({max(e[s], -1) for e in entry}) for s in range(STEPS)]

    row_place = lax.axis_index("row")
    col_place = lax.axis_index("col")
    table = lax.dynamic_slice(jnp.asarray(numbers), (row_place * cols + col_place, 0), (1, numbers.shape[1]))[0]

    buffers = {}
    for t in range(1, max(lane.rounds for lane in lanes) + 1):
        for d, lane in enumerate(lanes):
            if t > lane.rounds:
                continue
            pairs = lane.pairs(t)
            if not pairs:
                continue
            at = own_at[d, t]
            held = buffers.get((d, t - DEPTH))
            if held is None:
                start = (table[at + 1] * half_rows, table[at + 2] * group_size)
                held = lax.dynamic_slice(x, start, (half_rows, group_size))
            elif numbers[:, at].any():
                held = buffers[d, t - DEPTH] = relay(at, table, x, held)
            buffers[d, t] = lax.ppermute(held, ("row", "col"), pairs)

    back = [(i, (i - 1) % rows) for i in range(rows)]
    window = [y]
    for _ in range(STEPS - 1):
        window.append(lax.ppermute(window[-1], "row", back))

    factor = weight / jnp.sqrt(2.0 * freq * (1.0 - freq))
    span = STEPS * group_size

    def in_window(value):
        twice = jnp.concatenate([value, value])
        return lax.dynamic_slice(twice, (row_place * group_size,), (span,))

    window_factor = in_window(factor)
    window_twice = in_window(2.0 * freq)
    male_scale = np.float32(np.sqrt(0.5))
    male_rows = jnp.where(sex_rows > 0, male_scale, np.float32(1.0))[:, None]
    male_cols = jnp.where(sex_cols > 0, male_scale, np.float32(1.0))[None, :]
    zy = []
    for s, block in enumerate(window):
        part = slice(s * group_size, (s + 1) * group_size)
        value = block.astype(jnp.float32) - window_twice[part, None]
        zy.append((value * window_factor[part, None] * male_cols).astype(jnp.bfloat16))
    zy = jnp.concatenate(zy, axis=0)

    here = lambda value: lax.dynamic_slice(value, (col_place * local_vars,), (local_vars,))[None, :]
    zx = ((x.astype(jnp.float32) - here(2.0 * freq)) * here(factor) * male_rows).astype(jnp.bfloat16)
    squares = col_sum(jnp.sum(jnp.square(zx.astype(jnp.float32)), axis=1), cols)
    inbreeding = squares / jnp.float32(freq.shape[0]) - 1.0

    relation = None
    for half in range(HALVES):
        relation = product(
            half,
            place_at[half],
            candidates[half],
            table,
            x,
            [buffers[d, t] for t, d in used[half]],
            window_factor[None, :],
            window_twice[None, :],
            male_rows,
            zy,
            relation,
        )
    return relation, inbreeding


def solution(mesh):
    rows, cols = mesh.shape["row"], mesh.shape["col"]
    return jax.shard_map(
        functools.partial(local, rows, cols),
        mesh=mesh,
        in_specs=(P("row", "col"), P("row", "col"), P(), P(), P("row"), P("col")),
        out_specs=(P("row", "col"), P("row")),
        check_vma=False,
    )
```

time: 228 us -> 195 us (0.86)
  the two profiles are of different devices: /device:TPU:0 before, /device:TPU:2 now
where the time goes in v1:
time: 195 us; the launch traced here: 194 us
  waiting for transfers between devices  74.8 us (38%)
  starting transfers between devices  67.9 us (35%)
  Pallas kernels  26.2 us (13%)
  local copies, waits for them, and re-layouts  10.2 us (5%)
  other arithmetic  8.69 us (4%)
  between operations  6.38 us (3%)
    ppermute x20, waiting for transfers between devices, local(): buffers[d, t] = lax.ppermute(held, ('row', 'col'), pairs)  74.8 us
    ppermute x3, starting transfers between devices, local(): window.append(lax.ppermute(window[-1], 'row', back))  34.1 us
    pallas_call x2, Pallas kernels, product(): pl.pallas_call(functools.partial(product_kernel, half, at, candidates, sc...  20.8 us
    ppermute x20, starting transfers between devices, local(): buffers[d, t] = lax.ppermute(held, ('row', 'col'), pairs)  19.3 us
    ppermute x2, starting transfers between devices, col_sum(): lax.ppermute(value, 'col', [(i, i ^ bit) for i in range(cols)])  14.4 us
    pallas_call x8, Pallas kernels, relay(): pl.pallas_call(functools.partial(relay_kernel, at), out_shape=jax.ShapeDt...  5.45 us
  transfers between devices with their start and end apart: 25, of which 8 were waited for; matrix products, arithmetic and copies ran while one was open for 8% of the time, Pallas kernels for 8%

profile of v1, /device:TPU:2, one launch (start us, length us, event | category | flops | bytes accessed | tf_op | source)
XLA Modules:
  0.0 194.2 jit_solution(12620407165168184943)
XLA Ops:
  0.7 1.3 constant_dynamic-slice_fusion
  2.0 0.7 fusion.6
  7.8 3.0 %fusion.3 = (bf16[1024,256]{1,0:T(8,128)(2,1)}, bf16[1024,256]{1,0:T(8,128)(2,1)}, bf16[1024,256]{1,0:T(8,128)(2,1)S(1)}, bf16[1024,256]{1,0:T(8,128)(2,1)S(1)}) fusion(bf16[2048,512]{1,0:T(8,128)(2,1)} %refs_0_.3, s32[]{:T(128)S(6)} %select_n.49, s32[]{:T(128)S(6)} %select_n.50, s32[]{:T(128)S(6)} %select_n.47, s32[]{:T(128)S(6)} %select_n.48, ...), kind=kLoop, calls=%fused_computation.20 | loop fusion | bytes 4194336 | tf_op jit(solution)/shard_map/dynamic_slice | solution.py:261
  10.8 0.7 collective-permute-start.4
  11.5 1.3 collective-permute-start.2
  12.8 0.7 collective-permute-start.1
  13.5 1.3 collective-permute-start
  14.9 2.9 %collective-permute-start.21 = (bf16[256,2048]{1,0:T(8,128)(2,1)}, bf16[256,2048]{1,0:T(8,128)(2,1)}, u32[]{:S(2)}, u32[]{:S(2)}) collective-permute-start(bf16[256,2048]{1,0:T(8,128)(2,1)} %collective-permute-done.20), channel_id=1, source_target_pairs={{0,28},{4,0},{8,4},{12,8},{16,12},{20,16},{24,20},{28,24},{1,29},{... | collective-permute-start | bytes 3145736 | tf_op jit(solution)/shard_map/ppermute | solution.py:269
  17.7 0.1 dynamic_slice.34
  17.9 2.5 %multiply_reduce_fusion = f32[2048]{0:T(1024)S(1)} fusion(bf16[2048,512]{1,0:T(8,128)(2,1)} %refs_0_.3, f32[2048]{0:T(1024)S(1)} %compare_select_fusion.1, f32[512]{0:T(512)S(1)} %dynamic_slice.35, f32[512]{0:T(512)S(1)} %dynamic_slice.34), kind=kLoop, calls=%fused_computation.1 | loop fusion | flops 8386560 | bytes 2117632 | tf_op jit(solution)/shard_map/reduce_sum | solution.py:292
  20.4 7.2 %collective-permute-start.23 = (f32[2048]{0:T(1024)S(1)}, f32[2048]{0:T(1024)S(1)}, u32[]{:S(2)}, u32[]{:S(2)}) collective-permute-start(f32[2048]{0:T(1024)S(1)} %multiply_reduce_fusion), channel_id=1, source_target_pairs={{0,1},{1,0},{2,3},{3,2},{4,5},{5,4},{6,7},{7,6},{8,9},{9,8},{10,11... | collective-permute-start | bytes 24584 | tf_op jit(solution)/shard_map/ppermute | solution.py:192
  27.7 0.7 relay.12.refs_2_
  28.3 2.0 %collective-permute-done.2.held = bf16[1024,256]{1,0:T(8,128)(2,1)S(1)} collective-permute-done((bf16[1024,256]{1,0:T(8,128)(2,1)}, bf16[1024,256]{1,0:T(8,128)(2,1)S(1)}, u32[]{:S(2)}, u32[]{:S(2)}) %collective-permute-start.2) | collective-permute-done | bytes 524320 | tf_op jit(solution)/shard_map/ppermute | solution.py:264
  30.4 0.7 collective-permute-start.5
  31.1 0.2 copy-done.14
  31.2 0.7 relay.10.refs_1_
  31.9 1.3 collective-permute-start.3
  33.3 0.7 relay.9.refs_4_.refs_2_
  33.9 7.7 %collective-permute-done.held = bf16[1024,256]{1,0:T(8,128)(2,1)S(1)} collective-permute-done((bf16[1024,256]{1,0:T(8,128)(2,1)S(1)}, bf16[1024,256]{1,0:T(8,128)(2,1)S(1)}, u32[]{:S(2)}, u32[]{:S(2)}) %collective-permute-start) | collective-permute-done | bytes 524320 | tf_op jit(solution)/shard_map/ppermute | solution.py:264
  41.6 0.7 collective-permute-start.7
  42.3 0.1 copy-done
  42.4 0.7 relay.8.refs_3_.refs_1_
  43.1 1.3 collective-permute-start.6
  44.4 7.2 %collective-permute-start.24 = (f32[2048]{0:T(1024)S(1)}, f32[2048]{0:T(1024)S(1)}, u32[]{:S(2)}, u32[]{:S(2)}) collective-permute-start(f32[2048]{0:T(1024)S(1)} %add.57), channel_id=1, source_target_pairs={{0,2},{1,3},{2,0},{3,1},{4,6},{5,7},{6,4},{7,5},{8,10},{9,11},{10,... | collective-permute-start | bytes 24584 | tf_op jit(solution)/shard_map/ppermute | solution.py:192
  51.7 0.7 relay.13.refs_6_.refs_4_
  52.4 0.3 collective-permute-done.3.held
  52.6 0.7 collective-permute-start.9
  53.3 0.1 copy-done.6
  53.4 0.7 relay.11.refs_5_.refs_3_
  54.1 1.3 collective-permute-start.8
  55.4 0.7 relay.15.refs_8_.refs_6_
  56.1 2.2 %collective-permute-done.6.held = bf16[1024,256]{1,0:T(8,128)(2,1)S(1)} collective-permute-done((bf16[1024,256]{1,0:T(8,128)(2,1)}, bf16[1024,256]{1,0:T(8,128)(2,1)S(1)}, u32[]{:S(2)}, u32[]{:S(2)}) %collective-permute-start.6) | collective-permute-done | bytes 524320 | tf_op jit(solution)/shard_map/ppermute | solution.py:264
  58.3 0.7 collective-permute-start.11
  59.0 0.1 copy-done.10
  59.1 0.7 relay.14.refs_7_.refs_5_
  59.8 1.3 collective-permute-start.10
  61.1 31.2 %collective-permute-start.22 = (bf16[256,2048]{1,0:T(8,128)(2,1)}, bf16[256,2048]{1,0:T(8,128)(2,1)}, u32[]{:S(2)}, u32[]{:S(2)}) collective-permute-start(bf16[256,2048]{1,0:T(8,128)(2,1)} %collective-permute-done.21), channel_id=1, source_target_pairs={{0,28},{4,0},{8,4},{12,8},{16,12},{20,16},{24,20},{28,24},{1,29},{... | collective-permute-start | bytes 3145736 | tf_op jit(solution)/shard_map/ppermute | solution.py:269
  92.4 0.1 fusion
  92.4 0.7 collective-permute-start.13
  93.1 10.9 %collective-permute-done.8.refs_9_.refs_7_ = bf16[1024,256]{1,0:T(8,128)(2,1)S(1)} collective-permute-done((bf16[1024,256]{1,0:T(8,128)(2,1)}, bf16[1024,256]{1,0:T(8,128)(2,1)S(1)}, u32[]{:S(2)}, u32[]{:S(2)}) %collective-permute-start.8) | collective-permute-done | bytes 524320 | tf_op jit(solution)/shard_map/ppermute | solution.py:264
  104.0 1.3 collective-permute-start.12
  105.3 1.5 collective-permute-start.15
  106.8 38.3 %collective-permute-done.10.refs_11_.refs_9_ = bf16[1024,256]{1,0:T(8,128)(2,1)S(1)} collective-permute-done((bf16[1024,256]{1,0:T(8,128)(2,1)}, bf16[1024,256]{1,0:T(8,128)(2,1)S(1)}, u32[]{:S(2)}, u32[]{:S(2)}) %collective-permute-start.10) | collective-permute-done | bytes 524320 | tf_op jit(solution)/shard_map/ppermute | solution.py:264
  145.1 1.3 collective-permute-start.14
  146.4 1.4 copy.19.refs_15_.refs_21_
  147.8 0.6 multiply_add_fusion
  148.4 0.7 collective-permute-start.17
  149.1 7.3 %collective-permute-done.12.refs_11_ = bf16[1024,256]{1,0:T(8,128)(2,1)S(1)} collective-permute-done((bf16[1024,256]{1,0:T(8,128)(2,1)S(1)}, bf16[1024,256]{1,0:T(8,128)(2,1)S(1)}, u32[]{:S(2)}, u32[]{:S(2)}) %collective-permute-start.12) | collective-permute-done | bytes 524320 | tf_op jit(solution)/shard_map/ppermute | solution.py:264
  156.4 0.7 collective-permute-start.16
  157.1 0.7 collective-permute-start.19
  157.8 6.2 %collective-permute-done.14.refs_13_ = bf16[1024,256]{1,0:T(8,128)(2,1)} collective-permute-done((bf16[1024,256]{1,0:T(8,128)(2,1)S(1)}, bf16[1024,256]{1,0:T(8,128)(2,1)}, u32[]{:S(2)}, u32[]{:S(2)}) %collective-permute-start.14) | collective-permute-done | bytes 524320 | tf_op jit(solution)/shard_map/ppermute | solution.py:264
  163.9 0.7 collective-permute-start.18
  164.6 3.1 %multiply_convert_fusion.4 = (bf16[256,2048]{1,0:T(8,128)(2,1)S(1)}, bf16[256,2048]{1,0:T(8,128)(2,1)S(1)}, bf16[256,2048]{1,0:T(8,128)(2,1)S(1)}, bf16[256,2048]{1,0:T(8,128)(2,1)S(1)}) fusion(bf16[256,2048]{1,0:T(8,128)(2,1)} %param.8, f32[2048]{0:T(1024)S(1)} %compare_select_fusion, f32[256]{0:T(256)S(1)} %get-tuple-element.18, ...), kind=kLoop, calls=%fused_computation.6 | loop fusion | flops 10485760 | bytes 8404992 | tf_op jit(solution)/shard_map/convert_element_type | solution.py:287
  167.8 2.4 %pad_maximum_fusion.refs_16_.refs_22_ = bf16[1024,2048]{1,0:T(8,128)(2,1)} fusion(bf16[256,2048]{1,0:T(8,128)(2,1)S(1)} %get-tuple-element.11, bf16[256,2048]{1,0:T(8,128)(2,1)S(1)} %get-tuple-element.10, bf16[256,2048]{1,0:T(8,128)(2,1)S(1)} %get-tuple-element.9, bf16[256,2048]{1,0:T(8,128)(2,1)S(1)} %get-tuple-element.8), kind=kLoop, calls=%fused_computation | loop fusion | flops 16777216 | bytes 8388608 | tf_op jit(solution)/shard_map/concatenate | solution.py:288
  170.2 0.3 copy-done.9
  170.5 0.5 copy-done.11
  171.1 0.2 copy-done.15
  171.2 0.2 copy-done.17
  171.4 10.0 %product.2.refs_23_ = bf16[2048,2048]{1,0:T(8,128)(2,1)} custom-call(s32[68]{0:T(128)S(1)} %copy-done.18, bf16[2048,512]{1,0:T(8,128)(2,1)} %refs_0_.3, bf16[1024,256]{1,0:T(8,128)(2,1)S(1)} %copy-done.15, bf16[1024,256]{1,0:T(8,128)(2,1)S(1)} %copy-done.17, bf16[1024,256]{1,0:T(8,128)(2,1)S(1)} %copy-done.1, bf16[1024,256]{1,0:T(8,128)(2,1)S(1)} %copy-done.3, ...), custom_call_target="tpu_custom_call" | custom-call | flops 4294967296 | bytes 10485760 | tf_op jit(solution)/shard_map/product/pallas_call | solution.py:163
  181.4 0.8 copy-done.20
  182.2 0.2 copy-done.21
  182.4 0.2 copy-done.22
  182.6 0.8 copy-done.23
  183.4 10.8 %product.3 = bf16[2048,2048]{1,0:T(8,128)(2,1)} custom-call(s32[68]{0:T(128)S(1)} %copy-done.18, bf16[2048,512]{1,0:T(8,128)(2,1)} %refs_0_.3, bf16[1024,256]{1,0:T(8,128)(2,1)S(1)} %copy-done.1, bf16[1024,256]{1,0:T(8,128)(2,1)S(1)} %copy-done.3, bf16[1024,256]{1,0:T(8,128)(2,1)S(1)} %copy-done.7, ...), custom_call_target="tpu_custom_call", output_to_operand_aliasing={{}: (24, {})} | custom-call | flops 4294967296 | bytes 10485760 | tf_op jit(solution)/shard_map/product/pallas_call | solution.py:163
  (69 shorter events, 0.3 us)
Async XLA Ops:
  0.6 14.2 %collective-permute-start.20 = (bf16[256,2048]{1,0:T(8,128)(2,1)}, bf16[256,2048]{1,0:T(8,128)(2,1)}, u32[]{:S(2)}, u32[]{:S(2)}) collective-permute-start(bf16[256,2048]{1,0:T(8,128)(2,1)} %param.8), channel_id=1, source_target_pairs={{0,28},{4,0},{8,4},{12,8},{16,12},{20,16},{24,20},{28,24},{1,29},{... | collective-permute-start | bytes 3145736 | tf_op jit(solution)/shard_map/ppermute | solution.py:269
  7.8 7.1 %copy-start.26 = (f32[2048]{0:T(1024)S(1)}, f32[2048]{0:T(1024)}, u32[]{:S(2)}) copy-start(f32[2048]{0:T(1024)} %param.9) | copy-start | bytes 24580
  7.8 7.1 %copy-start.27 = (f32[2048]{0:T(1024)S(1)}, f32[2048]{0:T(1024)}, u32[]{:S(2)}) copy-start(f32[2048]{0:T(1024)} %param.10) | copy-start | bytes 24580
  7.8 9.9 %copy-start.24 = (s32[2048]{0:T(1024)S(1)}, s32[2048]{0:T(1024)}, u32[]{:S(2)}) copy-start(s32[2048]{0:T(1024)} %param.11) | copy-start | bytes 24580
  10.8 9.6 %collective-permute-start.4 = (bf16[1024,256]{1,0:T(8,128)(2,1)}, bf16[1024,256]{1,0:T(8,128)(2,1)S(1)}, u32[]{:S(2)}, u32[]{:S(2)}) collective-permute-start(bf16[1024,256]{1,0:T(8,128)(2,1)} %get-tuple-element.2), channel_id=1, source_target_pairs={{0,1},{1,2},{4,5},{5,6},{6,7},{9,10},{10,11},{13,14},{14,15},{18,1... | collective-permute-start | bytes 1572872 | tf_op jit(solution)/shard_map/ppermute | solution.py:264
  11.5 18.9 %collective-permute-start.2 = (bf16[1024,256]{1,0:T(8,128)(2,1)}, bf16[1024,256]{1,0:T(8,128)(2,1)S(1)}, u32[]{:S(2)}, u32[]{:S(2)}) collective-permute-start(bf16[1024,256]{1,0:T(8,128)(2,1)} %get-tuple-element.3), channel_id=1, source_target_pairs={{1,0},{5,4},{6,5},{9,8},{10,9},{13,12},{14,13},{15,14},{18,17},{19... | collective-permute-start | bytes 1572872 | tf_op jit(solution)/shard_map/ppermute | solution.py:264
  12.8 19.1 %collective-permute-start.1 = (bf16[1024,256]{1,0:T(8,128)(2,1)S(1)}, bf16[1024,256]{1,0:T(8,128)(2,1)S(1)}, u32[]{:S(2)}, u32[]{:S(2)}) collective-permute-start(bf16[1024,256]{1,0:T(8,128)(2,1)S(1)} %get-tuple-element.4), channel_id=1, source_target_pairs={{0,1},{1,2},{5,6},{6,7},{9,10},{10,11},{14,15},{18,19},{20,21},{22... | collective-permute-start | bytes 1572872 | tf_op jit(solution)/shard_map/ppermute | solution.py:264
  13.5 28.1 %collective-permute-start = (bf16[1024,256]{1,0:T(8,128)(2,1)S(1)}, bf16[1024,256]{1,0:T(8,128)(2,1)S(1)}, u32[]{:S(2)}, u32[]{:S(2)}) collective-permute-start(bf16[1024,256]{1,0:T(8,128)(2,1)S(1)} %get-tuple-element.5), channel_id=1, source_target_pairs={{1,0},{5,4},{9,8},{10,9},{13,12},{14,13},{18,17},{19,18},{22,21},{... | collective-permute-start | bytes 1572872 | tf_op jit(solution)/shard_map/ppermute | solution.py:264
  14.9 46.3 %collective-permute-start.21 = (bf16[256,2048]{1,0:T(8,128)(2,1)}, bf16[256,2048]{1,0:T(8,128)(2,1)}, u32[]{:S(2)}, u32[]{:S(2)}) collective-permute-start(bf16[256,2048]{1,0:T(8,128)(2,1)} %collective-permute-done.20), channel_id=1, source_target_pairs={{0,28},{4,0},{8,4},{12,8},{16,12},{20,16},{24,20},{28,24},{1,29},{... | collective-permute-start | bytes 3145736 | tf_op jit(solution)/shard_map/ppermute | solution.py:269
  20.4 7.2 %copy-start.16 = (bf16[1024,256]{1,0:T(8,128)(2,1)}, bf16[1024,256]{1,0:T(8,128)(2,1)S(1)}, u32[]{:S(2)}) copy-start(bf16[1024,256]{1,0:T(8,128)(2,1)S(1)} %collective-permute-done.4.held) | copy-start | bytes 1572868
  20.4 22.7 %collective-permute-start.23 = (f32[2048]{0:T(1024)S(1)}, f32[2048]{0:T(1024)S(1)}, u32[]{:S(2)}, u32[]{:S(2)}) collective-permute-start(f32[2048]{0:T(1024)S(1)} %multiply_reduce_fusion), channel_id=1, source_target_pairs={{0,1},{1,0},{2,3},{3,2},{4,5},{5,4},{6,7},{7,6},{8,9},{9,8},{10,11... | collective-permute-start | bytes 24584 | tf_op jit(solution)/shard_map/ppermute | solution.py:192
  30.4 0.9 copy-start.14
  30.4 14.0 %collective-permute-start.5 = (bf16[1024,256]{1,0:T(8,128)(2,1)}, bf16[1024,256]{1,0:T(8,128)(2,1)S(1)}, u32[]{:S(2)}, u32[]{:S(2)}) collective-permute-start(bf16[1024,256]{1,0:T(8,128)(2,1)} %relay.12.refs_2_), channel_id=1, source_target_pairs={{1,2},{2,3},{5,6},{6,7},{10,11},{14,15},{18,19},{21,22},{24,25},{2... | collective-permute-start | bytes 1572872 | tf_op jit(solution)/shard_map/ppermute | solution.py:264
  31.9 1.3 copy-start.2
  31.9 20.7 %collective-permute-start.3 = (bf16[1024,256]{1,0:T(8,128)(2,1)}, bf16[1024,256]{1,0:T(8,128)(2,1)S(1)}, u32[]{:S(2)}, u32[]{:S(2)}) collective-permute-start(bf16[1024,256]{1,0:T(8,128)(2,1)} %relay.10.refs_1_), channel_id=1, source_target_pairs={{1,0},{5,4},{9,8},{13,12},{14,13},{17,16},{18,17},{21,20},{22,21},... | collective-permute-start | bytes 1572872 | tf_op jit(solution)/shard_map/ppermute | solution.py:264
  41.6 0.8 copy-start
  41.6 12.5 %collective-permute-start.7 = (bf16[1024,256]{1,0:T(8,128)(2,1)}, bf16[1024,256]{1,0:T(8,128)(2,1)S(1)}, u32[]{:S(2)}, u32[]{:S(2)}) collective-permute-start(bf16[1024,256]{1,0:T(8,128)(2,1)} %relay.9.refs_4_.refs_2_), channel_id=1, source_target_pairs={{1,2},{2,3},{4,5},{5,6},{6,7},{10,11},{13,14},{14,15},{18,19},{21,... | collective-permute-start | bytes 1572872 | tf_op jit(solution)/shard_map/ppermute | solution.py:264
  43.1 15.2 %collective-permute-start.6 = (bf16[1024,256]{1,0:T(8,128)(2,1)}, bf16[1024,256]{1,0:T(8,128)(2,1)S(1)}, u32[]{:S(2)}, u32[]{:S(2)}) collective-permute-start(bf16[1024,256]{1,0:T(8,128)(2,1)} %relay.8.refs_3_.refs_1_), channel_id=1, source_target_pairs={{1,0},{5,4},{6,5},{9,8},{13,12},{14,13},{15,14},{17,16},{18,17},{2... | collective-permute-start | bytes 1572872 | tf_op jit(solution)/shard_map/ppermute | solution.py:264
  44.4 7.2 %copy-start.4 = (bf16[1024,256]{1,0:T(8,128)(2,1)}, bf16[1024,256]{1,0:T(8,128)(2,1)S(1)}, u32[]{:S(2)}) copy-start(bf16[1024,256]{1,0:T(8,128)(2,1)S(1)} %collective-permute-done.5.held) | copy-start | bytes 1572868
  44.4 15.4 %collective-permute-start.24 = (f32[2048]{0:T(1024)S(1)}, f32[2048]{0:T(1024)S(1)}, u32[]{:S(2)}, u32[]{:S(2)}) collective-permute-start(f32[2048]{0:T(1024)S(1)} %add.57), channel_id=1, source_target_pairs={{0,2},{1,3},{2,0},{3,1},{4,6},{5,7},{6,4},{7,5},{8,10},{9,11},{10,... | collective-permute-start | bytes 24584 | tf_op jit(solution)/shard_map/ppermute | solution.py:192
  52.6 0.8 copy-start.6
  52.6 39.8 %collective-permute-start.9 = (bf16[1024,256]{1,0:T(8,128)(2,1)}, bf16[1024,256]{1,0:T(8,128)(2,1)S(1)}, u32[]{:S(2)}, u32[]{:S(2)}) collective-permute-start(bf16[1024,256]{1,0:T(8,128)(2,1)} %relay.13.refs_6_.refs_4_), channel_id=1, source_target_pairs={{0,1},{1,2},{2,3},{5,6},{6,7},{9,10},{10,11},{14,15},{22,23},{25,2... | collective-permute-start | bytes 1572872 | tf_op jit(solution)/shard_map/ppermute | solution.py:264
  54.1 1.3 copy-start.8
  54.1 49.9 %collective-permute-start.8 = (bf16[1024,256]{1,0:T(8,128)(2,1)}, bf16[1024,256]{1,0:T(8,128)(2,1)S(1)}, u32[]{:S(2)}, u32[]{:S(2)}) collective-permute-start(bf16[1024,256]{1,0:T(8,128)(2,1)} %relay.11.refs_5_.refs_3_), channel_id=1, source_target_pairs={{5,4},{9,8},{10,9},{13,12},{14,13},{17,16},{18,17},{19,18},{21,20}... | collective-permute-start | bytes 1572872 | tf_op jit(solution)/shard_map/ppermute | solution.py:264
  56.1 91.7 %copy-start.25 = (s32[2048]{0:T(1024)S(1)}, s32[2048]{0:T(1024)}, u32[]{:S(2)}) copy-start(s32[2048]{0:T(1024)} %param.12) | copy-start | bytes 24580
  58.3 0.8 copy-start.10
  58.3 47.0 %collective-permute-start.11 = (bf16[1024,256]{1,0:T(8,128)(2,1)}, bf16[1024,256]{1,0:T(8,128)(2,1)S(1)}, u32[]{:S(2)}, u32[]{:S(2)}) collective-permute-start(bf16[1024,256]{1,0:T(8,128)(2,1)} %relay.15.refs_8_.refs_6_), channel_id=1, source_target_pairs={{0,1},{1,2},{2,3},{5,6},{6,7},{9,10},{10,11},{14,15},{22,23},{25,2... | collective-permute-start | bytes 1572872 | tf_op jit(solution)/shard_map/ppermute | solution.py:264
  59.8 85.3 %collective-permute-start.10 = (bf16[1024,256]{1,0:T(8,128)(2,1)}, bf16[1024,256]{1,0:T(8,128)(2,1)S(1)}, u32[]{:S(2)}, u32[]{:S(2)}) collective-permute-start(bf16[1024,256]{1,0:T(8,128)(2,1)} %relay.14.refs_7_.refs_5_), channel_id=1, source_target_pairs={{5,4},{9,8},{10,9},{13,12},{14,13},{17,16},{18,17},{19,18},{21,20}... | collective-permute-start | bytes 1572872 | tf_op jit(solution)/shard_map/ppermute | solution.py:264
  61.1 103.5 %collective-permute-start.22 = (bf16[256,2048]{1,0:T(8,128)(2,1)}, bf16[256,2048]{1,0:T(8,128)(2,1)}, u32[]{:S(2)}, u32[]{:S(2)}) collective-permute-start(bf16[256,2048]{1,0:T(8,128)(2,1)} %collective-permute-done.21), channel_id=1, source_target_pairs={{0,28},{4,0},{8,4},{12,8},{16,12},{20,16},{24,20},{28,24},{1,29},{... | collective-permute-start | bytes 3145736 | tf_op jit(solution)/shard_map/ppermute | solution.py:269
  92.4 56.0 %collective-permute-start.13 = (bf16[1024,256]{1,0:T(8,128)(2,1)S(1)}, bf16[1024,256]{1,0:T(8,128)(2,1)S(1)}, u32[]{:S(2)}, u32[]{:S(2)}) collective-permute-start(bf16[1024,256]{1,0:T(8,128)(2,1)S(1)} %collective-permute-done.9.refs_10_.refs_8_), channel_id=1, source_target_pairs={{1,2},{2,3},{6,7},{10,11},{26,27},{30,31}} | collective-permute-start | bytes 1572872 | tf_op jit(solution)/shard_map/ppermute | solution.py:264
  104.0 52.3 %collective-permute-start.12 = (bf16[1024,256]{1,0:T(8,128)(2,1)S(1)}, bf16[1024,256]{1,0:T(8,128)(2,1)S(1)}, u32[]{:S(2)}, u32[]{:S(2)}) collective-permute-start(bf16[1024,256]{1,0:T(8,128)(2,1)S(1)} %collective-permute-done.8.refs_9_.refs_7_), channel_id=1, source_target_pairs={{9,8},{13,12},{17,16},{18,17},{21,20},{25,24}} | collective-permute-start | bytes 1572872 | tf_op jit(solution)/shard_map/ppermute | solution.py:264
  105.3 62.4 %copy-start.12 = (bf16[1024,256]{1,0:T(8,128)(2,1)}, bf16[1024,256]{1,0:T(8,128)(2,1)S(1)}, u32[]{:S(2)}) copy-start(bf16[1024,256]{1,0:T(8,128)(2,1)S(1)} %collective-permute-done.11.refs_12_.refs_10_) | copy-start | bytes 1572868
  105.3 51.7 %collective-permute-start.15 = (bf16[1024,256]{1,0:T(8,128)(2,1)S(1)}, bf16[1024,256]{1,0:T(8,128)(2,1)}, u32[]{:S(2)}, u32[]{:S(2)}) collective-permute-start(bf16[1024,256]{1,0:T(8,128)(2,1)S(1)} %collective-permute-done.11.refs_12_.refs_10_), channel_id=1, source_target_pairs={{1,2},{2,3},{6,7},{10,11},{26,27},{30,31}} | collective-permute-start | bytes 1572872 | tf_op jit(solution)/shard_map/ppermute | solution.py:264
  145.1 18.8 %collective-permute-start.14 = (bf16[1024,256]{1,0:T(8,128)(2,1)S(1)}, bf16[1024,256]{1,0:T(8,128)(2,1)}, u32[]{:S(2)}, u32[]{:S(2)}) collective-permute-start(bf16[1024,256]{1,0:T(8,128)(2,1)S(1)} %collective-permute-done.10.refs_11_.refs_9_), channel_id=1, source_target_pairs={{9,8},{13,12},{17,16},{18,17},{21,20},{25,24}} | collective-permute-start | bytes 1572872 | tf_op jit(solution)/shard_map/ppermute | solution.py:264
  148.4 19.3 %copy-start.19 = (bf16[1024,256]{1,0:T(8,128)(2,1)}, bf16[1024,256]{1,0:T(8,128)(2,1)S(1)}, u32[]{:S(2)}) copy-start(bf16[1024,256]{1,0:T(8,128)(2,1)S(1)} %collective-permute-done.13.refs_12_) | copy-start | bytes 1572868
  148.4 33.0 %collective-permute-start.17 = (bf16[1024,256]{1,0:T(8,128)(2,1)S(1)}, bf16[1024,256]{1,0:T(8,128)(2,1)S(1)}, u32[]{:S(2)}, u32[]{:S(2)}) collective-permute-start(bf16[1024,256]{1,0:T(8,128)(2,1)S(1)} %collective-permute-done.13.refs_12_), channel_id=1, source_target_pairs={{2,3}} | collective-permute-start | bytes 1572872 | tf_op jit(solution)/shard_map/ppermute | solution.py:264
  156.4 25.0 %collective-permute-start.16 = (bf16[1024,256]{1,0:T(8,128)(2,1)S(1)}, bf16[1024,256]{1,0:T(8,128)(2,1)S(1)}, u32[]{:S(2)}, u32[]{:S(2)}) collective-permute-start(bf16[1024,256]{1,0:T(8,128)(2,1)S(1)} %collective-permute-done.12.refs_11_), channel_id=1, source_target_pairs={{17,16}} | collective-permute-start | bytes 1572872 | tf_op jit(solution)/shard_map/ppermute | solution.py:264
  157.1 24.4 %collective-permute-start.19 = (bf16[1024,256]{1,0:T(8,128)(2,1)}, bf16[1024,256]{1,0:T(8,128)(2,1)S(1)}, u32[]{:S(2)}, u32[]{:S(2)}) collective-permute-start(bf16[1024,256]{1,0:T(8,128)(2,1)} %collective-permute-done.15.refs_14_), channel_id=1, source_target_pairs={{2,3}} | collective-permute-start | bytes 1572872 | tf_op jit(solution)/shard_map/ppermute | solution.py:264
  163.9 17.5 %collective-permute-start.18 = (bf16[1024,256]{1,0:T(8,128)(2,1)}, bf16[1024,256]{1,0:T(8,128)(2,1)S(1)}, u32[]{:S(2)}, u32[]{:S(2)}) collective-permute-start(bf16[1024,256]{1,0:T(8,128)(2,1)} %collective-permute-done.14.refs_13_), channel_id=1, source_target_pairs={{17,16}} | collective-permute-start | bytes 1572872 | tf_op jit(solution)/shard_map/ppermute | solution.py:264
  167.7 2.5 %copy-start.1 = (bf16[1024,256]{1,0:T(8,128)(2,1)S(1)}, bf16[1024,256]{1,0:T(8,128)(2,1)}, u32[]{:S(2)}) copy-start(bf16[1024,256]{1,0:T(8,128)(2,1)} %relay.8.refs_3_.refs_1_) | copy-start | bytes 1572868
  167.7 2.5 %copy-start.3 = (bf16[1024,256]{1,0:T(8,128)(2,1)S(1)}, bf16[1024,256]{1,0:T(8,128)(2,1)}, u32[]{:S(2)}) copy-start(bf16[1024,256]{1,0:T(8,128)(2,1)} %relay.9.refs_4_.refs_2_) | copy-start | bytes 1572868
  167.8 2.5 %copy-start.5 = (bf16[1024,256]{1,0:T(8,128)(2,1)S(1)}, bf16[1024,256]{1,0:T(8,128)(2,1)}, u32[]{:S(2)}) copy-start(bf16[1024,256]{1,0:T(8,128)(2,1)} %relay.13.refs_6_.refs_4_) | copy-start | bytes 1572868
  167.8 2.4 %copy-start.7 = (bf16[1024,256]{1,0:T(8,128)(2,1)S(1)}, bf16[1024,256]{1,0:T(8,128)(2,1)}, u32[]{:S(2)}) copy-start(bf16[1024,256]{1,0:T(8,128)(2,1)} %relay.11.refs_5_.refs_3_) | copy-start | bytes 1572868
  167.8 2.8 %copy-start.9 = (bf16[1024,256]{1,0:T(8,128)(2,1)S(1)}, bf16[1024,256]{1,0:T(8,128)(2,1)}, u32[]{:S(2)}) copy-start(bf16[1024,256]{1,0:T(8,128)(2,1)} %relay.15.refs_8_.refs_6_) | copy-start | bytes 1572868
  167.8 3.3 %copy-start.11 = (bf16[1024,256]{1,0:T(8,128)(2,1)S(1)}, bf16[1024,256]{1,0:T(8,128)(2,1)}, u32[]{:S(2)}) copy-start(bf16[1024,256]{1,0:T(8,128)(2,1)} %relay.14.refs_7_.refs_5_) | copy-start | bytes 1572868
  167.8 3.5 %copy-start.15 = (bf16[1024,256]{1,0:T(8,128)(2,1)S(1)}, bf16[1024,256]{1,0:T(8,128)(2,1)}, u32[]{:S(2)}) copy-start(bf16[1024,256]{1,0:T(8,128)(2,1)} %relay.10.refs_1_) | copy-start | bytes 1572868
  167.8 3.6 %copy-start.17 = (bf16[1024,256]{1,0:T(8,128)(2,1)S(1)}, bf16[1024,256]{1,0:T(8,128)(2,1)}, u32[]{:S(2)}) copy-start(bf16[1024,256]{1,0:T(8,128)(2,1)} %relay.12.refs_2_) | copy-start | bytes 1572868
  167.8 3.6 %copy-start.18 = (s32[68]{0:T(128)S(1)}, s32[68]{0:T(128)}, u32[]{:S(2)}) copy-start(s32[68]{0:T(128)} %get-tuple-element.7.table) | copy-start | bytes 820
  171.4 12.0 %copy-start.13 = (bf16[1024,256]{1,0:T(8,128)(2,1)S(1)}, bf16[1024,256]{1,0:T(8,128)(2,1)}, u32[]{:S(2)}) copy-start(bf16[1024,256]{1,0:T(8,128)(2,1)} %copy-done.12) | copy-start | bytes 1572868
  181.4 0.9 copy-start.20
  181.4 1.0 copy-start.21
  181.4 1.2 copy-start.22
  182.6 0.8 copy-start.23

commit v2 on v1

--- a/solution.py
+++ b/solution.py
@@ -66,34 +66,6 @@
             if key[0] == half and key[2] == s and key[1] > p:
                 return slot - DEPTH * p
         return None
-
-
-def relay_kernel(at, table, x, held, out, sem):
-    half_rows, width = out.shape
-
-    @pl.when(table[at] == 1)
-    def _():
-        row = pl.multiple_of(table[at + 1] * half_rows, half_rows)
-        col = pl.multiple_of(table[at + 2] * width, width)
-        copy = pltpu.make_async_copy(x.at[pl.ds(row, half_rows), pl.ds(col, width)], out, sem)
-        copy.start()
-        copy.wait()
-
-
-def relay(at, table, x, held):
-    return pl.pallas_call(
-        functools.partial(relay_kernel, at),
-        out_shape=jax.ShapeDtypeStruct(held.shape, held.dtype),
-        grid_spec=pltpu.PrefetchScalarGridSpec(
-            num_scalar_prefetch=1,
-            grid=(1,),
-            in_specs=[pl.BlockSpec(memory_space=pl.ANY)] * 2,
-            out_specs=pl.BlockSpec(memory_space=pl.ANY),
-            scratch_shapes=[pltpu.SemaphoreType.DMA],
-        ),
-        input_output_aliases={2: 0},
-        name="relay",
-    )(table, x, held)
 
 
 def product_kernel(half, at, candidates, scale, n_buffers, table, *refs):
@@ -256,11 +228,10 @@
                 continue
             at = own_at[d, t]
             held = buffers.get((d, t - DEPTH))
-            if held is None:
+            if held is None or numbers[:, at].any():
                 start = (table[at + 1] * half_rows, table[at + 2] * group_size)
-                held = lax.dynamic_slice(x, start, (half_rows, group_size))
-            elif numbers[:, at].any():
-                held = buffers[d, t - DEPTH] = relay(at, table, x, held)
+                mine = lax.dynamic_slice(x, start, (half_rows, group_size))
+                held = mine if held is None else jnp.where(table[at] == 1, mine, held)
             buffers[d, t] = lax.ppermute(held, ("row", "col"), pairs)
 
     back = [(i, (i - 1) % rows) for i in range(rows)]

time: 195 us -> 152 us (0.78)
  the two profiles are of different devices: /device:TPU:2 before, /device:TPU:12 now
where the time goes in v2:
time: 152 us; the launch traced here: 151 us
  waiting for transfers between devices  43.3 us (28%)
  starting transfers between devices  42.4 us (28%)
  between operations  21.5 us (14%)
  Pallas kernels  21 us (14%)
  other arithmetic  14.9 us (10%)
  local copies, waits for them, and re-layouts  8.1 us (5%)
    ppermute x20, waiting for transfers between devices, local(): buffers[d, t] = lax.ppermute(held, ('row', 'col'), pairs)  43.3 us
    ppermute x20, starting transfers between devices, local(): buffers[d, t] = lax.ppermute(held, ('row', 'col'), pairs)  36.7 us
    pallas_call x2, Pallas kernels, product(): pl.pallas_call(functools.partial(product_kernel, half, at, candidates, sc...  21 us
    select_n x3, other arithmetic, local(): held = mine if held is None else jnp.where(table[at] == 1, mine, held)  7.75 us
    ppermute x3, starting transfers between devices, local(): window.append(lax.ppermute(window[-1], 'row', back))  3.94 us
    convert_element_type x1, other arithmetic, local(): (value * window_factor[part, None] * male_cols).astype(jnp.bfloat16)  3.07 us
  transfers between devices with their start and end apart: 25, of which 7 were waited for; matrix products, arithmetic and copies ran while one was open for 11% of the time, Pallas kernels for 7%

profile of v2, /device:TPU:12, one launch (start us, length us, event | category | flops | bytes accessed | tf_op | source)
XLA Modules:
  0.0 151.2 jit_solution(5041589159490844752)
XLA Ops:
  0.6 0.0 copy-start.4
  0.7 0.8 constant_dynamic-slice_fusion
  1.5 0.7 fusion.7
  4.7 2.3 %fusion.3 = (bf16[1024,256]{1,0:T(8,128)(2,1)}, bf16[1024,256]{1,0:T(8,128)(2,1)}) fusion(bf16[2048,512]{1,0:T(8,128)(2,1)} %refs_0_.3, s32[]{:T(128)S(6)} %select_n.143, s32[]{:T(128)S(6)} %select_n.144, s32[]{:T(128)S(6)} %select_n.141, s32[]{:T(128)S(6)} %select_n.142), kind=kLoop, calls=%fused_computation.28 | loop fusion | bytes 2097168 | tf_op jit(solution)/shard_map/dynamic_slice | solution.py:233
  7.0 0.7 collective-permute-start.1
  7.7 1.3 collective-permute-start
  9.0 1.7 %collective-permute-start.20 = (bf16[256,2048]{1,0:T(8,128)(2,1)}, bf16[256,2048]{1,0:T(8,128)(2,1)}, u32[]{:S(2)}, u32[]{:S(2)}) collective-permute-start(bf16[256,2048]{1,0:T(8,128)(2,1)} %param.8), channel_id=1, source_target_pairs={{0,28},{4,0},{8,4},{12,8},{16,12},{20,16},{24,20},{28,24},{1,29},{... | collective-permute-start | bytes 3145736 | tf_op jit(solution)/shard_map/ppermute | solution.py:240
  12.0 0.7 fusion.6
  17.9 0.1 dynamic_slice.66
  18.0 0.1 dynamic_slice.67
  18.0 7.8 %collective-permute-done.refs_3_.refs_1_ = bf16[1024,256]{1,0:T(8,128)(2,1)S(1)} collective-permute-done((bf16[1024,256]{1,0:T(8,128)(2,1)}, bf16[1024,256]{1,0:T(8,128)(2,1)S(1)}, u32[]{:S(2)}, u32[]{:S(2)}) %collective-permute-start) | collective-permute-done | bytes 524320 | tf_op jit(solution)/shard_map/ppermute | solution.py:235
  25.8 1.5 dynamic-slice_select_fusion.4
  27.3 0.7 collective-permute-start.4
  28.0 1.3 collective-permute-start.2
  29.3 1.1 multiply_reduce_fusion
  30.4 0.1 collective-permute-start.23
  34.2 0.7 collective-permute-start.7
  34.9 0.0 collective-permute-done.20
  34.9 3.9 %collective-permute-start.6 = (bf16[1024,256]{1,0:T(8,128)(2,1)}, bf16[1024,256]{1,0:T(8,128)(2,1)S(1)}, u32[]{:S(2)}, u32[]{:S(2)}) collective-permute-start(bf16[1024,256]{1,0:T(8,128)(2,1)} %get-tuple-element.7), channel_id=1, source_target_pairs={{1,0},{5,4},{6,5},{9,8},{13,12},{14,13},{15,14},{17,16},{18,17},{2... | collective-permute-start | bytes 1572872 | tf_op jit(solution)/shard_map/ppermute | solution.py:235
  38.9 2.2 %collective-permute-start.21 = (bf16[256,2048]{1,0:T(8,128)(2,1)}, bf16[256,2048]{1,0:T(8,128)(2,1)}, u32[]{:S(2)}, u32[]{:S(2)}) collective-permute-start(bf16[256,2048]{1,0:T(8,128)(2,1)} %collective-permute-done.20), channel_id=1, source_target_pairs={{0,28},{4,0},{8,4},{12,8},{16,12},{20,16},{24,20},{28,24},{1,29},{... | collective-permute-start | bytes 3145736 | tf_op jit(solution)/shard_map/ppermute | solution.py:240
  41.1 2.4 %collective-permute-done.2.refs_1_ = bf16[1024,256]{1,0:T(8,128)(2,1)S(1)} collective-permute-done((bf16[1024,256]{1,0:T(8,128)(2,1)}, bf16[1024,256]{1,0:T(8,128)(2,1)S(1)}, u32[]{:S(2)}, u32[]{:S(2)}) %collective-permute-start.2) | collective-permute-done | bytes 524320 | tf_op jit(solution)/shard_map/ppermute | solution.py:235
  43.5 2.7 %dynamic-slice_select_fusion.6 = (bf16[1024,256]{1,0:T(8,128)(2,1)}, bf16[1024,256]{1,0:T(8,128)(2,1)}) fusion(bf16[1024,256]{1,0:T(8,128)(2,1)S(1)} %collective-permute-done.4.refs_2_, bf16[2048,512]{1,0:T(8,128)(2,1)} %refs_0_.3, s32[]{:T(128)S(6)} %select_n.152, s32[]{:T(128)S(6)} %select_n.153, pred[]{:T(512)} %bitcast.10, ...), kind=kLoop, calls=%fused_computation.13 | loop fusion | flops 524288 | bytes 3145746 | tf_op jit(solution)/shard_map/jit(_where)/select_n | solution.py:234
  46.2 0.7 collective-permute-start.5
  46.9 0.0 collective-permute-done.23
  46.9 1.9 %collective-permute-start.3 = (bf16[1024,256]{1,0:T(8,128)(2,1)}, bf16[1024,256]{1,0:T(8,128)(2,1)S(1)}, u32[]{:S(2)}, u32[]{:S(2)}) collective-permute-start(bf16[1024,256]{1,0:T(8,128)(2,1)} %get-tuple-element.11), channel_id=1, source_target_pairs={{1,0},{5,4},{9,8},{13,12},{14,13},{17,16},{18,17},{21,20},{22,21},... | collective-permute-start | bytes 1572872 | tf_op jit(solution)/shard_map/ppermute | solution.py:235
  56.6 0.0 collective-permute-done.7.refs_8_.refs_6_
  56.6 1.7 %collective-permute-start.24 = (f32[2048]{0:T(1024)S(1)}, f32[2048]{0:T(1024)S(1)}, u32[]{:S(2)}, u32[]{:S(2)}) collective-permute-start(f32[2048]{0:T(1024)S(1)} %add.121), channel_id=1, source_target_pairs={{0,2},{1,3},{2,0},{3,1},{4,6},{5,7},{6,4},{7,5},{8,10},{9,11},{10,... | collective-permute-start | bytes 24584 | tf_op jit(solution)/shard_map/ppermute | solution.py:164
  58.2 0.0 collective-permute-done.6.refs_7_.refs_5_
  58.2 0.0 collective-permute-done.5.refs_6_.refs_4_
  58.2 8.2 %collective-permute-done.3.refs_5_.refs_3_ = bf16[1024,256]{1,0:T(8,128)(2,1)S(1)} collective-permute-done((bf16[1024,256]{1,0:T(8,128)(2,1)}, bf16[1024,256]{1,0:T(8,128)(2,1)S(1)}, u32[]{:S(2)}, u32[]{:S(2)}) %collective-permute-start.3) | collective-permute-done | bytes 524320 | tf_op jit(solution)/shard_map/ppermute | solution.py:235
  66.4 3.6 %dynamic-slice_select_fusion = (bf16[1024,256]{1,0:T(8,128)(2,1)}, bf16[1024,256]{1,0:T(8,128)(2,1)}, bf16[1024,256]{1,0:T(8,128)(2,1)}, bf16[1024,256]{1,0:T(8,128)(2,1)}) fusion(bf16[1024,256]{1,0:T(8,128)(2,1)S(1)} %collective-permute-done.7.refs_8_.refs_6_, bf16[2048,512]{1,0:T(8,128)(2,1)} %refs_0_.3, s32[]{:T(128)S(6)} %select_n.178, s32[]{:T(128)S(6)} %select_n.179, ...), kind=kLoop, calls=%fused_computation.7 | loop fusion | flops 1048576 | bytes 6291492 | tf_op jit(solution)/shard_map/jit(_where)/select_n | solution.py:234
  70.0 1.5 collective-permute-start.11
  71.5 1.9 %collective-permute-start.10 = (bf16[1024,256]{1,0:T(8,128)(2,1)}, bf16[1024,256]{1,0:T(8,128)(2,1)}, u32[]{:S(2)}, u32[]{:S(2)}) collective-permute-start(bf16[1024,256]{1,0:T(8,128)(2,1)} %get-tuple-element.3), channel_id=1, source_target_pairs={{5,4},{9,8},{10,9},{13,12},{14,13},{17,16},{18,17},{19,18},{21,20}... | collective-permute-start | bytes 1572872 | tf_op jit(solution)/shard_map/ppermute | solution.py:235
  73.4 1.5 collective-permute-start.9
  74.9 0.0 collective-permute-done.24
  74.9 1.9 %collective-permute-start.8 = (bf16[1024,256]{1,0:T(8,128)(2,1)}, bf16[1024,256]{1,0:T(8,128)(2,1)}, u32[]{:S(2)}, u32[]{:S(2)}) collective-permute-start(bf16[1024,256]{1,0:T(8,128)(2,1)} %get-tuple-element.5), channel_id=1, source_target_pairs={{5,4},{9,8},{10,9},{13,12},{14,13},{17,16},{18,17},{19,18},{21,20}... | collective-permute-start | bytes 1572872 | tf_op jit(solution)/shard_map/ppermute | solution.py:235
  76.8 0.0 collective-permute-done.21
  76.8 0.1 collective-permute-start.22
  76.9 0.1 fusion
  77.0 1.5 collective-permute-start.15
  78.5 10.1 %collective-permute-done.10.refs_11_.refs_9_ = bf16[1024,256]{1,0:T(8,128)(2,1)} collective-permute-done((bf16[1024,256]{1,0:T(8,128)(2,1)}, bf16[1024,256]{1,0:T(8,128)(2,1)}, u32[]{:S(2)}, u32[]{:S(2)}) %collective-permute-start.10) | collective-permute-done | bytes 524320 | tf_op jit(solution)/shard_map/ppermute | solution.py:235
  88.6 1.9 %collective-permute-start.14 = (bf16[1024,256]{1,0:T(8,128)(2,1)}, bf16[1024,256]{1,0:T(8,128)(2,1)}, u32[]{:S(2)}, u32[]{:S(2)}) collective-permute-start(bf16[1024,256]{1,0:T(8,128)(2,1)} %collective-permute-done.10.refs_11_.refs_9_), channel_id=1, source_target_pairs={{9,8},{13,12},{17,16},{18,17},{21,20},{25,24}} | collective-permute-start | bytes 1572872 | tf_op jit(solution)/shard_map/ppermute | solution.py:235
  90.5 1.5 collective-permute-start.13
  92.0 6.0 %collective-permute-done.8.refs_9_.refs_7_ = bf16[1024,256]{1,0:T(8,128)(2,1)} collective-permute-done((bf16[1024,256]{1,0:T(8,128)(2,1)}, bf16[1024,256]{1,0:T(8,128)(2,1)}, u32[]{:S(2)}, u32[]{:S(2)}) %collective-permute-start.8) | collective-permute-done | bytes 524320 | tf_op jit(solution)/shard_map/ppermute | solution.py:235
  98.1 3.7 %collective-permute-start.12 = (bf16[1024,256]{1,0:T(8,128)(2,1)}, bf16[1024,256]{1,0:T(8,128)(2,1)}, u32[]{:S(2)}, u32[]{:S(2)}) collective-permute-start(bf16[1024,256]{1,0:T(8,128)(2,1)} %collective-permute-done.8.refs_9_.refs_7_), channel_id=1, source_target_pairs={{9,8},{13,12},{17,16},{18,17},{21,20},{25,24}} | collective-permute-start | bytes 1572872 | tf_op jit(solution)/shard_map/ppermute | solution.py:235
  101.7 1.4 copy.11.refs_15_.refs_21_
  103.1 0.6 multiply_add_fusion
  103.7 0.0 collective-permute-done.15.refs_14_
  103.7 0.7 collective-permute-start.19
  104.4 4.2 %collective-permute-done.14.refs_13_ = bf16[1024,256]{1,0:T(8,128)(2,1)} collective-permute-done((bf16[1024,256]{1,0:T(8,128)(2,1)}, bf16[1024,256]{1,0:T(8,128)(2,1)}, u32[]{:S(2)}, u32[]{:S(2)}) %collective-permute-start.14) | collective-permute-done | bytes 524320 | tf_op jit(solution)/shard_map/ppermute | solution.py:235
  108.6 4.4 %collective-permute-start.18 = (bf16[1024,256]{1,0:T(8,128)(2,1)}, bf16[1024,256]{1,0:T(8,128)(2,1)S(1)}, u32[]{:S(2)}, u32[]{:S(2)}) collective-permute-start(bf16[1024,256]{1,0:T(8,128)(2,1)} %collective-permute-done.14.refs_13_), channel_id=1, source_target_pairs={{17,16}} | collective-permute-start | bytes 1572872 | tf_op jit(solution)/shard_map/ppermute | solution.py:235
  113.0 0.7 collective-permute-start.17
  113.7 4.6 %collective-permute-done.12.refs_11_ = bf16[1024,256]{1,0:T(8,128)(2,1)} collective-permute-done((bf16[1024,256]{1,0:T(8,128)(2,1)}, bf16[1024,256]{1,0:T(8,128)(2,1)}, u32[]{:S(2)}, u32[]{:S(2)}) %collective-permute-start.12) | collective-permute-done | bytes 524320 | tf_op jit(solution)/shard_map/ppermute | solution.py:235
  118.3 4.4 %collective-permute-start.16 = (bf16[1024,256]{1,0:T(8,128)(2,1)}, bf16[1024,256]{1,0:T(8,128)(2,1)S(1)}, u32[]{:S(2)}, u32[]{:S(2)}) collective-permute-start(bf16[1024,256]{1,0:T(8,128)(2,1)} %collective-permute-done.12.refs_11_), channel_id=1, source_target_pairs={{17,16}} | collective-permute-start | bytes 1572872 | tf_op jit(solution)/shard_map/ppermute | solution.py:235
  122.7 0.0 collective-permute-done.22
  122.8 3.1 %multiply_convert_fusion.4 = (bf16[256,2048]{1,0:T(8,128)(2,1)S(1)}, bf16[256,2048]{1,0:T(8,128)(2,1)S(1)}, bf16[256,2048]{1,0:T(8,128)(2,1)S(1)}, bf16[256,2048]{1,0:T(8,128)(2,1)S(1)}) fusion(bf16[256,2048]{1,0:T(8,128)(2,1)} %param.8, f32[2048]{0:T(1024)S(1)} %compare_select_fusion, f32[256]{0:T(256)S(1)} %get-tuple-element.26, ...), kind=kLoop, calls=%fused_computation.6 | loop fusion | flops 10485760 | bytes 8404992 | tf_op jit(solution)/shard_map/convert_element_type | solution.py:258
  125.9 2.3 %pad_maximum_fusion.refs_16_.refs_22_ = bf16[1024,2048]{1,0:T(8,128)(2,1)} fusion(bf16[256,2048]{1,0:T(8,128)(2,1)S(1)} %get-tuple-element.19, bf16[256,2048]{1,0:T(8,128)(2,1)S(1)} %get-tuple-element.18, bf16[256,2048]{1,0:T(8,128)(2,1)S(1)} %get-tuple-element.17, bf16[256,2048]{1,0:T(8,128)(2,1)S(1)} %get-tuple-element.16), kind=kLoop, calls=%fused_computation | loop fusion | flops 16777216 | bytes 8388608 | tf_op jit(solution)/shard_map/concatenate | solution.py:259
  128.2 10.0 %product.2.refs_23_ = bf16[2048,2048]{1,0:T(8,128)(2,1)} custom-call(s32[68]{0:T(128)S(1)} %get-tuple-element.15.table, bf16[2048,512]{1,0:T(8,128)(2,1)} %refs_0_.3, bf16[1024,256]{1,0:T(8,128)(2,1)S(1)} %copy-done.3, bf16[1024,256]{1,0:T(8,128)(2,1)S(1)} %copy-done.1, bf16[1024,256]{1,0:T(8,128)(2,1)S(1)} %collective-permute-done.refs_3_.refs_1_, ...), custom_call_target="tpu_custom_call" | custom-call | flops 4294967296 | bytes 10485760 | tf_op jit(solution)/shard_map/product/pallas_call | solution.py:135
  138.2 0.0 collective-permute-done.18.refs_17_
  138.2 0.7 copy-done.6
  139.0 0.2 copy-done.7
  139.2 0.2 copy-done.8
  139.4 0.8 copy-done.9
  140.2 11.0 %product.3 = bf16[2048,2048]{1,0:T(8,128)(2,1)} custom-call(s32[68]{0:T(128)S(1)} %get-tuple-element.15.table, bf16[2048,512]{1,0:T(8,128)(2,1)} %refs_0_.3, bf16[1024,256]{1,0:T(8,128)(2,1)S(1)} %collective-permute-done.refs_3_.refs_1_, bf16[1024,256]{1,0:T(8,128)(2,1)S(1)} %collective-permute-done.1.refs_4_.refs_2_, ...), custom_call_target="tpu_custom_call", output_to_operand_aliasing={{}: (24, {})} | custom-call | flops 4294967296 | bytes 10485760 | tf_op jit(solution)/shard_map/product/pallas_call | solution.py:135
  (37 shorter events, 0.1 us)
Async XLA Ops:
  0.6 25.2 %copy-start.4 = (bf16[2048,512]{1,0:T(8,128)(2,1)S(1)}, bf16[2048,512]{1,0:T(8,128)(2,1)}, u32[]{:S(2)}) copy-start(bf16[2048,512]{1,0:T(8,128)(2,1)} %refs_0_.3) | copy-start | bytes 6291460
  0.6 17.2 %copy-start.13 = (f32[2048]{0:T(1024)S(1)}, f32[2048]{0:T(1024)}, u32[]{:S(2)}) copy-start(f32[2048]{0:T(1024)} %param.10) | copy-start | bytes 24580
  0.7 17.2 %copy-start.12 = (f32[2048]{0:T(1024)S(1)}, f32[2048]{0:T(1024)}, u32[]{:S(2)}) copy-start(f32[2048]{0:T(1024)} %param.9) | copy-start | bytes 24580
  7.0 11.0 %collective-permute-start.1 = (bf16[1024,256]{1,0:T(8,128)(2,1)}, bf16[1024,256]{1,0:T(8,128)(2,1)S(1)}, u32[]{:S(2)}, u32[]{:S(2)}) collective-permute-start(bf16[1024,256]{1,0:T(8,128)(2,1)} %get-tuple-element.12), channel_id=1, source_target_pairs={{0,1},{1,2},{5,6},{6,7},{9,10},{10,11},{14,15},{18,19},{20,21},{22... | collective-permute-start | bytes 1572872 | tf_op jit(solution)/shard_map/ppermute | solution.py:235
  7.7 18.1 %collective-permute-start = (bf16[1024,256]{1,0:T(8,128)(2,1)}, bf16[1024,256]{1,0:T(8,128)(2,1)S(1)}, u32[]{:S(2)}, u32[]{:S(2)}) collective-permute-start(bf16[1024,256]{1,0:T(8,128)(2,1)} %get-tuple-element.13), channel_id=1, source_target_pairs={{1,0},{5,4},{9,8},{10,9},{13,12},{14,13},{18,17},{19,18},{22,21},{... | collective-permute-start | bytes 1572872 | tf_op jit(solution)/shard_map/ppermute | solution.py:235
  9.0 25.9 %collective-permute-start.20 = (bf16[256,2048]{1,0:T(8,128)(2,1)}, bf16[256,2048]{1,0:T(8,128)(2,1)}, u32[]{:S(2)}, u32[]{:S(2)}) collective-permute-start(bf16[256,2048]{1,0:T(8,128)(2,1)} %param.8), channel_id=1, source_target_pairs={{0,28},{4,0},{8,4},{12,8},{16,12},{20,16},{24,20},{28,24},{1,29},{... | collective-permute-start | bytes 3145736 | tf_op jit(solution)/shard_map/ppermute | solution.py:240
  25.8 3.5 %copy-start.10 = (s32[2048]{0:T(1024)S(1)}, s32[2048]{0:T(1024)}, u32[]{:S(2)}) copy-start(s32[2048]{0:T(1024)} %param.11) | copy-start | bytes 24580
  25.8 3.5 %copy-start.5 = (bf16[2048,512]{1,0:T(8,128)(2,1)S(1)}, bf16[2048,512]{1,0:T(8,128)(2,1)}, u32[]{:S(2)}) copy-start(bf16[2048,512]{1,0:T(8,128)(2,1)} %refs_0_.3) | copy-start | bytes 6291460
  27.3 11.6 %collective-permute-start.4 = (bf16[1024,256]{1,0:T(8,128)(2,1)}, bf16[1024,256]{1,0:T(8,128)(2,1)S(1)}, u32[]{:S(2)}, u32[]{:S(2)}) collective-permute-start(bf16[1024,256]{1,0:T(8,128)(2,1)} %get-tuple-element.8), channel_id=1, source_target_pairs={{0,1},{1,2},{4,5},{5,6},{6,7},{9,10},{10,11},{13,14},{14,15},{18,1... | collective-permute-start | bytes 1572872 | tf_op jit(solution)/shard_map/ppermute | solution.py:235
  28.0 15.5 %collective-permute-start.2 = (bf16[1024,256]{1,0:T(8,128)(2,1)}, bf16[1024,256]{1,0:T(8,128)(2,1)S(1)}, u32[]{:S(2)}, u32[]{:S(2)}) collective-permute-start(bf16[1024,256]{1,0:T(8,128)(2,1)} %get-tuple-element.9), channel_id=1, source_target_pairs={{1,0},{5,4},{6,5},{9,8},{10,9},{13,12},{14,13},{15,14},{18,17},{19... | collective-permute-start | bytes 1572872 | tf_op jit(solution)/shard_map/ppermute | solution.py:235
  30.4 16.5 %collective-permute-start.23 = (f32[2048]{0:T(1024)S(1)}, f32[2048]{0:T(1024)S(1)}, u32[]{:S(2)}, u32[]{:S(2)}) collective-permute-start(f32[2048]{0:T(1024)S(1)} %multiply_reduce_fusion), channel_id=1, source_target_pairs={{0,1},{1,0},{2,3},{3,2},{4,5},{5,4},{6,7},{7,6},{8,9},{9,8},{10,11... | collective-permute-start | bytes 24584 | tf_op jit(solution)/shard_map/ppermute | solution.py:164
  34.2 22.3 %collective-permute-start.7 = (bf16[1024,256]{1,0:T(8,128)(2,1)}, bf16[1024,256]{1,0:T(8,128)(2,1)S(1)}, u32[]{:S(2)}, u32[]{:S(2)}) collective-permute-start(bf16[1024,256]{1,0:T(8,128)(2,1)} %get-tuple-element.6), channel_id=1, source_target_pairs={{1,2},{2,3},{4,5},{5,6},{6,7},{10,11},{13,14},{14,15},{18,19},{21,... | collective-permute-start | bytes 1572872 | tf_op jit(solution)/shard_map/ppermute | solution.py:235
  34.9 23.3 %collective-permute-start.6 = (bf16[1024,256]{1,0:T(8,128)(2,1)}, bf16[1024,256]{1,0:T(8,128)(2,1)S(1)}, u32[]{:S(2)}, u32[]{:S(2)}) collective-permute-start(bf16[1024,256]{1,0:T(8,128)(2,1)} %get-tuple-element.7), channel_id=1, source_target_pairs={{1,0},{5,4},{6,5},{9,8},{13,12},{14,13},{15,14},{17,16},{18,17},{2... | collective-permute-start | bytes 1572872 | tf_op jit(solution)/shard_map/ppermute | solution.py:235
  38.9 7.3 %copy-start = (bf16[1024,256]{1,0:T(8,128)(2,1)}, bf16[1024,256]{1,0:T(8,128)(2,1)S(1)}, u32[]{:S(2)}) copy-start(bf16[1024,256]{1,0:T(8,128)(2,1)S(1)} %collective-permute-done.4.refs_2_) | copy-start | bytes 1572868
  38.9 37.9 %collective-permute-start.21 = (bf16[256,2048]{1,0:T(8,128)(2,1)}, bf16[256,2048]{1,0:T(8,128)(2,1)}, u32[]{:S(2)}, u32[]{:S(2)}) collective-permute-start(bf16[256,2048]{1,0:T(8,128)(2,1)} %collective-permute-done.20), channel_id=1, source_target_pairs={{0,28},{4,0},{8,4},{12,8},{16,12},{20,16},{24,20},{28,24},{1,29},{... | collective-permute-start | bytes 3145736 | tf_op jit(solution)/shard_map/ppermute | solution.py:240
  43.5 3.4 %copy-start.2 = (bf16[1024,256]{1,0:T(8,128)(2,1)}, bf16[1024,256]{1,0:T(8,128)(2,1)S(1)}, u32[]{:S(2)}) copy-start(bf16[1024,256]{1,0:T(8,128)(2,1)S(1)} %collective-permute-done.2.refs_1_) | copy-start | bytes 1572868
  46.2 12.1 %collective-permute-start.5 = (bf16[1024,256]{1,0:T(8,128)(2,1)}, bf16[1024,256]{1,0:T(8,128)(2,1)S(1)}, u32[]{:S(2)}, u32[]{:S(2)}) collective-permute-start(bf16[1024,256]{1,0:T(8,128)(2,1)} %get-tuple-element.10), channel_id=1, source_target_pairs={{1,2},{2,3},{5,6},{6,7},{10,11},{14,15},{18,19},{21,22},{24,25},{2... | collective-permute-start | bytes 1572872 | tf_op jit(solution)/shard_map/ppermute | solution.py:235
  46.9 19.6 %collective-permute-start.3 = (bf16[1024,256]{1,0:T(8,128)(2,1)}, bf16[1024,256]{1,0:T(8,128)(2,1)S(1)}, u32[]{:S(2)}, u32[]{:S(2)}) collective-permute-start(bf16[1024,256]{1,0:T(8,128)(2,1)} %get-tuple-element.11), channel_id=1, source_target_pairs={{1,0},{5,4},{9,8},{13,12},{14,13},{17,16},{18,17},{21,20},{22,21},... | collective-permute-start | bytes 1572872 | tf_op jit(solution)/shard_map/ppermute | solution.py:235
  56.6 18.3 %collective-permute-start.24 = (f32[2048]{0:T(1024)S(1)}, f32[2048]{0:T(1024)S(1)}, u32[]{:S(2)}, u32[]{:S(2)}) collective-permute-start(f32[2048]{0:T(1024)S(1)} %add.121), channel_id=1, source_target_pairs={{0,2},{1,3},{2,0},{3,1},{4,6},{5,7},{6,4},{7,5},{8,10},{9,11},{10,... | collective-permute-start | bytes 24584 | tf_op jit(solution)/shard_map/ppermute | solution.py:164
  66.4 36.7 %copy-start.11 = (s32[2048]{0:T(1024)S(1)}, s32[2048]{0:T(1024)}, u32[]{:S(2)}) copy-start(s32[2048]{0:T(1024)} %param.12) | copy-start | bytes 24580
  70.0 7.0 %collective-permute-start.11 = (bf16[1024,256]{1,0:T(8,128)(2,1)}, bf16[1024,256]{1,0:T(8,128)(2,1)}, u32[]{:S(2)}, u32[]{:S(2)}) collective-permute-start(bf16[1024,256]{1,0:T(8,128)(2,1)} %get-tuple-element.2), channel_id=1, source_target_pairs={{0,1},{1,2},{2,3},{5,6},{6,7},{9,10},{10,11},{14,15},{22,23},{25,2... | collective-permute-start | bytes 1572872 | tf_op jit(solution)/shard_map/ppermute | solution.py:235
  71.5 17.1 %collective-permute-start.10 = (bf16[1024,256]{1,0:T(8,128)(2,1)}, bf16[1024,256]{1,0:T(8,128)(2,1)}, u32[]{:S(2)}, u32[]{:S(2)}) collective-permute-start(bf16[1024,256]{1,0:T(8,128)(2,1)} %get-tuple-element.3), channel_id=1, source_target_pairs={{5,4},{9,8},{10,9},{13,12},{14,13},{17,16},{18,17},{19,18},{21,20}... | collective-permute-start | bytes 1572872 | tf_op jit(solution)/shard_map/ppermute | solution.py:235
  73.4 17.1 %collective-permute-start.9 = (bf16[1024,256]{1,0:T(8,128)(2,1)}, bf16[1024,256]{1,0:T(8,128)(2,1)}, u32[]{:S(2)}, u32[]{:S(2)}) collective-permute-start(bf16[1024,256]{1,0:T(8,128)(2,1)} %get-tuple-element.4), channel_id=1, source_target_pairs={{0,1},{1,2},{2,3},{5,6},{6,7},{9,10},{10,11},{14,15},{22,23},{25,2... | collective-permute-start | bytes 1572872 | tf_op jit(solution)/shard_map/ppermute | solution.py:235
  74.9 23.1 %collective-permute-start.8 = (bf16[1024,256]{1,0:T(8,128)(2,1)}, bf16[1024,256]{1,0:T(8,128)(2,1)}, u32[]{:S(2)}, u32[]{:S(2)}) collective-permute-start(bf16[1024,256]{1,0:T(8,128)(2,1)} %get-tuple-element.5), channel_id=1, source_target_pairs={{5,4},{9,8},{10,9},{13,12},{14,13},{17,16},{18,17},{19,18},{21,20}... | collective-permute-start | bytes 1572872 | tf_op jit(solution)/shard_map/ppermute | solution.py:235
  76.8 45.9 %collective-permute-start.22 = (bf16[256,2048]{1,0:T(8,128)(2,1)}, bf16[256,2048]{1,0:T(8,128)(2,1)}, u32[]{:S(2)}, u32[]{:S(2)}) collective-permute-start(bf16[256,2048]{1,0:T(8,128)(2,1)} %collective-permute-done.21), channel_id=1, source_target_pairs={{0,28},{4,0},{8,4},{12,8},{16,12},{20,16},{24,20},{28,24},{1,29},{... | collective-permute-start | bytes 3145736 | tf_op jit(solution)/shard_map/ppermute | solution.py:240
  77.0 26.7 %collective-permute-start.15 = (bf16[1024,256]{1,0:T(8,128)(2,1)}, bf16[1024,256]{1,0:T(8,128)(2,1)}, u32[]{:S(2)}, u32[]{:S(2)}) collective-permute-start(bf16[1024,256]{1,0:T(8,128)(2,1)} %collective-permute-done.11.refs_12_.refs_10_), channel_id=1, source_target_pairs={{1,2},{2,3},{6,7},{10,11},{26,27},{30,31}} | collective-permute-start | bytes 1572872 | tf_op jit(solution)/shard_map/ppermute | solution.py:235
  88.6 20.0 %collective-permute-start.14 = (bf16[1024,256]{1,0:T(8,128)(2,1)}, bf16[1024,256]{1,0:T(8,128)(2,1)}, u32[]{:S(2)}, u32[]{:S(2)}) collective-permute-start(bf16[1024,256]{1,0:T(8,128)(2,1)} %collective-permute-done.10.refs_11_.refs_9_), channel_id=1, source_target_pairs={{9,8},{13,12},{17,16},{18,17},{21,20},{25,24}} | collective-permute-start | bytes 1572872 | tf_op jit(solution)/shard_map/ppermute | solution.py:235
  90.5 22.5 %collective-permute-start.13 = (bf16[1024,256]{1,0:T(8,128)(2,1)}, bf16[1024,256]{1,0:T(8,128)(2,1)}, u32[]{:S(2)}, u32[]{:S(2)}) collective-permute-start(bf16[1024,256]{1,0:T(8,128)(2,1)} %collective-permute-done.9.refs_10_.refs_8_), channel_id=1, source_target_pairs={{1,2},{2,3},{6,7},{10,11},{26,27},{30,31}} | collective-permute-start | bytes 1572872 | tf_op jit(solution)/shard_map/ppermute | solution.py:235
  98.1 20.3 %collective-permute-start.12 = (bf16[1024,256]{1,0:T(8,128)(2,1)}, bf16[1024,256]{1,0:T(8,128)(2,1)}, u32[]{:S(2)}, u32[]{:S(2)}) collective-permute-start(bf16[1024,256]{1,0:T(8,128)(2,1)} %collective-permute-done.8.refs_9_.refs_7_), channel_id=1, source_target_pairs={{9,8},{13,12},{17,16},{18,17},{21,20},{25,24}} | collective-permute-start | bytes 1572872 | tf_op jit(solution)/shard_map/ppermute | solution.py:235
  103.7 34.4 %collective-permute-start.19 = (bf16[1024,256]{1,0:T(8,128)(2,1)}, bf16[1024,256]{1,0:T(8,128)(2,1)S(1)}, u32[]{:S(2)}, u32[]{:S(2)}) collective-permute-start(bf16[1024,256]{1,0:T(8,128)(2,1)} %collective-permute-done.15.refs_14_), channel_id=1, source_target_pairs={{2,3}} | collective-permute-start | bytes 1572872 | tf_op jit(solution)/shard_map/ppermute | solution.py:235
  108.6 29.6 %collective-permute-start.18 = (bf16[1024,256]{1,0:T(8,128)(2,1)}, bf16[1024,256]{1,0:T(8,128)(2,1)S(1)}, u32[]{:S(2)}, u32[]{:S(2)}) collective-permute-start(bf16[1024,256]{1,0:T(8,128)(2,1)} %collective-permute-done.14.refs_13_), channel_id=1, source_target_pairs={{17,16}} | collective-permute-start | bytes 1572872 | tf_op jit(solution)/shard_map/ppermute | solution.py:235
  113.0 25.2 %collective-permute-start.17 = (bf16[1024,256]{1,0:T(8,128)(2,1)}, bf16[1024,256]{1,0:T(8,128)(2,1)S(1)}, u32[]{:S(2)}, u32[]{:S(2)}) collective-permute-start(bf16[1024,256]{1,0:T(8,128)(2,1)} %collective-permute-done.13.refs_12_), channel_id=1, source_target_pairs={{2,3}} | collective-permute-start | bytes 1572872 | tf_op jit(solution)/shard_map/ppermute | solution.py:235
  118.3 19.9 %collective-permute-start.16 = (bf16[1024,256]{1,0:T(8,128)(2,1)}, bf16[1024,256]{1,0:T(8,128)(2,1)S(1)}, u32[]{:S(2)}, u32[]{:S(2)}) collective-permute-start(bf16[1024,256]{1,0:T(8,128)(2,1)} %collective-permute-done.12.refs_11_), channel_id=1, source_target_pairs={{17,16}} | collective-permute-start | bytes 1572872 | tf_op jit(solution)/shard_map/ppermute | solution.py:235
  125.8 2.3 %copy-start.1 = (bf16[1024,256]{1,0:T(8,128)(2,1)S(1)}, bf16[1024,256]{1,0:T(8,128)(2,1)}, u32[]{:S(2)}) copy-start(bf16[1024,256]{1,0:T(8,128)(2,1)} %copy-done) | copy-start | bytes 1572868
  125.9 2.3 %copy-start.3 = (bf16[1024,256]{1,0:T(8,128)(2,1)S(1)}, bf16[1024,256]{1,0:T(8,128)(2,1)}, u32[]{:S(2)}) copy-start(bf16[1024,256]{1,0:T(8,128)(2,1)} %copy-done.2) | copy-start | bytes 1572868
  138.2 0.8 copy-start.6
  138.2 1.0 copy-start.7
  138.2 1.1 copy-start.8
  139.4 0.8 copy-start.9

commit v3 on v2

v3 whole, which is shorter than its diff:
```python
import functools
import itertools

import jax
import jax.numpy as jnp
import numpy as np
from jax import lax
from jax.experimental import pallas as pl
from jax.experimental.pallas import tpu as pltpu
from jax.sharding import PartitionSpec as P

STEPS = 4
HALVES = 2
DEPTH = 2
HOP = 2
COL_TILE = 512
ROW_TILE = 128
VMEM_LIMIT = 40 * 2**20


class Item:
    def __init__(self, row, half, s, place, home=None):
        self.row, self.half, self.s, self.place = row, half, s, place
        self.home = home


def line_slots(items, cut):
    ends, inner = {}, {}
    todo = sorted(items, key=lambda i: (i.home is None, i.half, i.place, i.s))
    slot = 1
    while todo:
        for item in todo:
            first = 1 + DEPTH * (item.place - 1) + (HOP if item.home is not None else 0)
            if first <= slot:
                ends[slot] = item
                if item.place > 1:
                    inner[slot] = item
                todo.remove(item)
                break
        slot += 1
    for item in sorted(cut, key=lambda i: (i.place, i.half, i.s)):
        slot = 1 + DEPTH * (item.place - 1)
        if item.place > 1:
            while slot in inner:
                slot += 1
            inner[slot] = item
    return ends, inner


class Lane:
    def __init__(self, rows, cols, groups_here, towards_zero):
        self.rows, self.cols = rows, cols
        self.towards_zero = towards_zero
        self.items = []
        for r in range(rows):
            mine = [
                Item(r, half, s, self.place((r + s) % rows // groups_here))
                for half in range(HALVES)
                for s in range(STEPS)
            ]
            self.items.append([i for i in mine if i.place > 0])
        self.away = []
        self.lines = [line_slots(items, []) for items in self.items]
        if rows % 2 == 0 and cols > 3:
            for r in range(rows // 2):
                self.balance(r, r + rows // 2)
                self.balance(r + rows // 2, r)
        self.rounds = max(
            [max(ends, default=0) for ends, _ in self.lines] + [max(inner, default=0) - DEPTH for _, inner in self.lines]
        )

    def place(self, c):
        return c if self.towards_zero else self.cols - 1 - c

    col = place

    def balance(self, r, other):
        if len(self.items[r]) < len(self.items[other]) or any(i.row == other for i in self.away):
            return
        places = sorted({i.place for i in self.items[r]})
        best = None
        for counts in itertools.product(range(HALVES + 1), repeat=len(places)):
            gone = []
            for place, count in zip(places, counts):
                here = [i for i in self.items[r] if i.place == place]
                here.sort(key=lambda i: (-i.half, -i.s))
                gone += here[:count]
            visitors = [Item(other, i.half, i.s, i.place, home=r) for i in gone]
            mine = line_slots([i for i in self.items[r] if i not in gone], gone)
            theirs = line_slots(self.items[other] + visitors, [])
            score = (
                max(max(mine[0], default=0), max(theirs[0], default=0)),
                abs(len(mine[0]) - len(theirs[0])),
                max([slot for slot, i in theirs[0].items() if i.home is not None], default=0),
                len(gone),
            )
            if best is None or score < best[0]:
                best = score, gone, mine, theirs
        _, gone, mine, theirs = best
        self.away += gone
        if gone:
            self.lines[r], self.lines[other] = mine, theirs

    def sent(self, r, c, t):
        p = self.place(c)
        ends, inner = self.lines[r]
        if p == 0:
            return None
        item = ends.get(t) if p == 1 else inner.get(t + DEPTH * (p - 1))
        return item if item is not None and item.place >= p else None

    def pairs(self, t):
        found = []
        for r in range(self.rows):
            for c in range(self.cols):
                if self.sent(r, c, t) is not None:
                    found.append((r * self.cols + c, r * self.cols + self.col(self.place(c) - 1)))
        return found

    def arrival(self, r, c, half, s):
        p = self.place(c)
        for i in self.items[r]:
            if (i.half, i.s) == (half, s) and i.place > p:
                if p == 0 and i in self.away:
                    for ends, _ in self.lines:
                        for slot, v in ends.items():
                            if v.home == r and (v.half, v.s) == (half, s):
                                return slot, True
                ends, inner = self.lines[r]
                for slot, v in (ends if p == 0 else inner).items():
                    if v is i:
                        return slot - DEPTH * p, False
        return None


def lookup(values, device):
    known = [v for v in values if v is not None]
    if len(set(known)) <= 1:
        return known[0] if known else 0
    values = [known[0] if v is None else v for v in values]
    result = jnp.uint32(0)
    place = (device % 32).astype(jnp.uint32)
    for bit in range(max(values).bit_length()):
        ones = [v >> bit & 1 for v in values]
        words = [sum(b << i for i, b in enumerate(ones[at : at + 32])) for at in range(0, len(ones), 32)]
        word = jnp.uint32(words[0])
        for i, other in enumerate(words[1:], 1):
            word = jnp.where(device // 32 == i, jnp.uint32(other), word)
        result = result | (((word >> place) & jnp.uint32(1)) << jnp.uint32(bit))
    return result.astype(jnp.int32)


def product_kernel(half, candidates, scale, n_buffers, places, *refs):
    x, buffers = refs[0], refs[1 : 1 + n_buffers]
    factor, twice, male = refs[1 + n_buffers : 4 + n_buffers]
    zy = refs[4 + n_buffers : 4 + n_buffers + STEPS]
    out, raw, zx, sems = refs[-4:]
    half_rows = raw.shape[0]
    width = raw.shape[1] // STEPS

    @pl.when(pl.program_id(0) == 0)
    def _():
        for s in range(STEPS):
            place = places[s]
            target = raw.at[:, pl.ds(s * width, width)]
            for number in candidates[s]:
                if number >= 0:

                    @pl.when(place == number)
                    def _(number=number, target=target, s=s):
                        pltpu.make_async_copy(buffers[number], target, sems.at[s]).start()

                else:

                    @pl.when(place < 0)
                    def _(place=place, target=target, s=s):
                        col = pl.multiple_of((-1 - place) * width, width)
                        mine = x.at[pl.ds(half * half_rows, half_rows), pl.ds(col, width)]
                        pltpu.make_async_copy(mine, target, sems.at[s]).start()

        for s in range(STEPS):
            columns = pl.ds(s * width, width)
            part = raw.at[:, columns]
            pltpu.make_async_copy(part, part, sems.at[s]).wait()

            @pl.loop(0, half_rows // ROW_TILE)
            def _(i, columns=columns):
                rows = pl.ds(pl.multiple_of(i * ROW_TILE, ROW_TILE), ROW_TILE)
                value = raw[rows, columns].astype(jnp.float32) - twice[:, columns]
                zx[rows, columns] = (value * factor[:, columns] * male[rows, :]).astype(zx.dtype)

    right = jnp.concatenate([block[...] for block in zy], axis=0)
    total = jnp.dot(zx[...], right, preferred_element_type=jnp.float32)
    out[...] = (total * scale).astype(out.dtype)


def product(half, places, candidates, x, buffers, factor, twice, male, zy, before):
    rows, n = x.shape[0], zy[0].shape[1]
    half_rows = rows // HALVES
    group_size = zy[0].shape[0]
    depth = group_size * STEPS
    scale = float(1.0 / np.sqrt(np.float32(depth)))
    whole = lambda j, places: (0, 0)
    specs = [pl.BlockSpec(memory_space=pl.ANY)] * (1 + len(buffers)) + [
        pl.BlockSpec((1, depth), whole),
        pl.BlockSpec((1, depth), whole),
        pl.BlockSpec((half_rows, 1), lambda j, places: (half, 0)),
    ]
    specs += [pl.BlockSpec((group_size, COL_TILE), lambda j, places: (0, j))] * STEPS
    args = [places, x, *buffers, factor, twice, male, *zy]
    aliases = {}
    if before is not None:
        aliases = {len(args): 0}
        specs.append(pl.BlockSpec(memory_space=pl.ANY))
        args.append(before)
    return pl.pallas_call(
        functools.partial(product_kernel, half, candidates, scale, len(buffers)),
        out_shape=jax.ShapeDtypeStruct((rows, n), jnp.bfloat16),
        grid_spec=pltpu.PrefetchScalarGridSpec(
            num_scalar_prefetch=1,
            grid=(n // COL_TILE,),
            in_specs=specs,
            out_specs=pl.BlockSpec((half_rows, COL_TILE), lambda j, places: (half, j)),
            scratch_shapes=[
                pltpu.VMEM((half_rows, depth), jnp.bfloat16),
                pltpu.VMEM((half_rows, depth), jnp.bfloat16),
                pltpu.SemaphoreType.DMA((STEPS,)),
            ],
        ),
        input_output_aliases=aliases,
        compiler_params=pltpu.CompilerParams(vmem_limit_bytes=VMEM_LIMIT),
        cost_estimate=pl.CostEstimate(
            flops=2 * half_rows * depth * n,
            bytes_accessed=2 * (half_rows * depth + depth * n + half_rows * n),
            transcendentals=0,
        ),
        name="product",
    )(*args)


def col_sum(value, cols):
    if cols & (cols - 1):
        return lax.psum(value, "col")
    bit = 1
    while bit < cols:
        value = value + lax.ppermute(value, "col", [(i, i ^ bit) for i in range(cols)])
        bit *= 2
    return value


def local(rows, cols, x, y, freq, weight, sex_rows, sex_cols):
    group_size = y.shape[0]
    local_vars = x.shape[1]
    groups_here = local_vars // group_size
    half_rows = x.shape[0] // HALVES
    lanes = [Lane(rows, cols, groups_here, towards) for towards in (True, False)]
    devices = [(r, c) for r in range(rows) for c in range(cols)]
    both = ("row", "col")

    row_place = lax.axis_index("row")
    col_place = lax.axis_index("col")
    device = row_place * cols + col_place

    def local_group(item):
        return ((item.row if item.home is None else item.home) + item.s) % rows % groups_here

    def own_chunk(x, items):
        half = lookup([None if i is None else i.half for i in items], device)
        group = lookup([None if i is None else local_group(i) for i in items], device)
        return lax.dynamic_slice(x, (half * half_rows, group * group_size), (half_rows, group_size))

    crossings = []
    crossing_of = {}
    for d, lane in enumerate(lanes):
        for r in range(rows):
            for item in lane.lines[r][0].values():
                if item.home is None:
                    continue
                source = (item.home, lane.col(item.place))
                target = (r, lane.col(item.place))
                for number, crossing in enumerate(crossings):
                    if source not in crossing and target not in [to for to, _ in crossing.values()]:
                        break
                else:
                    number = len(crossings)
                    crossings.append({})
                crossings[number][source] = (target, item)
                crossing_of[d, r, item.half, item.s] = number

    def number(rc):
        return rc[0] * cols + rc[1]

    buffers = {}
    crossed = {}
    window = [y]
    back = [(i, (i - 1) % rows) for i in range(rows)]
    last = max(lane.rounds for lane in lanes)
    for t in range(1, last + 1):
        for d, lane in enumerate(lanes):
            pairs = lane.pairs(t)
            if not pairs:
                continue
            sent = [lane.sent(r, c, t) for r, c in devices]
            own = [i if i is not None and i.place == lane.place(c) else None for i, (r, c) in zip(sent, devices)]
            home = [i if i is not None and i.home is None else None for i in own]
            visits = [
                None if i is None or i.home is None else crossing_of[d, r, i.half, i.s]
                for i, (r, c) in zip(own, devices)
            ]
            forwards = any(i is not None and o is None for i, o in zip(sent, own))
            sources = [(None, buffers[d, t - DEPTH])] if forwards else []
            for visit in sorted({v for v in visits if v is not None}):
                sources.append(([v == visit for v in visits], crossed[visit]))
            held = None
            if any(home):
                tied = lax.optimization_barrier((x, *[b for _, b in sources]))
                sources = [(mask, b) for (mask, _), b in zip(sources, tied[1:])]
                held = own_chunk(tied[0], home)
            for mask, buffer in sources[::-1]:
                if held is None:
                    held = buffer
                elif mask is not None:
                    held = jnp.where(lookup([int(m) for m in mask], device) == 1, buffer, held)
                else:
                    kept = [
                        None if i is None else int(i.place != lane.place(c)) for i, (r, c) in zip(sent, devices)
                    ]
                    held = jnp.where(lookup(kept, device) == 1, buffer, held)
            if t in (4, 6, 7) and d == 0 and len(window) < STEPS:
                held, window[-1] = lax.optimization_barrier((held, window[-1]))
            buffers[d, t] = lax.ppermute(held, both, pairs)
        if t == 1:
            for crossing in crossings:
                own = [crossing[rc][1] if rc in crossing else None for rc in devices]
                held = own_chunk(lax.optimization_barrier(x), own)
                pairs = [(number(rc), number(to)) for rc, (to, _) in crossing.items()]
                crossed[crossings.index(crossing)] = lax.ppermute(held, both, pairs)
        if t in (1, 4, 6, 7) and len(window) < STEPS:
            window.append(lax.ppermute(window[-1], "row", back))
        pairs, by_lane = [], []
        for d, lane in enumerate(lanes):
            for r in range(rows):
                item = lane.lines[r][0].get(t)
                if item is not None and item.home is not None:
                    end = lane.col(0)
                    pairs.append((number((r, end)), number((item.home, end))))
                    by_lane.append(d)
        if pairs:
            if len(set(by_lane)) == 1:
                held = buffers[by_lane[0], t]
            else:
                held = jnp.where(col_place == lanes[0].col(0), buffers[0, t], buffers[1, t])
            buffers["back", t] = lax.ppermute(held, both, pairs)
    while len(window) < STEPS:
        window.append(lax.ppermute(window[-1], "row", back))

    factor = weight / jnp.sqrt(2.0 * freq * (1.0 - freq))
    span = STEPS * group_size

    def in_window(value):
        return lax.dynamic_slice(jnp.concatenate([value, value]), (row_place * group_size,), (span,))

    window_factor = in_window(factor)
    window_twice = in_window(2.0 * freq)
    male_scale = np.float32(np.sqrt(0.5))
    male_rows = jnp.where(sex_rows > 0, male_scale, np.float32(1.0))[:, None]
    male_cols = jnp.where(sex_cols > 0, male_scale, np.float32(1.0))[None, :]
    zy = []
    for s, block in enumerate(window):
        part = slice(s * group_size, (s + 1) * group_size)
        value = block.astype(jnp.float32) - window_twice[part, None]
        zy.append((value * window_factor[part, None] * male_cols).astype(jnp.bfloat16))

    here = lambda value: lax.dynamic_slice(value, (col_place * local_vars,), (local_vars,))[None, :]
    zx = ((x.astype(jnp.float32) - here(2.0 * freq)) * here(factor) * male_rows).astype(jnp.bfloat16)
    squares = col_sum(jnp.sum(jnp.square(zx.astype(jnp.float32)), axis=1), cols)
    inbreeding = squares / jnp.float32(freq.shape[0]) - 1.0

    relation = None
    for half in range(HALVES):
        found = []
        for r, c in devices:
            keys = []
            for s in range(STEPS):
                key = -1 - (r + s) % rows % groups_here
                for d, lane in enumerate(lanes):
                    arrival = lane.arrival(r, c, half, s)
                    if arrival is not None:
                        key = ("back" if arrival[1] else d, arrival[0])
                keys.append(key)
            found.append(keys)
        used = sorted({k for keys in found for k in keys if isinstance(k, tuple)}, key=lambda k: (k[1], str(k[0])))
        found = np.asarray([[k if isinstance(k, int) else used.index(k) for k in keys] for keys in found], np.int32)
        candidates = [sorted({max(int(k), -1) for k in found[:, s]}) for s in range(STEPS)]
        relation = product(
            half,
            lax.dynamic_slice(jnp.asarray(found), (device, 0), (1, STEPS))[0],
            candidates,
            x,
            [buffers[key] for key in used],
            window_factor[None, :],
            window_twice[None, :],
            male_rows,
            zy,
            relation,
        )
    return relation, inbreeding


def solution(mesh):
    rows, cols = mesh.shape["row"], mesh.shape["col"]
    return jax.shard_map(
        functools.partial(local, rows, cols),
        mesh=mesh,
        in_specs=(P("row", "col"), P("row", "col"), P(), P(), P("row"), P("col")),
        out_specs=(P("row", "col"), P("row")),
        check_vma=False,
    )
```

time: 152 us -> 148 us (0.974)
  the two profiles are of different devices: /device:TPU:12 before, /device:TPU:3 now
where the time goes in v3:
time: 148 us; the launch traced here: 147 us
  waiting for transfers between devices  70.5 us (48%)
  starting transfers between devices  40 us (27%)
  Pallas kernels  22 us (15%)
  other arithmetic  10 us (7%)
  local copies, waits for them, and re-layouts  3.62 us (2%)
    ppermute x16, waiting for transfers between devices, local(): buffers[d, t] = lax.ppermute(held, both, pairs)  44.7 us
    pallas_call x2, Pallas kernels, product(): pl.pallas_call(functools.partial(product_kernel, half, candidates, scale,...  22 us
    ppermute x16, starting transfers between devices, local(): buffers[d, t] = lax.ppermute(held, both, pairs)  16.4 us
    ppermute x5, waiting for transfers between devices, local(): buffers['back', t] = lax.ppermute(held, both, pairs)  15.3 us
    ppermute x2, waiting for transfers between devices, col_sum(): lax.ppermute(value, 'col', [(i, i ^ bit) for i in range(cols)])  10.4 us
    ppermute x2, starting transfers between devices, col_sum(): lax.ppermute(value, 'col', [(i, i ^ bit) for i in range(cols)])  8.95 us
    ppermute x3, starting transfers between devices, local(): window.append(lax.ppermute(window[-1], 'row', back))  8.14 us
    ppermute x5, starting transfers between devices, local(): buffers['back', t] = lax.ppermute(held, both, pairs)  4.63 us
  transfers between devices with their start and end apart: 28, of which 9 were waited for; matrix products, arithmetic and copies ran while one was open for 6% of the time, Pallas kernels for 7%

profile of v3, /device:TPU:3, one launch (start us, length us, event | category | flops | bytes accessed | tf_op | source)
XLA Modules:
  0.0 147.4 jit_solution(12491253681194380188)
XLA Ops:
  0.6 0.8 compare_select_fusion.1
  1.5 0.7 broadcast_multiply_fusion
  2.2 0.1 dynamic_slice.86
  2.3 0.1 dynamic_slice.87
  2.4 2.5 %multiply_reduce_fusion = f32[2048]{0:T(1024)S(1)} fusion(bf16[2048,512]{1,0:T(8,128)(2,1)} %refs_0_.3, f32[2048]{0:T(1024)S(1)} %compare_select_fusion.1, f32[512]{0:T(512)S(1)} %dynamic_slice.87, f32[512]{0:T(512)S(1)} %dynamic_slice.86), kind=kLoop, calls=%fused_computation | loop fusion | flops 8386560 | bytes 2117632 | tf_op jit(solution)/shard_map/reduce_sum | solution.py:376
  4.9 1.4 collective-permute-start.26
  6.3 1.0 collective-permute-start.9
  7.2 1.7 %fusion.4 = (bf16[1024,256]{1,0:T(8,128)(2,1)}, bf16[1024,256]{1,0:T(8,128)(2,1)}, bf16[1024,256]{1,0:T(8,128)(2,1)}, bf16[1024,256]{1,0:T(8,128)(2,1)}, bf16[10...) fusion(bf16[2048,512]{1,0:T(8,128)(2,1)S(1)} %copy-done, s32[]{:T(128)S(6)} %select_n.236, s32[]{:T(128)S(6)} %select_n.230, ...), kind=kLoop, calls=%fused_computation.39 | loop fusion | bytes 6291480 | tf_op jit(solution)/shard_map/dynamic_slice | solution.py:270
  8.9 1.4 collective-permute-start.5
  10.4 1.3 collective-permute-start.3
  11.6 1.3 collective-permute-start.2
  13.0 0.1 fusion
  13.1 0.7 fusion.3.places
  13.8 7.6 %collective-permute-start.27 = (f32[2048]{0:T(1024)S(1)}, f32[2048]{0:T(1024)S(1)}, u32[]{:S(2)}, u32[]{:S(2)}) collective-permute-start(f32[2048]{0:T(1024)S(1)} %add.106), channel_id=1, source_target_pairs={{0,2},{1,3},{2,0},{3,1},{4,6},{5,7},{6,4},{7,5},{8,10},{9,11},{10,... | collective-permute-start | bytes 24584 | tf_op jit(solution)/shard_map/ppermute | solution.py:246
  21.4 0.7 fusion.2.places
  22.1 0.4 copy.12.refs_15_.refs_22_
  22.4 10.4 %collective-permute-done.27 = f32[2048]{0:T(1024)S(1)} collective-permute-done((f32[2048]{0:T(1024)S(1)}, f32[2048]{0:T(1024)S(1)}, u32[]{:S(2)}, u32[]{:S(2)}) %collective-permute-start.27) | collective-permute-done | bytes 8224 | tf_op jit(solution)/shard_map/ppermute | solution.py:246
  32.9 0.7 collective-permute-start.8
  33.5 0.6 multiply_add_fusion
  34.2 0.7 collective-permute-start.1
  34.9 0.7 collective-permute-start
  35.6 1.2 select_select_fusion.2
  36.8 1.3 collective-permute-start.6
  38.2 0.2 select_select_fusion.3
  38.4 1.3 collective-permute-start.4
  39.7 0.2 select_select_fusion
  39.9 0.7 collective-permute-start.11
  40.6 0.2 select_select_fusion.1
  40.8 3.4 %collective-permute-done.6.refs_6_.refs_4_ = bf16[1024,256]{1,0:T(8,128)(2,1)S(1)} collective-permute-done((bf16[1024,256]{1,0:T(8,128)(2,1)S(1)}, bf16[1024,256]{1,0:T(8,128)(2,1)S(1)}, u32[]{:S(2)}, u32[]{:S(2)}) %collective-permute-start.6) | collective-permute-done | bytes 524320 | tf_op jit(solution)/shard_map/ppermute | solution.py:331
  44.2 0.1 slice_select_fusion.2
  44.3 0.7 collective-permute-start.14
  45.0 9.3 %collective-permute-done.4.refs_5_.refs_3_ = bf16[1024,256]{1,0:T(8,128)(2,1)S(1)} collective-permute-done((bf16[1024,256]{1,0:T(8,128)(2,1)S(1)}, bf16[1024,256]{1,0:T(8,128)(2,1)S(1)}, u32[]{:S(2)}, u32[]{:S(2)}) %collective-permute-start.4) | collective-permute-done | bytes 524320 | tf_op jit(solution)/shard_map/ppermute | solution.py:331
  54.3 1.3 collective-permute-start.13
  55.7 3.5 %collective-permute-start.16 = (bf16[256,2048]{1,0:T(8,128)(2,1)}, bf16[256,2048]{1,0:T(8,128)(2,1)S(1)}, u32[]{:S(2)}, u32[]{:S(2)}) collective-permute-start(bf16[256,2048]{1,0:T(8,128)(2,1)} %collective-permute-done.9), channel_id=1, source_target_pairs={{0,28},{4,0},{8,4},{12,8},{16,12},{20,16},{24,20},{28,24},{1,29},{... | collective-permute-start | bytes 3145736 | tf_op jit(solution)/shard_map/ppermute | solution.py:339
  59.2 0.1 dynamic-slice_select_fusion
  59.3 0.7 collective-permute-start.18
  60.0 1.3 collective-permute-start.10
  61.3 0.1 broadcast_select_fusion.4
  61.4 0.1 slice_select_fusion
  61.4 0.7 collective-permute-start.21
  62.1 9.6 %collective-permute-done.13.refs_9_ = bf16[1024,256]{1,0:T(8,128)(2,1)S(1)} collective-permute-done((bf16[1024,256]{1,0:T(8,128)(2,1)S(1)}, bf16[1024,256]{1,0:T(8,128)(2,1)S(1)}, u32[]{:S(2)}, u32[]{:S(2)}) %collective-permute-start.13) | collective-permute-done | bytes 524320 | tf_op jit(solution)/shard_map/ppermute | solution.py:331
  71.8 1.3 collective-permute-start.20
  73.1 9.9 %collective-permute-done.10.refs_7_.refs_6_ = bf16[1024,256]{1,0:T(8,128)(2,1)S(1)} collective-permute-done((bf16[1024,256]{1,0:T(8,128)(2,1)S(1)}, bf16[1024,256]{1,0:T(8,128)(2,1)S(1)}, u32[]{:S(2)}, u32[]{:S(2)}) %collective-permute-start.10) | collective-permute-done | bytes 524320 | tf_op jit(solution)/shard_map/ppermute | solution.py:331
  83.0 0.1 dynamic-slice_select_fusion.1
  83.2 3.7 %collective-permute-start.25 = (bf16[256,2048]{1,0:T(8,128)(2,1)S(1)}, bf16[256,2048]{1,0:T(8,128)(2,1)S(1)}, u32[]{:S(2)}, u32[]{:S(2)}) collective-permute-start(bf16[256,2048]{1,0:T(8,128)(2,1)S(1)} %collective-permute-done.16), channel_id=1, source_target_pairs={{0,28},{4,0},{8,4},{12,8},{16,12},{20,16},{24,20},{28,24},{1,29},{... | collective-permute-start | bytes 3145736 | tf_op jit(solution)/shard_map/ppermute | solution.py:339
  86.8 0.1 broadcast_select_fusion.2
  86.9 1.4 collective-permute-start.17
  88.3 0.1 broadcast_select_fusion.3
  88.4 1.3 collective-permute-start.7
  89.7 0.2 collective-permute-done.20.refs_15_
  89.9 1.3 collective-permute-start.15
  91.2 0.1 broadcast_select_fusion
  91.3 0.7 collective-permute-start.12
  92.0 12.2 %collective-permute-done.17.refs_11_.refs_12_ = bf16[1024,256]{1,0:T(8,128)(2,1)S(1)} collective-permute-done((bf16[1024,256]{1,0:T(8,128)(2,1)S(1)}, bf16[1024,256]{1,0:T(8,128)(2,1)S(1)}, u32[]{:S(2)}, u32[]{:S(2)}) %collective-permute-start.17) | collective-permute-done | bytes 524320 | tf_op jit(solution)/shard_map/ppermute | solution.py:331
  104.2 0.7 collective-permute-start.24
  104.9 0.1 broadcast_select_fusion.1
  105.0 4.8 %collective-permute-done.7.refs_5_ = bf16[1024,256]{1,0:T(8,128)(2,1)S(1)} collective-permute-done((bf16[1024,256]{1,0:T(8,128)(2,1)S(1)}, bf16[1024,256]{1,0:T(8,128)(2,1)S(1)}, u32[]{:S(2)}, u32[]{:S(2)}) %collective-permute-start.7) | collective-permute-done | bytes 524320 | tf_op jit(solution)/shard_map/ppermute | solution.py:353
  109.8 0.7 collective-permute-start.22
  110.5 10.5 %collective-permute-done.15.refs_11_ = bf16[1024,256]{1,0:T(8,128)(2,1)S(1)} collective-permute-done((bf16[1024,256]{1,0:T(8,128)(2,1)S(1)}, bf16[1024,256]{1,0:T(8,128)(2,1)S(1)}, u32[]{:S(2)}, u32[]{:S(2)}) %collective-permute-start.15) | collective-permute-done | bytes 524320 | tf_op jit(solution)/shard_map/ppermute | solution.py:353
  121.0 0.7 collective-permute-start.19
  121.7 0.9 collective-permute-start.23
  122.6 2.6 %multiply_convert_fusion.1 = (bf16[256,2048]{1,0:T(8,128)(2,1)S(1)}, bf16[256,2048]{1,0:T(8,128)(2,1)S(1)}, bf16[256,2048]{1,0:T(8,128)(2,1)S(1)}, bf16[256,2048]{1,0:T(8,128)(2,1)S(1)}) fusion(bf16[256,2048]{1,0:T(8,128)(2,1)S(1)} %collective-permute-done.25, f32[256]{0:T(256)S(1)} %get-tuple-element.74, f32[256]{0:T(256)S(1)} %get-tuple-element.70, ...), kind=kLoop, calls=%fused_computation.2 | loop fusion | flops 10485760 | bytes 8404992 | tf_op jit(solution)/shard_map/convert_element_type | solution.py:372
  125.2 10.9 %product.2.refs_27_ = bf16[2048,2048]{1,0:T(8,128)(2,1)} custom-call(s32[4]{0:T(128)S(1)} %fusion.3.places, bf16[2048,512]{1,0:T(8,128)(2,1)S(1)} %copy-done, bf16[1024,256]{1,0:T(8,128)(2,1)} %collective-permute-done.2.refs_1_, bf16[1024,256]{1,0:T(8,128)(2,1)} %collective-permute-done.5.refs_2_, ...), custom_call_target="tpu_custom_call" | custom-call | flops 4294967296 | bytes 10485760 | tf_op jit(solution)/shard_map/product/pallas_call | solution.py:216
  136.1 11.2 %product.3 = bf16[2048,2048]{1,0:T(8,128)(2,1)} custom-call(s32[4]{0:T(128)S(1)} %fusion.2.places, bf16[2048,512]{1,0:T(8,128)(2,1)} %refs_0_.3, bf16[1024,256]{1,0:T(8,128)(2,1)S(1)} %collective-permute-done.refs_3_.refs_1_, bf16[1024,256]{1,0:T(8,128)(2,1)S(1)} %collective-permute-done.1.refs_4_.refs_2_, ...), custom_call_target="tpu_custom_call", output_to_operand_aliasing={{}: (28, {})} | custom-call | flops 4294967296 | bytes 10485760 | tf_op jit(solution)/shard_map/product/pallas_call | solution.py:216
  (33 shorter events, 0.2 us)
Async XLA Ops:
  0.6 6.6 %copy-start = (bf16[2048,512]{1,0:T(8,128)(2,1)S(1)}, bf16[2048,512]{1,0:T(8,128)(2,1)}, u32[]{:S(2)}) copy-start(bf16[2048,512]{1,0:T(8,128)(2,1)} %refs_0_.3) | copy-start | bytes 6291460
  4.9 8.9 %collective-permute-start.26 = (f32[2048]{0:T(1024)S(1)}, f32[2048]{0:T(1024)S(1)}, u32[]{:S(2)}, u32[]{:S(2)}) collective-permute-start(f32[2048]{0:T(1024)S(1)} %multiply_reduce_fusion), channel_id=1, source_target_pairs={{0,1},{1,0},{2,3},{3,2},{4,5},{5,4},{6,7},{7,6},{8,9},{9,8},{10,11... | collective-permute-start | bytes 24584 | tf_op jit(solution)/shard_map/ppermute | solution.py:246
  6.3 49.4 %collective-permute-start.9 = (bf16[256,2048]{1,0:T(8,128)(2,1)}, bf16[256,2048]{1,0:T(8,128)(2,1)}, u32[]{:S(2)}, u32[]{:S(2)}) collective-permute-start(bf16[256,2048]{1,0:T(8,128)(2,1)} %param.9), channel_id=1, source_target_pairs={{0,28},{4,0},{8,4},{12,8},{16,12},{20,16},{24,20},{28,24},{1,29},{... | collective-permute-start | bytes 3145736 | tf_op jit(solution)/shard_map/ppermute | solution.py:339
  7.2 5.7 %copy-start.3 = (s32[2048]{0:T(1024)S(1)}, s32[2048]{0:T(1024)}, u32[]{:S(2)}) copy-start(s32[2048]{0:T(1024)} %param.13) | copy-start | bytes 24580
  8.9 25.2 %collective-permute-start.5 = (bf16[1024,256]{1,0:T(8,128)(2,1)}, bf16[1024,256]{1,0:T(8,128)(2,1)}, u32[]{:S(2)}, u32[]{:S(2)}) collective-permute-start(bf16[1024,256]{1,0:T(8,128)(2,1)} %get-tuple-element.59), channel_id=1, source_target_pairs={{0,1},{1,2},{4,5},{5,6},{6,7},{9,10},{10,11},{13,14},{14,15},{18,1... | collective-permute-start | bytes 1572872 | tf_op jit(solution)/shard_map/ppermute | solution.py:331
  10.4 24.5 %collective-permute-start.3 = (bf16[1024,256]{1,0:T(8,128)(2,1)}, bf16[1024,256]{1,0:T(8,128)(2,1)}, u32[]{:S(2)}, u32[]{:S(2)}) collective-permute-start(bf16[1024,256]{1,0:T(8,128)(2,1)} %get-tuple-element.60), channel_id=1, source_target_pairs={{18,2},{19,3},{23,7},{9,25},{13,29},{14,30},{28,12},{1,17},{0,16},... | collective-permute-start | bytes 1572872 | tf_op jit(solution)/shard_map/ppermute | solution.py:337
  11.6 25.2 %collective-permute-start.2 = (bf16[1024,256]{1,0:T(8,128)(2,1)}, bf16[1024,256]{1,0:T(8,128)(2,1)}, u32[]{:S(2)}, u32[]{:S(2)}) collective-permute-start(bf16[1024,256]{1,0:T(8,128)(2,1)} %get-tuple-element.61), channel_id=1, source_target_pairs={{1,0},{5,4},{6,5},{9,8},{10,9},{13,12},{14,13},{15,14},{18,17},{19... | collective-permute-start | bytes 1572872 | tf_op jit(solution)/shard_map/ppermute | solution.py:331
  13.8 19.1 %collective-permute-start.27 = (f32[2048]{0:T(1024)S(1)}, f32[2048]{0:T(1024)S(1)}, u32[]{:S(2)}, u32[]{:S(2)}) collective-permute-start(f32[2048]{0:T(1024)S(1)} %add.106), channel_id=1, source_target_pairs={{0,2},{1,3},{2,0},{3,1},{4,6},{5,7},{6,4},{7,5},{8,10},{9,11},{10,... | collective-permute-start | bytes 24584 | tf_op jit(solution)/shard_map/ppermute | solution.py:246
  32.9 5.5 %collective-permute-start.8 = (bf16[1024,256]{1,0:T(8,128)(2,1)}, bf16[1024,256]{1,0:T(8,128)(2,1)S(1)}, u32[]{:S(2)}, u32[]{:S(2)}) collective-permute-start(bf16[1024,256]{1,0:T(8,128)(2,1)} %get-tuple-element.58), channel_id=1, source_target_pairs={{18,2},{9,25},{1,17},{10,26}} | collective-permute-start | bytes 1572872 | tf_op jit(solution)/shard_map/ppermute | solution.py:337
  34.2 5.5 %collective-permute-start.1 = (bf16[1024,256]{1,0:T(8,128)(2,1)}, bf16[1024,256]{1,0:T(8,128)(2,1)S(1)}, u32[]{:S(2)}, u32[]{:S(2)}) collective-permute-start(bf16[1024,256]{1,0:T(8,128)(2,1)} %get-tuple-element.62), channel_id=1, source_target_pairs={{0,1},{1,2},{5,6},{9,10},{10,11},{14,15},{18,19},{20,21},{22,23},{... | collective-permute-start | bytes 1572872 | tf_op jit(solution)/shard_map/ppermute | solution.py:331
  34.9 5.7 %collective-permute-start = (bf16[1024,256]{1,0:T(8,128)(2,1)}, bf16[1024,256]{1,0:T(8,128)(2,1)S(1)}, u32[]{:S(2)}, u32[]{:S(2)}) collective-permute-start(bf16[1024,256]{1,0:T(8,128)(2,1)} %get-tuple-element.63), channel_id=1, source_target_pairs={{1,0},{5,4},{9,8},{10,9},{14,13},{18,17},{19,18},{22,21},{23,22},{... | collective-permute-start | bytes 1572872 | tf_op jit(solution)/shard_map/ppermute | solution.py:331
  36.8 7.4 %collective-permute-start.6 = (bf16[1024,256]{1,0:T(8,128)(2,1)S(1)}, bf16[1024,256]{1,0:T(8,128)(2,1)S(1)}, u32[]{:S(2)}, u32[]{:S(2)}) collective-permute-start(bf16[1024,256]{1,0:T(8,128)(2,1)S(1)} %select_select_fusion.2), channel_id=1, source_target_pairs={{0,1},{1,2},{2,3},{4,5},{5,6},{6,7},{9,10},{10,11},{12,13},{14,15}... | collective-permute-start | bytes 1572872 | tf_op jit(solution)/shard_map/ppermute | solution.py:331
  38.4 15.9 %collective-permute-start.4 = (bf16[1024,256]{1,0:T(8,128)(2,1)S(1)}, bf16[1024,256]{1,0:T(8,128)(2,1)S(1)}, u32[]{:S(2)}, u32[]{:S(2)}) collective-permute-start(bf16[1024,256]{1,0:T(8,128)(2,1)S(1)} %select_select_fusion.3), channel_id=1, source_target_pairs={{1,0},{2,1},{3,2},{5,4},{7,6},{9,8},{10,9},{13,12},{14,13},{15,14}... | collective-permute-start | bytes 1572872 | tf_op jit(solution)/shard_map/ppermute | solution.py:331
  39.9 15.7 %collective-permute-start.11 = (bf16[1024,256]{1,0:T(8,128)(2,1)S(1)}, bf16[1024,256]{1,0:T(8,128)(2,1)S(1)}, u32[]{:S(2)}, u32[]{:S(2)}) collective-permute-start(bf16[1024,256]{1,0:T(8,128)(2,1)S(1)} %select_select_fusion), channel_id=1, source_target_pairs={{1,2},{2,3},{5,6},{6,7},{9,10},{10,11},{13,14},{14,15},{17,18},{18... | collective-permute-start | bytes 1572872 | tf_op jit(solution)/shard_map/ppermute | solution.py:331
  44.3 17.1 %collective-permute-start.14 = (bf16[1024,256]{1,0:T(8,128)(2,1)S(1)}, bf16[1024,256]{1,0:T(8,128)(2,1)S(1)}, u32[]{:S(2)}, u32[]{:S(2)}) collective-permute-start(bf16[1024,256]{1,0:T(8,128)(2,1)S(1)} %slice_select_fusion.2), channel_id=1, source_target_pairs={{1,2},{2,3},{5,6},{6,7},{10,11},{13,14},{14,15},{17,18},{18,19},{2... | collective-permute-start | bytes 1572872 | tf_op jit(solution)/shard_map/ppermute | solution.py:331
  54.3 17.4 %collective-permute-start.13 = (bf16[1024,256]{1,0:T(8,128)(2,1)S(1)}, bf16[1024,256]{1,0:T(8,128)(2,1)S(1)}, u32[]{:S(2)}, u32[]{:S(2)}) collective-permute-start(bf16[1024,256]{1,0:T(8,128)(2,1)S(1)} %slice_select_fusion.3), channel_id=1, source_target_pairs={{1,0},{2,1},{5,4},{6,5},{9,8},{13,12},{14,13},{17,16},{18,17},{21,... | collective-permute-start | bytes 1572872 | tf_op jit(solution)/shard_map/ppermute | solution.py:331
  55.7 27.5 %collective-permute-start.16 = (bf16[256,2048]{1,0:T(8,128)(2,1)}, bf16[256,2048]{1,0:T(8,128)(2,1)S(1)}, u32[]{:S(2)}, u32[]{:S(2)}) collective-permute-start(bf16[256,2048]{1,0:T(8,128)(2,1)} %collective-permute-done.9), channel_id=1, source_target_pairs={{0,28},{4,0},{8,4},{12,8},{16,12},{20,16},{24,20},{28,24},{1,29},{... | collective-permute-start | bytes 3145736 | tf_op jit(solution)/shard_map/ppermute | solution.py:339
  59.3 32.0 %collective-permute-start.18 = (bf16[1024,256]{1,0:T(8,128)(2,1)S(1)}, bf16[1024,256]{1,0:T(8,128)(2,1)S(1)}, u32[]{:S(2)}, u32[]{:S(2)}) collective-permute-start(bf16[1024,256]{1,0:T(8,128)(2,1)S(1)} %dynamic-slice_select_fusion), channel_id=1, source_target_pairs={{0,1},{1,2},{2,3},{5,6},{6,7},{10,11},{14,15},{18,19},{22,23},{25,... | collective-permute-start | bytes 1572872 | tf_op jit(solution)/shard_map/ppermute | solution.py:331
  60.0 23.0 %collective-permute-start.10 = (bf16[1024,256]{1,0:T(8,128)(2,1)S(1)}, bf16[1024,256]{1,0:T(8,128)(2,1)S(1)}, u32[]{:S(2)}, u32[]{:S(2)}) collective-permute-start(bf16[1024,256]{1,0:T(8,128)(2,1)S(1)} %select_select_fusion.1), channel_id=1, source_target_pairs={{1,0},{2,1},{5,4},{6,5},{9,8},{10,9},{13,12},{14,13},{17,16},{18,1... | collective-permute-start | bytes 1572872 | tf_op jit(solution)/shard_map/ppermute | solution.py:331
  61.4 27.0 %collective-permute-start.21 = (bf16[1024,256]{1,0:T(8,128)(2,1)S(1)}, bf16[1024,256]{1,0:T(8,128)(2,1)S(1)}, u32[]{:S(2)}, u32[]{:S(2)}) collective-permute-start(bf16[1024,256]{1,0:T(8,128)(2,1)S(1)} %slice_select_fusion), channel_id=1, source_target_pairs={{1,2},{2,3},{6,7},{14,15},{18,19},{22,23},{26,27},{30,31}} | collective-permute-start | bytes 1572872 | tf_op jit(solution)/shard_map/ppermute | solution.py:331
  71.8 18.1 %collective-permute-start.20 = (bf16[1024,256]{1,0:T(8,128)(2,1)S(1)}, bf16[1024,256]{1,0:T(8,128)(2,1)S(1)}, u32[]{:S(2)}, u32[]{:S(2)}) collective-permute-start(bf16[1024,256]{1,0:T(8,128)(2,1)S(1)} %slice_select_fusion.1), channel_id=1, source_target_pairs={{1,0},{5,4},{13,12},{17,16},{18,17},{21,20},{25,24},{29,28}} | collective-permute-start | bytes 1572872 | tf_op jit(solution)/shard_map/ppermute | solution.py:331
  83.2 38.5 %collective-permute-start.25 = (bf16[256,2048]{1,0:T(8,128)(2,1)S(1)}, bf16[256,2048]{1,0:T(8,128)(2,1)S(1)}, u32[]{:S(2)}, u32[]{:S(2)}) collective-permute-start(bf16[256,2048]{1,0:T(8,128)(2,1)S(1)} %collective-permute-done.16), channel_id=1, source_target_pairs={{0,28},{4,0},{8,4},{12,8},{16,12},{20,16},{24,20},{28,24},{1,29},{... | collective-permute-start | bytes 3145736 | tf_op jit(solution)/shard_map/ppermute | solution.py:339
  86.9 35.7 %copy-start.2 = (bf16[256,2048]{1,0:T(8,128)(2,1)S(1)}, bf16[256,2048]{1,0:T(8,128)(2,1)}, u32[]{:S(2)}) copy-start(bf16[256,2048]{1,0:T(8,128)(2,1)} %param.9) | copy-start | bytes 3145732
  86.9 17.3 %collective-permute-start.17 = (bf16[1024,256]{1,0:T(8,128)(2,1)S(1)}, bf16[1024,256]{1,0:T(8,128)(2,1)S(1)}, u32[]{:S(2)}, u32[]{:S(2)}) collective-permute-start(bf16[1024,256]{1,0:T(8,128)(2,1)S(1)} %dynamic-slice_select_fusion.1), channel_id=1, source_target_pairs={{1,0},{5,4},{9,8},{13,12},{14,13},{17,16},{18,17},{19,18},{21,20},... | collective-permute-start | bytes 1572872 | tf_op jit(solution)/shard_map/ppermute | solution.py:331
  88.4 21.3 %collective-permute-start.7 = (bf16[1024,256]{1,0:T(8,128)(2,1)S(1)}, bf16[1024,256]{1,0:T(8,128)(2,1)S(1)}, u32[]{:S(2)}, u32[]{:S(2)}) collective-permute-start(bf16[1024,256]{1,0:T(8,128)(2,1)S(1)} %broadcast_select_fusion.4), channel_id=1, source_target_pairs={{24,8},{28,12},{23,7},{27,11}} | collective-permute-start | bytes 1572872 | tf_op jit(solution)/shard_map/ppermute | solution.py:353
  89.9 31.1 %collective-permute-start.15 = (bf16[1024,256]{1,0:T(8,128)(2,1)S(1)}, bf16[1024,256]{1,0:T(8,128)(2,1)S(1)}, u32[]{:S(2)}, u32[]{:S(2)}) collective-permute-start(bf16[1024,256]{1,0:T(8,128)(2,1)S(1)} %broadcast_select_fusion.2), channel_id=1, source_target_pairs={{0,16},{28,12},{19,3},{23,7}} | collective-permute-start | bytes 1572872 | tf_op jit(solution)/shard_map/ppermute | solution.py:353
  91.3 44.7 %collective-permute-start.12 = (bf16[1024,256]{1,0:T(8,128)(2,1)S(1)}, bf16[1024,256]{1,0:T(8,128)(2,1)S(1)}, u32[]{:S(2)}, u32[]{:S(2)}) collective-permute-start(bf16[1024,256]{1,0:T(8,128)(2,1)S(1)} %broadcast_select_fusion.3), channel_id=1, source_target_pairs={{24,8},{27,11}} | collective-permute-start | bytes 1572872 | tf_op jit(solution)/shard_map/ppermute | solution.py:353
  104.2 31.8 %collective-permute-start.24 = (bf16[1024,256]{1,0:T(8,128)(2,1)S(1)}, bf16[1024,256]{1,0:T(8,128)(2,1)S(1)}, u32[]{:S(2)}, u32[]{:S(2)}) collective-permute-start(bf16[1024,256]{1,0:T(8,128)(2,1)S(1)} %collective-permute-done.18.refs_12_.refs_13_), channel_id=1, source_target_pairs={{1,2},{26,27}} | collective-permute-start | bytes 1572872 | tf_op jit(solution)/shard_map/ppermute | solution.py:331
  109.8 26.3 %collective-permute-start.22 = (bf16[1024,256]{1,0:T(8,128)(2,1)S(1)}, bf16[1024,256]{1,0:T(8,128)(2,1)S(1)}, u32[]{:S(2)}, u32[]{:S(2)}) collective-permute-start(bf16[1024,256]{1,0:T(8,128)(2,1)S(1)} %broadcast_select_fusion), channel_id=1, source_target_pairs={{0,16},{4,20},{15,31},{19,3}} | collective-permute-start | bytes 1572872 | tf_op jit(solution)/shard_map/ppermute | solution.py:353
  121.0 15.1 %collective-permute-start.19 = (bf16[1024,256]{1,0:T(8,128)(2,1)S(1)}, bf16[1024,256]{1,0:T(8,128)(2,1)S(1)}, u32[]{:S(2)}, u32[]{:S(2)}) collective-permute-start(bf16[1024,256]{1,0:T(8,128)(2,1)S(1)} %broadcast_select_fusion.1), channel_id=1, source_target_pairs={{0,16},{19,3}} | collective-permute-start | bytes 1572872 | tf_op jit(solution)/shard_map/ppermute | solution.py:353
  121.7 14.4 %collective-permute-start.23 = (bf16[1024,256]{1,0:T(8,128)(2,1)S(1)}, bf16[1024,256]{1,0:T(8,128)(2,1)S(1)}, u32[]{:S(2)}, u32[]{:S(2)}) collective-permute-start(bf16[1024,256]{1,0:T(8,128)(2,1)S(1)} %collective-permute-done.17.refs_11_.refs_12_), channel_id=1, source_target_pairs={{18,17},{25,24}} | collective-permute-start | bytes 1572872 | tf_op jit(solution)/shard_map/ppermute | solution.py:331
  125.2 10.9 %copy-start.1 = (bf16[256,2048]{1,0:T(8,128)(2,1)}, bf16[256,2048]{1,0:T(8,128)(2,1)S(1)}, u32[]{:S(2)}) copy-start(bf16[256,2048]{1,0:T(8,128)(2,1)S(1)} %get-tuple-element.64.refs_19_.refs_26_) | copy-start | bytes 3145732

commit v4 on v3

v4 whole, which is shorter than its diff:
```python
import functools
import itertools

import jax
import jax.numpy as jnp
import numpy as np
from jax import lax
from jax.experimental import pallas as pl
from jax.experimental.pallas import tpu as pltpu
from jax.sharding import PartitionSpec as P

STEPS = 4
PIECES = 4
PARTS = ((0, 2), (2, 3), (3, 4))
DEPTH = 1
HOP = 2
COL_TILE = 512
ROW_TILE = 32
VMEM_LIMIT = 40 * 2**20


class Item:
    def __init__(self, row, blocks, place, home=None):
        self.row, self.blocks, self.place = row, blocks, place
        self.home = home

    @property
    def owner(self):
        return self.row if self.home is None else self.home


def items_of(row, steps, place):
    items = []
    for a, b in zip(steps[::2], steps[1::2]):
        items += [Item(row, ((q, a), (q, b)), place) for q in range(PIECES)]
    if len(steps) % 2:
        items += [Item(row, ((q, steps[-1]), (q + 1, steps[-1])), place) for q in range(0, PIECES, 2)]
    return items


def line_slots(items, cut):
    ends, inner = {}, {}
    todo = sorted(items, key=lambda i: (i.home is None, i.blocks[0][0], i.place, i.blocks))
    slot = 1
    while todo:
        for item in todo:
            first = 1 + DEPTH * (item.place - 1) + (HOP if item.home is not None else 0)
            if first <= slot:
                ends[slot] = item
                if item.place > 1:
                    inner[slot] = item
                todo.remove(item)
                break
        slot += 1
    for item in sorted(cut, key=lambda i: (i.place, i.blocks)):
        slot = 1 + DEPTH * (item.place - 1)
        if item.place > 1:
            while slot in inner:
                slot += 1
            inner[slot] = item
    return ends, inner


class Lane:
    def __init__(self, rows, cols, groups_here, towards_zero):
        self.rows, self.cols = rows, cols
        self.towards_zero = towards_zero
        self.items = []
        for r in range(rows):
            steps_at = {}
            for s in range(STEPS):
                steps_at.setdefault(self.place((r + s) % rows // groups_here), []).append(s)
            mine = [i for place, steps in steps_at.items() for i in items_of(r, steps, place)]
            self.items.append([i for i in mine if i.place > 0])
        self.away = []
        self.lines = [line_slots(items, []) for items in self.items]
        if rows % 2 == 0 and cols > 3:
            for r in range(rows // 2):
                self.balance(r, r + rows // 2)
                self.balance(r + rows // 2, r)
        self.rounds = max(
            [max(ends, default=0) for ends, _ in self.lines] + [max(inner, default=0) - DEPTH for _, inner in self.lines]
        )

    def place(self, c):
        return c if self.towards_zero else self.cols - 1 - c

    col = place

    def balance(self, r, other):
        if len(self.items[r]) < len(self.items[other]) or any(i.row == other for i in self.away):
            return
        places = sorted({i.place for i in self.items[r]})
        best = None
        for counts in itertools.product(range(3), repeat=len(places)):
            gone = []
            for place, count in zip(places, counts):
                here = [i for i in self.items[r] if i.place == place]
                here.sort(key=lambda i: i.blocks, reverse=True)
                gone += here[:count]
            visitors = [Item(other, i.blocks, i.place, home=r) for i in gone]
            mine = line_slots([i for i in self.items[r] if i not in gone], gone)
            theirs = line_slots(self.items[other] + visitors, [])
            score = (
                max(max(mine[0], default=0), max(theirs[0], default=0)),
                abs(len(mine[0]) - len(theirs[0])),
                max([slot for slot, i in theirs[0].items() if i.home is not None], default=0),
                len(gone),
            )
            if best is None or score < best[0]:
                best = score, gone, mine, theirs
        _, gone, mine, theirs = best
        self.away += gone
        if gone:
            self.lines[r], self.lines[other] = mine, theirs

    def sent(self, r, c, t):
        p = self.place(c)
        ends, inner = self.lines[r]
        if p == 0:
            return None
        item = ends.get(t) if p == 1 else inner.get(t + DEPTH * (p - 1))
        return item if item is not None and item.place >= p else None

    def pairs(self, t):
        found = []
        for r in range(self.rows):
            for c in range(self.cols):
                if self.sent(r, c, t) is not None:
                    found.append((r * self.cols + c, r * self.cols + self.col(self.place(c) - 1)))
        return found

    def arrival(self, r, c, block):
        p = self.place(c)
        for i in self.items[r]:
            if block not in i.blocks or i.place <= p:
                continue
            sub = i.blocks.index(block)
            ends, inner = self.lines[r]
            if p == 0 and i in self.away:
                for other, _ in self.lines:
                    for slot, v in other.items():
                        if v.home == r and v.blocks == i.blocks:
                            return slot, True, sub
            for slot, v in (ends if p == 0 else inner).items():
                if v is i:
                    return slot - DEPTH * p, False, sub
        return None


def lookup(values, device):
    known = [v for v in values if v is not None]
    if len(set(known)) <= 1:
        return known[0] if known else 0
    values = [known[0] if v is None else v for v in values]
    result = jnp.uint32(0)
    place = (device % 32).astype(jnp.uint32)
    for bit in range(max(values).bit_length()):
        ones = [v >> bit & 1 for v in values]
        words = [sum(b << i for i, b in enumerate(ones[at : at + 32])) for at in range(0, len(ones), 32)]
        word = jnp.uint32(words[0])
        for i, other in enumerate(words[1:], 1):
            word = jnp.where(device // 32 == i, jnp.uint32(other), word)
        result = result | (((word >> place) & jnp.uint32(1)) << jnp.uint32(bit))
    return result.astype(jnp.int32)


def window_kernel(*refs):
    blocks = refs[:STEPS]
    factor, twice, male, out = refs[STEPS:]
    group_size = blocks[0].shape[0]
    for s, block in enumerate(blocks):

        @pl.loop(0, group_size // ROW_TILE)
        def _(i, s=s, block=block):
            here = pl.ds(pl.multiple_of(i * ROW_TILE, ROW_TILE), ROW_TILE)
            rows = pl.ds(pl.multiple_of(s * group_size + i * ROW_TILE, ROW_TILE), ROW_TILE)
            value = block[here, :].astype(jnp.float32) - twice[rows, :]
            out[rows, :] = (value * factor[rows, :] * male[...]).astype(out.dtype)


def standardized_window(blocks, factor, twice, male):
    group_size, n = blocks[0].shape
    depth = STEPS * group_size
    column = lambda j: (0, 0)
    return pl.pallas_call(
        window_kernel,
        out_shape=jax.ShapeDtypeStruct((depth, n), jnp.bfloat16),
        grid=(n // COL_TILE,),
        in_specs=[pl.BlockSpec((group_size, COL_TILE), lambda j: (0, j))] * STEPS
        + [pl.BlockSpec((depth, 1), column)] * 2
        + [pl.BlockSpec((1, COL_TILE), lambda j: (0, j))],
        out_specs=pl.BlockSpec((depth, COL_TILE), lambda j: (0, j)),
        compiler_params=pltpu.CompilerParams(vmem_limit_bytes=VMEM_LIMIT),
        cost_estimate=pl.CostEstimate(flops=4 * depth * n, bytes_accessed=4 * depth * n, transcendentals=0),
        name="window",
    )(*blocks, factor, twice, male)


def product_kernel(first, candidates, scale, n_buffers, places, *refs):
    x, buffers = refs[0], refs[1 : 1 + n_buffers]
    factor, twice, male, zy = refs[1 + n_buffers : 5 + n_buffers]
    out, raw, zx, sems = refs[-4:]
    width = raw.shape[1] // STEPS
    piece_rows = buffers[0].shape[0] // 2
    pieces = raw.shape[0] // piece_rows

    @pl.when(pl.program_id(0) == 0)
    def _():
        for q in range(pieces):
            for s in range(STEPS):
                place = places[q * STEPS + s]
                target = raw.at[pl.ds(q * piece_rows, piece_rows), pl.ds(s * width, width)]
                for number in candidates[q * STEPS + s]:
                    if number >= 0:

                        @pl.when(place == number)
                        def _(number=number, target=target, q=q):
                            block = buffers[number // 2].at[pl.ds(number % 2 * piece_rows, piece_rows), :]
                            pltpu.make_async_copy(block, target, sems.at[q]).start()

                    else:

                        @pl.when(place < 0)
                        def _(place=place, target=target, q=q):
                            col = pl.multiple_of((-1 - place) * width, width)
                            block = x.at[pl.ds((first + q) * piece_rows, piece_rows), pl.ds(col, width)]
                            pltpu.make_async_copy(block, target, sems.at[q]).start()

        for q in range(pieces):
            part = raw.at[pl.ds(q * piece_rows, piece_rows), :]
            pltpu.make_async_copy(part, part, sems.at[q]).wait()

            @pl.loop(0, piece_rows // ROW_TILE)
            def _(i, q=q):
                rows = pl.ds(pl.multiple_of(q * piece_rows + i * ROW_TILE, ROW_TILE), ROW_TILE)
                value = raw[rows, :].astype(jnp.float32) - twice[...]
                zx[rows, :] = (value * factor[...] * male[rows, :]).astype(zx.dtype)

    total = jnp.dot(zx[...], zy[...], preferred_element_type=jnp.float32)
    out[...] = (total * scale).astype(out.dtype)


def product(part, places, candidates, x, buffers, factor, twice, male, zy, before):
    rows, (depth, n) = x.shape[0], zy.shape
    first, stop = part
    part_rows = rows // PIECES * (stop - first)
    number = first // (stop - first)
    scale = float(1.0 / np.sqrt(np.float32(depth)))
    whole = lambda j, places: (0, 0)
    specs = [pl.BlockSpec(memory_space=pl.ANY)] * (1 + len(buffers)) + [
        pl.BlockSpec((1, depth), whole),
        pl.BlockSpec((1, depth), whole),
        pl.BlockSpec((part_rows, 1), lambda j, places: (number, 0)),
        pl.BlockSpec((depth, COL_TILE), lambda j, places: (0, j)),
    ]
    args = [places, x, *buffers, factor, twice, male, zy]
    aliases = {}
    if before is not None:
        aliases = {len(args): 0}
        specs.append(pl.BlockSpec(memory_space=pl.ANY))
        args.append(before)
    return pl.pallas_call(
        functools.partial(product_kernel, first, candidates, scale, len(buffers)),
        out_shape=jax.ShapeDtypeStruct((rows, n), jnp.bfloat16),
        grid_spec=pltpu.PrefetchScalarGridSpec(
            num_scalar_prefetch=1,
            grid=(n // COL_TILE,),
            in_specs=specs,
            out_specs=pl.BlockSpec((part_rows, COL_TILE), lambda j, places: (number, j)),
            scratch_shapes=[
                pltpu.VMEM((part_rows, depth), jnp.bfloat16),
                pltpu.VMEM((part_rows, depth), jnp.bfloat16),
                pltpu.SemaphoreType.DMA((stop - first,)),
            ],
        ),
        input_output_aliases=aliases,
        compiler_params=pltpu.CompilerParams(vmem_limit_bytes=VMEM_LIMIT),
        cost_estimate=pl.CostEstimate(
            flops=2 * part_rows * depth * n,
            bytes_accessed=2 * (part_rows * depth + depth * n + part_rows * n),
            transcendentals=0,
        ),
        name="product",
    )(*args)


def col_sum(value, cols):
    if cols & (cols - 1):
        return lax.psum(value, "col")
    bit = 1
    while bit < cols:
        value = value + lax.ppermute(value, "col", [(i, i ^ bit) for i in range(cols)])
        bit *= 2
    return value


def local(rows, cols, x, y, freq, weight, sex_rows, sex_cols):
    group_size = y.shape[0]
    local_vars = x.shape[1]
    groups_here = local_vars // group_size
    piece_rows = x.shape[0] // PIECES
    lanes = [Lane(rows, cols, groups_here, towards) for towards in (True, False)]
    devices = [(r, c) for r in range(rows) for c in range(cols)]
    both = ("row", "col")

    row_place = lax.axis_index("row")
    col_place = lax.axis_index("col")
    device = row_place * cols + col_place

    def number(r, c):
        return r * cols + c

    def own_chunk(x, items):
        blocks = []
        for k in range(2):
            piece = lookup([None if i is None else i.blocks[k][0] for i in items], device)
            group = lookup(
                [None if i is None else (i.owner + i.blocks[k][1]) % rows % groups_here for i in items], device
            )
            start = (piece * piece_rows, group * group_size)
            blocks.append(lax.dynamic_slice(x, start, (piece_rows, group_size)))
        return jnp.concatenate(blocks, axis=0)

    crossings = []
    crossing_of = {}
    for d, lane in enumerate(lanes):
        for r in range(rows):
            for slot, item in sorted(lane.lines[r][0].items()):
                if item.home is None:
                    continue
                source, target = (item.home, lane.col(item.place)), (r, lane.col(item.place))
                for k, crossing in enumerate(crossings):
                    if source not in crossing and target not in [to for to, _ in crossing.values()]:
                        break
                else:
                    k = len(crossings)
                    crossings.append({})
                crossings[k][source] = (target, item)
                crossing_of[d, r, item.blocks] = k

    def lane_of(phase, r):
        return (r + phase) % 2

    buffers = {}
    crossed = {}
    window = [y]
    back = [(i, (i - 1) % rows) for i in range(rows)]

    def send(phase, t):
        lane = {r: lanes[lane_of(phase, r)] for r in range(rows)}
        sent = [lane[r].sent(r, c, t) for r, c in devices]
        pairs = [
            (number(r, c), number(r, lane[r].col(lane[r].place(c) - 1)))
            for i, (r, c) in zip(sent, devices)
            if i is not None
        ]
        if not pairs:
            return
        at = [lane[r].place(c) for r, c in devices]
        kinds = []
        for i, p, (r, c) in zip(sent, at, devices):
            if i is None:
                kinds.append(None)
            elif i.place != p:
                kinds.append(1)
            elif i.home is None:
                kinds.append(0)
            else:
                kinds.append(2 + crossing_of[lane_of(phase, r), r, i.blocks])
        sources = []
        for kind in sorted({k for k in kinds if k}):
            sources.append((kind, buffers[phase, t - DEPTH] if kind == 1 else crossed[kind - 2]))
        ties = [b for _, b in sources]
        other = buffers.get((1 - phase, t - 1 - (1 - phase)))
        if other is not None:
            ties.append(other)
        if phase == 0 and t in (3, 5, 7) and len(window) < STEPS:
            ties.append(window[-1])
        tied = lax.optimization_barrier((x, *ties))
        if phase == 0 and t in (3, 5, 7) and len(window) < STEPS:
            window[-1] = tied[-1]
        held = None
        if 0 in kinds:
            held = own_chunk(tied[0], [i if k == 0 else None for i, k in zip(sent, kinds)])
        for k, (kind, _) in enumerate(sources):
            buffer = tied[1 + k]
            if held is not None:
                mask = lookup([None if v is None else int(v == kind) for v in kinds], device)
                buffer = jnp.where(mask == 1, buffer, held)
            held = buffer
        buffers[phase, t] = lax.ppermute(held, both, pairs)

    def bring_back(phase, t):
        pairs = []
        for r in range(rows):
            lane = lanes[lane_of(phase, r)]
            item = lane.lines[r][0].get(t)
            if item is not None and item.home is not None:
                pairs.append((number(r, lane.col(0)), number(item.home, lane.col(0))))
        if pairs:
            buffers["back%d" % phase, t] = lax.ppermute(buffers[phase, t], both, pairs)

    for t in range(1, max(lane.rounds for lane in lanes) + 1):
        for phase in range(2):
            send(phase, t)
        if t == 1:
            for crossing in crossings:
                held = own_chunk(
                    lax.optimization_barrier(x), [crossing[rc][1] if rc in crossing else None for rc in devices]
                )
                pairs = [(number(*rc), number(*to)) for rc, (to, _) in crossing.items()]
                crossed[len(crossed)] = lax.ppermute(held, both, pairs)
        if t in (1, 3, 5, 7) and len(window) < STEPS:
            window.append(lax.ppermute(window[-1], "row", back))
        for phase in range(2):
            bring_back(phase, t)
    while len(window) < STEPS:
        window.append(lax.ppermute(window[-1], "row", back))

    factor = weight / jnp.sqrt(2.0 * freq * (1.0 - freq))
    span = STEPS * group_size

    def in_window(value):
        return lax.dynamic_slice(jnp.concatenate([value, value]), (row_place * group_size,), (span,))

    window_factor = in_window(factor)
    window_twice = in_window(2.0 * freq)
    male_scale = np.float32(np.sqrt(0.5))
    male_rows = jnp.where(sex_rows > 0, male_scale, np.float32(1.0))[:, None]
    male_cols = jnp.where(sex_cols > 0, male_scale, np.float32(1.0))[None, :]
    zy = standardized_window(window, window_factor[:, None], window_twice[:, None], male_cols)

    here = lambda value: lax.dynamic_slice(value, (col_place * local_vars,), (local_vars,))[None, :]
    zx = ((x.astype(jnp.float32) - here(2.0 * freq)) * here(factor) * male_rows).astype(jnp.bfloat16)
    squares = col_sum(jnp.sum(jnp.square(zx.astype(jnp.float32)), axis=1), cols)
    inbreeding = squares / jnp.float32(freq.shape[0]) - 1.0

    relation = None
    for part in PARTS:
        found = []
        for r, c in devices:
            keys = []
            for q in range(*part):
                for s in range(STEPS):
                    key = -1 - (r + s) % rows % groups_here
                    for d, lane in enumerate(lanes):
                        arrival = lane.arrival(r, c, (q, s))
                        if arrival is not None:
                            t, returned, sub = arrival
                            phase = (r + d) % 2
                            if returned:
                                phase = "back%d" % ((r + rows // 2 + d) % 2)
                            key = (phase, t), sub
                    keys.append(key)
            found.append(keys)
        used = {k[0] for keys in found for k in keys if isinstance(k, tuple)}
        used = sorted(used, key=lambda k: (k[1], str(k[0])))
        places = np.asarray(
            [[k if isinstance(k, int) else 2 * used.index(k[0]) + k[1] for k in keys] for keys in found], np.int32
        )
        candidates = [sorted({max(int(k), -1) for k in places[:, i]}) for i in range(places.shape[1])]
        relation = product(
            part,
            lax.dynamic_slice(jnp.asarray(places), (device, 0), (1, places.shape[1]))[0],
            candidates,
            x,
            [buffers[key] for key in used],
            window_factor[None, :],
            window_twice[None, :],
            male_rows,
            zy,
            relation,
        )
    return relation, inbreeding


def solution(mesh):
    rows, cols = mesh.shape["row"], mesh.shape["col"]
    return jax.shard_map(
        functools.partial(local, rows, cols),
        mesh=mesh,
        in_specs=(P("row", "col"), P("row", "col"), P(), P(), P("row"), P("col")),
        out_specs=(P("row", "col"), P("row")),
        check_vma=False,
    )
```

time: 148 us -> 162 us (1.095)
  the two profiles are of different devices: /device:TPU:3 before, /device:TPU:0 now
where the time goes in v4:
time: 162 us; the launch traced here: 161 us
  starting transfers between devices  46.7 us (29%)
  waiting for transfers between devices  46.5 us (29%)
  Pallas kernels  39.6 us (24%)
  other arithmetic  18.5 us (11%)
  local copies, waits for them, and re-layouts  8.2 us (5%)
    ppermute x16, waiting for transfers between devices, send(): buffers[phase, t] = lax.ppermute(held, both, pairs)  43 us
    pallas_call x3, Pallas kernels, product(): pl.pallas_call(functools.partial(product_kernel, first, candidates, scale...  27.5 us
    ppermute x16, starting transfers between devices, send(): buffers[phase, t] = lax.ppermute(held, both, pairs)  25.9 us
    select_n x12, other arithmetic, send(): buffer = jnp.where(mask == 1, buffer, held)  14.3 us
    pallas_call x1, Pallas kernels, standardized_window(): pl.pallas_call(window_kernel, out_shape=jax.ShapeDtypeStruct((depth, n),...  12.2 us
    ppermute x3, starting transfers between devices, local(): window.append(lax.ppermute(window[-1], 'row', back))  9.68 us
    ppermute x6, starting transfers between devices, bring_back(): buffers['back%d' % phase, t] = lax.ppermute(buffers[phase, t], both, pairs)  5.42 us
    ppermute x2, starting transfers between devices, col_sum(): lax.ppermute(value, 'col', [(i, i ^ bit) for i in range(cols)])  3.59 us
  transfers between devices with their start and end apart: 28, of which 8 were waited for; matrix products, arithmetic and copies ran while one was open for 12% of the time, Pallas kernels for 19%

profile of v4, /device:TPU:0, one launch (start us, length us, event | category | flops | bytes accessed | tf_op | source)
XLA Modules:
  0.0 161.2 jit_solution(13262829039300576974)
XLA Ops:
  0.7 1.5 fusion.12
  2.2 0.8 pad_maximum_fusion
  3.0 1.3 collective-permute-start
  4.3 5.3 %collective-permute-start.5 = (bf16[256,2048]{1,0:T(8,128)(2,1)}, bf16[256,2048]{1,0:T(8,128)(2,1)}, u32[]{:S(2)}, u32[]{:S(2)}) collective-permute-start(bf16[256,2048]{1,0:T(8,128)(2,1)} %refs_0_.4), channel_id=1, source_target_pairs={{0,28},{4,0},{8,4},{12,8},{16,12},{20,16},{24,20},{28,24},{1,29},{... | collective-permute-start | bytes 3145736 | tf_op jit(solution)/shard_map/ppermute | solution.py:415
  9.6 0.9 pad_maximum_fusion.1
  10.5 3.5 %collective-permute-start.2 = (bf16[1024,256]{1,0:T(8,128)(2,1)}, bf16[1024,256]{1,0:T(8,128)(2,1)S(1)}, u32[]{:S(2)}, u32[]{:S(2)}) collective-permute-start(bf16[1024,256]{1,0:T(8,128)(2,1)} %pad_maximum_fusion.1), channel_id=1, source_target_pairs={{0,1},{1,2},{5,4},{6,5},{9,10},{10,11},{13,12},{14,13},{15,14},{18... | collective-permute-start | bytes 1572872 | tf_op jit(solution)/shard_map/ppermute | solution.py:392
  13.9 0.9 pad_maximum_fusion.2
  14.8 2.1 %collective-permute-start.4 = (bf16[1024,256]{1,0:T(8,128)(2,1)}, bf16[1024,256]{1,0:T(8,128)(2,1)}, u32[]{:S(2)}, u32[]{:S(2)}) collective-permute-start(bf16[1024,256]{1,0:T(8,128)(2,1)} %pad_maximum_fusion.2), channel_id=1, source_target_pairs={{18,2},{19,3},{9,25},{13,29},{14,30},{1,17},{0,16},{6,22},{5,21},{... | collective-permute-start | bytes 1572872 | tf_op jit(solution)/shard_map/ppermute | solution.py:413
  16.9 0.8 copy-done.10
  17.7 0.9 maximum_select_fusion
  18.6 1.3 collective-permute-start.1
  19.9 1.0 collective-permute-done.2.refs_2_
  20.9 0.8 copy-done.12
  21.7 0.9 maximum_select_fusion.1
  22.6 0.7 collective-permute-start.3
  23.4 9.8 %collective-permute-done.1.refs_3_.refs_1_ = bf16[1024,256]{1,0:T(8,128)(2,1)S(1)} collective-permute-done((bf16[1024,256]{1,0:T(8,128)(2,1)}, bf16[1024,256]{1,0:T(8,128)(2,1)S(1)}, u32[]{:S(2)}, u32[]{:S(2)}) %collective-permute-start.1) | collective-permute-done | bytes 524320 | tf_op jit(solution)/shard_map/ppermute | solution.py:392
  33.2 1.0 fusion
  34.3 1.3 collective-permute-start.6
  35.6 1.0 fusion.1
  36.6 5.4 %collective-permute-start.8 = (bf16[1024,256]{1,0:T(8,128)(2,1)}, bf16[1024,256]{1,0:T(8,128)(2,1)}, u32[]{:S(2)}, u32[]{:S(2)}) collective-permute-start(bf16[1024,256]{1,0:T(8,128)(2,1)} %fusion.1), channel_id=1, source_target_pairs={{0,1},{1,2},{2,3},{5,4},{9,10},{10,11},{13,12},{14,13},{16,17},{17... | collective-permute-start | bytes 1572872 | tf_op jit(solution)/shard_map/ppermute | solution.py:392
  42.0 8.1 %collective-permute-done.6.refs_5_.refs_3_ = bf16[1024,256]{1,0:T(8,128)(2,1)} collective-permute-done((bf16[1024,256]{1,0:T(8,128)(2,1)}, bf16[1024,256]{1,0:T(8,128)(2,1)}, u32[]{:S(2)}, u32[]{:S(2)}) %collective-permute-start.6) | collective-permute-done | bytes 524320 | tf_op jit(solution)/shard_map/ppermute | solution.py:392
  50.1 2.0 %maximum_select_fusion.4 = bf16[1024,256]{1,0:T(8,128)(2,1)} fusion(bf16[1024,256]{1,0:T(8,128)(2,1)} %collective-permute-done.6.refs_5_.refs_3_, bf16[512,256]{1,0:T(8,128)(2,1)S(1)} %get-tuple-element.77, bf16[512,256]{1,0:T(8,128)(2,1)S(1)} %get-tuple-element.76, pred[]{:T(512)S(6)} %eq.94), kind=kLoop, calls=%fused_computation.11 | loop fusion | flops 1310720 | bytes 1572865 | tf_op jit(solution)/shard_map/jit(_where)/select_n | solution.py:390
  52.1 1.3 collective-permute-start.10
  53.5 2.0 %maximum_select_fusion.5 = bf16[1024,256]{1,0:T(8,128)(2,1)} fusion(bf16[1024,256]{1,0:T(8,128)(2,1)} %collective-permute-done.8.refs_6_.refs_4_, bf16[512,256]{1,0:T(8,128)(2,1)S(1)} %get-tuple-element.75, bf16[512,256]{1,0:T(8,128)(2,1)S(1)} %get-tuple-element.74, pred[]{:T(512)S(6)} %eq.95), kind=kLoop, calls=%fused_computation.12 | loop fusion | flops 1310720 | bytes 1572865 | tf_op jit(solution)/shard_map/jit(_where)/select_n | solution.py:390
  55.4 0.7 collective-permute-start.11
  56.2 12.8 %collective-permute-done.10.refs_7_.refs_5_ = bf16[1024,256]{1,0:T(8,128)(2,1)S(1)} collective-permute-done((bf16[1024,256]{1,0:T(8,128)(2,1)}, bf16[1024,256]{1,0:T(8,128)(2,1)S(1)}, u32[]{:S(2)}, u32[]{:S(2)}) %collective-permute-start.10) | collective-permute-done | bytes 524320 | tf_op jit(solution)/shard_map/ppermute | solution.py:392
  69.1 1.2 maximum_select_fusion.7
  70.2 2.1 %collective-permute-start.16 = (bf16[1024,256]{1,0:T(8,128)(2,1)}, bf16[1024,256]{1,0:T(8,128)(2,1)}, u32[]{:S(2)}, u32[]{:S(2)}) collective-permute-start(bf16[1024,256]{1,0:T(8,128)(2,1)} %maximum_select_fusion.7), channel_id=1, source_target_pairs={{0,1},{1,2},{2,3},{5,4},{9,10},{10,11},{13,12},{14,13},{18,19},{21... | collective-permute-start | bytes 1572872 | tf_op jit(solution)/shard_map/ppermute | solution.py:392
  72.4 0.9 maximum_select_fusion.6
  73.3 1.3 collective-permute-start.15
  74.8 3.7 %collective-permute-done.16.refs_10_ = bf16[1024,256]{1,0:T(8,128)(2,1)} collective-permute-done((bf16[1024,256]{1,0:T(8,128)(2,1)}, bf16[1024,256]{1,0:T(8,128)(2,1)}, u32[]{:S(2)}, u32[]{:S(2)}) %collective-permute-start.16) | collective-permute-done | bytes 524320 | tf_op jit(solution)/shard_map/ppermute | solution.py:392
  78.5 7.6 %collective-permute-done.15.refs_9_ = bf16[1024,256]{1,0:T(8,128)(2,1)} collective-permute-done((bf16[1024,256]{1,0:T(8,128)(2,1)}, bf16[1024,256]{1,0:T(8,128)(2,1)}, u32[]{:S(2)}, u32[]{:S(2)}) %collective-permute-start.15) | collective-permute-done | bytes 524320 | tf_op jit(solution)/shard_map/ppermute | solution.py:392
  86.2 2.0 %maximum_select_fusion.9 = bf16[1024,256]{1,0:T(8,128)(2,1)} fusion(bf16[1024,256]{1,0:T(8,128)(2,1)} %collective-permute-done.16.refs_10_, bf16[512,256]{1,0:T(8,128)(2,1)S(1)} %get-tuple-element.67, bf16[512,256]{1,0:T(8,128)(2,1)S(1)} %get-tuple-element.66, pred[]{:T(512)S(6)} %eq.99), kind=kLoop, calls=%fused_computation.16 | loop fusion | flops 1310720 | bytes 1572865 | tf_op jit(solution)/shard_map/jit(_where)/select_n | solution.py:390
  88.1 1.5 collective-permute-start.20
  89.6 0.9 maximum_select_fusion.8
  90.6 1.3 collective-permute-start.19
  91.8 1.0 multiply_reduce_fusion
  92.9 3.5 %collective-permute-start.26 = (f32[2048]{0:T(1024)S(1)}, f32[2048]{0:T(1024)S(1)}, u32[]{:S(2)}, u32[]{:S(2)}) collective-permute-start(f32[2048]{0:T(1024)S(1)} %multiply_reduce_fusion), channel_id=1, source_target_pairs={{0,1},{1,0},{2,3},{3,2},{4,5},{5,4},{6,7},{7,6},{8,9},{9,8},{10,11... | collective-permute-start | bytes 24584 | tf_op jit(solution)/shard_map/ppermute | solution.py:293
  96.4 0.7 fusion.6.places
  97.2 4.3 %collective-permute-start.25 = (bf16[256,2048]{1,0:T(8,128)(2,1)}, bf16[256,2048]{1,0:T(8,128)(2,1)}, u32[]{:S(2)}, u32[]{:S(2)}) collective-permute-start(bf16[256,2048]{1,0:T(8,128)(2,1)} %collective-permute-done.14.refs_2_), channel_id=1, source_target_pairs={{0,28},{4,0},{8,4},{12,8},{16,12},{20,16},{24,20},{28,24},{1,29},{... | collective-permute-start | bytes 3145736 | tf_op jit(solution)/shard_map/ppermute | solution.py:415
  101.5 0.7 fusion.5.places
  102.2 1.0 copy.13.refs_4_
  103.2 1.0 copy.14.refs_5_
  104.3 0.4 copy.17.refs_13_.refs_17_.refs_21_
  104.7 0.7 collective-permute-start.9
  105.4 0.7 collective-permute-start.7
  106.2 0.7 collective-permute-start.13
  107.0 0.2 maximum_select_fusion.11
  107.2 1.3 maximum_select_fusion.10
  108.4 0.8 collective-permute-done.27
  109.3 2.2 %collective-permute-start.22 = (bf16[1024,256]{1,0:T(8,128)(2,1)S(1)}, bf16[1024,256]{1,0:T(8,128)(2,1)S(1)}, u32[]{:S(2)}, u32[]{:S(2)}) collective-permute-start(bf16[1024,256]{1,0:T(8,128)(2,1)S(1)} %maximum_select_fusion.11), channel_id=1, source_target_pairs={{0,1},{1,2},{2,3},{10,11},{21,20},{26,27}} | collective-permute-start | bytes 1572872 | tf_op jit(solution)/shard_map/ppermute | solution.py:392
  111.5 2.6 %collective-permute-done.25.refs_3_ = bf16[256,2048]{1,0:T(8,128)(2,1)} collective-permute-done((bf16[256,2048]{1,0:T(8,128)(2,1)}, bf16[256,2048]{1,0:T(8,128)(2,1)}, u32[]{:S(2)}, u32[]{:S(2)}) %collective-permute-start.25) | collective-permute-done | bytes 1048608 | tf_op jit(solution)/shard_map/ppermute | solution.py:415
  114.1 0.7 collective-permute-start.21
  114.8 0.7 fusion.4.places
  115.5 0.6 multiply_add_fusion
  116.2 12.2 %window.1.refs_14_.refs_18_.refs_22_ = bf16[1024,2048]{1,0:T(8,128)(2,1)S(1)} custom-call(bf16[256,2048]{1,0:T(8,128)(2,1)} %refs_0_.4, bf16[256,2048]{1,0:T(8,128)(2,1)} %collective-permute-done.5.refs_1_, bf16[256,2048]{1,0:T(8,128)(2,1)} %collective-permute-done.14.refs_2_, bf16[256,2048]{1,0:T(8,128)(2,1)} %collective-permute-done.25.refs_3_, ...), custom_call_target="tpu_custom_call" | custom-call | flops 8388608 | bytes 8388608 | tf_op jit(solution)/shard_map/window/pallas_call | solution.py:186
  128.4 1.3 collective-permute-start.12
  129.7 0.7 collective-permute-start.18
  130.5 1.3 collective-permute-start.17
  131.8 0.7 collective-permute-start.24
  132.5 0.9 collective-permute-start.23
  133.4 10.0 %product.3.refs_19_ = bf16[2048,2048]{1,0:T(8,128)(2,1)} custom-call(s32[8]{0:T(128)S(1)} %fusion.6.places, bf16[2048,512]{1,0:T(8,128)(2,1)S(1)} %copy-done, bf16[1024,256]{1,0:T(8,128)(2,1)S(1)} %copy-done.11, bf16[1024,256]{1,0:T(8,128)(2,1)S(1)} %copy-done.13, bf16[1024,256]{1,0:T(8,128)(2,1)S(1)} %copy-done.7, bf16[1024,256]{1,0:T(8,128)(2,1)S(1)} %copy-done.9, ...), custom_call_target="tpu_custom_call" | custom-call | flops 4294967296 | bytes 10485760 | tf_op jit(solution)/shard_map/product/pallas_call | solution.py:263
  143.5 8.7 %product.4.refs_23_ = bf16[2048,2048]{1,0:T(8,128)(2,1)} custom-call(s32[4]{0:T(128)S(1)} %fusion.5.places, bf16[2048,512]{1,0:T(8,128)(2,1)S(1)} %copy-done, bf16[1024,256]{1,0:T(8,128)(2,1)S(1)} %copy-done.7, bf16[1024,256]{1,0:T(8,128)(2,1)S(1)} %copy-done.9, ...), custom_call_target="tpu_custom_call", output_to_operand_aliasing={{}: (20, {})} | custom-call | flops 2147483648 | bytes 7340032 | tf_op jit(solution)/shard_map/product/pallas_call | solution.py:263
  152.2 8.8 %product.5 = bf16[2048,2048]{1,0:T(8,128)(2,1)} custom-call(s32[4]{0:T(128)S(1)} %fusion.4.places, bf16[2048,512]{1,0:T(8,128)(2,1)S(1)} %copy-done, bf16[1024,256]{1,0:T(8,128)(2,1)S(1)} %copy-done.7, bf16[1024,256]{1,0:T(8,128)(2,1)S(1)} %copy-done.9, ...), custom_call_target="tpu_custom_call", output_to_operand_aliasing={{}: (24, {})} | custom-call | flops 2147483648 | bytes 7340032 | tf_op jit(solution)/shard_map/product/pallas_call | solution.py:263
  (79 shorter events, 0.9 us)
Async XLA Ops:
  2.1 14.8 %copy-start = (bf16[2048,512]{1,0:T(8,128)(2,1)S(1)}, bf16[2048,512]{1,0:T(8,128)(2,1)}, u32[]{:S(2)}) copy-start(bf16[2048,512]{1,0:T(8,128)(2,1)} %refs_0_.7) | copy-start | bytes 6291460
  3.0 13.9 %collective-permute-start = (bf16[1024,256]{1,0:T(8,128)(2,1)}, bf16[1024,256]{1,0:T(8,128)(2,1)S(1)}, u32[]{:S(2)}, u32[]{:S(2)}) collective-permute-start(bf16[1024,256]{1,0:T(8,128)(2,1)} %pad_maximum_fusion), channel_id=1, source_target_pairs={{1,0},{4,5},{5,6},{6,7},{9,8},{10,9},{13,14},{14,15},{18,17},{19,1... | collective-permute-start | bytes 1572872 | tf_op jit(solution)/shard_map/ppermute | solution.py:392
  4.3 28.9 %collective-permute-start.5 = (bf16[256,2048]{1,0:T(8,128)(2,1)}, bf16[256,2048]{1,0:T(8,128)(2,1)}, u32[]{:S(2)}, u32[]{:S(2)}) collective-permute-start(bf16[256,2048]{1,0:T(8,128)(2,1)} %refs_0_.4), channel_id=1, source_target_pairs={{0,28},{4,0},{8,4},{12,8},{16,12},{20,16},{24,20},{28,24},{1,29},{... | collective-permute-start | bytes 3145736 | tf_op jit(solution)/shard_map/ppermute | solution.py:415
  10.5 10.4 %collective-permute-start.2 = (bf16[1024,256]{1,0:T(8,128)(2,1)}, bf16[1024,256]{1,0:T(8,128)(2,1)S(1)}, u32[]{:S(2)}, u32[]{:S(2)}) collective-permute-start(bf16[1024,256]{1,0:T(8,128)(2,1)} %pad_maximum_fusion.1), channel_id=1, source_target_pairs={{0,1},{1,2},{5,4},{6,5},{9,10},{10,11},{13,12},{14,13},{15,14},{18... | collective-permute-start | bytes 1572872 | tf_op jit(solution)/shard_map/ppermute | solution.py:392
  14.8 8.6 %collective-permute-start.4 = (bf16[1024,256]{1,0:T(8,128)(2,1)}, bf16[1024,256]{1,0:T(8,128)(2,1)}, u32[]{:S(2)}, u32[]{:S(2)}) collective-permute-start(bf16[1024,256]{1,0:T(8,128)(2,1)} %pad_maximum_fusion.2), channel_id=1, source_target_pairs={{18,2},{19,3},{9,25},{13,29},{14,30},{1,17},{0,16},{6,22},{5,21},{... | collective-permute-start | bytes 1572872 | tf_op jit(solution)/shard_map/ppermute | solution.py:413
  16.9 0.8 copy-start.10
  18.6 14.6 %collective-permute-start.1 = (bf16[1024,256]{1,0:T(8,128)(2,1)}, bf16[1024,256]{1,0:T(8,128)(2,1)S(1)}, u32[]{:S(2)}, u32[]{:S(2)}) collective-permute-start(bf16[1024,256]{1,0:T(8,128)(2,1)} %maximum_select_fusion), channel_id=1, source_target_pairs={{1,0},{5,6},{6,7},{9,8},{14,15},{17,16},{18,17},{22,23},{27,26},{2... | collective-permute-start | bytes 1572872 | tf_op jit(solution)/shard_map/ppermute | solution.py:392
  20.9 0.8 copy-start.12
  22.6 12.9 %collective-permute-start.3 = (bf16[1024,256]{1,0:T(8,128)(2,1)}, bf16[1024,256]{1,0:T(8,128)(2,1)S(1)}, u32[]{:S(2)}, u32[]{:S(2)}) collective-permute-start(bf16[1024,256]{1,0:T(8,128)(2,1)} %maximum_select_fusion.1), channel_id=1, source_target_pairs={{1,2},{2,3},{5,4},{10,11},{13,12},{14,13},{18,19},{21,20},{22,21},... | collective-permute-start | bytes 1572872 | tf_op jit(solution)/shard_map/ppermute | solution.py:392
  33.2 2.4 %copy-start.6 = (bf16[1024,256]{1,0:T(8,128)(2,1)}, bf16[1024,256]{1,0:T(8,128)(2,1)S(1)}, u32[]{:S(2)}) copy-start(bf16[1024,256]{1,0:T(8,128)(2,1)S(1)} %collective-permute-done.1.refs_3_.refs_1_) | copy-start | bytes 1572868
  34.3 15.8 %collective-permute-start.6 = (bf16[1024,256]{1,0:T(8,128)(2,1)}, bf16[1024,256]{1,0:T(8,128)(2,1)}, u32[]{:S(2)}, u32[]{:S(2)}) collective-permute-start(bf16[1024,256]{1,0:T(8,128)(2,1)} %fusion), channel_id=1, source_target_pairs={{1,0},{2,1},{3,2},{5,6},{6,7},{9,8},{10,9},{14,15},{17,16},{18,17}... | collective-permute-start | bytes 1572872 | tf_op jit(solution)/shard_map/ppermute | solution.py:392
  35.6 14.6 %copy-start.8 = (bf16[1024,256]{1,0:T(8,128)(2,1)}, bf16[1024,256]{1,0:T(8,128)(2,1)S(1)}, u32[]{:S(2)}) copy-start(bf16[1024,256]{1,0:T(8,128)(2,1)S(1)} %collective-permute-done.3.refs_4_.refs_2_) | copy-start | bytes 1572868
  36.6 16.8 %collective-permute-start.8 = (bf16[1024,256]{1,0:T(8,128)(2,1)}, bf16[1024,256]{1,0:T(8,128)(2,1)}, u32[]{:S(2)}, u32[]{:S(2)}) collective-permute-start(bf16[1024,256]{1,0:T(8,128)(2,1)} %fusion.1), channel_id=1, source_target_pairs={{0,1},{1,2},{2,3},{5,4},{9,10},{10,11},{13,12},{14,13},{16,17},{17... | collective-permute-start | bytes 1572872 | tf_op jit(solution)/shard_map/ppermute | solution.py:392
  42.0 27.0 %collective-permute-start.14 = (bf16[256,2048]{1,0:T(8,128)(2,1)}, bf16[256,2048]{1,0:T(8,128)(2,1)}, u32[]{:S(2)}, u32[]{:S(2)}) collective-permute-start(bf16[256,2048]{1,0:T(8,128)(2,1)} %collective-permute-done.5.refs_1_), channel_id=1, source_target_pairs={{0,28},{4,0},{8,4},{12,8},{16,12},{20,16},{24,20},{28,24},{1,29},{... | collective-permute-start | bytes 3145736 | tf_op jit(solution)/shard_map/ppermute | solution.py:415
  52.1 16.9 %collective-permute-start.10 = (bf16[1024,256]{1,0:T(8,128)(2,1)}, bf16[1024,256]{1,0:T(8,128)(2,1)S(1)}, u32[]{:S(2)}, u32[]{:S(2)}) collective-permute-start(bf16[1024,256]{1,0:T(8,128)(2,1)} %maximum_select_fusion.4), channel_id=1, source_target_pairs={{1,0},{2,1},{4,5},{5,6},{6,7},{9,8},{13,14},{14,15},{17,16},{18,17... | collective-permute-start | bytes 1572872 | tf_op jit(solution)/shard_map/ppermute | solution.py:392
  55.4 13.5 %collective-permute-start.11 = (bf16[1024,256]{1,0:T(8,128)(2,1)}, bf16[1024,256]{1,0:T(8,128)(2,1)S(1)}, u32[]{:S(2)}, u32[]{:S(2)}) collective-permute-start(bf16[1024,256]{1,0:T(8,128)(2,1)} %maximum_select_fusion.5), channel_id=1, source_target_pairs={{1,2},{2,3},{5,4},{6,5},{10,11},{13,12},{14,13},{15,14},{17,18},{1... | collective-permute-start | bytes 1572872 | tf_op jit(solution)/shard_map/ppermute | solution.py:392
  69.0 4.4 %copy-start.2 = (bf16[1024,256]{1,0:T(8,128)(2,1)}, bf16[1024,256]{1,0:T(8,128)(2,1)S(1)}, u32[]{:S(2)}) copy-start(bf16[1024,256]{1,0:T(8,128)(2,1)S(1)} %collective-permute-done.10.refs_7_.refs_5_) | copy-start | bytes 1572868
  69.0 4.4 %copy-start.4 = (bf16[1024,256]{1,0:T(8,128)(2,1)}, bf16[1024,256]{1,0:T(8,128)(2,1)S(1)}, u32[]{:S(2)}) copy-start(bf16[1024,256]{1,0:T(8,128)(2,1)S(1)} %collective-permute-done.11.refs_8_.refs_6_) | copy-start | bytes 1572868
  69.0 5.6 %copy-start.18 = (f32[2048]{0:T(1024)S(1)}, f32[2048]{0:T(1024)}, u32[]{:S(2)}) copy-start(f32[2048]{0:T(1024)} %param.11) | copy-start | bytes 24580
  69.0 5.6 %copy-start.19 = (f32[2048]{0:T(1024)S(1)}, f32[2048]{0:T(1024)}, u32[]{:S(2)}) copy-start(f32[2048]{0:T(1024)} %param.12) | copy-start | bytes 24580
  69.1 5.8 %copy-start.16 = (s32[2048]{0:T(1024)S(1)}, s32[2048]{0:T(1024)}, u32[]{:S(2)}) copy-start(s32[2048]{0:T(1024)} %param.13) | copy-start | bytes 24580
  70.2 8.3 %collective-permute-start.16 = (bf16[1024,256]{1,0:T(8,128)(2,1)}, bf16[1024,256]{1,0:T(8,128)(2,1)}, u32[]{:S(2)}, u32[]{:S(2)}) collective-permute-start(bf16[1024,256]{1,0:T(8,128)(2,1)} %maximum_select_fusion.7), channel_id=1, source_target_pairs={{0,1},{1,2},{2,3},{5,4},{9,10},{10,11},{13,12},{14,13},{18,19},{21... | collective-permute-start | bytes 1572872 | tf_op jit(solution)/shard_map/ppermute | solution.py:392
  73.3 12.8 %collective-permute-start.15 = (bf16[1024,256]{1,0:T(8,128)(2,1)}, bf16[1024,256]{1,0:T(8,128)(2,1)}, u32[]{:S(2)}, u32[]{:S(2)}) collective-permute-start(bf16[1024,256]{1,0:T(8,128)(2,1)} %maximum_select_fusion.6), channel_id=1, source_target_pairs={{1,0},{5,6},{6,7},{9,8},{10,9},{14,15},{17,16},{18,17},{19,18},{21... | collective-permute-start | bytes 1572872 | tf_op jit(solution)/shard_map/ppermute | solution.py:392
  88.1 17.3 %collective-permute-start.20 = (bf16[1024,256]{1,0:T(8,128)(2,1)}, bf16[1024,256]{1,0:T(8,128)(2,1)}, u32[]{:S(2)}, u32[]{:S(2)}) collective-permute-start(bf16[1024,256]{1,0:T(8,128)(2,1)} %maximum_select_fusion.9), channel_id=1, source_target_pairs={{1,2},{2,3},{5,4},{9,10},{10,11},{13,12},{14,13},{18,19},{21,20},{... | collective-permute-start | bytes 1572872 | tf_op jit(solution)/shard_map/ppermute | solution.py:392
  90.6 15.6 %collective-permute-start.19 = (bf16[1024,256]{1,0:T(8,128)(2,1)}, bf16[1024,256]{1,0:T(8,128)(2,1)}, u32[]{:S(2)}, u32[]{:S(2)}) collective-permute-start(bf16[1024,256]{1,0:T(8,128)(2,1)} %maximum_select_fusion.8), channel_id=1, source_target_pairs={{1,0},{5,6},{6,7},{9,8},{10,9},{14,15},{17,16},{18,17},{22,23},{25... | collective-permute-start | bytes 1572872 | tf_op jit(solution)/shard_map/ppermute | solution.py:392
  92.9 11.8 %collective-permute-start.26 = (f32[2048]{0:T(1024)S(1)}, f32[2048]{0:T(1024)S(1)}, u32[]{:S(2)}, u32[]{:S(2)}) collective-permute-start(f32[2048]{0:T(1024)S(1)} %multiply_reduce_fusion), channel_id=1, source_target_pairs={{0,1},{1,0},{2,3},{3,2},{4,5},{5,4},{6,7},{7,6},{8,9},{9,8},{10,11... | collective-permute-start | bytes 24584 | tf_op jit(solution)/shard_map/ppermute | solution.py:293
  97.2 17.0 %collective-permute-start.25 = (bf16[256,2048]{1,0:T(8,128)(2,1)}, bf16[256,2048]{1,0:T(8,128)(2,1)}, u32[]{:S(2)}, u32[]{:S(2)}) collective-permute-start(bf16[256,2048]{1,0:T(8,128)(2,1)} %collective-permute-done.14.refs_2_), channel_id=1, source_target_pairs={{0,28},{4,0},{8,4},{12,8},{16,12},{20,16},{24,20},{28,24},{1,29},{... | collective-permute-start | bytes 3145736 | tf_op jit(solution)/shard_map/ppermute | solution.py:415
  104.7 4.6 %collective-permute-start.27 = (f32[2048]{0:T(1024)S(1)}, f32[2048]{0:T(1024)S(1)}, u32[]{:S(2)}, u32[]{:S(2)}) collective-permute-start(f32[2048]{0:T(1024)S(1)} %add.194), channel_id=1, source_target_pairs={{0,2},{1,3},{2,0},{3,1},{4,6},{5,7},{6,4},{7,5},{8,10},{9,11},{10,... | collective-permute-start | bytes 24584 | tf_op jit(solution)/shard_map/ppermute | solution.py:293
  104.7 25.7 %collective-permute-start.9 = (bf16[1024,256]{1,0:T(8,128)(2,1)}, bf16[1024,256]{1,0:T(8,128)(2,1)S(1)}, u32[]{:S(2)}, u32[]{:S(2)}) collective-permute-start(bf16[1024,256]{1,0:T(8,128)(2,1)} %collective-permute-done.8.refs_6_.refs_4_), channel_id=1, source_target_pairs={{27,11},{28,12}} | collective-permute-start | bytes 1572872 | tf_op jit(solution)/shard_map/ppermute | solution.py:402
  105.4 26.3 %collective-permute-start.7 = (bf16[1024,256]{1,0:T(8,128)(2,1)}, bf16[1024,256]{1,0:T(8,128)(2,1)S(1)}, u32[]{:S(2)}, u32[]{:S(2)}) collective-permute-start(bf16[1024,256]{1,0:T(8,128)(2,1)} %collective-permute-done.6.refs_5_.refs_3_), channel_id=1, source_target_pairs={{23,7},{24,8}} | collective-permute-start | bytes 1572872 | tf_op jit(solution)/shard_map/ppermute | solution.py:402
  106.2 26.3 %collective-permute-start.13 = (bf16[1024,256]{1,0:T(8,128)(2,1)}, bf16[1024,256]{1,0:T(8,128)(2,1)S(1)}, u32[]{:S(2)}, u32[]{:S(2)}) collective-permute-start(bf16[1024,256]{1,0:T(8,128)(2,1)} %copy-done.4), channel_id=1, source_target_pairs={{19,3},{28,12}} | collective-permute-start | bytes 1572872 | tf_op jit(solution)/shard_map/ppermute | solution.py:402
  106.9 8.6 %copy-start.17 = (s32[2048]{0:T(1024)S(1)}, s32[2048]{0:T(1024)}, u32[]{:S(2)}) copy-start(s32[2048]{0:T(1024)} %param.14) | copy-start | bytes 24580
  106.9 9.2 %copy-start.14 = (f32[1024,1]{1,0:T(8,128)S(1)}, f32[1024,1]{1,0:T(8,128)}, u32[]{:S(2)}) copy-start(f32[1024,1]{1,0:T(8,128)} %copy.13.refs_4_) | copy-start | bytes 12292
  106.9 9.2 %copy-start.15 = (f32[1024,1]{1,0:T(8,128)S(1)}, f32[1024,1]{1,0:T(8,128)}, u32[]{:S(2)}) copy-start(f32[1024,1]{1,0:T(8,128)} %copy.14.refs_5_) | copy-start | bytes 12292
  109.3 19.1 %collective-permute-start.22 = (bf16[1024,256]{1,0:T(8,128)(2,1)S(1)}, bf16[1024,256]{1,0:T(8,128)(2,1)S(1)}, u32[]{:S(2)}, u32[]{:S(2)}) collective-permute-start(bf16[1024,256]{1,0:T(8,128)(2,1)S(1)} %maximum_select_fusion.11), channel_id=1, source_target_pairs={{0,1},{1,2},{2,3},{10,11},{21,20},{26,27}} | collective-permute-start | bytes 1572872 | tf_op jit(solution)/shard_map/ppermute | solution.py:392
  114.1 15.6 %collective-permute-start.21 = (bf16[1024,256]{1,0:T(8,128)(2,1)S(1)}, bf16[1024,256]{1,0:T(8,128)(2,1)S(1)}, u32[]{:S(2)}, u32[]{:S(2)}) collective-permute-start(bf16[1024,256]{1,0:T(8,128)(2,1)S(1)} %maximum_select_fusion.10), channel_id=1, source_target_pairs={{9,8},{17,16},{18,17},{19,18},{25,24},{30,31}} | collective-permute-start | bytes 1572872 | tf_op jit(solution)/shard_map/ppermute | solution.py:392
  116.1 12.2 %copy-start.3 = (bf16[1024,256]{1,0:T(8,128)(2,1)S(1)}, bf16[1024,256]{1,0:T(8,128)(2,1)}, u32[]{:S(2)}) copy-start(bf16[1024,256]{1,0:T(8,128)(2,1)} %copy-done.2) | copy-start | bytes 1572868
  116.1 17.2 %copy-start.5 = (bf16[1024,256]{1,0:T(8,128)(2,1)S(1)}, bf16[1024,256]{1,0:T(8,128)(2,1)}, u32[]{:S(2)}) copy-start(bf16[1024,256]{1,0:T(8,128)(2,1)} %copy-done.4) | copy-start | bytes 1572868
  116.2 17.2 %copy-start.7 = (bf16[1024,256]{1,0:T(8,128)(2,1)S(1)}, bf16[1024,256]{1,0:T(8,128)(2,1)}, u32[]{:S(2)}) copy-start(bf16[1024,256]{1,0:T(8,128)(2,1)} %copy-done.6) | copy-start | bytes 1572868
  116.2 17.2 %copy-start.9 = (bf16[1024,256]{1,0:T(8,128)(2,1)S(1)}, bf16[1024,256]{1,0:T(8,128)(2,1)}, u32[]{:S(2)}) copy-start(bf16[1024,256]{1,0:T(8,128)(2,1)} %copy-done.8) | copy-start | bytes 1572868
  116.2 17.2 %copy-start.11 = (bf16[1024,256]{1,0:T(8,128)(2,1)S(1)}, bf16[1024,256]{1,0:T(8,128)(2,1)}, u32[]{:S(2)}) copy-start(bf16[1024,256]{1,0:T(8,128)(2,1)} %copy-done.10) | copy-start | bytes 1572868
  116.2 17.2 %copy-start.13 = (bf16[1024,256]{1,0:T(8,128)(2,1)S(1)}, bf16[1024,256]{1,0:T(8,128)(2,1)}, u32[]{:S(2)}) copy-start(bf16[1024,256]{1,0:T(8,128)(2,1)} %copy-done.12) | copy-start | bytes 1572868
  128.4 15.1 %copy-start.1 = (bf16[1024,2048]{1,0:T(8,128)(2,1)}, bf16[1024,2048]{1,0:T(8,128)(2,1)S(1)}, u32[]{:S(2)}) copy-start(bf16[1024,2048]{1,0:T(8,128)(2,1)S(1)} %window.1.refs_14_.refs_18_.refs_22_) | copy-start | bytes 12582916
  128.4 23.8 %collective-permute-start.12 = (bf16[1024,256]{1,0:T(8,128)(2,1)S(1)}, bf16[1024,256]{1,0:T(8,128)(2,1)S(1)}, u32[]{:S(2)}, u32[]{:S(2)}) collective-permute-start(bf16[1024,256]{1,0:T(8,128)(2,1)S(1)} %copy-done.3), channel_id=1, source_target_pairs={{0,16},{23,7}} | collective-permute-start | bytes 1572872 | tf_op jit(solution)/shard_map/ppermute | solution.py:402
  129.7 22.5 %collective-permute-start.18 = (bf16[1024,256]{1,0:T(8,128)(2,1)}, bf16[1024,256]{1,0:T(8,128)(2,1)S(1)}, u32[]{:S(2)}, u32[]{:S(2)}) collective-permute-start(bf16[1024,256]{1,0:T(8,128)(2,1)} %collective-permute-done.16.refs_10_), channel_id=1, source_target_pairs={{19,3}} | collective-permute-start | bytes 1572872 | tf_op jit(solution)/shard_map/ppermute | solution.py:402
  130.5 21.8 %collective-permute-start.17 = (bf16[1024,256]{1,0:T(8,128)(2,1)}, bf16[1024,256]{1,0:T(8,128)(2,1)S(1)}, u32[]{:S(2)}, u32[]{:S(2)}) collective-permute-start(bf16[1024,256]{1,0:T(8,128)(2,1)} %collective-permute-done.15.refs_9_), channel_id=1, source_target_pairs={{0,16}} | collective-permute-start | bytes 1572872 | tf_op jit(solution)/shard_map/ppermute | solution.py:402
  131.8 20.4 %collective-permute-start.24 = (bf16[1024,256]{1,0:T(8,128)(2,1)S(1)}, bf16[1024,256]{1,0:T(8,128)(2,1)S(1)}, u32[]{:S(2)}, u32[]{:S(2)}) collective-permute-start(bf16[1024,256]{1,0:T(8,128)(2,1)S(1)} %collective-permute-done.22.refs_14_.refs_16_), channel_id=1, source_target_pairs={{1,2}} | collective-permute-start | bytes 1572872 | tf_op jit(solution)/shard_map/ppermute | solution.py:392
  132.5 19.7 %collective-permute-start.23 = (bf16[1024,256]{1,0:T(8,128)(2,1)S(1)}, bf16[1024,256]{1,0:T(8,128)(2,1)S(1)}, u32[]{:S(2)}, u32[]{:S(2)}) collective-permute-start(bf16[1024,256]{1,0:T(8,128)(2,1)S(1)} %collective-permute-done.21.refs_13_.refs_15_), channel_id=1, source_target_pairs={{18,17}} | collective-permute-start | bytes 1572872 | tf_op jit(solution)/shard_map/ppermute | solution.py:392

commit v5 on v4

v5 whole, which is shorter than its diff:
```python
import functools
import itertools

import jax
import jax.numpy as jnp
import numpy as np
from jax import lax
from jax.experimental import pallas as pl
from jax.experimental.pallas import tpu as pltpu
from jax.sharding import PartitionSpec as P

STEPS = 4
PIECES = 2
DEPTH = 2
FLIGHT = 3
HOP = 2
COL_TILE = 512
ROW_TILE = 32
VMEM_LIMIT = 60 * 2**20


class Item:
    def __init__(self, row, piece, s, place, home=None):
        self.row, self.piece, self.s, self.place = row, piece, s, place
        self.home = home

    @property
    def owner(self):
        return self.row if self.home is None else self.home

    @property
    def key(self):
        return self.piece, self.s


def line_slots(items, cut):
    ends, inner = {}, {}
    todo = sorted(items, key=lambda i: (i.home is None, i.piece, i.place, i.s))
    slot = 1
    while todo:
        for item in todo:
            first = 1 + DEPTH * (item.place - 1) + (HOP if item.home is not None else 0)
            if first <= slot:
                ends[slot] = item
                if item.place > 1:
                    inner[slot] = item
                todo.remove(item)
                break
        slot += 1
    for item in sorted(cut, key=lambda i: (i.place, i.key)):
        slot = 1 + DEPTH * (item.place - 1)
        if item.place > 1:
            while slot in inner:
                slot += 1
            inner[slot] = item
    return ends, inner


class Lane:
    def __init__(self, rows, cols, groups_here, towards_zero):
        self.rows, self.cols = rows, cols
        self.towards_zero = towards_zero
        self.items = []
        for r in range(rows):
            mine = [
                Item(r, piece, s, self.place((r + s) % rows // groups_here))
                for piece in range(PIECES)
                for s in range(STEPS)
            ]
            self.items.append([i for i in mine if i.place > 0])
        self.away = []
        self.lines = [line_slots(items, []) for items in self.items]
        if rows % 2 == 0 and cols > 3:
            for r in range(rows // 2):
                self.balance(r, r + rows // 2)
                self.balance(r + rows // 2, r)
        self.rounds = max(
            [max(ends, default=0) for ends, _ in self.lines] + [max(inner, default=0) - DEPTH for _, inner in self.lines]
        )

    def place(self, c):
        return c if self.towards_zero else self.cols - 1 - c

    col = place

    def balance(self, r, other):
        if len(self.items[r]) < len(self.items[other]) or any(i.row == other for i in self.away):
            return
        places = sorted({i.place for i in self.items[r]})
        best = None
        for counts in itertools.product(range(3), repeat=len(places)):
            gone = []
            for place, count in zip(places, counts):
                here = [i for i in self.items[r] if i.place == place]
                here.sort(key=lambda i: i.key, reverse=True)
                gone += here[:count]
            visitors = [Item(other, i.piece, i.s, i.place, home=r) for i in gone]
            mine = line_slots([i for i in self.items[r] if i not in gone], gone)
            theirs = line_slots(self.items[other] + visitors, [])
            score = (
                max(max(mine[0], default=0), max(theirs[0], default=0)),
                abs(len(mine[0]) - len(theirs[0])),
                max([slot for slot, i in theirs[0].items() if i.home is not None], default=0),
                len(gone),
            )
            if best is None or score < best[0]:
                best = score, gone, mine, theirs
        _, gone, mine, theirs = best
        self.away += gone
        if gone:
            self.lines[r], self.lines[other] = mine, theirs

    def sent(self, r, c, t):
        p = self.place(c)
        ends, inner = self.lines[r]
        if p == 0:
            return None
        item = ends.get(t) if p == 1 else inner.get(t + DEPTH * (p - 1))
        return item if item is not None and item.place >= p else None

    def pairs(self, t):
        found = []
        for r in range(self.rows):
            for c in range(self.cols):
                if self.sent(r, c, t) is not None:
                    found.append((r * self.cols + c, r * self.cols + self.col(self.place(c) - 1)))
        return found

    def arrival(self, r, c, key):
        p = self.place(c)
        for i in self.items[r]:
            if i.key != key or i.place <= p:
                continue
            ends, inner = self.lines[r]
            if p == 0 and i in self.away:
                for other, _ in self.lines:
                    for slot, v in other.items():
                        if v.home == r and v.key == key:
                            return slot, True
            for slot, v in (ends if p == 0 else inner).items():
                if v is i:
                    return slot - DEPTH * p, False
        return None


def lookup(values, device):
    known = [v for v in values if v is not None]
    if len(set(known)) <= 1:
        return known[0] if known else 0
    values = [known[0] if v is None else v for v in values]
    result = jnp.uint32(0)
    place = (device % 32).astype(jnp.uint32)
    for bit in range(max(values).bit_length()):
        ones = [v >> bit & 1 for v in values]
        words = [sum(b << i for i, b in enumerate(ones[at : at + 32])) for at in range(0, len(ones), 32)]
        word = jnp.uint32(words[0])
        for i, other in enumerate(words[1:], 1):
            word = jnp.where(device // 32 == i, jnp.uint32(other), word)
        result = result | (((word >> place) & jnp.uint32(1)) << jnp.uint32(bit))
    return result.astype(jnp.int32)


def window_kernel(*refs):
    blocks = refs[:STEPS]
    factor, twice, male, out = refs[STEPS:]
    group_size = blocks[0].shape[0]
    for s, block in enumerate(blocks):

        @pl.loop(0, group_size // ROW_TILE)
        def _(i, s=s, block=block):
            here = pl.ds(pl.multiple_of(i * ROW_TILE, ROW_TILE), ROW_TILE)
            rows = pl.ds(pl.multiple_of(s * group_size + i * ROW_TILE, ROW_TILE), ROW_TILE)
            value = block[here, :].astype(jnp.float32) - twice[rows, :]
            out[rows, :] = (value * factor[rows, :] * male[...]).astype(out.dtype)


def standardized_window(blocks, factor, twice, male):
    group_size, n = blocks[0].shape
    depth = STEPS * group_size
    column = lambda j: (0, 0)
    return pl.pallas_call(
        window_kernel,
        out_shape=jax.ShapeDtypeStruct((depth, n), jnp.bfloat16),
        grid=(n // COL_TILE,),
        in_specs=[pl.BlockSpec((group_size, COL_TILE), lambda j: (0, j))] * STEPS
        + [pl.BlockSpec((depth, 1), column)] * 2
        + [pl.BlockSpec((1, COL_TILE), lambda j: (0, j))],
        out_specs=pl.BlockSpec((depth, COL_TILE), lambda j: (0, j)),
        compiler_params=pltpu.CompilerParams(vmem_limit_bytes=VMEM_LIMIT),
        cost_estimate=pl.CostEstimate(flops=4 * depth * n, bytes_accessed=4 * depth * n, transcendentals=0),
        name="window",
    )(*blocks, factor, twice, male)


def product_kernel(piece, candidates, scale, n_buffers, places, *refs):
    x, buffers = refs[0], refs[1 : 1 + n_buffers]
    factor, twice, male, zy = refs[1 + n_buffers : 5 + n_buffers]
    out, raw, zx, sems = refs[-4:]
    piece_rows = raw.shape[0]
    width = raw.shape[1] // STEPS

    @pl.when(pl.program_id(0) == 0)
    def _():
        for s in range(STEPS):
            place = places[s]
            target = raw.at[:, pl.ds(s * width, width)]
            for number in candidates[s]:
                if number >= 0:

                    @pl.when(place == number)
                    def _(number=number, target=target, s=s):
                        pltpu.make_async_copy(buffers[number], target, sems.at[s]).start()

                else:

                    @pl.when(place < 0)
                    def _(place=place, target=target, s=s):
                        col = pl.multiple_of((-1 - place) * width, width)
                        block = x.at[pl.ds(piece * piece_rows, piece_rows), pl.ds(col, width)]
                        pltpu.make_async_copy(block, target, sems.at[s]).start()

        for s in range(STEPS):
            part = raw.at[:, pl.ds(s * width, width)]
            pltpu.make_async_copy(part, part, sems.at[s]).wait()

        @pl.loop(0, piece_rows // ROW_TILE)
        def _(i):
            rows = pl.ds(pl.multiple_of(i * ROW_TILE, ROW_TILE), ROW_TILE)
            value = raw[rows, :].astype(jnp.float32) - twice[...]
            zx[rows, :] = (value * factor[...] * male[rows, :]).astype(zx.dtype)

    total = jnp.dot(zx[...], zy[...], preferred_element_type=jnp.float32)
    out[...] = (total * scale).astype(out.dtype)


def product(piece, places, candidates, x, buffers, factor, twice, male, zy, before):
    rows, (depth, n) = x.shape[0], zy.shape
    piece_rows = rows // PIECES
    scale = float(1.0 / np.sqrt(np.float32(depth)))
    whole = lambda j, places: (0, 0)
    specs = [pl.BlockSpec(memory_space=pl.ANY)] * (1 + len(buffers)) + [
        pl.BlockSpec((1, depth), whole),
        pl.BlockSpec((1, depth), whole),
        pl.BlockSpec((piece_rows, 1), lambda j, places: (piece, 0)),
        pl.BlockSpec((depth, COL_TILE), lambda j, places: (0, j)),
    ]
    args = [places, x, *buffers, factor, twice, male, zy]
    aliases = {}
    if before is not None:
        aliases = {len(args): 0}
        specs.append(pl.BlockSpec(memory_space=pl.ANY))
        args.append(before)
    return pl.pallas_call(
        functools.partial(product_kernel, piece, candidates, scale, len(buffers)),
        out_shape=jax.ShapeDtypeStruct((rows, n), jnp.bfloat16),
        grid_spec=pltpu.PrefetchScalarGridSpec(
            num_scalar_prefetch=1,
            grid=(n // COL_TILE,),
            in_specs=specs,
            out_specs=pl.BlockSpec((piece_rows, COL_TILE), lambda j, places: (piece, j)),
            scratch_shapes=[
                pltpu.VMEM((piece_rows, depth), jnp.bfloat16),
                pltpu.VMEM((piece_rows, depth), jnp.bfloat16),
                pltpu.SemaphoreType.DMA((STEPS,)),
            ],
        ),
        input_output_aliases=aliases,
        compiler_params=pltpu.CompilerParams(vmem_limit_bytes=VMEM_LIMIT),
        cost_estimate=pl.CostEstimate(
            flops=2 * piece_rows * depth * n,
            bytes_accessed=2 * (piece_rows * depth + depth * n + piece_rows * n),
            transcendentals=0,
        ),
        name="product",
    )(*args)


def local(rows, cols, x, y, freq, weight, sex_rows, sex_cols):
    group_size = y.shape[0]
    local_vars = x.shape[1]
    groups_here = local_vars // group_size
    piece_rows = x.shape[0] // PIECES
    lanes = [Lane(rows, cols, groups_here, towards) for towards in (True, False)]
    rounds = max(lane.rounds for lane in lanes)
    devices = [(r, c) for r in range(rows) for c in range(cols)]
    both = ("row", "col")

    row_place = lax.axis_index("row")
    col_place = lax.axis_index("col")
    device = row_place * cols + col_place

    def number(r, c):
        return r * cols + c

    chain = [x]

    def after(*values):
        *values, chain[0] = lax.optimization_barrier((*values, chain[0]))
        return values[0] if len(values) == 1 else values

    def own_chunk(items):
        piece = lookup([None if i is None else i.piece for i in items], device)
        group = lookup([None if i is None else (i.owner + i.s) % rows % groups_here for i in items], device)
        return lax.dynamic_slice(chain[0], (piece * piece_rows, group * group_size), (piece_rows, group_size))

    crossings = []
    crossing_of = {}
    for d, lane in enumerate(lanes):
        for r in range(rows):
            for slot, item in sorted(lane.lines[r][0].items()):
                if item.home is None:
                    continue
                source, target = (item.home, lane.col(item.place)), (r, lane.col(item.place))
                for k, crossing in enumerate(crossings):
                    if source not in crossing and target not in [to for to, _ in crossing.values()]:
                        break
                else:
                    k = len(crossings)
                    crossings.append({})
                crossings[k][source] = (target, item)
                crossing_of[d, r, item.key] = k

    def lane_of(phase, r):
        return (r + phase) % 2

    buffers = {}
    crossed = {}

    def send(phase, t):
        lane = {r: lanes[lane_of(phase, r)] for r in range(rows)}
        sent = [lane[r].sent(r, c, t) for r, c in devices]
        pairs = [
            (number(r, c), number(r, lane[r].col(lane[r].place(c) - 1)))
            for i, (r, c) in zip(sent, devices)
            if i is not None
        ]
        if not pairs:
            return
        kinds = []
        for i, (r, c) in zip(sent, devices):
            if i is None:
                kinds.append(None)
            elif i.place != lane[r].place(c):
                kinds.append(1)
            elif i.home is None:
                kinds.append(0)
            else:
                kinds.append(2 + crossing_of[lane_of(phase, r), r, i.key])
        held = None
        sources = [k for k in sorted(set(kinds) - {None}) if k]
        found = [buffers[phase, t - DEPTH] if k == 1 else crossed[k - 2] for k in sources]
        if 0 in kinds:
            held = own_chunk([i if k == 0 else None for i, k in zip(sent, kinds)])
        for kind, buffer in zip(sources, found):
            if held is not None:
                mask = lookup([None if v is None else int(v == kind) for v in kinds], device)
                buffer = jnp.where(mask == 1, buffer, held)
            held = buffer
        buffers[phase, t] = lax.ppermute(after(held), both, pairs)

    def cross(crossing):
        held = own_chunk([crossing[rc][1] if rc in crossing else None for rc in devices])
        pairs = [(number(*rc), number(*to)) for rc, (to, _) in crossing.items()]
        return lax.ppermute(after(held), both, pairs)

    def bring_back(t):
        pairs, phase_at = [], [None] * len(devices)
        for d, lane in enumerate(lanes):
            for r in range(rows):
                item = lane.lines[r][0].get(t)
                if item is not None and item.home is not None:
                    pairs.append((number(r, lane.col(0)), number(item.home, lane.col(0))))
                    phase_at[pairs[-1][0]] = (r + d) % 2
        if not pairs:
            return None
        phases = sorted(set(phase_at) - {None})
        held = buffers[phases[0], t]
        if len(phases) > 1:
            held = jnp.where(lookup(phase_at, device) == 1, buffers[1, t], held)
        return lax.ppermute(held, both, pairs)

    factor = weight / jnp.sqrt(2.0 * freq * (1.0 - freq))
    twice = 2.0 * freq
    male_scale = np.float32(np.sqrt(0.5))
    male_rows = jnp.where(sex_rows > 0, male_scale, np.float32(1.0))[:, None]
    male_cols = jnp.where(sex_cols > 0, male_scale, np.float32(1.0))[None, :]

    def in_window(value):
        span = STEPS * group_size
        return lax.dynamic_slice(jnp.concatenate([value, value]), (row_place * group_size,), (span,))

    def own_squares(x):
        here = lambda value: lax.dynamic_slice(value, (col_place * local_vars,), (local_vars,))[None, :]
        zx = ((x.astype(jnp.float32) - here(twice)) * here(factor) * male_rows).astype(jnp.bfloat16)
        return jnp.sum(jnp.square(zx.astype(jnp.float32)), axis=1)

    def piece_product(piece, zy, before):
        found = []
        for r, c in devices:
            keys = []
            for s in range(STEPS):
                key = -1 - (r + s) % rows % groups_here
                for d, lane in enumerate(lanes):
                    arrival = lane.arrival(r, c, (piece, s))
                    if arrival is not None:
                        t, returned = arrival
                        key = ("back" if returned else (r + d) % 2, t)
                keys.append(key)
            found.append(keys)
        used = sorted({k for keys in found for k in keys if isinstance(k, tuple)}, key=lambda k: (k[1], str(k[0])))
        places = [[k if isinstance(k, int) else used.index(k) for k in keys] for keys in found]
        places = np.asarray(places, np.int32)
        candidates = [sorted({max(int(k), -1) for k in places[:, s]}) for s in range(STEPS)]
        places = lax.dynamic_slice(jnp.asarray(places), (device, 0), (1, STEPS))[0]
        held = [buffers[key] for key in used]
        window_factor, window_twice = in_window(factor)[None, :], in_window(twice)[None, :]
        return product(piece, places, candidates, x, after(*held), window_factor, window_twice, male_rows, zy, before)

    later = []

    def join_later(place, put, value):
        later.append((place, put, value))

    def join(place):
        for entry in [e for e in later if e[0] <= place]:
            later.remove(entry)
            _, put, value = entry
            put(after(value))

    window = [y]
    back = [(i, (i - 1) % rows) for i in range(rows)]
    squares = [None]
    bits = [1 << k for k in range(cols.bit_length() - 1)] if cols & (cols - 1) == 0 else []

    def start_window(place):
        if len(window) < STEPS:

            def put(value):
                window.append(value)
                start_window(place + 3)

            join_later(place + 3, put, lax.ppermute(after(window[-1]), "row", back))

    def start_cross(place, todo):
        if todo:

            def put(value):
                crossed[len(crossed)] = value
                start_cross(place + 2, todo[1:])

            join_later(place + 2, put, cross(todo[0]))

    def start_sum(place):
        if bits:
            bit = bits.pop(0)

            def put(value):
                squares[0] = squares[0] + value
                start_sum(place + 3)

            join_later(place + 3, put, lax.ppermute(squares[0], "col", [(i, i ^ bit) for i in range(cols)]))

    def landed(phase, t, place):
        if (phase, t) in buffers:
            buffers[phase, t] = after(buffers[phase, t])
        returned = bring_back(t) if phase == 1 else None
        if returned is not None:
            join_later(place + 2, lambda value: buffers.__setitem__(("back", t), value), returned)

    sends = [(phase, t) for t in range(1, rounds + 1) for phase in range(2)]
    relation = zy = None
    done = 0
    last = {}
    for piece in range(PIECES):
        last[piece] = 0
        for d, lane in enumerate(lanes):
            for r, c in devices:
                for s in range(STEPS):
                    arrival = lane.arrival(r, c, (piece, s))
                    if arrival is not None:
                        t, returned = arrival
                        place = sends.index((1 if returned else (r + d) % 2, t)) + FLIGHT + (2 if returned else 0)
                        last[piece] = max(last[piece], place)
    for place, (phase, t) in enumerate(sends):
        if place >= FLIGHT:
            landed(*sends[place - FLIGHT], place)
        join(place)
        send(phase, t)
        if place == 1:
            start_cross(place, crossings)
            start_window(place)
        if place == 2:
            squares[0] = after(own_squares(chain[0]))
        if place == 7:
            start_sum(place)
        if len(window) == STEPS and zy is None:
            zy = standardized_window(after(*window), in_window(factor)[:, None], in_window(twice)[:, None], male_cols)
            zy = after(zy)
        while zy is not None and done < PIECES - 1 and last[done] <= place:
            relation = after(piece_product(done, zy, relation))
            done += 1
    for place in range(len(sends), len(sends) + FLIGHT):
        landed(*sends[place - FLIGHT], place)
        join(place)
    while later:
        join(max(place for place, _, _ in later))
    if not cols & (cols - 1) == 0:
        squares[0] = lax.psum(squares[0], "col")
    inbreeding = squares[0] / jnp.float32(freq.shape[0]) - 1.0
    if zy is None:
        zy = standardized_window(window, in_window(factor)[:, None], in_window(twice)[:, None], male_cols)
    for piece in range(done, PIECES):
        relation = piece_product(piece, zy, relation)
    return relation, inbreeding


def solution(mesh):
    rows, cols = mesh.shape["row"], mesh.shape["col"]
    return jax.shard_map(
        functools.partial(local, rows, cols),
        mesh=mesh,
        in_specs=(P("row", "col"), P("row", "col"), P(), P(), P("row"), P("col")),
        out_specs=(P("row", "col"), P("row")),
        check_vma=False,
    )
```

time: 162 us -> 171 us (1.056)
  the two profiles are of different devices: /device:TPU:0 before, /device:TPU:14 now
where the time goes in v5:
time: 171 us; the launch traced here: 170 us
  waiting for transfers between devices  50.8 us (30%)
  starting transfers between devices  48.2 us (28%)
  Pallas kernels  38.5 us (23%)
  other arithmetic  17.5 us (10%)
  local copies, waits for them, and re-layouts  13.7 us (8%)
    ppermute x2, waiting for transfers between devices, cross(): return lax.ppermute(after(held), both, pairs)  37.5 us
    ppermute x16, starting transfers between devices, send(): buffers[phase, t] = lax.ppermute(after(held), both, pairs)  37.1 us
    pallas_call x2, Pallas kernels, product(): pl.pallas_call(functools.partial(product_kernel, piece, candidates, scale...  25.2 us
    ppermute x16, waiting for transfers between devices, send(): buffers[phase, t] = lax.ppermute(after(held), both, pairs)  13.3 us
    pallas_call x1, Pallas kernels, standardized_window(): pl.pallas_call(window_kernel, out_shape=jax.ShapeDtypeStruct((depth, n),...  13.3 us
    select_n x10, other arithmetic, send(): buffer = jnp.where(mask == 1, buffer, held)  12.1 us
    dynamic_slice x6, local copies, waits for them, and re-layouts, own_chunk(): lax.dynamic_slice(chain[0], (piece * piece_rows, group * group_size), (pi...  7.29 us
    ppermute x5, starting transfers between devices, bring_back(): return lax.ppermute(held, both, pairs)  4.99 us
  transfers between devices with their start and end apart: 28, of which 6 were waited for; matrix products, arithmetic and copies ran while one was open for 15% of the time, Pallas kernels for 15%

profile of v5, /device:TPU:14, one launch (start us, length us, event | category | flops | bytes accessed | tf_op | source)
XLA Modules:
  0.0 169.8 jit_solution(12088288047800781742)
XLA Ops:
  0.7 2.0 %constant_dynamic-slice_fusion.3 = bf16[1024,256]{1,0:T(8,128)(2,1)} fusion(bf16[2048,512]{1,0:T(8,128)(2,1)} %refs_0_.4, s32[]{:T(128)S(6)} %select_n.247), kind=kLoop, calls=%fused_computation.31 | loop fusion | bytes 1048580 | tf_op jit(solution)/shard_map/dynamic_slice | solution.py:304
  2.7 1.9 %constant_dynamic-slice_fusion.2 = bf16[1024,256]{1,0:T(8,128)(2,1)} fusion(bf16[2048,512]{1,0:T(8,128)(2,1)} %refs_0_.4, s32[]{:T(128)S(6)} %select_n.248), kind=kLoop, calls=%fused_computation.30 | loop fusion | bytes 1048580 | tf_op jit(solution)/shard_map/dynamic_slice | solution.py:304
  4.6 0.8 constant_dynamic-slice_fusion
  5.5 0.8 dynamic_slice.74
  6.3 0.7 collective-permute-start
  7.0 1.3 collective-permute-start.1
  8.3 1.3 collective-permute-start.4
  9.6 1.5 collective-permute-start.2
  11.1 0.1 dynamic_slice.75
  11.3 1.0 multiply_reduce_fusion
  12.4 19.7 %collective-permute-done.1 = bf16[1024,256]{1,0:T(8,128)(2,1)} collective-permute-done((bf16[1024,256]{1,0:T(8,128)(2,1)}, bf16[1024,256]{1,0:T(8,128)(2,1)}, u32[]{:S(2)}, u32[]{:S(2)}) %collective-permute-start.1) | collective-permute-done | bytes 524320 | tf_op jit(solution)/shard_map/ppermute | solution.py:364
  32.1 0.8 dynamic_slice.77
  32.9 1.3 collective-permute-start.6
  34.2 0.9 dynamic_slice.78
  35.2 1.3 collective-permute-start.5
  36.5 1.2 select_select_fusion.3
  37.7 17.8 %collective-permute-done.6 = bf16[1024,256]{1,0:T(8,128)(2,1)} collective-permute-done((bf16[1024,256]{1,0:T(8,128)(2,1)}, bf16[1024,256]{1,0:T(8,128)(2,1)}, u32[]{:S(2)}, u32[]{:S(2)}) %collective-permute-start.6) | collective-permute-done | bytes 524320 | tf_op jit(solution)/shard_map/ppermute | solution.py:364
  55.5 1.9 %collective-permute-start.7 = (bf16[1024,256]{1,0:T(8,128)(2,1)S(1)}, bf16[1024,256]{1,0:T(8,128)(2,1)S(1)}, u32[]{:S(2)}, u32[]{:S(2)}) collective-permute-start(bf16[1024,256]{1,0:T(8,128)(2,1)S(1)} %select_select_fusion.3), channel_id=1, source_target_pairs={{1,0},{2,1},{3,2},{4,5},{5,6},{6,7},{9,8},{10,9},{12,13},{14,15},{... | collective-permute-start | bytes 1572872 | tf_op jit(solution)/shard_map/ppermute | solution.py:359
  57.4 0.2 select_select_fusion.2
  57.7 5.0 %collective-permute-start.8 = (bf16[1024,256]{1,0:T(8,128)(2,1)S(1)}, bf16[1024,256]{1,0:T(8,128)(2,1)S(1)}, u32[]{:S(2)}, u32[]{:S(2)}) collective-permute-start(bf16[1024,256]{1,0:T(8,128)(2,1)S(1)} %select_select_fusion.2), channel_id=1, source_target_pairs={{0,1},{1,2},{2,3},{5,4},{7,6},{9,10},{10,11},{13,12},{14,13},{15,1... | collective-permute-start | bytes 1572872 | tf_op jit(solution)/shard_map/ppermute | solution.py:359
  62.6 1.3 select_select_fusion.1
  63.9 1.9 %collective-permute-start.14 = (bf16[1024,256]{1,0:T(8,128)(2,1)S(1)}, bf16[1024,256]{1,0:T(8,128)(2,1)S(1)}, u32[]{:S(2)}, u32[]{:S(2)}) collective-permute-start(bf16[1024,256]{1,0:T(8,128)(2,1)S(1)} %select_select_fusion.1), channel_id=1, source_target_pairs={{1,0},{2,1},{5,6},{6,7},{9,8},{10,9},{13,14},{14,15},{17,16},{18,1... | collective-permute-start | bytes 1572872 | tf_op jit(solution)/shard_map/ppermute | solution.py:359
  65.8 0.7 collective-permute-done.7.refs_5_.refs_3_
  66.6 1.0 select_select_fusion
  67.6 1.7 collective-permute-done.8.refs_6_.refs_4_
  69.3 0.9 slice_select_fusion.3
  70.2 4.7 %collective-permute-done.14.refs_7_.refs_6_ = bf16[1024,256]{1,0:T(8,128)(2,1)S(1)} collective-permute-done((bf16[1024,256]{1,0:T(8,128)(2,1)S(1)}, bf16[1024,256]{1,0:T(8,128)(2,1)S(1)}, u32[]{:S(2)}, u32[]{:S(2)}) %collective-permute-start.14) | collective-permute-done | bytes 524320 | tf_op jit(solution)/shard_map/ppermute | solution.py:359
  75.0 1.9 %collective-permute-start.13 = (bf16[1024,256]{1,0:T(8,128)(2,1)}, bf16[1024,256]{1,0:T(8,128)(2,1)}, u32[]{:S(2)}, u32[]{:S(2)}) collective-permute-start(bf16[1024,256]{1,0:T(8,128)(2,1)} %select_select_fusion), channel_id=1, source_target_pairs={{1,2},{2,3},{5,4},{6,5},{9,10},{10,11},{13,12},{14,13},{17,18},{18... | collective-permute-start | bytes 1572872 | tf_op jit(solution)/shard_map/ppermute | solution.py:359
  76.9 1.1 slice_select_fusion.2
  78.0 1.5 collective-permute-start.10
  79.5 3.4 %collective-permute-start.11 = (f32[2048]{0:T(1024)S(1)}, f32[2048]{0:T(1024)S(1)}, u32[]{:S(2)}, u32[]{:S(2)}) collective-permute-start(f32[2048]{0:T(1024)S(1)} %multiply_reduce_fusion), channel_id=1, source_target_pairs={{0,1},{1,0},{2,3},{3,2},{4,5},{5,4},{6,7},{7,6},{8,9},{9,8},{10,11... | collective-permute-start | bytes 24584 | tf_op jit(solution)/shard_map/ppermute | solution.py:461
  82.9 1.9 %collective-permute-start.17 = (bf16[1024,256]{1,0:T(8,128)(2,1)}, bf16[1024,256]{1,0:T(8,128)(2,1)S(1)}, u32[]{:S(2)}, u32[]{:S(2)}) collective-permute-start(bf16[1024,256]{1,0:T(8,128)(2,1)} %slice_select_fusion.3), channel_id=1, source_target_pairs={{1,0},{2,1},{5,6},{6,7},{9,8},{13,14},{14,15},{17,16},{18,17},{21,... | collective-permute-start | bytes 1572872 | tf_op jit(solution)/shard_map/ppermute | solution.py:359
  84.8 0.6 compare_select_fusion
  85.5 1.0 copy.11.refs_4_
  86.5 1.0 copy.12.refs_5_
  87.6 5.2 %collective-permute-start.16 = (bf16[1024,256]{1,0:T(8,128)(2,1)}, bf16[1024,256]{1,0:T(8,128)(2,1)}, u32[]{:S(2)}, u32[]{:S(2)}) collective-permute-start(bf16[1024,256]{1,0:T(8,128)(2,1)} %get-tuple-element.170), channel_id=1, source_target_pairs={{1,2},{2,3},{5,4},{6,5},{10,11},{13,12},{14,13},{17,18},{18,19},{2... | collective-permute-start | bytes 1572872 | tf_op jit(solution)/shard_map/ppermute | solution.py:359
  92.8 0.9 dynamic-slice_select_fusion.1
  93.8 13.3 %window.1.refs_16_.refs_23_ = bf16[1024,2048]{1,0:T(8,128)(2,1)} custom-call(bf16[256,2048]{1,0:T(8,128)(2,1)} %refs_0_.2, bf16[256,2048]{1,0:T(8,128)(2,1)} %collective-permute-done.3.refs_1_, bf16[256,2048]{1,0:T(8,128)(2,1)} %collective-permute-done.9.refs_2_, bf16[256,2048]{1,0:T(8,128)(2,1)} %collective-permute-done.12.refs_3_, ...), custom_call_target="tpu_custom_call" | custom-call | flops 8388608 | bytes 8388608 | tf_op jit(solution)/shard_map/window/pallas_call | solution.py:181
  107.1 2.5 %dynamic-slice_select_fusion = (bf16[1024,256]{1,0:T(8,128)(2,1)}, bf16[1024,256]{1,0:T(8,128)(2,1)}) fusion(bf16[1024,256]{1,0:T(8,128)(2,1)} %collective-permute-done.13.refs_8_.refs_7_, bf16[2048,512]{1,0:T(8,128)(2,1)S(1)} %copy-done, s32[]{:T(128)S(6)} %select_n.289, pred[]{:T(512)S(6)} %eq.102, ...), kind=kLoop, calls=%fused_computation.4 | loop fusion | flops 524288 | bytes 2621446 | tf_op jit(solution)/shard_map/jit(_where)/select_n | solution.py:357
  109.6 1.5 collective-permute-start.15
  111.0 1.9 %collective-permute-start.19 = (bf16[1024,256]{1,0:T(8,128)(2,1)}, bf16[1024,256]{1,0:T(8,128)(2,1)S(1)}, u32[]{:S(2)}, u32[]{:S(2)}) collective-permute-start(bf16[1024,256]{1,0:T(8,128)(2,1)} %dynamic-slice_select_fusion.1), channel_id=1, source_target_pairs={{1,0},{5,6},{6,7},{9,8},{14,15},{17,16},{18,17},{19,18},{22,23},{2... | collective-permute-start | bytes 1572872 | tf_op jit(solution)/shard_map/ppermute | solution.py:359
  113.0 4.8 %collective-permute-start.20 = (bf16[1024,256]{1,0:T(8,128)(2,1)}, bf16[1024,256]{1,0:T(8,128)(2,1)}, u32[]{:S(2)}, u32[]{:S(2)}) collective-permute-start(bf16[1024,256]{1,0:T(8,128)(2,1)} %get-tuple-element.193), channel_id=1, source_target_pairs={{0,1},{1,2},{2,3},{5,4},{10,11},{13,12},{14,13},{18,19},{21,20},{2... | collective-permute-start | bytes 1572872 | tf_op jit(solution)/shard_map/ppermute | solution.py:359
  117.8 0.9 slice_select_fusion.1
  118.7 6.1 %collective-permute-done.19.refs_11_.refs_12_ = bf16[1024,256]{1,0:T(8,128)(2,1)S(1)} collective-permute-done((bf16[1024,256]{1,0:T(8,128)(2,1)}, bf16[1024,256]{1,0:T(8,128)(2,1)S(1)}, u32[]{:S(2)}, u32[]{:S(2)}) %collective-permute-start.19) | collective-permute-done | bytes 524320 | tf_op jit(solution)/shard_map/ppermute | solution.py:359
  124.7 5.1 %collective-permute-start.22 = (bf16[1024,256]{1,0:T(8,128)(2,1)}, bf16[1024,256]{1,0:T(8,128)(2,1)}, u32[]{:S(2)}, u32[]{:S(2)}) collective-permute-start(bf16[1024,256]{1,0:T(8,128)(2,1)} %slice_select_fusion.1), channel_id=1, source_target_pairs={{1,0},{6,7},{14,15},{17,16},{18,17},{22,23},{25,24},{30,31}} | collective-permute-start | bytes 1572872 | tf_op jit(solution)/shard_map/ppermute | solution.py:359
  129.8 2.1 %slice_select_fusion = (bf16[1024,256]{1,0:T(8,128)(2,1)}, bf16[1024,256]{1,0:T(8,128)(2,1)}) fusion(bf16[1024,256]{1,0:T(8,128)(2,1)} %collective-permute-done.16.refs_10_, bf16[2048,512]{1,0:T(8,128)(2,1)S(1)} %copy-done, pred[]{:T(512)S(6)} %eq.107, bf16[1024,256]{1,0:T(8,128)(2,1)S(1)} %collective-permute-done.17.refs_9_, pred[]{:T(512)S(6)} %eq.104), kind=kLoop, calls=%fused_computation.2 | loop fusion | flops 524288 | bytes 2621442 | tf_op jit(solution)/shard_map/jit(_where)/select_n | solution.py:357
  131.9 0.7 collective-permute-start.24
  132.6 1.4 copy.14.refs_15_.refs_22_
  134.0 1.3 fusion.2
  135.3 0.7 collective-permute-start.27
  136.0 0.9 broadcast_select_fusion.1
  136.9 0.7 collective-permute-start.21
  137.6 1.3 collective-permute-start.26
  138.9 0.7 collective-permute-start.18
  139.6 2.1 %broadcast_select_fusion = bf16[1024,256]{1,0:T(8,128)(2,1)} fusion(bf16[1024,256]{1,0:T(8,128)(2,1)S(1)} %collective-permute-done.24.refs_16_, bf16[1024,256]{1,0:T(8,128)(2,1)} %collective-permute-done.22.refs_15_, pred[]{:T(512)S(6)} %eq.108), kind=kLoop, calls=%fused_computation.12 | loop fusion | flops 262144 | bytes 1572865 | tf_op jit(solution)/shard_map/jit(_where)/select_n | solution.py:379
  141.7 0.7 collective-permute-start.25
  142.4 12.6 %product.2.refs_24_ = bf16[2048,2048]{1,0:T(8,128)(2,1)} custom-call(s32[4]{0:T(128)} %get-tuple-element.241.places, bf16[2048,512]{1,0:T(8,128)(2,1)} %refs_0_.4, bf16[1024,256]{1,0:T(8,128)(2,1)} %collective-permute-done.2.refs_1_, bf16[1024,256]{1,0:T(8,128)(2,1)} %copy-done.9, bf16[1024,256]{1,0:T(8,128)(2,1)} %copy-done.6, bf16[1024,256]{1,0:T(8,128)(2,1)} %copy-done.7, ...), custom_call_target="tpu_custom_call" | custom-call | flops 4294967296 | bytes 10485760 | tf_op jit(solution)/shard_map/product/pallas_call | solution.py:253
  155.1 0.6 multiply_add_fusion
  155.8 0.8 copy-done.10
  156.5 0.1 copy-done.11
  156.7 0.2 copy-done.12
  156.9 0.2 copy-done.13
  157.0 0.2 copy-done.14
  157.2 12.6 %product.3 = bf16[2048,2048]{1,0:T(8,128)(2,1)} custom-call(s32[4]{0:T(128)} %get-tuple-element.240.places, bf16[2048,512]{1,0:T(8,128)(2,1)} %refs_0_.4, bf16[1024,256]{1,0:T(8,128)(2,1)} %copy-done.6, bf16[1024,256]{1,0:T(8,128)(2,1)} %copy-done.7, bf16[1024,256]{1,0:T(8,128)(2,1)} %copy-done.1, ...), custom_call_target="tpu_custom_call", output_to_operand_aliasing={{}: (25, {})} | custom-call | flops 4294967296 | bytes 10485760 | tf_op jit(solution)/shard_map/product/pallas_call | solution.py:253
  (68 shorter events, 0.4 us)
Async XLA Ops:
  0.6 4.0 %copy-start = (bf16[2048,512]{1,0:T(8,128)(2,1)S(1)}, bf16[2048,512]{1,0:T(8,128)(2,1)}, u32[]{:S(2)}) copy-start(bf16[2048,512]{1,0:T(8,128)(2,1)} %refs_0_.4) | copy-start | bytes 6291460
  0.7 10.5 %copy-start.19 = (f32[2048]{0:T(1024)S(1)}, f32[2048]{0:T(1024)}, u32[]{:S(2)}) copy-start(f32[2048]{0:T(1024)} %param.10) | copy-start | bytes 24580
  0.7 10.5 %copy-start.20 = (f32[2048]{0:T(1024)S(1)}, f32[2048]{0:T(1024)}, u32[]{:S(2)}) copy-start(f32[2048]{0:T(1024)} %param.11) | copy-start | bytes 24580
  0.7 10.6 %copy-start.17 = (s32[2048]{0:T(1024)S(1)}, s32[2048]{0:T(1024)}, u32[]{:S(2)}) copy-start(s32[2048]{0:T(1024)} %param.12) | copy-start | bytes 24580
  5.5 29.6 %collective-permute-start.3 = (bf16[256,2048]{1,0:T(8,128)(2,1)}, bf16[256,2048]{1,0:T(8,128)(2,1)}, u32[]{:S(2)}, u32[]{:S(2)}) collective-permute-start(bf16[256,2048]{1,0:T(8,128)(2,1)} %refs_0_.2), channel_id=1, source_target_pairs={{0,28},{4,0},{8,4},{12,8},{16,12},{20,16},{24,20},{28,24},{1,29},{... | collective-permute-start | bytes 3145736 | tf_op jit(solution)/shard_map/ppermute | solution.py:442
  6.3 31.4 %collective-permute-start = (bf16[1024,256]{1,0:T(8,128)(2,1)}, bf16[1024,256]{1,0:T(8,128)(2,1)S(1)}, u32[]{:S(2)}, u32[]{:S(2)}) collective-permute-start(bf16[1024,256]{1,0:T(8,128)(2,1)} %dynamic_slice.74), channel_id=1, source_target_pairs={{1,0},{5,6},{9,8},{10,9},{14,15},{18,17},{19,18},{20,21},{22,23},{... | collective-permute-start | bytes 1572872 | tf_op jit(solution)/shard_map/ppermute | solution.py:359
  7.0 25.1 %collective-permute-start.1 = (bf16[1024,256]{1,0:T(8,128)(2,1)}, bf16[1024,256]{1,0:T(8,128)(2,1)}, u32[]{:S(2)}, u32[]{:S(2)}) collective-permute-start(bf16[1024,256]{1,0:T(8,128)(2,1)} %constant_dynamic-slice_fusion), channel_id=1, source_target_pairs={{18,2},{19,3},{23,7},{9,25},{13,29},{14,30},{28,12},{1,17},{0,16},... | collective-permute-start | bytes 1572872 | tf_op jit(solution)/shard_map/ppermute | solution.py:364
  8.3 26.8 %collective-permute-start.4 = (bf16[1024,256]{1,0:T(8,128)(2,1)}, bf16[1024,256]{1,0:T(8,128)(2,1)S(1)}, u32[]{:S(2)}, u32[]{:S(2)}) collective-permute-start(bf16[1024,256]{1,0:T(8,128)(2,1)} %constant_dynamic-slice_fusion.2), channel_id=1, source_target_pairs={{0,1},{1,2},{5,4},{6,5},{9,10},{10,11},{13,12},{14,13},{15,14},{18... | collective-permute-start | bytes 1572872 | tf_op jit(solution)/shard_map/ppermute | solution.py:359
  9.6 2.7 %collective-permute-start.2 = (bf16[1024,256]{1,0:T(8,128)(2,1)}, bf16[1024,256]{1,0:T(8,128)(2,1)}, u32[]{:S(2)}, u32[]{:S(2)}) collective-permute-start(bf16[1024,256]{1,0:T(8,128)(2,1)} %constant_dynamic-slice_fusion.3), channel_id=1, source_target_pairs={{1,0},{4,5},{5,6},{6,7},{9,8},{10,9},{13,14},{14,15},{18,17},{19,1... | collective-permute-start | bytes 1572872 | tf_op jit(solution)/shard_map/ppermute | solution.py:359
  32.9 22.6 %collective-permute-start.6 = (bf16[1024,256]{1,0:T(8,128)(2,1)}, bf16[1024,256]{1,0:T(8,128)(2,1)}, u32[]{:S(2)}, u32[]{:S(2)}) collective-permute-start(bf16[1024,256]{1,0:T(8,128)(2,1)} %dynamic_slice.77), channel_id=1, source_target_pairs={{18,2},{9,25},{1,17},{10,26}} | collective-permute-start | bytes 1572872 | tf_op jit(solution)/shard_map/ppermute | solution.py:364
  35.1 22.6 %copy-start.9 = (bf16[1024,256]{1,0:T(8,128)(2,1)}, bf16[1024,256]{1,0:T(8,128)(2,1)S(1)}, u32[]{:S(2)}) copy-start(bf16[1024,256]{1,0:T(8,128)(2,1)S(1)} %collective-permute-done.4.refs_2_) | copy-start | bytes 1572868
  35.1 31.5 %collective-permute-start.9 = (bf16[256,2048]{1,0:T(8,128)(2,1)}, bf16[256,2048]{1,0:T(8,128)(2,1)}, u32[]{:S(2)}, u32[]{:S(2)}) collective-permute-start(bf16[256,2048]{1,0:T(8,128)(2,1)} %collective-permute-done.3.refs_1_), channel_id=1, source_target_pairs={{0,28},{4,0},{8,4},{12,8},{16,12},{20,16},{24,20},{28,24},{1,29},{... | collective-permute-start | bytes 3145736 | tf_op jit(solution)/shard_map/ppermute | solution.py:442
  35.2 22.5 %collective-permute-start.5 = (bf16[1024,256]{1,0:T(8,128)(2,1)}, bf16[1024,256]{1,0:T(8,128)(2,1)S(1)}, u32[]{:S(2)}, u32[]{:S(2)}) collective-permute-start(bf16[1024,256]{1,0:T(8,128)(2,1)} %dynamic_slice.78), channel_id=1, source_target_pairs={{0,1},{1,2},{5,4},{9,10},{10,11},{14,13},{18,19},{22,21},{23,22},{... | collective-permute-start | bytes 1572872 | tf_op jit(solution)/shard_map/ppermute | solution.py:359
  37.7 24.9 %copy-start.6 = (bf16[1024,256]{1,0:T(8,128)(2,1)}, bf16[1024,256]{1,0:T(8,128)(2,1)S(1)}, u32[]{:S(2)}) copy-start(bf16[1024,256]{1,0:T(8,128)(2,1)S(1)} %collective-permute-done.refs_3_.refs_1_) | copy-start | bytes 1572868
  55.5 11.1 %collective-permute-start.7 = (bf16[1024,256]{1,0:T(8,128)(2,1)S(1)}, bf16[1024,256]{1,0:T(8,128)(2,1)S(1)}, u32[]{:S(2)}, u32[]{:S(2)}) collective-permute-start(bf16[1024,256]{1,0:T(8,128)(2,1)S(1)} %select_select_fusion.3), channel_id=1, source_target_pairs={{1,0},{2,1},{3,2},{4,5},{5,6},{6,7},{9,8},{10,9},{12,13},{14,15},{... | collective-permute-start | bytes 1572872 | tf_op jit(solution)/shard_map/ppermute | solution.py:359
  57.7 10.0 %copy-start.7 = (bf16[1024,256]{1,0:T(8,128)(2,1)}, bf16[1024,256]{1,0:T(8,128)(2,1)S(1)}, u32[]{:S(2)}) copy-start(bf16[1024,256]{1,0:T(8,128)(2,1)S(1)} %collective-permute-done.5.refs_4_.refs_2_) | copy-start | bytes 1572868
  57.7 11.6 %collective-permute-start.8 = (bf16[1024,256]{1,0:T(8,128)(2,1)S(1)}, bf16[1024,256]{1,0:T(8,128)(2,1)S(1)}, u32[]{:S(2)}, u32[]{:S(2)}) collective-permute-start(bf16[1024,256]{1,0:T(8,128)(2,1)S(1)} %select_select_fusion.2), channel_id=1, source_target_pairs={{0,1},{1,2},{2,3},{5,4},{7,6},{9,10},{10,11},{13,12},{14,13},{15,1... | collective-permute-start | bytes 1572872 | tf_op jit(solution)/shard_map/ppermute | solution.py:359
  63.9 11.1 %collective-permute-start.14 = (bf16[1024,256]{1,0:T(8,128)(2,1)S(1)}, bf16[1024,256]{1,0:T(8,128)(2,1)S(1)}, u32[]{:S(2)}, u32[]{:S(2)}) collective-permute-start(bf16[1024,256]{1,0:T(8,128)(2,1)S(1)} %select_select_fusion.1), channel_id=1, source_target_pairs={{1,0},{2,1},{5,6},{6,7},{9,8},{10,9},{13,14},{14,15},{17,16},{18,1... | collective-permute-start | bytes 1572872 | tf_op jit(solution)/shard_map/ppermute | solution.py:359
  66.6 11.4 %copy-start.1 = (bf16[1024,256]{1,0:T(8,128)(2,1)}, bf16[1024,256]{1,0:T(8,128)(2,1)S(1)}, u32[]{:S(2)}) copy-start(bf16[1024,256]{1,0:T(8,128)(2,1)S(1)} %collective-permute-done.7.refs_5_.refs_3_) | copy-start | bytes 1572868
  67.6 17.2 %copy-start.18 = (s32[2048]{0:T(1024)S(1)}, s32[2048]{0:T(1024)}, u32[]{:S(2)}) copy-start(s32[2048]{0:T(1024)} %param.13) | copy-start | bytes 24580
  69.3 8.7 %copy-start.4 = (bf16[1024,256]{1,0:T(8,128)(2,1)}, bf16[1024,256]{1,0:T(8,128)(2,1)S(1)}, u32[]{:S(2)}) copy-start(bf16[1024,256]{1,0:T(8,128)(2,1)S(1)} %collective-permute-done.8.refs_6_.refs_4_) | copy-start | bytes 1572868
  69.3 23.5 %collective-permute-start.12 = (bf16[256,2048]{1,0:T(8,128)(2,1)}, bf16[256,2048]{1,0:T(8,128)(2,1)}, u32[]{:S(2)}, u32[]{:S(2)}) collective-permute-start(bf16[256,2048]{1,0:T(8,128)(2,1)} %collective-permute-done.9.refs_2_), channel_id=1, source_target_pairs={{0,28},{4,0},{8,4},{12,8},{16,12},{20,16},{24,20},{28,24},{1,29},{... | collective-permute-start | bytes 3145736 | tf_op jit(solution)/shard_map/ppermute | solution.py:442
  75.0 32.1 %copy-start.3 = (bf16[1024,256]{1,0:T(8,128)(2,1)}, bf16[1024,256]{1,0:T(8,128)(2,1)S(1)}, u32[]{:S(2)}) copy-start(bf16[1024,256]{1,0:T(8,128)(2,1)S(1)} %collective-permute-done.14.refs_7_.refs_6_) | copy-start | bytes 1572868
  75.0 12.6 %collective-permute-start.13 = (bf16[1024,256]{1,0:T(8,128)(2,1)}, bf16[1024,256]{1,0:T(8,128)(2,1)}, u32[]{:S(2)}, u32[]{:S(2)}) collective-permute-start(bf16[1024,256]{1,0:T(8,128)(2,1)} %select_select_fusion), channel_id=1, source_target_pairs={{1,2},{2,3},{5,4},{6,5},{9,10},{10,11},{13,12},{14,13},{17,18},{18... | collective-permute-start | bytes 1572872 | tf_op jit(solution)/shard_map/ppermute | solution.py:359
  78.0 14.8 %collective-permute-start.10 = (bf16[1024,256]{1,0:T(8,128)(2,1)}, bf16[1024,256]{1,0:T(8,128)(2,1)}, u32[]{:S(2)}, u32[]{:S(2)}) collective-permute-start(bf16[1024,256]{1,0:T(8,128)(2,1)} %get-tuple-element.237), channel_id=1, source_target_pairs={{24,8},{28,12},{23,7},{27,11}} | collective-permute-start | bytes 1572872 | tf_op jit(solution)/shard_map/ppermute | solution.py:380
  79.5 13.4 %collective-permute-start.11 = (f32[2048]{0:T(1024)S(1)}, f32[2048]{0:T(1024)S(1)}, u32[]{:S(2)}, u32[]{:S(2)}) collective-permute-start(f32[2048]{0:T(1024)S(1)} %multiply_reduce_fusion), channel_id=1, source_target_pairs={{0,1},{1,0},{2,3},{3,2},{4,5},{5,4},{6,7},{7,6},{8,9},{9,8},{10,11... | collective-permute-start | bytes 24584 | tf_op jit(solution)/shard_map/ppermute | solution.py:461
  82.9 24.2 %collective-permute-start.17 = (bf16[1024,256]{1,0:T(8,128)(2,1)}, bf16[1024,256]{1,0:T(8,128)(2,1)S(1)}, u32[]{:S(2)}, u32[]{:S(2)}) collective-permute-start(bf16[1024,256]{1,0:T(8,128)(2,1)} %slice_select_fusion.3), channel_id=1, source_target_pairs={{1,0},{2,1},{5,6},{6,7},{9,8},{13,14},{14,15},{17,16},{18,17},{21,... | collective-permute-start | bytes 1572872 | tf_op jit(solution)/shard_map/ppermute | solution.py:359
  85.5 21.5 %copy-start.15 = (f32[1024]{0:T(1024)}, f32[1024]{0:T(1024)S(1)}, u32[]{:S(2)}) copy-start(f32[1024]{0:T(1024)S(1)} %get-tuple-element.242) | copy-start | bytes 12292
  85.5 21.5 %copy-start.16 = (f32[1024]{0:T(1024)}, f32[1024]{0:T(1024)S(1)}, u32[]{:S(2)}) copy-start(f32[1024]{0:T(1024)S(1)} %get-tuple-element.243) | copy-start | bytes 12292
  87.6 25.4 %collective-permute-start.16 = (bf16[1024,256]{1,0:T(8,128)(2,1)}, bf16[1024,256]{1,0:T(8,128)(2,1)}, u32[]{:S(2)}, u32[]{:S(2)}) collective-permute-start(bf16[1024,256]{1,0:T(8,128)(2,1)} %get-tuple-element.170), channel_id=1, source_target_pairs={{1,2},{2,3},{5,4},{6,5},{10,11},{13,12},{14,13},{17,18},{18,19},{2... | collective-permute-start | bytes 1572872 | tf_op jit(solution)/shard_map/ppermute | solution.py:359
  107.1 22.8 %copy-start.2 = (bf16[1024,256]{1,0:T(8,128)(2,1)}, bf16[1024,256]{1,0:T(8,128)(2,1)S(1)}, u32[]{:S(2)}) copy-start(bf16[1024,256]{1,0:T(8,128)(2,1)S(1)} %collective-permute-done.17.refs_9_) | copy-start | bytes 1572868
  109.6 8.2 %collective-permute-start.15 = (bf16[1024,256]{1,0:T(8,128)(2,1)}, bf16[1024,256]{1,0:T(8,128)(2,1)}, u32[]{:S(2)}, u32[]{:S(2)}) collective-permute-start(bf16[1024,256]{1,0:T(8,128)(2,1)} %get-tuple-element.235), channel_id=1, source_target_pairs={{24,8},{27,11}} | collective-permute-start | bytes 1572872 | tf_op jit(solution)/shard_map/ppermute | solution.py:380
  111.0 13.7 %collective-permute-start.19 = (bf16[1024,256]{1,0:T(8,128)(2,1)}, bf16[1024,256]{1,0:T(8,128)(2,1)S(1)}, u32[]{:S(2)}, u32[]{:S(2)}) collective-permute-start(bf16[1024,256]{1,0:T(8,128)(2,1)} %dynamic-slice_select_fusion.1), channel_id=1, source_target_pairs={{1,0},{5,6},{6,7},{9,8},{14,15},{17,16},{18,17},{19,18},{22,23},{2... | collective-permute-start | bytes 1572872 | tf_op jit(solution)/shard_map/ppermute | solution.py:359
  112.9 11.8 %collective-permute-start.23 = (f32[2048]{0:T(1024)S(1)}, f32[2048]{0:T(1024)S(1)}, u32[]{:S(2)}, u32[]{:S(2)}) collective-permute-start(f32[2048]{0:T(1024)S(1)} %add.115), channel_id=1, source_target_pairs={{0,2},{1,3},{2,0},{3,1},{4,6},{5,7},{6,4},{7,5},{8,10},{9,11},{10,... | collective-permute-start | bytes 24584 | tf_op jit(solution)/shard_map/ppermute | solution.py:461
  113.0 22.3 %collective-permute-start.20 = (bf16[1024,256]{1,0:T(8,128)(2,1)}, bf16[1024,256]{1,0:T(8,128)(2,1)}, u32[]{:S(2)}, u32[]{:S(2)}) collective-permute-start(bf16[1024,256]{1,0:T(8,128)(2,1)} %get-tuple-element.193), channel_id=1, source_target_pairs={{0,1},{1,2},{2,3},{5,4},{10,11},{13,12},{14,13},{18,19},{21,20},{2... | collective-permute-start | bytes 1572872 | tf_op jit(solution)/shard_map/ppermute | solution.py:359
  124.7 12.8 %copy-start.5 = (bf16[1024,256]{1,0:T(8,128)(2,1)}, bf16[1024,256]{1,0:T(8,128)(2,1)S(1)}, u32[]{:S(2)}) copy-start(bf16[1024,256]{1,0:T(8,128)(2,1)S(1)} %collective-permute-done.19.refs_11_.refs_12_) | copy-start | bytes 1572868
  124.7 14.2 %collective-permute-start.22 = (bf16[1024,256]{1,0:T(8,128)(2,1)}, bf16[1024,256]{1,0:T(8,128)(2,1)}, u32[]{:S(2)}, u32[]{:S(2)}) collective-permute-start(bf16[1024,256]{1,0:T(8,128)(2,1)} %slice_select_fusion.1), channel_id=1, source_target_pairs={{1,0},{6,7},{14,15},{17,16},{18,17},{22,23},{25,24},{30,31}} | collective-permute-start | bytes 1572872 | tf_op jit(solution)/shard_map/ppermute | solution.py:359
  131.9 7.7 %collective-permute-start.24 = (bf16[1024,256]{1,0:T(8,128)(2,1)}, bf16[1024,256]{1,0:T(8,128)(2,1)S(1)}, u32[]{:S(2)}, u32[]{:S(2)}) collective-permute-start(bf16[1024,256]{1,0:T(8,128)(2,1)} %get-tuple-element.198), channel_id=1, source_target_pairs={{1,2},{2,3},{5,4},{13,12},{18,19},{21,20},{26,27},{29,28}} | collective-permute-start | bytes 1572872 | tf_op jit(solution)/shard_map/ppermute | solution.py:359
  135.3 20.4 %collective-permute-start.27 = (bf16[1024,256]{1,0:T(8,128)(2,1)}, bf16[1024,256]{1,0:T(8,128)(2,1)S(1)}, u32[]{:S(2)}, u32[]{:S(2)}) collective-permute-start(bf16[1024,256]{1,0:T(8,128)(2,1)} %collective-permute-done.20.refs_12_.refs_13_), channel_id=1, source_target_pairs={{1,2},{26,27}} | collective-permute-start | bytes 1572872 | tf_op jit(solution)/shard_map/ppermute | solution.py:359
  136.9 18.8 %collective-permute-start.21 = (bf16[1024,256]{1,0:T(8,128)(2,1)}, bf16[1024,256]{1,0:T(8,128)(2,1)S(1)}, u32[]{:S(2)}, u32[]{:S(2)}) collective-permute-start(bf16[1024,256]{1,0:T(8,128)(2,1)} %broadcast_select_fusion.1), channel_id=1, source_target_pairs={{0,16},{19,3}} | collective-permute-start | bytes 1572872 | tf_op jit(solution)/shard_map/ppermute | solution.py:380
  137.6 18.1 %collective-permute-start.26 = (bf16[1024,256]{1,0:T(8,128)(2,1)S(1)}, bf16[1024,256]{1,0:T(8,128)(2,1)S(1)}, u32[]{:S(2)}, u32[]{:S(2)}) collective-permute-start(bf16[1024,256]{1,0:T(8,128)(2,1)S(1)} %collective-permute-done.19.refs_11_.refs_12_), channel_id=1, source_target_pairs={{18,17},{25,24}} | collective-permute-start | bytes 1572872 | tf_op jit(solution)/shard_map/ppermute | solution.py:359
  138.9 16.8 %collective-permute-start.18 = (bf16[1024,256]{1,0:T(8,128)(2,1)}, bf16[1024,256]{1,0:T(8,128)(2,1)S(1)}, u32[]{:S(2)}, u32[]{:S(2)}) collective-permute-start(bf16[1024,256]{1,0:T(8,128)(2,1)} %get-tuple-element.233), channel_id=1, source_target_pairs={{0,16},{28,12},{19,3},{23,7}} | collective-permute-start | bytes 1572872 | tf_op jit(solution)/shard_map/ppermute | solution.py:380
  139.6 15.4 %copy-start.8 = (bf16[1024,256]{1,0:T(8,128)(2,1)}, bf16[1024,256]{1,0:T(8,128)(2,1)S(1)}, u32[]{:S(2)}) copy-start(bf16[1024,256]{1,0:T(8,128)(2,1)S(1)} %collective-permute-done.24.refs_16_) | copy-start | bytes 1572868
  141.7 14.0 %collective-permute-start.25 = (bf16[1024,256]{1,0:T(8,128)(2,1)}, bf16[1024,256]{1,0:T(8,128)(2,1)S(1)}, u32[]{:S(2)}, u32[]{:S(2)}) collective-permute-start(bf16[1024,256]{1,0:T(8,128)(2,1)} %broadcast_select_fusion), channel_id=1, source_target_pairs={{0,16},{4,20},{15,31},{19,3}} | collective-permute-start | bytes 1572872 | tf_op jit(solution)/shard_map/ppermute | solution.py:380
  155.7 0.9 copy-start.10
  155.7 1.0 copy-start.11
  155.7 1.1 copy-start.12
  155.7 1.3 copy-start.13
  155.7 1.5 copy-start.14

commit v6 on v0

v6 whole, which is shorter than its diff:
```python
import functools

import jax
import jax.numpy as jnp
import numpy as np
from jax import lax
from jax.experimental import pallas as pl
from jax.experimental.pallas import tpu as pltpu
from jax.sharding import PartitionSpec as P

STEPS = 4
PIECES = 4
PARTS = ((0, 2), (2, 3), (3, 4))
CHAINS = 2
COL_TILE = 512
ROW_TILE = 32
LANES = 128
VMEM_LIMIT = 40 * 2**20
RELAY_LIMIT = 60 * 2**20


class Line:
    def __init__(self, chunks):
        self.slots = {}
        todo = sorted(chunks)
        slot = 1
        while todo:
            for chunk in todo:
                if chunk[1] <= slot:
                    self.slots[slot] = chunk
                    todo.remove(chunk)
                    break
            slot += 1

    def sent(self, p, t):
        chunk = self.slots.get(t + p - 1) if p > 0 else None
        return chunk if chunk is not None and chunk[1] >= p else None


class Plan:
    def __init__(self, rows, cols, groups_here):
        self.rows, self.cols = rows, cols
        self.lines = {}
        for phase in range(2):
            for r in range(rows):
                place = [self.position(phase, r, (r + s) % rows // groups_here) for s in range(STEPS)]
                order = sorted((q, place[s], s) for q in range(PIECES) for s in range(STEPS) if place[s] > 0)
                for chain in range(CHAINS):
                    self.lines[phase, chain, r] = Line(order[chain::CHAINS])
        self.rounds = max(max(line.slots, default=0) for line in self.lines.values())

    def position(self, phase, r, c):
        return c if (r + phase) % 2 == 0 else self.cols - 1 - c

    def sent(self, phase, chain, r, c, t):
        return self.lines[phase, chain, r].sent(self.position(phase, r, c), t)

    def pairs(self, phase, chain, t):
        found = []
        for r in range(self.rows):
            for c in range(self.cols):
                if self.sent(phase, chain, r, c, t) is not None:
                    to = self.position(phase, r, self.position(phase, r, c) - 1)
                    found.append((r * self.cols + c, r * self.cols + to))
        return found

    def arrival(self, r, c, q, s):
        for (phase, chain, row), line in self.lines.items():
            if row == r:
                p = self.position(phase, r, c)
                for slot, chunk in line.slots.items():
                    if (chunk[0], chunk[2]) == (q, s) and chunk[1] > p:
                        return phase, chain, slot - p
        return None


def lookup(values, device):
    known = [v for v in values if v is not None]
    if len(set(known)) <= 1:
        return known[0] if known else 0
    values = [known[0] if v is None else v for v in values]
    result = jnp.uint32(0)
    place = (device % 32).astype(jnp.uint32)
    for bit in range(max(values).bit_length()):
        ones = [v >> bit & 1 for v in values]
        words = [sum(b << i for i, b in enumerate(ones[at : at + 32])) for at in range(0, len(ones), 32)]
        word = jnp.uint32(words[0])
        for i, other in enumerate(words[1:], 1):
            word = jnp.where(device // 32 == i, jnp.uint32(other), word)
        result = result | (((word >> place) & jnp.uint32(1)) << jnp.uint32(bit))
    return result.astype(jnp.int32)


def relay_kernel(at, table, x, held, out, sem):
    rows, width = out.shape

    @pl.when(table[at] == 1)
    def _():
        row = pl.multiple_of(table[at + 1] * rows, rows)
        col = pl.multiple_of(table[at + 2] * width, width)
        copy = pltpu.make_async_copy(x.at[pl.ds(row, rows), pl.ds(col, width)], out, sem)
        copy.start()
        copy.wait()


def relay(at, table, x, held):
    return pl.pallas_call(
        functools.partial(relay_kernel, at),
        out_shape=jax.ShapeDtypeStruct(held.shape, held.dtype),
        grid_spec=pltpu.PrefetchScalarGridSpec(
            num_scalar_prefetch=1,
            grid=(1,),
            in_specs=[pl.BlockSpec(memory_space=pl.ANY)] * 2,
            out_specs=pl.BlockSpec(memory_space=pl.ANY),
            scratch_shapes=[pltpu.SemaphoreType.DMA],
        ),
        input_output_aliases={2: 0},
        compiler_params=pltpu.CompilerParams(vmem_limit_bytes=RELAY_LIMIT),
        cost_estimate=pl.CostEstimate(flops=0, bytes_accessed=0, transcendentals=0),
        name="relay",
    )(table, x, held)


def window_kernel(*refs):
    blocks = refs[:STEPS]
    factor, twice, male, out = refs[STEPS:]
    group_size, width = blocks[0].shape
    for s, block in enumerate(blocks):

        @pl.loop(0, group_size // ROW_TILE)
        def _(i, s=s, block=block):
            here = pl.ds(pl.multiple_of(i * ROW_TILE, ROW_TILE), ROW_TILE)
            rows = pl.ds(pl.multiple_of(s * group_size + i * ROW_TILE, ROW_TILE), ROW_TILE)
            for k in range(0, width, LANES):
                value = block[here, k : k + LANES].astype(jnp.float32) - twice[rows, :]
                out[rows, k : k + LANES] = (value * factor[rows, :] * male[:, k : k + LANES]).astype(out.dtype)


def standardized_window(blocks, factor, twice, male):
    group_size, n = blocks[0].shape
    depth = STEPS * group_size
    column = lambda j: (0, 0)
    return pl.pallas_call(
        window_kernel,
        out_shape=jax.ShapeDtypeStruct((depth, n), jnp.bfloat16),
        grid=(n // COL_TILE,),
        in_specs=[pl.BlockSpec((group_size, COL_TILE), lambda j: (0, j))] * STEPS
        + [pl.BlockSpec((depth, LANES), column)] * 2
        + [pl.BlockSpec((1, COL_TILE), lambda j: (0, j))],
        out_specs=pl.BlockSpec((depth, COL_TILE), lambda j: (0, j)),
        compiler_params=pltpu.CompilerParams(vmem_limit_bytes=VMEM_LIMIT),
        cost_estimate=pl.CostEstimate(flops=4 * depth * n, bytes_accessed=4 * depth * n, transcendentals=0),
        name="window",
    )(*blocks, factor, twice, male)


def product_kernel(first, candidates, scale, n_buffers, places, *refs):
    x, buffers = refs[0], refs[1 : 1 + n_buffers]
    factor, twice, male, zy = refs[1 + n_buffers : 5 + n_buffers]
    out, raw, zx, sems = refs[-4:]
    width = raw.shape[1] // STEPS
    piece_rows = buffers[0].shape[0]
    pieces = raw.shape[0] // piece_rows

    @pl.when(pl.program_id(0) == 0)
    def _():
        for q in range(pieces):
            for s in range(STEPS):
                place = places[q * STEPS + s]
                target = raw.at[pl.ds(q * piece_rows, piece_rows), pl.ds(s * width, width)]
                for number in candidates[q * STEPS + s]:
                    if number >= 0:

                        @pl.when(place == number)
                        def _(number=number, target=target, q=q):
                            pltpu.make_async_copy(buffers[number], target, sems.at[q]).start()

                    else:

                        @pl.when(place < 0)
                        def _(place=place, target=target, q=q):
                            col = pl.multiple_of((-1 - place) * width, width)
                            block = x.at[pl.ds((first + q) * piece_rows, piece_rows), pl.ds(col, width)]
                            pltpu.make_async_copy(block, target, sems.at[q]).start()

        for q in range(pieces):
            part = raw.at[pl.ds(q * piece_rows, piece_rows), :]
            pltpu.make_async_copy(part, part, sems.at[q]).wait()

            @pl.loop(0, piece_rows // ROW_TILE)
            def _(i, q=q):
                rows = pl.ds(pl.multiple_of(q * piece_rows + i * ROW_TILE, ROW_TILE), ROW_TILE)
                for k in range(0, raw.shape[1], LANES):
                    lanes = slice(k, k + LANES)
                    value = raw[rows, lanes].astype(jnp.float32) - twice[:, lanes]
                    zx[rows, lanes] = (value * factor[:, lanes] * male[rows, :]).astype(zx.dtype)

    total = jnp.dot(zx[...], zy[...], preferred_element_type=jnp.float32)
    out[...] = (total * scale).astype(out.dtype)


def product(part, places, candidates, x, buffers, factor, twice, male, zy, before):
    rows, (depth, n) = x.shape[0], zy.shape
    first, stop = part
    part_rows = rows // PIECES * (stop - first)
    number = first // (stop - first)
    scale = float(1.0 / np.sqrt(np.float32(depth)))
    whole = lambda j, places: (0, 0)
    specs = [pl.BlockSpec(memory_space=pl.ANY)] * (1 + len(buffers)) + [
        pl.BlockSpec((1, depth), whole),
        pl.BlockSpec((1, depth), whole),
        pl.BlockSpec((part_rows, LANES), lambda j, places: (number, 0)),
        pl.BlockSpec((depth, COL_TILE), lambda j, places: (0, j)),
    ]
    args = [places, x, *buffers, factor, twice, male, zy]
    aliases = {}
    if before is not None:
        aliases = {len(args): 0}
        specs.append(pl.BlockSpec(memory_space=pl.ANY))
        args.append(before)
    return pl.pallas_call(
        functools.partial(product_kernel, first, candidates, scale, len(buffers)),
        out_shape=jax.ShapeDtypeStruct((rows, n), jnp.bfloat16),
        grid_spec=pltpu.PrefetchScalarGridSpec(
            num_scalar_prefetch=1,
            grid=(n // COL_TILE,),
            in_specs=specs,
            out_specs=pl.BlockSpec((part_rows, COL_TILE), lambda j, places: (number, j)),
            scratch_shapes=[
                pltpu.VMEM((part_rows, depth), jnp.bfloat16),
                pltpu.VMEM((part_rows, depth), jnp.bfloat16),
                pltpu.SemaphoreType.DMA((stop - first,)),
            ],
        ),
        input_output_aliases=aliases,
        compiler_params=pltpu.CompilerParams(vmem_limit_bytes=VMEM_LIMIT),
        cost_estimate=pl.CostEstimate(
            flops=2 * part_rows * depth * n,
            bytes_accessed=2 * (part_rows * depth + depth * n + part_rows * n),
            transcendentals=0,
        ),
        name="product",
    )(*args)


def local(rows, cols, x, y, freq, weight, sex_rows, sex_cols):
    group_size = y.shape[0]
    local_vars = x.shape[1]
    groups_here = local_vars // group_size
    piece_rows = x.shape[0] // PIECES
    plan = Plan(rows, cols, groups_here)
    devices = [(r, c) for r in range(rows) for c in range(cols)]

    row_place = lax.axis_index("row")
    col_place = lax.axis_index("col")
    device = row_place * cols + col_place

    sends = [(phase, chain, t) for t in range(1, plan.rounds + 1) for chain in range(CHAINS) for phase in range(2)]
    own_of = {}
    for key in sends:
        own_of[key] = []
        for r, c in devices:
            chunk = plan.sent(*key[:2], r, c, key[2])
            mine = chunk is not None and chunk[1] == plan.position(key[0], r, c)
            own_of[key].append((chunk[0], (r + chunk[2]) % rows % groups_here) if mine else None)
    numbers = [[n for key in sends for n in ((1, *own_of[key][i]) if own_of[key][i] else (0, 0, 0))] for i in range(len(devices))]
    table = lax.dynamic_slice(jnp.asarray(numbers, jnp.int32), (device, 0), (1, 3 * len(sends)))[0]

    latest = [x]

    def after(*values):
        *values, latest[0] = lax.optimization_barrier((*values, latest[0]))
        return values[0] if len(values) == 1 else values

    buffers = {}

    def send(key):
        phase, chain, t = key
        pairs = plan.pairs(*key)
        if not pairs:
            return
        own = own_of[key]
        held = buffers.get((phase, chain, t - 1))
        if held is None:
            piece = lookup([None if o is None else o[0] for o in own], device)
            group = lookup([None if o is None else o[1] for o in own], device)
            start = (piece * piece_rows, group * group_size)
            held = after(lax.dynamic_slice(latest[0], start, (piece_rows, group_size)))
        elif any(own):
            held = buffers[phase, chain, t - 1] = relay(3 * sends.index(key), table, x, held)
        buffers[key] = lax.ppermute(beside(key, held), ("row", "col"), pairs)

    factor = weight / jnp.sqrt(2.0 * freq * (1.0 - freq))
    twice = 2.0 * freq
    male_scale = np.float32(np.sqrt(0.5))
    male_rows = jnp.where(sex_rows > 0, male_scale, np.float32(1.0))
    male_cols = jnp.where(sex_cols > 0, male_scale, np.float32(1.0))
    wide = lambda value: jnp.broadcast_to(value[:, None], (value.shape[0], LANES))

    def in_window(value):
        span = STEPS * group_size
        return lax.dynamic_slice(jnp.concatenate([value, value]), (row_place * group_size,), (span,))

    window_factor, window_twice = in_window(factor), in_window(twice)
    male_wide = wide(male_rows)

    def own_squares(x):
        here = lambda value: lax.dynamic_slice(value, (col_place * local_vars,), (local_vars,))[None, :]
        zx = ((x.astype(jnp.float32) - here(twice)) * here(factor) * male_rows[:, None]).astype(jnp.bfloat16)
        return jnp.sum(jnp.square(zx.astype(jnp.float32)), axis=1)

    def part_product(part, zy, before):
        found = []
        for r, c in devices:
            keys = []
            for q in range(*part):
                for s in range(STEPS):
                    arrival = plan.arrival(r, c, q, s)
                    keys.append(-1 - (r + s) % rows % groups_here if arrival is None else arrival)
            found.append(keys)
        used = sorted({k for keys in found for k in keys if isinstance(k, tuple)}, key=lambda k: (k[2], k[1], k[0]))
        places = [[k if isinstance(k, int) else used.index(k) for k in keys] for keys in found]
        places = np.asarray(places, np.int32)
        candidates = [sorted({max(int(k), -1) for k in places[:, i]}) for i in range(places.shape[1])]
        places = lax.dynamic_slice(jnp.asarray(places), (device, 0), (1, places.shape[1]))[0]
        held = [buffers[key] for key in used]
        return product(
            part, places, candidates, x, held, window_factor[None, :], window_twice[None, :], male_wide, zy, before
        )

    back = [(i, (i - 1) % rows) for i in range(rows)]
    window = [y]
    moving = [lax.ppermute(y, "row", back)]
    squares = own_squares(x)
    bits = [1 << k for k in range(cols.bit_length() - 1)] if cols & (cols - 1) == 0 else []
    relation = None

    def beside(key, held):
        phase, chain, t = key
        if phase == chain == 0 and t in (3, 5, 7) and len(window) < STEPS:
            held, block = lax.optimization_barrier((held, moving[0]))
            window.append(block)
            if len(window) < STEPS:
                moving[0] = lax.ppermute(block, "row", back)
        return held

    for key in sends:
        send(key)
    if cols & (cols - 1):
        squares = lax.psum(squares, "col")
    for bit in bits:
        squares = squares + lax.ppermute(squares, "col", [(i, i ^ bit) for i in range(cols)])
    inbreeding = squares / jnp.float32(freq.shape[0]) - 1.0
    while len(window) < STEPS:
        window.append(moving[0])
        if len(window) < STEPS:
            moving[0] = lax.ppermute(window[-1], "row", back)
    zy = standardized_window(window, wide(window_factor), wide(window_twice), male_cols[None, :])
    for part in PARTS:
        relation = part_product(part, zy, relation)
    return relation, inbreeding


def solution(mesh):
    rows, cols = mesh.shape["row"], mesh.shape["col"]
    return jax.shard_map(
        functools.partial(local, rows, cols),
        mesh=mesh,
        in_specs=(P("row", "col"), P("row", "col"), P(), P(), P("row"), P("col")),
        out_specs=(P("row", "col"), P("row")),
        check_vma=False,
    )
```

time: 228 us -> 314 us (1.38)
  the two profiles are of different devices: /device:TPU:0 before, /device:TPU:16 now
where the time goes in v6:
time: 314 us; the launch traced here: 313 us
  starting transfers between devices  172 us (55%)
  waiting for transfers between devices  75.6 us (24%)
  Pallas kernels  39 us (12%)
  local copies, waits for them, and re-layouts  22.1 us (7%)
    ppermute x36, starting transfers between devices, send(): buffers[key] = lax.ppermute(beside(key, held), ('row', 'col'), pairs)  85.9 us
    ppermute x36, waiting for transfers between devices, send(): buffers[key] = lax.ppermute(beside(key, held), ('row', 'col'), pairs)  69.3 us
    ppermute x2, starting transfers between devices, local(): lax.ppermute(squares, 'col', [(i, i ^ bit) for i in range(cols)])  62.9 us
    ppermute x2, starting transfers between devices, beside(): moving[0] = lax.ppermute(block, 'row', back)  21.2 us
    pallas_call x3, Pallas kernels, product(): pl.pallas_call(functools.partial(product_kernel, first, candidates, scale...  19.4 us
    pallas_call x22, Pallas kernels, relay(): pl.pallas_call(functools.partial(relay_kernel, at), out_shape=jax.ShapeDt...  15 us
    unnamed x104, local copies, waits for them, and re-layouts  14.1 us
  transfers between devices with their start and end apart: 41, of which 9 were waited for; matrix products, arithmetic and copies ran while one was open for 3% of the time, Pallas kernels for 11%

profile of v6, /device:TPU:16, one launch (start us, length us, event | category | flops | bytes accessed | tf_op | source)
XLA Modules:
  0.0 312.6 jit_solution(4181587492929171667)
XLA Ops:
  0.6 1.9 collective-permute-start.2
  2.6 1.0 constant_dynamic-slice_fusion.3
  4.2 1.2 fusion.3.table
  5.4 0.7 copy-done.43
  7.5 0.7 copy-done.38
  8.9 6.3 %collective-permute-done.2.refs_1_ = bf16[256,2048]{1,0:T(8,128)(2,1)} collective-permute-done((bf16[256,2048]{1,0:T(8,128)(2,1)}, bf16[256,2048]{1,0:T(8,128)(2,1)}, u32[]{:S(2)}, u32[]{:S(2)}) %collective-permute-start.2) | collective-permute-done | bytes 1048608 | tf_op jit(solution)/shard_map/ppermute | solution.py:333
  15.2 6.6 %collective-permute-start.17 = (bf16[256,2048]{1,0:T(8,128)(2,1)}, bf16[256,2048]{1,0:T(8,128)(2,1)}, u32[]{:S(2)}, u32[]{:S(2)}) collective-permute-start(bf16[256,2048]{1,0:T(8,128)(2,1)} %collective-permute-done.2.refs_1_), channel_id=1, source_target_pairs={{0,28},{4,0},{8,4},{12,8},{16,12},{20,16},{24,20},{28,24},{1,29},{... | collective-permute-start | bytes 3145736 | tf_op jit(solution)/shard_map/ppermute | solution.py:344
  21.8 1.0 constant_dynamic-slice_fusion.2
  22.8 1.0 dynamic_slice.40
  23.8 1.0 dynamic_slice.41
  24.8 1.3 collective-permute-start.13
  26.8 1.3 collective-permute-start.5
  28.1 19.5 %collective-permute-done.13.held = bf16[512,256]{1,0:T(8,128)(2,1)S(1)} collective-permute-done((bf16[512,256]{1,0:T(8,128)(2,1)S(1)}, bf16[512,256]{1,0:T(8,128)(2,1)S(1)}, u32[]{:S(2)}, u32[]{:S(2)}) %collective-permute-start.13) | collective-permute-done | bytes 262176 | tf_op jit(solution)/shard_map/ppermute | solution.py:291
  49.0 1.9 collective-permute-start.14
  50.9 0.7 copy-done.41
  53.0 0.7 copy-done.36
  54.4 1.9 collective-permute-start.6
  57.4 0.7 copy-done.30
  58.8 1.9 collective-permute-start.15
  60.8 0.7 copy-done.32
  62.2 32.2 %collective-permute-start.11 = (bf16[512,256]{1,0:T(8,128)(2,1)}, bf16[512,256]{1,0:T(8,128)(2,1)S(1)}, u32[]{:S(2)}, u32[]{:S(2)}) collective-permute-start(bf16[512,256]{1,0:T(8,128)(2,1)} %relay.31.refs_7_), channel_id=1, source_target_pairs={{1,0},{4,5},{5,6},{6,7},{9,8},{10,9},{14,15},{17,16},{18,17},{19,1... | collective-permute-start | bytes 786440 | tf_op jit(solution)/shard_map/ppermute | solution.py:291
  94.4 0.7 copy-done.34
  95.8 3.4 %collective-permute-start.7 = (bf16[512,256]{1,0:T(8,128)(2,1)}, bf16[512,256]{1,0:T(8,128)(2,1)S(1)}, u32[]{:S(2)}, u32[]{:S(2)}) collective-permute-start(bf16[512,256]{1,0:T(8,128)(2,1)} %relay.27.refs_6_), channel_id=1, source_target_pairs={{0,1},{1,2},{2,3},{5,4},{9,10},{10,11},{13,12},{14,13},{18,19},{21... | collective-permute-start | bytes 786440 | tf_op jit(solution)/shard_map/ppermute | solution.py:291
  99.2 0.7 copy-done.18
  101.3 0.7 copy-done.20
  102.7 1.9 collective-permute-start.16
  104.7 0.7 copy-done.22
  106.8 5.7 %collective-permute-done.7.held = bf16[512,256]{1,0:T(8,128)(2,1)S(1)} collective-permute-done((bf16[512,256]{1,0:T(8,128)(2,1)}, bf16[512,256]{1,0:T(8,128)(2,1)S(1)}, u32[]{:S(2)}, u32[]{:S(2)}) %collective-permute-start.7) | collective-permute-done | bytes 262176 | tf_op jit(solution)/shard_map/ppermute | solution.py:291
  112.5 0.7 copy-done.24
  113.9 1.9 collective-permute-start.8
  115.8 0.7 copy-done.10
  117.2 14.6 %collective-permute-start.26 = (bf16[256,2048]{1,0:T(8,128)(2,1)}, bf16[256,2048]{1,0:T(8,128)(2,1)}, u32[]{:S(2)}, u32[]{:S(2)}) collective-permute-start(bf16[256,2048]{1,0:T(8,128)(2,1)} %collective-permute-done.17.refs_2_), channel_id=1, source_target_pairs={{0,28},{4,0},{8,4},{12,8},{16,12},{20,16},{24,20},{28,24},{1,29},{... | collective-permute-start | bytes 3145736 | tf_op jit(solution)/shard_map/ppermute | solution.py:344
  131.8 0.7 copy-done.4
  133.2 1.9 collective-permute-start.21
  135.2 0.7 copy-done.6
  136.6 0.8 collective-permute-start.20
  137.4 4.1 %collective-permute-done.8.held = bf16[512,256]{1,0:T(8,128)(2,1)S(1)} collective-permute-done((bf16[512,256]{1,0:T(8,128)(2,1)}, bf16[512,256]{1,0:T(8,128)(2,1)S(1)}, u32[]{:S(2)}, u32[]{:S(2)}) %collective-permute-start.8) | collective-permute-done | bytes 262176 | tf_op jit(solution)/shard_map/ppermute | solution.py:291
  141.5 0.7 copy-done.8
  142.8 1.9 collective-permute-start.19
  145.7 30.9 %collective-permute-done.19.held = bf16[512,256]{1,0:T(8,128)(2,1)S(1)} collective-permute-done((bf16[512,256]{1,0:T(8,128)(2,1)}, bf16[512,256]{1,0:T(8,128)(2,1)S(1)}, u32[]{:S(2)}, u32[]{:S(2)}) %collective-permute-start.19) | collective-permute-done | bytes 262176 | tf_op jit(solution)/shard_map/ppermute | solution.py:291
  176.6 0.7 copy-done.12
  178.0 1.9 collective-permute-start.23
  179.9 1.9 collective-permute-start.25
  182.6 0.7 copy-done.2
  184.6 1.0 multiply_reduce_fusion
  185.7 5.2 %collective-permute-done.25.held = bf16[512,256]{1,0:T(8,128)(2,1)S(1)} collective-permute-done((bf16[512,256]{1,0:T(8,128)(2,1)S(1)}, bf16[512,256]{1,0:T(8,128)(2,1)S(1)}, u32[]{:S(2)}, u32[]{:S(2)}) %collective-permute-start.25) | collective-permute-done | bytes 262176 | tf_op jit(solution)/shard_map/ppermute | solution.py:291
  190.9 17.8 %collective-permute-start.39 = (f32[2048]{0:T(1024)S(1)}, f32[2048]{0:T(1024)S(1)}, u32[]{:S(2)}, u32[]{:S(2)}) collective-permute-start(f32[2048]{0:T(1024)S(1)} %multiply_reduce_fusion), channel_id=1, source_target_pairs={{0,1},{1,0},{2,3},{3,2},{4,5},{5,4},{6,7},{7,6},{8,9},{9,8},{10,11... | collective-permute-start | bytes 24584 | tf_op jit(solution)/shard_map/ppermute | solution.py:352
  209.5 3.4 %collective-permute-start.30 = (bf16[512,256]{1,0:T(8,128)(2,1)}, bf16[512,256]{1,0:T(8,128)(2,1)S(1)}, u32[]{:S(2)}, u32[]{:S(2)}) collective-permute-start(bf16[512,256]{1,0:T(8,128)(2,1)} %relay.43.refs_16_.refs_12_), channel_id=1, source_target_pairs={{0,1},{1,2},{2,3},{9,10},{10,11},{13,12},{14,13},{15,14},{21,20}} | collective-permute-start | bytes 786440 | tf_op jit(solution)/shard_map/ppermute | solution.py:291
  215.0 1.9 collective-permute-start.28
  218.4 0.7 fusion.5.places
  219.1 0.7 fusion.4.places
  219.8 45.1 %collective-permute-start.40 = (f32[2048]{0:T(1024)S(1)}, f32[2048]{0:T(1024)S(1)}, u32[]{:S(2)}, u32[]{:S(2)}) collective-permute-start(f32[2048]{0:T(1024)S(1)} %add.62), channel_id=1, source_target_pairs={{0,2},{1,3},{2,0},{3,1},{4,6},{5,7},{6,4},{7,5},{8,10},{9,11},{10,... | collective-permute-start | bytes 24584 | tf_op jit(solution)/shard_map/ppermute | solution.py:352
  264.9 3.4 %collective-permute-start.34 = (bf16[512,256]{1,0:T(8,128)(2,1)S(1)}, bf16[512,256]{1,0:T(8,128)(2,1)S(1)}, u32[]{:S(2)}, u32[]{:S(2)}) collective-permute-start(bf16[512,256]{1,0:T(8,128)(2,1)S(1)} %collective-permute-done.30.refs_20_.refs_16_), channel_id=1, source_target_pairs={{1,2},{2,3},{10,11},{13,12},{14,13}} | collective-permute-start | bytes 786440 | tf_op jit(solution)/shard_map/ppermute | solution.py:291
  269.0 1.9 collective-permute-start.32
  271.7 0.7 fusion.2.places
  273.0 2.9 collective-permute-done.34.refs_20_
  275.9 3.5 %collective-permute-start.38 = (bf16[512,256]{1,0:T(8,128)(2,1)S(1)}, bf16[512,256]{1,0:T(8,128)(2,1)S(1)}, u32[]{:S(2)}, u32[]{:S(2)}) collective-permute-start(bf16[512,256]{1,0:T(8,128)(2,1)S(1)} %collective-permute-done.34.refs_20_), channel_id=1, source_target_pairs={{2,3},{13,12}} | collective-permute-start | bytes 786440 | tf_op jit(solution)/shard_map/ppermute | solution.py:291
  280.6 4.4 %collective-permute-start.36 = (bf16[512,256]{1,0:T(8,128)(2,1)S(1)}, bf16[512,256]{1,0:T(8,128)(2,1)S(1)}, u32[]{:S(2)}, u32[]{:S(2)}) collective-permute-start(bf16[512,256]{1,0:T(8,128)(2,1)S(1)} %collective-permute-done.32.refs_18_), channel_id=1, source_target_pairs={{2,3}} | collective-permute-start | bytes 786440 | tf_op jit(solution)/shard_map/ppermute | solution.py:291
  285.4 1.2 copy-done.47
  286.8 4.6 %window.1.refs_24_.refs_28_ = bf16[1024,2048]{1,0:T(8,128)(2,1)S(1)} custom-call(bf16[256,2048]{1,0:T(8,128)(2,1)S(1)} %copy-done.47, bf16[256,2048]{1,0:T(8,128)(2,1)} %collective-permute-done.2.refs_1_, bf16[256,2048]{1,0:T(8,128)(2,1)} %collective-permute-done.17.refs_2_, bf16[256,2048]{1,0:T(8,128)(2,1)} %collective-permute-done.26.refs_3_, ...), custom_call_target="tpu_custom_call" | custom-call | flops 8388608 | bytes 8388608 | tf_op jit(solution)/shard_map/window/pallas_call | solution.py:143
  291.4 0.9 collective-permute-start.35
  292.8 8.5 %product.3.refs_25_ = bf16[2048,2048]{1,0:T(8,128)(2,1)} custom-call(s32[8]{0:T(128)S(1)} %fusion.5.places, bf16[2048,512]{1,0:T(8,128)(2,1)S(1)} %copy-done.1, bf16[512,256]{1,0:T(8,128)(2,1)S(1)} %copy-done.44, bf16[512,256]{1,0:T(8,128)(2,1)S(1)} %copy-done.37, bf16[512,256]{1,0:T(8,128)(2,1)S(1)} %copy-done.42, bf16[512,256]{1,0:T(8,128)(2,1)S(1)} %copy-done.46, ...), custom_call_target="tpu_custom_call" | custom-call | flops 4294967296 | bytes 10485760 | tf_op jit(solution)/shard_map/product/pallas_call | solution.py:221
  301.4 5.4 %product.4.refs_29_ = bf16[2048,2048]{1,0:T(8,128)(2,1)} custom-call(s32[4]{0:T(128)S(1)} %fusion.4.places, bf16[2048,512]{1,0:T(8,128)(2,1)S(1)} %copy-done.1, bf16[512,256]{1,0:T(8,128)(2,1)S(1)} %copy-done.19, bf16[512,256]{1,0:T(8,128)(2,1)S(1)} %copy-done.25, bf16[512,256]{1,0:T(8,128)(2,1)S(1)} %copy-done.23, ...), custom_call_target="tpu_custom_call", output_to_operand_aliasing={{}: (26, {})} | custom-call | flops 2147483648 | bytes 7340032 | tf_op jit(solution)/shard_map/product/pallas_call | solution.py:221
  306.9 5.5 %product.5 = bf16[2048,2048]{1,0:T(8,128)(2,1)} custom-call(s32[4]{0:T(128)S(1)} %fusion.2.places, bf16[2048,512]{1,0:T(8,128)(2,1)S(1)} %copy-done.1, bf16[512,256]{1,0:T(8,128)(2,1)S(1)} %copy-done.11, bf16[512,256]{1,0:T(8,128)(2,1)S(1)} %copy-done.9, bf16[512,256]{1,0:T(8,128)(2,1)S(1)} %copy-done.7, ...), custom_call_target="tpu_custom_call", output_to_operand_aliasing={{}: (30, {})} | custom-call | flops 2147483648 | bytes 7340032 | tf_op jit(solution)/shard_map/product/pallas_call | solution.py:221
  (168 shorter events, 28.6 us)
Async XLA Ops:
  0.6 14.6 %collective-permute-start.2 = (bf16[256,2048]{1,0:T(8,128)(2,1)}, bf16[256,2048]{1,0:T(8,128)(2,1)}, u32[]{:S(2)}, u32[]{:S(2)}) collective-permute-start(bf16[256,2048]{1,0:T(8,128)(2,1)} %refs_0_.4), channel_id=1, source_target_pairs={{0,28},{4,0},{8,4},{12,8},{16,12},{20,16},{24,20},{28,24},{1,29},{... | collective-permute-start | bytes 3145736 | tf_op jit(solution)/shard_map/ppermute | solution.py:333
  3.5 1.9 collective-permute-start
  6.8 0.7 collective-permute-start.1
  15.2 102.0 %collective-permute-start.17 = (bf16[256,2048]{1,0:T(8,128)(2,1)}, bf16[256,2048]{1,0:T(8,128)(2,1)}, u32[]{:S(2)}, u32[]{:S(2)}) collective-permute-start(bf16[256,2048]{1,0:T(8,128)(2,1)} %collective-permute-done.2.refs_1_), channel_id=1, source_target_pairs={{0,28},{4,0},{8,4},{12,8},{16,12},{20,16},{24,20},{28,24},{1,29},{... | collective-permute-start | bytes 3145736 | tf_op jit(solution)/shard_map/ppermute | solution.py:344
  23.8 32.6 %copy-start.39 = (bf16[512,256]{1,0:T(8,128)(2,1)S(1)}, bf16[512,256]{1,0:T(8,128)(2,1)}, u32[]{:S(2)}) copy-start(bf16[512,256]{1,0:T(8,128)(2,1)} %relay.23.refs_5_) | copy-start | bytes 786436
  24.8 22.8 %collective-permute-start.13 = (bf16[512,256]{1,0:T(8,128)(2,1)S(1)}, bf16[512,256]{1,0:T(8,128)(2,1)S(1)}, u32[]{:S(2)}, u32[]{:S(2)}) collective-permute-start(bf16[512,256]{1,0:T(8,128)(2,1)S(1)} %dynamic_slice.41), channel_id=1, source_target_pairs={{0,1},{1,2},{5,4},{9,10},{10,11},{14,13},{15,14},{18,19},{22,21},{... | collective-permute-start | bytes 786440 | tf_op jit(solution)/shard_map/ppermute | solution.py:291
  26.1 24.8 %collective-permute-start.9 = (bf16[512,256]{1,0:T(8,128)(2,1)S(1)}, bf16[512,256]{1,0:T(8,128)(2,1)S(1)}, u32[]{:S(2)}, u32[]{:S(2)}) collective-permute-start(bf16[512,256]{1,0:T(8,128)(2,1)S(1)} %dynamic_slice.40), channel_id=1, source_target_pairs={{1,0},{4,5},{5,6},{9,8},{10,9},{14,15},{18,17},{19,18},{20,21},{27... | collective-permute-start | bytes 786440 | tf_op jit(solution)/shard_map/ppermute | solution.py:291
  26.8 26.2 %collective-permute-start.5 = (bf16[512,256]{1,0:T(8,128)(2,1)S(1)}, bf16[512,256]{1,0:T(8,128)(2,1)S(1)}, u32[]{:S(2)}, u32[]{:S(2)}) collective-permute-start(bf16[512,256]{1,0:T(8,128)(2,1)S(1)} %constant_dynamic-slice_fusion.2), channel_id=1, source_target_pairs={{0,1},{1,2},{5,4},{6,5},{9,10},{10,11},{13,12},{14,13},{18,19},{22... | collective-permute-start | bytes 786440 | tf_op jit(solution)/shard_map/ppermute | solution.py:291
  49.0 8.5 %collective-permute-start.14 = (bf16[512,256]{1,0:T(8,128)(2,1)}, bf16[512,256]{1,0:T(8,128)(2,1)S(1)}, u32[]{:S(2)}, u32[]{:S(2)}) collective-permute-start(bf16[512,256]{1,0:T(8,128)(2,1)} %relay.34.refs_4_), channel_id=1, source_target_pairs={{1,2},{2,3},{5,4},{6,5},{10,11},{13,12},{14,13},{18,19},{21,20},{2... | collective-permute-start | bytes 786440 | tf_op jit(solution)/shard_map/ppermute | solution.py:291
  52.3 8.5 %collective-permute-start.10 = (bf16[512,256]{1,0:T(8,128)(2,1)}, bf16[512,256]{1,0:T(8,128)(2,1)S(1)}, u32[]{:S(2)}, u32[]{:S(2)}) collective-permute-start(bf16[512,256]{1,0:T(8,128)(2,1)} %relay.30.refs_3_), channel_id=1, source_target_pairs={{1,0},{5,6},{6,7},{9,8},{13,14},{14,15},{17,16},{18,17},{20,21},{2... | collective-permute-start | bytes 786440 | tf_op jit(solution)/shard_map/ppermute | solution.py:291
  54.4 40.0 %collective-permute-start.6 = (bf16[512,256]{1,0:T(8,128)(2,1)}, bf16[512,256]{1,0:T(8,128)(2,1)S(1)}, u32[]{:S(2)}, u32[]{:S(2)}) collective-permute-start(bf16[512,256]{1,0:T(8,128)(2,1)} %relay.26.refs_2_), channel_id=1, source_target_pairs={{1,2},{2,3},{5,4},{10,11},{13,12},{18,19},{21,20},{22,21},{23,22},... | collective-permute-start | bytes 786440 | tf_op jit(solution)/shard_map/ppermute | solution.py:291
  56.3 42.9 %collective-permute-start.3 = (bf16[512,256]{1,0:T(8,128)(2,1)S(1)}, bf16[512,256]{1,0:T(8,128)(2,1)S(1)}, u32[]{:S(2)}, u32[]{:S(2)}) collective-permute-start(bf16[512,256]{1,0:T(8,128)(2,1)S(1)} %copy-done.39), channel_id=1, source_target_pairs={{1,0},{5,6},{6,7},{9,8},{10,9},{14,15},{17,16},{18,17},{19,18},{22... | collective-permute-start | bytes 786440 | tf_op jit(solution)/shard_map/ppermute | solution.py:291
  58.8 42.5 %collective-permute-start.15 = (bf16[512,256]{1,0:T(8,128)(2,1)}, bf16[512,256]{1,0:T(8,128)(2,1)S(1)}, u32[]{:S(2)}, u32[]{:S(2)}) collective-permute-start(bf16[512,256]{1,0:T(8,128)(2,1)} %relay.35.refs_8_), channel_id=1, source_target_pairs={{0,1},{1,2},{2,3},{5,4},{9,10},{10,11},{13,12},{14,13},{15,14},{18... | collective-permute-start | bytes 786440 | tf_op jit(solution)/shard_map/ppermute | solution.py:291
  62.2 42.5 %collective-permute-start.11 = (bf16[512,256]{1,0:T(8,128)(2,1)}, bf16[512,256]{1,0:T(8,128)(2,1)S(1)}, u32[]{:S(2)}, u32[]{:S(2)}) collective-permute-start(bf16[512,256]{1,0:T(8,128)(2,1)} %relay.31.refs_7_), channel_id=1, source_target_pairs={{1,0},{4,5},{5,6},{6,7},{9,8},{10,9},{14,15},{17,16},{18,17},{19,1... | collective-permute-start | bytes 786440 | tf_op jit(solution)/shard_map/ppermute | solution.py:291
  95.8 16.7 %collective-permute-start.7 = (bf16[512,256]{1,0:T(8,128)(2,1)}, bf16[512,256]{1,0:T(8,128)(2,1)S(1)}, u32[]{:S(2)}, u32[]{:S(2)}) collective-permute-start(bf16[512,256]{1,0:T(8,128)(2,1)} %relay.27.refs_6_), channel_id=1, source_target_pairs={{0,1},{1,2},{2,3},{5,4},{9,10},{10,11},{13,12},{14,13},{18,19},{21... | collective-permute-start | bytes 786440 | tf_op jit(solution)/shard_map/ppermute | solution.py:291
  100.6 15.2 %collective-permute-start.4 = (bf16[512,256]{1,0:T(8,128)(2,1)}, bf16[512,256]{1,0:T(8,128)(2,1)S(1)}, u32[]{:S(2)}, u32[]{:S(2)}) collective-permute-start(bf16[512,256]{1,0:T(8,128)(2,1)} %relay.24.refs_9_.refs_1_), channel_id=1, source_target_pairs={{1,0},{6,7},{9,8},{13,14},{14,15},{17,16},{18,17},{22,23},{25,24},... | collective-permute-start | bytes 786440 | tf_op jit(solution)/shard_map/ppermute | solution.py:291
  102.7 29.1 %collective-permute-start.16 = (bf16[512,256]{1,0:T(8,128)(2,1)}, bf16[512,256]{1,0:T(8,128)(2,1)S(1)}, u32[]{:S(2)}, u32[]{:S(2)}) collective-permute-start(bf16[512,256]{1,0:T(8,128)(2,1)} %relay.36.refs_12_.refs_4_), channel_id=1, source_target_pairs={{1,2},{2,3},{5,4},{10,11},{13,12},{14,13},{18,19},{21,20},{22,21},... | collective-permute-start | bytes 786440 | tf_op jit(solution)/shard_map/ppermute | solution.py:291
  106.1 29.1 %collective-permute-start.12 = (bf16[512,256]{1,0:T(8,128)(2,1)}, bf16[512,256]{1,0:T(8,128)(2,1)S(1)}, u32[]{:S(2)}, u32[]{:S(2)}) collective-permute-start(bf16[512,256]{1,0:T(8,128)(2,1)} %relay.32.refs_11_.refs_3_), channel_id=1, source_target_pairs={{1,0},{5,6},{6,7},{9,8},{14,15},{17,16},{18,17},{20,21},{21,22},{2... | collective-permute-start | bytes 786440 | tf_op jit(solution)/shard_map/ppermute | solution.py:291
  113.9 27.6 %collective-permute-start.8 = (bf16[512,256]{1,0:T(8,128)(2,1)}, bf16[512,256]{1,0:T(8,128)(2,1)S(1)}, u32[]{:S(2)}, u32[]{:S(2)}) collective-permute-start(bf16[512,256]{1,0:T(8,128)(2,1)} %relay.28.refs_10_.refs_2_), channel_id=1, source_target_pairs={{1,2},{2,3},{5,4},{6,5},{10,11},{13,12},{18,19},{21,20},{22,21},{2... | collective-permute-start | bytes 786440 | tf_op jit(solution)/shard_map/ppermute | solution.py:291
  117.2 27.6 %copy-start.11 = (bf16[512,256]{1,0:T(8,128)(2,1)S(1)}, bf16[512,256]{1,0:T(8,128)(2,1)}, u32[]{:S(2)}) copy-start(bf16[512,256]{1,0:T(8,128)(2,1)} %relay.25.refs_13_.refs_5_.refs_1_) | copy-start | bytes 786436
  117.2 28.3 %copy-start.50 = (f32[2048]{0:T(1024)S(1)}, f32[2048]{0:T(1024)}, u32[]{:S(2)}) copy-start(f32[2048]{0:T(1024)} %param.12) | copy-start | bytes 24580
  117.2 28.3 %copy-start.51 = (f32[2048]{0:T(1024)S(1)}, f32[2048]{0:T(1024)}, u32[]{:S(2)}) copy-start(f32[2048]{0:T(1024)} %param.13) | copy-start | bytes 24580
  117.2 28.4 %copy-start.48 = (s32[2048]{0:T(1024)S(1)}, s32[2048]{0:T(1024)}, u32[]{:S(2)}) copy-start(s32[2048]{0:T(1024)} %param.14) | copy-start | bytes 24580
  117.2 100.4 %collective-permute-start.26 = (bf16[256,2048]{1,0:T(8,128)(2,1)}, bf16[256,2048]{1,0:T(8,128)(2,1)}, u32[]{:S(2)}, u32[]{:S(2)}) collective-permute-start(bf16[256,2048]{1,0:T(8,128)(2,1)} %collective-permute-done.17.refs_2_), channel_id=1, source_target_pairs={{0,28},{4,0},{8,4},{12,8},{16,12},{20,16},{24,20},{28,24},{1,29},{... | collective-permute-start | bytes 3145736 | tf_op jit(solution)/shard_map/ppermute | solution.py:344
  133.2 46.7 %collective-permute-start.21 = (bf16[512,256]{1,0:T(8,128)(2,1)}, bf16[512,256]{1,0:T(8,128)(2,1)S(1)}, u32[]{:S(2)}, u32[]{:S(2)}) collective-permute-start(bf16[512,256]{1,0:T(8,128)(2,1)} %relay.37.refs_16_.refs_8_.refs_4_), channel_id=1, source_target_pairs={{0,1},{1,2},{2,3},{5,4},{6,5},{9,10},{10,11},{13,12},{14,13},{15,1... | collective-permute-start | bytes 786440 | tf_op jit(solution)/shard_map/ppermute | solution.py:291
  136.6 48.1 %copy-start = (bf16[2048,512]{1,0:T(8,128)(2,1)S(1)}, bf16[2048,512]{1,0:T(8,128)(2,1)}, u32[]{:S(2)}) copy-start(bf16[2048,512]{1,0:T(8,128)(2,1)} %refs_0_.7) | copy-start | bytes 6291460
  136.6 45.3 %collective-permute-start.20 = (bf16[512,256]{1,0:T(8,128)(2,1)}, bf16[512,256]{1,0:T(8,128)(2,1)S(1)}, u32[]{:S(2)}, u32[]{:S(2)}) collective-permute-start(bf16[512,256]{1,0:T(8,128)(2,1)} %relay.33.refs_15_.refs_7_.refs_3_), channel_id=1, source_target_pairs={{4,5},{5,6},{6,7},{9,8},{10,9},{13,14},{14,15},{17,16},{18,17},{19... | collective-permute-start | bytes 786440 | tf_op jit(solution)/shard_map/ppermute | solution.py:291
  142.8 42.8 %copy-start.49 = (s32[2048]{0:T(1024)S(1)}, s32[2048]{0:T(1024)}, u32[]{:S(2)}) copy-start(s32[2048]{0:T(1024)} %param.15) | copy-start | bytes 24580
  142.8 33.7 %collective-permute-start.19 = (bf16[512,256]{1,0:T(8,128)(2,1)}, bf16[512,256]{1,0:T(8,128)(2,1)S(1)}, u32[]{:S(2)}, u32[]{:S(2)}) collective-permute-start(bf16[512,256]{1,0:T(8,128)(2,1)} %relay.29.refs_14_.refs_6_.refs_2_), channel_id=1, source_target_pairs={{0,1},{1,2},{2,3},{5,4},{9,10},{10,11},{13,12},{14,13},{21,20},{22... | collective-permute-start | bytes 786440 | tf_op jit(solution)/shard_map/ppermute | solution.py:291
  144.8 37.8 %collective-permute-start.18 = (bf16[512,256]{1,0:T(8,128)(2,1)S(1)}, bf16[512,256]{1,0:T(8,128)(2,1)S(1)}, u32[]{:S(2)}, u32[]{:S(2)}) collective-permute-start(bf16[512,256]{1,0:T(8,128)(2,1)S(1)} %copy-done.11), channel_id=1, source_target_pairs={{5,6},{6,7},{9,8},{10,9},{14,15},{17,16},{18,17},{19,18},{25,24},{... | collective-permute-start | bytes 786440 | tf_op jit(solution)/shard_map/ppermute | solution.py:291
  178.0 35.6 %collective-permute-start.23 = (bf16[512,256]{1,0:T(8,128)(2,1)}, bf16[512,256]{1,0:T(8,128)(2,1)S(1)}, u32[]{:S(2)}, u32[]{:S(2)}) collective-permute-start(bf16[512,256]{1,0:T(8,128)(2,1)} %relay.39.refs_18_.refs_10_.refs_6_), channel_id=1, source_target_pairs={{1,2},{2,3},{5,4},{10,11},{13,12},{21,20},{22,21},{26,27}} | collective-permute-start | bytes 786440 | tf_op jit(solution)/shard_map/ppermute | solution.py:291
  179.9 11.0 %collective-permute-start.25 = (bf16[512,256]{1,0:T(8,128)(2,1)S(1)}, bf16[512,256]{1,0:T(8,128)(2,1)S(1)}, u32[]{:S(2)}, u32[]{:S(2)}) collective-permute-start(bf16[512,256]{1,0:T(8,128)(2,1)S(1)} %collective-permute-done.21.refs_20_.refs_12_.refs_8_), channel_id=1, source_target_pairs={{1,2},{2,3},{5,4},{10,11},{13,12},{14,13},{21,20},{22,21},{26,27},... | collective-permute-start | bytes 786440 | tf_op jit(solution)/shard_map/ppermute | solution.py:291
  181.9 27.6 %collective-permute-start.24 = (bf16[512,256]{1,0:T(8,128)(2,1)S(1)}, bf16[512,256]{1,0:T(8,128)(2,1)S(1)}, u32[]{:S(2)}, u32[]{:S(2)}) collective-permute-start(bf16[512,256]{1,0:T(8,128)(2,1)S(1)} %collective-permute-done.20.refs_19_.refs_11_.refs_7_), channel_id=1, source_target_pairs={{5,6},{6,7},{9,8},{14,15},{17,16},{18,17},{22,23},{25,24},{29,30},... | collective-permute-start | bytes 786440 | tf_op jit(solution)/shard_map/ppermute | solution.py:291
  183.9 31.1 %collective-permute-start.22 = (bf16[512,256]{1,0:T(8,128)(2,1)}, bf16[512,256]{1,0:T(8,128)(2,1)S(1)}, u32[]{:S(2)}, u32[]{:S(2)}) collective-permute-start(bf16[512,256]{1,0:T(8,128)(2,1)} %relay.38.refs_17_.refs_9_.refs_5_), channel_id=1, source_target_pairs={{6,7},{9,8},{14,15},{17,16},{18,17},{25,24},{29,30},{30,31}} | collective-permute-start | bytes 786440 | tf_op jit(solution)/shard_map/ppermute | solution.py:291
  190.9 17.9 %copy-start.28 = (bf16[512,256]{1,0:T(8,128)(2,1)}, bf16[512,256]{1,0:T(8,128)(2,1)S(1)}, u32[]{:S(2)}) copy-start(bf16[512,256]{1,0:T(8,128)(2,1)S(1)} %collective-permute-done.25.held) | copy-start | bytes 786436
  190.9 28.9 %collective-permute-start.39 = (f32[2048]{0:T(1024)S(1)}, f32[2048]{0:T(1024)S(1)}, u32[]{:S(2)}, u32[]{:S(2)}) collective-permute-start(f32[2048]{0:T(1024)S(1)} %multiply_reduce_fusion), channel_id=1, source_target_pairs={{0,1},{1,0},{2,3},{3,2},{4,5},{5,4},{6,7},{7,6},{8,9},{9,8},{10,11... | collective-permute-start | bytes 24584 | tf_op jit(solution)/shard_map/ppermute | solution.py:352
  209.5 55.5 %collective-permute-start.30 = (bf16[512,256]{1,0:T(8,128)(2,1)}, bf16[512,256]{1,0:T(8,128)(2,1)S(1)}, u32[]{:S(2)}, u32[]{:S(2)}) collective-permute-start(bf16[512,256]{1,0:T(8,128)(2,1)} %relay.43.refs_16_.refs_12_), channel_id=1, source_target_pairs={{0,1},{1,2},{2,3},{9,10},{10,11},{13,12},{14,13},{15,14},{21,20}} | collective-permute-start | bytes 786440 | tf_op jit(solution)/shard_map/ppermute | solution.py:291
  213.6 54.7 %collective-permute-start.29 = (bf16[512,256]{1,0:T(8,128)(2,1)}, bf16[512,256]{1,0:T(8,128)(2,1)S(1)}, u32[]{:S(2)}, u32[]{:S(2)}) collective-permute-start(bf16[512,256]{1,0:T(8,128)(2,1)} %relay.42.refs_15_.refs_11_), channel_id=1, source_target_pairs={{4,5},{5,6},{6,7},{9,8},{10,9},{17,16},{18,17},{19,18},{30,31}} | collective-permute-start | bytes 786440 | tf_op jit(solution)/shard_map/ppermute | solution.py:291
  215.0 54.0 %collective-permute-start.28 = (bf16[512,256]{1,0:T(8,128)(2,1)}, bf16[512,256]{1,0:T(8,128)(2,1)S(1)}, u32[]{:S(2)}, u32[]{:S(2)}) collective-permute-start(bf16[512,256]{1,0:T(8,128)(2,1)} %relay.41.refs_14_.refs_10_), channel_id=1, source_target_pairs={{0,1},{1,2},{2,3},{9,10},{10,11},{13,12},{14,13},{21,20}} | collective-permute-start | bytes 786440 | tf_op jit(solution)/shard_map/ppermute | solution.py:291
  217.7 53.3 %collective-permute-start.27 = (bf16[512,256]{1,0:T(8,128)(2,1)}, bf16[512,256]{1,0:T(8,128)(2,1)S(1)}, u32[]{:S(2)}, u32[]{:S(2)}) collective-permute-start(bf16[512,256]{1,0:T(8,128)(2,1)} %relay.40.refs_13_.refs_9_), channel_id=1, source_target_pairs={{5,6},{6,7},{9,8},{10,9},{17,16},{18,17},{19,18},{30,31}} | collective-permute-start | bytes 786440 | tf_op jit(solution)/shard_map/ppermute | solution.py:291
  219.8 52.5 %collective-permute-start.40 = (f32[2048]{0:T(1024)S(1)}, f32[2048]{0:T(1024)S(1)}, u32[]{:S(2)}, u32[]{:S(2)}) collective-permute-start(f32[2048]{0:T(1024)S(1)} %add.62), channel_id=1, source_target_pairs={{0,2},{1,3},{2,0},{3,1},{4,6},{5,7},{6,4},{7,5},{8,10},{9,11},{10,... | collective-permute-start | bytes 24584 | tf_op jit(solution)/shard_map/ppermute | solution.py:352
  264.9 10.9 %collective-permute-start.34 = (bf16[512,256]{1,0:T(8,128)(2,1)S(1)}, bf16[512,256]{1,0:T(8,128)(2,1)S(1)}, u32[]{:S(2)}, u32[]{:S(2)}) collective-permute-start(bf16[512,256]{1,0:T(8,128)(2,1)S(1)} %collective-permute-done.30.refs_20_.refs_16_), channel_id=1, source_target_pairs={{1,2},{2,3},{10,11},{13,12},{14,13}} | collective-permute-start | bytes 786440 | tf_op jit(solution)/shard_map/ppermute | solution.py:291
  268.3 11.1 %collective-permute-start.33 = (bf16[512,256]{1,0:T(8,128)(2,1)S(1)}, bf16[512,256]{1,0:T(8,128)(2,1)S(1)}, u32[]{:S(2)}, u32[]{:S(2)}) collective-permute-start(bf16[512,256]{1,0:T(8,128)(2,1)S(1)} %collective-permute-done.29.refs_19_.refs_15_), channel_id=1, source_target_pairs={{5,6},{6,7},{9,8},{17,16},{18,17}} | collective-permute-start | bytes 786440 | tf_op jit(solution)/shard_map/ppermute | solution.py:291
  269.0 11.6 %collective-permute-start.32 = (bf16[512,256]{1,0:T(8,128)(2,1)S(1)}, bf16[512,256]{1,0:T(8,128)(2,1)S(1)}, u32[]{:S(2)}, u32[]{:S(2)}) collective-permute-start(bf16[512,256]{1,0:T(8,128)(2,1)S(1)} %collective-permute-done.28.refs_18_.refs_14_), channel_id=1, source_target_pairs={{1,2},{2,3},{10,11},{13,12}} | collective-permute-start | bytes 786440 | tf_op jit(solution)/shard_map/ppermute | solution.py:291
  271.0 20.4 %collective-permute-start.31 = (bf16[512,256]{1,0:T(8,128)(2,1)S(1)}, bf16[512,256]{1,0:T(8,128)(2,1)S(1)}, u32[]{:S(2)}, u32[]{:S(2)}) collective-permute-start(bf16[512,256]{1,0:T(8,128)(2,1)S(1)} %collective-permute-done.27.refs_17_.refs_13_), channel_id=1, source_target_pairs={{6,7},{9,8},{17,16},{18,17}} | collective-permute-start | bytes 786440 | tf_op jit(solution)/shard_map/ppermute | solution.py:291
  275.9 31.0 %collective-permute-start.38 = (bf16[512,256]{1,0:T(8,128)(2,1)S(1)}, bf16[512,256]{1,0:T(8,128)(2,1)S(1)}, u32[]{:S(2)}, u32[]{:S(2)}) collective-permute-start(bf16[512,256]{1,0:T(8,128)(2,1)S(1)} %collective-permute-done.34.refs_20_), channel_id=1, source_target_pairs={{2,3},{13,12}} | collective-permute-start | bytes 786440 | tf_op jit(solution)/shard_map/ppermute | solution.py:291
  279.4 27.4 %collective-permute-start.37 = (bf16[512,256]{1,0:T(8,128)(2,1)S(1)}, bf16[512,256]{1,0:T(8,128)(2,1)S(1)}, u32[]{:S(2)}, u32[]{:S(2)}) collective-permute-start(bf16[512,256]{1,0:T(8,128)(2,1)S(1)} %collective-permute-done.33.refs_19_), channel_id=1, source_target_pairs={{6,7},{17,16}} | collective-permute-start | bytes 786440 | tf_op jit(solution)/shard_map/ppermute | solution.py:291
  280.6 26.2 %collective-permute-start.36 = (bf16[512,256]{1,0:T(8,128)(2,1)S(1)}, bf16[512,256]{1,0:T(8,128)(2,1)S(1)}, u32[]{:S(2)}, u32[]{:S(2)}) collective-permute-start(bf16[512,256]{1,0:T(8,128)(2,1)S(1)} %collective-permute-done.32.refs_18_), channel_id=1, source_target_pairs={{2,3}} | collective-permute-start | bytes 786440 | tf_op jit(solution)/shard_map/ppermute | solution.py:291
  286.7 6.0 %copy-start.9 = (bf16[512,256]{1,0:T(8,128)(2,1)S(1)}, bf16[512,256]{1,0:T(8,128)(2,1)}, u32[]{:S(2)}) copy-start(bf16[512,256]{1,0:T(8,128)(2,1)} %relay.29.refs_14_.refs_6_.refs_2_) | copy-start | bytes 786436
  286.7 6.0 %copy-start.13 = (bf16[512,256]{1,0:T(8,128)(2,1)S(1)}, bf16[512,256]{1,0:T(8,128)(2,1)}, u32[]{:S(2)}) copy-start(bf16[512,256]{1,0:T(8,128)(2,1)} %relay.39.refs_18_.refs_10_.refs_6_) | copy-start | bytes 786436
  286.7 6.0 %copy-start.19 = (bf16[512,256]{1,0:T(8,128)(2,1)S(1)}, bf16[512,256]{1,0:T(8,128)(2,1)}, u32[]{:S(2)}) copy-start(bf16[512,256]{1,0:T(8,128)(2,1)} %relay.24.refs_9_.refs_1_) | copy-start | bytes 786436
  286.7 6.0 %copy-start.21 = (bf16[512,256]{1,0:T(8,128)(2,1)S(1)}, bf16[512,256]{1,0:T(8,128)(2,1)}, u32[]{:S(2)}) copy-start(bf16[512,256]{1,0:T(8,128)(2,1)} %relay.36.refs_12_.refs_4_) | copy-start | bytes 786436
  286.7 6.0 %copy-start.23 = (bf16[512,256]{1,0:T(8,128)(2,1)S(1)}, bf16[512,256]{1,0:T(8,128)(2,1)}, u32[]{:S(2)}) copy-start(bf16[512,256]{1,0:T(8,128)(2,1)} %relay.32.refs_11_.refs_3_) | copy-start | bytes 786436
  286.7 6.0 %copy-start.25 = (bf16[512,256]{1,0:T(8,128)(2,1)S(1)}, bf16[512,256]{1,0:T(8,128)(2,1)}, u32[]{:S(2)}) copy-start(bf16[512,256]{1,0:T(8,128)(2,1)} %relay.28.refs_10_.refs_2_) | copy-start | bytes 786436
  286.7 6.0 %copy-start.31 = (bf16[512,256]{1,0:T(8,128)(2,1)S(1)}, bf16[512,256]{1,0:T(8,128)(2,1)}, u32[]{:S(2)}) copy-start(bf16[512,256]{1,0:T(8,128)(2,1)} %relay.35.refs_8_) | copy-start | bytes 786436
  286.7 6.0 %copy-start.33 = (bf16[512,256]{1,0:T(8,128)(2,1)S(1)}, bf16[512,256]{1,0:T(8,128)(2,1)}, u32[]{:S(2)}) copy-start(bf16[512,256]{1,0:T(8,128)(2,1)} %relay.31.refs_7_) | copy-start | bytes 786436
  286.7 6.0 %copy-start.35 = (bf16[512,256]{1,0:T(8,128)(2,1)S(1)}, bf16[512,256]{1,0:T(8,128)(2,1)}, u32[]{:S(2)}) copy-start(bf16[512,256]{1,0:T(8,128)(2,1)} %relay.27.refs_6_) | copy-start | bytes 786436
  286.8 6.0 %copy-start.37 = (bf16[512,256]{1,0:T(8,128)(2,1)S(1)}, bf16[512,256]{1,0:T(8,128)(2,1)}, u32[]{:S(2)}) copy-start(bf16[512,256]{1,0:T(8,128)(2,1)} %relay.26.refs_2_) | copy-start | bytes 786436
  286.8 6.0 %copy-start.40 = (bf16[512,256]{1,0:T(8,128)(2,1)S(1)}, bf16[512,256]{1,0:T(8,128)(2,1)}, u32[]{:S(2)}) copy-start(bf16[512,256]{1,0:T(8,128)(2,1)} %relay.23.refs_5_) | copy-start | bytes 786436
  291.4 15.4 %collective-permute-start.35 = (bf16[512,256]{1,0:T(8,128)(2,1)S(1)}, bf16[512,256]{1,0:T(8,128)(2,1)S(1)}, u32[]{:S(2)}, u32[]{:S(2)}) collective-permute-start(bf16[512,256]{1,0:T(8,128)(2,1)S(1)} %collective-permute-done.31.refs_17_), channel_id=1, source_target_pairs={{17,16}} | collective-permute-start | bytes 786440 | tf_op jit(solution)/shard_map/ppermute | solution.py:291
  292.8 8.6 %copy-start.15 = (bf16[512,256]{1,0:T(8,128)(2,1)S(1)}, bf16[512,256]{1,0:T(8,128)(2,1)}, u32[]{:S(2)}) copy-start(bf16[512,256]{1,0:T(8,128)(2,1)} %relay.41.refs_14_.refs_10_) | copy-start | bytes 786436
  292.8 8.6 %copy-start.17 = (bf16[512,256]{1,0:T(8,128)(2,1)S(1)}, bf16[512,256]{1,0:T(8,128)(2,1)}, u32[]{:S(2)}) copy-start(bf16[512,256]{1,0:T(8,128)(2,1)} %relay.40.refs_13_.refs_9_) | copy-start | bytes 786436
  292.8 8.6 %copy-start.27 = (bf16[512,256]{1,0:T(8,128)(2,1)S(1)}, bf16[512,256]{1,0:T(8,128)(2,1)}, u32[]{:S(2)}) copy-start(bf16[512,256]{1,0:T(8,128)(2,1)} %relay.42.refs_15_.refs_11_) | copy-start | bytes 786436
  292.8 8.6 %copy-start.29 = (bf16[512,256]{1,0:T(8,128)(2,1)S(1)}, bf16[512,256]{1,0:T(8,128)(2,1)}, u32[]{:S(2)}) copy-start(bf16[512,256]{1,0:T(8,128)(2,1)} %relay.43.refs_16_.refs_12_) | copy-start | bytes 786436
  (29 other events, 62.0 us)

commit v7 on v6

--- a/solution.py
+++ b/solution.py
@@ -15,8 +15,8 @@
 COL_TILE = 512
 ROW_TILE = 32
 LANES = 128
-VMEM_LIMIT = 40 * 2**20
-RELAY_LIMIT = 60 * 2**20
+VMEM_LIMIT = 20 * 2**20
+RELAY_LIMIT = 8 * 2**20
 
 
 class Line:
@@ -91,34 +91,38 @@
     return result.astype(jnp.int32)
 
 
-def relay_kernel(at, table, x, held, out, sem):
+def relay_kernel(at, table, x, held, out):
     rows, width = out.shape
 
     @pl.when(table[at] == 1)
     def _():
         row = pl.multiple_of(table[at + 1] * rows, rows)
         col = pl.multiple_of(table[at + 2] * width, width)
-        copy = pltpu.make_async_copy(x.at[pl.ds(row, rows), pl.ds(col, width)], out, sem)
-        copy.start()
-        copy.wait()
+        out[...] = x[pl.ds(row, rows), pl.ds(col, width)]
+
+    @pl.when(table[at] == 0)
+    def _():
+        out[...] = held[...]
 
 
 def relay(at, table, x, held):
     return pl.pallas_call(
         functools.partial(relay_kernel, at),
         out_shape=jax.ShapeDtypeStruct(held.shape, held.dtype),
-        grid_spec=pltpu.PrefetchScalarGridSpec(
-            num_scalar_prefetch=1,
-            grid=(1,),
-            in_specs=[pl.BlockSpec(memory_space=pl.ANY)] * 2,
-            out_specs=pl.BlockSpec(memory_space=pl.ANY),
-            scratch_shapes=[pltpu.SemaphoreType.DMA],
-        ),
+        in_specs=[pl.BlockSpec(memory_space=pltpu.SMEM)] + [pl.BlockSpec(memory_space=pltpu.VMEM)] * 2,
+        out_specs=pl.BlockSpec(memory_space=pltpu.VMEM),
         input_output_aliases={2: 0},
         compiler_params=pltpu.CompilerParams(vmem_limit_bytes=RELAY_LIMIT),
         cost_estimate=pl.CostEstimate(flops=0, bytes_accessed=0, transcendentals=0),
         name="relay",
-    )(table, x, held)
+    )(table, in_vmem(x), in_vmem(held))
+
+
+def in_vmem(value):
+    return pltpu.with_memory_space_constraint(value, pltpu.VMEM)
+
+
+VMEM = pl.BlockSpec(memory_space=pltpu.VMEM)
 
 
 def window_kernel(*refs):
@@ -139,104 +143,94 @@
 def standardized_window(blocks, factor, twice, male):
     group_size, n = blocks[0].shape
     depth = STEPS * group_size
-    column = lambda j: (0, 0)
     return pl.pallas_call(
         window_kernel,
-        out_shape=jax.ShapeDtypeStruct((depth, n), jnp.bfloat16),
-        grid=(n // COL_TILE,),
-        in_specs=[pl.BlockSpec((group_size, COL_TILE), lambda j: (0, j))] * STEPS
-        + [pl.BlockSpec((depth, LANES), column)] * 2
-        + [pl.BlockSpec((1, COL_TILE), lambda j: (0, j))],
-        out_specs=pl.BlockSpec((depth, COL_TILE), lambda j: (0, j)),
+        out_shape=pltpu.VMEM((depth, n), jnp.bfloat16),
+        in_specs=[VMEM] * (STEPS + 3),
+        out_specs=VMEM,
         compiler_params=pltpu.CompilerParams(vmem_limit_bytes=VMEM_LIMIT),
         cost_estimate=pl.CostEstimate(flops=4 * depth * n, bytes_accessed=4 * depth * n, transcendentals=0),
         name="window",
-    )(*blocks, factor, twice, male)
-
-
-def product_kernel(first, candidates, scale, n_buffers, places, *refs):
-    x, buffers = refs[0], refs[1 : 1 + n_buffers]
-    factor, twice, male, zy = refs[1 + n_buffers : 5 + n_buffers]
-    out, raw, zx, sems = refs[-4:]
-    width = raw.shape[1] // STEPS
-    piece_rows = buffers[0].shape[0]
-    pieces = raw.shape[0] // piece_rows
-
-    @pl.when(pl.program_id(0) == 0)
-    def _():
-        for q in range(pieces):
-            for s in range(STEPS):
-                place = places[q * STEPS + s]
-                target = raw.at[pl.ds(q * piece_rows, piece_rows), pl.ds(s * width, width)]
-                for number in candidates[q * STEPS + s]:
-                    if number >= 0:
-
-                        @pl.when(place == number)
-                        def _(number=number, target=target, q=q):
-                            pltpu.make_async_copy(buffers[number], target, sems.at[q]).start()
-
-                    else:
-
-                        @pl.when(place < 0)
-                        def _(place=place, target=target, q=q):
-                            col = pl.multiple_of((-1 - place) * width, width)
-                            block = x.at[pl.ds((first + q) * piece_rows, piece_rows), pl.ds(col, width)]
-                            pltpu.make_async_copy(block, target, sems.at[q]).start()
-
-        for q in range(pieces):
-            part = raw.at[pl.ds(q * piece_rows, piece_rows), :]
-            pltpu.make_async_copy(part, part, sems.at[q]).wait()
-
-            @pl.loop(0, piece_rows // ROW_TILE)
-            def _(i, q=q):
-                rows = pl.ds(pl.multiple_of(q * piece_rows + i * ROW_TILE, ROW_TILE), ROW_TILE)
-                for k in range(0, raw.shape[1], LANES):
-                    lanes = slice(k, k + LANES)
-                    value = raw[rows, lanes].astype(jnp.float32) - twice[:, lanes]
-                    zx[rows, lanes] = (value * factor[:, lanes] * male[rows, :]).astype(zx.dtype)
-
-    total = jnp.dot(zx[...], zy[...], preferred_element_type=jnp.float32)
-    out[...] = (total * scale).astype(out.dtype)
+    )(*[in_vmem(v) for v in (*blocks, factor, twice, male)])
+
+
+def product_kernel(part, candidates, scale, n_buffers, places, x, *refs):
+    buffers = refs[:n_buffers]
+    factor, twice, male, zy = refs[n_buffers : n_buffers + 4]
+    out, zx, tiles, sems = refs[-4:]
+    piece_rows, width = buffers[0].shape
+    first, stop = part
+
+    def standardize(source, row, col, q, s):
+        @pl.loop(0, piece_rows // ROW_TILE)
+        def _(i):
+            at = i * ROW_TILE
+            here = pl.ds(pl.multiple_of(row + at, ROW_TILE), ROW_TILE)
+            rows = pl.ds(pl.multiple_of((q - first) * piece_rows + at, ROW_TILE), ROW_TILE)
+            sexes = male[pl.ds(pl.multiple_of(q * piece_rows + at, ROW_TILE), ROW_TILE), :]
+            for k in range(0, width, LANES):
+                lanes = slice(s * width + k, s * width + k + LANES)
+                value = source[here, pl.ds(pl.multiple_of(col + k, LANES), LANES)].astype(jnp.float32)
+                zx[rows, lanes] = ((value - twice[:, lanes]) * factor[:, lanes] * sexes).astype(zx.dtype)
+
+    for q in range(first, stop):
+        for s in range(STEPS):
+            place = places[(q - first) * STEPS + s]
+            for number in candidates[(q - first) * STEPS + s]:
+                if number >= 0:
+
+                    @pl.when(place == number)
+                    def _(number=number, q=q, s=s):
+                        standardize(buffers[number], 0, 0, q, s)
+
+                else:
+
+                    @pl.when(place < 0)
+                    def _(place=place, q=q, s=s):
+                        standardize(x, q * piece_rows, (-1 - place) * width, q, s)
+
+    def copy(j):
+        where = out.at[pl.ds(first * piece_rows, zx.shape[0]), pl.ds(j * COL_TILE, COL_TILE)]
+        return pltpu.make_async_copy(tiles.at[j % 2], where, sems.at[j % 2])
+
+    count = zy.shape[1] // COL_TILE
+    for j in range(count):
+        if j >= 2:
+            copy(j - 2).wait()
+        total = jnp.dot(zx[...], zy[:, j * COL_TILE : (j + 1) * COL_TILE], preferred_element_type=jnp.float32)
+        tiles[j % 2] = (total * scale).astype(tiles.dtype)
+        copy(j).start()
+    for j in range(max(count - 2, 0), count):
+        copy(j).wait()
 
 
 def product(part, places, candidates, x, buffers, factor, twice, male, zy, before):
     rows, (depth, n) = x.shape[0], zy.shape
-    first, stop = part
-    part_rows = rows // PIECES * (stop - first)
-    number = first // (stop - first)
+    part_rows = rows // PIECES * (part[1] - part[0])
     scale = float(1.0 / np.sqrt(np.float32(depth)))
-    whole = lambda j, places: (0, 0)
-    specs = [pl.BlockSpec(memory_space=pl.ANY)] * (1 + len(buffers)) + [
-        pl.BlockSpec((1, depth), whole),
-        pl.BlockSpec((1, depth), whole),
-        pl.BlockSpec((part_rows, LANES), lambda j, places: (number, 0)),
-        pl.BlockSpec((depth, COL_TILE), lambda j, places: (0, j)),
-    ]
-    args = [places, x, *buffers, factor, twice, male, zy]
+    args = [places, *[in_vmem(v) for v in (x, *buffers, factor, twice, male, zy)]]
+    specs = [pl.BlockSpec(memory_space=pltpu.SMEM)] + [VMEM] * (len(args) - 1)
     aliases = {}
+    kernel = functools.partial(product_kernel, part, candidates, scale, len(buffers))
     if before is not None:
         aliases = {len(args): 0}
         specs.append(pl.BlockSpec(memory_space=pl.ANY))
         args.append(before)
     return pl.pallas_call(
-        functools.partial(product_kernel, first, candidates, scale, len(buffers)),
+        kernel,
         out_shape=jax.ShapeDtypeStruct((rows, n), jnp.bfloat16),
-        grid_spec=pltpu.PrefetchScalarGridSpec(
-            num_scalar_prefetch=1,
-            grid=(n // COL_TILE,),
-            in_specs=specs,
-            out_specs=pl.BlockSpec((part_rows, COL_TILE), lambda j, places: (number, j)),
-            scratch_shapes=[
-                pltpu.VMEM((part_rows, depth), jnp.bfloat16),
-                pltpu.VMEM((part_rows, depth), jnp.bfloat16),
-                pltpu.SemaphoreType.DMA((stop - first,)),
-            ],
-        ),
+        in_specs=specs,
+        out_specs=pl.BlockSpec(memory_space=pl.ANY),
+        scratch_shapes=[
+            pltpu.VMEM((part_rows, depth), jnp.bfloat16),
+            pltpu.VMEM((2, part_rows, COL_TILE), jnp.bfloat16),
+            pltpu.SemaphoreType.DMA((2,)),
+        ],
         input_output_aliases=aliases,
         compiler_params=pltpu.CompilerParams(vmem_limit_bytes=VMEM_LIMIT),
         cost_estimate=pl.CostEstimate(
             flops=2 * part_rows * depth * n,
-            bytes_accessed=2 * (part_rows * depth + depth * n + part_rows * n),
+            bytes_accessed=2 * part_rows * n,
             transcendentals=0,
         ),
         name="product",
@@ -266,13 +260,16 @@
     numbers = [[n for key in sends for n in ((1, *own_of[key][i]) if own_of[key][i] else (0, 0, 0))] for i in range(len(devices))]
     table = lax.dynamic_slice(jnp.asarray(numbers, jnp.int32), (device, 0), (1, 3 * len(sends)))[0]
 
-    latest = [x]
-
-    def after(*values):
-        *values, latest[0] = lax.optimization_barrier((*values, latest[0]))
-        return values[0] if len(values) == 1 else values
-
     buffers = {}
+
+    def first(key):
+        own = own_of[key]
+        piece = lookup([None if o is None else o[0] for o in own], device)
+        group = lookup([None if o is None else o[1] for o in own], device)
+        return lax.dynamic_slice(x, (piece * piece_rows, group * group_size), (piece_rows, group_size))
+
+    firsts = [key for key in sends if key[2] == 1 and plan.pairs(*key)]
+    starts = dict(zip(firsts, lax.optimization_barrier([first(key) for key in firsts])))
 
     def send(key):
         phase, chain, t = key
@@ -282,13 +279,10 @@
         own = own_of[key]
         held = buffers.get((phase, chain, t - 1))
         if held is None:
-            piece = lookup([None if o is None else o[0] for o in own], device)
-            group = lookup([None if o is None else o[1] for o in own], device)
-            start = (piece * piece_rows, group * group_size)
-            held = after(lax.dynamic_slice(latest[0], start, (piece_rows, group_size)))
+            held = starts.pop(key) if key in starts else first(key)
         elif any(own):
             held = buffers[phase, chain, t - 1] = relay(3 * sends.index(key), table, x, held)
-        buffers[key] = lax.ppermute(beside(key, held), ("row", "col"), pairs)
+        buffers[key] = lax.ppermute(held, ("row", "col"), pairs)
 
     factor = weight / jnp.sqrt(2.0 * freq * (1.0 - freq))
     twice = 2.0 * freq
@@ -335,29 +329,25 @@
     bits = [1 << k for k in range(cols.bit_length() - 1)] if cols & (cols - 1) == 0 else []
     relation = None
 
-    def beside(key, held):
-        phase, chain, t = key
-        if phase == chain == 0 and t in (3, 5, 7) and len(window) < STEPS:
-            held, block = lax.optimization_barrier((held, moving[0]))
-            window.append(block)
-            if len(window) < STEPS:
-                moving[0] = lax.ppermute(block, "row", back)
-        return held
-
     for key in sends:
         send(key)
-    if cols & (cols - 1):
-        squares = lax.psum(squares, "col")
-    for bit in bits:
-        squares = squares + lax.ppermute(squares, "col", [(i, i ^ bit) for i in range(cols)])
-    inbreeding = squares / jnp.float32(freq.shape[0]) - 1.0
     while len(window) < STEPS:
         window.append(moving[0])
         if len(window) < STEPS:
             moving[0] = lax.ppermute(window[-1], "row", back)
     zy = standardized_window(window, wide(window_factor), wide(window_twice), male_cols[None, :])
+    if cols & (cols - 1):
+        squares = lax.psum(squares, "col")
     for part in PARTS:
         relation = part_product(part, zy, relation)
+        if bits:
+            bit = bits.pop(0)
+            other = lax.ppermute(squares, "col", [(i, i ^ bit) for i in range(cols)])
+            relation, other = lax.optimization_barrier((relation, other))
+            squares = squares + other
+    for bit in bits:
+        squares = squares + lax.ppermute(squares, "col", [(i, i ^ bit) for i in range(cols)])
+    inbreeding = squares / jnp.float32(freq.shape[0]) - 1.0
     return relation, inbreeding
 
 

time: 314 us -> 148 us (0.47)
  the two profiles are of different devices: /device:TPU:16 before, /device:TPU:0 now
where the time goes in v7:
time: 148 us; the launch traced here: 147 us
  starting transfers between devices  88.4 us (60%)
  Pallas kernels  43.9 us (30%)
  local copies, waits for them, and re-layouts  6.67 us (5%)
  waiting for transfers between devices  4.37 us (3%)
  between operations  1.87 us (1%)
  other arithmetic  1.74 us (1%)
    ppermute x36, starting transfers between devices, send(): buffers[key] = lax.ppermute(held, ('row', 'col'), pairs)  68.2 us
    pallas_call x3, Pallas kernels, product(): pl.pallas_call(kernel, out_shape=jax.ShapeDtypeStruct((rows, n), jnp.bflo...  21.9 us
    pallas_call x22, Pallas kernels, relay(): pl.pallas_call(functools.partial(relay_kernel, at), out_shape=jax.ShapeDt...  18.5 us
    ppermute x2, starting transfers between devices, local(): other = lax.ppermute(squares, 'col', [(i, i ^ bit) for i in range(cols)])  12.6 us
    ppermute x36, waiting for transfers between devices, send(): buffers[key] = lax.ppermute(held, ('row', 'col'), pairs)  4.35 us
    ppermute x2, starting transfers between devices, local(): moving[0] = lax.ppermute(window[-1], 'row', back)  4.3 us
    pallas_call x1, Pallas kernels, standardized_window(): pl.pallas_call(window_kernel, out_shape=pltpu.VMEM((depth, n), jnp.bfloat...  3.52 us
    ppermute x1, starting transfers between devices, local(): moving = [lax.ppermute(y, 'row', back)]  3.39 us
  transfers between devices with their start and end apart: 41, of which 4 were waited for; matrix products, arithmetic and copies ran while one was open for 5% of the time, Pallas kernels for 26%

profile of v7, /device:TPU:0, one launch (start us, length us, event | category | flops | bytes accessed | tf_op | source)
XLA Modules:
  0.0 147.0 jit_solution(6126660907927049627)
XLA Ops:
  0.6 3.4 %collective-permute-start.36 = (bf16[256,2048]{1,0:T(8,128)(2,1)}, bf16[256,2048]{1,0:T(8,128)(2,1)}, u32[]{:S(2)}, u32[]{:S(2)}) collective-permute-start(bf16[256,2048]{1,0:T(8,128)(2,1)} %refs_0_.1), channel_id=1, source_target_pairs={{0,28},{4,0},{8,4},{12,8},{16,12},{20,16},{24,20},{28,24},{1,29},{... | collective-permute-start | bytes 3145736 | tf_op jit(solution)/shard_map/ppermute | solution.py:327
  4.0 1.3 fusion.6
  5.3 3.5 %collective-permute-start.4 = (bf16[512,256]{1,0:T(8,128)(2,1)S(1)}, bf16[512,256]{1,0:T(8,128)(2,1)S(1)}, u32[]{:S(2)}, u32[]{:S(2)}) collective-permute-start(bf16[512,256]{1,0:T(8,128)(2,1)S(1)} %get-tuple-element.11), channel_id=1, source_target_pairs={{0,1},{1,2},{5,4},{6,5},{9,10},{10,11},{13,12},{14,13},{18,19},{22... | collective-permute-start | bytes 786440 | tf_op jit(solution)/shard_map/ppermute | solution.py:285
  8.8 1.3 collective-permute-start
  10.1 1.3 collective-permute-start.8
  11.4 4.6 %collective-permute-start.12 = (bf16[512,256]{1,0:T(8,128)(2,1)S(1)}, bf16[512,256]{1,0:T(8,128)(2,1)S(1)}, u32[]{:S(2)}, u32[]{:S(2)}) collective-permute-start(bf16[512,256]{1,0:T(8,128)(2,1)S(1)} %get-tuple-element.13), channel_id=1, source_target_pairs={{0,1},{1,2},{5,4},{9,10},{10,11},{14,13},{15,14},{18,19},{22,21},{... | collective-permute-start | bytes 786440 | tf_op jit(solution)/shard_map/ppermute | solution.py:285
  16.0 0.7 fusion.3.table
  16.7 1.6 %copy-done = bf16[2048,512]{1,0:T(8,128)(2,1)S(1)} copy-done((bf16[2048,512]{1,0:T(8,128)(2,1)S(1)}, bf16[2048,512]{1,0:T(8,128)(2,1)}, u32[]{:S(2)}) %copy-start) | copy-done | bytes 2097176
  18.9 0.7 collective-permute-start.5
  20.2 1.3 collective-permute-start.1
  21.5 1.2 collective-permute-done.8.held
  23.4 1.3 collective-permute-start.9
  25.3 0.7 collective-permute-start.13
  26.0 1.3 collective-permute-start.37
  27.9 4.2 %collective-permute-start.6 = (bf16[512,256]{1,0:T(8,128)(2,1)S(1)}, bf16[512,256]{1,0:T(8,128)(2,1)S(1)}, u32[]{:S(2)}, u32[]{:S(2)}) collective-permute-start(bf16[512,256]{1,0:T(8,128)(2,1)S(1)} %relay.27.refs_5_), channel_id=1, source_target_pairs={{0,1},{1,2},{2,3},{5,4},{9,10},{10,11},{13,12},{14,13},{18,19},{21... | collective-permute-start | bytes 786440 | tf_op jit(solution)/shard_map/ppermute | solution.py:285
  32.1 0.6 relay.23.refs_4_
  32.7 1.3 collective-permute-start.2
  34.0 1.0 collective-permute-done.9.held
  35.7 5.0 %collective-permute-start.10 = (bf16[512,256]{1,0:T(8,128)(2,1)S(1)}, bf16[512,256]{1,0:T(8,128)(2,1)S(1)}, u32[]{:S(2)}, u32[]{:S(2)}) collective-permute-start(bf16[512,256]{1,0:T(8,128)(2,1)S(1)} %relay.31.refs_6_), channel_id=1, source_target_pairs={{1,0},{4,5},{5,6},{6,7},{9,8},{10,9},{14,15},{17,16},{18,17},{19,1... | collective-permute-start | bytes 786440 | tf_op jit(solution)/shard_map/ppermute | solution.py:285
  41.3 4.5 %collective-permute-start.14 = (bf16[512,256]{1,0:T(8,128)(2,1)S(1)}, bf16[512,256]{1,0:T(8,128)(2,1)S(1)}, u32[]{:S(2)}, u32[]{:S(2)}) collective-permute-start(bf16[512,256]{1,0:T(8,128)(2,1)S(1)} %relay.35.refs_7_), channel_id=1, source_target_pairs={{0,1},{1,2},{2,3},{5,4},{9,10},{10,11},{13,12},{14,13},{15,14},{18... | collective-permute-start | bytes 786440 | tf_op jit(solution)/shard_map/ppermute | solution.py:285
  45.8 0.6 relay.28.refs_9_.refs_1_
  46.4 0.7 collective-permute-start.7
  47.7 1.3 collective-permute-start.3
  49.7 1.3 collective-permute-start.11
  51.6 1.4 collective-permute-start.15
  53.6 6.3 %collective-permute-start.17 = (bf16[512,256]{1,0:T(8,128)(2,1)S(1)}, bf16[512,256]{1,0:T(8,128)(2,1)S(1)}, u32[]{:S(2)}, u32[]{:S(2)}) collective-permute-start(bf16[512,256]{1,0:T(8,128)(2,1)S(1)} %relay.29.refs_13_.refs_5_.refs_1_), channel_id=1, source_target_pairs={{0,1},{1,2},{2,3},{5,4},{9,10},{10,11},{13,12},{14,13},{21,20},{22... | collective-permute-start | bytes 786440 | tf_op jit(solution)/shard_map/ppermute | solution.py:285
  60.5 0.7 collective-permute-start.16
  61.2 0.9 collective-permute-done.11.held
  62.7 1.4 collective-permute-start.18
  64.1 1.7 %relay.37.refs_15_.refs_7_.refs_3_ = bf16[512,256]{1,0:T(8,128)(2,1)} custom-call(s32[108]{0:T(128)S(1)} %fusion.3.table, bf16[2048,512]{1,0:T(8,128)(2,1)S(1)} %copy-done, bf16[512,256]{1,0:T(8,128)(2,1)} %collective-permute-done.15.held), custom_call_target="tpu_custom_call", output_to_operand_aliasing={{}: (2, {})} | custom-call | tf_op jit(solution)/shard_map/relay/pallas_call | solution.py:109
  65.8 2.1 %collective-permute-start.19 = (bf16[512,256]{1,0:T(8,128)(2,1)}, bf16[512,256]{1,0:T(8,128)(2,1)}, u32[]{:S(2)}, u32[]{:S(2)}) collective-permute-start(bf16[512,256]{1,0:T(8,128)(2,1)} %relay.37.refs_15_.refs_7_.refs_3_), channel_id=1, source_target_pairs={{0,1},{1,2},{2,3},{5,4},{6,5},{9,10},{10,11},{13,12},{14,13},{15,1... | collective-permute-start | bytes 786440 | tf_op jit(solution)/shard_map/ppermute | solution.py:285
  68.1 3.0 %collective-permute-start.38 = (bf16[256,2048]{1,0:T(8,128)(2,1)}, bf16[256,2048]{1,0:T(8,128)(2,1)}, u32[]{:S(2)}, u32[]{:S(2)}) collective-permute-start(bf16[256,2048]{1,0:T(8,128)(2,1)} %collective-permute-done.37.refs_2_), channel_id=1, source_target_pairs={{0,28},{4,0},{8,4},{12,8},{16,12},{20,16},{24,20},{28,24},{1,29},{... | collective-permute-start | bytes 3145736 | tf_op jit(solution)/shard_map/ppermute | solution.py:337
  71.1 0.7 fusion.5.places
  72.4 1.4 collective-permute-start.21
  74.4 1.4 collective-permute-start.20
  75.8 1.4 collective-permute-start.22
  77.2 1.4 collective-permute-start.23
  78.5 0.7 fusion.4.places
  79.4 1.7 %relay.41.refs_13_.refs_9_ = bf16[512,256]{1,0:T(8,128)(2,1)} custom-call(s32[108]{0:T(128)S(1)} %fusion.3.table, bf16[2048,512]{1,0:T(8,128)(2,1)S(1)} %copy-done.1, bf16[512,256]{1,0:T(8,128)(2,1)} %collective-permute-done.21.held), custom_call_target="tpu_custom_call", output_to_operand_aliasing={{}: (2, {})} | custom-call | tf_op jit(solution)/shard_map/relay/pallas_call | solution.py:109
  81.1 7.1 %collective-permute-start.25 = (bf16[512,256]{1,0:T(8,128)(2,1)}, bf16[512,256]{1,0:T(8,128)(2,1)S(1)}, u32[]{:S(2)}, u32[]{:S(2)}) collective-permute-start(bf16[512,256]{1,0:T(8,128)(2,1)} %relay.41.refs_13_.refs_9_), channel_id=1, source_target_pairs={{0,1},{1,2},{2,3},{9,10},{10,11},{13,12},{14,13},{21,20}} | collective-permute-start | bytes 786440 | tf_op jit(solution)/shard_map/ppermute | solution.py:285
  88.2 1.8 %relay.40.refs_12_.refs_8_ = bf16[512,256]{1,0:T(8,128)(2,1)} custom-call(s32[108]{0:T(128)S(1)} %fusion.3.table, bf16[2048,512]{1,0:T(8,128)(2,1)S(1)} %copy-done.1, bf16[512,256]{1,0:T(8,128)(2,1)} %collective-permute-done.20.held), custom_call_target="tpu_custom_call", output_to_operand_aliasing={{}: (2, {})} | custom-call | tf_op jit(solution)/shard_map/relay/pallas_call | solution.py:109
  90.0 0.8 collective-permute-start.24
  90.8 1.7 %relay.42.refs_14_.refs_10_ = bf16[512,256]{1,0:T(8,128)(2,1)} custom-call(s32[108]{0:T(128)S(1)} %fusion.3.table, bf16[2048,512]{1,0:T(8,128)(2,1)S(1)} %copy-done.1, bf16[512,256]{1,0:T(8,128)(2,1)} %collective-permute-done.22.held), custom_call_target="tpu_custom_call", output_to_operand_aliasing={{}: (2, {})} | custom-call | tf_op jit(solution)/shard_map/relay/pallas_call | solution.py:109
  92.5 0.7 collective-permute-start.26
  93.2 1.7 %relay.43.refs_15_.refs_11_ = bf16[512,256]{1,0:T(8,128)(2,1)} custom-call(s32[108]{0:T(128)S(1)} %fusion.3.table, bf16[2048,512]{1,0:T(8,128)(2,1)S(1)} %copy-done.1, bf16[512,256]{1,0:T(8,128)(2,1)} %collective-permute-done.23.held), custom_call_target="tpu_custom_call", output_to_operand_aliasing={{}: (2, {})} | custom-call | tf_op jit(solution)/shard_map/relay/pallas_call | solution.py:109
  94.9 3.9 %collective-permute-start.27 = (bf16[512,256]{1,0:T(8,128)(2,1)}, bf16[512,256]{1,0:T(8,128)(2,1)S(1)}, u32[]{:S(2)}, u32[]{:S(2)}) collective-permute-start(bf16[512,256]{1,0:T(8,128)(2,1)} %relay.43.refs_15_.refs_11_), channel_id=1, source_target_pairs={{0,1},{1,2},{2,3},{9,10},{10,11},{13,12},{14,13},{15,14},{21,20}} | collective-permute-start | bytes 786440 | tf_op jit(solution)/shard_map/ppermute | solution.py:285
  98.8 1.0 multiply_reduce_fusion
  99.9 0.7 collective-permute-start.29
  100.6 0.7 collective-permute-start.28
  101.3 0.7 collective-permute-start.30
  102.0 1.1 collective-permute-done.27.refs_19_.refs_15_
  103.0 0.7 collective-permute-start.31
  103.7 0.7 fusion.2.places
  104.4 6.5 %collective-permute-start.39 = (f32[2048]{0:T(1024)S(1)}, f32[2048]{0:T(1024)S(1)}, u32[]{:S(2)}, u32[]{:S(2)}) collective-permute-start(f32[2048]{0:T(1024)S(1)} %multiply_reduce_fusion), channel_id=1, source_target_pairs={{0,1},{1,0},{2,3},{3,2},{4,5},{5,4},{6,7},{7,6},{8,9},{9,8},{10,11... | collective-permute-start | bytes 24584 | tf_op jit(solution)/shard_map/ppermute | solution.py:345
  110.9 0.7 collective-permute-start.33
  111.6 0.7 collective-permute-start.32
  112.3 0.7 collective-permute-start.34
  113.0 0.7 collective-permute-start.35
  114.2 3.5 %window.1.refs_23_.refs_27_ = bf16[1024,2048]{1,0:T(8,128)(2,1)S(1)} custom-call(bf16[256,2048]{1,0:T(8,128)(2,1)S(1)} %copy-done.26, bf16[256,2048]{1,0:T(8,128)(2,1)} %collective-permute-done.36.refs_1_, bf16[256,2048]{1,0:T(8,128)(2,1)} %collective-permute-done.37.refs_2_, bf16[256,2048]{1,0:T(8,128)(2,1)} %collective-permute-done.38.refs_3_, ...), custom_call_target="tpu_custom_call" | custom-call | flops 8388608 | bytes 8388608 | tf_op jit(solution)/shard_map/window/pallas_call | solution.py:146
  118.2 9.1 %product.3.refs_24_ = bf16[2048,2048]{1,0:T(8,128)(2,1)} custom-call(s32[8]{0:T(128)S(1)} %fusion.5.places, bf16[2048,512]{1,0:T(8,128)(2,1)S(1)} %copy-done.1, bf16[512,256]{1,0:T(8,128)(2,1)S(1)} %copy-done.23, bf16[512,256]{1,0:T(8,128)(2,1)S(1)} %copy-done.25, bf16[512,256]{1,0:T(8,128)(2,1)S(1)} %copy-done.21, bf16[512,256]{1,0:T(8,128)(2,1)S(1)} %copy-done.11, ...), custom_call_target="tpu_custom_call" | custom-call | flops 4294967296 | bytes 4194304 | tf_op jit(solution)/shard_map/product/pallas_call | solution.py:219
  127.3 6.1 %collective-permute-start.40 = (f32[2048]{0:T(1024)S(1)}, f32[2048]{0:T(1024)S(1)}, u32[]{:S(2)}, u32[]{:S(2)}) collective-permute-start(f32[2048]{0:T(1024)S(1)} %add.62), channel_id=1, source_target_pairs={{0,2},{1,3},{2,0},{3,1},{4,6},{5,7},{6,4},{7,5},{8,10},{9,11},{10,... | collective-permute-start | bytes 24584 | tf_op jit(solution)/shard_map/ppermute | solution.py:345
  133.4 6.5 %product.4.refs_28_ = bf16[2048,2048]{1,0:T(8,128)(2,1)} custom-call(s32[4]{0:T(128)S(1)} %fusion.4.places, bf16[2048,512]{1,0:T(8,128)(2,1)S(1)} %copy-done.1, bf16[512,256]{1,0:T(8,128)(2,1)S(1)} %copy-done.5, bf16[512,256]{1,0:T(8,128)(2,1)S(1)} %copy-done.3, bf16[512,256]{1,0:T(8,128)(2,1)S(1)} %copy-done.7, ...), custom_call_target="tpu_custom_call", output_to_operand_aliasing={{}: (26, {})} | custom-call | flops 2147483648 | bytes 2097152 | tf_op jit(solution)/shard_map/product/pallas_call | solution.py:219
  139.9 0.6 multiply_add_fusion
  140.6 6.3 %product.5 = bf16[2048,2048]{1,0:T(8,128)(2,1)} custom-call(s32[4]{0:T(128)S(1)} %fusion.2.places, bf16[2048,512]{1,0:T(8,128)(2,1)S(1)} %copy-done.1, bf16[512,256]{1,0:T(8,128)(2,1)S(1)} %relay.25.refs_12_.refs_4_.refs_0_, bf16[512,256]{1,0:T(8,128)(2,1)S(1)} %relay.29.refs_13_.refs_5_.refs_1_, ...), custom_call_target="tpu_custom_call", output_to_operand_aliasing={{}: (30, {})} | custom-call | flops 2147483648 | bytes 2097152 | tf_op jit(solution)/shard_map/product/pallas_call | solution.py:219
  (123 shorter events, 10.0 us)
Async XLA Ops:
  0.6 25.3 %collective-permute-start.36 = (bf16[256,2048]{1,0:T(8,128)(2,1)}, bf16[256,2048]{1,0:T(8,128)(2,1)}, u32[]{:S(2)}, u32[]{:S(2)}) collective-permute-start(bf16[256,2048]{1,0:T(8,128)(2,1)} %refs_0_.1), channel_id=1, source_target_pairs={{0,28},{4,0},{8,4},{12,8},{16,12},{20,16},{24,20},{28,24},{1,29},{... | collective-permute-start | bytes 3145736 | tf_op jit(solution)/shard_map/ppermute | solution.py:327
  5.3 11.4 %collective-permute-start.4 = (bf16[512,256]{1,0:T(8,128)(2,1)S(1)}, bf16[512,256]{1,0:T(8,128)(2,1)S(1)}, u32[]{:S(2)}, u32[]{:S(2)}) collective-permute-start(bf16[512,256]{1,0:T(8,128)(2,1)S(1)} %get-tuple-element.11), channel_id=1, source_target_pairs={{0,1},{1,2},{5,4},{6,5},{9,10},{10,11},{13,12},{14,13},{18,19},{22... | collective-permute-start | bytes 786440 | tf_op jit(solution)/shard_map/ppermute | solution.py:285
  8.8 10.8 %collective-permute-start = (bf16[512,256]{1,0:T(8,128)(2,1)S(1)}, bf16[512,256]{1,0:T(8,128)(2,1)S(1)}, u32[]{:S(2)}, u32[]{:S(2)}) collective-permute-start(bf16[512,256]{1,0:T(8,128)(2,1)S(1)} %get-tuple-element.10), channel_id=1, source_target_pairs={{1,0},{5,6},{6,7},{9,8},{10,9},{13,14},{14,15},{18,17},{19,18},{22... | collective-permute-start | bytes 786440 | tf_op jit(solution)/shard_map/ppermute | solution.py:285
  10.1 12.6 %collective-permute-start.8 = (bf16[512,256]{1,0:T(8,128)(2,1)S(1)}, bf16[512,256]{1,0:T(8,128)(2,1)S(1)}, u32[]{:S(2)}, u32[]{:S(2)}) collective-permute-start(bf16[512,256]{1,0:T(8,128)(2,1)S(1)} %get-tuple-element.12), channel_id=1, source_target_pairs={{1,0},{4,5},{5,6},{9,8},{10,9},{14,15},{18,17},{19,18},{20,21},{27... | collective-permute-start | bytes 786440 | tf_op jit(solution)/shard_map/ppermute | solution.py:285
  11.4 13.2 %collective-permute-start.12 = (bf16[512,256]{1,0:T(8,128)(2,1)S(1)}, bf16[512,256]{1,0:T(8,128)(2,1)S(1)}, u32[]{:S(2)}, u32[]{:S(2)}) collective-permute-start(bf16[512,256]{1,0:T(8,128)(2,1)S(1)} %get-tuple-element.13), channel_id=1, source_target_pairs={{0,1},{1,2},{5,4},{9,10},{10,11},{14,13},{15,14},{18,19},{22,21},{... | collective-permute-start | bytes 786440 | tf_op jit(solution)/shard_map/ppermute | solution.py:285
  18.9 8.9 %copy-start.24 = (bf16[512,256]{1,0:T(8,128)(2,1)}, bf16[512,256]{1,0:T(8,128)(2,1)S(1)}, u32[]{:S(2)}) copy-start(bf16[512,256]{1,0:T(8,128)(2,1)S(1)} %relay.26.refs_1_) | copy-start | bytes 786436
  18.9 8.3 %collective-permute-start.5 = (bf16[512,256]{1,0:T(8,128)(2,1)S(1)}, bf16[512,256]{1,0:T(8,128)(2,1)S(1)}, u32[]{:S(2)}, u32[]{:S(2)}) collective-permute-start(bf16[512,256]{1,0:T(8,128)(2,1)S(1)} %relay.26.refs_1_), channel_id=1, source_target_pairs={{1,2},{2,3},{5,4},{10,11},{13,12},{18,19},{21,20},{22,21},{23,22},... | collective-permute-start | bytes 786440 | tf_op jit(solution)/shard_map/ppermute | solution.py:285
  20.2 12.5 %copy-start.22 = (bf16[512,256]{1,0:T(8,128)(2,1)}, bf16[512,256]{1,0:T(8,128)(2,1)S(1)}, u32[]{:S(2)}) copy-start(bf16[512,256]{1,0:T(8,128)(2,1)S(1)} %relay.22.refs_0_) | copy-start | bytes 786436
  20.2 11.8 %collective-permute-start.1 = (bf16[512,256]{1,0:T(8,128)(2,1)S(1)}, bf16[512,256]{1,0:T(8,128)(2,1)S(1)}, u32[]{:S(2)}, u32[]{:S(2)}) collective-permute-start(bf16[512,256]{1,0:T(8,128)(2,1)S(1)} %relay.22.refs_0_), channel_id=1, source_target_pairs={{1,0},{6,7},{9,8},{14,15},{17,16},{18,17},{22,23},{26,25},{27,26},... | collective-permute-start | bytes 786440 | tf_op jit(solution)/shard_map/ppermute | solution.py:285
  23.4 12.3 %copy-start.20 = (bf16[512,256]{1,0:T(8,128)(2,1)}, bf16[512,256]{1,0:T(8,128)(2,1)S(1)}, u32[]{:S(2)}) copy-start(bf16[512,256]{1,0:T(8,128)(2,1)S(1)} %relay.30.refs_2_) | copy-start | bytes 786436
  23.4 11.7 %collective-permute-start.9 = (bf16[512,256]{1,0:T(8,128)(2,1)S(1)}, bf16[512,256]{1,0:T(8,128)(2,1)S(1)}, u32[]{:S(2)}, u32[]{:S(2)}) collective-permute-start(bf16[512,256]{1,0:T(8,128)(2,1)S(1)} %relay.30.refs_2_), channel_id=1, source_target_pairs={{1,0},{5,6},{6,7},{9,8},{13,14},{14,15},{17,16},{18,17},{20,21},{2... | collective-permute-start | bytes 786440 | tf_op jit(solution)/shard_map/ppermute | solution.py:285
  25.3 16.0 %copy-start.10 = (bf16[512,256]{1,0:T(8,128)(2,1)}, bf16[512,256]{1,0:T(8,128)(2,1)S(1)}, u32[]{:S(2)}) copy-start(bf16[512,256]{1,0:T(8,128)(2,1)S(1)} %relay.34.refs_3_) | copy-start | bytes 786436
  25.3 15.4 %collective-permute-start.13 = (bf16[512,256]{1,0:T(8,128)(2,1)S(1)}, bf16[512,256]{1,0:T(8,128)(2,1)S(1)}, u32[]{:S(2)}, u32[]{:S(2)}) collective-permute-start(bf16[512,256]{1,0:T(8,128)(2,1)S(1)} %relay.34.refs_3_), channel_id=1, source_target_pairs={{1,2},{2,3},{5,4},{6,5},{10,11},{13,12},{14,13},{18,19},{21,20},{2... | collective-permute-start | bytes 786440 | tf_op jit(solution)/shard_map/ppermute | solution.py:285
  26.0 42.1 %collective-permute-start.37 = (bf16[256,2048]{1,0:T(8,128)(2,1)}, bf16[256,2048]{1,0:T(8,128)(2,1)}, u32[]{:S(2)}, u32[]{:S(2)}) collective-permute-start(bf16[256,2048]{1,0:T(8,128)(2,1)} %collective-permute-done.36.refs_1_), channel_id=1, source_target_pairs={{0,28},{4,0},{8,4},{12,8},{16,12},{20,16},{24,20},{28,24},{1,29},{... | collective-permute-start | bytes 3145736 | tf_op jit(solution)/shard_map/ppermute | solution.py:337
  27.9 18.5 %copy-start.12 = (bf16[512,256]{1,0:T(8,128)(2,1)}, bf16[512,256]{1,0:T(8,128)(2,1)S(1)}, u32[]{:S(2)}) copy-start(bf16[512,256]{1,0:T(8,128)(2,1)S(1)} %relay.27.refs_5_) | copy-start | bytes 786436
  27.9 17.9 %collective-permute-start.6 = (bf16[512,256]{1,0:T(8,128)(2,1)S(1)}, bf16[512,256]{1,0:T(8,128)(2,1)S(1)}, u32[]{:S(2)}, u32[]{:S(2)}) collective-permute-start(bf16[512,256]{1,0:T(8,128)(2,1)S(1)} %relay.27.refs_5_), channel_id=1, source_target_pairs={{0,1},{1,2},{2,3},{5,4},{9,10},{10,11},{13,12},{14,13},{18,19},{21... | collective-permute-start | bytes 786440 | tf_op jit(solution)/shard_map/ppermute | solution.py:285
  32.7 15.0 %copy-start.14 = (bf16[512,256]{1,0:T(8,128)(2,1)}, bf16[512,256]{1,0:T(8,128)(2,1)S(1)}, u32[]{:S(2)}) copy-start(bf16[512,256]{1,0:T(8,128)(2,1)S(1)} %relay.23.refs_4_) | copy-start | bytes 786436
  32.7 14.4 %collective-permute-start.2 = (bf16[512,256]{1,0:T(8,128)(2,1)S(1)}, bf16[512,256]{1,0:T(8,128)(2,1)S(1)}, u32[]{:S(2)}, u32[]{:S(2)}) collective-permute-start(bf16[512,256]{1,0:T(8,128)(2,1)S(1)} %relay.23.refs_4_), channel_id=1, source_target_pairs={{1,0},{5,6},{6,7},{9,8},{10,9},{14,15},{17,16},{18,17},{19,18},{22... | collective-permute-start | bytes 786440 | tf_op jit(solution)/shard_map/ppermute | solution.py:285
  35.6 14.0 %copy-start.16 = (bf16[512,256]{1,0:T(8,128)(2,1)}, bf16[512,256]{1,0:T(8,128)(2,1)S(1)}, u32[]{:S(2)}) copy-start(bf16[512,256]{1,0:T(8,128)(2,1)S(1)} %relay.31.refs_6_) | copy-start | bytes 786436
  35.7 13.4 %collective-permute-start.10 = (bf16[512,256]{1,0:T(8,128)(2,1)S(1)}, bf16[512,256]{1,0:T(8,128)(2,1)S(1)}, u32[]{:S(2)}, u32[]{:S(2)}) collective-permute-start(bf16[512,256]{1,0:T(8,128)(2,1)S(1)} %relay.31.refs_6_), channel_id=1, source_target_pairs={{1,0},{4,5},{5,6},{6,7},{9,8},{10,9},{14,15},{17,16},{18,17},{19,1... | collective-permute-start | bytes 786440 | tf_op jit(solution)/shard_map/ppermute | solution.py:285
  41.3 10.3 %copy-start.18 = (bf16[512,256]{1,0:T(8,128)(2,1)}, bf16[512,256]{1,0:T(8,128)(2,1)S(1)}, u32[]{:S(2)}) copy-start(bf16[512,256]{1,0:T(8,128)(2,1)S(1)} %relay.35.refs_7_) | copy-start | bytes 786436
  41.3 9.6 %collective-permute-start.14 = (bf16[512,256]{1,0:T(8,128)(2,1)S(1)}, bf16[512,256]{1,0:T(8,128)(2,1)S(1)}, u32[]{:S(2)}, u32[]{:S(2)}) collective-permute-start(bf16[512,256]{1,0:T(8,128)(2,1)S(1)} %relay.35.refs_7_), channel_id=1, source_target_pairs={{0,1},{1,2},{2,3},{5,4},{9,10},{10,11},{13,12},{14,13},{15,14},{18... | collective-permute-start | bytes 786440 | tf_op jit(solution)/shard_map/ppermute | solution.py:285
  46.4 7.1 %copy-start.2 = (bf16[512,256]{1,0:T(8,128)(2,1)}, bf16[512,256]{1,0:T(8,128)(2,1)S(1)}, u32[]{:S(2)}) copy-start(bf16[512,256]{1,0:T(8,128)(2,1)S(1)} %relay.28.refs_9_.refs_1_) | copy-start | bytes 786436
  46.4 6.6 %collective-permute-start.7 = (bf16[512,256]{1,0:T(8,128)(2,1)S(1)}, bf16[512,256]{1,0:T(8,128)(2,1)S(1)}, u32[]{:S(2)}, u32[]{:S(2)}) collective-permute-start(bf16[512,256]{1,0:T(8,128)(2,1)S(1)} %relay.28.refs_9_.refs_1_), channel_id=1, source_target_pairs={{1,2},{2,3},{5,4},{6,5},{10,11},{13,12},{18,19},{21,20},{22,21},{2... | collective-permute-start | bytes 786440 | tf_op jit(solution)/shard_map/ppermute | solution.py:285
  47.7 12.2 %copy-start.4 = (bf16[512,256]{1,0:T(8,128)(2,1)}, bf16[512,256]{1,0:T(8,128)(2,1)S(1)}, u32[]{:S(2)}) copy-start(bf16[512,256]{1,0:T(8,128)(2,1)S(1)} %relay.24.refs_8_.refs_0_) | copy-start | bytes 786436
  47.7 12.1 %collective-permute-start.3 = (bf16[512,256]{1,0:T(8,128)(2,1)S(1)}, bf16[512,256]{1,0:T(8,128)(2,1)S(1)}, u32[]{:S(2)}, u32[]{:S(2)}) collective-permute-start(bf16[512,256]{1,0:T(8,128)(2,1)S(1)} %relay.24.refs_8_.refs_0_), channel_id=1, source_target_pairs={{1,0},{6,7},{9,8},{13,14},{14,15},{17,16},{18,17},{22,23},{25,24},... | collective-permute-start | bytes 786440 | tf_op jit(solution)/shard_map/ppermute | solution.py:285
  49.7 13.1 %copy-start.6 = (bf16[512,256]{1,0:T(8,128)(2,1)}, bf16[512,256]{1,0:T(8,128)(2,1)S(1)}, u32[]{:S(2)}) copy-start(bf16[512,256]{1,0:T(8,128)(2,1)S(1)} %relay.32.refs_10_.refs_2_) | copy-start | bytes 786436
  49.7 12.5 %collective-permute-start.11 = (bf16[512,256]{1,0:T(8,128)(2,1)S(1)}, bf16[512,256]{1,0:T(8,128)(2,1)S(1)}, u32[]{:S(2)}, u32[]{:S(2)}) collective-permute-start(bf16[512,256]{1,0:T(8,128)(2,1)S(1)} %relay.32.refs_10_.refs_2_), channel_id=1, source_target_pairs={{1,0},{5,6},{6,7},{9,8},{14,15},{17,16},{18,17},{20,21},{21,22},{2... | collective-permute-start | bytes 786440 | tf_op jit(solution)/shard_map/ppermute | solution.py:285
  51.6 14.2 %copy-start.8 = (bf16[512,256]{1,0:T(8,128)(2,1)}, bf16[512,256]{1,0:T(8,128)(2,1)S(1)}, u32[]{:S(2)}) copy-start(bf16[512,256]{1,0:T(8,128)(2,1)S(1)} %relay.36.refs_11_.refs_3_) | copy-start | bytes 786436
  51.6 12.5 %collective-permute-start.15 = (bf16[512,256]{1,0:T(8,128)(2,1)S(1)}, bf16[512,256]{1,0:T(8,128)(2,1)}, u32[]{:S(2)}, u32[]{:S(2)}) collective-permute-start(bf16[512,256]{1,0:T(8,128)(2,1)S(1)} %relay.36.refs_11_.refs_3_), channel_id=1, source_target_pairs={{1,2},{2,3},{5,4},{10,11},{13,12},{14,13},{18,19},{21,20},{22,21},... | collective-permute-start | bytes 786440 | tf_op jit(solution)/shard_map/ppermute | solution.py:285
  53.6 14.4 %copy-start.29 = (f32[2048]{0:T(1024)S(1)}, f32[2048]{0:T(1024)}, u32[]{:S(2)}) copy-start(f32[2048]{0:T(1024)} %param.12) | copy-start | bytes 24580
  53.6 14.4 %copy-start.30 = (f32[2048]{0:T(1024)S(1)}, f32[2048]{0:T(1024)}, u32[]{:S(2)}) copy-start(f32[2048]{0:T(1024)} %param.13) | copy-start | bytes 24580
  53.6 18.2 %copy-start.1 = (bf16[2048,512]{1,0:T(8,128)(2,1)S(1)}, bf16[2048,512]{1,0:T(8,128)(2,1)}, u32[]{:S(2)}) copy-start(bf16[2048,512]{1,0:T(8,128)(2,1)} %x.49) | copy-start | bytes 6291460
  53.6 18.2 %collective-permute-start.17 = (bf16[512,256]{1,0:T(8,128)(2,1)S(1)}, bf16[512,256]{1,0:T(8,128)(2,1)S(1)}, u32[]{:S(2)}, u32[]{:S(2)}) collective-permute-start(bf16[512,256]{1,0:T(8,128)(2,1)S(1)} %relay.29.refs_13_.refs_5_.refs_1_), channel_id=1, source_target_pairs={{0,1},{1,2},{2,3},{5,4},{9,10},{10,11},{13,12},{14,13},{21,20},{22... | collective-permute-start | bytes 786440 | tf_op jit(solution)/shard_map/ppermute | solution.py:285
  60.5 13.3 %collective-permute-start.16 = (bf16[512,256]{1,0:T(8,128)(2,1)S(1)}, bf16[512,256]{1,0:T(8,128)(2,1)S(1)}, u32[]{:S(2)}, u32[]{:S(2)}) collective-permute-start(bf16[512,256]{1,0:T(8,128)(2,1)S(1)} %relay.25.refs_12_.refs_4_.refs_0_), channel_id=1, source_target_pairs={{5,6},{6,7},{9,8},{10,9},{14,15},{17,16},{18,17},{19,18},{25,24},{... | collective-permute-start | bytes 786440 | tf_op jit(solution)/shard_map/ppermute | solution.py:285
  62.7 16.6 %copy-start.27 = (s32[2048]{0:T(1024)S(1)}, s32[2048]{0:T(1024)}, u32[]{:S(2)}) copy-start(s32[2048]{0:T(1024)} %param.14) | copy-start | bytes 24580
  62.7 13.1 %collective-permute-start.18 = (bf16[512,256]{1,0:T(8,128)(2,1)S(1)}, bf16[512,256]{1,0:T(8,128)(2,1)}, u32[]{:S(2)}, u32[]{:S(2)}) collective-permute-start(bf16[512,256]{1,0:T(8,128)(2,1)S(1)} %relay.33.refs_14_.refs_6_.refs_2_), channel_id=1, source_target_pairs={{4,5},{5,6},{6,7},{9,8},{10,9},{13,14},{14,15},{17,16},{18,17},{19... | collective-permute-start | bytes 786440 | tf_op jit(solution)/shard_map/ppermute | solution.py:285
  65.8 11.4 %collective-permute-start.19 = (bf16[512,256]{1,0:T(8,128)(2,1)}, bf16[512,256]{1,0:T(8,128)(2,1)}, u32[]{:S(2)}, u32[]{:S(2)}) collective-permute-start(bf16[512,256]{1,0:T(8,128)(2,1)} %relay.37.refs_15_.refs_7_.refs_3_), channel_id=1, source_target_pairs={{0,1},{1,2},{2,3},{5,4},{6,5},{9,10},{10,11},{13,12},{14,13},{15,1... | collective-permute-start | bytes 786440 | tf_op jit(solution)/shard_map/ppermute | solution.py:285
  68.1 44.9 %collective-permute-start.38 = (bf16[256,2048]{1,0:T(8,128)(2,1)}, bf16[256,2048]{1,0:T(8,128)(2,1)}, u32[]{:S(2)}, u32[]{:S(2)}) collective-permute-start(bf16[256,2048]{1,0:T(8,128)(2,1)} %collective-permute-done.37.refs_2_), channel_id=1, source_target_pairs={{0,28},{4,0},{8,4},{12,8},{16,12},{20,16},{24,20},{28,24},{1,29},{... | collective-permute-start | bytes 3145736 | tf_op jit(solution)/shard_map/ppermute | solution.py:337
  72.4 7.0 %collective-permute-start.21 = (bf16[512,256]{1,0:T(8,128)(2,1)S(1)}, bf16[512,256]{1,0:T(8,128)(2,1)}, u32[]{:S(2)}, u32[]{:S(2)}) collective-permute-start(bf16[512,256]{1,0:T(8,128)(2,1)S(1)} %relay.39.refs_17_.refs_9_.refs_5_), channel_id=1, source_target_pairs={{1,2},{2,3},{5,4},{10,11},{13,12},{21,20},{22,21},{26,27}} | collective-permute-start | bytes 786440 | tf_op jit(solution)/shard_map/ppermute | solution.py:285
  74.4 13.9 %collective-permute-start.20 = (bf16[512,256]{1,0:T(8,128)(2,1)S(1)}, bf16[512,256]{1,0:T(8,128)(2,1)}, u32[]{:S(2)}, u32[]{:S(2)}) collective-permute-start(bf16[512,256]{1,0:T(8,128)(2,1)S(1)} %relay.38.refs_16_.refs_8_.refs_4_), channel_id=1, source_target_pairs={{6,7},{9,8},{14,15},{17,16},{18,17},{25,24},{29,30},{30,31}} | collective-permute-start | bytes 786440 | tf_op jit(solution)/shard_map/ppermute | solution.py:285
  75.8 15.0 %collective-permute-start.22 = (bf16[512,256]{1,0:T(8,128)(2,1)}, bf16[512,256]{1,0:T(8,128)(2,1)}, u32[]{:S(2)}, u32[]{:S(2)}) collective-permute-start(bf16[512,256]{1,0:T(8,128)(2,1)} %collective-permute-done.18.refs_18_.refs_10_.refs_6_), channel_id=1, source_target_pairs={{5,6},{6,7},{9,8},{14,15},{17,16},{18,17},{22,23},{25,24},{29,30},... | collective-permute-start | bytes 786440 | tf_op jit(solution)/shard_map/ppermute | solution.py:285
  77.2 16.0 %collective-permute-start.23 = (bf16[512,256]{1,0:T(8,128)(2,1)}, bf16[512,256]{1,0:T(8,128)(2,1)}, u32[]{:S(2)}, u32[]{:S(2)}) collective-permute-start(bf16[512,256]{1,0:T(8,128)(2,1)} %collective-permute-done.19.refs_19_.refs_11_.refs_7_), channel_id=1, source_target_pairs={{1,2},{2,3},{5,4},{10,11},{13,12},{14,13},{21,20},{22,21},{26,27},... | collective-permute-start | bytes 786440 | tf_op jit(solution)/shard_map/ppermute | solution.py:285
  81.1 18.8 %collective-permute-start.25 = (bf16[512,256]{1,0:T(8,128)(2,1)}, bf16[512,256]{1,0:T(8,128)(2,1)S(1)}, u32[]{:S(2)}, u32[]{:S(2)}) collective-permute-start(bf16[512,256]{1,0:T(8,128)(2,1)} %relay.41.refs_13_.refs_9_), channel_id=1, source_target_pairs={{0,1},{1,2},{2,3},{9,10},{10,11},{13,12},{14,13},{21,20}} | collective-permute-start | bytes 786440 | tf_op jit(solution)/shard_map/ppermute | solution.py:285
  90.0 14.4 %copy-start.28 = (s32[2048]{0:T(1024)S(1)}, s32[2048]{0:T(1024)}, u32[]{:S(2)}) copy-start(s32[2048]{0:T(1024)} %param.15) | copy-start | bytes 24580
  90.0 24.1 %copy-start.26 = (bf16[256,2048]{1,0:T(8,128)(2,1)S(1)}, bf16[256,2048]{1,0:T(8,128)(2,1)}, u32[]{:S(2)}) copy-start(bf16[256,2048]{1,0:T(8,128)(2,1)} %refs_0_.1) | copy-start | bytes 3145732
  90.0 10.6 %collective-permute-start.24 = (bf16[512,256]{1,0:T(8,128)(2,1)}, bf16[512,256]{1,0:T(8,128)(2,1)S(1)}, u32[]{:S(2)}, u32[]{:S(2)}) collective-permute-start(bf16[512,256]{1,0:T(8,128)(2,1)} %relay.40.refs_12_.refs_8_), channel_id=1, source_target_pairs={{5,6},{6,7},{9,8},{10,9},{17,16},{18,17},{19,18},{30,31}} | collective-permute-start | bytes 786440 | tf_op jit(solution)/shard_map/ppermute | solution.py:285
  92.5 8.8 %collective-permute-start.26 = (bf16[512,256]{1,0:T(8,128)(2,1)}, bf16[512,256]{1,0:T(8,128)(2,1)S(1)}, u32[]{:S(2)}, u32[]{:S(2)}) collective-permute-start(bf16[512,256]{1,0:T(8,128)(2,1)} %relay.42.refs_14_.refs_10_), channel_id=1, source_target_pairs={{4,5},{5,6},{6,7},{9,8},{10,9},{17,16},{18,17},{19,18},{30,31}} | collective-permute-start | bytes 786440 | tf_op jit(solution)/shard_map/ppermute | solution.py:285
  94.9 8.1 %collective-permute-start.27 = (bf16[512,256]{1,0:T(8,128)(2,1)}, bf16[512,256]{1,0:T(8,128)(2,1)S(1)}, u32[]{:S(2)}, u32[]{:S(2)}) collective-permute-start(bf16[512,256]{1,0:T(8,128)(2,1)} %relay.43.refs_15_.refs_11_), channel_id=1, source_target_pairs={{0,1},{1,2},{2,3},{9,10},{10,11},{13,12},{14,13},{15,14},{21,20}} | collective-permute-start | bytes 786440 | tf_op jit(solution)/shard_map/ppermute | solution.py:285
  99.9 4.5 %collective-permute-start.29 = (bf16[512,256]{1,0:T(8,128)(2,1)S(1)}, bf16[512,256]{1,0:T(8,128)(2,1)S(1)}, u32[]{:S(2)}, u32[]{:S(2)}) collective-permute-start(bf16[512,256]{1,0:T(8,128)(2,1)S(1)} %collective-permute-done.25.refs_17_.refs_13_), channel_id=1, source_target_pairs={{1,2},{2,3},{10,11},{13,12}} | collective-permute-start | bytes 786440 | tf_op jit(solution)/shard_map/ppermute | solution.py:285
  100.6 10.3 %collective-permute-start.28 = (bf16[512,256]{1,0:T(8,128)(2,1)S(1)}, bf16[512,256]{1,0:T(8,128)(2,1)S(1)}, u32[]{:S(2)}, u32[]{:S(2)}) collective-permute-start(bf16[512,256]{1,0:T(8,128)(2,1)S(1)} %collective-permute-done.24.refs_16_.refs_12_), channel_id=1, source_target_pairs={{6,7},{9,8},{17,16},{18,17}} | collective-permute-start | bytes 786440 | tf_op jit(solution)/shard_map/ppermute | solution.py:285
  101.3 10.3 %collective-permute-start.30 = (bf16[512,256]{1,0:T(8,128)(2,1)S(1)}, bf16[512,256]{1,0:T(8,128)(2,1)S(1)}, u32[]{:S(2)}, u32[]{:S(2)}) collective-permute-start(bf16[512,256]{1,0:T(8,128)(2,1)S(1)} %collective-permute-done.26.refs_18_.refs_14_), channel_id=1, source_target_pairs={{5,6},{6,7},{9,8},{17,16},{18,17}} | collective-permute-start | bytes 786440 | tf_op jit(solution)/shard_map/ppermute | solution.py:285
  103.0 9.3 %collective-permute-start.31 = (bf16[512,256]{1,0:T(8,128)(2,1)S(1)}, bf16[512,256]{1,0:T(8,128)(2,1)S(1)}, u32[]{:S(2)}, u32[]{:S(2)}) collective-permute-start(bf16[512,256]{1,0:T(8,128)(2,1)S(1)} %collective-permute-done.27.refs_19_.refs_15_), channel_id=1, source_target_pairs={{1,2},{2,3},{10,11},{13,12},{14,13}} | collective-permute-start | bytes 786440 | tf_op jit(solution)/shard_map/ppermute | solution.py:285
  104.4 22.9 %collective-permute-start.39 = (f32[2048]{0:T(1024)S(1)}, f32[2048]{0:T(1024)S(1)}, u32[]{:S(2)}, u32[]{:S(2)}) collective-permute-start(f32[2048]{0:T(1024)S(1)} %multiply_reduce_fusion), channel_id=1, source_target_pairs={{0,1},{1,0},{2,3},{3,2},{4,5},{5,4},{6,7},{7,6},{8,9},{9,8},{10,11... | collective-permute-start | bytes 24584 | tf_op jit(solution)/shard_map/ppermute | solution.py:345
  110.9 29.6 %collective-permute-start.33 = (bf16[512,256]{1,0:T(8,128)(2,1)S(1)}, bf16[512,256]{1,0:T(8,128)(2,1)S(1)}, u32[]{:S(2)}, u32[]{:S(2)}) collective-permute-start(bf16[512,256]{1,0:T(8,128)(2,1)S(1)} %collective-permute-done.29.refs_17_), channel_id=1, source_target_pairs={{2,3}} | collective-permute-start | bytes 786440 | tf_op jit(solution)/shard_map/ppermute | solution.py:285
  111.6 28.9 %collective-permute-start.32 = (bf16[512,256]{1,0:T(8,128)(2,1)S(1)}, bf16[512,256]{1,0:T(8,128)(2,1)S(1)}, u32[]{:S(2)}, u32[]{:S(2)}) collective-permute-start(bf16[512,256]{1,0:T(8,128)(2,1)S(1)} %collective-permute-done.28.refs_16_), channel_id=1, source_target_pairs={{17,16}} | collective-permute-start | bytes 786440 | tf_op jit(solution)/shard_map/ppermute | solution.py:285
  112.3 28.2 %collective-permute-start.34 = (bf16[512,256]{1,0:T(8,128)(2,1)S(1)}, bf16[512,256]{1,0:T(8,128)(2,1)S(1)}, u32[]{:S(2)}, u32[]{:S(2)}) collective-permute-start(bf16[512,256]{1,0:T(8,128)(2,1)S(1)} %collective-permute-done.30.refs_18_), channel_id=1, source_target_pairs={{6,7},{17,16}} | collective-permute-start | bytes 786440 | tf_op jit(solution)/shard_map/ppermute | solution.py:285
  113.0 27.6 %collective-permute-start.35 = (bf16[512,256]{1,0:T(8,128)(2,1)S(1)}, bf16[512,256]{1,0:T(8,128)(2,1)S(1)}, u32[]{:S(2)}, u32[]{:S(2)}) collective-permute-start(bf16[512,256]{1,0:T(8,128)(2,1)S(1)} %collective-permute-done.31.refs_19_), channel_id=1, source_target_pairs={{2,3},{13,12}} | collective-permute-start | bytes 786440 | tf_op jit(solution)/shard_map/ppermute | solution.py:285
  114.1 4.0 %copy-start.3 = (bf16[512,256]{1,0:T(8,128)(2,1)S(1)}, bf16[512,256]{1,0:T(8,128)(2,1)}, u32[]{:S(2)}) copy-start(bf16[512,256]{1,0:T(8,128)(2,1)} %copy-done.2) | copy-start | bytes 786436
  114.1 4.0 %copy-start.5 = (bf16[512,256]{1,0:T(8,128)(2,1)S(1)}, bf16[512,256]{1,0:T(8,128)(2,1)}, u32[]{:S(2)}) copy-start(bf16[512,256]{1,0:T(8,128)(2,1)} %copy-done.4) | copy-start | bytes 786436
  114.1 4.0 %copy-start.7 = (bf16[512,256]{1,0:T(8,128)(2,1)S(1)}, bf16[512,256]{1,0:T(8,128)(2,1)}, u32[]{:S(2)}) copy-start(bf16[512,256]{1,0:T(8,128)(2,1)} %copy-done.6) | copy-start | bytes 786436
  114.1 4.0 %copy-start.9 = (bf16[512,256]{1,0:T(8,128)(2,1)S(1)}, bf16[512,256]{1,0:T(8,128)(2,1)}, u32[]{:S(2)}) copy-start(bf16[512,256]{1,0:T(8,128)(2,1)} %copy-done.8) | copy-start | bytes 786436
  114.1 4.0 %copy-start.11 = (bf16[512,256]{1,0:T(8,128)(2,1)S(1)}, bf16[512,256]{1,0:T(8,128)(2,1)}, u32[]{:S(2)}) copy-start(bf16[512,256]{1,0:T(8,128)(2,1)} %copy-done.10) | copy-start | bytes 786436
  127.3 12.6 %collective-permute-start.40 = (f32[2048]{0:T(1024)S(1)}, f32[2048]{0:T(1024)S(1)}, u32[]{:S(2)}, u32[]{:S(2)}) collective-permute-start(f32[2048]{0:T(1024)S(1)} %add.62), channel_id=1, source_target_pairs={{0,2},{1,3},{2,0},{3,1},{4,6},{5,7},{6,4},{7,5},{8,10},{9,11},{10,... | collective-permute-start | bytes 24584 | tf_op jit(solution)/shard_map/ppermute | solution.py:345
  (8 other events, 29.5 us)

commit v8 on v7

--- a/solution.py
+++ b/solution.py
@@ -1,4 +1,5 @@
 import functools
+import itertools
 
 import jax
 import jax.numpy as jnp
@@ -9,9 +10,10 @@
 from jax.sharding import PartitionSpec as P
 
 STEPS = 4
-PIECES = 4
-PARTS = ((0, 2), (2, 3), (3, 4))
-CHAINS = 2
+PIECES = 2
+PARTS = ((0, 1), (1, 2))
+DEPTH = 1
+HOP = 2
 COL_TILE = 512
 ROW_TILE = 32
 LANES = 128
@@ -19,58 +21,127 @@
 RELAY_LIMIT = 8 * 2**20
 
 
-class Line:
-    def __init__(self, chunks):
-        self.slots = {}
-        todo = sorted(chunks)
-        slot = 1
-        while todo:
-            for chunk in todo:
-                if chunk[1] <= slot:
-                    self.slots[slot] = chunk
-                    todo.remove(chunk)
-                    break
-            slot += 1
-
-    def sent(self, p, t):
-        chunk = self.slots.get(t + p - 1) if p > 0 else None
-        return chunk if chunk is not None and chunk[1] >= p else None
-
-
-class Plan:
-    def __init__(self, rows, cols, groups_here):
+class Item:
+    def __init__(self, row, piece, s, place, home=None):
+        self.row, self.piece, self.s, self.place = row, piece, s, place
+        self.home = home
+
+    @property
+    def owner(self):
+        return self.row if self.home is None else self.home
+
+    @property
+    def key(self):
+        return self.piece, self.s
+
+
+def line_slots(items, cut):
+    ends, inner = {}, {}
+    todo = sorted(items, key=lambda i: (i.home is None, i.piece, i.place, i.s))
+    slot = 1
+    while todo:
+        for item in todo:
+            first = 1 + DEPTH * (item.place - 1) + (HOP if item.home is not None else 0)
+            if first <= slot:
+                ends[slot] = item
+                if item.place > 1:
+                    inner[slot] = item
+                todo.remove(item)
+                break
+        slot += 1
+    for item in sorted(cut, key=lambda i: (i.place, i.key)):
+        slot = 1 + DEPTH * (item.place - 1)
+        if item.place > 1:
+            while slot in inner:
+                slot += 1
+            inner[slot] = item
+    return ends, inner
+
+
+class Lane:
+    def __init__(self, rows, cols, groups_here, towards_zero):
         self.rows, self.cols = rows, cols
-        self.lines = {}
-        for phase in range(2):
-            for r in range(rows):
-                place = [self.position(phase, r, (r + s) % rows // groups_here) for s in range(STEPS)]
-                order = sorted((q, place[s], s) for q in range(PIECES) for s in range(STEPS) if place[s] > 0)
-                for chain in range(CHAINS):
-                    self.lines[phase, chain, r] = Line(order[chain::CHAINS])
-        self.rounds = max(max(line.slots, default=0) for line in self.lines.values())
-
-    def position(self, phase, r, c):
-        return c if (r + phase) % 2 == 0 else self.cols - 1 - c
-
-    def sent(self, phase, chain, r, c, t):
-        return self.lines[phase, chain, r].sent(self.position(phase, r, c), t)
-
-    def pairs(self, phase, chain, t):
+        self.towards_zero = towards_zero
+        self.items = []
+        for r in range(rows):
+            mine = [
+                Item(r, piece, s, self.place((r + s) % rows // groups_here))
+                for piece in range(PIECES)
+                for s in range(STEPS)
+            ]
+            self.items.append([i for i in mine if i.place > 0])
+        self.away = []
+        self.lines = [line_slots(items, []) for items in self.items]
+        if rows % 2 == 0 and cols > 3:
+            for r in range(rows // 2):
+                self.balance(r, r + rows // 2)
+                self.balance(r + rows // 2, r)
+        self.rounds = max(
+            [max(ends, default=0) for ends, _ in self.lines] + [max(inner, default=0) - DEPTH for _, inner in self.lines]
+        )
+
+    def place(self, c):
+        return c if self.towards_zero else self.cols - 1 - c
+
+    col = place
+
+    def balance(self, r, other):
+        if len(self.items[r]) < len(self.items[other]) or any(i.row == other for i in self.away):
+            return
+        places = sorted({i.place for i in self.items[r]})
+        best = None
+        for counts in itertools.product(range(3), repeat=len(places)):
+            gone = []
+            for place, count in zip(places, counts):
+                here = [i for i in self.items[r] if i.place == place]
+                here.sort(key=lambda i: i.key, reverse=True)
+                gone += here[:count]
+            visitors = [Item(other, i.piece, i.s, i.place, home=r) for i in gone]
+            mine = line_slots([i for i in self.items[r] if i not in gone], gone)
+            theirs = line_slots(self.items[other] + visitors, [])
+            score = (
+                max(max(mine[0], default=0), max(theirs[0], default=0)),
+                abs(len(mine[0]) - len(theirs[0])),
+                max([slot for slot, i in theirs[0].items() if i.home is not None], default=0),
+                len(gone),
+            )
+            if best is None or score < best[0]:
+                best = score, gone, mine, theirs
+        _, gone, mine, theirs = best
+        self.away += gone
+        if gone:
+            self.lines[r], self.lines[other] = mine, theirs
+
+    def sent(self, r, c, t):
+        p = self.place(c)
+        ends, inner = self.lines[r]
+        if p == 0:
+            return None
+        item = ends.get(t) if p == 1 else inner.get(t + DEPTH * (p - 1))
+        return item if item is not None and item.place >= p else None
+
+    def pairs(self, t):
         found = []
         for r in range(self.rows):
             for c in range(self.cols):
-                if self.sent(phase, chain, r, c, t) is not None:
-                    to = self.position(phase, r, self.position(phase, r, c) - 1)
-                    found.append((r * self.cols + c, r * self.cols + to))
+                if self.sent(r, c, t) is not None:
+                    found.append((r * self.cols + c, r * self.cols + self.col(self.place(c) - 1)))
         return found
 
-    def arrival(self, r, c, q, s):
-        for (phase, chain, row), line in self.lines.items():
-            if row == r:
-                p = self.position(phase, r, c)
-                for slot, chunk in line.slots.items():
-                    if (chunk[0], chunk[2]) == (q, s) and chunk[1] > p:
-                        return phase, chain, slot - p
+    def arrival(self, r, c, key):
+        p = self.place(c)
+        for i in self.items[r]:
+            if i.key != key or i.place <= p:
+                continue
+            ends, inner = self.lines[r]
+            if p == 0 and i in self.away:
+                for other, _ in self.lines:
+                    for slot, v in other.items():
+                        if v.home == r and v.key == key:
+                            return slot, True
+            for slot, v in (ends if p == 0 else inner).items():
+                if v is i:
+                    return slot - DEPTH * p, False
         return None
 
 
@@ -91,31 +162,33 @@
     return result.astype(jnp.int32)
 
 
-def relay_kernel(at, table, x, held, out):
+def relay_kernel(at, table, x, *refs):
+    *sources, out = refs
     rows, width = out.shape
 
-    @pl.when(table[at] == 1)
+    @pl.when(table[at] == 0)
     def _():
         row = pl.multiple_of(table[at + 1] * rows, rows)
         col = pl.multiple_of(table[at + 2] * width, width)
         out[...] = x[pl.ds(row, rows), pl.ds(col, width)]
 
-    @pl.when(table[at] == 0)
-    def _():
-        out[...] = held[...]
-
-
-def relay(at, table, x, held):
+    for i, source in enumerate(sources):
+
+        @pl.when(table[at] == i + 1)
+        def _(source=source):
+            out[...] = source[...]
+
+
+def relay(at, table, x, sources):
     return pl.pallas_call(
         functools.partial(relay_kernel, at),
-        out_shape=jax.ShapeDtypeStruct(held.shape, held.dtype),
-        in_specs=[pl.BlockSpec(memory_space=pltpu.SMEM)] + [pl.BlockSpec(memory_space=pltpu.VMEM)] * 2,
-        out_specs=pl.BlockSpec(memory_space=pltpu.VMEM),
-        input_output_aliases={2: 0},
+        out_shape=pltpu.VMEM(sources[0].shape, sources[0].dtype),
+        in_specs=[pl.BlockSpec(memory_space=pltpu.SMEM)] + [VMEM] * (1 + len(sources)),
+        out_specs=VMEM,
         compiler_params=pltpu.CompilerParams(vmem_limit_bytes=RELAY_LIMIT),
         cost_estimate=pl.CostEstimate(flops=0, bytes_accessed=0, transcendentals=0),
         name="relay",
-    )(table, in_vmem(x), in_vmem(held))
+    )(table, *[in_vmem(v) for v in (x, *sources)])
 
 
 def in_vmem(value):
@@ -242,47 +315,106 @@
     local_vars = x.shape[1]
     groups_here = local_vars // group_size
     piece_rows = x.shape[0] // PIECES
-    plan = Plan(rows, cols, groups_here)
+    lanes = [Lane(rows, cols, groups_here, towards) for towards in (True, False)]
+    rounds = max(lane.rounds for lane in lanes)
     devices = [(r, c) for r in range(rows) for c in range(cols)]
+    both = ("row", "col")
 
     row_place = lax.axis_index("row")
     col_place = lax.axis_index("col")
     device = row_place * cols + col_place
 
-    sends = [(phase, chain, t) for t in range(1, plan.rounds + 1) for chain in range(CHAINS) for phase in range(2)]
-    own_of = {}
+    def number(r, c):
+        return r * cols + c
+
+    def group_here(item):
+        return (item.owner + item.s) % rows % groups_here
+
+    crossings = []
+    crossing_of = {}
+    for d, lane in enumerate(lanes):
+        for r in range(rows):
+            for slot, item in sorted(lane.lines[r][0].items()):
+                if item.home is None:
+                    continue
+                source, target = (item.home, lane.col(item.place)), (r, lane.col(item.place))
+                for k, crossing in enumerate(crossings):
+                    if source not in crossing and target not in [to for to, _ in crossing.values()]:
+                        break
+                else:
+                    k = len(crossings)
+                    crossings.append({})
+                crossings[k][source] = (target, item)
+                crossing_of[d, r, item.key] = k
+
+    def lane_of(phase, r):
+        return (r + phase) % 2
+
+    sends = [(phase, t) for t in range(1, rounds + 1) for phase in range(2)]
+    pairs_of, kinds_of, own_of = {}, {}, {}
+    for phase, t in sends:
+        pairs, kinds, own = [], [], []
+        for r, c in devices:
+            lane = lanes[lane_of(phase, r)]
+            item = lane.sent(r, c, t)
+            if item is not None:
+                pairs.append((number(r, c), number(r, lane.col(lane.place(c) - 1))))
+            if item is None:
+                kinds.append(None)
+            elif item.place != lane.place(c):
+                kinds.append("forward")
+            elif item.home is not None:
+                kinds.append(crossing_of[lane_of(phase, r), r, item.key])
+            else:
+                kinds.append("own")
+            own.append(item if kinds[-1] == "own" else None)
+        pairs_of[phase, t], kinds_of[phase, t], own_of[phase, t] = pairs, kinds, own
+
+    returns = {}
+    for t in range(1, rounds + 1):
+        pairs, phases = [], [None] * len(devices)
+        for d, lane in enumerate(lanes):
+            for r in range(rows):
+                item = lane.lines[r][0].get(t)
+                if item is not None and item.home is not None:
+                    pairs.append((number(r, lane.col(0)), number(item.home, lane.col(0))))
+                    phases[pairs[-1][0]] = (r + d) % 2
+        if pairs:
+            returns[t] = pairs, phases
+
+    columns = []
+
+    def add(entries):
+        columns.append(np.asarray(entries, np.int32))
+        return sum(c.shape[1] for c in columns[:-1])
+
+    relays = {}
     for key in sends:
-        own_of[key] = []
-        for r, c in devices:
-            chunk = plan.sent(*key[:2], r, c, key[2])
-            mine = chunk is not None and chunk[1] == plan.position(key[0], r, c)
-            own_of[key].append((chunk[0], (r + chunk[2]) % rows % groups_here) if mine else None)
-    numbers = [[n for key in sends for n in ((1, *own_of[key][i]) if own_of[key][i] else (0, 0, 0))] for i in range(len(devices))]
-    table = lax.dynamic_slice(jnp.asarray(numbers, jnp.int32), (device, 0), (1, 3 * len(sends)))[0]
-
-    buffers = {}
-
-    def first(key):
-        own = own_of[key]
-        piece = lookup([None if o is None else o[0] for o in own], device)
-        group = lookup([None if o is None else o[1] for o in own], device)
+        kinds = kinds_of[key]
+        names = sorted(set(kinds) - {None, "own"}, key=str)
+        if names and (len(names) > 1 or "own" in kinds):
+            entries = []
+            for kind, item in zip(kinds, own_of[key]):
+                if kind == "own":
+                    entries.append((0, item.piece, group_here(item)))
+                else:
+                    entries.append((1 + names.index(kind) if kind is not None else 1, 0, 0))
+            relays[key] = names, add(entries)
+    for t, (pairs, phases) in returns.items():
+        if len(set(phases) - {None}) > 1:
+            relays["back", t] = None, add([(1 + (p or 0), 0, 0) for p in phases])
+    table = np.concatenate(columns, axis=1) if columns else np.zeros((len(devices), 1), np.int32)
+    table = lax.dynamic_slice(jnp.asarray(table), (device, 0), (1, table.shape[1]))[0]
+
+    def own_chunk(items):
+        piece = lookup([None if i is None else i.piece for i in items], device)
+        group = lookup([None if i is None else group_here(i) for i in items], device)
         return lax.dynamic_slice(x, (piece * piece_rows, group * group_size), (piece_rows, group_size))
 
-    firsts = [key for key in sends if key[2] == 1 and plan.pairs(*key)]
-    starts = dict(zip(firsts, lax.optimization_barrier([first(key) for key in firsts])))
-
-    def send(key):
-        phase, chain, t = key
-        pairs = plan.pairs(*key)
-        if not pairs:
-            return
-        own = own_of[key]
-        held = buffers.get((phase, chain, t - 1))
-        if held is None:
-            held = starts.pop(key) if key in starts else first(key)
-        elif any(own):
-            held = buffers[phase, chain, t - 1] = relay(3 * sends.index(key), table, x, held)
-        buffers[key] = lax.ppermute(held, ("row", "col"), pairs)
+    firsts = {key: own_of[key] for key in sends if key[1] == 1 and any(own_of[key])}
+    for k, crossing in enumerate(crossings):
+        firsts["cross", k] = [crossing[rc][1] if rc in crossing else None for rc in devices]
+    starts = dict(zip(firsts, lax.optimization_barrier([own_chunk(items) for items in firsts.values()])))
 
     factor = weight / jnp.sqrt(2.0 * freq * (1.0 - freq))
     twice = 2.0 * freq
@@ -298,10 +430,13 @@
     window_factor, window_twice = in_window(factor), in_window(twice)
     male_wide = wide(male_rows)
 
-    def own_squares(x):
+    def own_squares():
         here = lambda value: lax.dynamic_slice(value, (col_place * local_vars,), (local_vars,))[None, :]
         zx = ((x.astype(jnp.float32) - here(twice)) * here(factor) * male_rows[:, None]).astype(jnp.bfloat16)
         return jnp.sum(jnp.square(zx.astype(jnp.float32)), axis=1)
+
+    buffers = {}
+    last = [0] * len(PARTS)
 
     def part_product(part, zy, before):
         found = []
@@ -309,10 +444,15 @@
             keys = []
             for q in range(*part):
                 for s in range(STEPS):
-                    arrival = plan.arrival(r, c, q, s)
-                    keys.append(-1 - (r + s) % rows % groups_here if arrival is None else arrival)
+                    key = -1 - (r + s) % rows % groups_here
+                    for d, lane in enumerate(lanes):
+                        arrival = lane.arrival(r, c, (q, s))
+                        if arrival is not None:
+                            t, returned = arrival
+                            key = ("back" if returned else (r + d) % 2, t)
+                    keys.append(key)
             found.append(keys)
-        used = sorted({k for keys in found for k in keys if isinstance(k, tuple)}, key=lambda k: (k[2], k[1], k[0]))
+        used = sorted({k for keys in found for k in keys if isinstance(k, tuple)}, key=lambda k: (k[1], str(k[0])))
         places = [[k if isinstance(k, int) else used.index(k) for k in keys] for keys in found]
         places = np.asarray(places, np.int32)
         candidates = [sorted({max(int(k), -1) for k in places[:, i]}) for i in range(places.shape[1])]
@@ -322,29 +462,80 @@
             part, places, candidates, x, held, window_factor[None, :], window_twice[None, :], male_wide, zy, before
         )
 
+    for number_of_part, part in enumerate(PARTS):
+        for d, lane in enumerate(lanes):
+            for r, c in devices:
+                for q in range(*part):
+                    for s in range(STEPS):
+                        arrival = lane.arrival(r, c, (q, s))
+                        if arrival is not None:
+                            t = arrival[0] + (2 if arrival[1] else 0)
+                            last[number_of_part] = max(last[number_of_part], t)
+
     back = [(i, (i - 1) % rows) for i in range(rows)]
     window = [y]
-    moving = [lax.ppermute(y, "row", back)]
-    squares = own_squares(x)
+    while len(window) < STEPS:
+        window.append(lax.ppermute(window[-1], "row", back))
+    zy = relation = None
+    squares = own_squares()
     bits = [1 << k for k in range(cols.bit_length() - 1)] if cols & (cols - 1) == 0 else []
-    relation = None
-
-    for key in sends:
-        send(key)
-    while len(window) < STEPS:
-        window.append(moving[0])
-        if len(window) < STEPS:
-            moving[0] = lax.ppermute(window[-1], "row", back)
-    zy = standardized_window(window, wide(window_factor), wide(window_twice), male_cols[None, :])
     if cols & (cols - 1):
         squares = lax.psum(squares, "col")
-    for part in PARTS:
+
+    def sum_beside(value, squares):
+        if not bits:
+            return value, squares
+        bit = bits.pop(0)
+        other = lax.ppermute(squares, "col", [(i, i ^ bit) for i in range(cols)])
+        value, other = lax.optimization_barrier((value, other))
+        return value, squares + other
+
+    def window_product():
+        return standardized_window(window, wide(window_factor), wide(window_twice), male_cols[None, :])
+
+    crossed = {}
+    done = 0
+    for key in sends:
+        phase, t = key
+        if not pairs_of[key]:
+            continue
+        if key in relays:
+            names, at = relays[key]
+            sources = [buffers[phase, t - DEPTH] if name == "forward" else crossed[name] for name in names]
+            held = relay(at, table, x, sources)
+        elif key in starts:
+            held = starts[key]
+        elif "forward" in kinds_of[key]:
+            held = buffers[phase, t - DEPTH]
+        elif "own" in kinds_of[key]:
+            held = own_chunk(own_of[key])
+        else:
+            held = crossed[next(k for k in kinds_of[key] if k is not None)]
+        if phase == 1 and t == last[0]:
+            zy, squares = sum_beside(window_product(), squares)
+            held, zy = lax.optimization_barrier((held, zy))
+        if phase == 1 and t == last[0] + 2 and zy is not None:
+            relation, squares = sum_beside(part_product(PARTS[0], zy, relation), squares)
+            held, relation = lax.optimization_barrier((held, relation))
+            done = 1
+        if phase == 1 and ("back", t - 2) in buffers:
+            held, buffers["back", t - 2] = lax.optimization_barrier((held, buffers["back", t - 2]))
+        buffers[key] = lax.ppermute(held, both, pairs_of[key])
+        if key == (1, 1):
+            for k, crossing in enumerate(crossings):
+                pairs = [(number(*rc), number(*to)) for rc, (to, _) in crossing.items()]
+                crossed[k] = lax.ppermute(starts["cross", k], both, pairs)
+        if phase == 1 and t in returns:
+            pairs, phases = returns[t]
+            if ("back", t) in relays:
+                held = relay(relays["back", t][1], table, x, [buffers[0, t], buffers[1, t]])
+            else:
+                held = buffers[next(p for p in phases if p is not None), t]
+            buffers["back", t] = lax.ppermute(held, both, pairs)
+    if zy is None:
+        zy = window_product()
+    for part in PARTS[done:]:
         relation = part_product(part, zy, relation)
-        if bits:
-            bit = bits.pop(0)
-            other = lax.ppermute(squares, "col", [(i, i ^ bit) for i in range(cols)])
-            relation, other = lax.optimization_barrier((relation, other))
-            squares = squares + other
     for bit in bits:
         squares = squares + lax.ppermute(squares, "col", [(i, i ^ bit) for i in range(cols)])
     inbreeding = squares / jnp.float32(freq.shape[0]) - 1.0

time: 148 us -> 145 us (0.980)
  the two profiles are of different devices: /device:TPU:0 before, /device:TPU:16 now
where the time goes in v8:
time: 145 us; the launch traced here: 144 us
  starting transfers between devices  57.3 us (40%)
  waiting for transfers between devices  39.6 us (27%)
  Pallas kernels  38 us (26%)
  local copies, waits for them, and re-layouts  5.58 us (4%)
  other arithmetic  1.74 us (1%)
    ppermute x16, starting transfers between devices, local(): buffers[key] = lax.ppermute(held, both, pairs_of[key])  46.3 us
    ppermute x16, waiting for transfers between devices, local(): buffers[key] = lax.ppermute(held, both, pairs_of[key])  34.8 us
    pallas_call x2, Pallas kernels, product(): pl.pallas_call(kernel, out_shape=jax.ShapeDtypeStruct((rows, n), jnp.bflo...  17.6 us
    pallas_call x15, Pallas kernels, relay(): pl.pallas_call(functools.partial(relay_kernel, at), out_shape=pltpu.VMEM(...  17 us
    ppermute x3, starting transfers between devices, local(): window.append(lax.ppermute(window[-1], 'row', back))  6.75 us
    ppermute x3, waiting for transfers between devices, local(): window.append(lax.ppermute(window[-1], 'row', back))  4.82 us
    pallas_call x1, Pallas kernels, standardized_window(): pl.pallas_call(window_kernel, out_shape=pltpu.VMEM((depth, n), jnp.bfloat...  3.37 us
  transfers between devices with their start and end apart: 25, of which 8 were waited for; matrix products, arithmetic and copies ran while one was open for 5% of the time, Pallas kernels for 20%

profile of v8, /device:TPU:16, one launch (start us, length us, event | category | flops | bytes accessed | tf_op | source)
XLA Modules:
  0.0 143.6 jit_solution(17736641827455748932)
XLA Ops:
  0.6 1.9 %collective-permute-start.8 = (bf16[256,2048]{1,0:T(8,128)(2,1)}, bf16[256,2048]{1,0:T(8,128)(2,1)}, u32[]{:S(2)}, u32[]{:S(2)}) collective-permute-start(bf16[256,2048]{1,0:T(8,128)(2,1)} %refs_0_.1), channel_id=1, source_target_pairs={{0,28},{4,0},{8,4},{12,8},{16,12},{20,16},{24,20},{28,24},{1,29},{... | collective-permute-start | bytes 3145736 | tf_op jit(solution)/shard_map/ppermute | solution.py:478
  2.6 2.6 %constant_dynamic-slice_fusion.5 = (bf16[1024,256]{1,0:T(8,128)(2,1)}, bf16[1024,256]{1,0:T(8,128)(2,1)}, bf16[1024,256]{1,0:T(8,128)(2,1)}) fusion(bf16[2048,512]{1,0:T(8,128)(2,1)} %x.33, s32[]{:T(128)S(6)} %select_n.44, s32[]{:T(128)S(6)} %select_n.43, s32[]{:T(128)S(6)} %select_n.42), kind=kLoop, calls=%fused_computation.21 | loop fusion | bytes 3145740 | tf_op jit(solution)/shard_map/dynamic_slice | solution.py:412
  5.1 0.7 collective-permute-start
  5.8 1.3 collective-permute-start.2
  7.1 1.3 collective-permute-start.4
  8.4 0.7 fusion.3.table
  9.1 0.6 relay.15
  9.7 0.7 collective-permute-start.1
  10.4 4.8 %collective-permute-done.8.refs_1_ = bf16[256,2048]{1,0:T(8,128)(2,1)} collective-permute-done((bf16[256,2048]{1,0:T(8,128)(2,1)}, bf16[256,2048]{1,0:T(8,128)(2,1)}, u32[]{:S(2)}, u32[]{:S(2)}) %collective-permute-start.8) | collective-permute-done | bytes 1048608 | tf_op jit(solution)/shard_map/ppermute | solution.py:478
  15.3 3.7 %collective-permute-start.9 = (bf16[256,2048]{1,0:T(8,128)(2,1)}, bf16[256,2048]{1,0:T(8,128)(2,1)}, u32[]{:S(2)}, u32[]{:S(2)}) collective-permute-start(bf16[256,2048]{1,0:T(8,128)(2,1)} %collective-permute-done.8.refs_1_), channel_id=1, source_target_pairs={{0,28},{4,0},{8,4},{12,8},{16,12},{20,16},{24,20},{28,24},{1,29},{... | collective-permute-start | bytes 3145736 | tf_op jit(solution)/shard_map/ppermute | solution.py:478
  18.9 0.7 collective-permute-done.2.refs_0_.refs_1_
  19.7 0.6 relay.16
  20.3 1.9 %collective-permute-start.3 = (bf16[1024,256]{1,0:T(8,128)(2,1)S(1)}, bf16[1024,256]{1,0:T(8,128)(2,1)S(1)}, u32[]{:S(2)}, u32[]{:S(2)}) collective-permute-start(bf16[1024,256]{1,0:T(8,128)(2,1)S(1)} %relay.16), channel_id=1, source_target_pairs={{0,1},{1,2},{2,3},{5,4},{6,5},{9,10},{10,11},{13,12},{14,13},{15,1... | collective-permute-start | bytes 1572872 | tf_op jit(solution)/shard_map/ppermute | solution.py:523
  22.2 0.0 copy-start.1
  22.2 1.3 relay.17
  23.6 15.0 %collective-permute-start.5 = (bf16[1024,256]{1,0:T(8,128)(2,1)S(1)}, bf16[1024,256]{1,0:T(8,128)(2,1)S(1)}, u32[]{:S(2)}, u32[]{:S(2)}) collective-permute-start(bf16[1024,256]{1,0:T(8,128)(2,1)S(1)} %relay.17), channel_id=1, source_target_pairs={{1,0},{2,1},{3,2},{5,6},{6,7},{9,8},{10,9},{14,15},{17,16},{18,17}... | collective-permute-start | bytes 1572872 | tf_op jit(solution)/shard_map/ppermute | solution.py:523
  38.6 2.1 %relay.18 = bf16[1024,256]{1,0:T(8,128)(2,1)} custom-call(s32[45]{0:T(128)S(1)} %fusion.3.table, bf16[2048,512]{1,0:T(8,128)(2,1)S(1)} %copy-done, bf16[1024,256]{1,0:T(8,128)(2,1)} %collective-permute-done.4.refs_0_, bf16[1024,256]{1,0:T(8,128)(2,1)S(1)} %collective-permute-done.3.refs_1_.refs_3_), custom_call_target="tpu_custom_call" | custom-call | tf_op jit(solution)/shard_map/relay/pallas_call | solution.py:183
  40.6 1.9 %collective-permute-start.6 = (bf16[1024,256]{1,0:T(8,128)(2,1)}, bf16[1024,256]{1,0:T(8,128)(2,1)S(1)}, u32[]{:S(2)}, u32[]{:S(2)}) collective-permute-start(bf16[1024,256]{1,0:T(8,128)(2,1)} %relay.18), channel_id=1, source_target_pairs={{0,1},{1,2},{2,3},{5,4},{9,10},{10,11},{13,12},{14,13},{16,17},{17... | collective-permute-start | bytes 1572872 | tf_op jit(solution)/shard_map/ppermute | solution.py:523
  42.6 2.6 %collective-permute-done.5.refs_0_.refs_4_.refs_2_ = bf16[1024,256]{1,0:T(8,128)(2,1)S(1)} collective-permute-done((bf16[1024,256]{1,0:T(8,128)(2,1)S(1)}, bf16[1024,256]{1,0:T(8,128)(2,1)S(1)}, u32[]{:S(2)}, u32[]{:S(2)}) %collective-permute-start.5) | collective-permute-done | bytes 524320 | tf_op jit(solution)/shard_map/ppermute | solution.py:523
  45.2 1.4 relay.22
  46.6 8.6 %collective-permute-start.13 = (bf16[1024,256]{1,0:T(8,128)(2,1)}, bf16[1024,256]{1,0:T(8,128)(2,1)}, u32[]{:S(2)}, u32[]{:S(2)}) collective-permute-start(bf16[1024,256]{1,0:T(8,128)(2,1)} %relay.22), channel_id=1, source_target_pairs={{1,0},{2,1},{4,5},{5,6},{6,7},{9,8},{14,15},{17,16},{18,17},{20,21... | collective-permute-start | bytes 1572872 | tf_op jit(solution)/shard_map/ppermute | solution.py:523
  55.2 1.1 collective-permute-start.10
  56.3 0.1 dynamic_slice.37
  56.4 0.1 dynamic_slice.38
  56.5 0.2 collective-permute-done.6.refs_0_.refs_1_.refs_5_.refs_3_
  56.7 1.4 relay.19
  58.1 2.0 %collective-permute-start.7 = (bf16[1024,256]{1,0:T(8,128)(2,1)}, bf16[1024,256]{1,0:T(8,128)(2,1)}, u32[]{:S(2)}, u32[]{:S(2)}) collective-permute-start(bf16[1024,256]{1,0:T(8,128)(2,1)} %relay.19), channel_id=1, source_target_pairs={{1,2},{2,3},{5,4},{10,11},{13,12},{14,13},{15,14},{17,18},{18,19},... | collective-permute-start | bytes 1572872 | tf_op jit(solution)/shard_map/ppermute | solution.py:523
  60.1 1.4 relay.21
  61.5 1.5 %collective-permute-start.12 = (bf16[1024,256]{1,0:T(8,128)(2,1)}, bf16[1024,256]{1,0:T(8,128)(2,1)}, u32[]{:S(2)}, u32[]{:S(2)}) collective-permute-start(bf16[1024,256]{1,0:T(8,128)(2,1)} %relay.21), channel_id=1, source_target_pairs={{24,8},{28,12},{23,7},{27,11}} | collective-permute-start | bytes 1572872 | tf_op jit(solution)/shard_map/ppermute | solution.py:534
  63.0 1.9 %relay.25 = bf16[1024,256]{1,0:T(8,128)(2,1)} custom-call(s32[45]{0:T(128)S(1)} %fusion.3.table, bf16[2048,512]{1,0:T(8,128)(2,1)S(1)} %copy-done, bf16[1024,256]{1,0:T(8,128)(2,1)} %collective-permute-done.13.refs_0_.refs_6_.refs_5_), custom_call_target="tpu_custom_call" | custom-call | tf_op jit(solution)/shard_map/relay/pallas_call | solution.py:183
  64.9 1.5 %collective-permute-start.16 = (bf16[1024,256]{1,0:T(8,128)(2,1)}, bf16[1024,256]{1,0:T(8,128)(2,1)}, u32[]{:S(2)}, u32[]{:S(2)}) collective-permute-start(bf16[1024,256]{1,0:T(8,128)(2,1)} %relay.25), channel_id=1, source_target_pairs={{1,0},{5,6},{6,7},{9,8},{10,9},{13,14},{14,15},{17,16},{18,17},{19... | collective-permute-start | bytes 1572872 | tf_op jit(solution)/shard_map/ppermute | solution.py:523
  66.4 1.0 multiply_reduce_fusion
  67.4 0.1 collective-permute-start.11
  67.5 0.1 fusion
  67.6 3.1 %collective-permute-done.7.refs_0_.refs_1_.refs_7_.refs_6_ = bf16[1024,256]{1,0:T(8,128)(2,1)} collective-permute-done((bf16[1024,256]{1,0:T(8,128)(2,1)}, bf16[1024,256]{1,0:T(8,128)(2,1)}, u32[]{:S(2)}, u32[]{:S(2)}) %collective-permute-start.7) | collective-permute-done | bytes 524320 | tf_op jit(solution)/shard_map/ppermute | solution.py:523
  70.7 1.1 relay.20
  71.8 0.2 broadcast_in_dim.21.refs_5_
  72.0 0.2 broadcast_in_dim.20.refs_4_
  72.2 3.4 %window.1.refs_13_.refs_20_ = bf16[1024,2048]{1,0:T(8,128)(2,1)S(1)} custom-call(bf16[256,2048]{1,0:T(8,128)(2,1)S(1)} %copy-done.9, bf16[256,2048]{1,0:T(8,128)(2,1)} %collective-permute-done.8.refs_1_, bf16[256,2048]{1,0:T(8,128)(2,1)} %collective-permute-done.9.refs_2_, bf16[256,2048]{1,0:T(8,128)(2,1)} %collective-permute-done.10.refs_3_, ...), custom_call_target="tpu_custom_call" | custom-call | flops 8388608 | bytes 8388608 | tf_op jit(solution)/shard_map/window/pallas_call | solution.py:219
  75.6 1.9 %collective-permute-start.14 = (bf16[1024,256]{1,0:T(8,128)(2,1)S(1)}, bf16[1024,256]{1,0:T(8,128)(2,1)S(1)}, u32[]{:S(2)}, u32[]{:S(2)}) collective-permute-start(bf16[1024,256]{1,0:T(8,128)(2,1)S(1)} %relay.20), channel_id=1, source_target_pairs={{0,1},{1,2},{2,3},{5,4},{6,5},{9,10},{10,11},{13,12},{14,13},{18,1... | collective-permute-start | bytes 1572872 | tf_op jit(solution)/shard_map/ppermute | solution.py:523
  77.5 1.3 relay.24
  78.8 0.7 collective-permute-start.15
  79.5 1.1 relay.28
  80.6 0.7 collective-permute-start.20
  81.3 13.7 %collective-permute-done.14.refs_0_.refs_9_.refs_1_ = bf16[1024,256]{1,0:T(8,128)(2,1)S(1)} collective-permute-done((bf16[1024,256]{1,0:T(8,128)(2,1)S(1)}, bf16[1024,256]{1,0:T(8,128)(2,1)S(1)}, u32[]{:S(2)}, u32[]{:S(2)}) %collective-permute-start.14) | collective-permute-done | bytes 524320 | tf_op jit(solution)/shard_map/ppermute | solution.py:523
  95.1 0.6 relay.23
  95.7 2.1 %collective-permute-start.17 = (bf16[1024,256]{1,0:T(8,128)(2,1)S(1)}, bf16[1024,256]{1,0:T(8,128)(2,1)S(1)}, u32[]{:S(2)}, u32[]{:S(2)}) collective-permute-start(bf16[1024,256]{1,0:T(8,128)(2,1)S(1)} %relay.23), channel_id=1, source_target_pairs={{1,2},{2,3},{5,4},{9,10},{10,11},{13,12},{14,13},{18,19},{21,20},{... | collective-permute-start | bytes 1572872 | tf_op jit(solution)/shard_map/ppermute | solution.py:523
  97.8 1.1 relay.27
  98.9 0.7 collective-permute-start.19
  99.6 0.7 fusion.4.places
  100.3 0.1 collective-permute-start.18
  100.3 0.6 relay.29
  100.9 0.7 collective-permute-start.21
  101.6 0.3 broadcast_in_dim.46.refs_12_.refs_19_
  102.0 8.6 %product.2.refs_21_ = bf16[2048,2048]{1,0:T(8,128)(2,1)} custom-call(s32[4]{0:T(128)S(1)} %fusion.4.places, bf16[2048,512]{1,0:T(8,128)(2,1)S(1)} %copy-done, bf16[1024,256]{1,0:T(8,128)(2,1)S(1)} %copy-done.6, bf16[1024,256]{1,0:T(8,128)(2,1)S(1)} %copy-done.8, bf16[1024,256]{1,0:T(8,128)(2,1)S(1)} %copy-done.2, bf16[1024,256]{1,0:T(8,128)(2,1)S(1)} %copy-done.4, ...), custom_call_target="tpu_custom_call" | custom-call | flops 4294967296 | bytes 4194304 | tf_op jit(solution)/shard_map/product/pallas_call | solution.py:292
  110.6 0.6 relay.26
  111.2 5.5 %collective-permute-start.22 = (bf16[1024,256]{1,0:T(8,128)(2,1)S(1)}, bf16[1024,256]{1,0:T(8,128)(2,1)S(1)}, u32[]{:S(2)}, u32[]{:S(2)}) collective-permute-start(bf16[1024,256]{1,0:T(8,128)(2,1)S(1)} %relay.26), channel_id=1, source_target_pairs={{0,1},{1,2},{2,3},{10,11},{21,20},{26,27}} | collective-permute-start | bytes 1572872 | tf_op jit(solution)/shard_map/ppermute | solution.py:523
  116.7 0.7 collective-permute-start.23
  117.4 6.0 %collective-permute-done.22.refs_14_ = bf16[1024,256]{1,0:T(8,128)(2,1)S(1)} collective-permute-done((bf16[1024,256]{1,0:T(8,128)(2,1)S(1)}, bf16[1024,256]{1,0:T(8,128)(2,1)S(1)}, u32[]{:S(2)}, u32[]{:S(2)}) %collective-permute-start.22) | collective-permute-done | bytes 524320 | tf_op jit(solution)/shard_map/ppermute | solution.py:523
  123.4 1.3 collective-permute-start.24
  124.7 0.7 fusion.2.places
  125.4 0.6 multiply_add_fusion
  126.0 8.5 %collective-permute-done.24.refs_16_ = bf16[1024,256]{1,0:T(8,128)(2,1)S(1)} collective-permute-done((bf16[1024,256]{1,0:T(8,128)(2,1)S(1)}, bf16[1024,256]{1,0:T(8,128)(2,1)S(1)}, u32[]{:S(2)}, u32[]{:S(2)}) %collective-permute-start.24) | collective-permute-done | bytes 524320 | tf_op jit(solution)/shard_map/ppermute | solution.py:523
  134.4 9.0 %product.3 = bf16[2048,2048]{1,0:T(8,128)(2,1)} custom-call(s32[4]{0:T(128)S(1)} %fusion.2.places, bf16[2048,512]{1,0:T(8,128)(2,1)S(1)} %copy-done, bf16[1024,256]{1,0:T(8,128)(2,1)S(1)} %copy-done.2, bf16[1024,256]{1,0:T(8,128)(2,1)S(1)} %copy-done.4, ...), custom_call_target="tpu_custom_call", output_to_operand_aliasing={{}: (23, {})} | custom-call | flops 4294967296 | bytes 4194304 | tf_op jit(solution)/shard_map/product/pallas_call | solution.py:292
  (48 shorter events, 0.1 us)
Async XLA Ops:
  0.6 8.5 %copy-start = (bf16[2048,512]{1,0:T(8,128)(2,1)S(1)}, bf16[2048,512]{1,0:T(8,128)(2,1)}, u32[]{:S(2)}) copy-start(bf16[2048,512]{1,0:T(8,128)(2,1)} %x.33) | copy-start | bytes 6291460
  0.6 14.6 %collective-permute-start.8 = (bf16[256,2048]{1,0:T(8,128)(2,1)}, bf16[256,2048]{1,0:T(8,128)(2,1)}, u32[]{:S(2)}, u32[]{:S(2)}) collective-permute-start(bf16[256,2048]{1,0:T(8,128)(2,1)} %refs_0_.1), channel_id=1, source_target_pairs={{0,28},{4,0},{8,4},{12,8},{16,12},{20,16},{24,20},{28,24},{1,29},{... | collective-permute-start | bytes 3145736 | tf_op jit(solution)/shard_map/ppermute | solution.py:478
  5.1 4.0 %collective-permute-start = (bf16[1024,256]{1,0:T(8,128)(2,1)}, bf16[1024,256]{1,0:T(8,128)(2,1)S(1)}, u32[]{:S(2)}, u32[]{:S(2)}) collective-permute-start(bf16[1024,256]{1,0:T(8,128)(2,1)} %get-tuple-element.19), channel_id=1, source_target_pairs={{1,0},{5,6},{6,7},{9,8},{14,15},{18,17},{22,23},{28,29},{29,30}} | collective-permute-start | bytes 1572872 | tf_op jit(solution)/shard_map/ppermute | solution.py:523
  5.8 13.8 %collective-permute-start.2 = (bf16[1024,256]{1,0:T(8,128)(2,1)}, bf16[1024,256]{1,0:T(8,128)(2,1)S(1)}, u32[]{:S(2)}, u32[]{:S(2)}) collective-permute-start(bf16[1024,256]{1,0:T(8,128)(2,1)} %get-tuple-element.20), channel_id=1, source_target_pairs={{1,2},{5,4},{10,11},{13,12},{14,13},{18,19},{22,21},{23,22},{29,28}} | collective-permute-start | bytes 1572872 | tf_op jit(solution)/shard_map/ppermute | solution.py:523
  7.1 15.1 %collective-permute-start.4 = (bf16[1024,256]{1,0:T(8,128)(2,1)}, bf16[1024,256]{1,0:T(8,128)(2,1)}, u32[]{:S(2)}, u32[]{:S(2)}) collective-permute-start(bf16[1024,256]{1,0:T(8,128)(2,1)} %get-tuple-element.21), channel_id=1, source_target_pairs={{18,2},{19,3},{9,25},{13,29},{14,30},{1,17},{0,16},{6,22},{5,21},{... | collective-permute-start | bytes 1572872 | tf_op jit(solution)/shard_map/ppermute | solution.py:527
  9.1 13.1 %copy-start.5 = (bf16[1024,256]{1,0:T(8,128)(2,1)}, bf16[1024,256]{1,0:T(8,128)(2,1)S(1)}, u32[]{:S(2)}) copy-start(bf16[1024,256]{1,0:T(8,128)(2,1)S(1)} %collective-permute-done.refs_0_) | copy-start | bytes 1572868
  9.7 12.5 %collective-permute-start.1 = (bf16[1024,256]{1,0:T(8,128)(2,1)S(1)}, bf16[1024,256]{1,0:T(8,128)(2,1)S(1)}, u32[]{:S(2)}, u32[]{:S(2)}) collective-permute-start(bf16[1024,256]{1,0:T(8,128)(2,1)S(1)} %relay.15), channel_id=1, source_target_pairs={{1,0},{4,5},{5,6},{6,7},{9,8},{10,9},{13,14},{14,15},{17,16},{18,1... | collective-permute-start | bytes 1572872 | tf_op jit(solution)/shard_map/ppermute | solution.py:523
  15.3 39.9 %collective-permute-start.9 = (bf16[256,2048]{1,0:T(8,128)(2,1)}, bf16[256,2048]{1,0:T(8,128)(2,1)}, u32[]{:S(2)}, u32[]{:S(2)}) collective-permute-start(bf16[256,2048]{1,0:T(8,128)(2,1)} %collective-permute-done.8.refs_1_), channel_id=1, source_target_pairs={{0,28},{4,0},{8,4},{12,8},{16,12},{20,16},{24,20},{28,24},{1,29},{... | collective-permute-start | bytes 3145736 | tf_op jit(solution)/shard_map/ppermute | solution.py:478
  19.7 18.9 %copy-start.7 = (bf16[1024,256]{1,0:T(8,128)(2,1)}, bf16[1024,256]{1,0:T(8,128)(2,1)S(1)}, u32[]{:S(2)}) copy-start(bf16[1024,256]{1,0:T(8,128)(2,1)S(1)} %collective-permute-done.2.refs_0_.refs_1_) | copy-start | bytes 1572868
  20.3 18.3 %collective-permute-start.3 = (bf16[1024,256]{1,0:T(8,128)(2,1)S(1)}, bf16[1024,256]{1,0:T(8,128)(2,1)S(1)}, u32[]{:S(2)}, u32[]{:S(2)}) collective-permute-start(bf16[1024,256]{1,0:T(8,128)(2,1)S(1)} %relay.16), channel_id=1, source_target_pairs={{0,1},{1,2},{2,3},{5,4},{6,5},{9,10},{10,11},{13,12},{14,13},{15,1... | collective-permute-start | bytes 1572872 | tf_op jit(solution)/shard_map/ppermute | solution.py:523
  22.2 24.4 %copy-start.1 = (bf16[1024,256]{1,0:T(8,128)(2,1)}, bf16[1024,256]{1,0:T(8,128)(2,1)S(1)}, u32[]{:S(2)}) copy-start(bf16[1024,256]{1,0:T(8,128)(2,1)S(1)} %collective-permute-done.1.refs_1_.refs_2_.refs_0_) | copy-start | bytes 1572868
  23.5 32.8 %copy-start.12 = (f32[2048]{0:T(1024)S(1)}, f32[2048]{0:T(1024)}, u32[]{:S(2)}) copy-start(f32[2048]{0:T(1024)} %param.11) | copy-start | bytes 24580
  23.5 32.8 %copy-start.13 = (f32[2048]{0:T(1024)S(1)}, f32[2048]{0:T(1024)}, u32[]{:S(2)}) copy-start(f32[2048]{0:T(1024)} %param.12) | copy-start | bytes 24580
  23.6 32.9 %copy-start.10 = (s32[2048]{0:T(1024)S(1)}, s32[2048]{0:T(1024)}, u32[]{:S(2)}) copy-start(s32[2048]{0:T(1024)} %param.13) | copy-start | bytes 24580
  23.6 21.6 %collective-permute-start.5 = (bf16[1024,256]{1,0:T(8,128)(2,1)S(1)}, bf16[1024,256]{1,0:T(8,128)(2,1)S(1)}, u32[]{:S(2)}, u32[]{:S(2)}) collective-permute-start(bf16[1024,256]{1,0:T(8,128)(2,1)S(1)} %relay.17), channel_id=1, source_target_pairs={{1,0},{2,1},{3,2},{5,6},{6,7},{9,8},{10,9},{14,15},{17,16},{18,17}... | collective-permute-start | bytes 1572872 | tf_op jit(solution)/shard_map/ppermute | solution.py:523
  38.5 6.7 %copy-start.3 = (bf16[1024,256]{1,0:T(8,128)(2,1)}, bf16[1024,256]{1,0:T(8,128)(2,1)S(1)}, u32[]{:S(2)}) copy-start(bf16[1024,256]{1,0:T(8,128)(2,1)S(1)} %collective-permute-done.3.refs_1_.refs_3_) | copy-start | bytes 1572868
  40.6 16.0 %collective-permute-start.6 = (bf16[1024,256]{1,0:T(8,128)(2,1)}, bf16[1024,256]{1,0:T(8,128)(2,1)S(1)}, u32[]{:S(2)}, u32[]{:S(2)}) collective-permute-start(bf16[1024,256]{1,0:T(8,128)(2,1)} %relay.18), channel_id=1, source_target_pairs={{0,1},{1,2},{2,3},{5,4},{9,10},{10,11},{13,12},{14,13},{16,17},{17... | collective-permute-start | bytes 1572872 | tf_op jit(solution)/shard_map/ppermute | solution.py:523
  46.6 16.4 %collective-permute-start.13 = (bf16[1024,256]{1,0:T(8,128)(2,1)}, bf16[1024,256]{1,0:T(8,128)(2,1)}, u32[]{:S(2)}, u32[]{:S(2)}) collective-permute-start(bf16[1024,256]{1,0:T(8,128)(2,1)} %relay.22), channel_id=1, source_target_pairs={{1,0},{2,1},{4,5},{5,6},{6,7},{9,8},{14,15},{17,16},{18,17},{20,21... | collective-permute-start | bytes 1572872 | tf_op jit(solution)/shard_map/ppermute | solution.py:523
  55.2 16.6 %collective-permute-start.10 = (bf16[256,2048]{1,0:T(8,128)(2,1)}, bf16[256,2048]{1,0:T(8,128)(2,1)}, u32[]{:S(2)}, u32[]{:S(2)}) collective-permute-start(bf16[256,2048]{1,0:T(8,128)(2,1)} %collective-permute-done.9.refs_2_), channel_id=1, source_target_pairs={{0,28},{4,0},{8,4},{12,8},{16,12},{20,16},{24,20},{28,24},{1,29},{... | collective-permute-start | bytes 3145736 | tf_op jit(solution)/shard_map/ppermute | solution.py:478
  58.1 9.4 %copy-start.11 = (s32[2048]{0:T(1024)S(1)}, s32[2048]{0:T(1024)}, u32[]{:S(2)}) copy-start(s32[2048]{0:T(1024)} %param.14) | copy-start | bytes 24580
  58.1 12.6 %collective-permute-start.7 = (bf16[1024,256]{1,0:T(8,128)(2,1)}, bf16[1024,256]{1,0:T(8,128)(2,1)}, u32[]{:S(2)}, u32[]{:S(2)}) collective-permute-start(bf16[1024,256]{1,0:T(8,128)(2,1)} %relay.19), channel_id=1, source_target_pairs={{1,2},{2,3},{5,4},{10,11},{13,12},{14,13},{15,14},{17,18},{18,19},... | collective-permute-start | bytes 1572872 | tf_op jit(solution)/shard_map/ppermute | solution.py:523
  61.5 14.1 %collective-permute-start.12 = (bf16[1024,256]{1,0:T(8,128)(2,1)}, bf16[1024,256]{1,0:T(8,128)(2,1)}, u32[]{:S(2)}, u32[]{:S(2)}) collective-permute-start(bf16[1024,256]{1,0:T(8,128)(2,1)} %relay.21), channel_id=1, source_target_pairs={{24,8},{28,12},{23,7},{27,11}} | collective-permute-start | bytes 1572872 | tf_op jit(solution)/shard_map/ppermute | solution.py:534
  64.9 14.6 %collective-permute-start.16 = (bf16[1024,256]{1,0:T(8,128)(2,1)}, bf16[1024,256]{1,0:T(8,128)(2,1)}, u32[]{:S(2)}, u32[]{:S(2)}) collective-permute-start(bf16[1024,256]{1,0:T(8,128)(2,1)} %relay.25), channel_id=1, source_target_pairs={{1,0},{5,6},{6,7},{9,8},{10,9},{13,14},{14,15},{17,16},{18,17},{19... | collective-permute-start | bytes 1572872 | tf_op jit(solution)/shard_map/ppermute | solution.py:523
  67.4 8.2 %collective-permute-start.11 = (f32[2048]{0:T(1024)S(1)}, f32[2048]{0:T(1024)S(1)}, u32[]{:S(2)}, u32[]{:S(2)}) collective-permute-start(f32[2048]{0:T(1024)S(1)} %multiply_reduce_fusion), channel_id=1, source_target_pairs={{0,1},{1,0},{2,3},{3,2},{4,5},{5,4},{6,7},{7,6},{8,9},{9,8},{10,11... | collective-permute-start | bytes 24584 | tf_op jit(solution)/shard_map/ppermute | solution.py:489
  67.5 4.7 %copy-start.9 = (bf16[256,2048]{1,0:T(8,128)(2,1)S(1)}, bf16[256,2048]{1,0:T(8,128)(2,1)}, u32[]{:S(2)}) copy-start(bf16[256,2048]{1,0:T(8,128)(2,1)} %refs_0_.1) | copy-start | bytes 3145732
  75.6 19.4 %collective-permute-start.14 = (bf16[1024,256]{1,0:T(8,128)(2,1)S(1)}, bf16[1024,256]{1,0:T(8,128)(2,1)S(1)}, u32[]{:S(2)}, u32[]{:S(2)}) collective-permute-start(bf16[1024,256]{1,0:T(8,128)(2,1)S(1)} %relay.20), channel_id=1, source_target_pairs={{0,1},{1,2},{2,3},{5,4},{6,5},{9,10},{10,11},{13,12},{14,13},{18,1... | collective-permute-start | bytes 1572872 | tf_op jit(solution)/shard_map/ppermute | solution.py:523
  78.8 16.9 %collective-permute-start.15 = (bf16[1024,256]{1,0:T(8,128)(2,1)S(1)}, bf16[1024,256]{1,0:T(8,128)(2,1)S(1)}, u32[]{:S(2)}, u32[]{:S(2)}) collective-permute-start(bf16[1024,256]{1,0:T(8,128)(2,1)S(1)} %relay.24), channel_id=1, source_target_pairs={{0,16},{28,12},{19,3},{23,7}} | collective-permute-start | bytes 1572872 | tf_op jit(solution)/shard_map/ppermute | solution.py:534
  80.6 19.7 %collective-permute-start.20 = (bf16[1024,256]{1,0:T(8,128)(2,1)S(1)}, bf16[1024,256]{1,0:T(8,128)(2,1)S(1)}, u32[]{:S(2)}, u32[]{:S(2)}) collective-permute-start(bf16[1024,256]{1,0:T(8,128)(2,1)S(1)} %relay.28), channel_id=1, source_target_pairs={{1,0},{5,6},{6,7},{9,8},{10,9},{14,15},{17,16},{18,17},{22,23},{25... | collective-permute-start | bytes 1572872 | tf_op jit(solution)/shard_map/ppermute | solution.py:523
  95.7 6.3 %copy-start.2 = (bf16[1024,256]{1,0:T(8,128)(2,1)S(1)}, bf16[1024,256]{1,0:T(8,128)(2,1)}, u32[]{:S(2)}) copy-start(bf16[1024,256]{1,0:T(8,128)(2,1)} %copy-done.1) | copy-start | bytes 1572868
  95.7 6.3 %copy-start.4 = (bf16[1024,256]{1,0:T(8,128)(2,1)S(1)}, bf16[1024,256]{1,0:T(8,128)(2,1)}, u32[]{:S(2)}) copy-start(bf16[1024,256]{1,0:T(8,128)(2,1)} %copy-done.3) | copy-start | bytes 1572868
  95.7 6.3 %copy-start.6 = (bf16[1024,256]{1,0:T(8,128)(2,1)S(1)}, bf16[1024,256]{1,0:T(8,128)(2,1)}, u32[]{:S(2)}) copy-start(bf16[1024,256]{1,0:T(8,128)(2,1)} %copy-done.5) | copy-start | bytes 1572868
  95.7 6.3 %copy-start.8 = (bf16[1024,256]{1,0:T(8,128)(2,1)S(1)}, bf16[1024,256]{1,0:T(8,128)(2,1)}, u32[]{:S(2)}) copy-start(bf16[1024,256]{1,0:T(8,128)(2,1)} %copy-done.7) | copy-start | bytes 1572868
  95.7 14.9 %collective-permute-start.17 = (bf16[1024,256]{1,0:T(8,128)(2,1)S(1)}, bf16[1024,256]{1,0:T(8,128)(2,1)S(1)}, u32[]{:S(2)}, u32[]{:S(2)}) collective-permute-start(bf16[1024,256]{1,0:T(8,128)(2,1)S(1)} %relay.23), channel_id=1, source_target_pairs={{1,2},{2,3},{5,4},{9,10},{10,11},{13,12},{14,13},{18,19},{21,20},{... | collective-permute-start | bytes 1572872 | tf_op jit(solution)/shard_map/ppermute | solution.py:523
  98.9 12.3 %collective-permute-start.19 = (bf16[1024,256]{1,0:T(8,128)(2,1)S(1)}, bf16[1024,256]{1,0:T(8,128)(2,1)S(1)}, u32[]{:S(2)}, u32[]{:S(2)}) collective-permute-start(bf16[1024,256]{1,0:T(8,128)(2,1)S(1)} %relay.27), channel_id=1, source_target_pairs={{0,16},{19,3}} | collective-permute-start | bytes 1572872 | tf_op jit(solution)/shard_map/ppermute | solution.py:534
  100.3 10.3 %collective-permute-start.18 = (f32[2048]{0:T(1024)S(1)}, f32[2048]{0:T(1024)S(1)}, u32[]{:S(2)}, u32[]{:S(2)}) collective-permute-start(f32[2048]{0:T(1024)S(1)} %add.46), channel_id=1, source_target_pairs={{0,2},{1,3},{2,0},{3,1},{4,6},{5,7},{6,4},{7,5},{8,10},{9,11},{10,... | collective-permute-start | bytes 24584 | tf_op jit(solution)/shard_map/ppermute | solution.py:489
  100.9 15.8 %collective-permute-start.21 = (bf16[1024,256]{1,0:T(8,128)(2,1)S(1)}, bf16[1024,256]{1,0:T(8,128)(2,1)S(1)}, u32[]{:S(2)}, u32[]{:S(2)}) collective-permute-start(bf16[1024,256]{1,0:T(8,128)(2,1)S(1)} %relay.29), channel_id=1, source_target_pairs={{9,8},{17,16},{18,17},{19,18},{25,24},{30,31}} | collective-permute-start | bytes 1572872 | tf_op jit(solution)/shard_map/ppermute | solution.py:523
  111.2 12.1 %collective-permute-start.22 = (bf16[1024,256]{1,0:T(8,128)(2,1)S(1)}, bf16[1024,256]{1,0:T(8,128)(2,1)S(1)}, u32[]{:S(2)}, u32[]{:S(2)}) collective-permute-start(bf16[1024,256]{1,0:T(8,128)(2,1)S(1)} %relay.26), channel_id=1, source_target_pairs={{0,1},{1,2},{2,3},{10,11},{21,20},{26,27}} | collective-permute-start | bytes 1572872 | tf_op jit(solution)/shard_map/ppermute | solution.py:523
  116.7 9.3 %collective-permute-start.23 = (bf16[1024,256]{1,0:T(8,128)(2,1)S(1)}, bf16[1024,256]{1,0:T(8,128)(2,1)S(1)}, u32[]{:S(2)}, u32[]{:S(2)}) collective-permute-start(bf16[1024,256]{1,0:T(8,128)(2,1)S(1)} %collective-permute-done.21.refs_13_), channel_id=1, source_target_pairs={{18,17}} | collective-permute-start | bytes 1572872 | tf_op jit(solution)/shard_map/ppermute | solution.py:523
  123.4 11.1 %collective-permute-start.24 = (bf16[1024,256]{1,0:T(8,128)(2,1)S(1)}, bf16[1024,256]{1,0:T(8,128)(2,1)S(1)}, u32[]{:S(2)}, u32[]{:S(2)}) collective-permute-start(bf16[1024,256]{1,0:T(8,128)(2,1)S(1)} %collective-permute-done.22.refs_14_), channel_id=1, source_target_pairs={{1,2}} | collective-permute-start | bytes 1572872 | tf_op jit(solution)/shard_map/ppermute | solution.py:523

commit v9 on v8

--- a/solution.py
+++ b/solution.py
@@ -10,15 +10,15 @@
 from jax.sharding import PartitionSpec as P
 
 STEPS = 4
-PIECES = 2
-PARTS = ((0, 1), (1, 2))
+PIECES = 1
 DEPTH = 1
-HOP = 2
+HOP = 1
 COL_TILE = 512
+ROW_BLOCK = 512
 ROW_TILE = 32
 LANES = 128
-VMEM_LIMIT = 20 * 2**20
-RELAY_LIMIT = 8 * 2**20
+VMEM_LIMIT = 10 * 2**20
+RELAY_LIMIT = 2 * 2**20
 
 
 class Item:
@@ -198,116 +198,145 @@
 VMEM = pl.BlockSpec(memory_space=pltpu.VMEM)
 
 
-def window_kernel(*refs):
+def window_kernel(at, table, *refs):
     blocks = refs[:STEPS]
     factor, twice, male, out = refs[STEPS:]
     group_size, width = blocks[0].shape
     for s, block in enumerate(blocks):
+        rank = table[at + s]
 
         @pl.loop(0, group_size // ROW_TILE)
-        def _(i, s=s, block=block):
+        def _(i, s=s, block=block, rank=rank):
             here = pl.ds(pl.multiple_of(i * ROW_TILE, ROW_TILE), ROW_TILE)
             rows = pl.ds(pl.multiple_of(s * group_size + i * ROW_TILE, ROW_TILE), ROW_TILE)
+            to = pl.ds(pl.multiple_of(rank * group_size + i * ROW_TILE, ROW_TILE), ROW_TILE)
             for k in range(0, width, LANES):
                 value = block[here, k : k + LANES].astype(jnp.float32) - twice[rows, :]
-                out[rows, k : k + LANES] = (value * factor[rows, :] * male[:, k : k + LANES]).astype(out.dtype)
-
-
-def standardized_window(blocks, factor, twice, male):
+                out[to, k : k + LANES] = (value * factor[rows, :] * male[:, k : k + LANES]).astype(out.dtype)
+
+
+def standardized_window(at, table, blocks, factor, twice, male):
     group_size, n = blocks[0].shape
     depth = STEPS * group_size
     return pl.pallas_call(
-        window_kernel,
+        functools.partial(window_kernel, at),
         out_shape=pltpu.VMEM((depth, n), jnp.bfloat16),
-        in_specs=[VMEM] * (STEPS + 3),
+        in_specs=[pl.BlockSpec(memory_space=pltpu.SMEM)] + [VMEM] * (STEPS + 3),
         out_specs=VMEM,
         compiler_params=pltpu.CompilerParams(vmem_limit_bytes=VMEM_LIMIT),
         cost_estimate=pl.CostEstimate(flops=4 * depth * n, bytes_accessed=4 * depth * n, transcendentals=0),
         name="window",
-    )(*[in_vmem(v) for v in (*blocks, factor, twice, male)])
-
-
-def product_kernel(part, candidates, scale, n_buffers, places, x, *refs):
+    )(table, *[in_vmem(v) for v in (*blocks, factor, twice, male)])
+
+
+def standardize(table, at, candidates, x, buffers, factor, twice, male, zx, columns, first, count):
+    width = columns.stop - columns.start
+    place, step = table[at], table[at + 1]
+
+    def from_source(source, col):
+        @pl.loop(0, count // ROW_TILE)
+        def _(i):
+            here = pl.ds(pl.multiple_of(first + i * ROW_TILE, ROW_TILE), ROW_TILE)
+            to = pl.ds(pl.multiple_of(i * ROW_TILE, ROW_TILE), ROW_TILE)
+            for k in range(0, width, LANES):
+                lanes = pl.ds(pl.multiple_of(step * width + k, LANES), LANES)
+                value = source[here, pl.ds(pl.multiple_of(col + k, LANES), LANES)].astype(jnp.float32)
+                value = (value - twice[:, lanes]) * factor[:, lanes] * male[here, :]
+                zx[to, columns.start + k : columns.start + k + LANES] = value.astype(zx.dtype)
+
+    for number in candidates:
+        if number >= 0:
+
+            @pl.when(place == number)
+            def _(number=number):
+                from_source(buffers[number], 0)
+
+        else:
+
+            @pl.when(place < 0)
+            def _():
+                from_source(x, (-1 - place) * width)
+
+
+def early_kernel(at, candidates, n_buffers, table, x, *refs):
     buffers = refs[:n_buffers]
-    factor, twice, male, zy = refs[n_buffers : n_buffers + 4]
-    out, zx, tiles, sems = refs[-4:]
-    piece_rows, width = buffers[0].shape
-    first, stop = part
-
-    def standardize(source, row, col, q, s):
-        @pl.loop(0, piece_rows // ROW_TILE)
-        def _(i):
-            at = i * ROW_TILE
-            here = pl.ds(pl.multiple_of(row + at, ROW_TILE), ROW_TILE)
-            rows = pl.ds(pl.multiple_of((q - first) * piece_rows + at, ROW_TILE), ROW_TILE)
-            sexes = male[pl.ds(pl.multiple_of(q * piece_rows + at, ROW_TILE), ROW_TILE), :]
-            for k in range(0, width, LANES):
-                lanes = slice(s * width + k, s * width + k + LANES)
-                value = source[here, pl.ds(pl.multiple_of(col + k, LANES), LANES)].astype(jnp.float32)
-                zx[rows, lanes] = ((value - twice[:, lanes]) * factor[:, lanes] * sexes).astype(zx.dtype)
-
-    for q in range(first, stop):
-        for s in range(STEPS):
-            place = places[(q - first) * STEPS + s]
-            for number in candidates[(q - first) * STEPS + s]:
-                if number >= 0:
-
-                    @pl.when(place == number)
-                    def _(number=number, q=q, s=s):
-                        standardize(buffers[number], 0, 0, q, s)
-
-                else:
-
-                    @pl.when(place < 0)
-                    def _(place=place, q=q, s=s):
-                        standardize(x, q * piece_rows, (-1 - place) * width, q, s)
-
-    def copy(j):
-        where = out.at[pl.ds(first * piece_rows, zx.shape[0]), pl.ds(j * COL_TILE, COL_TILE)]
-        return pltpu.make_async_copy(tiles.at[j % 2], where, sems.at[j % 2])
-
-    count = zy.shape[1] // COL_TILE
-    for j in range(count):
-        if j >= 2:
-            copy(j - 2).wait()
-        total = jnp.dot(zx[...], zy[:, j * COL_TILE : (j + 1) * COL_TILE], preferred_element_type=jnp.float32)
-        tiles[j % 2] = (total * scale).astype(tiles.dtype)
-        copy(j).start()
-    for j in range(max(count - 2, 0), count):
-        copy(j).wait()
-
-
-def product(part, places, candidates, x, buffers, factor, twice, male, zy, before):
+    factor, twice, male, zy, total, zx = refs[n_buffers:]
+    rows, depth = zx.shape
+    width = depth // (STEPS - 1)
+    for rank in range(STEPS - 1):
+        columns = slice(rank * width, (rank + 1) * width)
+        standardize(table, at + 2 * rank, candidates[rank], x, buffers, factor, twice, male, zx, columns, 0, rows)
+
+    @pl.loop(0, rows // ROW_BLOCK)
+    def _(i):
+        block = pl.ds(pl.multiple_of(i * ROW_BLOCK, ROW_BLOCK), ROW_BLOCK)
+        for j in range(0, total.shape[1], COL_TILE):
+            right = zy[:depth, j : j + COL_TILE]
+            total[block, j : j + COL_TILE] = jnp.dot(zx[block, :], right, preferred_element_type=jnp.float32)
+
+
+def early_product(at, candidates, table, x, buffers, factor, twice, male, zy):
     rows, (depth, n) = x.shape[0], zy.shape
-    part_rows = rows // PIECES * (part[1] - part[0])
+    depth = depth // STEPS * (STEPS - 1)
+    args = [in_vmem(v) for v in (x, *buffers, factor, twice, male, zy)]
+    return pl.pallas_call(
+        functools.partial(early_kernel, at, candidates, len(buffers)),
+        out_shape=pltpu.VMEM((rows, n), jnp.float32),
+        in_specs=[pl.BlockSpec(memory_space=pltpu.SMEM)] + [VMEM] * len(args),
+        out_specs=VMEM,
+        scratch_shapes=[pltpu.VMEM((rows, depth), jnp.bfloat16)],
+        compiler_params=pltpu.CompilerParams(vmem_limit_bytes=VMEM_LIMIT),
+        cost_estimate=pl.CostEstimate(flops=2 * rows * depth * n, bytes_accessed=0, transcendentals=0),
+        name="early",
+    )(table, *args)
+
+
+def last_kernel(at, candidates, scale, n_buffers, table, x, *refs):
+    buffers = refs[:n_buffers]
+    factor, twice, male, zy, total, out, zx, blocks, sems = refs[n_buffers:]
+    rows, n = total.shape
+    width = zx.shape[1]
+
+    def copy(i):
+        return pltpu.make_async_copy(blocks.at[i % 2], out.at[pl.ds(i * ROW_BLOCK, ROW_BLOCK), :], sems.at[i % 2])
+
+    count = rows // ROW_BLOCK
+    for i in range(count):
+        first = i * ROW_BLOCK
+        standardize(
+            table, at, candidates, x, buffers, factor, twice, male, zx, slice(0, width), first, ROW_BLOCK
+        )
+        if i >= 2:
+            copy(i - 2).wait()
+        for j in range(0, n, COL_TILE):
+            right = zy[zy.shape[0] - width :, j : j + COL_TILE]
+            product = jnp.dot(zx[...], right, preferred_element_type=jnp.float32)
+            product = product + total[first : first + ROW_BLOCK, j : j + COL_TILE]
+            blocks[i % 2, :, j : j + COL_TILE] = (product * scale).astype(blocks.dtype)
+        copy(i).start()
+    for i in range(max(count - 2, 0), count):
+        copy(i).wait()
+
+
+def last_product(at, candidates, table, x, buffers, factor, twice, male, zy, total):
+    rows, (depth, n) = x.shape[0], zy.shape
+    width = depth // STEPS
     scale = float(1.0 / np.sqrt(np.float32(depth)))
-    args = [places, *[in_vmem(v) for v in (x, *buffers, factor, twice, male, zy)]]
-    specs = [pl.BlockSpec(memory_space=pltpu.SMEM)] + [VMEM] * (len(args) - 1)
-    aliases = {}
-    kernel = functools.partial(product_kernel, part, candidates, scale, len(buffers))
-    if before is not None:
-        aliases = {len(args): 0}
-        specs.append(pl.BlockSpec(memory_space=pl.ANY))
-        args.append(before)
+    args = [in_vmem(v) for v in (x, *buffers, factor, twice, male, zy, total)]
     return pl.pallas_call(
-        kernel,
+        functools.partial(last_kernel, at, candidates, scale, len(buffers)),
         out_shape=jax.ShapeDtypeStruct((rows, n), jnp.bfloat16),
-        in_specs=specs,
+        in_specs=[pl.BlockSpec(memory_space=pltpu.SMEM)] + [VMEM] * len(args),
         out_specs=pl.BlockSpec(memory_space=pl.ANY),
         scratch_shapes=[
-            pltpu.VMEM((part_rows, depth), jnp.bfloat16),
-            pltpu.VMEM((2, part_rows, COL_TILE), jnp.bfloat16),
+            pltpu.VMEM((ROW_BLOCK, width), jnp.bfloat16),
+            pltpu.VMEM((2, ROW_BLOCK, n), jnp.bfloat16),
             pltpu.SemaphoreType.DMA((2,)),
         ],
-        input_output_aliases=aliases,
         compiler_params=pltpu.CompilerParams(vmem_limit_bytes=VMEM_LIMIT),
-        cost_estimate=pl.CostEstimate(
-            flops=2 * part_rows * depth * n,
-            bytes_accessed=2 * part_rows * n,
-            transcendentals=0,
-        ),
-        name="product",
-    )(*args)
+        cost_estimate=pl.CostEstimate(flops=2 * rows * width * n, bytes_accessed=2 * rows * n, transcendentals=0),
+        name="last",
+    )(table, *args)
 
 
 def local(rows, cols, x, y, freq, weight, sex_rows, sex_cols):
@@ -403,18 +432,39 @@
     for t, (pairs, phases) in returns.items():
         if len(set(phases) - {None}) > 1:
             relays["back", t] = None, add([(1 + (p or 0), 0, 0) for p in phases])
-    table = np.concatenate(columns, axis=1) if columns else np.zeros((len(devices), 1), np.int32)
+
+    order = []
+    for r, c in devices:
+        arrivals = []
+        for s in range(STEPS):
+            when, key = 0, -1 - (r + s) % rows % groups_here
+            for d, lane in enumerate(lanes):
+                arrival = lane.arrival(r, c, (0, s))
+                if arrival is not None:
+                    t, returned = arrival
+                    when, key = (t + 0.7, ("back", t)) if returned else (t, ((r + d) % 2, t))
+            arrivals.append((when, s, key))
+        order.append(sorted(arrivals, key=lambda a: a[:2]))
+    rank_at = add([[[a[1] for a in arrivals].index(s) for s in range(STEPS)] for arrivals in order])
+    used, candidates, source_at = [], [], []
+    for ranks in (range(STEPS - 1), range(STEPS - 1, STEPS)):
+        keys = {arrivals[k][2] for arrivals in order for k in ranks}
+        used.append(sorted((k for k in keys if isinstance(k, tuple)), key=lambda k: (k[1], str(k[0]))))
+        places = [
+            [arrivals[k][2] if isinstance(arrivals[k][2], int) else used[-1].index(arrivals[k][2]) for k in ranks]
+            for arrivals in order
+        ]
+        candidates.append([sorted({max(p[i], -1) for p in places}) for i in range(len(ranks))])
+        source_at.append(
+            add([[n for p, k in zip(row, ranks) for n in (p, arrivals[k][1])] for row, arrivals in zip(places, order)])
+        )
+    table = np.concatenate(columns, axis=1)
     table = lax.dynamic_slice(jnp.asarray(table), (device, 0), (1, table.shape[1]))[0]
 
-    def own_chunk(items):
+    def own_chunk(items, x=x):
         piece = lookup([None if i is None else i.piece for i in items], device)
         group = lookup([None if i is None else group_here(i) for i in items], device)
         return lax.dynamic_slice(x, (piece * piece_rows, group * group_size), (piece_rows, group_size))
-
-    firsts = {key: own_of[key] for key in sends if key[1] == 1 and any(own_of[key])}
-    for k, crossing in enumerate(crossings):
-        firsts["cross", k] = [crossing[rc][1] if rc in crossing else None for rc in devices]
-    starts = dict(zip(firsts, lax.optimization_barrier([own_chunk(items) for items in firsts.values()])))
 
     factor = weight / jnp.sqrt(2.0 * freq * (1.0 - freq))
     twice = 2.0 * freq
@@ -435,49 +485,20 @@
         zx = ((x.astype(jnp.float32) - here(twice)) * here(factor) * male_rows[:, None]).astype(jnp.bfloat16)
         return jnp.sum(jnp.square(zx.astype(jnp.float32)), axis=1)
 
-    buffers = {}
-    last = [0] * len(PARTS)
-
-    def part_product(part, zy, before):
-        found = []
-        for r, c in devices:
-            keys = []
-            for q in range(*part):
-                for s in range(STEPS):
-                    key = -1 - (r + s) % rows % groups_here
-                    for d, lane in enumerate(lanes):
-                        arrival = lane.arrival(r, c, (q, s))
-                        if arrival is not None:
-                            t, returned = arrival
-                            key = ("back" if returned else (r + d) % 2, t)
-                    keys.append(key)
-            found.append(keys)
-        used = sorted({k for keys in found for k in keys if isinstance(k, tuple)}, key=lambda k: (k[1], str(k[0])))
-        places = [[k if isinstance(k, int) else used.index(k) for k in keys] for keys in found]
-        places = np.asarray(places, np.int32)
-        candidates = [sorted({max(int(k), -1) for k in places[:, i]}) for i in range(places.shape[1])]
-        places = lax.dynamic_slice(jnp.asarray(places), (device, 0), (1, places.shape[1]))[0]
-        held = [buffers[key] for key in used]
-        return product(
-            part, places, candidates, x, held, window_factor[None, :], window_twice[None, :], male_wide, zy, before
-        )
-
-    for number_of_part, part in enumerate(PARTS):
-        for d, lane in enumerate(lanes):
-            for r, c in devices:
-                for q in range(*part):
-                    for s in range(STEPS):
-                        arrival = lane.arrival(r, c, (q, s))
-                        if arrival is not None:
-                            t = arrival[0] + (2 if arrival[1] else 0)
-                            last[number_of_part] = max(last[number_of_part], t)
-
     back = [(i, (i - 1) % rows) for i in range(rows)]
     window = [y]
     while len(window) < STEPS:
         window.append(lax.ppermute(window[-1], "row", back))
-    zy = relation = None
     squares = own_squares()
+
+    starts = {}
+    if any(own_of[0, 1]):
+        starts[0, 1] = own_chunk(own_of[0, 1])
+    for k, crossing in enumerate(crossings):
+        starts["cross", k] = own_chunk([crossing[rc][1] if rc in crossing else None for rc in devices])
+    later_x, squares = lax.optimization_barrier((x, squares))
+    if any(own_of[1, 1]):
+        starts[1, 1] = own_chunk(own_of[1, 1], later_x)
     bits = [1 << k for k in range(cols.bit_length() - 1)] if cols & (cols - 1) == 0 else []
     if cols & (cols - 1):
         squares = lax.psum(squares, "col")
@@ -490,38 +511,31 @@
         value, other = lax.optimization_barrier((value, other))
         return value, squares + other
 
-    def window_product():
-        return standardized_window(window, wide(window_factor), wide(window_twice), male_cols[None, :])
-
-    crossed = {}
-    done = 0
+    buffers, crossed = {}, {}
+    zy = None
     for key in sends:
         phase, t = key
-        if not pairs_of[key]:
-            continue
-        if key in relays:
-            names, at = relays[key]
-            sources = [buffers[phase, t - DEPTH] if name == "forward" else crossed[name] for name in names]
-            held = relay(at, table, x, sources)
-        elif key in starts:
-            held = starts[key]
-        elif "forward" in kinds_of[key]:
-            held = buffers[phase, t - DEPTH]
-        elif "own" in kinds_of[key]:
-            held = own_chunk(own_of[key])
-        else:
-            held = crossed[next(k for k in kinds_of[key] if k is not None)]
-        if phase == 1 and t == last[0]:
-            zy, squares = sum_beside(window_product(), squares)
-            held, zy = lax.optimization_barrier((held, zy))
-        if phase == 1 and t == last[0] + 2 and zy is not None:
-            relation, squares = sum_beside(part_product(PARTS[0], zy, relation), squares)
-            held, relation = lax.optimization_barrier((held, relation))
-            done = 1
-        if phase == 1 and ("back", t - 2) in buffers:
-            held, buffers["back", t - 2] = lax.optimization_barrier((held, buffers["back", t - 2]))
-        buffers[key] = lax.ppermute(held, both, pairs_of[key])
-        if key == (1, 1):
+        if pairs_of[key]:
+            if key in relays:
+                names, at = relays[key]
+                sources = [buffers[phase, t - DEPTH] if name == "forward" else crossed[name] for name in names]
+                held = relay(at, table, x, sources)
+            elif key in starts:
+                held = starts[key]
+            elif "forward" in kinds_of[key]:
+                held = buffers[phase, t - DEPTH]
+            elif "own" in kinds_of[key]:
+                held = own_chunk(own_of[key])
+            else:
+                held = crossed[next(k for k in kinds_of[key] if k is not None)]
+            if key == (1, STEPS):
+                zy = standardized_window(
+                    rank_at, table, window, wide(window_factor), wide(window_twice), male_cols[None, :]
+                )
+                zy, squares = sum_beside(zy, squares)
+                held, zy = lax.optimization_barrier((held, zy))
+            buffers[key] = lax.ppermute(held, both, pairs_of[key])
+        if key == (0, 1):
             for k, crossing in enumerate(crossings):
                 pairs = [(number(*rc), number(*to)) for rc, (to, _) in crossing.items()]
                 crossed[k] = lax.ppermute(starts["cross", k], both, pairs)
@@ -533,9 +547,11 @@
                 held = buffers[next(p for p in phases if p is not None), t]
             buffers["back", t] = lax.ppermute(held, both, pairs)
     if zy is None:
-        zy = window_product()
-    for part in PARTS[done:]:
-        relation = part_product(part, zy, relation)
+        zy = standardized_window(rank_at, table, window, wide(window_factor), wide(window_twice), male_cols[None, :])
+    shared = window_factor[None, :], window_twice[None, :], male_wide, zy
+    total = early_product(source_at[0], candidates[0], table, x, [buffers[k] for k in used[0]], *shared)
+    total, squares = sum_beside(total, squares)
+    relation = last_product(source_at[1], candidates[1][0], table, x, [buffers[k] for k in used[1]], *shared, total)
     for bit in bits:
         squares = squares + lax.ppermute(squares, "col", [(i, i ^ bit) for i in range(cols)])
     inbreeding = squares / jnp.float32(freq.shape[0]) - 1.0

time: 145 us -> 140 us (0.966)
  the two profiles are of different devices: /device:TPU:16 before, /device:TPU:31 now
where the time goes in v9:
time: 140 us; the launch traced here: 139 us
  waiting for transfers between devices  77.8 us (56%)
  Pallas kernels  28.4 us (20%)
  starting transfers between devices  22.2 us (16%)
  local copies, waits for them, and re-layouts  8.03 us (6%)
  other arithmetic  1.74 us (1%)
    ppermute x8, waiting for transfers between devices, local(): buffers[key] = lax.ppermute(held, both, pairs_of[key])  77.8 us
    pallas_call x1, Pallas kernels, early_product(): pl.pallas_call(functools.partial(early_kernel, at, candidates, len(buffer...  11.4 us
    ppermute x8, starting transfers between devices, local(): buffers[key] = lax.ppermute(held, both, pairs_of[key])  9.95 us
    pallas_call x6, Pallas kernels, relay(): pl.pallas_call(functools.partial(relay_kernel, at), out_shape=pltpu.VMEM(...  7.91 us
    pallas_call x1, Pallas kernels, last_product(): pl.pallas_call(functools.partial(last_kernel, at, candidates, scale, len(...  5.73 us
    ppermute x3, starting transfers between devices, local(): window.append(lax.ppermute(window[-1], 'row', back))  4.31 us
    dynamic_slice x2, local copies, waits for them, and re-layouts, own_chunk(): lax.dynamic_slice(x, (piece * piece_rows, group * group_size), (piece_row...  4.21 us
    pallas_call x1, Pallas kernels, standardized_window(): pl.pallas_call(functools.partial(window_kernel, at), out_shape=pltpu.VMEM...  3.41 us
  transfers between devices with their start and end apart: 16, of which 4 were waited for; matrix products, arithmetic and copies ran while one was open for 3% of the time, Pallas kernels for 16%

profile of v9, /device:TPU:31, one launch (start us, length us, event | category | flops | bytes accessed | tf_op | source)
XLA Modules:
  0.0 139.2 jit_solution(10785815719389180338)
XLA Ops:
  0.6 0.0 copy-start
  0.6 0.0 copy-start.13
  0.7 0.0 copy-start.12
  0.7 3.1 %constant_dynamic-slice_fusion.1 = (bf16[2048,256]{1,0:T(8,128)(2,1)}, bf16[2048,256]{1,0:T(8,128)(2,1)}) fusion(bf16[2048,512]{1,0:T(8,128)(2,1)} %x.15, s32[]{:T(128)S(6)} %select_n.41, s32[]{:T(128)S(6)} %select_n.40), kind=kLoop, calls=%fused_computation.14 | loop fusion | bytes 4194312 | tf_op jit(solution)/shard_map/dynamic_slice | solution.py:467
  3.8 1.6 %collective-permute-start = (bf16[2048,256]{1,0:T(8,128)(2,1)}, bf16[2048,256]{1,0:T(8,128)(2,1)}, u32[]{:S(2)}, u32[]{:S(2)}) collective-permute-start(bf16[2048,256]{1,0:T(8,128)(2,1)} %get-tuple-element.19), channel_id=1, source_target_pairs={{18,2},{9,25},{13,29},{1,17},{6,22},{10,26}} | collective-permute-start | bytes 3145736 | tf_op jit(solution)/shard_map/ppermute | solution.py:541
  5.5 0.0 copy-done.12
  5.5 0.1 dynamic_slice.27
  5.6 0.1 dynamic_slice.28
  5.6 0.0 copy-done.10
  5.6 1.0 multiply_reduce_fusion
  6.7 1.1 constant_dynamic-slice_fusion
  7.8 2.1 %collective-permute-start.3 = (bf16[2048,256]{1,0:T(8,128)(2,1)}, bf16[2048,256]{1,0:T(8,128)(2,1)S(1)}, u32[]{:S(2)}, u32[]{:S(2)}) collective-permute-start(bf16[2048,256]{1,0:T(8,128)(2,1)} %constant_dynamic-slice_fusion), channel_id=1, source_target_pairs={{0,1},{1,2},{5,4},{9,10},{10,11},{14,13},{18,19},{22,21},{23,22},{... | collective-permute-start | bytes 3145736 | tf_op jit(solution)/shard_map/ppermute | solution.py:537
  9.9 1.7 %collective-permute-start.1 = (bf16[2048,256]{1,0:T(8,128)(2,1)}, bf16[2048,256]{1,0:T(8,128)(2,1)}, u32[]{:S(2)}, u32[]{:S(2)}) collective-permute-start(bf16[2048,256]{1,0:T(8,128)(2,1)} %get-tuple-element.18), channel_id=1, source_target_pairs={{1,0},{5,6},{9,8},{10,9},{14,15},{18,17},{19,18},{20,21},{22,23},{... | collective-permute-start | bytes 3145736 | tf_op jit(solution)/shard_map/ppermute | solution.py:537
  11.6 0.6 collective-permute-start.8
  12.2 0.7 fusion.2.table
  12.9 0.0 collective-permute-done.refs_0_
  12.9 18.6 %collective-permute-done.3.refs_1_ = bf16[2048,256]{1,0:T(8,128)(2,1)S(1)} collective-permute-done((bf16[2048,256]{1,0:T(8,128)(2,1)}, bf16[2048,256]{1,0:T(8,128)(2,1)S(1)}, u32[]{:S(2)}, u32[]{:S(2)}) %collective-permute-start.3) | collective-permute-done | bytes 1048608 | tf_op jit(solution)/shard_map/ppermute | solution.py:537
  31.5 1.7 %relay.7 = bf16[2048,256]{1,0:T(8,128)(2,1)S(1)} custom-call(s32[30]{0:T(128)S(1)} %fusion.2.table, bf16[2048,512]{1,0:T(8,128)(2,1)S(1)} %copy-done, bf16[2048,256]{1,0:T(8,128)(2,1)} %collective-permute-done.refs_0_, bf16[2048,256]{1,0:T(8,128)(2,1)S(1)} %collective-permute-done.3.refs_1_), custom_call_target="tpu_custom_call" | custom-call | tf_op jit(solution)/shard_map/relay/pallas_call | solution.py:183
  33.2 0.7 collective-permute-start.4
  33.9 0.0 collective-permute-done.1.refs_1_.refs_0_
  33.9 1.6 %relay.6 = bf16[2048,256]{1,0:T(8,128)(2,1)S(1)} custom-call(s32[30]{0:T(128)S(1)} %fusion.2.table, bf16[2048,512]{1,0:T(8,128)(2,1)S(1)} %copy-done, bf16[2048,256]{1,0:T(8,128)(2,1)} %collective-permute-done.refs_0_, bf16[2048,256]{1,0:T(8,128)(2,1)} %collective-permute-done.1.refs_1_.refs_0_), custom_call_target="tpu_custom_call" | custom-call | tf_op jit(solution)/shard_map/relay/pallas_call | solution.py:183
  35.6 0.0 copy-start.11
  35.6 1.3 collective-permute-start.2
  36.9 0.0 collective-permute-done.8.refs_1_
  36.9 3.6 %collective-permute-start.9 = (bf16[256,2048]{1,0:T(8,128)(2,1)}, bf16[256,2048]{1,0:T(8,128)(2,1)}, u32[]{:S(2)}, u32[]{:S(2)}) collective-permute-start(bf16[256,2048]{1,0:T(8,128)(2,1)} %collective-permute-done.8.refs_1_), channel_id=1, source_target_pairs={{0,28},{4,0},{8,4},{12,8},{16,12},{20,16},{24,20},{28,24},{1,29},{... | collective-permute-start | bytes 3145736 | tf_op jit(solution)/shard_map/ppermute | solution.py:491
  40.5 0.0 collective-permute-done.4.refs_1_.refs_3_
  40.6 0.7 collective-permute-start.6
  41.3 19.8 %collective-permute-done.2.refs_0_.refs_2_ = bf16[2048,256]{1,0:T(8,128)(2,1)S(1)} collective-permute-done((bf16[2048,256]{1,0:T(8,128)(2,1)S(1)}, bf16[2048,256]{1,0:T(8,128)(2,1)S(1)}, u32[]{:S(2)}, u32[]{:S(2)}) %collective-permute-start.2) | collective-permute-done | bytes 1048608 | tf_op jit(solution)/shard_map/ppermute | solution.py:537
  61.1 1.3 collective-permute-start.5
  62.4 0.0 collective-permute-done.9.refs_2_
  62.4 0.1 collective-permute-start.10
  62.5 1.7 %relay.10 = bf16[2048,256]{1,0:T(8,128)(2,1)} custom-call(s32[30]{0:T(128)S(1)} %fusion.2.table, bf16[2048,512]{1,0:T(8,128)(2,1)S(1)} %copy-done, bf16[2048,256]{1,0:T(8,128)(2,1)S(1)} %collective-permute-done.2.refs_0_.refs_2_, bf16[2048,256]{1,0:T(8,128)(2,1)S(1)} %collective-permute-done.4.refs_1_.refs_3_), custom_call_target="tpu_custom_call" | custom-call | tf_op jit(solution)/shard_map/relay/pallas_call | solution.py:183
  64.2 1.7 %collective-permute-start.13 = (bf16[2048,256]{1,0:T(8,128)(2,1)}, bf16[2048,256]{1,0:T(8,128)(2,1)}, u32[]{:S(2)}, u32[]{:S(2)}) collective-permute-start(bf16[2048,256]{1,0:T(8,128)(2,1)} %relay.10), channel_id=1, source_target_pairs={{24,8},{28,12},{23,7},{27,11}} | collective-permute-start | bytes 3145736 | tf_op jit(solution)/shard_map/ppermute | solution.py:548
  65.8 0.0 collective-permute-done.6.refs_0_.refs_1_.refs_6_.refs_3_
  65.8 27.3 %collective-permute-done.5.refs_0_.refs_5_.refs_2_ = bf16[2048,256]{1,0:T(8,128)(2,1)S(1)} collective-permute-done((bf16[2048,256]{1,0:T(8,128)(2,1)S(1)}, bf16[2048,256]{1,0:T(8,128)(2,1)S(1)}, u32[]{:S(2)}, u32[]{:S(2)}) %collective-permute-start.5) | collective-permute-done | bytes 1048608 | tf_op jit(solution)/shard_map/ppermute | solution.py:537
  93.1 1.6 %relay.11 = bf16[2048,256]{1,0:T(8,128)(2,1)} custom-call(s32[30]{0:T(128)S(1)} %fusion.2.table, bf16[2048,512]{1,0:T(8,128)(2,1)S(1)} %copy-done, bf16[2048,256]{1,0:T(8,128)(2,1)S(1)} %collective-permute-done.5.refs_0_.refs_5_.refs_2_, bf16[2048,256]{1,0:T(8,128)(2,1)S(1)} %collective-permute-done.6.refs_0_.refs_1_.refs_6_.refs_3_), custom_call_target="tpu_custom_call" | custom-call | tf_op jit(solution)/shard_map/relay/pallas_call | solution.py:183
  94.7 0.0 copy-done.5
  94.8 1.0 copy-done.1
  95.7 1.6 %collective-permute-start.14 = (bf16[2048,256]{1,0:T(8,128)(2,1)}, bf16[2048,256]{1,0:T(8,128)(2,1)}, u32[]{:S(2)}, u32[]{:S(2)}) collective-permute-start(bf16[2048,256]{1,0:T(8,128)(2,1)} %relay.11), channel_id=1, source_target_pairs={{0,16},{19,3}} | collective-permute-start | bytes 3145736 | tf_op jit(solution)/shard_map/ppermute | solution.py:548
  97.4 2.9 %collective-permute-start.11 = (f32[2048]{0:T(1024)S(1)}, f32[2048]{0:T(1024)S(1)}, u32[]{:S(2)}, u32[]{:S(2)}) collective-permute-start(f32[2048]{0:T(1024)S(1)} %multiply_reduce_fusion), channel_id=1, source_target_pairs={{0,1},{1,0},{2,3},{3,2},{4,5},{5,4},{6,7},{7,6},{8,9},{9,8},{10,11... | collective-permute-start | bytes 24584 | tf_op jit(solution)/shard_map/ppermute | solution.py:510
  100.3 0.1 fusion
  100.3 0.0 collective-permute-done.10.refs_3_
  100.3 0.2 broadcast_in_dim.21.refs_4_
  100.5 0.2 broadcast_in_dim.40.refs_5_
  100.8 0.0 copy-start.9
  100.8 1.2 copy-done.9
  102.0 3.4 %window.1.refs_11_.refs_9_ = bf16[1024,2048]{1,0:T(8,128)(2,1)S(1)} custom-call(s32[30]{0:T(128)S(1)} %fusion.2.table, bf16[256,2048]{1,0:T(8,128)(2,1)S(1)} %copy-done.9, bf16[256,2048]{1,0:T(8,128)(2,1)} %collective-permute-done.8.refs_1_, bf16[256,2048]{1,0:T(8,128)(2,1)} %collective-permute-done.9.refs_2_, ...), custom_call_target="tpu_custom_call" | custom-call | flops 8388608 | bytes 8388608 | tf_op jit(solution)/shard_map/window/pallas_call | solution.py:221
  105.4 0.0 copy-start.6
  105.4 0.0 copy-start.8
  105.4 0.0 collective-permute-done.11
  105.4 0.6 relay.9
  106.1 0.9 collective-permute-start.12
  107.0 0.6 relay.8
  107.6 1.3 collective-permute-start.7
  108.9 0.1 collective-permute-start.15
  109.0 0.0 collective-permute-done.13.refs_4_
  109.0 0.0 collective-permute-done.14.refs_7_
  109.0 0.3 broadcast_in_dim.44.refs_10_.refs_8_
  109.4 11.4 %early.1.refs_10_ = f32[2048,2048]{1,0:T(8,128)S(1)} custom-call(s32[30]{0:T(128)S(1)} %fusion.2.table, bf16[2048,512]{1,0:T(8,128)(2,1)S(1)} %copy-done, bf16[2048,256]{1,0:T(8,128)(2,1)} %collective-permute-done.1.refs_1_.refs_0_, bf16[2048,256]{1,0:T(8,128)(2,1)S(1)} %copy-done.8, bf16[2048,256]{1,0:T(8,128)(2,1)S(1)} %copy-done.6, ...), custom_call_target="tpu_custom_call" | custom-call | flops 6442450944 | tf_op jit(solution)/shard_map/early/pallas_call | solution.py:282
  120.8 0.0 collective-permute-done.15
  120.8 0.6 multiply_add_fusion
  121.4 0.0 collective-permute-done.12.refs_5_
  121.4 12.1 %collective-permute-done.7.refs_4_ = bf16[2048,256]{1,0:T(8,128)(2,1)S(1)} collective-permute-done((bf16[2048,256]{1,0:T(8,128)(2,1)S(1)}, bf16[2048,256]{1,0:T(8,128)(2,1)S(1)}, u32[]{:S(2)}, u32[]{:S(2)}) %collective-permute-start.7) | collective-permute-done | bytes 1048608 | tf_op jit(solution)/shard_map/ppermute | solution.py:537
  133.4 5.7 %last.1 = bf16[2048,2048]{1,0:T(8,128)(2,1)} custom-call(s32[30]{0:T(128)S(1)} %fusion.2.table, bf16[2048,512]{1,0:T(8,128)(2,1)S(1)} %copy-done, bf16[2048,256]{1,0:T(8,128)(2,1)S(1)} %copy-done.6, bf16[2048,256]{1,0:T(8,128)(2,1)S(1)} %copy-done.4, bf16[2048,256]{1,0:T(8,128)(2,1)S(1)} %copy-done.2, ...), custom_call_target="tpu_custom_call" | custom-call | flops 2147483648 | bytes 8388608 | tf_op jit(solution)/shard_map/last/pallas_call | solution.py:326
  (20 shorter events, 0.0 us)
Async XLA Ops:
  0.6 5.0 %copy-start = (bf16[2048,512]{1,0:T(8,128)(2,1)S(1)}, bf16[2048,512]{1,0:T(8,128)(2,1)}, u32[]{:S(2)}) copy-start(bf16[2048,512]{1,0:T(8,128)(2,1)} %x.15) | copy-start | bytes 6291460
  0.6 4.8 %copy-start.13 = (f32[2048]{0:T(1024)S(1)}, f32[2048]{0:T(1024)}, u32[]{:S(2)}) copy-start(f32[2048]{0:T(1024)} %param.10) | copy-start | bytes 24580
  0.7 4.8 %copy-start.12 = (f32[2048]{0:T(1024)S(1)}, f32[2048]{0:T(1024)}, u32[]{:S(2)}) copy-start(f32[2048]{0:T(1024)} %param.9) | copy-start | bytes 24580
  0.7 5.0 %copy-start.10 = (s32[2048]{0:T(1024)S(1)}, s32[2048]{0:T(1024)}, u32[]{:S(2)}) copy-start(s32[2048]{0:T(1024)} %param.11) | copy-start | bytes 24580
  3.8 9.1 %collective-permute-start = (bf16[2048,256]{1,0:T(8,128)(2,1)}, bf16[2048,256]{1,0:T(8,128)(2,1)}, u32[]{:S(2)}, u32[]{:S(2)}) collective-permute-start(bf16[2048,256]{1,0:T(8,128)(2,1)} %get-tuple-element.19), channel_id=1, source_target_pairs={{18,2},{9,25},{13,29},{1,17},{6,22},{10,26}} | collective-permute-start | bytes 3145736 | tf_op jit(solution)/shard_map/ppermute | solution.py:541
  7.8 23.7 %collective-permute-start.3 = (bf16[2048,256]{1,0:T(8,128)(2,1)}, bf16[2048,256]{1,0:T(8,128)(2,1)S(1)}, u32[]{:S(2)}, u32[]{:S(2)}) collective-permute-start(bf16[2048,256]{1,0:T(8,128)(2,1)} %constant_dynamic-slice_fusion), channel_id=1, source_target_pairs={{0,1},{1,2},{5,4},{9,10},{10,11},{14,13},{18,19},{22,21},{23,22},{... | collective-permute-start | bytes 3145736 | tf_op jit(solution)/shard_map/ppermute | solution.py:537
  9.9 24.0 %collective-permute-start.1 = (bf16[2048,256]{1,0:T(8,128)(2,1)}, bf16[2048,256]{1,0:T(8,128)(2,1)}, u32[]{:S(2)}, u32[]{:S(2)}) collective-permute-start(bf16[2048,256]{1,0:T(8,128)(2,1)} %get-tuple-element.18), channel_id=1, source_target_pairs={{1,0},{5,6},{9,8},{10,9},{14,15},{18,17},{19,18},{20,21},{22,23},{... | collective-permute-start | bytes 3145736 | tf_op jit(solution)/shard_map/ppermute | solution.py:537
  11.6 25.4 %collective-permute-start.8 = (bf16[256,2048]{1,0:T(8,128)(2,1)}, bf16[256,2048]{1,0:T(8,128)(2,1)}, u32[]{:S(2)}, u32[]{:S(2)}) collective-permute-start(bf16[256,2048]{1,0:T(8,128)(2,1)} %refs_0_.1), channel_id=1, source_target_pairs={{0,28},{4,0},{8,4},{12,8},{16,12},{20,16},{24,20},{28,24},{1,29},{... | collective-permute-start | bytes 3145736 | tf_op jit(solution)/shard_map/ppermute | solution.py:491
  31.5 4.1 %copy-start.7 = (bf16[2048,256]{1,0:T(8,128)(2,1)}, bf16[2048,256]{1,0:T(8,128)(2,1)S(1)}, u32[]{:S(2)}) copy-start(bf16[2048,256]{1,0:T(8,128)(2,1)S(1)} %collective-permute-done.3.refs_1_) | copy-start | bytes 3145732
  33.2 7.3 %collective-permute-start.4 = (bf16[2048,256]{1,0:T(8,128)(2,1)S(1)}, bf16[2048,256]{1,0:T(8,128)(2,1)S(1)}, u32[]{:S(2)}, u32[]{:S(2)}) collective-permute-start(bf16[2048,256]{1,0:T(8,128)(2,1)S(1)} %relay.7), channel_id=1, source_target_pairs={{0,1},{1,2},{2,3},{5,4},{6,5},{9,10},{10,11},{13,12},{14,13},{15,1... | collective-permute-start | bytes 3145736 | tf_op jit(solution)/shard_map/ppermute | solution.py:537
  35.6 64.7 %copy-start.11 = (s32[2048]{0:T(1024)S(1)}, s32[2048]{0:T(1024)}, u32[]{:S(2)}) copy-start(s32[2048]{0:T(1024)} %param.12) | copy-start | bytes 24580
  35.6 25.5 %collective-permute-start.2 = (bf16[2048,256]{1,0:T(8,128)(2,1)S(1)}, bf16[2048,256]{1,0:T(8,128)(2,1)S(1)}, u32[]{:S(2)}, u32[]{:S(2)}) collective-permute-start(bf16[2048,256]{1,0:T(8,128)(2,1)S(1)} %relay.6), channel_id=1, source_target_pairs={{1,0},{2,1},{4,5},{5,6},{6,7},{9,8},{10,9},{13,14},{14,15},{17,16}... | collective-permute-start | bytes 3145736 | tf_op jit(solution)/shard_map/ppermute | solution.py:537
  36.9 25.5 %collective-permute-start.9 = (bf16[256,2048]{1,0:T(8,128)(2,1)}, bf16[256,2048]{1,0:T(8,128)(2,1)}, u32[]{:S(2)}, u32[]{:S(2)}) collective-permute-start(bf16[256,2048]{1,0:T(8,128)(2,1)} %collective-permute-done.8.refs_1_), channel_id=1, source_target_pairs={{0,28},{4,0},{8,4},{12,8},{16,12},{20,16},{24,20},{28,24},{1,29},{... | collective-permute-start | bytes 3145736 | tf_op jit(solution)/shard_map/ppermute | solution.py:491
  40.5 54.2 %copy-start.3 = (bf16[2048,256]{1,0:T(8,128)(2,1)}, bf16[2048,256]{1,0:T(8,128)(2,1)S(1)}, u32[]{:S(2)}) copy-start(bf16[2048,256]{1,0:T(8,128)(2,1)S(1)} %collective-permute-done.4.refs_1_.refs_3_) | copy-start | bytes 3145732
  40.6 25.3 %collective-permute-start.6 = (bf16[2048,256]{1,0:T(8,128)(2,1)S(1)}, bf16[2048,256]{1,0:T(8,128)(2,1)S(1)}, u32[]{:S(2)}, u32[]{:S(2)}) collective-permute-start(bf16[2048,256]{1,0:T(8,128)(2,1)S(1)} %collective-permute-done.4.refs_1_.refs_3_), channel_id=1, source_target_pairs={{1,2},{2,3},{5,4},{10,11},{13,12},{14,13},{18,19},{21,20},{22,21},... | collective-permute-start | bytes 3145736 | tf_op jit(solution)/shard_map/ppermute | solution.py:537
  61.1 33.7 %copy-start.5 = (bf16[2048,256]{1,0:T(8,128)(2,1)}, bf16[2048,256]{1,0:T(8,128)(2,1)S(1)}, u32[]{:S(2)}) copy-start(bf16[2048,256]{1,0:T(8,128)(2,1)S(1)} %collective-permute-done.2.refs_0_.refs_2_) | copy-start | bytes 3145732
  61.1 32.0 %collective-permute-start.5 = (bf16[2048,256]{1,0:T(8,128)(2,1)S(1)}, bf16[2048,256]{1,0:T(8,128)(2,1)S(1)}, u32[]{:S(2)}, u32[]{:S(2)}) collective-permute-start(bf16[2048,256]{1,0:T(8,128)(2,1)S(1)} %collective-permute-done.2.refs_0_.refs_2_), channel_id=1, source_target_pairs={{1,0},{5,6},{6,7},{9,8},{14,15},{17,16},{18,17},{22,23},{25,24},{2... | collective-permute-start | bytes 3145736 | tf_op jit(solution)/shard_map/ppermute | solution.py:537
  62.4 38.0 %collective-permute-start.10 = (bf16[256,2048]{1,0:T(8,128)(2,1)}, bf16[256,2048]{1,0:T(8,128)(2,1)}, u32[]{:S(2)}, u32[]{:S(2)}) collective-permute-start(bf16[256,2048]{1,0:T(8,128)(2,1)} %collective-permute-done.9.refs_2_), channel_id=1, source_target_pairs={{0,28},{4,0},{8,4},{12,8},{16,12},{20,16},{24,20},{28,24},{1,29},{... | collective-permute-start | bytes 3145736 | tf_op jit(solution)/shard_map/ppermute | solution.py:491
  64.2 44.8 %collective-permute-start.13 = (bf16[2048,256]{1,0:T(8,128)(2,1)}, bf16[2048,256]{1,0:T(8,128)(2,1)}, u32[]{:S(2)}, u32[]{:S(2)}) collective-permute-start(bf16[2048,256]{1,0:T(8,128)(2,1)} %relay.10), channel_id=1, source_target_pairs={{24,8},{28,12},{23,7},{27,11}} | collective-permute-start | bytes 3145736 | tf_op jit(solution)/shard_map/ppermute | solution.py:548
  94.7 1.0 copy-start.1
  95.7 13.3 %collective-permute-start.14 = (bf16[2048,256]{1,0:T(8,128)(2,1)}, bf16[2048,256]{1,0:T(8,128)(2,1)}, u32[]{:S(2)}, u32[]{:S(2)}) collective-permute-start(bf16[2048,256]{1,0:T(8,128)(2,1)} %relay.11), channel_id=1, source_target_pairs={{0,16},{19,3}} | collective-permute-start | bytes 3145736 | tf_op jit(solution)/shard_map/ppermute | solution.py:548
  97.4 8.1 %collective-permute-start.11 = (f32[2048]{0:T(1024)S(1)}, f32[2048]{0:T(1024)S(1)}, u32[]{:S(2)}, u32[]{:S(2)}) collective-permute-start(f32[2048]{0:T(1024)S(1)} %multiply_reduce_fusion), channel_id=1, source_target_pairs={{0,1},{1,0},{2,3},{3,2},{4,5},{5,4},{6,7},{7,6},{8,9},{9,8},{10,11... | collective-permute-start | bytes 24584 | tf_op jit(solution)/shard_map/ppermute | solution.py:510
  100.8 1.2 copy-start.9
  105.4 1.6 %copy-start.2 = (bf16[2048,256]{1,0:T(8,128)(2,1)S(1)}, bf16[2048,256]{1,0:T(8,128)(2,1)}, u32[]{:S(2)}) copy-start(bf16[2048,256]{1,0:T(8,128)(2,1)} %copy-done.1) | copy-start | bytes 3145732
  105.4 3.9 %copy-start.4 = (bf16[2048,256]{1,0:T(8,128)(2,1)S(1)}, bf16[2048,256]{1,0:T(8,128)(2,1)}, u32[]{:S(2)}) copy-start(bf16[2048,256]{1,0:T(8,128)(2,1)} %copy-done.3) | copy-start | bytes 3145732
  105.4 3.9 %copy-start.6 = (bf16[2048,256]{1,0:T(8,128)(2,1)S(1)}, bf16[2048,256]{1,0:T(8,128)(2,1)}, u32[]{:S(2)}) copy-start(bf16[2048,256]{1,0:T(8,128)(2,1)} %copy-done.5) | copy-start | bytes 3145732
  105.4 3.9 %copy-start.8 = (bf16[2048,256]{1,0:T(8,128)(2,1)S(1)}, bf16[2048,256]{1,0:T(8,128)(2,1)}, u32[]{:S(2)}) copy-start(bf16[2048,256]{1,0:T(8,128)(2,1)} %copy-done.7) | copy-start | bytes 3145732
  106.1 15.3 %collective-permute-start.12 = (bf16[2048,256]{1,0:T(8,128)(2,1)S(1)}, bf16[2048,256]{1,0:T(8,128)(2,1)S(1)}, u32[]{:S(2)}, u32[]{:S(2)}) collective-permute-start(bf16[2048,256]{1,0:T(8,128)(2,1)S(1)} %relay.9), channel_id=1, source_target_pairs={{1,2},{2,3},{13,12},{21,20},{26,27}} | collective-permute-start | bytes 3145736 | tf_op jit(solution)/shard_map/ppermute | solution.py:537
  107.6 25.8 %collective-permute-start.7 = (bf16[2048,256]{1,0:T(8,128)(2,1)S(1)}, bf16[2048,256]{1,0:T(8,128)(2,1)S(1)}, u32[]{:S(2)}, u32[]{:S(2)}) collective-permute-start(bf16[2048,256]{1,0:T(8,128)(2,1)S(1)} %relay.8), channel_id=1, source_target_pairs={{6,7},{17,16},{18,17},{25,24},{30,31}} | collective-permute-start | bytes 3145736 | tf_op jit(solution)/shard_map/ppermute | solution.py:537
  108.9 11.9 %collective-permute-start.15 = (f32[2048]{0:T(1024)S(1)}, f32[2048]{0:T(1024)S(1)}, u32[]{:S(2)}, u32[]{:S(2)}) collective-permute-start(f32[2048]{0:T(1024)S(1)} %add.44), channel_id=1, source_target_pairs={{0,2},{1,3},{2,0},{3,1},{4,6},{5,7},{6,4},{7,5},{8,10},{9,11},{10,... | collective-permute-start | bytes 24584 | tf_op jit(solution)/shard_map/ppermute | solution.py:510

commit v10 on v9

--- a/solution.py
+++ b/solution.py
@@ -492,13 +492,15 @@
     squares = own_squares()
 
     starts = {}
+    if any(own_of[1, 1]):
+        starts[1, 1] = own_chunk(own_of[1, 1])
+    later_x = x
+    for k, crossing in enumerate(crossings):
+        later_x = lax.optimization_barrier(later_x)
+        starts["cross", k] = own_chunk([crossing[rc][1] if rc in crossing else None for rc in devices], later_x)
+    later_x, squares = lax.optimization_barrier((later_x, squares))
     if any(own_of[0, 1]):
-        starts[0, 1] = own_chunk(own_of[0, 1])
-    for k, crossing in enumerate(crossings):
-        starts["cross", k] = own_chunk([crossing[rc][1] if rc in crossing else None for rc in devices])
-    later_x, squares = lax.optimization_barrier((x, squares))
-    if any(own_of[1, 1]):
-        starts[1, 1] = own_chunk(own_of[1, 1], later_x)
+        starts[0, 1] = own_chunk(own_of[0, 1], later_x)
     bits = [1 << k for k in range(cols.bit_length() - 1)] if cols & (cols - 1) == 0 else []
     if cols & (cols - 1):
         squares = lax.psum(squares, "col")
@@ -512,7 +514,16 @@
         return value, squares + other
 
     buffers, crossed = {}, {}
-    zy = None
+
+    def bring_back(t):
+        if t in returns:
+            pairs, phases = returns[t]
+            if ("back", t) in relays:
+                held = relay(relays["back", t][1], table, x, [buffers[0, t], buffers[1, t]])
+            else:
+                held = buffers[next(p for p in phases if p is not None), t]
+            buffers["back", t] = lax.ppermute(held, both, pairs)
+
     for key in sends:
         phase, t = key
         if pairs_of[key]:
@@ -528,29 +539,21 @@
                 held = own_chunk(own_of[key])
             else:
                 held = crossed[next(k for k in kinds_of[key] if k is not None)]
-            if key == (1, STEPS):
-                zy = standardized_window(
-                    rank_at, table, window, wide(window_factor), wide(window_twice), male_cols[None, :]
-                )
-                zy, squares = sum_beside(zy, squares)
-                held, zy = lax.optimization_barrier((held, zy))
+            if phase == 1 and t in (2, 3):
+                held, squares = sum_beside(held, squares)
+            if phase == 1 and t - 1 in returns:
+                held, table = lax.optimization_barrier((held, table))
             buffers[key] = lax.ppermute(held, both, pairs_of[key])
         if key == (0, 1):
             for k, crossing in enumerate(crossings):
                 pairs = [(number(*rc), number(*to)) for rc, (to, _) in crossing.items()]
                 crossed[k] = lax.ppermute(starts["cross", k], both, pairs)
-        if phase == 1 and t in returns:
-            pairs, phases = returns[t]
-            if ("back", t) in relays:
-                held = relay(relays["back", t][1], table, x, [buffers[0, t], buffers[1, t]])
-            else:
-                held = buffers[next(p for p in phases if p is not None), t]
-            buffers["back", t] = lax.ppermute(held, both, pairs)
-    if zy is None:
-        zy = standardized_window(rank_at, table, window, wide(window_factor), wide(window_twice), male_cols[None, :])
+        if phase == 1:
+            bring_back(t - 1)
+    bring_back(rounds)
+    zy = standardized_window(rank_at, table, window, wide(window_factor), wide(window_twice), male_cols[None, :])
     shared = window_factor[None, :], window_twice[None, :], male_wide, zy
     total = early_product(source_at[0], candidates[0], table, x, [buffers[k] for k in used[0]], *shared)
-    total, squares = sum_beside(total, squares)
     relation = last_product(source_at[1], candidates[1][0], table, x, [buffers[k] for k in used[1]], *shared, total)
     for bit in bits:
         squares = squares + lax.ppermute(squares, "col", [(i, i ^ bit) for i in range(cols)])

time: 140 us -> 137 us (0.979)
  waiting for transfers between devices: 77.8 us -> 49.4 us
  starting transfers between devices: 22.2 us -> 45.2 us
  local copies, waits for them, and re-layouts: 8.03 us -> 10.5 us
    ppermute x8, waiting for transfers between devices: 77.8 us -> 31.6 us  [local(): buffers[key] = lax.ppermute(held, both, pairs_of[key])]
    ppermute x2, starting transfers between devices: 2.96 us -> 28.2 us  [sum_beside(): other = lax.ppermute(squares, 'col', [(i, i ^ bit) for i in range(cols)])]
    ppermute x2, waiting for transfers between devices: 0.01 us -> 17.8 us  [sum_beside(): other = lax.ppermute(squares, 'col', [(i, i ^ bit) for i in range(cols)])]
    ppermute x3, starting transfers between devices: 4.31 us -> 2.24 us  [local(): window.append(lax.ppermute(window[-1], 'row', back))]
    dynamic_slice x2 -> x3, local copies, waits for them, and re-layouts: 4.21 us -> 5.7 us  [own_chunk(): lax.dynamic_slice(x, (piece * piece_rows, group * group_size), (piece_row...]
    unnamed x28 -> x32, local copies, waits for them, and re-layouts: 2.26 us -> 3.24 us
  transfers between devices with their start and end apart: 16 -> 16, of which waited for: 4 -> 4; matrix products, arithmetic and copies ran while one was open for 3% -> 5% of each run, Pallas kernels for 16% -> 17%
where the time goes in v10:
time: 137 us; the launch traced here: 136 us
  waiting for transfers between devices  49.4 us (36%)
  starting transfers between devices  45.2 us (33%)
  Pallas kernels  28.5 us (21%)
  local copies, waits for them, and re-layouts  10.5 us (8%)
  other arithmetic  1.73 us (1%)
    ppermute x8, waiting for transfers between devices, local(): buffers[key] = lax.ppermute(held, both, pairs_of[key])  31.6 us
    ppermute x2, starting transfers between devices, sum_beside(): other = lax.ppermute(squares, 'col', [(i, i ^ bit) for i in range(cols)])  28.2 us
    ppermute x2, waiting for transfers between devices, sum_beside(): other = lax.ppermute(squares, 'col', [(i, i ^ bit) for i in range(cols)])  17.8 us
    pallas_call x1, Pallas kernels, early_product(): pl.pallas_call(functools.partial(early_kernel, at, candidates, len(buffer...  11.4 us
    ppermute x8, starting transfers between devices, local(): buffers[key] = lax.ppermute(held, both, pairs_of[key])  9.81 us
    pallas_call x6, Pallas kernels, relay(): pl.pallas_call(functools.partial(relay_kernel, at), out_shape=pltpu.VMEM(...  7.84 us
    pallas_call x1, Pallas kernels, last_product(): pl.pallas_call(functools.partial(last_kernel, at, candidates, scale, len(...  5.75 us
    dynamic_slice x3, local copies, waits for them, and re-layouts, own_chunk(): lax.dynamic_slice(x, (piece * piece_rows, group * group_size), (piece_row...  5.7 us
  transfers between devices with their start and end apart: 16, of which 4 were waited for; matrix products, arithmetic and copies ran while one was open for 5% of the time, Pallas kernels for 17%

profile of v10, /device:TPU:31, one launch (start us, length us, event | category | flops | bytes accessed | tf_op | source)
XLA Modules:
  0.0 136.4 jit_solution(5623782467736606670)
XLA Ops:
  0.6 0.0 copy-start
  0.6 0.0 copy-start.12
  0.7 0.0 copy-start.15
  0.7 0.0 copy-start.14
  0.7 2.4 %constant_dynamic-slice_fusion.1 = bf16[2048,256]{1,0:T(8,128)(2,1)} fusion(bf16[2048,512]{1,0:T(8,128)(2,1)} %x.15, s32[]{:T(128)S(6)} %select_n.41), kind=kLoop, calls=%fused_computation.14 | loop fusion | bytes 2097156 | tf_op jit(solution)/shard_map/dynamic_slice | solution.py:467
  3.1 2.1 %collective-permute-start.1 = (bf16[2048,256]{1,0:T(8,128)(2,1)}, bf16[2048,256]{1,0:T(8,128)(2,1)S(1)}, u32[]{:S(2)}, u32[]{:S(2)}) collective-permute-start(bf16[2048,256]{1,0:T(8,128)(2,1)} %constant_dynamic-slice_fusion.1), channel_id=1, source_target_pairs={{0,1},{1,2},{5,4},{9,10},{10,11},{14,13},{18,19},{22,21},{23,22},{... | collective-permute-start | bytes 3145736 | tf_op jit(solution)/shard_map/ppermute | solution.py:546
  5.2 2.3 %constant_dynamic-slice_fusion.2 = bf16[2048,256]{1,0:T(8,128)(2,1)} fusion(bf16[2048,512]{1,0:T(8,128)(2,1)} %x.15, s32[]{:T(128)S(6)} %select_n.40), kind=kLoop, calls=%fused_computation.15 | loop fusion | bytes 2097156 | tf_op jit(solution)/shard_map/dynamic_slice | solution.py:467
  7.5 1.7 %collective-permute-start = (bf16[2048,256]{1,0:T(8,128)(2,1)}, bf16[2048,256]{1,0:T(8,128)(2,1)}, u32[]{:S(2)}, u32[]{:S(2)}) collective-permute-start(bf16[2048,256]{1,0:T(8,128)(2,1)} %constant_dynamic-slice_fusion.2), channel_id=1, source_target_pairs={{18,2},{9,25},{13,29},{1,17},{6,22},{10,26}} | collective-permute-start | bytes 3145736 | tf_op jit(solution)/shard_map/ppermute | solution.py:550
  9.2 0.1 dynamic_slice.27
  9.3 0.1 dynamic_slice.28
  9.3 1.0 multiply_reduce_fusion
  10.4 1.0 constant_dynamic-slice_fusion
  11.4 1.6 %collective-permute-start.6 = (bf16[2048,256]{1,0:T(8,128)(2,1)}, bf16[2048,256]{1,0:T(8,128)(2,1)}, u32[]{:S(2)}, u32[]{:S(2)}) collective-permute-start(bf16[2048,256]{1,0:T(8,128)(2,1)} %constant_dynamic-slice_fusion), channel_id=1, source_target_pairs={{1,0},{5,6},{9,8},{10,9},{14,15},{18,17},{19,18},{20,21},{22,23},{... | collective-permute-start | bytes 3145736 | tf_op jit(solution)/shard_map/ppermute | solution.py:546
  13.1 0.0 collective-permute-start.2
  13.1 0.6 collective-permute-start.11
  13.7 0.7 fusion.2.table
  14.4 6.3 %collective-permute-done.1.refs_1_ = bf16[2048,256]{1,0:T(8,128)(2,1)S(1)} collective-permute-done((bf16[2048,256]{1,0:T(8,128)(2,1)}, bf16[2048,256]{1,0:T(8,128)(2,1)S(1)}, u32[]{:S(2)}, u32[]{:S(2)}) %collective-permute-start.1) | collective-permute-done | bytes 1048608 | tf_op jit(solution)/shard_map/ppermute | solution.py:546
  20.7 0.0 collective-permute-done.refs_0_
  20.7 1.7 %relay.6 = bf16[2048,256]{1,0:T(8,128)(2,1)S(1)} custom-call(s32[30]{0:T(128)S(1)} %fusion.2.table, bf16[2048,512]{1,0:T(8,128)(2,1)S(1)} %copy-done, bf16[2048,256]{1,0:T(8,128)(2,1)} %collective-permute-done.refs_0_, bf16[2048,256]{1,0:T(8,128)(2,1)S(1)} %collective-permute-done.1.refs_1_), custom_call_target="tpu_custom_call" | custom-call | tf_op jit(solution)/shard_map/relay/pallas_call | solution.py:183
  22.4 0.0 collective-permute-done.2
  22.4 0.7 collective-permute-start.3
  23.1 0.0 collective-permute-done.6.refs_1_.refs_0_
  23.1 1.6 %relay.8 = bf16[2048,256]{1,0:T(8,128)(2,1)S(1)} custom-call(s32[30]{0:T(128)S(1)} %fusion.2.table, bf16[2048,512]{1,0:T(8,128)(2,1)S(1)} %copy-done, bf16[2048,256]{1,0:T(8,128)(2,1)} %collective-permute-done.refs_0_, bf16[2048,256]{1,0:T(8,128)(2,1)} %collective-permute-done.6.refs_1_.refs_0_), custom_call_target="tpu_custom_call" | custom-call | tf_op jit(solution)/shard_map/relay/pallas_call | solution.py:183
  24.8 1.3 collective-permute-start.7
  26.1 28.2 %collective-permute-start.4 = (f32[2048]{0:T(1024)S(1)}, f32[2048]{0:T(1024)S(1)}, u32[]{:S(2)}, u32[]{:S(2)}) collective-permute-start(f32[2048]{0:T(1024)S(1)} %add.42), channel_id=1, source_target_pairs={{0,2},{1,3},{2,0},{3,1},{4,6},{5,7},{6,4},{7,5},{8,10},{9,11},{10,... | collective-permute-start | bytes 24584 | tf_op jit(solution)/shard_map/ppermute | solution.py:512
  54.3 0.0 collective-permute-done.11.refs_1_
  54.3 1.6 %collective-permute-start.12 = (bf16[256,2048]{1,0:T(8,128)(2,1)}, bf16[256,2048]{1,0:T(8,128)(2,1)}, u32[]{:S(2)}, u32[]{:S(2)}) collective-permute-start(bf16[256,2048]{1,0:T(8,128)(2,1)} %collective-permute-done.11.refs_1_), channel_id=1, source_target_pairs={{0,28},{4,0},{8,4},{12,8},{16,12},{20,16},{24,20},{28,24},{1,29},{... | collective-permute-start | bytes 3145736 | tf_op jit(solution)/shard_map/ppermute | solution.py:491
  55.9 17.8 %collective-permute-done.4 = f32[2048]{0:T(1024)S(1)} collective-permute-done((f32[2048]{0:T(1024)S(1)}, f32[2048]{0:T(1024)S(1)}, u32[]{:S(2)}, u32[]{:S(2)}) %collective-permute-start.4) | collective-permute-done | bytes 8224 | tf_op jit(solution)/shard_map/ppermute | solution.py:512
  73.7 0.0 collective-permute-done.3.refs_1_.refs_3_
  73.7 0.7 collective-permute-start.5
  74.4 0.0 collective-permute-done.7.refs_0_.refs_2_
  74.4 0.0 copy-start.6
  74.4 1.3 collective-permute-start.8
  75.7 0.0 collective-permute-done.12.refs_2_
  75.7 0.1 collective-permute-start.13
  75.8 1.6 %relay.10 = bf16[2048,256]{1,0:T(8,128)(2,1)} custom-call(s32[30]{0:T(128)S(1)} %fusion.2.table, bf16[2048,512]{1,0:T(8,128)(2,1)S(1)} %copy-done, bf16[2048,256]{1,0:T(8,128)(2,1)S(1)} %collective-permute-done.7.refs_0_.refs_2_, bf16[2048,256]{1,0:T(8,128)(2,1)S(1)} %collective-permute-done.3.refs_1_.refs_3_), custom_call_target="tpu_custom_call" | custom-call | tf_op jit(solution)/shard_map/relay/pallas_call | solution.py:183
  77.4 1.6 %collective-permute-start.14 = (bf16[2048,256]{1,0:T(8,128)(2,1)}, bf16[2048,256]{1,0:T(8,128)(2,1)}, u32[]{:S(2)}, u32[]{:S(2)}) collective-permute-start(bf16[2048,256]{1,0:T(8,128)(2,1)} %relay.10), channel_id=1, source_target_pairs={{24,8},{28,12},{23,7},{27,11}} | collective-permute-start | bytes 3145736 | tf_op jit(solution)/shard_map/ppermute | solution.py:525
  79.1 0.0 collective-permute-done.5.refs_0_.refs_1_.refs_6_.refs_3_
  79.1 0.6 relay.7
  79.7 1.0 copy-done.10
  80.7 18.3 %collective-permute-done.8.refs_0_.refs_5_.refs_2_ = bf16[2048,256]{1,0:T(8,128)(2,1)S(1)} collective-permute-done((bf16[2048,256]{1,0:T(8,128)(2,1)S(1)}, bf16[2048,256]{1,0:T(8,128)(2,1)S(1)}, u32[]{:S(2)}, u32[]{:S(2)}) %collective-permute-start.8) | collective-permute-done | bytes 1048608 | tf_op jit(solution)/shard_map/ppermute | solution.py:546
  99.0 1.6 %relay.11 = bf16[2048,256]{1,0:T(8,128)(2,1)} custom-call(s32[30]{0:T(128)S(1)} %fusion.2.table, bf16[2048,512]{1,0:T(8,128)(2,1)S(1)} %copy-done, bf16[2048,256]{1,0:T(8,128)(2,1)S(1)} %collective-permute-done.8.refs_0_.refs_5_.refs_2_, bf16[2048,256]{1,0:T(8,128)(2,1)S(1)} %collective-permute-done.5.refs_0_.refs_1_.refs_6_.refs_3_), custom_call_target="tpu_custom_call" | custom-call | tf_op jit(solution)/shard_map/relay/pallas_call | solution.py:183
  100.7 1.0 copy-done.1
  101.6 1.6 %collective-permute-start.15 = (bf16[2048,256]{1,0:T(8,128)(2,1)}, bf16[2048,256]{1,0:T(8,128)(2,1)}, u32[]{:S(2)}, u32[]{:S(2)}) collective-permute-start(bf16[2048,256]{1,0:T(8,128)(2,1)} %relay.11), channel_id=1, source_target_pairs={{0,16},{19,3}} | collective-permute-start | bytes 3145736 | tf_op jit(solution)/shard_map/ppermute | solution.py:525
  103.2 0.1 fusion
  103.3 0.7 collective-permute-start.10
  104.1 1.2 copy-done.2
  105.3 0.6 relay.9
  105.9 1.3 collective-permute-start.9
  107.2 0.0 copy-done.13
  107.2 0.6 multiply_add_fusion
  107.8 0.0 collective-permute-done.13.refs_3_
  107.8 0.2 broadcast_in_dim.43.refs_5_
  108.0 0.2 broadcast_in_dim.42.refs_4_
  108.3 0.0 copy-start.7
  108.3 0.0 copy-start.9
  108.3 3.6 %window.1.refs_11_.refs_9_ = bf16[1024,2048]{1,0:T(8,128)(2,1)S(1)} custom-call(s32[30]{0:T(128)S(1)} %fusion.2.table, bf16[256,2048]{1,0:T(8,128)(2,1)S(1)} %copy-done.11, bf16[256,2048]{1,0:T(8,128)(2,1)} %collective-permute-done.11.refs_1_, bf16[256,2048]{1,0:T(8,128)(2,1)} %collective-permute-done.12.refs_2_, ...), custom_call_target="tpu_custom_call" | custom-call | flops 8388608 | bytes 8388608 | tf_op jit(solution)/shard_map/window/pallas_call | solution.py:221
  111.9 0.0 collective-permute-done.14.refs_4_
  111.9 0.0 collective-permute-done.15.refs_7_
  111.9 0.3 broadcast_in_dim.41.refs_10_.refs_8_
  112.2 11.4 %early.1.refs_10_ = f32[2048,2048]{1,0:T(8,128)S(1)} custom-call(s32[30]{0:T(128)S(1)} %fusion.2.table, bf16[2048,512]{1,0:T(8,128)(2,1)S(1)} %copy-done, bf16[2048,256]{1,0:T(8,128)(2,1)} %collective-permute-done.6.refs_1_.refs_0_, bf16[2048,256]{1,0:T(8,128)(2,1)S(1)} %copy-done.9, bf16[2048,256]{1,0:T(8,128)(2,1)S(1)} %copy-done.7, ...), custom_call_target="tpu_custom_call" | custom-call | flops 6442450944 | tf_op jit(solution)/shard_map/early/pallas_call | solution.py:282
  123.6 0.0 collective-permute-done.10.refs_5_
  123.6 7.0 %collective-permute-done.9.refs_4_ = bf16[2048,256]{1,0:T(8,128)(2,1)S(1)} collective-permute-done((bf16[2048,256]{1,0:T(8,128)(2,1)S(1)}, bf16[2048,256]{1,0:T(8,128)(2,1)S(1)}, u32[]{:S(2)}, u32[]{:S(2)}) %collective-permute-start.9) | collective-permute-done | bytes 1048608 | tf_op jit(solution)/shard_map/ppermute | solution.py:546
  130.7 5.7 %last.1 = bf16[2048,2048]{1,0:T(8,128)(2,1)} custom-call(s32[30]{0:T(128)S(1)} %fusion.2.table, bf16[2048,512]{1,0:T(8,128)(2,1)S(1)} %copy-done, bf16[2048,256]{1,0:T(8,128)(2,1)S(1)} %copy-done.7, bf16[2048,256]{1,0:T(8,128)(2,1)S(1)} %copy-done.5, bf16[2048,256]{1,0:T(8,128)(2,1)S(1)} %copy-done.3, ...), custom_call_target="tpu_custom_call" | custom-call | flops 2147483648 | bytes 8388608 | tf_op jit(solution)/shard_map/last/pallas_call | solution.py:326
  (25 shorter events, 0.1 us)
Async XLA Ops:
  0.6 8.7 %copy-start = (bf16[2048,512]{1,0:T(8,128)(2,1)S(1)}, bf16[2048,512]{1,0:T(8,128)(2,1)}, u32[]{:S(2)}) copy-start(bf16[2048,512]{1,0:T(8,128)(2,1)} %x.15) | copy-start | bytes 6291460
  0.6 8.5 %copy-start.12 = (s32[2048]{0:T(1024)S(1)}, s32[2048]{0:T(1024)}, u32[]{:S(2)}) copy-start(s32[2048]{0:T(1024)} %param.11) | copy-start | bytes 24580
  0.7 8.5 %copy-start.15 = (f32[2048]{0:T(1024)S(1)}, f32[2048]{0:T(1024)}, u32[]{:S(2)}) copy-start(f32[2048]{0:T(1024)} %param.10) | copy-start | bytes 24580
  0.7 8.5 %copy-start.14 = (f32[2048]{0:T(1024)S(1)}, f32[2048]{0:T(1024)}, u32[]{:S(2)}) copy-start(f32[2048]{0:T(1024)} %param.9) | copy-start | bytes 24580
  3.1 17.6 %collective-permute-start.1 = (bf16[2048,256]{1,0:T(8,128)(2,1)}, bf16[2048,256]{1,0:T(8,128)(2,1)S(1)}, u32[]{:S(2)}, u32[]{:S(2)}) collective-permute-start(bf16[2048,256]{1,0:T(8,128)(2,1)} %constant_dynamic-slice_fusion.1), channel_id=1, source_target_pairs={{0,1},{1,2},{5,4},{9,10},{10,11},{14,13},{18,19},{22,21},{23,22},{... | collective-permute-start | bytes 3145736 | tf_op jit(solution)/shard_map/ppermute | solution.py:546
  7.5 13.2 %collective-permute-start = (bf16[2048,256]{1,0:T(8,128)(2,1)}, bf16[2048,256]{1,0:T(8,128)(2,1)}, u32[]{:S(2)}, u32[]{:S(2)}) collective-permute-start(bf16[2048,256]{1,0:T(8,128)(2,1)} %constant_dynamic-slice_fusion.2), channel_id=1, source_target_pairs={{18,2},{9,25},{13,29},{1,17},{6,22},{10,26}} | collective-permute-start | bytes 3145736 | tf_op jit(solution)/shard_map/ppermute | solution.py:550
  11.4 11.7 %collective-permute-start.6 = (bf16[2048,256]{1,0:T(8,128)(2,1)}, bf16[2048,256]{1,0:T(8,128)(2,1)}, u32[]{:S(2)}, u32[]{:S(2)}) collective-permute-start(bf16[2048,256]{1,0:T(8,128)(2,1)} %constant_dynamic-slice_fusion), channel_id=1, source_target_pairs={{1,0},{5,6},{9,8},{10,9},{14,15},{18,17},{19,18},{20,21},{22,23},{... | collective-permute-start | bytes 3145736 | tf_op jit(solution)/shard_map/ppermute | solution.py:546
  13.1 9.3 %collective-permute-start.2 = (f32[2048]{0:T(1024)S(1)}, f32[2048]{0:T(1024)S(1)}, u32[]{:S(2)}, u32[]{:S(2)}) collective-permute-start(f32[2048]{0:T(1024)S(1)} %multiply_reduce_fusion), channel_id=1, source_target_pairs={{0,1},{1,0},{2,3},{3,2},{4,5},{5,4},{6,7},{7,6},{8,9},{9,8},{10,11... | collective-permute-start | bytes 24584 | tf_op jit(solution)/shard_map/ppermute | solution.py:512
  13.1 41.2 %collective-permute-start.11 = (bf16[256,2048]{1,0:T(8,128)(2,1)}, bf16[256,2048]{1,0:T(8,128)(2,1)}, u32[]{:S(2)}, u32[]{:S(2)}) collective-permute-start(bf16[256,2048]{1,0:T(8,128)(2,1)} %refs_0_.1), channel_id=1, source_target_pairs={{0,28},{4,0},{8,4},{12,8},{16,12},{20,16},{24,20},{28,24},{1,29},{... | collective-permute-start | bytes 3145736 | tf_op jit(solution)/shard_map/ppermute | solution.py:491
  20.7 4.1 %copy-start.8 = (bf16[2048,256]{1,0:T(8,128)(2,1)}, bf16[2048,256]{1,0:T(8,128)(2,1)S(1)}, u32[]{:S(2)}) copy-start(bf16[2048,256]{1,0:T(8,128)(2,1)S(1)} %collective-permute-done.1.refs_1_) | copy-start | bytes 3145732
  22.4 51.3 %collective-permute-start.3 = (bf16[2048,256]{1,0:T(8,128)(2,1)S(1)}, bf16[2048,256]{1,0:T(8,128)(2,1)S(1)}, u32[]{:S(2)}, u32[]{:S(2)}) collective-permute-start(bf16[2048,256]{1,0:T(8,128)(2,1)S(1)} %relay.6), channel_id=1, source_target_pairs={{0,1},{1,2},{2,3},{5,4},{6,5},{9,10},{10,11},{13,12},{14,13},{15,1... | collective-permute-start | bytes 3145736 | tf_op jit(solution)/shard_map/ppermute | solution.py:546
  24.8 49.6 %collective-permute-start.7 = (bf16[2048,256]{1,0:T(8,128)(2,1)S(1)}, bf16[2048,256]{1,0:T(8,128)(2,1)S(1)}, u32[]{:S(2)}, u32[]{:S(2)}) collective-permute-start(bf16[2048,256]{1,0:T(8,128)(2,1)S(1)} %relay.8), channel_id=1, source_target_pairs={{1,0},{2,1},{4,5},{5,6},{6,7},{9,8},{10,9},{13,14},{14,15},{17,16}... | collective-permute-start | bytes 3145736 | tf_op jit(solution)/shard_map/ppermute | solution.py:546
  26.1 47.6 %collective-permute-start.4 = (f32[2048]{0:T(1024)S(1)}, f32[2048]{0:T(1024)S(1)}, u32[]{:S(2)}, u32[]{:S(2)}) collective-permute-start(f32[2048]{0:T(1024)S(1)} %add.42), channel_id=1, source_target_pairs={{0,2},{1,3},{2,0},{3,1},{4,6},{5,7},{6,4},{7,5},{8,10},{9,11},{10,... | collective-permute-start | bytes 24584 | tf_op jit(solution)/shard_map/ppermute | solution.py:512
  54.3 21.4 %collective-permute-start.12 = (bf16[256,2048]{1,0:T(8,128)(2,1)}, bf16[256,2048]{1,0:T(8,128)(2,1)}, u32[]{:S(2)}, u32[]{:S(2)}) collective-permute-start(bf16[256,2048]{1,0:T(8,128)(2,1)} %collective-permute-done.11.refs_1_), channel_id=1, source_target_pairs={{0,28},{4,0},{8,4},{12,8},{16,12},{20,16},{24,20},{28,24},{1,29},{... | collective-permute-start | bytes 3145736 | tf_op jit(solution)/shard_map/ppermute | solution.py:491
  73.7 6.0 %copy-start.4 = (bf16[2048,256]{1,0:T(8,128)(2,1)}, bf16[2048,256]{1,0:T(8,128)(2,1)S(1)}, u32[]{:S(2)}) copy-start(bf16[2048,256]{1,0:T(8,128)(2,1)S(1)} %collective-permute-done.3.refs_1_.refs_3_) | copy-start | bytes 3145732
  73.7 5.4 %collective-permute-start.5 = (bf16[2048,256]{1,0:T(8,128)(2,1)S(1)}, bf16[2048,256]{1,0:T(8,128)(2,1)S(1)}, u32[]{:S(2)}, u32[]{:S(2)}) collective-permute-start(bf16[2048,256]{1,0:T(8,128)(2,1)S(1)} %collective-permute-done.3.refs_1_.refs_3_), channel_id=1, source_target_pairs={{1,2},{2,3},{5,4},{10,11},{13,12},{14,13},{18,19},{21,20},{22,21},... | collective-permute-start | bytes 3145736 | tf_op jit(solution)/shard_map/ppermute | solution.py:546
  74.4 5.3 %copy-start.6 = (bf16[2048,256]{1,0:T(8,128)(2,1)}, bf16[2048,256]{1,0:T(8,128)(2,1)S(1)}, u32[]{:S(2)}) copy-start(bf16[2048,256]{1,0:T(8,128)(2,1)S(1)} %collective-permute-done.7.refs_0_.refs_2_) | copy-start | bytes 3145732
  74.4 24.6 %collective-permute-start.8 = (bf16[2048,256]{1,0:T(8,128)(2,1)S(1)}, bf16[2048,256]{1,0:T(8,128)(2,1)S(1)}, u32[]{:S(2)}, u32[]{:S(2)}) collective-permute-start(bf16[2048,256]{1,0:T(8,128)(2,1)S(1)} %collective-permute-done.7.refs_0_.refs_2_), channel_id=1, source_target_pairs={{1,0},{5,6},{6,7},{9,8},{14,15},{17,16},{18,17},{22,23},{25,24},{2... | collective-permute-start | bytes 3145736 | tf_op jit(solution)/shard_map/ppermute | solution.py:546
  75.7 32.1 %collective-permute-start.13 = (bf16[256,2048]{1,0:T(8,128)(2,1)}, bf16[256,2048]{1,0:T(8,128)(2,1)}, u32[]{:S(2)}, u32[]{:S(2)}) collective-permute-start(bf16[256,2048]{1,0:T(8,128)(2,1)} %collective-permute-done.12.refs_2_), channel_id=1, source_target_pairs={{0,28},{4,0},{8,4},{12,8},{16,12},{20,16},{24,20},{28,24},{1,29},{... | collective-permute-start | bytes 3145736 | tf_op jit(solution)/shard_map/ppermute | solution.py:491
  77.4 34.4 %collective-permute-start.14 = (bf16[2048,256]{1,0:T(8,128)(2,1)}, bf16[2048,256]{1,0:T(8,128)(2,1)}, u32[]{:S(2)}, u32[]{:S(2)}) collective-permute-start(bf16[2048,256]{1,0:T(8,128)(2,1)} %relay.10), channel_id=1, source_target_pairs={{24,8},{28,12},{23,7},{27,11}} | collective-permute-start | bytes 3145736 | tf_op jit(solution)/shard_map/ppermute | solution.py:525
  79.7 1.0 copy-start.10
  80.7 26.5 %copy-start.13 = (s32[2048]{0:T(1024)S(1)}, s32[2048]{0:T(1024)}, u32[]{:S(2)}) copy-start(s32[2048]{0:T(1024)} %param.12) | copy-start | bytes 24580
  100.6 1.0 copy-start.1
  101.6 10.2 %collective-permute-start.15 = (bf16[2048,256]{1,0:T(8,128)(2,1)}, bf16[2048,256]{1,0:T(8,128)(2,1)}, u32[]{:S(2)}, u32[]{:S(2)}) collective-permute-start(bf16[2048,256]{1,0:T(8,128)(2,1)} %relay.11), channel_id=1, source_target_pairs={{0,16},{19,3}} | collective-permute-start | bytes 3145736 | tf_op jit(solution)/shard_map/ppermute | solution.py:525
  103.3 20.3 %collective-permute-start.10 = (bf16[2048,256]{1,0:T(8,128)(2,1)}, bf16[2048,256]{1,0:T(8,128)(2,1)S(1)}, u32[]{:S(2)}, u32[]{:S(2)}) collective-permute-start(bf16[2048,256]{1,0:T(8,128)(2,1)} %copy-done.10), channel_id=1, source_target_pairs={{1,2},{2,3},{13,12},{21,20},{26,27}} | collective-permute-start | bytes 3145736 | tf_op jit(solution)/shard_map/ppermute | solution.py:546
  104.1 1.2 copy-start.2
  105.3 3.0 %copy-start.11 = (bf16[256,2048]{1,0:T(8,128)(2,1)S(1)}, bf16[256,2048]{1,0:T(8,128)(2,1)}, u32[]{:S(2)}) copy-start(bf16[256,2048]{1,0:T(8,128)(2,1)} %refs_0_.1) | copy-start | bytes 3145732
  105.9 24.8 %collective-permute-start.9 = (bf16[2048,256]{1,0:T(8,128)(2,1)S(1)}, bf16[2048,256]{1,0:T(8,128)(2,1)S(1)}, u32[]{:S(2)}, u32[]{:S(2)}) collective-permute-start(bf16[2048,256]{1,0:T(8,128)(2,1)S(1)} %relay.9), channel_id=1, source_target_pairs={{6,7},{17,16},{18,17},{25,24},{30,31}} | collective-permute-start | bytes 3145736 | tf_op jit(solution)/shard_map/ppermute | solution.py:546
  108.2 4.0 %copy-start.3 = (bf16[2048,256]{1,0:T(8,128)(2,1)S(1)}, bf16[2048,256]{1,0:T(8,128)(2,1)}, u32[]{:S(2)}) copy-start(bf16[2048,256]{1,0:T(8,128)(2,1)} %copy-done.1) | copy-start | bytes 3145732
  108.3 4.0 %copy-start.5 = (bf16[2048,256]{1,0:T(8,128)(2,1)S(1)}, bf16[2048,256]{1,0:T(8,128)(2,1)}, u32[]{:S(2)}) copy-start(bf16[2048,256]{1,0:T(8,128)(2,1)} %copy-done.4) | copy-start | bytes 3145732
  108.3 4.0 %copy-start.7 = (bf16[2048,256]{1,0:T(8,128)(2,1)S(1)}, bf16[2048,256]{1,0:T(8,128)(2,1)}, u32[]{:S(2)}) copy-start(bf16[2048,256]{1,0:T(8,128)(2,1)} %copy-done.6) | copy-start | bytes 3145732
  108.3 4.0 %copy-start.9 = (bf16[2048,256]{1,0:T(8,128)(2,1)S(1)}, bf16[2048,256]{1,0:T(8,128)(2,1)}, u32[]{:S(2)}) copy-start(bf16[2048,256]{1,0:T(8,128)(2,1)} %copy-done.8) | copy-start | bytes 3145732

commit v11 on v10

--- a/solution.py
+++ b/solution.py
@@ -101,9 +101,8 @@
             theirs = line_slots(self.items[other] + visitors, [])
             score = (
                 max(max(mine[0], default=0), max(theirs[0], default=0)),
-                abs(len(mine[0]) - len(theirs[0])),
+                len(gone),
                 max([slot for slot, i in theirs[0].items() if i.home is not None], default=0),
-                len(gone),
             )
             if best is None or score < best[0]:
                 best = score, gone, mine, theirs
@@ -539,10 +538,6 @@
                 held = own_chunk(own_of[key])
             else:
                 held = crossed[next(k for k in kinds_of[key] if k is not None)]
-            if phase == 1 and t in (2, 3):
-                held, squares = sum_beside(held, squares)
-            if phase == 1 and t - 1 in returns:
-                held, table = lax.optimization_barrier((held, table))
             buffers[key] = lax.ppermute(held, both, pairs_of[key])
         if key == (0, 1):
             for k, crossing in enumerate(crossings):
@@ -552,8 +547,10 @@
             bring_back(t - 1)
     bring_back(rounds)
     zy = standardized_window(rank_at, table, window, wide(window_factor), wide(window_twice), male_cols[None, :])
+    zy, squares = sum_beside(zy, squares)
     shared = window_factor[None, :], window_twice[None, :], male_wide, zy
     total = early_product(source_at[0], candidates[0], table, x, [buffers[k] for k in used[0]], *shared)
+    total, squares = sum_beside(total, squares)
     relation = last_product(source_at[1], candidates[1][0], table, x, [buffers[k] for k in used[1]], *shared, total)
     for bit in bits:
         squares = squares + lax.ppermute(squares, "col", [(i, i ^ bit) for i in range(cols)])

time: 137 us -> 120 us (0.88)
  the two profiles are of different devices: /device:TPU:31 before, /device:TPU:0 now
where the time goes in v11:
time: 120 us; the launch traced here: 119 us
  waiting for transfers between devices  43.6 us (36%)
  starting transfers between devices  33.2 us (28%)
  Pallas kernels  30.9 us (26%)
  local copies, waits for them, and re-layouts  8.58 us (7%)
  other arithmetic  1.73 us (1%)
    ppermute x8, waiting for transfers between devices, local(): buffers[key] = lax.ppermute(held, both, pairs_of[key])  43.6 us
    ppermute x8, starting transfers between devices, local(): buffers[key] = lax.ppermute(held, both, pairs_of[key])  21.8 us
    pallas_call x1, Pallas kernels, early_product(): pl.pallas_call(functools.partial(early_kernel, at, candidates, len(buffer...  11.1 us
    pallas_call x7, Pallas kernels, relay(): pl.pallas_call(functools.partial(relay_kernel, at), out_shape=pltpu.VMEM(...  9.5 us
    pallas_call x1, Pallas kernels, last_product(): pl.pallas_call(functools.partial(last_kernel, at, candidates, scale, len(...  6.76 us
    ppermute x1, starting transfers between devices, bring_back(): buffers['back', t] = lax.ppermute(held, both, pairs)  6.22 us
    dynamic_slice x3, local copies, waits for them, and re-layouts, own_chunk(): lax.dynamic_slice(x, (piece * piece_rows, group * group_size), (piece_row...  5.75 us
    pallas_call x1, Pallas kernels, standardized_window(): pl.pallas_call(functools.partial(window_kernel, at), out_shape=pltpu.VMEM...  3.56 us
  transfers between devices with their start and end apart: 15, of which 5 were waited for; matrix products, arithmetic and copies ran while one was open for 6% of the time, Pallas kernels for 20%

profile of v11, /device:TPU:0, one launch (start us, length us, event | category | flops | bytes accessed | tf_op | source)
XLA Modules:
  0.0 119.0 jit_solution(8221874165225300657)
XLA Ops:
  0.6 0.0 copy-start
  0.6 0.0 copy-start.13
  0.7 0.0 copy-start.12
  0.7 0.0 copy-start.10
  0.7 2.4 %constant_dynamic-slice_fusion = bf16[2048,256]{1,0:T(8,128)(2,1)} fusion(bf16[2048,512]{1,0:T(8,128)(2,1)} %x.17, s32[]{:T(128)S(6)} %select_n.38), kind=kLoop, calls=%fused_computation.13 | loop fusion | bytes 2097156 | tf_op jit(solution)/shard_map/dynamic_slice | solution.py:466
  3.1 5.0 %collective-permute-start.3 = (bf16[2048,256]{1,0:T(8,128)(2,1)}, bf16[2048,256]{1,0:T(8,128)(2,1)S(1)}, u32[]{:S(2)}, u32[]{:S(2)}) collective-permute-start(bf16[2048,256]{1,0:T(8,128)(2,1)} %constant_dynamic-slice_fusion), channel_id=1, source_target_pairs={{0,1},{1,2},{5,4},{10,11},{13,12},{14,13},{18,19},{22,21},{23,22},... | collective-permute-start | bytes 3145736 | tf_op jit(solution)/shard_map/ppermute | solution.py:541
  8.1 2.3 %dynamic_slice.32 = bf16[2048,256]{1,0:T(8,128)(2,1)} slice(bf16[2048,512]{1,0:T(8,128)(2,1)} %x.17), slice={[0:2048], [256:512]} | slice | bytes 2097152 | tf_op jit(solution)/shard_map/dynamic_slice | solution.py:466
  10.3 1.6 %collective-permute-start = (bf16[2048,256]{1,0:T(8,128)(2,1)}, bf16[2048,256]{1,0:T(8,128)(2,1)}, u32[]{:S(2)}, u32[]{:S(2)}) collective-permute-start(bf16[2048,256]{1,0:T(8,128)(2,1)} %dynamic_slice.32), channel_id=1, source_target_pairs={{18,2},{1,17}} | collective-permute-start | bytes 3145736 | tf_op jit(solution)/shard_map/ppermute | solution.py:545
  12.0 0.0 copy-done.13
  12.0 0.0 copy-done.12
  12.0 0.1 dynamic_slice.26
  12.1 0.1 dynamic_slice.27
  12.1 0.0 copy-done.10
  12.1 0.0 copy-done
  12.1 1.0 multiply_reduce_fusion
  13.2 1.1 constant_dynamic-slice_fusion.1
  14.3 1.3 %collective-permute-start.1 = (bf16[2048,256]{1,0:T(8,128)(2,1)}, bf16[2048,256]{1,0:T(8,128)(2,1)}, u32[]{:S(2)}, u32[]{:S(2)}) collective-permute-start(bf16[2048,256]{1,0:T(8,128)(2,1)} %constant_dynamic-slice_fusion.1), channel_id=1, source_target_pairs={{1,0},{5,6},{6,7},{9,8},{14,15},{18,17},{19,18},{20,21},{22,23},{2... | collective-permute-start | bytes 3145736 | tf_op jit(solution)/shard_map/ppermute | solution.py:541
  15.6 3.4 %collective-permute-start.9 = (bf16[256,2048]{1,0:T(8,128)(2,1)}, bf16[256,2048]{1,0:T(8,128)(2,1)}, u32[]{:S(2)}, u32[]{:S(2)}) collective-permute-start(bf16[256,2048]{1,0:T(8,128)(2,1)} %refs_0_.1), channel_id=1, source_target_pairs={{0,28},{4,0},{8,4},{12,8},{16,12},{20,16},{24,20},{28,24},{1,29},{... | collective-permute-start | bytes 3145736 | tf_op jit(solution)/shard_map/ppermute | solution.py:490
  19.0 0.7 fusion.2.table
  19.7 1.0 collective-permute-done.3.refs_1_
  20.6 0.0 collective-permute-done.refs_0_
  20.6 1.7 %relay.8 = bf16[2048,256]{1,0:T(8,128)(2,1)S(1)} custom-call(s32[33]{0:T(128)S(1)} %fusion.2.table, bf16[2048,512]{1,0:T(8,128)(2,1)S(1)} %copy-done, bf16[2048,256]{1,0:T(8,128)(2,1)} %collective-permute-done.refs_0_, bf16[2048,256]{1,0:T(8,128)(2,1)S(1)} %collective-permute-done.3.refs_1_), custom_call_target="tpu_custom_call" | custom-call | tf_op jit(solution)/shard_map/relay/pallas_call | solution.py:182
  22.3 8.9 %collective-permute-start.4 = (bf16[2048,256]{1,0:T(8,128)(2,1)S(1)}, bf16[2048,256]{1,0:T(8,128)(2,1)S(1)}, u32[]{:S(2)}, u32[]{:S(2)}) collective-permute-start(bf16[2048,256]{1,0:T(8,128)(2,1)S(1)} %relay.8), channel_id=1, source_target_pairs={{0,1},{1,2},{2,3},{5,4},{6,5},{9,10},{10,11},{13,12},{14,13},{15,1... | collective-permute-start | bytes 3145736 | tf_op jit(solution)/shard_map/ppermute | solution.py:541
  31.3 5.6 %collective-permute-done.1.refs_1_.refs_0_ = bf16[2048,256]{1,0:T(8,128)(2,1)} collective-permute-done((bf16[2048,256]{1,0:T(8,128)(2,1)}, bf16[2048,256]{1,0:T(8,128)(2,1)}, u32[]{:S(2)}, u32[]{:S(2)}) %collective-permute-start.1) | collective-permute-done | bytes 1048608 | tf_op jit(solution)/shard_map/ppermute | solution.py:541
  36.8 1.6 %relay.7 = bf16[2048,256]{1,0:T(8,128)(2,1)S(1)} custom-call(s32[33]{0:T(128)S(1)} %fusion.2.table, bf16[2048,512]{1,0:T(8,128)(2,1)S(1)} %copy-done, bf16[2048,256]{1,0:T(8,128)(2,1)} %collective-permute-done.refs_0_, bf16[2048,256]{1,0:T(8,128)(2,1)} %collective-permute-done.1.refs_1_.refs_0_), custom_call_target="tpu_custom_call" | custom-call | tf_op jit(solution)/shard_map/relay/pallas_call | solution.py:182
  38.5 0.0 copy-done.7
  38.5 1.3 %collective-permute-start.2 = (bf16[2048,256]{1,0:T(8,128)(2,1)S(1)}, bf16[2048,256]{1,0:T(8,128)(2,1)S(1)}, u32[]{:S(2)}, u32[]{:S(2)}) collective-permute-start(bf16[2048,256]{1,0:T(8,128)(2,1)S(1)} %relay.7), channel_id=1, source_target_pairs={{1,0},{2,1},{4,5},{5,6},{6,7},{9,8},{10,9},{13,14},{14,15},{17,16}... | collective-permute-start | bytes 3145736 | tf_op jit(solution)/shard_map/ppermute | solution.py:541
  39.8 0.0 collective-permute-done.9.refs_1_
  39.8 0.1 collective-permute-start.10
  39.9 9.8 %collective-permute-done.4.refs_0_.refs_3_.refs_1_ = bf16[2048,256]{1,0:T(8,128)(2,1)S(1)} collective-permute-done((bf16[2048,256]{1,0:T(8,128)(2,1)S(1)}, bf16[2048,256]{1,0:T(8,128)(2,1)S(1)}, u32[]{:S(2)}, u32[]{:S(2)}) %collective-permute-start.4) | collective-permute-done | bytes 1048608 | tf_op jit(solution)/shard_map/ppermute | solution.py:541
  49.7 0.6 relay.10
  50.3 0.7 collective-permute-start.6
  51.1 11.9 %collective-permute-done.2.refs_0_.refs_2_ = bf16[2048,256]{1,0:T(8,128)(2,1)S(1)} collective-permute-done((bf16[2048,256]{1,0:T(8,128)(2,1)S(1)}, bf16[2048,256]{1,0:T(8,128)(2,1)S(1)}, u32[]{:S(2)}, u32[]{:S(2)}) %collective-permute-start.2) | collective-permute-done | bytes 1048608 | tf_op jit(solution)/shard_map/ppermute | solution.py:541
  63.0 0.0 copy-done.3
  63.0 0.6 relay.9
  63.6 1.3 %collective-permute-start.5 = (bf16[2048,256]{1,0:T(8,128)(2,1)S(1)}, bf16[2048,256]{1,0:T(8,128)(2,1)S(1)}, u32[]{:S(2)}, u32[]{:S(2)}) collective-permute-start(bf16[2048,256]{1,0:T(8,128)(2,1)S(1)} %relay.9), channel_id=1, source_target_pairs={{1,0},{5,6},{6,7},{9,8},{10,9},{14,15},{17,16},{18,17},{22,23},{25... | collective-permute-start | bytes 3145736 | tf_op jit(solution)/shard_map/ppermute | solution.py:541
  64.9 0.0 collective-permute-done.10.refs_2_
  64.9 0.1 collective-permute-start.11
  65.0 0.0 collective-permute-done.6.refs_0_.refs_1_.refs_5_.refs_3_
  65.0 15.3 %collective-permute-done.5.refs_0_.refs_4_.refs_2_ = bf16[2048,256]{1,0:T(8,128)(2,1)S(1)} collective-permute-done((bf16[2048,256]{1,0:T(8,128)(2,1)S(1)}, bf16[2048,256]{1,0:T(8,128)(2,1)S(1)}, u32[]{:S(2)}, u32[]{:S(2)}) %collective-permute-start.5) | collective-permute-done | bytes 1048608 | tf_op jit(solution)/shard_map/ppermute | solution.py:541
  80.3 1.6 %relay.13 = bf16[2048,256]{1,0:T(8,128)(2,1)} custom-call(s32[33]{0:T(128)S(1)} %fusion.2.table, bf16[2048,512]{1,0:T(8,128)(2,1)S(1)} %copy-done, bf16[2048,256]{1,0:T(8,128)(2,1)S(1)} %collective-permute-done.5.refs_0_.refs_4_.refs_2_, bf16[2048,256]{1,0:T(8,128)(2,1)S(1)} %collective-permute-done.6.refs_0_.refs_1_.refs_5_.refs_3_), custom_call_target="tpu_custom_call" | custom-call | tf_op jit(solution)/shard_map/relay/pallas_call | solution.py:182
  81.9 6.2 %collective-permute-start.13 = (bf16[2048,256]{1,0:T(8,128)(2,1)}, bf16[2048,256]{1,0:T(8,128)(2,1)}, u32[]{:S(2)}, u32[]{:S(2)}) collective-permute-start(bf16[2048,256]{1,0:T(8,128)(2,1)} %relay.13), channel_id=1, source_target_pairs={{0,16},{19,3}} | collective-permute-start | bytes 3145736 | tf_op jit(solution)/shard_map/ppermute | solution.py:524
  88.2 0.0 collective-permute-start.12
  88.2 1.6 %relay.12 = bf16[2048,256]{1,0:T(8,128)(2,1)} custom-call(s32[33]{0:T(128)S(1)} %fusion.2.table, bf16[2048,512]{1,0:T(8,128)(2,1)S(1)} %copy-done, bf16[2048,256]{1,0:T(8,128)(2,1)S(1)} %collective-permute-done.6.refs_0_.refs_1_.refs_5_.refs_3_), custom_call_target="tpu_custom_call" | custom-call | tf_op jit(solution)/shard_map/relay/pallas_call | solution.py:182
  89.8 1.7 %collective-permute-start.8 = (bf16[2048,256]{1,0:T(8,128)(2,1)}, bf16[2048,256]{1,0:T(8,128)(2,1)}, u32[]{:S(2)}, u32[]{:S(2)}) collective-permute-start(bf16[2048,256]{1,0:T(8,128)(2,1)} %relay.12), channel_id=1, source_target_pairs={{1,2},{2,3},{10,11},{13,12},{21,20},{26,27}} | collective-permute-start | bytes 3145736 | tf_op jit(solution)/shard_map/ppermute | solution.py:541
  91.4 1.7 %relay.11 = bf16[2048,256]{1,0:T(8,128)(2,1)} custom-call(s32[33]{0:T(128)S(1)} %fusion.2.table, bf16[2048,512]{1,0:T(8,128)(2,1)S(1)} %copy-done, bf16[2048,256]{1,0:T(8,128)(2,1)S(1)} %collective-permute-done.5.refs_0_.refs_4_.refs_2_), custom_call_target="tpu_custom_call" | custom-call | tf_op jit(solution)/shard_map/relay/pallas_call | solution.py:182
  93.1 1.6 %collective-permute-start.7 = (bf16[2048,256]{1,0:T(8,128)(2,1)}, bf16[2048,256]{1,0:T(8,128)(2,1)}, u32[]{:S(2)}, u32[]{:S(2)}) collective-permute-start(bf16[2048,256]{1,0:T(8,128)(2,1)} %relay.11), channel_id=1, source_target_pairs={{6,7},{9,8},{17,16},{18,17},{25,24},{30,31}} | collective-permute-start | bytes 3145736 | tf_op jit(solution)/shard_map/ppermute | solution.py:541
  94.8 0.1 fusion
  94.8 0.0 collective-permute-done.11.refs_3_
  94.8 0.2 broadcast_in_dim.42.refs_4_
  95.0 0.2 broadcast_in_dim.43.refs_5_
  95.2 0.0 copy-start.9
  95.3 1.2 %copy-done.9 = bf16[256,2048]{1,0:T(8,128)(2,1)S(1)} copy-done((bf16[256,2048]{1,0:T(8,128)(2,1)S(1)}, bf16[256,2048]{1,0:T(8,128)(2,1)}, u32[]{:S(2)}) %copy-start.9) | copy-done | bytes 1048600
  96.5 3.6 %window.1.refs_10_.refs_9_ = bf16[1024,2048]{1,0:T(8,128)(2,1)S(1)} custom-call(s32[33]{0:T(128)S(1)} %fusion.2.table, bf16[256,2048]{1,0:T(8,128)(2,1)S(1)} %copy-done.9, bf16[256,2048]{1,0:T(8,128)(2,1)} %collective-permute-done.9.refs_1_, bf16[256,2048]{1,0:T(8,128)(2,1)} %collective-permute-done.10.refs_2_, ...), custom_call_target="tpu_custom_call" | custom-call | flops 8388608 | bytes 8388608 | tf_op jit(solution)/shard_map/window/pallas_call | solution.py:220
  100.1 0.0 collective-permute-done.12
  100.1 0.1 collective-permute-start.14
  100.2 0.0 collective-permute-done.13.refs_6_
  100.2 0.3 broadcast_in_dim.41.refs_9_.refs_8_
  100.5 11.1 %early.1.refs_10_ = f32[2048,2048]{1,0:T(8,128)S(1)} custom-call(s32[33]{0:T(128)S(1)} %fusion.2.table, bf16[2048,512]{1,0:T(8,128)(2,1)S(1)} %copy-done, bf16[2048,256]{1,0:T(8,128)(2,1)} %collective-permute-done.1.refs_1_.refs_0_, bf16[2048,256]{1,0:T(8,128)(2,1)S(1)} %copy-done.8, bf16[2048,256]{1,0:T(8,128)(2,1)S(1)} %copy-done.6, ...), custom_call_target="tpu_custom_call" | custom-call | flops 6442450944 | tf_op jit(solution)/shard_map/early/pallas_call | solution.py:281
  111.6 0.0 collective-permute-done.14
  111.6 0.6 multiply_add_fusion
  112.2 0.0 collective-permute-done.8.refs_5_
  112.3 0.0 collective-permute-done.7.refs_4_
  112.3 6.8 %last.1 = bf16[2048,2048]{1,0:T(8,128)(2,1)} custom-call(s32[33]{0:T(128)S(1)} %fusion.2.table, bf16[2048,512]{1,0:T(8,128)(2,1)S(1)} %copy-done, bf16[2048,256]{1,0:T(8,128)(2,1)S(1)} %copy-done.6, bf16[2048,256]{1,0:T(8,128)(2,1)S(1)} %copy-done.4, bf16[2048,256]{1,0:T(8,128)(2,1)S(1)} %copy-done.2, ...), custom_call_target="tpu_custom_call" | custom-call | flops 2147483648 | bytes 8388608 | tf_op jit(solution)/shard_map/last/pallas_call | solution.py:325
  (20 shorter events, 0.0 us)
Async XLA Ops:
  0.6 11.5 %copy-start = (bf16[2048,512]{1,0:T(8,128)(2,1)S(1)}, bf16[2048,512]{1,0:T(8,128)(2,1)}, u32[]{:S(2)}) copy-start(bf16[2048,512]{1,0:T(8,128)(2,1)} %x.17) | copy-start | bytes 6291460
  0.6 11.3 %copy-start.13 = (f32[2048]{0:T(1024)S(1)}, f32[2048]{0:T(1024)}, u32[]{:S(2)}) copy-start(f32[2048]{0:T(1024)} %param.10) | copy-start | bytes 24580
  0.7 11.3 %copy-start.12 = (f32[2048]{0:T(1024)S(1)}, f32[2048]{0:T(1024)}, u32[]{:S(2)}) copy-start(f32[2048]{0:T(1024)} %param.9) | copy-start | bytes 24580
  0.7 11.5 %copy-start.10 = (s32[2048]{0:T(1024)S(1)}, s32[2048]{0:T(1024)}, u32[]{:S(2)}) copy-start(s32[2048]{0:T(1024)} %param.11) | copy-start | bytes 24580
  3.1 17.5 %collective-permute-start.3 = (bf16[2048,256]{1,0:T(8,128)(2,1)}, bf16[2048,256]{1,0:T(8,128)(2,1)S(1)}, u32[]{:S(2)}, u32[]{:S(2)}) collective-permute-start(bf16[2048,256]{1,0:T(8,128)(2,1)} %constant_dynamic-slice_fusion), channel_id=1, source_target_pairs={{0,1},{1,2},{5,4},{10,11},{13,12},{14,13},{18,19},{22,21},{23,22},... | collective-permute-start | bytes 3145736 | tf_op jit(solution)/shard_map/ppermute | solution.py:541
  10.3 10.3 %collective-permute-start = (bf16[2048,256]{1,0:T(8,128)(2,1)}, bf16[2048,256]{1,0:T(8,128)(2,1)}, u32[]{:S(2)}, u32[]{:S(2)}) collective-permute-start(bf16[2048,256]{1,0:T(8,128)(2,1)} %dynamic_slice.32), channel_id=1, source_target_pairs={{18,2},{1,17}} | collective-permute-start | bytes 3145736 | tf_op jit(solution)/shard_map/ppermute | solution.py:545
  14.3 22.6 %collective-permute-start.1 = (bf16[2048,256]{1,0:T(8,128)(2,1)}, bf16[2048,256]{1,0:T(8,128)(2,1)}, u32[]{:S(2)}, u32[]{:S(2)}) collective-permute-start(bf16[2048,256]{1,0:T(8,128)(2,1)} %constant_dynamic-slice_fusion.1), channel_id=1, source_target_pairs={{1,0},{5,6},{6,7},{9,8},{14,15},{18,17},{19,18},{20,21},{22,23},{2... | collective-permute-start | bytes 3145736 | tf_op jit(solution)/shard_map/ppermute | solution.py:541
  15.6 24.2 %collective-permute-start.9 = (bf16[256,2048]{1,0:T(8,128)(2,1)}, bf16[256,2048]{1,0:T(8,128)(2,1)}, u32[]{:S(2)}, u32[]{:S(2)}) collective-permute-start(bf16[256,2048]{1,0:T(8,128)(2,1)} %refs_0_.1), channel_id=1, source_target_pairs={{0,28},{4,0},{8,4},{12,8},{16,12},{20,16},{24,20},{28,24},{1,29},{... | collective-permute-start | bytes 3145736 | tf_op jit(solution)/shard_map/ppermute | solution.py:490
  20.6 17.9 %copy-start.7 = (bf16[2048,256]{1,0:T(8,128)(2,1)}, bf16[2048,256]{1,0:T(8,128)(2,1)S(1)}, u32[]{:S(2)}) copy-start(bf16[2048,256]{1,0:T(8,128)(2,1)S(1)} %collective-permute-done.3.refs_1_) | copy-start | bytes 3145732
  22.3 27.4 %collective-permute-start.4 = (bf16[2048,256]{1,0:T(8,128)(2,1)S(1)}, bf16[2048,256]{1,0:T(8,128)(2,1)S(1)}, u32[]{:S(2)}, u32[]{:S(2)}) collective-permute-start(bf16[2048,256]{1,0:T(8,128)(2,1)S(1)} %relay.8), channel_id=1, source_target_pairs={{0,1},{1,2},{2,3},{5,4},{6,5},{9,10},{10,11},{13,12},{14,13},{15,1... | collective-permute-start | bytes 3145736 | tf_op jit(solution)/shard_map/ppermute | solution.py:541
  38.5 24.5 %collective-permute-start.2 = (bf16[2048,256]{1,0:T(8,128)(2,1)S(1)}, bf16[2048,256]{1,0:T(8,128)(2,1)S(1)}, u32[]{:S(2)}, u32[]{:S(2)}) collective-permute-start(bf16[2048,256]{1,0:T(8,128)(2,1)S(1)} %relay.7), channel_id=1, source_target_pairs={{1,0},{2,1},{4,5},{5,6},{6,7},{9,8},{10,9},{13,14},{14,15},{17,16}... | collective-permute-start | bytes 3145736 | tf_op jit(solution)/shard_map/ppermute | solution.py:541
  39.8 25.1 %collective-permute-start.10 = (bf16[256,2048]{1,0:T(8,128)(2,1)}, bf16[256,2048]{1,0:T(8,128)(2,1)}, u32[]{:S(2)}, u32[]{:S(2)}) collective-permute-start(bf16[256,2048]{1,0:T(8,128)(2,1)} %collective-permute-done.9.refs_1_), channel_id=1, source_target_pairs={{0,28},{4,0},{8,4},{12,8},{16,12},{20,16},{24,20},{28,24},{1,29},{... | collective-permute-start | bytes 3145736 | tf_op jit(solution)/shard_map/ppermute | solution.py:490
  49.7 13.3 %copy-start.3 = (bf16[2048,256]{1,0:T(8,128)(2,1)}, bf16[2048,256]{1,0:T(8,128)(2,1)S(1)}, u32[]{:S(2)}) copy-start(bf16[2048,256]{1,0:T(8,128)(2,1)S(1)} %collective-permute-done.4.refs_0_.refs_3_.refs_1_) | copy-start | bytes 3145732
  50.3 14.6 %collective-permute-start.6 = (bf16[2048,256]{1,0:T(8,128)(2,1)S(1)}, bf16[2048,256]{1,0:T(8,128)(2,1)S(1)}, u32[]{:S(2)}, u32[]{:S(2)}) collective-permute-start(bf16[2048,256]{1,0:T(8,128)(2,1)S(1)} %relay.10), channel_id=1, source_target_pairs={{1,2},{2,3},{5,4},{9,10},{10,11},{13,12},{14,13},{18,19},{21,20},{... | collective-permute-start | bytes 3145736 | tf_op jit(solution)/shard_map/ppermute | solution.py:541
  63.0 19.0 %copy-start.5 = (bf16[2048,256]{1,0:T(8,128)(2,1)}, bf16[2048,256]{1,0:T(8,128)(2,1)S(1)}, u32[]{:S(2)}) copy-start(bf16[2048,256]{1,0:T(8,128)(2,1)S(1)} %collective-permute-done.2.refs_0_.refs_2_) | copy-start | bytes 3145732
  63.6 16.7 %collective-permute-start.5 = (bf16[2048,256]{1,0:T(8,128)(2,1)S(1)}, bf16[2048,256]{1,0:T(8,128)(2,1)S(1)}, u32[]{:S(2)}, u32[]{:S(2)}) collective-permute-start(bf16[2048,256]{1,0:T(8,128)(2,1)S(1)} %relay.9), channel_id=1, source_target_pairs={{1,0},{5,6},{6,7},{9,8},{10,9},{14,15},{17,16},{18,17},{22,23},{25... | collective-permute-start | bytes 3145736 | tf_op jit(solution)/shard_map/ppermute | solution.py:541
  64.9 29.9 %collective-permute-start.11 = (bf16[256,2048]{1,0:T(8,128)(2,1)}, bf16[256,2048]{1,0:T(8,128)(2,1)}, u32[]{:S(2)}, u32[]{:S(2)}) collective-permute-start(bf16[256,2048]{1,0:T(8,128)(2,1)} %collective-permute-done.10.refs_2_), channel_id=1, source_target_pairs={{0,28},{4,0},{8,4},{12,8},{16,12},{20,16},{24,20},{28,24},{1,29},{... | collective-permute-start | bytes 3145736 | tf_op jit(solution)/shard_map/ppermute | solution.py:490
  80.3 11.1 %copy-start.1 = (bf16[2048,256]{1,0:T(8,128)(2,1)}, bf16[2048,256]{1,0:T(8,128)(2,1)S(1)}, u32[]{:S(2)}) copy-start(bf16[2048,256]{1,0:T(8,128)(2,1)S(1)} %collective-permute-done.5.refs_0_.refs_4_.refs_2_) | copy-start | bytes 3145732
  81.9 12.8 %copy-start.11 = (s32[2048]{0:T(1024)S(1)}, s32[2048]{0:T(1024)}, u32[]{:S(2)}) copy-start(s32[2048]{0:T(1024)} %param.12) | copy-start | bytes 24580
  81.9 18.2 %collective-permute-start.13 = (bf16[2048,256]{1,0:T(8,128)(2,1)}, bf16[2048,256]{1,0:T(8,128)(2,1)}, u32[]{:S(2)}, u32[]{:S(2)}) collective-permute-start(bf16[2048,256]{1,0:T(8,128)(2,1)} %relay.13), channel_id=1, source_target_pairs={{0,16},{19,3}} | collective-permute-start | bytes 3145736 | tf_op jit(solution)/shard_map/ppermute | solution.py:524
  88.2 11.9 %collective-permute-start.12 = (f32[2048]{0:T(1024)S(1)}, f32[2048]{0:T(1024)S(1)}, u32[]{:S(2)}, u32[]{:S(2)}) collective-permute-start(f32[2048]{0:T(1024)S(1)} %multiply_reduce_fusion), channel_id=1, source_target_pairs={{0,1},{1,0},{2,3},{3,2},{4,5},{5,4},{6,7},{7,6},{8,9},{9,8},{10,11... | collective-permute-start | bytes 24584 | tf_op jit(solution)/shard_map/ppermute | solution.py:511
  89.8 22.5 %collective-permute-start.8 = (bf16[2048,256]{1,0:T(8,128)(2,1)}, bf16[2048,256]{1,0:T(8,128)(2,1)}, u32[]{:S(2)}, u32[]{:S(2)}) collective-permute-start(bf16[2048,256]{1,0:T(8,128)(2,1)} %relay.12), channel_id=1, source_target_pairs={{1,2},{2,3},{10,11},{13,12},{21,20},{26,27}} | collective-permute-start | bytes 3145736 | tf_op jit(solution)/shard_map/ppermute | solution.py:541
  93.1 19.1 %collective-permute-start.7 = (bf16[2048,256]{1,0:T(8,128)(2,1)}, bf16[2048,256]{1,0:T(8,128)(2,1)}, u32[]{:S(2)}, u32[]{:S(2)}) collective-permute-start(bf16[2048,256]{1,0:T(8,128)(2,1)} %relay.11), channel_id=1, source_target_pairs={{6,7},{9,8},{17,16},{18,17},{25,24},{30,31}} | collective-permute-start | bytes 3145736 | tf_op jit(solution)/shard_map/ppermute | solution.py:541
  95.2 1.2 %copy-start.9 = (bf16[256,2048]{1,0:T(8,128)(2,1)S(1)}, bf16[256,2048]{1,0:T(8,128)(2,1)}, u32[]{:S(2)}) copy-start(bf16[256,2048]{1,0:T(8,128)(2,1)} %refs_0_.1) | copy-start | bytes 3145732
  96.5 4.0 %copy-start.2 = (bf16[2048,256]{1,0:T(8,128)(2,1)S(1)}, bf16[2048,256]{1,0:T(8,128)(2,1)}, u32[]{:S(2)}) copy-start(bf16[2048,256]{1,0:T(8,128)(2,1)} %copy-done.1) | copy-start | bytes 3145732
  96.5 4.0 %copy-start.4 = (bf16[2048,256]{1,0:T(8,128)(2,1)S(1)}, bf16[2048,256]{1,0:T(8,128)(2,1)}, u32[]{:S(2)}) copy-start(bf16[2048,256]{1,0:T(8,128)(2,1)} %copy-done.3) | copy-start | bytes 3145732
  96.5 4.0 %copy-start.6 = (bf16[2048,256]{1,0:T(8,128)(2,1)S(1)}, bf16[2048,256]{1,0:T(8,128)(2,1)}, u32[]{:S(2)}) copy-start(bf16[2048,256]{1,0:T(8,128)(2,1)} %copy-done.5) | copy-start | bytes 3145732
  96.5 4.0 %copy-start.8 = (bf16[2048,256]{1,0:T(8,128)(2,1)S(1)}, bf16[2048,256]{1,0:T(8,128)(2,1)}, u32[]{:S(2)}) copy-start(bf16[2048,256]{1,0:T(8,128)(2,1)} %copy-done.7) | copy-start | bytes 3145732
  100.1 11.6 %collective-permute-start.14 = (f32[2048]{0:T(1024)S(1)}, f32[2048]{0:T(1024)S(1)}, u32[]{:S(2)}, u32[]{:S(2)}) collective-permute-start(f32[2048]{0:T(1024)S(1)} %add.39), channel_id=1, source_target_pairs={{0,2},{1,3},{2,0},{3,1},{4,6},{5,7},{6,4},{7,5},{8,10},{9,11},{10,... | collective-permute-start | bytes 24584 | tf_op jit(solution)/shard_map/ppermute | solution.py:511

commit v12 on v11

--- a/solution.py
+++ b/solution.py
@@ -491,15 +491,14 @@
     squares = own_squares()
 
     starts = {}
-    if any(own_of[1, 1]):
-        starts[1, 1] = own_chunk(own_of[1, 1])
     later_x = x
+    for phase in (1, 0):
+        if any(own_of[phase, 1]):
+            starts[phase, 1] = own_chunk(own_of[phase, 1], later_x)
+        later_x = lax.optimization_barrier(later_x)
+    later_x, squares = lax.optimization_barrier((later_x, squares))
     for k, crossing in enumerate(crossings):
-        later_x = lax.optimization_barrier(later_x)
         starts["cross", k] = own_chunk([crossing[rc][1] if rc in crossing else None for rc in devices], later_x)
-    later_x, squares = lax.optimization_barrier((later_x, squares))
-    if any(own_of[0, 1]):
-        starts[0, 1] = own_chunk(own_of[0, 1], later_x)
     bits = [1 << k for k in range(cols.bit_length() - 1)] if cols & (cols - 1) == 0 else []
     if cols & (cols - 1):
         squares = lax.psum(squares, "col")
@@ -513,6 +512,10 @@
         return value, squares + other
 
     buffers, crossed = {}, {}
+    zy = None
+
+    def window_product():
+        return standardized_window(rank_at, table, window, wide(window_factor), wide(window_twice), male_cols[None, :])
 
     def bring_back(t):
         if t in returns:
@@ -538,6 +541,11 @@
                 held = own_chunk(own_of[key])
             else:
                 held = crossed[next(k for k in kinds_of[key] if k is not None)]
+            if key == (0, 3):
+                while bits:
+                    bit = bits.pop(0)
+                    squares = squares + lax.ppermute(squares, "col", [(i, i ^ bit) for i in range(cols)])
+                held, squares = lax.optimization_barrier((held, squares))
             buffers[key] = lax.ppermute(held, both, pairs_of[key])
         if key == (0, 1):
             for k, crossing in enumerate(crossings):
@@ -546,11 +554,10 @@
         if phase == 1:
             bring_back(t - 1)
     bring_back(rounds)
-    zy = standardized_window(rank_at, table, window, wide(window_factor), wide(window_twice), male_cols[None, :])
-    zy, squares = sum_beside(zy, squares)
+    if zy is None:
+        zy = window_product()
     shared = window_factor[None, :], window_twice[None, :], male_wide, zy
     total = early_product(source_at[0], candidates[0], table, x, [buffers[k] for k in used[0]], *shared)
-    total, squares = sum_beside(total, squares)
     relation = last_product(source_at[1], candidates[1][0], table, x, [buffers[k] for k in used[1]], *shared, total)
     for bit in bits:
         squares = squares + lax.ppermute(squares, "col", [(i, i ^ bit) for i in range(cols)])

time: 120 us -> 135 us (1.12)
  the two profiles are of different devices: /device:TPU:0 before, /device:TPU:24 now
where the time goes in v12:
time: 135 us
  waiting for transfers between devices  49.4 us (37%)
  starting transfers between devices  44.9 us (33%)
  Pallas kernels  27.7 us (21%)
  local copies, waits for them, and re-layouts  7.05 us (5%)
  other arithmetic  4.8 us (4%)
    ppermute x2, starting transfers between devices, local(): lax.ppermute(squares, 'col', [(i, i ^ bit) for i in range(cols)])  26.6 us
    ppermute x2, waiting for transfers between devices, local(): lax.ppermute(squares, 'col', [(i, i ^ bit) for i in range(cols)])  20.1 us
    ppermute x8, waiting for transfers between devices, local(): buffers[key] = lax.ppermute(held, both, pairs_of[key])  15.1 us
    pallas_call x1, Pallas kernels, early_product(): pl.pallas_call(functools.partial(early_kernel, at, candidates, len(buffer...  10.9 us
    ppermute x8, starting transfers between devices, local(): buffers[key] = lax.ppermute(held, both, pairs_of[key])  8.44 us
    ppermute x1, waiting for transfers between devices, bring_back(): buffers['back', t] = lax.ppermute(held, both, pairs)  7.67 us
    pallas_call x7, Pallas kernels, relay(): pl.pallas_call(functools.partial(relay_kernel, at), out_shape=pltpu.VMEM(...  7.53 us
    ppermute x3, starting transfers between devices, local(): window.append(lax.ppermute(window[-1], 'row', back))  7.02 us
  transfers between devices with their start and end apart: 15, of which 6 were waited for; matrix products, arithmetic and copies ran while one was open for 3% of the time, Pallas kernels for 16%

profile of v12, /device:TPU:24, one launch (start us, length us, event | category | flops | bytes accessed | tf_op | source)
XLA Modules:
  0.0 134.8 jit_solution(4296275827489070440)
XLA Ops:
  0.6 0.0 copy-start
  0.6 0.8 compare_select_fusion.1
  1.5 0.7 broadcast_multiply_fusion
  2.2 0.1 dynamic_slice.25
  2.3 0.1 dynamic_slice.26
  2.4 2.5 %multiply_reduce_fusion = f32[2048]{0:T(1024)S(1)} fusion(bf16[2048,512]{1,0:T(8,128)(2,1)} %x.17, f32[2048]{0:T(1024)S(1)} %compare_select_fusion.1, f32[512]{0:T(512)S(1)} %dynamic_slice.26, f32[512]{0:T(512)S(1)} %dynamic_slice.25), kind=kLoop, calls=%fused_computation | loop fusion | flops 8386560 | bytes 2117632 | tf_op jit(solution)/shard_map/reduce_sum | solution.py:485
  4.9 2.3 %dynamic_slice.27 = bf16[2048,256]{1,0:T(8,128)(2,1)} slice(bf16[2048,512]{1,0:T(8,128)(2,1)} %x.17), slice={[0:2048], [256:512]} | slice | bytes 2097152 | tf_op jit(solution)/shard_map/dynamic_slice | solution.py:466
  7.2 1.6 %collective-permute-start = (bf16[2048,256]{1,0:T(8,128)(2,1)}, bf16[2048,256]{1,0:T(8,128)(2,1)}, u32[]{:S(2)}, u32[]{:S(2)}) collective-permute-start(bf16[2048,256]{1,0:T(8,128)(2,1)} %dynamic_slice.27), channel_id=1, source_target_pairs={{18,2},{1,17}} | collective-permute-start | bytes 3145736 | tf_op jit(solution)/shard_map/ppermute | solution.py:553
  8.8 0.0 copy-done
  8.8 1.0 constant_dynamic-slice_fusion
  9.8 0.7 collective-permute-start.3
  10.6 1.1 constant_dynamic-slice_fusion.1
  11.6 1.7 %collective-permute-start.1 = (bf16[2048,256]{1,0:T(8,128)(2,1)}, bf16[2048,256]{1,0:T(8,128)(2,1)}, u32[]{:S(2)}, u32[]{:S(2)}) collective-permute-start(bf16[2048,256]{1,0:T(8,128)(2,1)} %constant_dynamic-slice_fusion.1), channel_id=1, source_target_pairs={{1,0},{5,6},{6,7},{9,8},{14,15},{18,17},{19,18},{20,21},{22,23},{2... | collective-permute-start | bytes 3145736 | tf_op jit(solution)/shard_map/ppermute | solution.py:549
  13.3 3.3 %collective-permute-start.11 = (bf16[256,2048]{1,0:T(8,128)(2,1)}, bf16[256,2048]{1,0:T(8,128)(2,1)}, u32[]{:S(2)}, u32[]{:S(2)}) collective-permute-start(bf16[256,2048]{1,0:T(8,128)(2,1)} %refs_0_.1), channel_id=1, source_target_pairs={{0,28},{4,0},{8,4},{12,8},{16,12},{20,16},{24,20},{28,24},{1,29},{... | collective-permute-start | bytes 3145736 | tf_op jit(solution)/shard_map/ppermute | solution.py:490
  16.6 0.7 fusion.2.table
  17.3 0.0 collective-permute-done.refs_0_
  17.3 0.0 collective-permute-done.3.refs_1_
  17.3 0.0 copy-start.7
  17.3 1.7 %relay.8 = bf16[2048,256]{1,0:T(8,128)(2,1)S(1)} custom-call(s32[33]{0:T(128)S(1)} %fusion.2.table, bf16[2048,512]{1,0:T(8,128)(2,1)S(1)} %copy-done, bf16[2048,256]{1,0:T(8,128)(2,1)} %collective-permute-done.refs_0_, bf16[2048,256]{1,0:T(8,128)(2,1)S(1)} %collective-permute-done.3.refs_1_), custom_call_target="tpu_custom_call" | custom-call | tf_op jit(solution)/shard_map/relay/pallas_call | solution.py:182
  19.0 1.3 collective-permute-start.4
  20.3 0.0 collective-permute-done.1.refs_1_.refs_0_
  20.3 1.6 %relay.7 = bf16[2048,256]{1,0:T(8,128)(2,1)S(1)} custom-call(s32[33]{0:T(128)S(1)} %fusion.2.table, bf16[2048,512]{1,0:T(8,128)(2,1)S(1)} %copy-done, bf16[2048,256]{1,0:T(8,128)(2,1)} %collective-permute-done.refs_0_, bf16[2048,256]{1,0:T(8,128)(2,1)} %collective-permute-done.1.refs_1_.refs_0_), custom_call_target="tpu_custom_call" | custom-call | tf_op jit(solution)/shard_map/relay/pallas_call | solution.py:182
  22.0 0.0 copy-done.7
  22.0 0.7 collective-permute-start.2
  22.7 25.7 %collective-permute-start.5 = (f32[2048]{0:T(1024)S(1)}, f32[2048]{0:T(1024)S(1)}, u32[]{:S(2)}, u32[]{:S(2)}) collective-permute-start(f32[2048]{0:T(1024)S(1)} %multiply_reduce_fusion), channel_id=1, source_target_pairs={{0,1},{1,0},{2,3},{3,2},{4,5},{5,4},{6,7},{7,6},{8,9},{9,8},{10,11... | collective-permute-start | bytes 24584 | tf_op jit(solution)/shard_map/ppermute | solution.py:547
  48.5 17.3 %collective-permute-done.5 = f32[2048]{0:T(1024)S(1)} collective-permute-done((f32[2048]{0:T(1024)S(1)}, f32[2048]{0:T(1024)S(1)}, u32[]{:S(2)}, u32[]{:S(2)}) %collective-permute-start.5) | collective-permute-done | bytes 8224 | tf_op jit(solution)/shard_map/ppermute | solution.py:547
  65.8 0.8 collective-permute-start.6
  66.6 0.0 collective-permute-done.11.refs_1_
  66.6 0.9 collective-permute-start.12
  67.6 2.8 %collective-permute-done.6 = f32[2048]{0:T(1024)S(1)} collective-permute-done((f32[2048]{0:T(1024)S(1)}, f32[2048]{0:T(1024)S(1)}, u32[]{:S(2)}, u32[]{:S(2)}) %collective-permute-start.6) | collective-permute-done | bytes 8224 | tf_op jit(solution)/shard_map/ppermute | solution.py:547
  70.4 0.0 collective-permute-done.4.refs_0_.refs_3_.refs_1_
  70.4 0.6 relay.10
  71.0 1.3 collective-permute-start.8
  72.3 0.0 collective-permute-done.2.refs_0_.refs_2_
  72.3 0.0 copy-start.5
  72.3 0.6 relay.9
  72.9 0.0 copy-done.3
  73.0 0.7 collective-permute-start.7
  73.7 6.5 %collective-permute-done.12.refs_2_ = bf16[256,2048]{1,0:T(8,128)(2,1)} collective-permute-done((bf16[256,2048]{1,0:T(8,128)(2,1)}, bf16[256,2048]{1,0:T(8,128)(2,1)}, u32[]{:S(2)}, u32[]{:S(2)}) %collective-permute-start.12) | collective-permute-done | bytes 1048608 | tf_op jit(solution)/shard_map/ppermute | solution.py:490
  80.2 2.8 %collective-permute-start.13 = (bf16[256,2048]{1,0:T(8,128)(2,1)}, bf16[256,2048]{1,0:T(8,128)(2,1)}, u32[]{:S(2)}, u32[]{:S(2)}) collective-permute-start(bf16[256,2048]{1,0:T(8,128)(2,1)} %collective-permute-done.12.refs_2_), channel_id=1, source_target_pairs={{0,28},{4,0},{8,4},{12,8},{16,12},{20,16},{24,20},{28,24},{1,29},{... | collective-permute-start | bytes 3145736 | tf_op jit(solution)/shard_map/ppermute | solution.py:490
  83.0 14.2 %collective-permute-done.8.refs_0_.refs_1_.refs_5_.refs_3_ = bf16[2048,256]{1,0:T(8,128)(2,1)S(1)} collective-permute-done((bf16[2048,256]{1,0:T(8,128)(2,1)S(1)}, bf16[2048,256]{1,0:T(8,128)(2,1)S(1)}, u32[]{:S(2)}, u32[]{:S(2)}) %collective-permute-start.8) | collective-permute-done | bytes 1048608 | tf_op jit(solution)/shard_map/ppermute | solution.py:549
  97.2 0.0 collective-permute-done.7.refs_0_.refs_4_.refs_2_
  97.2 1.7 %relay.13 = bf16[2048,256]{1,0:T(8,128)(2,1)} custom-call(s32[33]{0:T(128)S(1)} %fusion.2.table, bf16[2048,512]{1,0:T(8,128)(2,1)S(1)} %copy-done, bf16[2048,256]{1,0:T(8,128)(2,1)S(1)} %collective-permute-done.7.refs_0_.refs_4_.refs_2_, bf16[2048,256]{1,0:T(8,128)(2,1)S(1)} %collective-permute-done.8.refs_0_.refs_1_.refs_5_.refs_3_), custom_call_target="tpu_custom_call" | custom-call | tf_op jit(solution)/shard_map/relay/pallas_call | solution.py:182
  98.9 0.0 copy-done.5
  98.9 1.1 copy-done.1
  100.0 1.3 collective-permute-start.14
  101.3 0.1 fusion
  101.4 0.6 relay.12
  102.0 1.3 collective-permute-start.10
  103.3 0.6 relay.11
  104.0 0.7 collective-permute-start.9
  104.7 0.0 copy-done.10
  104.7 0.6 multiply_add_fusion
  105.3 0.0 collective-permute-done.13.refs_3_
  105.3 0.2 broadcast_in_dim.43.refs_5_
  105.5 0.2 broadcast_in_dim.42.refs_4_
  105.7 0.0 copy-start.6
  105.8 3.6 %window.1.refs_10_.refs_9_ = bf16[1024,2048]{1,0:T(8,128)(2,1)S(1)} custom-call(s32[33]{0:T(128)S(1)} %fusion.2.table, bf16[256,2048]{1,0:T(8,128)(2,1)S(1)} %copy-done.9, bf16[256,2048]{1,0:T(8,128)(2,1)} %collective-permute-done.11.refs_1_, bf16[256,2048]{1,0:T(8,128)(2,1)} %collective-permute-done.12.refs_2_, ...), custom_call_target="tpu_custom_call" | custom-call | flops 8388608 | bytes 8388608 | tf_op jit(solution)/shard_map/window/pallas_call | solution.py:220
  109.3 7.7 %collective-permute-done.14.refs_6_ = bf16[2048,256]{1,0:T(8,128)(2,1)} collective-permute-done((bf16[2048,256]{1,0:T(8,128)(2,1)}, bf16[2048,256]{1,0:T(8,128)(2,1)}, u32[]{:S(2)}, u32[]{:S(2)}) %collective-permute-start.14) | collective-permute-done | bytes 1048608 | tf_op jit(solution)/shard_map/ppermute | solution.py:527
  117.0 0.3 broadcast_in_dim.41.refs_9_.refs_8_
  117.4 10.9 %early.1.refs_10_ = f32[2048,2048]{1,0:T(8,128)S(1)} custom-call(s32[33]{0:T(128)S(1)} %fusion.2.table, bf16[2048,512]{1,0:T(8,128)(2,1)S(1)} %copy-done, bf16[2048,256]{1,0:T(8,128)(2,1)} %collective-permute-done.1.refs_1_.refs_0_, bf16[2048,256]{1,0:T(8,128)(2,1)S(1)} %copy-done.8, bf16[2048,256]{1,0:T(8,128)(2,1)S(1)} %copy-done.6, ...), custom_call_target="tpu_custom_call" | custom-call | flops 6442450944 | tf_op jit(solution)/shard_map/early/pallas_call | solution.py:281
  128.2 0.8 collective-permute-done.10.refs_5_
  129.1 0.0 collective-permute-done.9.refs_4_
  129.1 5.8 %last.1 = bf16[2048,2048]{1,0:T(8,128)(2,1)} custom-call(s32[33]{0:T(128)S(1)} %fusion.2.table, bf16[2048,512]{1,0:T(8,128)(2,1)S(1)} %copy-done, bf16[2048,256]{1,0:T(8,128)(2,1)S(1)} %copy-done.6, bf16[2048,256]{1,0:T(8,128)(2,1)S(1)} %copy-done.4, bf16[2048,256]{1,0:T(8,128)(2,1)S(1)} %copy-done.2, ...), custom_call_target="tpu_custom_call" | custom-call | flops 2147483648 | bytes 8388608 | tf_op jit(solution)/shard_map/last/pallas_call | solution.py:325
  (15 shorter events, 0.0 us)
Async XLA Ops:
  0.6 8.2 %copy-start = (bf16[2048,512]{1,0:T(8,128)(2,1)S(1)}, bf16[2048,512]{1,0:T(8,128)(2,1)}, u32[]{:S(2)}) copy-start(bf16[2048,512]{1,0:T(8,128)(2,1)} %x.17) | copy-start | bytes 6291460
  7.2 10.1 %collective-permute-start = (bf16[2048,256]{1,0:T(8,128)(2,1)}, bf16[2048,256]{1,0:T(8,128)(2,1)}, u32[]{:S(2)}, u32[]{:S(2)}) collective-permute-start(bf16[2048,256]{1,0:T(8,128)(2,1)} %dynamic_slice.27), channel_id=1, source_target_pairs={{18,2},{1,17}} | collective-permute-start | bytes 3145736 | tf_op jit(solution)/shard_map/ppermute | solution.py:553
  9.8 7.5 %collective-permute-start.3 = (bf16[2048,256]{1,0:T(8,128)(2,1)}, bf16[2048,256]{1,0:T(8,128)(2,1)S(1)}, u32[]{:S(2)}, u32[]{:S(2)}) collective-permute-start(bf16[2048,256]{1,0:T(8,128)(2,1)} %constant_dynamic-slice_fusion), channel_id=1, source_target_pairs={{0,1},{1,2},{5,4},{10,11},{13,12},{14,13},{18,19},{22,21},{23,22},... | collective-permute-start | bytes 3145736 | tf_op jit(solution)/shard_map/ppermute | solution.py:549
  11.6 8.7 %collective-permute-start.1 = (bf16[2048,256]{1,0:T(8,128)(2,1)}, bf16[2048,256]{1,0:T(8,128)(2,1)}, u32[]{:S(2)}, u32[]{:S(2)}) collective-permute-start(bf16[2048,256]{1,0:T(8,128)(2,1)} %constant_dynamic-slice_fusion.1), channel_id=1, source_target_pairs={{1,0},{5,6},{6,7},{9,8},{14,15},{18,17},{19,18},{20,21},{22,23},{2... | collective-permute-start | bytes 3145736 | tf_op jit(solution)/shard_map/ppermute | solution.py:549
  13.3 53.3 %collective-permute-start.11 = (bf16[256,2048]{1,0:T(8,128)(2,1)}, bf16[256,2048]{1,0:T(8,128)(2,1)}, u32[]{:S(2)}, u32[]{:S(2)}) collective-permute-start(bf16[256,2048]{1,0:T(8,128)(2,1)} %refs_0_.1), channel_id=1, source_target_pairs={{0,28},{4,0},{8,4},{12,8},{16,12},{20,16},{24,20},{28,24},{1,29},{... | collective-permute-start | bytes 3145736 | tf_op jit(solution)/shard_map/ppermute | solution.py:490
  17.3 4.7 %copy-start.7 = (bf16[2048,256]{1,0:T(8,128)(2,1)}, bf16[2048,256]{1,0:T(8,128)(2,1)S(1)}, u32[]{:S(2)}) copy-start(bf16[2048,256]{1,0:T(8,128)(2,1)S(1)} %collective-permute-done.3.refs_1_) | copy-start | bytes 3145732
  19.0 51.3 %collective-permute-start.4 = (bf16[2048,256]{1,0:T(8,128)(2,1)S(1)}, bf16[2048,256]{1,0:T(8,128)(2,1)S(1)}, u32[]{:S(2)}, u32[]{:S(2)}) collective-permute-start(bf16[2048,256]{1,0:T(8,128)(2,1)S(1)} %relay.8), channel_id=1, source_target_pairs={{0,1},{1,2},{2,3},{5,4},{6,5},{9,10},{10,11},{13,12},{14,13},{15,1... | collective-permute-start | bytes 3145736 | tf_op jit(solution)/shard_map/ppermute | solution.py:549
  22.0 50.3 %collective-permute-start.2 = (bf16[2048,256]{1,0:T(8,128)(2,1)S(1)}, bf16[2048,256]{1,0:T(8,128)(2,1)S(1)}, u32[]{:S(2)}, u32[]{:S(2)}) collective-permute-start(bf16[2048,256]{1,0:T(8,128)(2,1)S(1)} %relay.7), channel_id=1, source_target_pairs={{1,0},{2,1},{4,5},{5,6},{6,7},{9,8},{10,9},{13,14},{14,15},{17,16}... | collective-permute-start | bytes 3145736 | tf_op jit(solution)/shard_map/ppermute | solution.py:549
  22.7 43.1 %collective-permute-start.5 = (f32[2048]{0:T(1024)S(1)}, f32[2048]{0:T(1024)S(1)}, u32[]{:S(2)}, u32[]{:S(2)}) collective-permute-start(f32[2048]{0:T(1024)S(1)} %multiply_reduce_fusion), channel_id=1, source_target_pairs={{0,1},{1,0},{2,3},{3,2},{4,5},{5,4},{6,7},{7,6},{8,9},{9,8},{10,11... | collective-permute-start | bytes 24584 | tf_op jit(solution)/shard_map/ppermute | solution.py:547
  65.8 4.5 %collective-permute-start.6 = (f32[2048]{0:T(1024)S(1)}, f32[2048]{0:T(1024)S(1)}, u32[]{:S(2)}, u32[]{:S(2)}) collective-permute-start(f32[2048]{0:T(1024)S(1)} %add.38), channel_id=1, source_target_pairs={{0,2},{1,3},{2,0},{3,1},{4,6},{5,7},{6,4},{7,5},{8,10},{9,11},{10,... | collective-permute-start | bytes 24584 | tf_op jit(solution)/shard_map/ppermute | solution.py:547
  66.6 13.6 %collective-permute-start.12 = (bf16[256,2048]{1,0:T(8,128)(2,1)}, bf16[256,2048]{1,0:T(8,128)(2,1)}, u32[]{:S(2)}, u32[]{:S(2)}) collective-permute-start(bf16[256,2048]{1,0:T(8,128)(2,1)} %collective-permute-done.11.refs_1_), channel_id=1, source_target_pairs={{0,28},{4,0},{8,4},{12,8},{16,12},{20,16},{24,20},{28,24},{1,29},{... | collective-permute-start | bytes 3145736 | tf_op jit(solution)/shard_map/ppermute | solution.py:490
  70.4 2.6 %copy-start.3 = (bf16[2048,256]{1,0:T(8,128)(2,1)}, bf16[2048,256]{1,0:T(8,128)(2,1)S(1)}, u32[]{:S(2)}) copy-start(bf16[2048,256]{1,0:T(8,128)(2,1)S(1)} %collective-permute-done.4.refs_0_.refs_3_.refs_1_) | copy-start | bytes 3145732
  71.0 26.2 %collective-permute-start.8 = (bf16[2048,256]{1,0:T(8,128)(2,1)S(1)}, bf16[2048,256]{1,0:T(8,128)(2,1)S(1)}, u32[]{:S(2)}, u32[]{:S(2)}) collective-permute-start(bf16[2048,256]{1,0:T(8,128)(2,1)S(1)} %relay.10), channel_id=1, source_target_pairs={{1,2},{2,3},{5,4},{9,10},{10,11},{13,12},{14,13},{18,19},{21,20},{... | collective-permute-start | bytes 3145736 | tf_op jit(solution)/shard_map/ppermute | solution.py:549
  72.3 26.6 %copy-start.5 = (bf16[2048,256]{1,0:T(8,128)(2,1)}, bf16[2048,256]{1,0:T(8,128)(2,1)S(1)}, u32[]{:S(2)}) copy-start(bf16[2048,256]{1,0:T(8,128)(2,1)S(1)} %collective-permute-done.2.refs_0_.refs_2_) | copy-start | bytes 3145732
  73.0 24.3 %collective-permute-start.7 = (bf16[2048,256]{1,0:T(8,128)(2,1)S(1)}, bf16[2048,256]{1,0:T(8,128)(2,1)S(1)}, u32[]{:S(2)}, u32[]{:S(2)}) collective-permute-start(bf16[2048,256]{1,0:T(8,128)(2,1)S(1)} %relay.9), channel_id=1, source_target_pairs={{1,0},{5,6},{6,7},{9,8},{10,9},{14,15},{17,16},{18,17},{22,23},{25... | collective-permute-start | bytes 3145736 | tf_op jit(solution)/shard_map/ppermute | solution.py:549
  80.2 25.1 %collective-permute-start.13 = (bf16[256,2048]{1,0:T(8,128)(2,1)}, bf16[256,2048]{1,0:T(8,128)(2,1)}, u32[]{:S(2)}, u32[]{:S(2)}) collective-permute-start(bf16[256,2048]{1,0:T(8,128)(2,1)} %collective-permute-done.12.refs_2_), channel_id=1, source_target_pairs={{0,28},{4,0},{8,4},{12,8},{16,12},{20,16},{24,20},{28,24},{1,29},{... | collective-permute-start | bytes 3145736 | tf_op jit(solution)/shard_map/ppermute | solution.py:490
  98.9 1.1 copy-start.1
  100.0 17.0 %collective-permute-start.14 = (bf16[2048,256]{1,0:T(8,128)(2,1)}, bf16[2048,256]{1,0:T(8,128)(2,1)}, u32[]{:S(2)}, u32[]{:S(2)}) collective-permute-start(bf16[2048,256]{1,0:T(8,128)(2,1)} %relay.13), channel_id=1, source_target_pairs={{0,16},{19,3}} | collective-permute-start | bytes 3145736 | tf_op jit(solution)/shard_map/ppermute | solution.py:527
  101.3 2.0 %copy-start.2 = (bf16[2048,256]{1,0:T(8,128)(2,1)S(1)}, bf16[2048,256]{1,0:T(8,128)(2,1)}, u32[]{:S(2)}) copy-start(bf16[2048,256]{1,0:T(8,128)(2,1)} %copy-done.1) | copy-start | bytes 3145732
  101.4 3.3 %copy-start.10 = (s32[2048]{0:T(1024)S(1)}, s32[2048]{0:T(1024)}, u32[]{:S(2)}) copy-start(s32[2048]{0:T(1024)} %param.12) | copy-start | bytes 24580
  101.4 4.3 %copy-start.9 = (bf16[256,2048]{1,0:T(8,128)(2,1)S(1)}, bf16[256,2048]{1,0:T(8,128)(2,1)}, u32[]{:S(2)}) copy-start(bf16[256,2048]{1,0:T(8,128)(2,1)} %refs_0_.1) | copy-start | bytes 3145732
  102.0 27.0 %collective-permute-start.10 = (bf16[2048,256]{1,0:T(8,128)(2,1)S(1)}, bf16[2048,256]{1,0:T(8,128)(2,1)S(1)}, u32[]{:S(2)}, u32[]{:S(2)}) collective-permute-start(bf16[2048,256]{1,0:T(8,128)(2,1)S(1)} %relay.12), channel_id=1, source_target_pairs={{1,2},{2,3},{10,11},{13,12},{21,20},{26,27}} | collective-permute-start | bytes 3145736 | tf_op jit(solution)/shard_map/ppermute | solution.py:549
  104.0 25.1 %collective-permute-start.9 = (bf16[2048,256]{1,0:T(8,128)(2,1)S(1)}, bf16[2048,256]{1,0:T(8,128)(2,1)S(1)}, u32[]{:S(2)}, u32[]{:S(2)}) collective-permute-start(bf16[2048,256]{1,0:T(8,128)(2,1)S(1)} %relay.11), channel_id=1, source_target_pairs={{6,7},{9,8},{17,16},{18,17},{25,24},{30,31}} | collective-permute-start | bytes 3145736 | tf_op jit(solution)/shard_map/ppermute | solution.py:549
  105.7 11.6 %copy-start.4 = (bf16[2048,256]{1,0:T(8,128)(2,1)S(1)}, bf16[2048,256]{1,0:T(8,128)(2,1)}, u32[]{:S(2)}) copy-start(bf16[2048,256]{1,0:T(8,128)(2,1)} %copy-done.3) | copy-start | bytes 3145732
  105.7 11.6 %copy-start.6 = (bf16[2048,256]{1,0:T(8,128)(2,1)S(1)}, bf16[2048,256]{1,0:T(8,128)(2,1)}, u32[]{:S(2)}) copy-start(bf16[2048,256]{1,0:T(8,128)(2,1)} %copy-done.5) | copy-start | bytes 3145732
  105.8 11.6 %copy-start.8 = (bf16[2048,256]{1,0:T(8,128)(2,1)S(1)}, bf16[2048,256]{1,0:T(8,128)(2,1)}, u32[]{:S(2)}) copy-start(bf16[2048,256]{1,0:T(8,128)(2,1)} %copy-done.7) | copy-start | bytes 3145732

commit v13 on v11

--- a/solution.py
+++ b/solution.py
@@ -400,15 +400,12 @@
 
     returns = {}
     for t in range(1, rounds + 1):
-        pairs, phases = [], [None] * len(devices)
         for d, lane in enumerate(lanes):
             for r in range(rows):
                 item = lane.lines[r][0].get(t)
                 if item is not None and item.home is not None:
-                    pairs.append((number(r, lane.col(0)), number(item.home, lane.col(0))))
-                    phases[pairs[-1][0]] = (r + d) % 2
-        if pairs:
-            returns[t] = pairs, phases
+                    pair = number(r, lane.col(0)), number(item.home, lane.col(0))
+                    returns.setdefault(((r + d) % 2, t), []).append(pair)
 
     columns = []
 
@@ -428,9 +425,6 @@
                 else:
                     entries.append((1 + names.index(kind) if kind is not None else 1, 0, 0))
             relays[key] = names, add(entries)
-    for t, (pairs, phases) in returns.items():
-        if len(set(phases) - {None}) > 1:
-            relays["back", t] = None, add([(1 + (p or 0), 0, 0) for p in phases])
 
     order = []
     for r, c in devices:
@@ -441,7 +435,9 @@
                 arrival = lane.arrival(r, c, (0, s))
                 if arrival is not None:
                     t, returned = arrival
-                    when, key = (t + 0.7, ("back", t)) if returned else (t, ((r + d) % 2, t))
+                    when, key = t, ((r + d) % 2, t)
+                    if returned:
+                        when, key = t + 0.7, ("back%d" % ((r + rows // 2 + d) % 2), t)
             arrivals.append((when, s, key))
         order.append(sorted(arrivals, key=lambda a: a[:2]))
     rank_at = add([[[a[1] for a in arrivals].index(s) for s in range(STEPS)] for arrivals in order])
@@ -514,14 +510,10 @@
 
     buffers, crossed = {}, {}
 
-    def bring_back(t):
-        if t in returns:
-            pairs, phases = returns[t]
-            if ("back", t) in relays:
-                held = relay(relays["back", t][1], table, x, [buffers[0, t], buffers[1, t]])
-            else:
-                held = buffers[next(p for p in phases if p is not None), t]
-            buffers["back", t] = lax.ppermute(held, both, pairs)
+    def bring_back(key):
+        if key in returns:
+            phase, t = key
+            buffers["back%d" % phase, t] = lax.ppermute(buffers[key], both, returns[key])
 
     for key in sends:
         phase, t = key
@@ -543,15 +535,13 @@
             for k, crossing in enumerate(crossings):
                 pairs = [(number(*rc), number(*to)) for rc, (to, _) in crossing.items()]
                 crossed[k] = lax.ppermute(starts["cross", k], both, pairs)
-        if phase == 1:
-            bring_back(t - 1)
-    bring_back(rounds)
+        bring_back(key)
     zy = standardized_window(rank_at, table, window, wide(window_factor), wide(window_twice), male_cols[None, :])
-    zy, squares = sum_beside(zy, squares)
     shared = window_factor[None, :], window_twice[None, :], male_wide, zy
     total = early_product(source_at[0], candidates[0], table, x, [buffers[k] for k in used[0]], *shared)
     total, squares = sum_beside(total, squares)
     relation = last_product(source_at[1], candidates[1][0], table, x, [buffers[k] for k in used[1]], *shared, total)
+    relation, squares = sum_beside(relation, squares)
     for bit in bits:
         squares = squares + lax.ppermute(squares, "col", [(i, i ^ bit) for i in range(cols)])
     inbreeding = squares / jnp.float32(freq.shape[0]) - 1.0

time: 120 us -> 136 us (1.13)
  starting transfers between devices: 33.2 us -> 46.9 us
    ppermute x2, starting transfers between devices: 0.07 us -> 11.5 us  [sum_beside(): other = lax.ppermute(squares, 'col', [(i, i ^ bit) for i in range(cols)])]
    ppermute x8, starting transfers between devices: 21.8 us -> 29.1 us  [local(): buffers[key] = lax.ppermute(held, both, pairs_of[key])]
    ppermute x3, starting transfers between devices: 3.52 us -> 0.75 us  [local(): window.append(lax.ppermute(window[-1], 'row', back))]
    ppermute x1 -> x2, starting transfers between devices: 6.22 us -> 3.93 us  [bring_back(): lax.ppermute(buffers[key], both, returns[key])]
    pallas_call x7 -> x6, Pallas kernels: 9.5 us -> 8.9 us  [relay(): pl.pallas_call(functools.partial(relay_kernel, at), out_shape=pltpu.VMEM(...]
  transfers between devices with their start and end apart: 15 -> 16, of which waited for: 5 -> 4; matrix products, arithmetic and copies ran while one was open for 6% -> 4% of each run, Pallas kernels for 20% -> 24%
where the time goes in v13:
time: 136 us; the launch traced here: 135 us
  starting transfers between devices  46.9 us (34%)
  waiting for transfers between devices  44.3 us (33%)
  Pallas kernels  31.9 us (23%)
  local copies, waits for them, and re-layouts  9.5 us (7%)
  other arithmetic  1.73 us (1%)
    ppermute x8, waiting for transfers between devices, local(): buffers[key] = lax.ppermute(held, both, pairs_of[key])  44.3 us
    ppermute x8, starting transfers between devices, local(): buffers[key] = lax.ppermute(held, both, pairs_of[key])  29.1 us
    pallas_call x1, Pallas kernels, early_product(): pl.pallas_call(functools.partial(early_kernel, at, candidates, len(buffer...  12 us
    ppermute x2, starting transfers between devices, sum_beside(): other = lax.ppermute(squares, 'col', [(i, i ^ bit) for i in range(cols)])  11.5 us
    pallas_call x6, Pallas kernels, relay(): pl.pallas_call(functools.partial(relay_kernel, at), out_shape=pltpu.VMEM(...  8.9 us
    pallas_call x1, Pallas kernels, last_product(): pl.pallas_call(functools.partial(last_kernel, at, candidates, scale, len(...  7.4 us
    dynamic_slice x3, local copies, waits for them, and re-layouts, own_chunk(): lax.dynamic_slice(x, (piece * piece_rows, group * group_size), (piece_row...  5.73 us
    ppermute x2, starting transfers between devices, bring_back(): lax.ppermute(buffers[key], both, returns[key])  3.93 us
  transfers between devices with their start and end apart: 16, of which 4 were waited for; matrix products, arithmetic and copies ran while one was open for 4% of the time, Pallas kernels for 24%

profile of v13, /device:TPU:0, one launch (start us, length us, event | category | flops | bytes accessed | tf_op | source)
XLA Modules:
  0.0 135.3 jit_solution(13614308153781403650)
XLA Ops:
  0.6 0.0 copy-start
  0.6 0.0 copy-start.6
  0.7 0.0 copy-start.9
  0.7 0.0 copy-start.8
  0.7 2.4 %dynamic_slice.32 = bf16[2048,256]{1,0:T(8,128)(2,1)} slice(bf16[2048,512]{1,0:T(8,128)(2,1)} %x.15), slice={[0:2048], [256:512]} | slice | bytes 2097152 | tf_op jit(solution)/shard_map/dynamic_slice | solution.py:462
  3.1 1.6 %collective-permute-start = (bf16[2048,256]{1,0:T(8,128)(2,1)}, bf16[2048,256]{1,0:T(8,128)(2,1)}, u32[]{:S(2)}, u32[]{:S(2)}) collective-permute-start(bf16[2048,256]{1,0:T(8,128)(2,1)} %dynamic_slice.32), channel_id=1, source_target_pairs={{18,2},{1,17}} | collective-permute-start | bytes 3145736 | tf_op jit(solution)/shard_map/ppermute | solution.py:537
  4.7 2.3 %constant_dynamic-slice_fusion = bf16[2048,256]{1,0:T(8,128)(2,1)} fusion(bf16[2048,512]{1,0:T(8,128)(2,1)} %x.15, s32[]{:T(128)S(6)} %select_n.38), kind=kLoop, calls=%fused_computation.13 | loop fusion | bytes 2097156 | tf_op jit(solution)/shard_map/dynamic_slice | solution.py:462
  7.0 7.7 %collective-permute-start.3 = (bf16[2048,256]{1,0:T(8,128)(2,1)}, bf16[2048,256]{1,0:T(8,128)(2,1)S(1)}, u32[]{:S(2)}, u32[]{:S(2)}) collective-permute-start(bf16[2048,256]{1,0:T(8,128)(2,1)} %constant_dynamic-slice_fusion), channel_id=1, source_target_pairs={{0,1},{1,2},{5,4},{10,11},{13,12},{14,13},{18,19},{22,21},{23,22},... | collective-permute-start | bytes 3145736 | tf_op jit(solution)/shard_map/ppermute | solution.py:533
  14.7 0.0 copy-done.6
  14.8 0.1 dynamic_slice.26
  14.9 0.1 dynamic_slice.27
  14.9 1.0 multiply_reduce_fusion
  16.0 1.1 constant_dynamic-slice_fusion.1
  17.0 1.3 collective-permute-start.1
  18.3 0.6 collective-permute-start.9
  19.0 0.7 fusion.2.table
  19.6 0.0 collective-permute-done.refs_0_
  19.6 7.6 %collective-permute-done.3.refs_1_ = bf16[2048,256]{1,0:T(8,128)(2,1)S(1)} collective-permute-done((bf16[2048,256]{1,0:T(8,128)(2,1)}, bf16[2048,256]{1,0:T(8,128)(2,1)S(1)}, u32[]{:S(2)}, u32[]{:S(2)}) %collective-permute-start.3) | collective-permute-done | bytes 1048608 | tf_op jit(solution)/shard_map/ppermute | solution.py:533
  27.3 1.3 relay.7
  28.6 1.0 copy-done.3
  29.6 12.5 %collective-permute-start.4 = (bf16[2048,256]{1,0:T(8,128)(2,1)S(1)}, bf16[2048,256]{1,0:T(8,128)(2,1)S(1)}, u32[]{:S(2)}, u32[]{:S(2)}) collective-permute-start(bf16[2048,256]{1,0:T(8,128)(2,1)S(1)} %relay.7), channel_id=1, source_target_pairs={{0,1},{1,2},{2,3},{5,4},{6,5},{9,10},{10,11},{13,12},{14,13},{15,1... | collective-permute-start | bytes 3145736 | tf_op jit(solution)/shard_map/ppermute | solution.py:533
  42.1 0.0 collective-permute-done.1.refs_1_.refs_0_
  42.1 1.6 %relay.6 = bf16[2048,256]{1,0:T(8,128)(2,1)S(1)} custom-call(s32[30]{0:T(128)S(1)} %fusion.2.table, bf16[2048,512]{1,0:T(8,128)(2,1)S(1)} %copy-done, bf16[2048,256]{1,0:T(8,128)(2,1)} %collective-permute-done.refs_0_, bf16[2048,256]{1,0:T(8,128)(2,1)} %collective-permute-done.1.refs_1_.refs_0_), custom_call_target="tpu_custom_call" | custom-call | tf_op jit(solution)/shard_map/relay/pallas_call | solution.py:182
  43.8 1.3 collective-permute-start.2
  45.1 0.0 collective-permute-done.9.refs_1_
  45.1 0.1 collective-permute-start.10
  45.1 19.6 %collective-permute-done.4.refs_0_.refs_3_.refs_1_ = bf16[2048,256]{1,0:T(8,128)(2,1)S(1)} collective-permute-done((bf16[2048,256]{1,0:T(8,128)(2,1)S(1)}, bf16[2048,256]{1,0:T(8,128)(2,1)S(1)}, u32[]{:S(2)}, u32[]{:S(2)}) %collective-permute-start.4) | collective-permute-done | bytes 1048608 | tf_op jit(solution)/shard_map/ppermute | solution.py:533
  64.8 0.6 relay.9
  65.4 1.7 %collective-permute-start.6 = (bf16[2048,256]{1,0:T(8,128)(2,1)S(1)}, bf16[2048,256]{1,0:T(8,128)(2,1)}, u32[]{:S(2)}, u32[]{:S(2)}) collective-permute-start(bf16[2048,256]{1,0:T(8,128)(2,1)S(1)} %relay.9), channel_id=1, source_target_pairs={{1,2},{2,3},{5,4},{9,10},{10,11},{13,12},{14,13},{18,19},{21,20},{... | collective-permute-start | bytes 3145736 | tf_op jit(solution)/shard_map/ppermute | solution.py:533
  67.0 3.1 %collective-permute-done.2.refs_0_.refs_2_ = bf16[2048,256]{1,0:T(8,128)(2,1)S(1)} collective-permute-done((bf16[2048,256]{1,0:T(8,128)(2,1)S(1)}, bf16[2048,256]{1,0:T(8,128)(2,1)S(1)}, u32[]{:S(2)}, u32[]{:S(2)}) %collective-permute-start.2) | collective-permute-done | bytes 1048608 | tf_op jit(solution)/shard_map/ppermute | solution.py:533
  70.1 0.6 relay.8
  70.7 0.0 copy-start.7
  70.7 1.3 collective-permute-start.5
  72.0 0.0 collective-permute-done.10.refs_2_
  72.1 0.1 collective-permute-start.11
  72.1 0.0 collective-permute-done.6.refs_0_.refs_5_.refs_3_
  72.1 1.7 %collective-permute-start.13 = (bf16[2048,256]{1,0:T(8,128)(2,1)}, bf16[2048,256]{1,0:T(8,128)(2,1)}, u32[]{:S(2)}, u32[]{:S(2)}) collective-permute-start(bf16[2048,256]{1,0:T(8,128)(2,1)} %collective-permute-done.6.refs_0_.refs_5_.refs_3_), channel_id=1, source_target_pairs={{19,3}} | collective-permute-start | bytes 3145736 | tf_op jit(solution)/shard_map/ppermute | solution.py:516
  73.8 14.0 %collective-permute-done.5.refs_0_.refs_4_.refs_2_ = bf16[2048,256]{1,0:T(8,128)(2,1)} collective-permute-done((bf16[2048,256]{1,0:T(8,128)(2,1)S(1)}, bf16[2048,256]{1,0:T(8,128)(2,1)}, u32[]{:S(2)}, u32[]{:S(2)}) %collective-permute-start.5) | collective-permute-done | bytes 1048608 | tf_op jit(solution)/shard_map/ppermute | solution.py:533
  87.8 2.3 %collective-permute-start.12 = (bf16[2048,256]{1,0:T(8,128)(2,1)}, bf16[2048,256]{1,0:T(8,128)(2,1)}, u32[]{:S(2)}, u32[]{:S(2)}) collective-permute-start(bf16[2048,256]{1,0:T(8,128)(2,1)} %collective-permute-done.5.refs_0_.refs_4_.refs_2_), channel_id=1, source_target_pairs={{0,16}} | collective-permute-start | bytes 3145736 | tf_op jit(solution)/shard_map/ppermute | solution.py:516
  90.0 2.4 %relay.11 = bf16[2048,256]{1,0:T(8,128)(2,1)} custom-call(s32[30]{0:T(128)S(1)} %fusion.2.table, bf16[2048,512]{1,0:T(8,128)(2,1)S(1)} %copy-done, bf16[2048,256]{1,0:T(8,128)(2,1)} %collective-permute-done.6.refs_0_.refs_5_.refs_3_), custom_call_target="tpu_custom_call" | custom-call | tf_op jit(solution)/shard_map/relay/pallas_call | solution.py:182
  92.4 1.6 %collective-permute-start.8 = (bf16[2048,256]{1,0:T(8,128)(2,1)}, bf16[2048,256]{1,0:T(8,128)(2,1)}, u32[]{:S(2)}, u32[]{:S(2)}) collective-permute-start(bf16[2048,256]{1,0:T(8,128)(2,1)} %relay.11), channel_id=1, source_target_pairs={{1,2},{2,3},{10,11},{13,12},{21,20},{26,27}} | collective-permute-start | bytes 3145736 | tf_op jit(solution)/shard_map/ppermute | solution.py:533
  94.1 2.3 %relay.10 = bf16[2048,256]{1,0:T(8,128)(2,1)} custom-call(s32[30]{0:T(128)S(1)} %fusion.2.table, bf16[2048,512]{1,0:T(8,128)(2,1)S(1)} %copy-done, bf16[2048,256]{1,0:T(8,128)(2,1)} %collective-permute-done.5.refs_0_.refs_4_.refs_2_), custom_call_target="tpu_custom_call" | custom-call | tf_op jit(solution)/shard_map/relay/pallas_call | solution.py:182
  96.4 1.6 %collective-permute-start.7 = (bf16[2048,256]{1,0:T(8,128)(2,1)}, bf16[2048,256]{1,0:T(8,128)(2,1)}, u32[]{:S(2)}, u32[]{:S(2)}) collective-permute-start(bf16[2048,256]{1,0:T(8,128)(2,1)} %relay.10), channel_id=1, source_target_pairs={{6,7},{9,8},{17,16},{18,17},{25,24},{30,31}} | collective-permute-start | bytes 3145736 | tf_op jit(solution)/shard_map/ppermute | solution.py:533
  98.0 0.1 fusion
  98.1 0.0 collective-permute-done.11.refs_3_
  98.1 10.8 %collective-permute-start.14 = (f32[2048]{0:T(1024)S(1)}, f32[2048]{0:T(1024)S(1)}, u32[]{:S(2)}, u32[]{:S(2)}) collective-permute-start(f32[2048]{0:T(1024)S(1)} %multiply_reduce_fusion), channel_id=1, source_target_pairs={{0,1},{1,0},{2,3},{3,2},{4,5},{5,4},{6,7},{7,6},{8,9},{9,8},{10,11... | collective-permute-start | bytes 24584 | tf_op jit(solution)/shard_map/ppermute | solution.py:507
  108.9 0.2 broadcast_in_dim.43.refs_5_
  109.1 0.2 broadcast_in_dim.42.refs_4_
  109.3 0.0 copy-start.5
  109.3 1.2 copy-done.5
  110.5 3.6 %window.1.refs_11_.refs_9_ = bf16[1024,2048]{1,0:T(8,128)(2,1)S(1)} custom-call(s32[30]{0:T(128)S(1)} %fusion.2.table, bf16[256,2048]{1,0:T(8,128)(2,1)S(1)} %copy-done.5, bf16[256,2048]{1,0:T(8,128)(2,1)} %collective-permute-done.9.refs_1_, bf16[256,2048]{1,0:T(8,128)(2,1)} %collective-permute-done.10.refs_2_, ...), custom_call_target="tpu_custom_call" | custom-call | flops 8388608 | bytes 8388608 | tf_op jit(solution)/shard_map/window/pallas_call | solution.py:220
  114.1 0.0 collective-permute-done.13.refs_7_
  114.1 0.0 collective-permute-done.12.refs_6_
  114.1 0.3 broadcast_in_dim.41.refs_10_.refs_8_
  114.4 0.0 copy-done.2
  114.5 0.0 copy-done.4
  114.5 12.0 %early.1.refs_10_ = f32[2048,2048]{1,0:T(8,128)S(1)} custom-call(s32[30]{0:T(128)S(1)} %fusion.2.table, bf16[2048,512]{1,0:T(8,128)(2,1)S(1)} %copy-done, bf16[2048,256]{1,0:T(8,128)(2,1)} %collective-permute-done.1.refs_1_.refs_0_, bf16[2048,256]{1,0:T(8,128)(2,1)S(1)} %copy-done.4, bf16[2048,256]{1,0:T(8,128)(2,1)S(1)} %copy-done.2, ...), custom_call_target="tpu_custom_call" | custom-call | flops 6442450944 | tf_op jit(solution)/shard_map/early/pallas_call | solution.py:281
  126.5 0.0 collective-permute-done.14
  126.5 0.7 collective-permute-start.15
  127.2 0.0 collective-permute-done.8.refs_5_
  127.2 0.0 collective-permute-done.7.refs_4_
  127.2 7.4 %last.1 = bf16[2048,2048]{1,0:T(8,128)(2,1)} custom-call(s32[30]{0:T(128)S(1)} %fusion.2.table, bf16[2048,512]{1,0:T(8,128)(2,1)S(1)} %copy-done, bf16[2048,256]{1,0:T(8,128)(2,1)S(1)} %copy-done.2, bf16[2048,256]{1,0:T(8,128)(2,1)S(1)} %collective-permute-done.4.refs_0_.refs_3_.refs_1_, bf16[2048,256]{1,0:T(8,128)(2,1)} %collective-permute-done.5.refs_0_.refs_4_.refs_2_, ...), custom_call_target="tpu_custom_call" | custom-call | flops 2147483648 | bytes 8388608 | tf_op jit(solution)/shard_map/last/pallas_call | solution.py:325
  134.7 0.0 collective-permute-done.15
  134.7 0.6 multiply_add_fusion
  (13 shorter events, 0.0 us)
Async XLA Ops:
  0.6 14.3 %copy-start = (bf16[2048,512]{1,0:T(8,128)(2,1)S(1)}, bf16[2048,512]{1,0:T(8,128)(2,1)}, u32[]{:S(2)}) copy-start(bf16[2048,512]{1,0:T(8,128)(2,1)} %x.15) | copy-start | bytes 6291460
  0.6 14.1 %copy-start.6 = (s32[2048]{0:T(1024)S(1)}, s32[2048]{0:T(1024)}, u32[]{:S(2)}) copy-start(s32[2048]{0:T(1024)} %param.11) | copy-start | bytes 24580
  0.7 14.1 %copy-start.9 = (f32[2048]{0:T(1024)S(1)}, f32[2048]{0:T(1024)}, u32[]{:S(2)}) copy-start(f32[2048]{0:T(1024)} %param.10) | copy-start | bytes 24580
  0.7 14.1 %copy-start.8 = (f32[2048]{0:T(1024)S(1)}, f32[2048]{0:T(1024)}, u32[]{:S(2)}) copy-start(f32[2048]{0:T(1024)} %param.9) | copy-start | bytes 24580
  3.1 16.6 %collective-permute-start = (bf16[2048,256]{1,0:T(8,128)(2,1)}, bf16[2048,256]{1,0:T(8,128)(2,1)}, u32[]{:S(2)}, u32[]{:S(2)}) collective-permute-start(bf16[2048,256]{1,0:T(8,128)(2,1)} %dynamic_slice.32), channel_id=1, source_target_pairs={{18,2},{1,17}} | collective-permute-start | bytes 3145736 | tf_op jit(solution)/shard_map/ppermute | solution.py:537
  7.0 20.3 %collective-permute-start.3 = (bf16[2048,256]{1,0:T(8,128)(2,1)}, bf16[2048,256]{1,0:T(8,128)(2,1)S(1)}, u32[]{:S(2)}, u32[]{:S(2)}) collective-permute-start(bf16[2048,256]{1,0:T(8,128)(2,1)} %constant_dynamic-slice_fusion), channel_id=1, source_target_pairs={{0,1},{1,2},{5,4},{10,11},{13,12},{14,13},{18,19},{22,21},{23,22},... | collective-permute-start | bytes 3145736 | tf_op jit(solution)/shard_map/ppermute | solution.py:533
  17.0 25.1 %collective-permute-start.1 = (bf16[2048,256]{1,0:T(8,128)(2,1)}, bf16[2048,256]{1,0:T(8,128)(2,1)}, u32[]{:S(2)}, u32[]{:S(2)}) collective-permute-start(bf16[2048,256]{1,0:T(8,128)(2,1)} %constant_dynamic-slice_fusion.1), channel_id=1, source_target_pairs={{1,0},{5,6},{6,7},{9,8},{14,15},{18,17},{19,18},{20,21},{22,23},{2... | collective-permute-start | bytes 3145736 | tf_op jit(solution)/shard_map/ppermute | solution.py:533
  18.3 26.7 %collective-permute-start.9 = (bf16[256,2048]{1,0:T(8,128)(2,1)}, bf16[256,2048]{1,0:T(8,128)(2,1)}, u32[]{:S(2)}, u32[]{:S(2)}) collective-permute-start(bf16[256,2048]{1,0:T(8,128)(2,1)} %refs_0_.1), channel_id=1, source_target_pairs={{0,28},{4,0},{8,4},{12,8},{16,12},{20,16},{24,20},{28,24},{1,29},{... | collective-permute-start | bytes 3145736 | tf_op jit(solution)/shard_map/ppermute | solution.py:486
  28.6 1.0 copy-start.3
  29.6 35.2 %collective-permute-start.4 = (bf16[2048,256]{1,0:T(8,128)(2,1)S(1)}, bf16[2048,256]{1,0:T(8,128)(2,1)S(1)}, u32[]{:S(2)}, u32[]{:S(2)}) collective-permute-start(bf16[2048,256]{1,0:T(8,128)(2,1)S(1)} %relay.7), channel_id=1, source_target_pairs={{0,1},{1,2},{2,3},{5,4},{6,5},{9,10},{10,11},{13,12},{14,13},{15,1... | collective-permute-start | bytes 3145736 | tf_op jit(solution)/shard_map/ppermute | solution.py:533
  43.8 26.3 %collective-permute-start.2 = (bf16[2048,256]{1,0:T(8,128)(2,1)S(1)}, bf16[2048,256]{1,0:T(8,128)(2,1)S(1)}, u32[]{:S(2)}, u32[]{:S(2)}) collective-permute-start(bf16[2048,256]{1,0:T(8,128)(2,1)S(1)} %relay.6), channel_id=1, source_target_pairs={{1,0},{2,1},{4,5},{5,6},{6,7},{9,8},{10,9},{13,14},{14,15},{17,16}... | collective-permute-start | bytes 3145736 | tf_op jit(solution)/shard_map/ppermute | solution.py:533
  45.1 27.0 %collective-permute-start.10 = (bf16[256,2048]{1,0:T(8,128)(2,1)}, bf16[256,2048]{1,0:T(8,128)(2,1)}, u32[]{:S(2)}, u32[]{:S(2)}) collective-permute-start(bf16[256,2048]{1,0:T(8,128)(2,1)} %collective-permute-done.9.refs_1_), channel_id=1, source_target_pairs={{0,28},{4,0},{8,4},{12,8},{16,12},{20,16},{24,20},{28,24},{1,29},{... | collective-permute-start | bytes 3145736 | tf_op jit(solution)/shard_map/ppermute | solution.py:486
  65.4 6.7 %collective-permute-start.6 = (bf16[2048,256]{1,0:T(8,128)(2,1)S(1)}, bf16[2048,256]{1,0:T(8,128)(2,1)}, u32[]{:S(2)}, u32[]{:S(2)}) collective-permute-start(bf16[2048,256]{1,0:T(8,128)(2,1)S(1)} %relay.9), channel_id=1, source_target_pairs={{1,2},{2,3},{5,4},{9,10},{10,11},{13,12},{14,13},{18,19},{21,20},{... | collective-permute-start | bytes 3145736 | tf_op jit(solution)/shard_map/ppermute | solution.py:533
  70.1 22.3 %copy-start.1 = (bf16[2048,256]{1,0:T(8,128)(2,1)}, bf16[2048,256]{1,0:T(8,128)(2,1)S(1)}, u32[]{:S(2)}) copy-start(bf16[2048,256]{1,0:T(8,128)(2,1)S(1)} %collective-permute-done.2.refs_0_.refs_2_) | copy-start | bytes 3145732
  70.7 27.3 %copy-start.7 = (s32[2048]{0:T(1024)S(1)}, s32[2048]{0:T(1024)}, u32[]{:S(2)}) copy-start(s32[2048]{0:T(1024)} %param.12) | copy-start | bytes 24580
  70.7 17.0 %collective-permute-start.5 = (bf16[2048,256]{1,0:T(8,128)(2,1)S(1)}, bf16[2048,256]{1,0:T(8,128)(2,1)}, u32[]{:S(2)}, u32[]{:S(2)}) collective-permute-start(bf16[2048,256]{1,0:T(8,128)(2,1)S(1)} %relay.8), channel_id=1, source_target_pairs={{1,0},{5,6},{6,7},{9,8},{10,9},{14,15},{17,16},{18,17},{22,23},{25... | collective-permute-start | bytes 3145736 | tf_op jit(solution)/shard_map/ppermute | solution.py:533
  72.1 26.0 %collective-permute-start.11 = (bf16[256,2048]{1,0:T(8,128)(2,1)}, bf16[256,2048]{1,0:T(8,128)(2,1)}, u32[]{:S(2)}, u32[]{:S(2)}) collective-permute-start(bf16[256,2048]{1,0:T(8,128)(2,1)} %collective-permute-done.10.refs_2_), channel_id=1, source_target_pairs={{0,28},{4,0},{8,4},{12,8},{16,12},{20,16},{24,20},{28,24},{1,29},{... | collective-permute-start | bytes 3145736 | tf_op jit(solution)/shard_map/ppermute | solution.py:486
  72.1 42.0 %collective-permute-start.13 = (bf16[2048,256]{1,0:T(8,128)(2,1)}, bf16[2048,256]{1,0:T(8,128)(2,1)}, u32[]{:S(2)}, u32[]{:S(2)}) collective-permute-start(bf16[2048,256]{1,0:T(8,128)(2,1)} %collective-permute-done.6.refs_0_.refs_5_.refs_3_), channel_id=1, source_target_pairs={{19,3}} | collective-permute-start | bytes 3145736 | tf_op jit(solution)/shard_map/ppermute | solution.py:516
  87.8 26.4 %collective-permute-start.12 = (bf16[2048,256]{1,0:T(8,128)(2,1)}, bf16[2048,256]{1,0:T(8,128)(2,1)}, u32[]{:S(2)}, u32[]{:S(2)}) collective-permute-start(bf16[2048,256]{1,0:T(8,128)(2,1)} %collective-permute-done.5.refs_0_.refs_4_.refs_2_), channel_id=1, source_target_pairs={{0,16}} | collective-permute-start | bytes 3145736 | tf_op jit(solution)/shard_map/ppermute | solution.py:516
  92.4 34.8 %collective-permute-start.8 = (bf16[2048,256]{1,0:T(8,128)(2,1)}, bf16[2048,256]{1,0:T(8,128)(2,1)}, u32[]{:S(2)}, u32[]{:S(2)}) collective-permute-start(bf16[2048,256]{1,0:T(8,128)(2,1)} %relay.11), channel_id=1, source_target_pairs={{1,2},{2,3},{10,11},{13,12},{21,20},{26,27}} | collective-permute-start | bytes 3145736 | tf_op jit(solution)/shard_map/ppermute | solution.py:533
  96.4 30.9 %collective-permute-start.7 = (bf16[2048,256]{1,0:T(8,128)(2,1)}, bf16[2048,256]{1,0:T(8,128)(2,1)}, u32[]{:S(2)}, u32[]{:S(2)}) collective-permute-start(bf16[2048,256]{1,0:T(8,128)(2,1)} %relay.10), channel_id=1, source_target_pairs={{6,7},{9,8},{17,16},{18,17},{25,24},{30,31}} | collective-permute-start | bytes 3145736 | tf_op jit(solution)/shard_map/ppermute | solution.py:533
  98.1 28.4 %collective-permute-start.14 = (f32[2048]{0:T(1024)S(1)}, f32[2048]{0:T(1024)S(1)}, u32[]{:S(2)}, u32[]{:S(2)}) collective-permute-start(f32[2048]{0:T(1024)S(1)} %multiply_reduce_fusion), channel_id=1, source_target_pairs={{0,1},{1,0},{2,3},{3,2},{4,5},{5,4},{6,7},{7,6},{8,9},{9,8},{10,11... | collective-permute-start | bytes 24584 | tf_op jit(solution)/shard_map/ppermute | solution.py:507
  109.3 1.2 copy-start.5
  110.5 3.9 %copy-start.2 = (bf16[2048,256]{1,0:T(8,128)(2,1)S(1)}, bf16[2048,256]{1,0:T(8,128)(2,1)}, u32[]{:S(2)}) copy-start(bf16[2048,256]{1,0:T(8,128)(2,1)} %copy-done.1) | copy-start | bytes 3145732
  110.5 3.9 %copy-start.4 = (bf16[2048,256]{1,0:T(8,128)(2,1)S(1)}, bf16[2048,256]{1,0:T(8,128)(2,1)}, u32[]{:S(2)}) copy-start(bf16[2048,256]{1,0:T(8,128)(2,1)} %copy-done.3) | copy-start | bytes 3145732
  126.5 8.1 %collective-permute-start.15 = (f32[2048]{0:T(1024)S(1)}, f32[2048]{0:T(1024)S(1)}, u32[]{:S(2)}, u32[]{:S(2)}) collective-permute-start(f32[2048]{0:T(1024)S(1)} %add.39), channel_id=1, source_target_pairs={{0,2},{1,3},{2,0},{3,1},{4,6},{5,7},{6,4},{7,5},{8,10},{9,11},{10,... | collective-permute-start | bytes 24584 | tf_op jit(solution)/shard_map/ppermute | solution.py:507

commit v14 on v0

v14 whole, which is shorter than its diff:
```python
import functools

import jax
import jax.numpy as jnp
import numpy as np
from jax import lax
from jax.experimental import pallas as pl
from jax.experimental.pallas import tpu as pltpu
from jax.sharding import PartitionSpec as P

STEPS = 4
EARLY = 3
DRAWS = 400
COL_TILE = 512
ROW_BLOCK = 512
ROW_TILE = 32
LANES = 128
VMEM_LIMIT = 10 * 2**20
RELAY_LIMIT = 2 * 2**20


def exchange(own):
    cols = len(own)
    rng = np.random.RandomState(0)
    best = None
    for _ in range(DRAWS):
        held = [set(o) for o in own]
        rounds, hops = [], 0
        while any(len(h) < STEPS for h in held):
            before = [set(h) for h in held]
            sends, busy = {}, set()
            draw = rng.rand(cols)
            for c in sorted(range(cols), key=lambda c: (len(before[c]), draw[c])):
                choices = []
                for other in range(cols):
                    if other not in sends:
                        for step in before[other] - before[c]:
                            rare = sum(step in h for h in before)
                            choices.append((rare + rng.rand() * 2, abs(other - c), other, step))
                if choices and c not in busy:
                    _, far, other, step = min(choices)
                    sends[other] = c, step
                    busy.add(c)
                    held[c].add(step)
                    hops += far
            rounds.append(sends)
        if best is None or (len(rounds), hops) < best[0]:
            best = (len(rounds), hops), rounds
    return best[1]


def lookup(values, device):
    known = [v for v in values if v is not None]
    if len(set(known)) <= 1:
        return known[0] if known else 0
    values = [known[0] if v is None else v for v in values]
    result = jnp.uint32(0)
    place = (device % 32).astype(jnp.uint32)
    for bit in range(max(values).bit_length()):
        ones = [v >> bit & 1 for v in values]
        words = [sum(b << i for i, b in enumerate(ones[at : at + 32])) for at in range(0, len(ones), 32)]
        word = jnp.uint32(words[0])
        for i, other in enumerate(words[1:], 1):
            word = jnp.where(device // 32 == i, jnp.uint32(other), word)
        result = result | (((word >> place) & jnp.uint32(1)) << jnp.uint32(bit))
    return result.astype(jnp.int32)


def relay_kernel(at, table, x, *refs):
    *sources, out = refs
    rows, width = out.shape

    @pl.when(table[at] == 0)
    def _():
        col = pl.multiple_of(table[at + 1] * width, width)
        out[...] = x[:, pl.ds(col, width)]

    for i, source in enumerate(sources):

        @pl.when(table[at] == i + 1)
        def _(source=source):
            out[...] = source[...]


def relay(at, table, x, sources):
    return pl.pallas_call(
        functools.partial(relay_kernel, at),
        out_shape=pltpu.VMEM(sources[0].shape, sources[0].dtype),
        in_specs=[pl.BlockSpec(memory_space=pltpu.SMEM)] + [VMEM] * (1 + len(sources)),
        out_specs=VMEM,
        compiler_params=pltpu.CompilerParams(vmem_limit_bytes=RELAY_LIMIT),
        cost_estimate=pl.CostEstimate(flops=0, bytes_accessed=0, transcendentals=0),
        name="relay",
    )(table, *[in_vmem(v) for v in (x, *sources)])


def in_vmem(value):
    return pltpu.with_memory_space_constraint(value, pltpu.VMEM)


VMEM = pl.BlockSpec(memory_space=pltpu.VMEM)


def window_kernel(at, table, *refs):
    blocks = refs[:STEPS]
    factor, twice, male, out = refs[STEPS:]
    group_size, width = blocks[0].shape
    for s, block in enumerate(blocks):
        rank = table[at + s]

        @pl.loop(0, group_size // ROW_TILE)
        def _(i, s=s, block=block, rank=rank):
            here = pl.ds(pl.multiple_of(i * ROW_TILE, ROW_TILE), ROW_TILE)
            rows = pl.ds(pl.multiple_of(s * group_size + i * ROW_TILE, ROW_TILE), ROW_TILE)
            to = pl.ds(pl.multiple_of(rank * group_size + i * ROW_TILE, ROW_TILE), ROW_TILE)
            for k in range(0, width, LANES):
                value = block[here, k : k + LANES].astype(jnp.float32) - twice[rows, :]
                out[to, k : k + LANES] = (value * factor[rows, :] * male[:, k : k + LANES]).astype(out.dtype)


def standardized_window(at, table, blocks, factor, twice, male):
    group_size, n = blocks[0].shape
    depth = STEPS * group_size
    return pl.pallas_call(
        functools.partial(window_kernel, at),
        out_shape=pltpu.VMEM((depth, n), jnp.bfloat16),
        in_specs=[pl.BlockSpec(memory_space=pltpu.SMEM)] + [VMEM] * (STEPS + 3),
        out_specs=VMEM,
        compiler_params=pltpu.CompilerParams(vmem_limit_bytes=VMEM_LIMIT),
        cost_estimate=pl.CostEstimate(flops=4 * depth * n, bytes_accessed=4 * depth * n, transcendentals=0),
        name="window",
    )(table, *[in_vmem(v) for v in (*blocks, factor, twice, male)])


def standardize(table, at, candidates, x, buffers, factor, twice, male, zx, columns, first, count):
    width = columns.stop - columns.start
    place, step = table[at], table[at + 1]

    def from_source(source, col):
        @pl.loop(0, count // ROW_TILE)
        def _(i):
            here = pl.ds(pl.multiple_of(first + i * ROW_TILE, ROW_TILE), ROW_TILE)
            to = pl.ds(pl.multiple_of(i * ROW_TILE, ROW_TILE), ROW_TILE)
            for k in range(0, width, LANES):
                lanes = pl.ds(pl.multiple_of(step * width + k, LANES), LANES)
                value = source[here, pl.ds(pl.multiple_of(col + k, LANES), LANES)].astype(jnp.float32)
                value = (value - twice[:, lanes]) * factor[:, lanes] * male[here, :]
                zx[to, columns.start + k : columns.start + k + LANES] = value.astype(zx.dtype)

    for number in candidates:
        if number >= 0:

            @pl.when(place == number)
            def _(number=number):
                from_source(buffers[number], 0)

        else:

            @pl.when(place < 0)
            def _():
                from_source(x, (-1 - place) * width)


def early_kernel(at, candidates, n_buffers, table, x, *refs):
    buffers = refs[:n_buffers]
    factor, twice, male, zy, total, zx = refs[n_buffers:]
    rows, depth = zx.shape
    width = depth // EARLY
    for rank in range(EARLY):
        columns = slice(rank * width, (rank + 1) * width)
        standardize(table, at + 2 * rank, candidates[rank], x, buffers, factor, twice, male, zx, columns, 0, rows)

    @pl.loop(0, rows // ROW_BLOCK)
    def _(i):
        block = pl.ds(pl.multiple_of(i * ROW_BLOCK, ROW_BLOCK), ROW_BLOCK)
        for j in range(0, total.shape[1], COL_TILE):
            right = zy[:depth, j : j + COL_TILE]
            total[block, j : j + COL_TILE] = jnp.dot(zx[block, :], right, preferred_element_type=jnp.float32)


def early_product(at, candidates, table, x, buffers, factor, twice, male, zy):
    rows, (depth, n) = x.shape[0], zy.shape
    depth = depth // STEPS * EARLY
    args = [in_vmem(v) for v in (x, *buffers, factor, twice, male, zy)]
    return pl.pallas_call(
        functools.partial(early_kernel, at, candidates, len(buffers)),
        out_shape=pltpu.VMEM((rows, n), jnp.float32),
        in_specs=[pl.BlockSpec(memory_space=pltpu.SMEM)] + [VMEM] * len(args),
        out_specs=VMEM,
        scratch_shapes=[pltpu.VMEM((rows, depth), jnp.bfloat16)],
        compiler_params=pltpu.CompilerParams(vmem_limit_bytes=VMEM_LIMIT),
        cost_estimate=pl.CostEstimate(flops=2 * rows * depth * n, bytes_accessed=0, transcendentals=0),
        name="early",
    )(table, *args)


def last_kernel(at, candidates, scale, n_buffers, table, x, *refs):
    buffers = refs[:n_buffers]
    factor, twice, male, zy, total, out, zx, blocks, sems = refs[n_buffers:]
    rows, n = total.shape
    depth = zx.shape[1]
    width = depth // (STEPS - EARLY)

    def copy(i):
        return pltpu.make_async_copy(blocks.at[i % 2], out.at[pl.ds(i * ROW_BLOCK, ROW_BLOCK), :], sems.at[i % 2])

    count = rows // ROW_BLOCK
    for i in range(count):
        first = i * ROW_BLOCK
        for rank in range(STEPS - EARLY):
            columns = slice(rank * width, (rank + 1) * width)
            standardize(
                table,
                at + 2 * rank,
                candidates[rank],
                x,
                buffers,
                factor,
                twice,
                male,
                zx,
                columns,
                first,
                ROW_BLOCK,
            )
        if i >= 2:
            copy(i - 2).wait()
        for j in range(0, n, COL_TILE):
            right = zy[zy.shape[0] - depth :, j : j + COL_TILE]
            product = jnp.dot(zx[...], right, preferred_element_type=jnp.float32)
            product = product + total[first : first + ROW_BLOCK, j : j + COL_TILE]
            blocks[i % 2, :, j : j + COL_TILE] = (product * scale).astype(blocks.dtype)
        copy(i).start()
    for i in range(max(count - 2, 0), count):
        copy(i).wait()


def last_product(at, candidates, table, x, buffers, factor, twice, male, zy, total):
    rows, (depth, n) = x.shape[0], zy.shape
    width = depth // STEPS * (STEPS - EARLY)
    scale = float(1.0 / np.sqrt(np.float32(depth)))
    args = [in_vmem(v) for v in (x, *buffers, factor, twice, male, zy, total)]
    return pl.pallas_call(
        functools.partial(last_kernel, at, candidates, scale, len(buffers)),
        out_shape=jax.ShapeDtypeStruct((rows, n), jnp.bfloat16),
        in_specs=[pl.BlockSpec(memory_space=pltpu.SMEM)] + [VMEM] * len(args),
        out_specs=pl.BlockSpec(memory_space=pl.ANY),
        scratch_shapes=[
            pltpu.VMEM((ROW_BLOCK, width), jnp.bfloat16),
            pltpu.VMEM((2, ROW_BLOCK, n), jnp.bfloat16),
            pltpu.SemaphoreType.DMA((2,)),
        ],
        compiler_params=pltpu.CompilerParams(vmem_limit_bytes=VMEM_LIMIT),
        cost_estimate=pl.CostEstimate(flops=2 * rows * width * n, bytes_accessed=2 * rows * n, transcendentals=0),
        name="last",
    )(table, *args)


def local(rows, cols, x, y, freq, weight, sex_rows, sex_cols):
    group_size = y.shape[0]
    local_vars = x.shape[1]
    groups_here = local_vars // group_size
    devices = [(r, c) for r in range(rows) for c in range(cols)]

    row_place = lax.axis_index("row")
    col_place = lax.axis_index("col")
    device = row_place * cols + col_place

    def group_here(r, s):
        return (r + s) % rows % groups_here

    def owner(r, s):
        return (r + s) % rows // groups_here

    plans = [exchange([[s for s in range(STEPS) if owner(r, s) == c] for c in range(cols)]) for r in range(rows)]
    rounds = max(len(plan) for plan in plans)
    arrival = {}
    for r, plan in enumerate(plans):
        for t, sends in enumerate(plan, 1):
            for receiver, s in sends.values():
                arrival[r, receiver, s] = t

    columns = []

    def add(entries):
        columns.append(np.asarray(entries, np.int32))
        return sum(c.shape[1] for c in columns[:-1])

    pairs_of, own_of, relays = {}, {}, {}
    for t in range(1, rounds + 1):
        pairs, own, came = [], [], []
        for r, c in devices:
            receiver, s = plans[r][t - 1].get(c, (None, None)) if t <= len(plans[r]) else (None, None)
            if s is not None:
                pairs.append((r * cols + c, r * cols + receiver))
            mine = s is not None and owner(r, s) == c
            own.append(group_here(r, s) if mine else None)
            came.append(None if s is None or mine else arrival[r, c, s])
        pairs_of[t], own_of[t] = pairs, own
        names = sorted(set(came) - {None})
        if names:
            entries = [(0, g) if g is not None else (1 + (names.index(n) if n else 0), 0) for g, n in zip(own, came)]
            relays[t] = names, add(entries)

    order = []
    for r, c in devices:
        arrivals = []
        for s in range(STEPS):
            t = arrival.get((r, c, s), 0)
            arrivals.append((t, s, t if t else -1 - group_here(r, s)))
        order.append(sorted(arrivals, key=lambda a: a[:2]))
    rank_at = add([[[a[1] for a in arrivals].index(s) for s in range(STEPS)] for arrivals in order])
    used, candidates, source_at = [], [], []
    for ranks in (range(EARLY), range(EARLY, STEPS)):
        used.append(sorted({arrivals[k][2] for arrivals in order for k in ranks if arrivals[k][2] > 0}))
        places = [[used[-1].index(a[k][2]) if a[k][2] > 0 else a[k][2] for k in ranks] for a in order]
        candidates.append([sorted({max(p[i], -1) for p in places}) for i in range(len(ranks))])
        source_at.append(add([[n for p, k in zip(row, ranks) for n in (p, a[k][1])] for row, a in zip(places, order)]))
    table = np.concatenate(columns, axis=1)
    table = lax.dynamic_slice(jnp.asarray(table), (device, 0), (1, table.shape[1]))[0]

    factor = weight / jnp.sqrt(2.0 * freq * (1.0 - freq))
    twice = 2.0 * freq
    male_scale = np.float32(np.sqrt(0.5))
    male_rows = jnp.where(sex_rows > 0, male_scale, np.float32(1.0))
    male_cols = jnp.where(sex_cols > 0, male_scale, np.float32(1.0))
    wide = lambda value: jnp.broadcast_to(value[:, None], (value.shape[0], LANES))

    def in_window(value):
        span = STEPS * group_size
        return lax.dynamic_slice(jnp.concatenate([value, value]), (row_place * group_size,), (span,))

    window_factor, window_twice = in_window(factor), in_window(twice)
    male_wide = wide(male_rows)

    def own_squares():
        here = lambda value: lax.dynamic_slice(value, (col_place * local_vars,), (local_vars,))[None, :]
        zx = ((x.astype(jnp.float32) - here(twice)) * here(factor) * male_rows[:, None]).astype(jnp.bfloat16)
        return jnp.sum(jnp.square(zx.astype(jnp.float32)), axis=1)

    back = [(i, (i - 1) % rows) for i in range(rows)]
    window = [y]
    while len(window) < STEPS:
        window.append(lax.ppermute(window[-1], "row", back))
    squares = own_squares()

    def col_sum_beside(value, squares):
        if cols & (cols - 1):
            return value, lax.psum(squares, "col")
        parts = [squares]
        for mask in range(1, cols):
            parts.append(lax.ppermute(squares, "col", [(i, i ^ mask) for i in range(cols)]))
        value, *parts = lax.optimization_barrier((value, *parts))
        while len(parts) > 1:
            parts = [a + b for a, b in zip(parts[::2], parts[1::2])]
        return value, parts[0]

    buffers = {}
    for t in range(1, rounds + 1):
        if t == 2:
            table, squares = lax.optimization_barrier((table, squares))
        if t in relays:
            names, at = relays[t]
            held = relay(at, table, x, [buffers[n] for n in names])
        else:
            start = (0, lookup(own_of[t], device) * group_size)
            held = lax.dynamic_slice(x, start, (x.shape[0], group_size))
        buffers[t] = lax.ppermute(held, ("row", "col"), pairs_of[t])
    zy = standardized_window(rank_at, table, window, wide(window_factor), wide(window_twice), male_cols[None, :])
    shared = window_factor[None, :], window_twice[None, :], male_wide, zy
    total = early_product(source_at[0], candidates[0], table, x, [buffers[k] for k in used[0]], *shared)
    total, squares = lax.optimization_barrier((total, squares))
    relation = last_product(source_at[1], candidates[1], table, x, [buffers[k] for k in used[1]], *shared, total)
    relation, squares = col_sum_beside(relation, squares)
    inbreeding = squares / jnp.float32(freq.shape[0]) - 1.0
    return relation, inbreeding


def solution(mesh):
    rows, cols = mesh.shape["row"], mesh.shape["col"]
    return jax.shard_map(
        functools.partial(local, rows, cols),
        mesh=mesh,
        in_specs=(P("row", "col"), P("row", "col"), P(), P(), P("row"), P("col")),
        out_specs=(P("row", "col"), P("row")),
        check_vma=False,
    )
```

time: 228 us -> 138 us (0.61)
  the two profiles are of different devices: /device:TPU:0 before, /device:TPU:20 now
where the time goes in v14:
time: 138 us; the launch traced here: 137 us
  waiting for transfers between devices  83.8 us (61%)
  Pallas kernels  22.9 us (17%)
  starting transfers between devices  18.6 us (13%)
  local copies, waits for them, and re-layouts  6.22 us (5%)
  other arithmetic  4.64 us (3%)
    ppermute x4, waiting for transfers between devices, local(): buffers[t] = lax.ppermute(held, ('row', 'col'), pairs_of[t])  83.8 us
    ppermute x4, starting transfers between devices, local(): buffers[t] = lax.ppermute(held, ('row', 'col'), pairs_of[t])  14.3 us
    pallas_call x1, Pallas kernels, early_product(): pl.pallas_call(functools.partial(early_kernel, at, candidates, len(buffer...  10 us
    pallas_call x1, Pallas kernels, last_product(): pl.pallas_call(functools.partial(last_kernel, at, candidates, scale, len(...  6.42 us
    pallas_call x1, Pallas kernels, standardized_window(): pl.pallas_call(functools.partial(window_kernel, at), out_shape=pltpu.VMEM...  3.56 us
    ppermute x3, starting transfers between devices, col_sum_beside(): lax.ppermute(squares, 'col', [(i, i ^ mask) for i in range(cols)])  3.55 us
    pallas_call x3, Pallas kernels, relay(): pl.pallas_call(functools.partial(relay_kernel, at), out_shape=pltpu.VMEM(...  2.87 us
  transfers between devices with their start and end apart: 10, of which 3 were waited for; matrix products, arithmetic and copies ran while one was open for 4% of the time, Pallas kernels for 17%

profile of v14, /device:TPU:20, one launch (start us, length us, event | category | flops | bytes accessed | tf_op | source)
XLA Modules:
  0.0 137.0 jit_solution(2118250495020349464)
XLA Ops:
  0.6 0.0 copy-start
  0.7 2.4 %constant_dynamic-slice_fusion = bf16[2048,256]{1,0:T(8,128)(2,1)} fusion(bf16[2048,512]{1,0:T(8,128)(2,1)} %x.9, s32[]{:T(128)S(6)} %select_n.32), kind=kLoop, calls=%fused_computation.14 | loop fusion | bytes 2097156 | tf_op jit(solution)/shard_map/dynamic_slice | solution.py:367
  3.1 2.4 %collective-permute-start = (bf16[2048,256]{1,0:T(8,128)(2,1)}, bf16[2048,256]{1,0:T(8,128)(2,1)S(1)}, u32[]{:S(2)}, u32[]{:S(2)}) collective-permute-start(bf16[2048,256]{1,0:T(8,128)(2,1)} %constant_dynamic-slice_fusion), channel_id=1, source_target_pairs={{0,2},{1,3},{4,5},{5,6},{6,7},{9,8},{10,11},{13,15},{14,13},{15,12... | collective-permute-start | bytes 3145736 | tf_op jit(solution)/shard_map/ppermute | solution.py:368
  5.5 0.6 collective-permute-start.4
  6.1 0.7 broadcast_multiply_fusion
  6.9 0.1 dynamic_slice.19
  6.9 0.1 dynamic_slice.20
  7.0 0.7 dynamic-slice_bitcast_fusion.table
  7.7 0.7 compare_select_fusion.1
  8.4 2.5 %multiply_reduce_fusion = f32[2048]{0:T(1024)S(1)} fusion(bf16[2048,512]{1,0:T(8,128)(2,1)} %x.9, f32[2048]{0:T(1024)S(1)} %compare_select_fusion.1, f32[512]{0:T(512)S(1)} %dynamic_slice.20, f32[512]{0:T(512)S(1)} %dynamic_slice.19), kind=kLoop, calls=%fused_computation | loop fusion | flops 8386560 | bytes 2117632 | tf_op jit(solution)/shard_map/reduce_sum | solution.py:339
  10.9 50.8 %collective-permute-done.refs_0_ = bf16[2048,256]{1,0:T(8,128)(2,1)S(1)} collective-permute-done((bf16[2048,256]{1,0:T(8,128)(2,1)}, bf16[2048,256]{1,0:T(8,128)(2,1)S(1)}, u32[]{:S(2)}, u32[]{:S(2)}) %collective-permute-start) | collective-permute-done | bytes 1048608 | tf_op jit(solution)/shard_map/ppermute | solution.py:368
  61.7 0.0 copy-done
  61.7 0.6 relay.3
  62.4 4.3 %collective-permute-start.1 = (bf16[2048,256]{1,0:T(8,128)(2,1)S(1)}, bf16[2048,256]{1,0:T(8,128)(2,1)S(1)}, u32[]{:S(2)}, u32[]{:S(2)}) collective-permute-start(bf16[2048,256]{1,0:T(8,128)(2,1)S(1)} %relay.3), channel_id=1, source_target_pairs={{0,1},{1,2},{2,3},{3,0},{4,6},{5,4},{6,7},{7,5},{8,10},{9,11},{10,... | collective-permute-start | bytes 3145736 | tf_op jit(solution)/shard_map/ppermute | solution.py:368
  66.7 0.0 collective-permute-done.4.refs_1_
  66.7 0.1 collective-permute-start.5
  66.7 12.3 %collective-permute-done.1.refs_1_.refs_0_ = bf16[2048,256]{1,0:T(8,128)(2,1)S(1)} collective-permute-done((bf16[2048,256]{1,0:T(8,128)(2,1)S(1)}, bf16[2048,256]{1,0:T(8,128)(2,1)S(1)}, u32[]{:S(2)}, u32[]{:S(2)}) %collective-permute-start.1) | collective-permute-done | bytes 1048608 | tf_op jit(solution)/shard_map/ppermute | solution.py:368
  79.1 0.0 copy-start.1
  79.1 0.6 relay.4
  79.7 0.0 copy-start.6
  79.7 4.3 %collective-permute-start.2 = (bf16[2048,256]{1,0:T(8,128)(2,1)S(1)}, bf16[2048,256]{1,0:T(8,128)(2,1)S(1)}, u32[]{:S(2)}, u32[]{:S(2)}) collective-permute-start(bf16[2048,256]{1,0:T(8,128)(2,1)S(1)} %relay.4), channel_id=1, source_target_pairs={{0,2},{1,0},{2,3},{5,7},{6,4},{8,9},{9,8},{10,11},{11,10},{12,13},... | collective-permute-start | bytes 3145736 | tf_op jit(solution)/shard_map/ppermute | solution.py:368
  84.0 0.0 collective-permute-done.5.refs_2_
  84.0 0.1 collective-permute-start.6
  84.1 20.7 %collective-permute-done.2.refs_2_.refs_1_ = bf16[2048,256]{1,0:T(8,128)(2,1)S(1)} collective-permute-done((bf16[2048,256]{1,0:T(8,128)(2,1)S(1)}, bf16[2048,256]{1,0:T(8,128)(2,1)S(1)}, u32[]{:S(2)}, u32[]{:S(2)}) %collective-permute-start.2) | collective-permute-done | bytes 1048608 | tf_op jit(solution)/shard_map/ppermute | solution.py:368
  104.8 1.6 %relay.5 = bf16[2048,256]{1,0:T(8,128)(2,1)} custom-call(s32[18]{0:T(128)S(1)} %dynamic-slice_bitcast_fusion.table, bf16[2048,512]{1,0:T(8,128)(2,1)S(1)} %copy-done, bf16[2048,256]{1,0:T(8,128)(2,1)S(1)} %collective-permute-done.refs_0_, bf16[2048,256]{1,0:T(8,128)(2,1)S(1)} %collective-permute-done.1.refs_1_.refs_0_, ...), custom_call_target="tpu_custom_call" | custom-call | tf_op jit(solution)/shard_map/relay/pallas_call | solution.py:86
  106.4 0.0 copy-done.1
  106.4 0.0 copy-start.3
  106.4 1.0 copy-done.3
  107.4 3.3 %collective-permute-start.3 = (bf16[2048,256]{1,0:T(8,128)(2,1)}, bf16[2048,256]{1,0:T(8,128)(2,1)}, u32[]{:S(2)}, u32[]{:S(2)}) collective-permute-start(bf16[2048,256]{1,0:T(8,128)(2,1)} %relay.5), channel_id=1, source_target_pairs={{0,1},{2,3},{3,2},{5,4},{6,7},{7,6},{9,8},{10,11},{13,12},{14,15},... | collective-permute-start | bytes 3145736 | tf_op jit(solution)/shard_map/ppermute | solution.py:368
  110.7 0.1 fusion
  110.8 0.0 copy-done.6
  110.8 0.0 collective-permute-done.6.refs_3_
  110.8 0.2 broadcast_in_dim.43.refs_5_
  111.0 0.2 broadcast_in_dim.42.refs_4_
  111.2 0.0 copy-start.5
  111.2 1.2 copy-done.5
  112.5 0.0 copy-start.2
  112.5 0.0 copy-start.4
  112.5 3.6 %window.1.refs_6_ = bf16[1024,2048]{1,0:T(8,128)(2,1)S(1)} custom-call(s32[18]{0:T(128)S(1)} %dynamic-slice_bitcast_fusion.table, bf16[256,2048]{1,0:T(8,128)(2,1)S(1)} %copy-done.5, bf16[256,2048]{1,0:T(8,128)(2,1)} %collective-permute-done.4.refs_1_, bf16[256,2048]{1,0:T(8,128)(2,1)} %collective-permute-done.5.refs_2_, ...), custom_call_target="tpu_custom_call" | custom-call | flops 8388608 | bytes 8388608 | tf_op jit(solution)/shard_map/window/pallas_call | solution.py:124
  116.0 0.3 broadcast_in_dim.41.refs_5_
  116.4 0.0 copy-done.2
  116.4 0.0 copy-done.4
  116.4 10.0 %early.1.refs_7_ = f32[2048,2048]{1,0:T(8,128)S(1)} custom-call(s32[18]{0:T(128)S(1)} %dynamic-slice_bitcast_fusion.table, bf16[2048,512]{1,0:T(8,128)(2,1)S(1)} %copy-done, bf16[2048,256]{1,0:T(8,128)(2,1)S(1)} %collective-permute-done.refs_0_, bf16[2048,256]{1,0:T(8,128)(2,1)S(1)} %copy-done.2, bf16[2048,256]{1,0:T(8,128)(2,1)S(1)} %copy-done.4, ...), custom_call_target="tpu_custom_call" | custom-call | flops 6442450944 | tf_op jit(solution)/shard_map/early/pallas_call | solution.py:185
  126.4 0.1 collective-permute-start.9
  126.5 0.8 collective-permute-start.8
  127.2 2.7 %collective-permute-start.7 = (f32[2048]{0:T(1024)S(1)}, f32[2048]{0:T(1024)S(1)}, u32[]{:S(2)}, u32[]{:S(2)}) collective-permute-start(f32[2048]{0:T(1024)S(1)} %multiply_reduce_fusion), channel_id=1, source_target_pairs={{0,1},{1,0},{2,3},{3,2},{4,5},{5,4},{6,7},{7,6},{8,9},{9,8},{10,11... | collective-permute-start | bytes 24584 | tf_op jit(solution)/shard_map/ppermute | solution.py:352
  130.0 0.0 collective-permute-done.3.refs_2_
  130.0 6.4 %last.1 = bf16[2048,2048]{1,0:T(8,128)(2,1)} custom-call(s32[18]{0:T(128)S(1)} %dynamic-slice_bitcast_fusion.table, bf16[2048,512]{1,0:T(8,128)(2,1)S(1)} %copy-done, bf16[2048,256]{1,0:T(8,128)(2,1)S(1)} %copy-done.2, bf16[2048,256]{1,0:T(8,128)(2,1)S(1)} %copy-done.4, bf16[2048,256]{1,0:T(8,128)(2,1)} %collective-permute-done.3.refs_2_, ...), custom_call_target="tpu_custom_call" | custom-call | flops 2147483648 | bytes 8388608 | tf_op jit(solution)/shard_map/last/pallas_call | solution.py:243
  136.4 0.0 collective-permute-done.9
  136.4 0.0 collective-permute-done.8
  136.4 0.0 collective-permute-done.7
  136.4 0.6 multiply_add_fusion
  (1 shorter events, 0.0 us)
Async XLA Ops:
  0.6 61.1 %copy-start = (bf16[2048,512]{1,0:T(8,128)(2,1)S(1)}, bf16[2048,512]{1,0:T(8,128)(2,1)}, u32[]{:S(2)}) copy-start(bf16[2048,512]{1,0:T(8,128)(2,1)} %x.9) | copy-start | bytes 6291460
  3.1 58.7 %collective-permute-start = (bf16[2048,256]{1,0:T(8,128)(2,1)}, bf16[2048,256]{1,0:T(8,128)(2,1)S(1)}, u32[]{:S(2)}, u32[]{:S(2)}) collective-permute-start(bf16[2048,256]{1,0:T(8,128)(2,1)} %constant_dynamic-slice_fusion), channel_id=1, source_target_pairs={{0,2},{1,3},{4,5},{5,6},{6,7},{9,8},{10,11},{13,15},{14,13},{15,12... | collective-permute-start | bytes 3145736 | tf_op jit(solution)/shard_map/ppermute | solution.py:368
  5.5 61.2 %collective-permute-start.4 = (bf16[256,2048]{1,0:T(8,128)(2,1)}, bf16[256,2048]{1,0:T(8,128)(2,1)}, u32[]{:S(2)}, u32[]{:S(2)}) collective-permute-start(bf16[256,2048]{1,0:T(8,128)(2,1)} %refs_0_.1), channel_id=1, source_target_pairs={{0,28},{4,0},{8,4},{12,8},{16,12},{20,16},{24,20},{28,24},{1,29},{... | collective-permute-start | bytes 3145736 | tf_op jit(solution)/shard_map/ppermute | solution.py:344
  62.4 16.7 %collective-permute-start.1 = (bf16[2048,256]{1,0:T(8,128)(2,1)S(1)}, bf16[2048,256]{1,0:T(8,128)(2,1)S(1)}, u32[]{:S(2)}, u32[]{:S(2)}) collective-permute-start(bf16[2048,256]{1,0:T(8,128)(2,1)S(1)} %relay.3), channel_id=1, source_target_pairs={{0,1},{1,2},{2,3},{3,0},{4,6},{5,4},{6,7},{7,5},{8,10},{9,11},{10,... | collective-permute-start | bytes 3145736 | tf_op jit(solution)/shard_map/ppermute | solution.py:368
  66.7 17.3 %collective-permute-start.5 = (bf16[256,2048]{1,0:T(8,128)(2,1)}, bf16[256,2048]{1,0:T(8,128)(2,1)}, u32[]{:S(2)}, u32[]{:S(2)}) collective-permute-start(bf16[256,2048]{1,0:T(8,128)(2,1)} %collective-permute-done.4.refs_1_), channel_id=1, source_target_pairs={{0,28},{4,0},{8,4},{12,8},{16,12},{20,16},{24,20},{28,24},{1,29},{... | collective-permute-start | bytes 3145736 | tf_op jit(solution)/shard_map/ppermute | solution.py:344
  79.1 27.3 %copy-start.1 = (bf16[2048,256]{1,0:T(8,128)(2,1)}, bf16[2048,256]{1,0:T(8,128)(2,1)S(1)}, u32[]{:S(2)}) copy-start(bf16[2048,256]{1,0:T(8,128)(2,1)S(1)} %collective-permute-done.1.refs_1_.refs_0_) | copy-start | bytes 3145732
  79.7 31.1 %copy-start.6 = (s32[2048]{0:T(1024)S(1)}, s32[2048]{0:T(1024)}, u32[]{:S(2)}) copy-start(s32[2048]{0:T(1024)} %param.12) | copy-start | bytes 24580
  79.7 25.1 %collective-permute-start.2 = (bf16[2048,256]{1,0:T(8,128)(2,1)S(1)}, bf16[2048,256]{1,0:T(8,128)(2,1)S(1)}, u32[]{:S(2)}, u32[]{:S(2)}) collective-permute-start(bf16[2048,256]{1,0:T(8,128)(2,1)S(1)} %relay.4), channel_id=1, source_target_pairs={{0,2},{1,0},{2,3},{5,7},{6,4},{8,9},{9,8},{10,11},{11,10},{12,13},... | collective-permute-start | bytes 3145736 | tf_op jit(solution)/shard_map/ppermute | solution.py:368
  84.0 26.8 %collective-permute-start.6 = (bf16[256,2048]{1,0:T(8,128)(2,1)}, bf16[256,2048]{1,0:T(8,128)(2,1)}, u32[]{:S(2)}, u32[]{:S(2)}) collective-permute-start(bf16[256,2048]{1,0:T(8,128)(2,1)} %collective-permute-done.5.refs_2_), channel_id=1, source_target_pairs={{0,28},{4,0},{8,4},{12,8},{16,12},{20,16},{24,20},{28,24},{1,29},{... | collective-permute-start | bytes 3145736 | tf_op jit(solution)/shard_map/ppermute | solution.py:344
  106.4 1.0 copy-start.3
  107.4 22.6 %collective-permute-start.3 = (bf16[2048,256]{1,0:T(8,128)(2,1)}, bf16[2048,256]{1,0:T(8,128)(2,1)}, u32[]{:S(2)}, u32[]{:S(2)}) collective-permute-start(bf16[2048,256]{1,0:T(8,128)(2,1)} %relay.5), channel_id=1, source_target_pairs={{0,1},{2,3},{3,2},{5,4},{6,7},{7,6},{9,8},{10,11},{13,12},{14,15},... | collective-permute-start | bytes 3145736 | tf_op jit(solution)/shard_map/ppermute | solution.py:368
  111.2 1.2 copy-start.5
  112.5 3.9 %copy-start.2 = (bf16[2048,256]{1,0:T(8,128)(2,1)S(1)}, bf16[2048,256]{1,0:T(8,128)(2,1)}, u32[]{:S(2)}) copy-start(bf16[2048,256]{1,0:T(8,128)(2,1)} %copy-done.1) | copy-start | bytes 3145732
  112.5 3.9 %copy-start.4 = (bf16[2048,256]{1,0:T(8,128)(2,1)S(1)}, bf16[2048,256]{1,0:T(8,128)(2,1)}, u32[]{:S(2)}) copy-start(bf16[2048,256]{1,0:T(8,128)(2,1)} %copy-done.3) | copy-start | bytes 3145732
  126.4 10.0 %collective-permute-start.9 = (f32[2048]{0:T(1024)S(1)}, f32[2048]{0:T(1024)S(1)}, u32[]{:S(2)}, u32[]{:S(2)}) collective-permute-start(f32[2048]{0:T(1024)S(1)} %multiply_reduce_fusion), channel_id=1, source_target_pairs={{0,3},{1,2},{2,1},{3,0},{4,7},{5,6},{6,5},{7,4},{8,11},{9,10},{10,... | collective-permute-start | bytes 24584 | tf_op jit(solution)/shard_map/ppermute | solution.py:352
  126.5 9.9 %collective-permute-start.8 = (f32[2048]{0:T(1024)S(1)}, f32[2048]{0:T(1024)S(1)}, u32[]{:S(2)}, u32[]{:S(2)}) collective-permute-start(f32[2048]{0:T(1024)S(1)} %multiply_reduce_fusion), channel_id=1, source_target_pairs={{0,2},{1,3},{2,0},{3,1},{4,6},{5,7},{6,4},{7,5},{8,10},{9,11},{10,... | collective-permute-start | bytes 24584 | tf_op jit(solution)/shard_map/ppermute | solution.py:352
  127.2 9.2 %collective-permute-start.7 = (f32[2048]{0:T(1024)S(1)}, f32[2048]{0:T(1024)S(1)}, u32[]{:S(2)}, u32[]{:S(2)}) collective-permute-start(f32[2048]{0:T(1024)S(1)} %multiply_reduce_fusion), channel_id=1, source_target_pairs={{0,1},{1,0},{2,3},{3,2},{4,5},{5,4},{6,7},{7,6},{8,9},{9,8},{10,11... | collective-permute-start | bytes 24584 | tf_op jit(solution)/shard_map/ppermute | solution.py:352

commit v15 on v11

--- a/solution.py
+++ b/solution.py
@@ -72,10 +72,11 @@
             self.items.append([i for i in mine if i.place > 0])
         self.away = []
         self.lines = [line_slots(items, []) for items in self.items]
-        if rows % 2 == 0 and cols > 3:
+        if rows % 4 == 0 and cols > 3:
             for r in range(rows // 2):
-                self.balance(r, r + rows // 2)
-                self.balance(r + rows // 2, r)
+                other = r + rows // 2 if towards_zero else (r + rows // 2) ^ 1
+                self.balance(r, other)
+                self.balance(other, r)
         self.rounds = max(
             [max(ends, default=0) for ends, _ in self.lines] + [max(inner, default=0) - DEPTH for _, inner in self.lines]
         )
@@ -100,7 +101,7 @@
             mine = line_slots([i for i in self.items[r] if i not in gone], gone)
             theirs = line_slots(self.items[other] + visitors, [])
             score = (
-                max(max(mine[0], default=0), max(theirs[0], default=0)),
+                max(max(mine[0], default=0), max(theirs[0], default=0), STEPS),
                 len(gone),
                 max([slot for slot, i in theirs[0].items() if i.home is not None], default=0),
             )
@@ -491,15 +492,15 @@
     squares = own_squares()
 
     starts = {}
-    if any(own_of[1, 1]):
-        starts[1, 1] = own_chunk(own_of[1, 1])
+    if any(own_of[0, 1]):
+        starts[0, 1] = own_chunk(own_of[0, 1])
     later_x = x
     for k, crossing in enumerate(crossings):
         later_x = lax.optimization_barrier(later_x)
         starts["cross", k] = own_chunk([crossing[rc][1] if rc in crossing else None for rc in devices], later_x)
     later_x, squares = lax.optimization_barrier((later_x, squares))
-    if any(own_of[0, 1]):
-        starts[0, 1] = own_chunk(own_of[0, 1], later_x)
+    if any(own_of[1, 1]):
+        starts[1, 1] = own_chunk(own_of[1, 1], later_x)
     bits = [1 << k for k in range(cols.bit_length() - 1)] if cols & (cols - 1) == 0 else []
     if cols & (cols - 1):
         squares = lax.psum(squares, "col")

time: 120 us -> 118 us (0.983)
  the two profiles are of different devices: /device:TPU:0 before, /device:TPU:3 now
where the time goes in v15:
time: 118 us; the launch traced here: 117 us
  waiting for transfers between devices  56.4 us (48%)
  Pallas kernels  29.7 us (25%)
  starting transfers between devices  17.9 us (15%)
  local copies, waits for them, and re-layouts  10.5 us (9%)
  other arithmetic  1.74 us (1%)
    ppermute x8, waiting for transfers between devices, local(): buffers[key] = lax.ppermute(held, both, pairs_of[key])  56.4 us
    pallas_call x1, Pallas kernels, early_product(): pl.pallas_call(functools.partial(early_kernel, at, candidates, len(buffer...  11.2 us
    ppermute x8, starting transfers between devices, local(): buffers[key] = lax.ppermute(held, both, pairs_of[key])  9.83 us
    pallas_call x6, Pallas kernels, relay(): pl.pallas_call(functools.partial(relay_kernel, at), out_shape=pltpu.VMEM(...  7.87 us
    pallas_call x1, Pallas kernels, last_product(): pl.pallas_call(functools.partial(last_kernel, at, candidates, scale, len(...  7.08 us
    dynamic_slice x3, local copies, waits for them, and re-layouts, own_chunk(): lax.dynamic_slice(x, (piece * piece_rows, group * group_size), (piece_row...  5.7 us
    pallas_call x1, Pallas kernels, standardized_window(): pl.pallas_call(functools.partial(window_kernel, at), out_shape=pltpu.VMEM...  3.56 us
    unnamed x24, local copies, waits for them, and re-layouts  3.23 us
  transfers between devices with their start and end apart: 15, of which 4 were waited for; matrix products, arithmetic and copies ran while one was open for 6% of the time, Pallas kernels for 19%

profile of v15, /device:TPU:3, one launch (start us, length us, event | category | flops | bytes accessed | tf_op | source)
XLA Modules:
  0.0 117.2 jit_solution(9901794186942740649)
XLA Ops:
  0.6 0.0 copy-start
  0.6 0.0 copy-start.11
  0.7 0.0 copy-start.10
  0.7 0.0 copy-start.8
  0.7 2.4 %constant_dynamic-slice_fusion.1 = bf16[2048,256]{1,0:T(8,128)(2,1)} fusion(bf16[2048,512]{1,0:T(8,128)(2,1)} %x.15, s32[]{:T(128)S(6)} %select_n.35), kind=kLoop, calls=%fused_computation.14 | loop fusion | bytes 2097156 | tf_op jit(solution)/shard_map/dynamic_slice | solution.py:467
  3.1 0.7 collective-permute-start.1
  3.8 2.3 %dynamic_slice.32 = bf16[2048,256]{1,0:T(8,128)(2,1)} slice(bf16[2048,512]{1,0:T(8,128)(2,1)} %x.15), slice={[0:2048], [256:512]} | slice | bytes 2097152 | tf_op jit(solution)/shard_map/dynamic_slice | solution.py:467
  6.1 1.6 %collective-permute-start = (bf16[2048,256]{1,0:T(8,128)(2,1)}, bf16[2048,256]{1,0:T(8,128)(2,1)}, u32[]{:S(2)}, u32[]{:S(2)}) collective-permute-start(bf16[2048,256]{1,0:T(8,128)(2,1)} %dynamic_slice.32), channel_id=1, source_target_pairs={{18,2},{1,21}} | collective-permute-start | bytes 3145736 | tf_op jit(solution)/shard_map/ppermute | solution.py:546
  7.7 0.0 copy-done.11
  7.7 0.0 copy-done.10
  7.7 0.1 dynamic_slice.27
  7.8 0.1 dynamic_slice.28
  7.9 0.0 copy-done.8
  7.9 0.0 copy-done
  7.9 1.0 multiply_reduce_fusion
  8.9 1.0 constant_dynamic-slice_fusion
  10.0 1.3 %collective-permute-start.3 = (bf16[2048,256]{1,0:T(8,128)(2,1)}, bf16[2048,256]{1,0:T(8,128)(2,1)}, u32[]{:S(2)}, u32[]{:S(2)}) collective-permute-start(bf16[2048,256]{1,0:T(8,128)(2,1)} %constant_dynamic-slice_fusion), channel_id=1, source_target_pairs={{0,1},{1,2},{5,4},{10,11},{13,12},{14,13},{18,19},{22,21},{23,22},... | collective-permute-start | bytes 3145736 | tf_op jit(solution)/shard_map/ppermute | solution.py:542
  11.3 1.6 %collective-permute-start.9 = (bf16[256,2048]{1,0:T(8,128)(2,1)}, bf16[256,2048]{1,0:T(8,128)(2,1)}, u32[]{:S(2)}, u32[]{:S(2)}) collective-permute-start(bf16[256,2048]{1,0:T(8,128)(2,1)} %refs_0_.1), channel_id=1, source_target_pairs={{0,28},{4,0},{8,4},{12,8},{16,12},{20,16},{24,20},{28,24},{1,29},{... | collective-permute-start | bytes 3145736 | tf_op jit(solution)/shard_map/ppermute | solution.py:491
  12.9 0.7 fusion.2.table
  13.6 0.0 collective-permute-done.1.refs_1_.refs_0_
  13.6 0.0 collective-permute-done.refs_0_
  13.6 1.3 %relay.6 = bf16[2048,256]{1,0:T(8,128)(2,1)S(1)} custom-call(s32[30]{0:T(128)S(1)} %fusion.2.table, bf16[2048,512]{1,0:T(8,128)(2,1)S(1)} %copy-done, bf16[2048,256]{1,0:T(8,128)(2,1)} %collective-permute-done.refs_0_, bf16[2048,256]{1,0:T(8,128)(2,1)S(1)} %collective-permute-done.1.refs_1_.refs_0_), custom_call_target="tpu_custom_call" | custom-call | tf_op jit(solution)/shard_map/relay/pallas_call | solution.py:183
  14.9 1.0 copy-done.5
  15.9 0.7 collective-permute-start.2
  16.6 14.7 %collective-permute-done.3.refs_0_.refs_1_ = bf16[2048,256]{1,0:T(8,128)(2,1)} collective-permute-done((bf16[2048,256]{1,0:T(8,128)(2,1)}, bf16[2048,256]{1,0:T(8,128)(2,1)}, u32[]{:S(2)}, u32[]{:S(2)}) %collective-permute-start.3) | collective-permute-done | bytes 1048608 | tf_op jit(solution)/shard_map/ppermute | solution.py:542
  31.3 1.3 %relay.7 = bf16[2048,256]{1,0:T(8,128)(2,1)S(1)} custom-call(s32[30]{0:T(128)S(1)} %fusion.2.table, bf16[2048,512]{1,0:T(8,128)(2,1)S(1)} %copy-done, bf16[2048,256]{1,0:T(8,128)(2,1)} %collective-permute-done.3.refs_0_.refs_1_), custom_call_target="tpu_custom_call" | custom-call | tf_op jit(solution)/shard_map/relay/pallas_call | solution.py:183
  32.6 1.3 %collective-permute-start.4 = (bf16[2048,256]{1,0:T(8,128)(2,1)S(1)}, bf16[2048,256]{1,0:T(8,128)(2,1)S(1)}, u32[]{:S(2)}, u32[]{:S(2)}) collective-permute-start(bf16[2048,256]{1,0:T(8,128)(2,1)S(1)} %relay.7), channel_id=1, source_target_pairs={{0,1},{1,2},{2,3},{5,4},{6,5},{9,10},{10,11},{13,12},{14,13},{15,1... | collective-permute-start | bytes 3145736 | tf_op jit(solution)/shard_map/ppermute | solution.py:542
  33.9 0.0 collective-permute-done.9.refs_1_
  33.9 0.1 collective-permute-start.10
  34.0 0.0 collective-permute-done.2.refs_0_.refs_2_
  34.0 0.6 relay.8
  34.6 1.6 %collective-permute-start.5 = (bf16[2048,256]{1,0:T(8,128)(2,1)S(1)}, bf16[2048,256]{1,0:T(8,128)(2,1)}, u32[]{:S(2)}, u32[]{:S(2)}) collective-permute-start(bf16[2048,256]{1,0:T(8,128)(2,1)S(1)} %relay.8), channel_id=1, source_target_pairs={{1,0},{5,6},{6,7},{9,8},{10,9},{14,15},{17,16},{18,17},{21,22},{22... | collective-permute-start | bytes 3145736 | tf_op jit(solution)/shard_map/ppermute | solution.py:542
  36.3 19.3 %collective-permute-done.4.refs_0_.refs_3_.refs_1_ = bf16[2048,256]{1,0:T(8,128)(2,1)S(1)} collective-permute-done((bf16[2048,256]{1,0:T(8,128)(2,1)S(1)}, bf16[2048,256]{1,0:T(8,128)(2,1)S(1)}, u32[]{:S(2)}, u32[]{:S(2)}) %collective-permute-start.4) | collective-permute-done | bytes 1048608 | tf_op jit(solution)/shard_map/ppermute | solution.py:542
  55.6 0.6 relay.9
  56.2 0.0 copy-start.9
  56.2 1.3 %collective-permute-start.6 = (bf16[2048,256]{1,0:T(8,128)(2,1)S(1)}, bf16[2048,256]{1,0:T(8,128)(2,1)S(1)}, u32[]{:S(2)}, u32[]{:S(2)}) collective-permute-start(bf16[2048,256]{1,0:T(8,128)(2,1)S(1)} %relay.9), channel_id=1, source_target_pairs={{1,2},{2,3},{5,4},{9,10},{10,11},{13,12},{14,13},{21,20},{22,21},{... | collective-permute-start | bytes 3145736 | tf_op jit(solution)/shard_map/ppermute | solution.py:542
  57.5 0.0 collective-permute-done.10.refs_2_
  57.6 0.1 collective-permute-start.11
  57.6 0.0 collective-permute-done.5.refs_0_.refs_4_.refs_2_
  57.6 1.7 %collective-permute-start.13 = (bf16[2048,256]{1,0:T(8,128)(2,1)}, bf16[2048,256]{1,0:T(8,128)(2,1)}, u32[]{:S(2)}, u32[]{:S(2)}) collective-permute-start(bf16[2048,256]{1,0:T(8,128)(2,1)} %collective-permute-done.5.refs_0_.refs_4_.refs_2_), channel_id=1, source_target_pairs={{0,16},{23,3}} | collective-permute-start | bytes 3145736 | tf_op jit(solution)/shard_map/ppermute | solution.py:525
  59.4 2.9 %collective-permute-start.12 = (f32[2048]{0:T(1024)S(1)}, f32[2048]{0:T(1024)S(1)}, u32[]{:S(2)}, u32[]{:S(2)}) collective-permute-start(f32[2048]{0:T(1024)S(1)} %multiply_reduce_fusion), channel_id=1, source_target_pairs={{0,1},{1,0},{2,3},{3,2},{4,5},{5,4},{6,7},{7,6},{8,9},{9,8},{10,11... | collective-permute-start | bytes 24584 | tf_op jit(solution)/shard_map/ppermute | solution.py:512
  62.3 2.3 %relay.10 = bf16[2048,256]{1,0:T(8,128)(2,1)} custom-call(s32[30]{0:T(128)S(1)} %fusion.2.table, bf16[2048,512]{1,0:T(8,128)(2,1)S(1)} %copy-done, bf16[2048,256]{1,0:T(8,128)(2,1)} %collective-permute-done.5.refs_0_.refs_4_.refs_2_), custom_call_target="tpu_custom_call" | custom-call | tf_op jit(solution)/shard_map/relay/pallas_call | solution.py:183
  64.6 1.6 %collective-permute-start.7 = (bf16[2048,256]{1,0:T(8,128)(2,1)}, bf16[2048,256]{1,0:T(8,128)(2,1)}, u32[]{:S(2)}, u32[]{:S(2)}) collective-permute-start(bf16[2048,256]{1,0:T(8,128)(2,1)} %relay.10), channel_id=1, source_target_pairs={{6,7},{9,8},{17,16},{18,17},{22,23},{25,24},{30,31}} | collective-permute-start | bytes 3145736 | tf_op jit(solution)/shard_map/ppermute | solution.py:542
  66.2 14.1 %collective-permute-done.6.refs_0_.refs_5_.refs_3_ = bf16[2048,256]{1,0:T(8,128)(2,1)S(1)} collective-permute-done((bf16[2048,256]{1,0:T(8,128)(2,1)S(1)}, bf16[2048,256]{1,0:T(8,128)(2,1)S(1)}, u32[]{:S(2)}, u32[]{:S(2)}) %collective-permute-start.6) | collective-permute-done | bytes 1048608 | tf_op jit(solution)/shard_map/ppermute | solution.py:542
  80.3 1.7 %relay.11 = bf16[2048,256]{1,0:T(8,128)(2,1)} custom-call(s32[30]{0:T(128)S(1)} %fusion.2.table, bf16[2048,512]{1,0:T(8,128)(2,1)S(1)} %copy-done, bf16[2048,256]{1,0:T(8,128)(2,1)S(1)} %collective-permute-done.6.refs_0_.refs_5_.refs_3_), custom_call_target="tpu_custom_call" | custom-call | tf_op jit(solution)/shard_map/relay/pallas_call | solution.py:183
  82.0 1.0 copy-done.3
  83.0 1.3 %collective-permute-start.8 = (bf16[2048,256]{1,0:T(8,128)(2,1)}, bf16[2048,256]{1,0:T(8,128)(2,1)}, u32[]{:S(2)}, u32[]{:S(2)}) collective-permute-start(bf16[2048,256]{1,0:T(8,128)(2,1)} %relay.11), channel_id=1, source_target_pairs={{1,2},{2,3},{10,11},{13,12},{21,20},{26,27}} | collective-permute-start | bytes 3145736 | tf_op jit(solution)/shard_map/ppermute | solution.py:542
  84.3 0.1 fusion
  84.4 0.0 collective-permute-done.11.refs_3_
  84.4 0.2 broadcast_in_dim.42.refs_4_
  84.6 0.2 broadcast_in_dim.43.refs_5_
  84.8 0.0 copy-start.7
  84.8 1.2 %copy-done.7 = bf16[256,2048]{1,0:T(8,128)(2,1)S(1)} copy-done((bf16[256,2048]{1,0:T(8,128)(2,1)S(1)}, bf16[256,2048]{1,0:T(8,128)(2,1)}, u32[]{:S(2)}) %copy-start.7) | copy-done | bytes 1048600
  86.0 3.6 %window.1.refs_10_.refs_9_ = bf16[1024,2048]{1,0:T(8,128)(2,1)S(1)} custom-call(s32[30]{0:T(128)S(1)} %fusion.2.table, bf16[256,2048]{1,0:T(8,128)(2,1)S(1)} %copy-done.7, bf16[256,2048]{1,0:T(8,128)(2,1)} %collective-permute-done.9.refs_1_, bf16[256,2048]{1,0:T(8,128)(2,1)} %collective-permute-done.10.refs_2_, ...), custom_call_target="tpu_custom_call" | custom-call | flops 8388608 | bytes 8388608 | tf_op jit(solution)/shard_map/window/pallas_call | solution.py:221
  89.6 0.0 collective-permute-done.12
  89.6 0.1 collective-permute-start.14
  89.7 0.0 collective-permute-done.13.refs_6_
  89.7 0.3 broadcast_in_dim.41.refs_9_.refs_8_
  90.1 11.2 %early.1.refs_10_ = f32[2048,2048]{1,0:T(8,128)S(1)} custom-call(s32[30]{0:T(128)S(1)} %fusion.2.table, bf16[2048,512]{1,0:T(8,128)(2,1)S(1)} %copy-done, bf16[2048,256]{1,0:T(8,128)(2,1)S(1)} %copy-done.6, bf16[2048,256]{1,0:T(8,128)(2,1)} %collective-permute-done.3.refs_0_.refs_1_, bf16[2048,256]{1,0:T(8,128)(2,1)S(1)} %collective-permute-done.2.refs_0_.refs_2_, ...), custom_call_target="tpu_custom_call" | custom-call | flops 6442450944 | tf_op jit(solution)/shard_map/early/pallas_call | solution.py:282
  101.2 0.0 collective-permute-done.14
  101.2 0.6 multiply_add_fusion
  101.8 0.0 collective-permute-done.7.refs_4_
  101.8 8.3 %collective-permute-done.8.refs_5_ = bf16[2048,256]{1,0:T(8,128)(2,1)} collective-permute-done((bf16[2048,256]{1,0:T(8,128)(2,1)}, bf16[2048,256]{1,0:T(8,128)(2,1)}, u32[]{:S(2)}, u32[]{:S(2)}) %collective-permute-start.8) | collective-permute-done | bytes 1048608 | tf_op jit(solution)/shard_map/ppermute | solution.py:542
  110.1 7.1 %last.1 = bf16[2048,2048]{1,0:T(8,128)(2,1)} custom-call(s32[30]{0:T(128)S(1)} %fusion.2.table, bf16[2048,512]{1,0:T(8,128)(2,1)S(1)} %copy-done, bf16[2048,256]{1,0:T(8,128)(2,1)S(1)} %collective-permute-done.2.refs_0_.refs_2_, bf16[2048,256]{1,0:T(8,128)(2,1)S(1)} %copy-done.2, bf16[2048,256]{1,0:T(8,128)(2,1)} %collective-permute-done.5.refs_0_.refs_4_.refs_2_, ...), custom_call_target="tpu_custom_call" | custom-call | flops 2147483648 | bytes 8388608 | tf_op jit(solution)/shard_map/last/pallas_call | solution.py:326
  (15 shorter events, 0.0 us)
Async XLA Ops:
  0.6 7.3 %copy-start = (bf16[2048,512]{1,0:T(8,128)(2,1)S(1)}, bf16[2048,512]{1,0:T(8,128)(2,1)}, u32[]{:S(2)}) copy-start(bf16[2048,512]{1,0:T(8,128)(2,1)} %x.15) | copy-start | bytes 6291460
  0.6 7.1 %copy-start.11 = (f32[2048]{0:T(1024)S(1)}, f32[2048]{0:T(1024)}, u32[]{:S(2)}) copy-start(f32[2048]{0:T(1024)} %param.10) | copy-start | bytes 24580
  0.7 7.1 %copy-start.10 = (f32[2048]{0:T(1024)S(1)}, f32[2048]{0:T(1024)}, u32[]{:S(2)}) copy-start(f32[2048]{0:T(1024)} %param.9) | copy-start | bytes 24580
  0.7 7.2 %copy-start.8 = (s32[2048]{0:T(1024)S(1)}, s32[2048]{0:T(1024)}, u32[]{:S(2)}) copy-start(s32[2048]{0:T(1024)} %param.11) | copy-start | bytes 24580
  3.1 10.5 %collective-permute-start.1 = (bf16[2048,256]{1,0:T(8,128)(2,1)}, bf16[2048,256]{1,0:T(8,128)(2,1)S(1)}, u32[]{:S(2)}, u32[]{:S(2)}) collective-permute-start(bf16[2048,256]{1,0:T(8,128)(2,1)} %constant_dynamic-slice_fusion.1), channel_id=1, source_target_pairs={{1,0},{5,6},{6,7},{9,8},{14,15},{18,17},{19,18},{22,23},{27,26},{2... | collective-permute-start | bytes 3145736 | tf_op jit(solution)/shard_map/ppermute | solution.py:542
  6.1 7.5 %collective-permute-start = (bf16[2048,256]{1,0:T(8,128)(2,1)}, bf16[2048,256]{1,0:T(8,128)(2,1)}, u32[]{:S(2)}, u32[]{:S(2)}) collective-permute-start(bf16[2048,256]{1,0:T(8,128)(2,1)} %dynamic_slice.32), channel_id=1, source_target_pairs={{18,2},{1,21}} | collective-permute-start | bytes 3145736 | tf_op jit(solution)/shard_map/ppermute | solution.py:546
  10.0 21.3 %collective-permute-start.3 = (bf16[2048,256]{1,0:T(8,128)(2,1)}, bf16[2048,256]{1,0:T(8,128)(2,1)}, u32[]{:S(2)}, u32[]{:S(2)}) collective-permute-start(bf16[2048,256]{1,0:T(8,128)(2,1)} %constant_dynamic-slice_fusion), channel_id=1, source_target_pairs={{0,1},{1,2},{5,4},{10,11},{13,12},{14,13},{18,19},{22,21},{23,22},... | collective-permute-start | bytes 3145736 | tf_op jit(solution)/shard_map/ppermute | solution.py:542
  11.3 22.7 %collective-permute-start.9 = (bf16[256,2048]{1,0:T(8,128)(2,1)}, bf16[256,2048]{1,0:T(8,128)(2,1)}, u32[]{:S(2)}, u32[]{:S(2)}) collective-permute-start(bf16[256,2048]{1,0:T(8,128)(2,1)} %refs_0_.1), channel_id=1, source_target_pairs={{0,28},{4,0},{8,4},{12,8},{16,12},{20,16},{24,20},{28,24},{1,29},{... | collective-permute-start | bytes 3145736 | tf_op jit(solution)/shard_map/ppermute | solution.py:491
  14.9 1.0 copy-start.5
  15.9 18.1 %collective-permute-start.2 = (bf16[2048,256]{1,0:T(8,128)(2,1)S(1)}, bf16[2048,256]{1,0:T(8,128)(2,1)S(1)}, u32[]{:S(2)}, u32[]{:S(2)}) collective-permute-start(bf16[2048,256]{1,0:T(8,128)(2,1)S(1)} %relay.6), channel_id=1, source_target_pairs={{1,0},{2,1},{4,5},{5,6},{6,7},{9,8},{10,9},{13,14},{14,15},{17,16}... | collective-permute-start | bytes 3145736 | tf_op jit(solution)/shard_map/ppermute | solution.py:542
  32.6 23.0 %collective-permute-start.4 = (bf16[2048,256]{1,0:T(8,128)(2,1)S(1)}, bf16[2048,256]{1,0:T(8,128)(2,1)S(1)}, u32[]{:S(2)}, u32[]{:S(2)}) collective-permute-start(bf16[2048,256]{1,0:T(8,128)(2,1)S(1)} %relay.7), channel_id=1, source_target_pairs={{0,1},{1,2},{2,3},{5,4},{6,5},{9,10},{10,11},{13,12},{14,13},{15,1... | collective-permute-start | bytes 3145736 | tf_op jit(solution)/shard_map/ppermute | solution.py:542
  33.9 23.6 %collective-permute-start.10 = (bf16[256,2048]{1,0:T(8,128)(2,1)}, bf16[256,2048]{1,0:T(8,128)(2,1)}, u32[]{:S(2)}, u32[]{:S(2)}) collective-permute-start(bf16[256,2048]{1,0:T(8,128)(2,1)} %collective-permute-done.9.refs_1_), channel_id=1, source_target_pairs={{0,28},{4,0},{8,4},{12,8},{16,12},{20,16},{24,20},{28,24},{1,29},{... | collective-permute-start | bytes 3145736 | tf_op jit(solution)/shard_map/ppermute | solution.py:491
  34.6 23.0 %collective-permute-start.5 = (bf16[2048,256]{1,0:T(8,128)(2,1)S(1)}, bf16[2048,256]{1,0:T(8,128)(2,1)}, u32[]{:S(2)}, u32[]{:S(2)}) collective-permute-start(bf16[2048,256]{1,0:T(8,128)(2,1)S(1)} %relay.8), channel_id=1, source_target_pairs={{1,0},{5,6},{6,7},{9,8},{10,9},{14,15},{17,16},{18,17},{21,22},{22... | collective-permute-start | bytes 3145736 | tf_op jit(solution)/shard_map/ppermute | solution.py:542
  55.6 9.0 %copy-start.1 = (bf16[2048,256]{1,0:T(8,128)(2,1)}, bf16[2048,256]{1,0:T(8,128)(2,1)S(1)}, u32[]{:S(2)}) copy-start(bf16[2048,256]{1,0:T(8,128)(2,1)S(1)} %collective-permute-done.4.refs_0_.refs_3_.refs_1_) | copy-start | bytes 3145732
  56.2 28.0 %copy-start.9 = (s32[2048]{0:T(1024)S(1)}, s32[2048]{0:T(1024)}, u32[]{:S(2)}) copy-start(s32[2048]{0:T(1024)} %param.12) | copy-start | bytes 24580
  56.2 24.0 %collective-permute-start.6 = (bf16[2048,256]{1,0:T(8,128)(2,1)S(1)}, bf16[2048,256]{1,0:T(8,128)(2,1)S(1)}, u32[]{:S(2)}, u32[]{:S(2)}) collective-permute-start(bf16[2048,256]{1,0:T(8,128)(2,1)S(1)} %relay.9), channel_id=1, source_target_pairs={{1,2},{2,3},{5,4},{9,10},{10,11},{13,12},{14,13},{21,20},{22,21},{... | collective-permute-start | bytes 3145736 | tf_op jit(solution)/shard_map/ppermute | solution.py:542
  57.6 26.8 %collective-permute-start.11 = (bf16[256,2048]{1,0:T(8,128)(2,1)}, bf16[256,2048]{1,0:T(8,128)(2,1)}, u32[]{:S(2)}, u32[]{:S(2)}) collective-permute-start(bf16[256,2048]{1,0:T(8,128)(2,1)} %collective-permute-done.10.refs_2_), channel_id=1, source_target_pairs={{0,28},{4,0},{8,4},{12,8},{16,12},{20,16},{24,20},{28,24},{1,29},{... | collective-permute-start | bytes 3145736 | tf_op jit(solution)/shard_map/ppermute | solution.py:491
  57.6 32.1 %collective-permute-start.13 = (bf16[2048,256]{1,0:T(8,128)(2,1)}, bf16[2048,256]{1,0:T(8,128)(2,1)}, u32[]{:S(2)}, u32[]{:S(2)}) collective-permute-start(bf16[2048,256]{1,0:T(8,128)(2,1)} %collective-permute-done.5.refs_0_.refs_4_.refs_2_), channel_id=1, source_target_pairs={{0,16},{23,3}} | collective-permute-start | bytes 3145736 | tf_op jit(solution)/shard_map/ppermute | solution.py:525
  59.4 30.2 %collective-permute-start.12 = (f32[2048]{0:T(1024)S(1)}, f32[2048]{0:T(1024)S(1)}, u32[]{:S(2)}, u32[]{:S(2)}) collective-permute-start(f32[2048]{0:T(1024)S(1)} %multiply_reduce_fusion), channel_id=1, source_target_pairs={{0,1},{1,0},{2,3},{3,2},{4,5},{5,4},{6,7},{7,6},{8,9},{9,8},{10,11... | collective-permute-start | bytes 24584 | tf_op jit(solution)/shard_map/ppermute | solution.py:512
  64.6 37.3 %collective-permute-start.7 = (bf16[2048,256]{1,0:T(8,128)(2,1)}, bf16[2048,256]{1,0:T(8,128)(2,1)}, u32[]{:S(2)}, u32[]{:S(2)}) collective-permute-start(bf16[2048,256]{1,0:T(8,128)(2,1)} %relay.10), channel_id=1, source_target_pairs={{6,7},{9,8},{17,16},{18,17},{22,23},{25,24},{30,31}} | collective-permute-start | bytes 3145736 | tf_op jit(solution)/shard_map/ppermute | solution.py:542
  82.0 1.0 copy-start.3
  83.0 27.2 %collective-permute-start.8 = (bf16[2048,256]{1,0:T(8,128)(2,1)}, bf16[2048,256]{1,0:T(8,128)(2,1)}, u32[]{:S(2)}, u32[]{:S(2)}) collective-permute-start(bf16[2048,256]{1,0:T(8,128)(2,1)} %relay.11), channel_id=1, source_target_pairs={{1,2},{2,3},{10,11},{13,12},{21,20},{26,27}} | collective-permute-start | bytes 3145736 | tf_op jit(solution)/shard_map/ppermute | solution.py:542
  84.8 1.2 %copy-start.7 = (bf16[256,2048]{1,0:T(8,128)(2,1)S(1)}, bf16[256,2048]{1,0:T(8,128)(2,1)}, u32[]{:S(2)}) copy-start(bf16[256,2048]{1,0:T(8,128)(2,1)} %refs_0_.1) | copy-start | bytes 3145732
  86.0 4.0 %copy-start.2 = (bf16[2048,256]{1,0:T(8,128)(2,1)S(1)}, bf16[2048,256]{1,0:T(8,128)(2,1)}, u32[]{:S(2)}) copy-start(bf16[2048,256]{1,0:T(8,128)(2,1)} %copy-done.1) | copy-start | bytes 3145732
  86.0 4.0 %copy-start.4 = (bf16[2048,256]{1,0:T(8,128)(2,1)S(1)}, bf16[2048,256]{1,0:T(8,128)(2,1)}, u32[]{:S(2)}) copy-start(bf16[2048,256]{1,0:T(8,128)(2,1)} %copy-done.3) | copy-start | bytes 3145732
  86.0 4.0 %copy-start.6 = (bf16[2048,256]{1,0:T(8,128)(2,1)S(1)}, bf16[2048,256]{1,0:T(8,128)(2,1)}, u32[]{:S(2)}) copy-start(bf16[2048,256]{1,0:T(8,128)(2,1)} %copy-done.5) | copy-start | bytes 3145732
  89.6 11.6 %collective-permute-start.14 = (f32[2048]{0:T(1024)S(1)}, f32[2048]{0:T(1024)S(1)}, u32[]{:S(2)}, u32[]{:S(2)}) collective-permute-start(f32[2048]{0:T(1024)S(1)} %add.39), channel_id=1, source_target_pairs={{0,2},{1,3},{2,0},{3,1},{4,6},{5,7},{6,4},{7,5},{8,10},{9,11},{10,... | collective-permute-start | bytes 24584 | tf_op jit(solution)/shard_map/ppermute | solution.py:512

commit v16 on v13

--- a/solution.py
+++ b/solution.py
@@ -35,27 +35,19 @@
         return self.piece, self.s
 
 
-def line_slots(items, cut):
-    ends, inner = {}, {}
+def line_slots(items):
+    slots = {}
     todo = sorted(items, key=lambda i: (i.home is None, i.piece, i.place, i.s))
     slot = 1
     while todo:
         for item in todo:
             first = 1 + DEPTH * (item.place - 1) + (HOP if item.home is not None else 0)
             if first <= slot:
-                ends[slot] = item
-                if item.place > 1:
-                    inner[slot] = item
+                slots[slot] = item
                 todo.remove(item)
                 break
         slot += 1
-    for item in sorted(cut, key=lambda i: (i.place, i.key)):
-        slot = 1 + DEPTH * (item.place - 1)
-        if item.place > 1:
-            while slot in inner:
-                slot += 1
-            inner[slot] = item
-    return ends, inner
+    return slots
 
 
 class Lane:
@@ -71,14 +63,13 @@
             ]
             self.items.append([i for i in mine if i.place > 0])
         self.away = []
-        self.lines = [line_slots(items, []) for items in self.items]
-        if rows % 2 == 0 and cols > 3:
+        self.lines = [line_slots(items) for items in self.items]
+        if rows % 4 == 0 and cols > 3:
             for r in range(rows // 2):
-                self.balance(r, r + rows // 2)
-                self.balance(r + rows // 2, r)
-        self.rounds = max(
-            [max(ends, default=0) for ends, _ in self.lines] + [max(inner, default=0) - DEPTH for _, inner in self.lines]
-        )
+                other = r + rows // 2 if towards_zero else (r + rows // 2) ^ 1
+                self.balance(r, other)
+                self.balance(other, r)
+        self.rounds = max([max(slots, default=0) for slots in self.lines])
 
     def place(self, c):
         return c if self.towards_zero else self.cols - 1 - c
@@ -97,12 +88,12 @@
                 here.sort(key=lambda i: i.key, reverse=True)
                 gone += here[:count]
             visitors = [Item(other, i.piece, i.s, i.place, home=r) for i in gone]
-            mine = line_slots([i for i in self.items[r] if i not in gone], gone)
-            theirs = line_slots(self.items[other] + visitors, [])
+            mine = line_slots([i for i in self.items[r] if i not in gone])
+            theirs = line_slots(self.items[other] + visitors)
             score = (
-                max(max(mine[0], default=0), max(theirs[0], default=0)),
+                max(max(mine, default=0), max(theirs, default=0), STEPS),
                 len(gone),
-                max([slot for slot, i in theirs[0].items() if i.home is not None], default=0),
+                max([slot for slot, i in theirs.items() if i.home is not None], default=0),
             )
             if best is None or score < best[0]:
                 best = score, gone, mine, theirs
@@ -113,10 +104,7 @@
 
     def sent(self, r, c, t):
         p = self.place(c)
-        ends, inner = self.lines[r]
-        if p == 0:
-            return None
-        item = ends.get(t) if p == 1 else inner.get(t + DEPTH * (p - 1))
+        item = self.lines[r].get(t + DEPTH * (p - 1)) if p > 0 else None
         return item if item is not None and item.place >= p else None
 
     def pairs(self, t):
@@ -130,17 +118,11 @@
     def arrival(self, r, c, key):
         p = self.place(c)
         for i in self.items[r]:
-            if i.key != key or i.place <= p:
-                continue
-            ends, inner = self.lines[r]
-            if p == 0 and i in self.away:
-                for other, _ in self.lines:
-                    for slot, v in other.items():
-                        if v.home == r and v.key == key:
-                            return slot, True
-            for slot, v in (ends if p == 0 else inner).items():
-                if v is i:
-                    return slot - DEPTH * p, False
+            if i.key == key and i.place > p:
+                for slots in self.lines:
+                    for slot, v in slots.items():
+                        if v is i or (v.home == r and v.key == key):
+                            return slot - DEPTH * p, v is not i
         return None
 
 
@@ -362,7 +344,7 @@
     crossing_of = {}
     for d, lane in enumerate(lanes):
         for r in range(rows):
-            for slot, item in sorted(lane.lines[r][0].items()):
+            for slot, item in sorted(lane.lines[r].items()):
                 if item.home is None:
                     continue
                 source, target = (item.home, lane.col(item.place)), (r, lane.col(item.place))
@@ -399,13 +381,13 @@
         pairs_of[phase, t], kinds_of[phase, t], own_of[phase, t] = pairs, kinds, own
 
     returns = {}
-    for t in range(1, rounds + 1):
-        for d, lane in enumerate(lanes):
-            for r in range(rows):
-                item = lane.lines[r][0].get(t)
-                if item is not None and item.home is not None:
-                    pair = number(r, lane.col(0)), number(item.home, lane.col(0))
-                    returns.setdefault(((r + d) % 2, t), []).append(pair)
+    for d, lane in enumerate(lanes):
+        for r in range(rows):
+            for slot, item in lane.lines[r].items():
+                if item.home is not None:
+                    for p in range(item.place):
+                        pair = number(r, lane.col(p)), number(item.home, lane.col(p))
+                        returns.setdefault(((r + d) % 2, slot - DEPTH * p), []).append(pair)
 
     columns = []
 
@@ -437,7 +419,8 @@
                     t, returned = arrival
                     when, key = t, ((r + d) % 2, t)
                     if returned:
-                        when, key = t + 0.7, ("back%d" % ((r + rows // 2 + d) % 2), t)
+                        phase = 0 if any(to == number(r, c) for _, to in returns.get((0, t), [])) else 1
+                        when, key = t + 0.7, ("back%d" % phase, t)
             arrivals.append((when, s, key))
         order.append(sorted(arrivals, key=lambda a: a[:2]))
     rank_at = add([[[a[1] for a in arrivals].index(s) for s in range(STEPS)] for arrivals in order])
@@ -487,26 +470,25 @@
     squares = own_squares()
 
     starts = {}
-    if any(own_of[1, 1]):
-        starts[1, 1] = own_chunk(own_of[1, 1])
+    if any(own_of[0, 1]):
+        starts[0, 1] = own_chunk(own_of[0, 1])
     later_x = x
     for k, crossing in enumerate(crossings):
         later_x = lax.optimization_barrier(later_x)
         starts["cross", k] = own_chunk([crossing[rc][1] if rc in crossing else None for rc in devices], later_x)
     later_x, squares = lax.optimization_barrier((later_x, squares))
-    if any(own_of[0, 1]):
-        starts[0, 1] = own_chunk(own_of[0, 1], later_x)
-    bits = [1 << k for k in range(cols.bit_length() - 1)] if cols & (cols - 1) == 0 else []
-    if cols & (cols - 1):
-        squares = lax.psum(squares, "col")
-
-    def sum_beside(value, squares):
-        if not bits:
-            return value, squares
-        bit = bits.pop(0)
-        other = lax.ppermute(squares, "col", [(i, i ^ bit) for i in range(cols)])
-        value, other = lax.optimization_barrier((value, other))
-        return value, squares + other
+    if any(own_of[1, 1]):
+        starts[1, 1] = own_chunk(own_of[1, 1], later_x)
+    def col_sum_beside(value, squares):
+        if cols & (cols - 1):
+            return value, lax.psum(squares, "col")
+        parts = [squares]
+        for mask in range(1, cols):
+            parts.append(lax.ppermute(squares, "col", [(i, i ^ mask) for i in range(cols)]))
+        value, *parts = lax.optimization_barrier((value, *parts))
+        while len(parts) > 1:
+            parts = [a + b for a, b in zip(parts[::2], parts[1::2])]
+        return value, parts[0]
 
     buffers, crossed = {}, {}
 
@@ -530,6 +512,9 @@
                 held = own_chunk(own_of[key])
             else:
                 held = crossed[next(k for k in kinds_of[key] if k is not None)]
+            name = "back%d" % phase, t - 2
+            if name in buffers:
+                held, buffers[name] = lax.optimization_barrier((held, buffers[name]))
             buffers[key] = lax.ppermute(held, both, pairs_of[key])
         if key == (0, 1):
             for k, crossing in enumerate(crossings):
@@ -539,11 +524,9 @@
     zy = standardized_window(rank_at, table, window, wide(window_factor), wide(window_twice), male_cols[None, :])
     shared = window_factor[None, :], window_twice[None, :], male_wide, zy
     total = early_product(source_at[0], candidates[0], table, x, [buffers[k] for k in used[0]], *shared)
-    total, squares = sum_beside(total, squares)
+    total, squares = lax.optimization_barrier((total, squares))
     relation = last_product(source_at[1], candidates[1][0], table, x, [buffers[k] for k in used[1]], *shared, total)
-    relation, squares = sum_beside(relation, squares)
-    for bit in bits:
-        squares = squares + lax.ppermute(squares, "col", [(i, i ^ bit) for i in range(cols)])
+    relation, squares = col_sum_beside(relation, squares)
     inbreeding = squares / jnp.float32(freq.shape[0]) - 1.0
     return relation, inbreeding
 

time: 136 us -> 134 us (0.985)
  waiting for transfers between devices: 44.3 us -> 60.7 us
  starting transfers between devices: 46.9 us -> 32.5 us
  Pallas kernels: 31.9 us -> 26.6 us
    ppermute x8, waiting for transfers between devices: 44.3 us -> 58.7 us  [local(): buffers[key] = lax.ppermute(held, both, pairs_of[key])]
    ppermute x8, starting transfers between devices: 29.1 us -> 21.6 us  [local(): buffers[key] = lax.ppermute(held, both, pairs_of[key])]
    ppermute x2 -> x3, starting transfers between devices: 11.5 us -> 4.44 us  [col_sum_beside(): lax.ppermute(squares, 'col', [(i, i ^ mask) for i in range(cols)])]
    pallas_call x6 -> x4, Pallas kernels: 8.9 us -> 3.88 us  [relay(): pl.pallas_call(functools.partial(relay_kernel, at), out_shape=pltpu.VMEM(...]
    ppermute x2, waiting for transfers between devices: 0.01 us -> 2 us  [bring_back(): lax.ppermute(buffers[key], both, returns[key])]
    unnamed x20 -> x24, local copies, waits for them, and re-layouts: 2.22 us -> 3.25 us
  transfers between devices with their start and end apart: 16 -> 17, of which waited for: 4 -> 4; matrix products, arithmetic and copies ran while one was open for 4% -> 5% of each run, Pallas kernels for 24% -> 20%
where the time goes in v16:
time: 134 us; the launch traced here: 133 us
  waiting for transfers between devices  60.7 us (45%)
  starting transfers between devices  32.5 us (24%)
  Pallas kernels  26.6 us (20%)
  local copies, waits for them, and re-layouts  10.6 us (8%)
  other arithmetic  1.73 us (1%)
    ppermute x8, waiting for transfers between devices, local(): buffers[key] = lax.ppermute(held, both, pairs_of[key])  58.7 us
    ppermute x8, starting transfers between devices, local(): buffers[key] = lax.ppermute(held, both, pairs_of[key])  21.6 us
    pallas_call x1, Pallas kernels, early_product(): pl.pallas_call(functools.partial(early_kernel, at, candidates, len(buffer...  11.7 us
    pallas_call x1, Pallas kernels, last_product(): pl.pallas_call(functools.partial(last_kernel, at, candidates, scale, len(...  7.4 us
    dynamic_slice x3, local copies, waits for them, and re-layouts, own_chunk(): lax.dynamic_slice(x, (piece * piece_rows, group * group_size), (piece_row...  5.78 us
    ppermute x2, starting transfers between devices, bring_back(): lax.ppermute(buffers[key], both, returns[key])  4.79 us
    ppermute x3, starting transfers between devices, col_sum_beside(): lax.ppermute(squares, 'col', [(i, i ^ mask) for i in range(cols)])  4.44 us
    pallas_call x4, Pallas kernels, relay(): pl.pallas_call(functools.partial(relay_kernel, at), out_shape=pltpu.VMEM(...  3.88 us
  transfers between devices with their start and end apart: 17, of which 4 were waited for; matrix products, arithmetic and copies ran while one was open for 5% of the time, Pallas kernels for 20%

profile of v16, /device:TPU:0, one launch (start us, length us, event | category | flops | bytes accessed | tf_op | source)
XLA Modules:
  0.0 133.1 jit_solution(523043139836589790)
XLA Ops:
  0.6 0.0 copy-start
  0.6 0.0 copy-start.11
  0.7 0.0 copy-start.10
  0.7 0.0 copy-start.8
  0.7 2.4 %dynamic_slice.32 = bf16[2048,256]{1,0:T(8,128)(2,1)} slice(bf16[2048,512]{1,0:T(8,128)(2,1)} %x.11), slice={[0:2048], [256:512]} | slice | bytes 2097152 | tf_op jit(solution)/shard_map/dynamic_slice | solution.py:445
  3.1 1.6 %collective-permute-start = (bf16[2048,256]{1,0:T(8,128)(2,1)}, bf16[2048,256]{1,0:T(8,128)(2,1)}, u32[]{:S(2)}, u32[]{:S(2)}) collective-permute-start(bf16[2048,256]{1,0:T(8,128)(2,1)} %dynamic_slice.32), channel_id=1, source_target_pairs={{18,2},{1,21}} | collective-permute-start | bytes 3145736 | tf_op jit(solution)/shard_map/ppermute | solution.py:522
  4.7 2.3 %constant_dynamic-slice_fusion.1 = bf16[2048,256]{1,0:T(8,128)(2,1)} fusion(bf16[2048,512]{1,0:T(8,128)(2,1)} %x.11, s32[]{:T(128)S(6)} %select_n.35), kind=kLoop, calls=%fused_computation.14 | loop fusion | bytes 2097156 | tf_op jit(solution)/shard_map/dynamic_slice | solution.py:445
  7.0 1.3 collective-permute-start.1
  8.4 0.1 dynamic_slice.27
  8.4 0.1 dynamic_slice.28
  8.5 1.0 multiply_reduce_fusion
  9.5 1.1 constant_dynamic-slice_fusion
  10.6 8.2 %collective-permute-start.3 = (bf16[2048,256]{1,0:T(8,128)(2,1)}, bf16[2048,256]{1,0:T(8,128)(2,1)}, u32[]{:S(2)}, u32[]{:S(2)}) collective-permute-start(bf16[2048,256]{1,0:T(8,128)(2,1)} %constant_dynamic-slice_fusion), channel_id=1, source_target_pairs={{0,1},{1,2},{5,4},{10,11},{13,12},{14,13},{18,19},{22,21},{23,22},... | collective-permute-start | bytes 3145736 | tf_op jit(solution)/shard_map/ppermute | solution.py:518
  18.8 0.0 collective-permute-start.10
  18.8 0.7 fusion.2.table
  19.5 0.0 collective-permute-done.refs_0_
  19.5 15.6 %collective-permute-done.1.refs_1_.refs_0_ = bf16[2048,256]{1,0:T(8,128)(2,1)S(1)} collective-permute-done((bf16[2048,256]{1,0:T(8,128)(2,1)}, bf16[2048,256]{1,0:T(8,128)(2,1)S(1)}, u32[]{:S(2)}, u32[]{:S(2)}) %collective-permute-start.1) | collective-permute-done | bytes 1048608 | tf_op jit(solution)/shard_map/ppermute | solution.py:518
  35.1 1.3 relay.4
  36.4 0.0 copy-start.3
  36.5 1.0 copy-done.3
  37.5 1.3 collective-permute-start.2
  38.8 0.0 collective-permute-done.3.refs_0_.refs_1_
  38.8 1.3 relay.5
  40.1 0.0 copy-start.9
  40.1 4.6 %collective-permute-start.4 = (bf16[2048,256]{1,0:T(8,128)(2,1)S(1)}, bf16[2048,256]{1,0:T(8,128)(2,1)S(1)}, u32[]{:S(2)}, u32[]{:S(2)}) collective-permute-start(bf16[2048,256]{1,0:T(8,128)(2,1)S(1)} %relay.5), channel_id=1, source_target_pairs={{0,1},{1,2},{2,3},{5,4},{6,5},{9,10},{10,11},{13,12},{14,13},{15,1... | collective-permute-start | bytes 3145736 | tf_op jit(solution)/shard_map/ppermute | solution.py:518
  44.7 0.0 collective-permute-done.10.refs_1_
  44.7 0.1 collective-permute-start.11
  44.8 20.1 %collective-permute-done.2.refs_0_.refs_2_ = bf16[2048,256]{1,0:T(8,128)(2,1)S(1)} collective-permute-done((bf16[2048,256]{1,0:T(8,128)(2,1)S(1)}, bf16[2048,256]{1,0:T(8,128)(2,1)S(1)}, u32[]{:S(2)}, u32[]{:S(2)}) %collective-permute-start.2) | collective-permute-done | bytes 1048608 | tf_op jit(solution)/shard_map/ppermute | solution.py:518
  64.9 0.6 relay.6
  65.5 1.3 collective-permute-start.5
  66.8 0.7 collective-permute-start.7
  67.6 0.0 collective-permute-done.4.refs_0_.refs_3_.refs_1_
  67.6 0.0 copy-start.1
  67.6 0.6 relay.7
  68.2 1.7 %collective-permute-start.6 = (bf16[2048,256]{1,0:T(8,128)(2,1)S(1)}, bf16[2048,256]{1,0:T(8,128)(2,1)}, u32[]{:S(2)}, u32[]{:S(2)}) collective-permute-start(bf16[2048,256]{1,0:T(8,128)(2,1)S(1)} %relay.7), channel_id=1, source_target_pairs={{1,2},{2,3},{5,4},{9,10},{10,11},{13,12},{14,13},{21,20},{22,21},{... | collective-permute-start | bytes 3145736 | tf_op jit(solution)/shard_map/ppermute | solution.py:518
  69.9 0.0 collective-permute-done.11.refs_2_
  69.9 0.0 collective-permute-start.12
  69.9 23.0 %collective-permute-done.5.refs_5_.refs_2_ = bf16[2048,256]{1,0:T(8,128)(2,1)} collective-permute-done((bf16[2048,256]{1,0:T(8,128)(2,1)S(1)}, bf16[2048,256]{1,0:T(8,128)(2,1)}, u32[]{:S(2)}, u32[]{:S(2)}) %collective-permute-start.5) | collective-permute-done | bytes 1048608 | tf_op jit(solution)/shard_map/ppermute | solution.py:518
  92.9 4.1 %collective-permute-start.13 = (bf16[2048,256]{1,0:T(8,128)(2,1)}, bf16[2048,256]{1,0:T(8,128)(2,1)}, u32[]{:S(2)}, u32[]{:S(2)}) collective-permute-start(bf16[2048,256]{1,0:T(8,128)(2,1)} %collective-permute-done.5.refs_5_.refs_2_), channel_id=1, source_target_pairs={{0,16},{23,3}} | collective-permute-start | bytes 3145736 | tf_op jit(solution)/shard_map/ppermute | solution.py:498
  97.0 0.0 collective-permute-done.7.refs_4_
  97.0 1.0 copy-done.5
  97.9 1.6 %collective-permute-start.8 = (bf16[2048,256]{1,0:T(8,128)(2,1)}, bf16[2048,256]{1,0:T(8,128)(2,1)}, u32[]{:S(2)}, u32[]{:S(2)}) collective-permute-start(bf16[2048,256]{1,0:T(8,128)(2,1)} %collective-permute-done.5.refs_5_.refs_2_), channel_id=1, source_target_pairs={{6,7},{9,8},{17,16},{22,23},{25,24},{30,31}} | collective-permute-start | bytes 3145736 | tf_op jit(solution)/shard_map/ppermute | solution.py:518
  99.6 0.0 collective-permute-done.6.refs_6_.refs_3_
  99.6 1.6 %collective-permute-start.9 = (bf16[2048,256]{1,0:T(8,128)(2,1)}, bf16[2048,256]{1,0:T(8,128)(2,1)}, u32[]{:S(2)}, u32[]{:S(2)}) collective-permute-start(bf16[2048,256]{1,0:T(8,128)(2,1)} %collective-permute-done.6.refs_6_.refs_3_), channel_id=1, source_target_pairs={{2,3},{10,11},{13,12},{21,20},{26,27}} | collective-permute-start | bytes 3145736 | tf_op jit(solution)/shard_map/ppermute | solution.py:518
  101.2 0.1 fusion
  101.3 0.0 collective-permute-done.12.refs_3_
  101.3 0.2 broadcast_in_dim.43.refs_5_
  101.5 0.2 broadcast_in_dim.42.refs_4_
  101.7 0.0 copy-start.7
  101.7 1.2 copy-done.7
  102.9 3.6 %window.1.refs_11_.refs_9_ = bf16[1024,2048]{1,0:T(8,128)(2,1)S(1)} custom-call(s32[24]{0:T(128)S(1)} %fusion.2.table, bf16[256,2048]{1,0:T(8,128)(2,1)S(1)} %copy-done.7, bf16[256,2048]{1,0:T(8,128)(2,1)} %collective-permute-done.10.refs_1_, bf16[256,2048]{1,0:T(8,128)(2,1)} %collective-permute-done.11.refs_2_, ...), custom_call_target="tpu_custom_call" | custom-call | flops 8388608 | bytes 8388608 | tf_op jit(solution)/shard_map/window/pallas_call | solution.py:202
  106.5 2.0 %collective-permute-done.13.refs_7_ = bf16[2048,256]{1,0:T(8,128)(2,1)} collective-permute-done((bf16[2048,256]{1,0:T(8,128)(2,1)}, bf16[2048,256]{1,0:T(8,128)(2,1)}, u32[]{:S(2)}, u32[]{:S(2)}) %collective-permute-start.13) | collective-permute-done | bytes 1048608 | tf_op jit(solution)/shard_map/ppermute | solution.py:498
  108.5 0.3 broadcast_in_dim.41.refs_10_.refs_8_
  108.8 11.7 %early.1.refs_10_ = f32[2048,2048]{1,0:T(8,128)S(1)} custom-call(s32[24]{0:T(128)S(1)} %fusion.2.table, bf16[2048,512]{1,0:T(8,128)(2,1)S(1)} %copy-done, bf16[2048,256]{1,0:T(8,128)(2,1)S(1)} %copy-done.4, bf16[2048,256]{1,0:T(8,128)(2,1)} %collective-permute-done.3.refs_0_.refs_1_, bf16[2048,256]{1,0:T(8,128)(2,1)S(1)} %collective-permute-done.2.refs_0_.refs_2_, ...), custom_call_target="tpu_custom_call" | custom-call | flops 6442450944 | tf_op jit(solution)/shard_map/early/pallas_call | solution.py:263
  120.6 0.1 collective-permute-start.16
  120.7 0.1 collective-permute-start.15
  120.7 4.3 %collective-permute-start.14 = (f32[2048]{0:T(1024)S(1)}, f32[2048]{0:T(1024)S(1)}, u32[]{:S(2)}, u32[]{:S(2)}) collective-permute-start(f32[2048]{0:T(1024)S(1)} %multiply_reduce_fusion), channel_id=1, source_target_pairs={{0,1},{1,0},{2,3},{3,2},{4,5},{5,4},{6,7},{7,6},{8,9},{9,8},{10,11... | collective-permute-start | bytes 24584 | tf_op jit(solution)/shard_map/ppermute | solution.py:487
  125.0 0.0 collective-permute-done.8.refs_4_
  125.0 0.0 collective-permute-done.9.refs_5_
  125.0 7.4 %last.1 = bf16[2048,2048]{1,0:T(8,128)(2,1)} custom-call(s32[24]{0:T(128)S(1)} %fusion.2.table, bf16[2048,512]{1,0:T(8,128)(2,1)S(1)} %copy-done, bf16[2048,256]{1,0:T(8,128)(2,1)S(1)} %collective-permute-done.2.refs_0_.refs_2_, bf16[2048,256]{1,0:T(8,128)(2,1)S(1)} %copy-done.2, bf16[2048,256]{1,0:T(8,128)(2,1)} %collective-permute-done.5.refs_5_.refs_2_, ...), custom_call_target="tpu_custom_call" | custom-call | flops 2147483648 | bytes 8388608 | tf_op jit(solution)/shard_map/last/pallas_call | solution.py:307
  132.5 0.0 collective-permute-done.16
  132.5 0.0 collective-permute-done.15
  132.5 0.0 collective-permute-done.14
  132.5 0.6 multiply_add_fusion
  (16 shorter events, 0.0 us)
Async XLA Ops:
  0.6 7.9 %copy-start = (bf16[2048,512]{1,0:T(8,128)(2,1)S(1)}, bf16[2048,512]{1,0:T(8,128)(2,1)}, u32[]{:S(2)}) copy-start(bf16[2048,512]{1,0:T(8,128)(2,1)} %x.11) | copy-start | bytes 6291460
  0.6 7.6 %copy-start.11 = (f32[2048]{0:T(1024)S(1)}, f32[2048]{0:T(1024)}, u32[]{:S(2)}) copy-start(f32[2048]{0:T(1024)} %param.10) | copy-start | bytes 24580
  0.7 7.6 %copy-start.10 = (f32[2048]{0:T(1024)S(1)}, f32[2048]{0:T(1024)}, u32[]{:S(2)}) copy-start(f32[2048]{0:T(1024)} %param.9) | copy-start | bytes 24580
  0.7 7.7 %copy-start.8 = (s32[2048]{0:T(1024)S(1)}, s32[2048]{0:T(1024)}, u32[]{:S(2)}) copy-start(s32[2048]{0:T(1024)} %param.11) | copy-start | bytes 24580
  3.1 16.4 %collective-permute-start = (bf16[2048,256]{1,0:T(8,128)(2,1)}, bf16[2048,256]{1,0:T(8,128)(2,1)}, u32[]{:S(2)}, u32[]{:S(2)}) collective-permute-start(bf16[2048,256]{1,0:T(8,128)(2,1)} %dynamic_slice.32), channel_id=1, source_target_pairs={{18,2},{1,21}} | collective-permute-start | bytes 3145736 | tf_op jit(solution)/shard_map/ppermute | solution.py:522
  7.0 28.1 %collective-permute-start.1 = (bf16[2048,256]{1,0:T(8,128)(2,1)}, bf16[2048,256]{1,0:T(8,128)(2,1)S(1)}, u32[]{:S(2)}, u32[]{:S(2)}) collective-permute-start(bf16[2048,256]{1,0:T(8,128)(2,1)} %constant_dynamic-slice_fusion.1), channel_id=1, source_target_pairs={{1,0},{5,6},{6,7},{9,8},{14,15},{18,17},{19,18},{22,23},{27,26},{2... | collective-permute-start | bytes 3145736 | tf_op jit(solution)/shard_map/ppermute | solution.py:518
  10.6 28.1 %collective-permute-start.3 = (bf16[2048,256]{1,0:T(8,128)(2,1)}, bf16[2048,256]{1,0:T(8,128)(2,1)}, u32[]{:S(2)}, u32[]{:S(2)}) collective-permute-start(bf16[2048,256]{1,0:T(8,128)(2,1)} %constant_dynamic-slice_fusion), channel_id=1, source_target_pairs={{0,1},{1,2},{5,4},{10,11},{13,12},{14,13},{18,19},{22,21},{23,22},... | collective-permute-start | bytes 3145736 | tf_op jit(solution)/shard_map/ppermute | solution.py:518
  18.8 25.9 %collective-permute-start.10 = (bf16[256,2048]{1,0:T(8,128)(2,1)}, bf16[256,2048]{1,0:T(8,128)(2,1)}, u32[]{:S(2)}, u32[]{:S(2)}) collective-permute-start(bf16[256,2048]{1,0:T(8,128)(2,1)} %refs_0_.1), channel_id=1, source_target_pairs={{0,28},{4,0},{8,4},{12,8},{16,12},{20,16},{24,20},{28,24},{1,29},{... | collective-permute-start | bytes 3145736 | tf_op jit(solution)/shard_map/ppermute | solution.py:469
  36.4 1.0 copy-start.3
  37.5 27.4 %collective-permute-start.2 = (bf16[2048,256]{1,0:T(8,128)(2,1)S(1)}, bf16[2048,256]{1,0:T(8,128)(2,1)S(1)}, u32[]{:S(2)}, u32[]{:S(2)}) collective-permute-start(bf16[2048,256]{1,0:T(8,128)(2,1)S(1)} %relay.4), channel_id=1, source_target_pairs={{1,0},{2,1},{4,5},{5,6},{6,7},{9,8},{10,9},{13,14},{14,15},{17,16}... | collective-permute-start | bytes 3145736 | tf_op jit(solution)/shard_map/ppermute | solution.py:518
  40.1 61.2 %copy-start.9 = (s32[2048]{0:T(1024)S(1)}, s32[2048]{0:T(1024)}, u32[]{:S(2)}) copy-start(s32[2048]{0:T(1024)} %param.12) | copy-start | bytes 24580
  40.1 27.5 %collective-permute-start.4 = (bf16[2048,256]{1,0:T(8,128)(2,1)S(1)}, bf16[2048,256]{1,0:T(8,128)(2,1)S(1)}, u32[]{:S(2)}, u32[]{:S(2)}) collective-permute-start(bf16[2048,256]{1,0:T(8,128)(2,1)S(1)} %relay.5), channel_id=1, source_target_pairs={{0,1},{1,2},{2,3},{5,4},{6,5},{9,10},{10,11},{13,12},{14,13},{15,1... | collective-permute-start | bytes 3145736 | tf_op jit(solution)/shard_map/ppermute | solution.py:518
  44.7 25.1 %collective-permute-start.11 = (bf16[256,2048]{1,0:T(8,128)(2,1)}, bf16[256,2048]{1,0:T(8,128)(2,1)}, u32[]{:S(2)}, u32[]{:S(2)}) collective-permute-start(bf16[256,2048]{1,0:T(8,128)(2,1)} %collective-permute-done.10.refs_1_), channel_id=1, source_target_pairs={{0,28},{4,0},{8,4},{12,8},{16,12},{20,16},{24,20},{28,24},{1,29},{... | collective-permute-start | bytes 3145736 | tf_op jit(solution)/shard_map/ppermute | solution.py:469
  65.5 27.4 %collective-permute-start.5 = (bf16[2048,256]{1,0:T(8,128)(2,1)S(1)}, bf16[2048,256]{1,0:T(8,128)(2,1)}, u32[]{:S(2)}, u32[]{:S(2)}) collective-permute-start(bf16[2048,256]{1,0:T(8,128)(2,1)S(1)} %relay.6), channel_id=1, source_target_pairs={{1,0},{5,6},{6,7},{9,8},{10,9},{14,15},{17,16},{18,17},{21,22},{22... | collective-permute-start | bytes 3145736 | tf_op jit(solution)/shard_map/ppermute | solution.py:518
  66.8 30.1 %collective-permute-start.7 = (bf16[2048,256]{1,0:T(8,128)(2,1)S(1)}, bf16[2048,256]{1,0:T(8,128)(2,1)S(1)}, u32[]{:S(2)}, u32[]{:S(2)}) collective-permute-start(bf16[2048,256]{1,0:T(8,128)(2,1)S(1)} %collective-permute-done.2.refs_0_.refs_2_), channel_id=1, source_target_pairs={{1,17},{22,2}} | collective-permute-start | bytes 3145736 | tf_op jit(solution)/shard_map/ppermute | solution.py:498
  67.6 29.4 %copy-start.1 = (bf16[2048,256]{1,0:T(8,128)(2,1)}, bf16[2048,256]{1,0:T(8,128)(2,1)S(1)}, u32[]{:S(2)}) copy-start(bf16[2048,256]{1,0:T(8,128)(2,1)S(1)} %collective-permute-done.4.refs_0_.refs_3_.refs_1_) | copy-start | bytes 3145732
  68.2 31.4 %collective-permute-start.6 = (bf16[2048,256]{1,0:T(8,128)(2,1)S(1)}, bf16[2048,256]{1,0:T(8,128)(2,1)}, u32[]{:S(2)}, u32[]{:S(2)}) collective-permute-start(bf16[2048,256]{1,0:T(8,128)(2,1)S(1)} %relay.7), channel_id=1, source_target_pairs={{1,2},{2,3},{5,4},{9,10},{10,11},{13,12},{14,13},{21,20},{22,21},{... | collective-permute-start | bytes 3145736 | tf_op jit(solution)/shard_map/ppermute | solution.py:518
  69.9 31.4 %collective-permute-start.12 = (bf16[256,2048]{1,0:T(8,128)(2,1)}, bf16[256,2048]{1,0:T(8,128)(2,1)}, u32[]{:S(2)}, u32[]{:S(2)}) collective-permute-start(bf16[256,2048]{1,0:T(8,128)(2,1)} %collective-permute-done.11.refs_2_), channel_id=1, source_target_pairs={{0,28},{4,0},{8,4},{12,8},{16,12},{20,16},{24,20},{28,24},{1,29},{... | collective-permute-start | bytes 3145736 | tf_op jit(solution)/shard_map/ppermute | solution.py:469
  92.9 15.6 %collective-permute-start.13 = (bf16[2048,256]{1,0:T(8,128)(2,1)}, bf16[2048,256]{1,0:T(8,128)(2,1)}, u32[]{:S(2)}, u32[]{:S(2)}) collective-permute-start(bf16[2048,256]{1,0:T(8,128)(2,1)} %collective-permute-done.5.refs_5_.refs_2_), channel_id=1, source_target_pairs={{0,16},{23,3}} | collective-permute-start | bytes 3145736 | tf_op jit(solution)/shard_map/ppermute | solution.py:498
  97.0 1.0 copy-start.5
  97.9 27.1 %collective-permute-start.8 = (bf16[2048,256]{1,0:T(8,128)(2,1)}, bf16[2048,256]{1,0:T(8,128)(2,1)}, u32[]{:S(2)}, u32[]{:S(2)}) collective-permute-start(bf16[2048,256]{1,0:T(8,128)(2,1)} %collective-permute-done.5.refs_5_.refs_2_), channel_id=1, source_target_pairs={{6,7},{9,8},{17,16},{22,23},{25,24},{30,31}} | collective-permute-start | bytes 3145736 | tf_op jit(solution)/shard_map/ppermute | solution.py:518
  99.6 25.5 %collective-permute-start.9 = (bf16[2048,256]{1,0:T(8,128)(2,1)}, bf16[2048,256]{1,0:T(8,128)(2,1)}, u32[]{:S(2)}, u32[]{:S(2)}) collective-permute-start(bf16[2048,256]{1,0:T(8,128)(2,1)} %collective-permute-done.6.refs_6_.refs_3_), channel_id=1, source_target_pairs={{2,3},{10,11},{13,12},{21,20},{26,27}} | collective-permute-start | bytes 3145736 | tf_op jit(solution)/shard_map/ppermute | solution.py:518
  101.7 1.2 copy-start.7
  102.9 5.9 %copy-start.2 = (bf16[2048,256]{1,0:T(8,128)(2,1)S(1)}, bf16[2048,256]{1,0:T(8,128)(2,1)}, u32[]{:S(2)}) copy-start(bf16[2048,256]{1,0:T(8,128)(2,1)} %copy-done.1) | copy-start | bytes 3145732
  102.9 5.9 %copy-start.4 = (bf16[2048,256]{1,0:T(8,128)(2,1)S(1)}, bf16[2048,256]{1,0:T(8,128)(2,1)}, u32[]{:S(2)}) copy-start(bf16[2048,256]{1,0:T(8,128)(2,1)} %copy-done.3) | copy-start | bytes 3145732
  102.9 5.9 %copy-start.6 = (bf16[2048,256]{1,0:T(8,128)(2,1)S(1)}, bf16[2048,256]{1,0:T(8,128)(2,1)}, u32[]{:S(2)}) copy-start(bf16[2048,256]{1,0:T(8,128)(2,1)} %copy-done.5) | copy-start | bytes 3145732
  120.6 11.9 %collective-permute-start.16 = (f32[2048]{0:T(1024)S(1)}, f32[2048]{0:T(1024)S(1)}, u32[]{:S(2)}, u32[]{:S(2)}) collective-permute-start(f32[2048]{0:T(1024)S(1)} %multiply_reduce_fusion), channel_id=1, source_target_pairs={{0,3},{1,2},{2,1},{3,0},{4,7},{5,6},{6,5},{7,4},{8,11},{9,10},{10,... | collective-permute-start | bytes 24584 | tf_op jit(solution)/shard_map/ppermute | solution.py:487
  120.7 11.8 %collective-permute-start.15 = (f32[2048]{0:T(1024)S(1)}, f32[2048]{0:T(1024)S(1)}, u32[]{:S(2)}, u32[]{:S(2)}) collective-permute-start(f32[2048]{0:T(1024)S(1)} %multiply_reduce_fusion), channel_id=1, source_target_pairs={{0,2},{1,3},{2,0},{3,1},{4,6},{5,7},{6,4},{7,5},{8,10},{9,11},{10,... | collective-permute-start | bytes 24584 | tf_op jit(solution)/shard_map/ppermute | solution.py:487
  120.7 11.7 %collective-permute-start.14 = (f32[2048]{0:T(1024)S(1)}, f32[2048]{0:T(1024)S(1)}, u32[]{:S(2)}, u32[]{:S(2)}) collective-permute-start(f32[2048]{0:T(1024)S(1)} %multiply_reduce_fusion), channel_id=1, source_target_pairs={{0,1},{1,0},{2,3},{3,2},{4,5},{5,4},{6,7},{7,6},{8,9},{9,8},{10,11... | collective-permute-start | bytes 24584 | tf_op jit(solution)/shard_map/ppermute | solution.py:487

commit v17 on v16

--- a/solution.py
+++ b/solution.py
@@ -479,16 +479,17 @@
     later_x, squares = lax.optimization_barrier((later_x, squares))
     if any(own_of[1, 1]):
         starts[1, 1] = own_chunk(own_of[1, 1], later_x)
-    def col_sum_beside(value, squares):
-        if cols & (cols - 1):
-            return value, lax.psum(squares, "col")
-        parts = [squares]
-        for mask in range(1, cols):
-            parts.append(lax.ppermute(squares, "col", [(i, i ^ mask) for i in range(cols)]))
-        value, *parts = lax.optimization_barrier((value, *parts))
-        while len(parts) > 1:
-            parts = [a + b for a, b in zip(parts[::2], parts[1::2])]
-        return value, parts[0]
+    bits = [1 << k for k in range(cols.bit_length() - 1)] if cols & (cols - 1) == 0 else []
+    if cols & (cols - 1):
+        squares = lax.psum(squares, "col")
+
+    def sum_beside(value, squares):
+        if not bits:
+            return value, squares
+        bit = bits.pop(0)
+        other = lax.ppermute(squares, "col", [(i, i ^ bit) for i in range(cols)])
+        value, other = lax.optimization_barrier((value, other))
+        return value, squares + other
 
     buffers, crossed = {}, {}
 
@@ -522,11 +523,13 @@
                 crossed[k] = lax.ppermute(starts["cross", k], both, pairs)
         bring_back(key)
     zy = standardized_window(rank_at, table, window, wide(window_factor), wide(window_twice), male_cols[None, :])
+    zy, squares = sum_beside(zy, squares)
     shared = window_factor[None, :], window_twice[None, :], male_wide, zy
     total = early_product(source_at[0], candidates[0], table, x, [buffers[k] for k in used[0]], *shared)
-    total, squares = lax.optimization_barrier((total, squares))
+    total, squares = sum_beside(total, squares)
     relation = last_product(source_at[1], candidates[1][0], table, x, [buffers[k] for k in used[1]], *shared, total)
-    relation, squares = col_sum_beside(relation, squares)
+    for bit in bits:
+        squares = squares + lax.ppermute(squares, "col", [(i, i ^ bit) for i in range(cols)])
     inbreeding = squares / jnp.float32(freq.shape[0]) - 1.0
     return relation, inbreeding
 

time: 134 us -> 116 us (0.87)
  the two profiles are of different devices: /device:TPU:0 before, /device:TPU:2 now
where the time goes in v17:
time: 116 us; the launch traced here: 115 us
  waiting for transfers between devices  56.3 us (49%)
  Pallas kernels  26.1 us (22%)
  starting transfers between devices  19.5 us (17%)
  local copies, waits for them, and re-layouts  10.5 us (9%)
  other arithmetic  1.73 us (1%)
    ppermute x8, waiting for transfers between devices, local(): buffers[key] = lax.ppermute(held, both, pairs_of[key])  56.3 us
    pallas_call x1, Pallas kernels, early_product(): pl.pallas_call(functools.partial(early_kernel, at, candidates, len(buffer...  11.3 us
    ppermute x8, starting transfers between devices, local(): buffers[key] = lax.ppermute(held, both, pairs_of[key])  10.8 us
    pallas_call x1, Pallas kernels, last_product(): pl.pallas_call(functools.partial(last_kernel, at, candidates, scale, len(...  7.39 us
    dynamic_slice x3, local copies, waits for them, and re-layouts, own_chunk(): lax.dynamic_slice(x, (piece * piece_rows, group * group_size), (piece_row...  5.72 us
    pallas_call x4, Pallas kernels, relay(): pl.pallas_call(functools.partial(relay_kernel, at), out_shape=pltpu.VMEM(...  3.88 us
    pallas_call x1, Pallas kernels, standardized_window(): pl.pallas_call(functools.partial(window_kernel, at), out_shape=pltpu.VMEM...  3.54 us
    unnamed x24, local copies, waits for them, and re-layouts  3.23 us
  transfers between devices with their start and end apart: 16, of which 4 were waited for; matrix products, arithmetic and copies ran while one was open for 6% of the time, Pallas kernels for 16%

profile of v17, /device:TPU:2, one launch (start us, length us, event | category | flops | bytes accessed | tf_op | source)
XLA Modules:
  0.0 115.1 jit_solution(8024676124709228540)
XLA Ops:
  0.6 0.0 copy-start
  0.6 0.0 copy-start.11
  0.7 0.0 copy-start.10
  0.7 2.4 %constant_dynamic-slice_fusion.1 = bf16[2048,256]{1,0:T(8,128)(2,1)} fusion(bf16[2048,512]{1,0:T(8,128)(2,1)} %x.11, s32[]{:T(128)S(6)} %select_n.35), kind=kLoop, calls=%fused_computation.14 | loop fusion | bytes 2097156 | tf_op jit(solution)/shard_map/dynamic_slice | solution.py:445
  3.1 1.3 %collective-permute-start.1 = (bf16[2048,256]{1,0:T(8,128)(2,1)}, bf16[2048,256]{1,0:T(8,128)(2,1)S(1)}, u32[]{:S(2)}, u32[]{:S(2)}) collective-permute-start(bf16[2048,256]{1,0:T(8,128)(2,1)} %constant_dynamic-slice_fusion.1), channel_id=1, source_target_pairs={{1,0},{5,6},{6,7},{9,8},{14,15},{18,17},{19,18},{22,23},{27,26},{2... | collective-permute-start | bytes 3145736 | tf_op jit(solution)/shard_map/ppermute | solution.py:519
  4.4 2.3 %dynamic_slice.32 = bf16[2048,256]{1,0:T(8,128)(2,1)} slice(bf16[2048,512]{1,0:T(8,128)(2,1)} %x.11), slice={[0:2048], [256:512]} | slice | bytes 2097152 | tf_op jit(solution)/shard_map/dynamic_slice | solution.py:445
  6.7 1.7 %collective-permute-start = (bf16[2048,256]{1,0:T(8,128)(2,1)}, bf16[2048,256]{1,0:T(8,128)(2,1)}, u32[]{:S(2)}, u32[]{:S(2)}) collective-permute-start(bf16[2048,256]{1,0:T(8,128)(2,1)} %dynamic_slice.32), channel_id=1, source_target_pairs={{18,2},{1,21}} | collective-permute-start | bytes 3145736 | tf_op jit(solution)/shard_map/ppermute | solution.py:523
  8.3 0.0 copy-done.10
  8.3 0.1 dynamic_slice.27
  8.4 0.1 dynamic_slice.28
  8.5 0.0 copy-done.8
  8.5 0.0 copy-done
  8.5 1.0 multiply_reduce_fusion
  9.6 1.0 constant_dynamic-slice_fusion
  10.6 1.7 %collective-permute-start.3 = (bf16[2048,256]{1,0:T(8,128)(2,1)}, bf16[2048,256]{1,0:T(8,128)(2,1)}, u32[]{:S(2)}, u32[]{:S(2)}) collective-permute-start(bf16[2048,256]{1,0:T(8,128)(2,1)} %constant_dynamic-slice_fusion), channel_id=1, source_target_pairs={{0,1},{1,2},{5,4},{10,11},{13,12},{14,13},{18,19},{22,21},{23,22},... | collective-permute-start | bytes 3145736 | tf_op jit(solution)/shard_map/ppermute | solution.py:519
  12.2 0.0 collective-permute-start.10
  12.3 0.7 fusion.2.table
  12.9 12.5 %collective-permute-done.1.refs_1_.refs_0_ = bf16[2048,256]{1,0:T(8,128)(2,1)S(1)} collective-permute-done((bf16[2048,256]{1,0:T(8,128)(2,1)}, bf16[2048,256]{1,0:T(8,128)(2,1)S(1)}, u32[]{:S(2)}, u32[]{:S(2)}) %collective-permute-start.1) | collective-permute-done | bytes 1048608 | tf_op jit(solution)/shard_map/ppermute | solution.py:519
  25.4 0.0 collective-permute-done.refs_0_
  25.4 1.3 %relay.4 = bf16[2048,256]{1,0:T(8,128)(2,1)S(1)} custom-call(s32[24]{0:T(128)S(1)} %fusion.2.table, bf16[2048,512]{1,0:T(8,128)(2,1)S(1)} %copy-done, bf16[2048,256]{1,0:T(8,128)(2,1)} %collective-permute-done.refs_0_, bf16[2048,256]{1,0:T(8,128)(2,1)S(1)} %collective-permute-done.1.refs_1_.refs_0_), custom_call_target="tpu_custom_call" | custom-call | tf_op jit(solution)/shard_map/relay/pallas_call | solution.py:164
  26.8 1.0 copy-done.3
  27.8 1.3 %collective-permute-start.2 = (bf16[2048,256]{1,0:T(8,128)(2,1)S(1)}, bf16[2048,256]{1,0:T(8,128)(2,1)S(1)}, u32[]{:S(2)}, u32[]{:S(2)}) collective-permute-start(bf16[2048,256]{1,0:T(8,128)(2,1)S(1)} %relay.4), channel_id=1, source_target_pairs={{1,0},{2,1},{4,5},{5,6},{6,7},{9,8},{10,9},{13,14},{14,15},{17,16}... | collective-permute-start | bytes 3145736 | tf_op jit(solution)/shard_map/ppermute | solution.py:519
  29.1 0.0 collective-permute-done.3.refs_0_.refs_1_
  29.1 1.3 %relay.5 = bf16[2048,256]{1,0:T(8,128)(2,1)S(1)} custom-call(s32[24]{0:T(128)S(1)} %fusion.2.table, bf16[2048,512]{1,0:T(8,128)(2,1)S(1)} %copy-done, bf16[2048,256]{1,0:T(8,128)(2,1)} %collective-permute-done.3.refs_0_.refs_1_), custom_call_target="tpu_custom_call" | custom-call | tf_op jit(solution)/shard_map/relay/pallas_call | solution.py:164
  30.4 0.0 copy-start.9
  30.4 0.7 collective-permute-start.4
  31.1 0.0 collective-permute-done.10.refs_1_
  31.1 2.8 %collective-permute-start.11 = (bf16[256,2048]{1,0:T(8,128)(2,1)}, bf16[256,2048]{1,0:T(8,128)(2,1)}, u32[]{:S(2)}, u32[]{:S(2)}) collective-permute-start(bf16[256,2048]{1,0:T(8,128)(2,1)} %collective-permute-done.10.refs_1_), channel_id=1, source_target_pairs={{0,28},{4,0},{8,4},{12,8},{16,12},{20,16},{24,20},{28,24},{1,29},{... | collective-permute-start | bytes 3145736 | tf_op jit(solution)/shard_map/ppermute | solution.py:469
  33.9 17.9 %collective-permute-done.2.refs_0_.refs_2_ = bf16[2048,256]{1,0:T(8,128)(2,1)S(1)} collective-permute-done((bf16[2048,256]{1,0:T(8,128)(2,1)S(1)}, bf16[2048,256]{1,0:T(8,128)(2,1)S(1)}, u32[]{:S(2)}, u32[]{:S(2)}) %collective-permute-start.2) | collective-permute-done | bytes 1048608 | tf_op jit(solution)/shard_map/ppermute | solution.py:519
  51.8 0.6 relay.6
  52.5 1.3 %collective-permute-start.5 = (bf16[2048,256]{1,0:T(8,128)(2,1)S(1)}, bf16[2048,256]{1,0:T(8,128)(2,1)}, u32[]{:S(2)}, u32[]{:S(2)}) collective-permute-start(bf16[2048,256]{1,0:T(8,128)(2,1)S(1)} %relay.6), channel_id=1, source_target_pairs={{1,0},{5,6},{6,7},{9,8},{10,9},{14,15},{17,16},{18,17},{21,22},{22... | collective-permute-start | bytes 3145736 | tf_op jit(solution)/shard_map/ppermute | solution.py:519
  53.8 0.7 collective-permute-start.7
  54.5 0.0 collective-permute-done.4.refs_0_.refs_3_.refs_1_
  54.5 0.0 copy-start.1
  54.5 0.6 relay.7
  55.1 1.7 %collective-permute-start.6 = (bf16[2048,256]{1,0:T(8,128)(2,1)S(1)}, bf16[2048,256]{1,0:T(8,128)(2,1)}, u32[]{:S(2)}, u32[]{:S(2)}) collective-permute-start(bf16[2048,256]{1,0:T(8,128)(2,1)S(1)} %relay.7), channel_id=1, source_target_pairs={{1,2},{2,3},{5,4},{9,10},{10,11},{13,12},{14,13},{21,20},{22,21},{... | collective-permute-start | bytes 3145736 | tf_op jit(solution)/shard_map/ppermute | solution.py:519
  56.8 0.0 collective-permute-done.11.refs_2_
  56.8 0.0 collective-permute-start.12
  56.8 20.9 %collective-permute-done.5.refs_5_.refs_2_ = bf16[2048,256]{1,0:T(8,128)(2,1)} collective-permute-done((bf16[2048,256]{1,0:T(8,128)(2,1)S(1)}, bf16[2048,256]{1,0:T(8,128)(2,1)}, u32[]{:S(2)}, u32[]{:S(2)}) %collective-permute-start.5) | collective-permute-done | bytes 1048608 | tf_op jit(solution)/shard_map/ppermute | solution.py:519
  77.7 1.7 %collective-permute-start.14 = (bf16[2048,256]{1,0:T(8,128)(2,1)}, bf16[2048,256]{1,0:T(8,128)(2,1)}, u32[]{:S(2)}, u32[]{:S(2)}) collective-permute-start(bf16[2048,256]{1,0:T(8,128)(2,1)} %collective-permute-done.5.refs_5_.refs_2_), channel_id=1, source_target_pairs={{0,16},{23,3}} | collective-permute-start | bytes 3145736 | tf_op jit(solution)/shard_map/ppermute | solution.py:499
  79.4 0.0 collective-permute-start.13
  79.5 0.0 collective-permute-done.7.refs_4_
  79.5 1.0 copy-done.5
  80.4 1.3 %collective-permute-start.8 = (bf16[2048,256]{1,0:T(8,128)(2,1)}, bf16[2048,256]{1,0:T(8,128)(2,1)}, u32[]{:S(2)}, u32[]{:S(2)}) collective-permute-start(bf16[2048,256]{1,0:T(8,128)(2,1)} %collective-permute-done.5.refs_5_.refs_2_), channel_id=1, source_target_pairs={{6,7},{9,8},{17,16},{22,23},{25,24},{30,31}} | collective-permute-start | bytes 3145736 | tf_op jit(solution)/shard_map/ppermute | solution.py:519
  81.7 0.0 collective-permute-done.6.refs_6_.refs_3_
  81.7 1.6 %collective-permute-start.9 = (bf16[2048,256]{1,0:T(8,128)(2,1)}, bf16[2048,256]{1,0:T(8,128)(2,1)}, u32[]{:S(2)}, u32[]{:S(2)}) collective-permute-start(bf16[2048,256]{1,0:T(8,128)(2,1)} %collective-permute-done.6.refs_6_.refs_3_), channel_id=1, source_target_pairs={{2,3},{10,11},{13,12},{21,20},{26,27}} | collective-permute-start | bytes 3145736 | tf_op jit(solution)/shard_map/ppermute | solution.py:519
  83.4 0.0 copy-done.9
  83.4 0.1 fusion
  83.5 0.0 collective-permute-done.12.refs_3_
  83.5 0.2 broadcast_in_dim.42.refs_4_
  83.7 0.2 broadcast_in_dim.43.refs_5_
  83.9 0.0 copy-start.7
  83.9 1.2 %copy-done.7 = bf16[256,2048]{1,0:T(8,128)(2,1)S(1)} copy-done((bf16[256,2048]{1,0:T(8,128)(2,1)S(1)}, bf16[256,2048]{1,0:T(8,128)(2,1)}, u32[]{:S(2)}) %copy-start.7) | copy-done | bytes 1048600
  85.1 3.5 %window.1.refs_11_.refs_9_ = bf16[1024,2048]{1,0:T(8,128)(2,1)S(1)} custom-call(s32[24]{0:T(128)S(1)} %fusion.2.table, bf16[256,2048]{1,0:T(8,128)(2,1)S(1)} %copy-done.7, bf16[256,2048]{1,0:T(8,128)(2,1)} %collective-permute-done.10.refs_1_, bf16[256,2048]{1,0:T(8,128)(2,1)} %collective-permute-done.11.refs_2_, ...), custom_call_target="tpu_custom_call" | custom-call | flops 8388608 | bytes 8388608 | tf_op jit(solution)/shard_map/window/pallas_call | solution.py:202
  88.6 0.0 collective-permute-done.13
  88.7 1.8 %collective-permute-start.15 = (f32[2048]{0:T(1024)S(1)}, f32[2048]{0:T(1024)S(1)}, u32[]{:S(2)}, u32[]{:S(2)}) collective-permute-start(f32[2048]{0:T(1024)S(1)} %add.39), channel_id=1, source_target_pairs={{0,2},{1,3},{2,0},{3,1},{4,6},{5,7},{6,4},{7,5},{8,10},{9,11},{10,... | collective-permute-start | bytes 24584 | tf_op jit(solution)/shard_map/ppermute | solution.py:490
  90.5 0.0 collective-permute-done.14.refs_7_
  90.5 0.3 broadcast_in_dim.41.refs_10_.refs_8_
  90.8 11.3 %early.1.refs_10_ = f32[2048,2048]{1,0:T(8,128)S(1)} custom-call(s32[24]{0:T(128)S(1)} %fusion.2.table, bf16[2048,512]{1,0:T(8,128)(2,1)S(1)} %copy-done, bf16[2048,256]{1,0:T(8,128)(2,1)S(1)} %copy-done.4, bf16[2048,256]{1,0:T(8,128)(2,1)} %collective-permute-done.3.refs_0_.refs_1_, bf16[2048,256]{1,0:T(8,128)(2,1)S(1)} %collective-permute-done.2.refs_0_.refs_2_, ...), custom_call_target="tpu_custom_call" | custom-call | flops 6442450944 | tf_op jit(solution)/shard_map/early/pallas_call | solution.py:263
  102.1 0.0 collective-permute-done.15
  102.2 0.6 multiply_add_fusion
  102.8 5.0 %collective-permute-done.8.refs_4_ = bf16[2048,256]{1,0:T(8,128)(2,1)} collective-permute-done((bf16[2048,256]{1,0:T(8,128)(2,1)}, bf16[2048,256]{1,0:T(8,128)(2,1)}, u32[]{:S(2)}, u32[]{:S(2)}) %collective-permute-start.8) | collective-permute-done | bytes 1048608 | tf_op jit(solution)/shard_map/ppermute | solution.py:519
  107.8 0.0 collective-permute-done.9.refs_5_
  107.8 7.4 %last.1 = bf16[2048,2048]{1,0:T(8,128)(2,1)} custom-call(s32[24]{0:T(128)S(1)} %fusion.2.table, bf16[2048,512]{1,0:T(8,128)(2,1)S(1)} %copy-done, bf16[2048,256]{1,0:T(8,128)(2,1)S(1)} %collective-permute-done.2.refs_0_.refs_2_, bf16[2048,256]{1,0:T(8,128)(2,1)S(1)} %copy-done.2, bf16[2048,256]{1,0:T(8,128)(2,1)} %collective-permute-done.5.refs_5_.refs_2_, ...), custom_call_target="tpu_custom_call" | custom-call | flops 2147483648 | bytes 8388608 | tf_op jit(solution)/shard_map/last/pallas_call | solution.py:307
  (15 shorter events, 0.0 us)
Async XLA Ops:
  0.6 7.9 %copy-start = (bf16[2048,512]{1,0:T(8,128)(2,1)S(1)}, bf16[2048,512]{1,0:T(8,128)(2,1)}, u32[]{:S(2)}) copy-start(bf16[2048,512]{1,0:T(8,128)(2,1)} %x.11) | copy-start | bytes 6291460
  0.6 7.7 %copy-start.11 = (f32[2048]{0:T(1024)S(1)}, f32[2048]{0:T(1024)}, u32[]{:S(2)}) copy-start(f32[2048]{0:T(1024)} %param.10) | copy-start | bytes 24580
  0.7 7.7 %copy-start.10 = (f32[2048]{0:T(1024)S(1)}, f32[2048]{0:T(1024)}, u32[]{:S(2)}) copy-start(f32[2048]{0:T(1024)} %param.9) | copy-start | bytes 24580
  0.7 7.8 %copy-start.8 = (s32[2048]{0:T(1024)S(1)}, s32[2048]{0:T(1024)}, u32[]{:S(2)}) copy-start(s32[2048]{0:T(1024)} %param.11) | copy-start | bytes 24580
  3.1 22.3 %collective-permute-start.1 = (bf16[2048,256]{1,0:T(8,128)(2,1)}, bf16[2048,256]{1,0:T(8,128)(2,1)S(1)}, u32[]{:S(2)}, u32[]{:S(2)}) collective-permute-start(bf16[2048,256]{1,0:T(8,128)(2,1)} %constant_dynamic-slice_fusion.1), channel_id=1, source_target_pairs={{1,0},{5,6},{6,7},{9,8},{14,15},{18,17},{19,18},{22,23},{27,26},{2... | collective-permute-start | bytes 3145736 | tf_op jit(solution)/shard_map/ppermute | solution.py:519
  6.7 18.8 %collective-permute-start = (bf16[2048,256]{1,0:T(8,128)(2,1)}, bf16[2048,256]{1,0:T(8,128)(2,1)}, u32[]{:S(2)}, u32[]{:S(2)}) collective-permute-start(bf16[2048,256]{1,0:T(8,128)(2,1)} %dynamic_slice.32), channel_id=1, source_target_pairs={{18,2},{1,21}} | collective-permute-start | bytes 3145736 | tf_op jit(solution)/shard_map/ppermute | solution.py:523
  10.6 18.5 %collective-permute-start.3 = (bf16[2048,256]{1,0:T(8,128)(2,1)}, bf16[2048,256]{1,0:T(8,128)(2,1)}, u32[]{:S(2)}, u32[]{:S(2)}) collective-permute-start(bf16[2048,256]{1,0:T(8,128)(2,1)} %constant_dynamic-slice_fusion), channel_id=1, source_target_pairs={{0,1},{1,2},{5,4},{10,11},{13,12},{14,13},{18,19},{22,21},{23,22},... | collective-permute-start | bytes 3145736 | tf_op jit(solution)/shard_map/ppermute | solution.py:519
  12.2 18.9 %collective-permute-start.10 = (bf16[256,2048]{1,0:T(8,128)(2,1)}, bf16[256,2048]{1,0:T(8,128)(2,1)}, u32[]{:S(2)}, u32[]{:S(2)}) collective-permute-start(bf16[256,2048]{1,0:T(8,128)(2,1)} %refs_0_.1), channel_id=1, source_target_pairs={{0,28},{4,0},{8,4},{12,8},{16,12},{20,16},{24,20},{28,24},{1,29},{... | collective-permute-start | bytes 3145736 | tf_op jit(solution)/shard_map/ppermute | solution.py:469
  26.8 1.0 copy-start.3
  27.8 24.1 %collective-permute-start.2 = (bf16[2048,256]{1,0:T(8,128)(2,1)S(1)}, bf16[2048,256]{1,0:T(8,128)(2,1)S(1)}, u32[]{:S(2)}, u32[]{:S(2)}) collective-permute-start(bf16[2048,256]{1,0:T(8,128)(2,1)S(1)} %relay.4), channel_id=1, source_target_pairs={{1,0},{2,1},{4,5},{5,6},{6,7},{9,8},{10,9},{13,14},{14,15},{17,16}... | collective-permute-start | bytes 3145736 | tf_op jit(solution)/shard_map/ppermute | solution.py:519
  30.4 53.0 %copy-start.9 = (s32[2048]{0:T(1024)S(1)}, s32[2048]{0:T(1024)}, u32[]{:S(2)}) copy-start(s32[2048]{0:T(1024)} %param.12) | copy-start | bytes 24580
  30.4 24.1 %collective-permute-start.4 = (bf16[2048,256]{1,0:T(8,128)(2,1)S(1)}, bf16[2048,256]{1,0:T(8,128)(2,1)S(1)}, u32[]{:S(2)}, u32[]{:S(2)}) collective-permute-start(bf16[2048,256]{1,0:T(8,128)(2,1)S(1)} %relay.5), channel_id=1, source_target_pairs={{0,1},{1,2},{2,3},{5,4},{6,5},{9,10},{10,11},{13,12},{14,13},{15,1... | collective-permute-start | bytes 3145736 | tf_op jit(solution)/shard_map/ppermute | solution.py:519
  31.1 25.7 %collective-permute-start.11 = (bf16[256,2048]{1,0:T(8,128)(2,1)}, bf16[256,2048]{1,0:T(8,128)(2,1)}, u32[]{:S(2)}, u32[]{:S(2)}) collective-permute-start(bf16[256,2048]{1,0:T(8,128)(2,1)} %collective-permute-done.10.refs_1_), channel_id=1, source_target_pairs={{0,28},{4,0},{8,4},{12,8},{16,12},{20,16},{24,20},{28,24},{1,29},{... | collective-permute-start | bytes 3145736 | tf_op jit(solution)/shard_map/ppermute | solution.py:469
  52.5 25.3 %collective-permute-start.5 = (bf16[2048,256]{1,0:T(8,128)(2,1)S(1)}, bf16[2048,256]{1,0:T(8,128)(2,1)}, u32[]{:S(2)}, u32[]{:S(2)}) collective-permute-start(bf16[2048,256]{1,0:T(8,128)(2,1)S(1)} %relay.6), channel_id=1, source_target_pairs={{1,0},{5,6},{6,7},{9,8},{10,9},{14,15},{17,16},{18,17},{21,22},{22... | collective-permute-start | bytes 3145736 | tf_op jit(solution)/shard_map/ppermute | solution.py:519
  53.8 25.7 %collective-permute-start.7 = (bf16[2048,256]{1,0:T(8,128)(2,1)S(1)}, bf16[2048,256]{1,0:T(8,128)(2,1)S(1)}, u32[]{:S(2)}, u32[]{:S(2)}) collective-permute-start(bf16[2048,256]{1,0:T(8,128)(2,1)S(1)} %collective-permute-done.2.refs_0_.refs_2_), channel_id=1, source_target_pairs={{1,17},{22,2}} | collective-permute-start | bytes 3145736 | tf_op jit(solution)/shard_map/ppermute | solution.py:499
  54.5 25.0 %copy-start.1 = (bf16[2048,256]{1,0:T(8,128)(2,1)}, bf16[2048,256]{1,0:T(8,128)(2,1)S(1)}, u32[]{:S(2)}) copy-start(bf16[2048,256]{1,0:T(8,128)(2,1)S(1)} %collective-permute-done.4.refs_0_.refs_3_.refs_1_) | copy-start | bytes 3145732
  55.1 26.6 %collective-permute-start.6 = (bf16[2048,256]{1,0:T(8,128)(2,1)S(1)}, bf16[2048,256]{1,0:T(8,128)(2,1)}, u32[]{:S(2)}, u32[]{:S(2)}) collective-permute-start(bf16[2048,256]{1,0:T(8,128)(2,1)S(1)} %relay.7), channel_id=1, source_target_pairs={{1,2},{2,3},{5,4},{9,10},{10,11},{13,12},{14,13},{21,20},{22,21},{... | collective-permute-start | bytes 3145736 | tf_op jit(solution)/shard_map/ppermute | solution.py:519
  56.8 26.6 %collective-permute-start.12 = (bf16[256,2048]{1,0:T(8,128)(2,1)}, bf16[256,2048]{1,0:T(8,128)(2,1)}, u32[]{:S(2)}, u32[]{:S(2)}) collective-permute-start(bf16[256,2048]{1,0:T(8,128)(2,1)} %collective-permute-done.11.refs_2_), channel_id=1, source_target_pairs={{0,28},{4,0},{8,4},{12,8},{16,12},{20,16},{24,20},{28,24},{1,29},{... | collective-permute-start | bytes 3145736 | tf_op jit(solution)/shard_map/ppermute | solution.py:469
  77.7 12.7 %collective-permute-start.14 = (bf16[2048,256]{1,0:T(8,128)(2,1)}, bf16[2048,256]{1,0:T(8,128)(2,1)}, u32[]{:S(2)}, u32[]{:S(2)}) collective-permute-start(bf16[2048,256]{1,0:T(8,128)(2,1)} %collective-permute-done.5.refs_5_.refs_2_), channel_id=1, source_target_pairs={{0,16},{23,3}} | collective-permute-start | bytes 3145736 | tf_op jit(solution)/shard_map/ppermute | solution.py:499
  79.4 9.2 %collective-permute-start.13 = (f32[2048]{0:T(1024)S(1)}, f32[2048]{0:T(1024)S(1)}, u32[]{:S(2)}, u32[]{:S(2)}) collective-permute-start(f32[2048]{0:T(1024)S(1)} %multiply_reduce_fusion), channel_id=1, source_target_pairs={{0,1},{1,0},{2,3},{3,2},{4,5},{5,4},{6,7},{7,6},{8,9},{9,8},{10,11... | collective-permute-start | bytes 24584 | tf_op jit(solution)/shard_map/ppermute | solution.py:490
  79.5 1.0 copy-start.5
  80.4 27.3 %collective-permute-start.8 = (bf16[2048,256]{1,0:T(8,128)(2,1)}, bf16[2048,256]{1,0:T(8,128)(2,1)}, u32[]{:S(2)}, u32[]{:S(2)}) collective-permute-start(bf16[2048,256]{1,0:T(8,128)(2,1)} %collective-permute-done.5.refs_5_.refs_2_), channel_id=1, source_target_pairs={{6,7},{9,8},{17,16},{22,23},{25,24},{30,31}} | collective-permute-start | bytes 3145736 | tf_op jit(solution)/shard_map/ppermute | solution.py:519
  81.7 26.0 %collective-permute-start.9 = (bf16[2048,256]{1,0:T(8,128)(2,1)}, bf16[2048,256]{1,0:T(8,128)(2,1)}, u32[]{:S(2)}, u32[]{:S(2)}) collective-permute-start(bf16[2048,256]{1,0:T(8,128)(2,1)} %collective-permute-done.6.refs_6_.refs_3_), channel_id=1, source_target_pairs={{2,3},{10,11},{13,12},{21,20},{26,27}} | collective-permute-start | bytes 3145736 | tf_op jit(solution)/shard_map/ppermute | solution.py:519
  83.9 1.2 %copy-start.7 = (bf16[256,2048]{1,0:T(8,128)(2,1)S(1)}, bf16[256,2048]{1,0:T(8,128)(2,1)}, u32[]{:S(2)}) copy-start(bf16[256,2048]{1,0:T(8,128)(2,1)} %refs_0_.1) | copy-start | bytes 3145732
  85.1 5.7 %copy-start.2 = (bf16[2048,256]{1,0:T(8,128)(2,1)S(1)}, bf16[2048,256]{1,0:T(8,128)(2,1)}, u32[]{:S(2)}) copy-start(bf16[2048,256]{1,0:T(8,128)(2,1)} %copy-done.1) | copy-start | bytes 3145732
  85.1 5.7 %copy-start.4 = (bf16[2048,256]{1,0:T(8,128)(2,1)S(1)}, bf16[2048,256]{1,0:T(8,128)(2,1)}, u32[]{:S(2)}) copy-start(bf16[2048,256]{1,0:T(8,128)(2,1)} %copy-done.3) | copy-start | bytes 3145732
  85.1 5.7 %copy-start.6 = (bf16[2048,256]{1,0:T(8,128)(2,1)S(1)}, bf16[2048,256]{1,0:T(8,128)(2,1)}, u32[]{:S(2)}) copy-start(bf16[2048,256]{1,0:T(8,128)(2,1)} %copy-done.5) | copy-start | bytes 3145732
  88.7 13.5 %collective-permute-start.15 = (f32[2048]{0:T(1024)S(1)}, f32[2048]{0:T(1024)S(1)}, u32[]{:S(2)}, u32[]{:S(2)}) collective-permute-start(f32[2048]{0:T(1024)S(1)} %add.39), channel_id=1, source_target_pairs={{0,2},{1,3},{2,0},{3,1},{4,6},{5,7},{6,4},{7,5},{8,10},{9,11},{10,... | collective-permute-start | bytes 24584 | tf_op jit(solution)/shard_map/ppermute | solution.py:490

commit v18 on v17

--- a/solution.py
+++ b/solution.py
@@ -54,6 +54,7 @@
     def __init__(self, rows, cols, groups_here, towards_zero):
         self.rows, self.cols = rows, cols
         self.towards_zero = towards_zero
+        self.short = groups_here > 1
         self.items = []
         for r in range(rows):
             mine = [
@@ -79,6 +80,7 @@
     def balance(self, r, other):
         if len(self.items[r]) < len(self.items[other]) or any(i.row == other for i in self.away):
             return
+        crowded = self.short and r % 2 == 0 and min(len(self.items[r]), len(self.items[r ^ 1])) >= STEPS
         places = sorted({i.place for i in self.items[r]})
         best = None
         for counts in itertools.product(range(3), repeat=len(places)):
@@ -92,6 +94,7 @@
             theirs = line_slots(self.items[other] + visitors)
             score = (
                 max(max(mine, default=0), max(theirs, default=0), STEPS),
+                max(len(mine), STEPS - 1) if crowded else 0,
                 len(gone),
                 max([slot for slot, i in theirs.items() if i.home is not None], default=0),
             )

time: 116 us -> 122 us (1.052)
  the two profiles are of different devices: /device:TPU:2 before, /device:TPU:6 now
where the time goes in v18:
time: 122 us; the launch traced here: 121 us
  starting transfers between devices  44.6 us (37%)
  waiting for transfers between devices  37 us (30%)
  Pallas kernels  25.6 us (21%)
  local copies, waits for them, and re-layouts  11.5 us (9%)
  other arithmetic  1.73 us (1%)
    ppermute x8, waiting for transfers between devices, local(): buffers[key] = lax.ppermute(held, both, pairs_of[key])  36 us
    ppermute x8, starting transfers between devices, local(): buffers[key] = lax.ppermute(held, both, pairs_of[key])  22.8 us
    pallas_call x1, Pallas kernels, early_product(): pl.pallas_call(functools.partial(early_kernel, at, candidates, len(buffer...  11.7 us
    ppermute x2, starting transfers between devices, bring_back(): lax.ppermute(buffers[key], both, returns[key])  10.7 us
    ppermute x2, starting transfers between devices, sum_beside(): other = lax.ppermute(squares, 'col', [(i, i ^ bit) for i in range(cols)])  9.34 us
    pallas_call x1, Pallas kernels, last_product(): pl.pallas_call(functools.partial(last_kernel, at, candidates, scale, len(...  7.4 us
    dynamic_slice x3, local copies, waits for them, and re-layouts, own_chunk(): lax.dynamic_slice(x, (piece * piece_rows, group * group_size), (piece_row...  5.72 us
    unnamed x24, local copies, waits for them, and re-layouts  4.19 us
  transfers between devices with their start and end apart: 16, of which 4 were waited for; matrix products, arithmetic and copies ran while one was open for 5% of the time, Pallas kernels for 15%

profile of v18, /device:TPU:6, one launch (start us, length us, event | category | flops | bytes accessed | tf_op | source)
XLA Modules:
  0.0 121.2 jit_solution(9059012429135799862)
XLA Ops:
  0.6 0.0 copy-start
  0.6 0.0 copy-start.11
  0.7 0.0 copy-start.10
  0.7 0.0 copy-start.8
  0.7 2.4 %constant_dynamic-slice_fusion.1 = bf16[2048,256]{1,0:T(8,128)(2,1)} fusion(bf16[2048,512]{1,0:T(8,128)(2,1)} %x.9, s32[]{:T(128)S(6)} %select_n.35), kind=kLoop, calls=%fused_computation.14 | loop fusion | bytes 2097156 | tf_op jit(solution)/shard_map/dynamic_slice | solution.py:448
  3.1 1.7 %collective-permute-start.1 = (bf16[2048,256]{1,0:T(8,128)(2,1)}, bf16[2048,256]{1,0:T(8,128)(2,1)}, u32[]{:S(2)}, u32[]{:S(2)}) collective-permute-start(bf16[2048,256]{1,0:T(8,128)(2,1)} %constant_dynamic-slice_fusion.1), channel_id=1, source_target_pairs={{1,0},{5,6},{6,7},{9,8},{10,9},{14,15},{18,17},{19,18},{22,23},{27... | collective-permute-start | bytes 3145736 | tf_op jit(solution)/shard_map/ppermute | solution.py:522
  4.7 2.3 %dynamic_slice.32 = bf16[2048,256]{1,0:T(8,128)(2,1)} slice(bf16[2048,512]{1,0:T(8,128)(2,1)} %x.9), slice={[0:2048], [256:512]} | slice | bytes 2097152 | tf_op jit(solution)/shard_map/dynamic_slice | solution.py:448
  7.0 1.7 %collective-permute-start = (bf16[2048,256]{1,0:T(8,128)(2,1)}, bf16[2048,256]{1,0:T(8,128)(2,1)}, u32[]{:S(2)}, u32[]{:S(2)}) collective-permute-start(bf16[2048,256]{1,0:T(8,128)(2,1)} %dynamic_slice.32), channel_id=1, source_target_pairs={{18,2},{9,25},{1,21}} | collective-permute-start | bytes 3145736 | tf_op jit(solution)/shard_map/ppermute | solution.py:526
  8.7 0.0 copy-done.11
  8.7 0.0 copy-done.10
  8.7 0.1 dynamic_slice.27
  8.8 0.1 dynamic_slice.28
  8.8 0.0 copy-done.8
  8.8 1.0 multiply_reduce_fusion
  9.9 1.1 constant_dynamic-slice_fusion
  11.0 3.2 %collective-permute-start.3 = (bf16[2048,256]{1,0:T(8,128)(2,1)}, bf16[2048,256]{1,0:T(8,128)(2,1)S(1)}, u32[]{:S(2)}, u32[]{:S(2)}) collective-permute-start(bf16[2048,256]{1,0:T(8,128)(2,1)} %constant_dynamic-slice_fusion), channel_id=1, source_target_pairs={{0,1},{1,2},{5,4},{10,11},{13,12},{14,13},{18,19},{22,21},{23,22},... | collective-permute-start | bytes 3145736 | tf_op jit(solution)/shard_map/ppermute | solution.py:522
  14.2 0.1 collective-permute-start.10
  14.2 0.7 fusion.2.table
  14.9 0.0 collective-permute-done.1.refs_1_.refs_0_
  14.9 0.0 collective-permute-done.refs_0_
  14.9 1.6 %relay.3 = bf16[2048,256]{1,0:T(8,128)(2,1)S(1)} custom-call(s32[21]{0:T(128)S(1)} %fusion.2.table, bf16[2048,512]{1,0:T(8,128)(2,1)S(1)} %copy-done, bf16[2048,256]{1,0:T(8,128)(2,1)} %collective-permute-done.refs_0_, bf16[2048,256]{1,0:T(8,128)(2,1)} %collective-permute-done.1.refs_1_.refs_0_), custom_call_target="tpu_custom_call" | custom-call | tf_op jit(solution)/shard_map/relay/pallas_call | solution.py:167
  16.6 0.0 copy-start.9
  16.6 1.3 %collective-permute-start.2 = (bf16[2048,256]{1,0:T(8,128)(2,1)S(1)}, bf16[2048,256]{1,0:T(8,128)(2,1)S(1)}, u32[]{:S(2)}, u32[]{:S(2)}) collective-permute-start(bf16[2048,256]{1,0:T(8,128)(2,1)S(1)} %relay.3), channel_id=1, source_target_pairs={{1,0},{2,1},{4,5},{5,6},{6,7},{9,8},{10,9},{13,14},{14,15},{17,16}... | collective-permute-start | bytes 3145736 | tf_op jit(solution)/shard_map/ppermute | solution.py:522
  17.9 13.7 %collective-permute-done.3.refs_0_.refs_1_ = bf16[2048,256]{1,0:T(8,128)(2,1)S(1)} collective-permute-done((bf16[2048,256]{1,0:T(8,128)(2,1)}, bf16[2048,256]{1,0:T(8,128)(2,1)S(1)}, u32[]{:S(2)}, u32[]{:S(2)}) %collective-permute-start.3) | collective-permute-done | bytes 1048608 | tf_op jit(solution)/shard_map/ppermute | solution.py:522
  31.6 0.6 relay.4
  32.2 1.0 copy-done.1
  33.2 10.8 %collective-permute-start.4 = (bf16[2048,256]{1,0:T(8,128)(2,1)S(1)}, bf16[2048,256]{1,0:T(8,128)(2,1)S(1)}, u32[]{:S(2)}, u32[]{:S(2)}) collective-permute-start(bf16[2048,256]{1,0:T(8,128)(2,1)S(1)} %relay.4), channel_id=1, source_target_pairs={{0,1},{1,2},{2,3},{5,4},{6,5},{9,10},{10,11},{13,12},{14,13},{15,1... | collective-permute-start | bytes 3145736 | tf_op jit(solution)/shard_map/ppermute | solution.py:522
  44.0 0.0 collective-permute-done.10.refs_1_
  44.0 0.1 collective-permute-start.11
  44.1 9.1 %collective-permute-done.2.refs_2_.refs_0_ = bf16[2048,256]{1,0:T(8,128)(2,1)S(1)} collective-permute-done((bf16[2048,256]{1,0:T(8,128)(2,1)S(1)}, bf16[2048,256]{1,0:T(8,128)(2,1)S(1)}, u32[]{:S(2)}, u32[]{:S(2)}) %collective-permute-start.2) | collective-permute-done | bytes 1048608 | tf_op jit(solution)/shard_map/ppermute | solution.py:522
  53.2 1.3 %collective-permute-start.5 = (bf16[2048,256]{1,0:T(8,128)(2,1)S(1)}, bf16[2048,256]{1,0:T(8,128)(2,1)}, u32[]{:S(2)}, u32[]{:S(2)}) collective-permute-start(bf16[2048,256]{1,0:T(8,128)(2,1)S(1)} %collective-permute-done.2.refs_2_.refs_0_), channel_id=1, source_target_pairs={{1,0},{5,6},{6,7},{9,8},{14,15},{17,16},{18,17},{21,22},{22,23},{2... | collective-permute-start | bytes 3145736 | tf_op jit(solution)/shard_map/ppermute | solution.py:522
  54.4 8.9 %collective-permute-start.7 = (bf16[2048,256]{1,0:T(8,128)(2,1)S(1)}, bf16[2048,256]{1,0:T(8,128)(2,1)S(1)}, u32[]{:S(2)}, u32[]{:S(2)}) collective-permute-start(bf16[2048,256]{1,0:T(8,128)(2,1)S(1)} %collective-permute-done.2.refs_2_.refs_0_), channel_id=1, source_target_pairs={{1,17},{24,8},{22,2}} | collective-permute-start | bytes 3145736 | tf_op jit(solution)/shard_map/ppermute | solution.py:502
  63.4 0.0 copy-start.3
  63.4 1.0 copy-done.3
  64.3 0.0 collective-permute-done.4.refs_0_.refs_3_.refs_1_
  64.3 0.6 relay.5
  65.0 1.7 %collective-permute-start.6 = (bf16[2048,256]{1,0:T(8,128)(2,1)S(1)}, bf16[2048,256]{1,0:T(8,128)(2,1)}, u32[]{:S(2)}, u32[]{:S(2)}) collective-permute-start(bf16[2048,256]{1,0:T(8,128)(2,1)S(1)} %relay.5), channel_id=1, source_target_pairs={{1,2},{2,3},{5,4},{9,10},{10,11},{13,12},{14,13},{21,20},{22,21},{... | collective-permute-start | bytes 3145736 | tf_op jit(solution)/shard_map/ppermute | solution.py:522
  66.6 0.0 collective-permute-done.11.refs_2_
  66.6 0.0 collective-permute-start.12
  66.6 13.2 %collective-permute-done.5.refs_5_.refs_2_ = bf16[2048,256]{1,0:T(8,128)(2,1)} collective-permute-done((bf16[2048,256]{1,0:T(8,128)(2,1)S(1)}, bf16[2048,256]{1,0:T(8,128)(2,1)}, u32[]{:S(2)}, u32[]{:S(2)}) %collective-permute-start.5) | collective-permute-done | bytes 1048608 | tf_op jit(solution)/shard_map/ppermute | solution.py:522
  79.8 1.7 %collective-permute-start.14 = (bf16[2048,256]{1,0:T(8,128)(2,1)}, bf16[2048,256]{1,0:T(8,128)(2,1)}, u32[]{:S(2)}, u32[]{:S(2)}) collective-permute-start(bf16[2048,256]{1,0:T(8,128)(2,1)} %collective-permute-done.5.refs_5_.refs_2_), channel_id=1, source_target_pairs={{0,16},{23,3}} | collective-permute-start | bytes 3145736 | tf_op jit(solution)/shard_map/ppermute | solution.py:502
  81.6 0.0 collective-permute-start.13
  81.6 1.0 collective-permute-done.7.refs_4_
  82.6 1.0 copy-done.5
  83.6 1.3 %collective-permute-start.8 = (bf16[2048,256]{1,0:T(8,128)(2,1)}, bf16[2048,256]{1,0:T(8,128)(2,1)}, u32[]{:S(2)}, u32[]{:S(2)}) collective-permute-start(bf16[2048,256]{1,0:T(8,128)(2,1)} %collective-permute-done.5.refs_5_.refs_2_), channel_id=1, source_target_pairs={{6,7},{17,16},{22,23},{25,24},{30,31}} | collective-permute-start | bytes 3145736 | tf_op jit(solution)/shard_map/ppermute | solution.py:522
  84.8 0.0 collective-permute-done.6.refs_6_.refs_3_
  84.9 1.6 %collective-permute-start.9 = (bf16[2048,256]{1,0:T(8,128)(2,1)}, bf16[2048,256]{1,0:T(8,128)(2,1)}, u32[]{:S(2)}, u32[]{:S(2)}) collective-permute-start(bf16[2048,256]{1,0:T(8,128)(2,1)} %collective-permute-done.6.refs_6_.refs_3_), channel_id=1, source_target_pairs={{2,3},{10,11},{13,12},{21,20},{26,27}} | collective-permute-start | bytes 3145736 | tf_op jit(solution)/shard_map/ppermute | solution.py:522
  86.5 0.1 fusion
  86.6 0.0 collective-permute-done.12.refs_3_
  86.6 0.2 broadcast_in_dim.42.refs_4_
  86.8 0.2 broadcast_in_dim.43.refs_5_
  87.0 0.0 copy-start.7
  87.0 1.2 %copy-done.7 = bf16[256,2048]{1,0:T(8,128)(2,1)S(1)} copy-done((bf16[256,2048]{1,0:T(8,128)(2,1)S(1)}, bf16[256,2048]{1,0:T(8,128)(2,1)}, u32[]{:S(2)}) %copy-start.7) | copy-done | bytes 1048600
  88.2 3.5 %window.1.refs_11_.refs_9_ = bf16[1024,2048]{1,0:T(8,128)(2,1)S(1)} custom-call(s32[21]{0:T(128)S(1)} %fusion.2.table, bf16[256,2048]{1,0:T(8,128)(2,1)S(1)} %copy-done.7, bf16[256,2048]{1,0:T(8,128)(2,1)} %collective-permute-done.10.refs_1_, bf16[256,2048]{1,0:T(8,128)(2,1)} %collective-permute-done.11.refs_2_, ...), custom_call_target="tpu_custom_call" | custom-call | flops 8388608 | bytes 8388608 | tf_op jit(solution)/shard_map/window/pallas_call | solution.py:205
  91.8 0.0 collective-permute-done.13
  91.8 9.3 %collective-permute-start.15 = (f32[2048]{0:T(1024)S(1)}, f32[2048]{0:T(1024)S(1)}, u32[]{:S(2)}, u32[]{:S(2)}) collective-permute-start(f32[2048]{0:T(1024)S(1)} %add.39), channel_id=1, source_target_pairs={{0,2},{1,3},{2,0},{3,1},{4,6},{5,7},{6,4},{7,5},{8,10},{9,11},{10,... | collective-permute-start | bytes 24584 | tf_op jit(solution)/shard_map/ppermute | solution.py:493
  101.1 0.0 collective-permute-done.14.refs_7_
  101.1 0.3 broadcast_in_dim.41.refs_10_.refs_8_
  101.5 11.7 %early.1.refs_10_ = f32[2048,2048]{1,0:T(8,128)S(1)} custom-call(s32[21]{0:T(128)S(1)} %fusion.2.table, bf16[2048,512]{1,0:T(8,128)(2,1)S(1)} %copy-done, bf16[2048,256]{1,0:T(8,128)(2,1)} %collective-permute-done.1.refs_1_.refs_0_, bf16[2048,256]{1,0:T(8,128)(2,1)S(1)} %copy-done.2, bf16[2048,256]{1,0:T(8,128)(2,1)S(1)} %copy-done.4, ...), custom_call_target="tpu_custom_call" | custom-call | flops 6442450944 | tf_op jit(solution)/shard_map/early/pallas_call | solution.py:266
  113.2 0.0 collective-permute-done.15
  113.2 0.6 multiply_add_fusion
  113.8 0.0 collective-permute-done.8.refs_4_
  113.8 0.0 collective-permute-done.9.refs_5_
  113.9 7.4 %last.1 = bf16[2048,2048]{1,0:T(8,128)(2,1)} custom-call(s32[21]{0:T(128)S(1)} %fusion.2.table, bf16[2048,512]{1,0:T(8,128)(2,1)S(1)} %copy-done, bf16[2048,256]{1,0:T(8,128)(2,1)S(1)} %copy-done.4, bf16[2048,256]{1,0:T(8,128)(2,1)S(1)} %collective-permute-done.4.refs_0_.refs_3_.refs_1_, bf16[2048,256]{1,0:T(8,128)(2,1)} %collective-permute-done.5.refs_5_.refs_2_, ...), custom_call_target="tpu_custom_call" | custom-call | flops 2147483648 | bytes 8388608 | tf_op jit(solution)/shard_map/last/pallas_call | solution.py:310
  (14 shorter events, 0.0 us)
Async XLA Ops:
  0.6 8.2 %copy-start = (bf16[2048,512]{1,0:T(8,128)(2,1)S(1)}, bf16[2048,512]{1,0:T(8,128)(2,1)}, u32[]{:S(2)}) copy-start(bf16[2048,512]{1,0:T(8,128)(2,1)} %x.9) | copy-start | bytes 6291460
  0.6 8.0 %copy-start.11 = (f32[2048]{0:T(1024)S(1)}, f32[2048]{0:T(1024)}, u32[]{:S(2)}) copy-start(f32[2048]{0:T(1024)} %param.10) | copy-start | bytes 24580
  0.7 8.0 %copy-start.10 = (f32[2048]{0:T(1024)S(1)}, f32[2048]{0:T(1024)}, u32[]{:S(2)}) copy-start(f32[2048]{0:T(1024)} %param.9) | copy-start | bytes 24580
  0.7 8.2 %copy-start.8 = (s32[2048]{0:T(1024)S(1)}, s32[2048]{0:T(1024)}, u32[]{:S(2)}) copy-start(s32[2048]{0:T(1024)} %param.11) | copy-start | bytes 24580
  3.1 11.9 %collective-permute-start.1 = (bf16[2048,256]{1,0:T(8,128)(2,1)}, bf16[2048,256]{1,0:T(8,128)(2,1)}, u32[]{:S(2)}, u32[]{:S(2)}) collective-permute-start(bf16[2048,256]{1,0:T(8,128)(2,1)} %constant_dynamic-slice_fusion.1), channel_id=1, source_target_pairs={{1,0},{5,6},{6,7},{9,8},{10,9},{14,15},{18,17},{19,18},{22,23},{27... | collective-permute-start | bytes 3145736 | tf_op jit(solution)/shard_map/ppermute | solution.py:522
  7.0 7.9 %collective-permute-start = (bf16[2048,256]{1,0:T(8,128)(2,1)}, bf16[2048,256]{1,0:T(8,128)(2,1)}, u32[]{:S(2)}, u32[]{:S(2)}) collective-permute-start(bf16[2048,256]{1,0:T(8,128)(2,1)} %dynamic_slice.32), channel_id=1, source_target_pairs={{18,2},{9,25},{1,21}} | collective-permute-start | bytes 3145736 | tf_op jit(solution)/shard_map/ppermute | solution.py:526
  11.0 20.6 %collective-permute-start.3 = (bf16[2048,256]{1,0:T(8,128)(2,1)}, bf16[2048,256]{1,0:T(8,128)(2,1)S(1)}, u32[]{:S(2)}, u32[]{:S(2)}) collective-permute-start(bf16[2048,256]{1,0:T(8,128)(2,1)} %constant_dynamic-slice_fusion), channel_id=1, source_target_pairs={{0,1},{1,2},{5,4},{10,11},{13,12},{14,13},{18,19},{22,21},{23,22},... | collective-permute-start | bytes 3145736 | tf_op jit(solution)/shard_map/ppermute | solution.py:522
  14.2 29.9 %collective-permute-start.10 = (bf16[256,2048]{1,0:T(8,128)(2,1)}, bf16[256,2048]{1,0:T(8,128)(2,1)}, u32[]{:S(2)}, u32[]{:S(2)}) collective-permute-start(bf16[256,2048]{1,0:T(8,128)(2,1)} %refs_0_.1), channel_id=1, source_target_pairs={{0,28},{4,0},{8,4},{12,8},{16,12},{20,16},{24,20},{28,24},{1,29},{... | collective-permute-start | bytes 3145736 | tf_op jit(solution)/shard_map/ppermute | solution.py:472
  16.6 69.9 %copy-start.9 = (s32[2048]{0:T(1024)S(1)}, s32[2048]{0:T(1024)}, u32[]{:S(2)}) copy-start(s32[2048]{0:T(1024)} %param.12) | copy-start | bytes 24580
  16.6 36.6 %collective-permute-start.2 = (bf16[2048,256]{1,0:T(8,128)(2,1)S(1)}, bf16[2048,256]{1,0:T(8,128)(2,1)S(1)}, u32[]{:S(2)}, u32[]{:S(2)}) collective-permute-start(bf16[2048,256]{1,0:T(8,128)(2,1)S(1)} %relay.3), channel_id=1, source_target_pairs={{1,0},{2,1},{4,5},{5,6},{6,7},{9,8},{10,9},{13,14},{14,15},{17,16}... | collective-permute-start | bytes 3145736 | tf_op jit(solution)/shard_map/ppermute | solution.py:522
  32.2 1.0 copy-start.1
  33.2 31.1 %collective-permute-start.4 = (bf16[2048,256]{1,0:T(8,128)(2,1)S(1)}, bf16[2048,256]{1,0:T(8,128)(2,1)S(1)}, u32[]{:S(2)}, u32[]{:S(2)}) collective-permute-start(bf16[2048,256]{1,0:T(8,128)(2,1)S(1)} %relay.4), channel_id=1, source_target_pairs={{0,1},{1,2},{2,3},{5,4},{6,5},{9,10},{10,11},{13,12},{14,13},{15,1... | collective-permute-start | bytes 3145736 | tf_op jit(solution)/shard_map/ppermute | solution.py:522
  44.0 22.6 %collective-permute-start.11 = (bf16[256,2048]{1,0:T(8,128)(2,1)}, bf16[256,2048]{1,0:T(8,128)(2,1)}, u32[]{:S(2)}, u32[]{:S(2)}) collective-permute-start(bf16[256,2048]{1,0:T(8,128)(2,1)} %collective-permute-done.10.refs_1_), channel_id=1, source_target_pairs={{0,28},{4,0},{8,4},{12,8},{16,12},{20,16},{24,20},{28,24},{1,29},{... | collective-permute-start | bytes 3145736 | tf_op jit(solution)/shard_map/ppermute | solution.py:472
  53.2 26.7 %collective-permute-start.5 = (bf16[2048,256]{1,0:T(8,128)(2,1)S(1)}, bf16[2048,256]{1,0:T(8,128)(2,1)}, u32[]{:S(2)}, u32[]{:S(2)}) collective-permute-start(bf16[2048,256]{1,0:T(8,128)(2,1)S(1)} %collective-permute-done.2.refs_2_.refs_0_), channel_id=1, source_target_pairs={{1,0},{5,6},{6,7},{9,8},{14,15},{17,16},{18,17},{21,22},{22,23},{2... | collective-permute-start | bytes 3145736 | tf_op jit(solution)/shard_map/ppermute | solution.py:522
  54.4 28.1 %collective-permute-start.7 = (bf16[2048,256]{1,0:T(8,128)(2,1)S(1)}, bf16[2048,256]{1,0:T(8,128)(2,1)S(1)}, u32[]{:S(2)}, u32[]{:S(2)}) collective-permute-start(bf16[2048,256]{1,0:T(8,128)(2,1)S(1)} %collective-permute-done.2.refs_2_.refs_0_), channel_id=1, source_target_pairs={{1,17},{24,8},{22,2}} | collective-permute-start | bytes 3145736 | tf_op jit(solution)/shard_map/ppermute | solution.py:502
  63.4 1.0 copy-start.3
  65.0 19.9 %collective-permute-start.6 = (bf16[2048,256]{1,0:T(8,128)(2,1)S(1)}, bf16[2048,256]{1,0:T(8,128)(2,1)}, u32[]{:S(2)}, u32[]{:S(2)}) collective-permute-start(bf16[2048,256]{1,0:T(8,128)(2,1)S(1)} %relay.5), channel_id=1, source_target_pairs={{1,2},{2,3},{5,4},{9,10},{10,11},{13,12},{14,13},{21,20},{22,21},{... | collective-permute-start | bytes 3145736 | tf_op jit(solution)/shard_map/ppermute | solution.py:522
  66.6 19.9 %collective-permute-start.12 = (bf16[256,2048]{1,0:T(8,128)(2,1)}, bf16[256,2048]{1,0:T(8,128)(2,1)}, u32[]{:S(2)}, u32[]{:S(2)}) collective-permute-start(bf16[256,2048]{1,0:T(8,128)(2,1)} %collective-permute-done.11.refs_2_), channel_id=1, source_target_pairs={{0,28},{4,0},{8,4},{12,8},{16,12},{20,16},{24,20},{28,24},{1,29},{... | collective-permute-start | bytes 3145736 | tf_op jit(solution)/shard_map/ppermute | solution.py:472
  79.8 21.3 %collective-permute-start.14 = (bf16[2048,256]{1,0:T(8,128)(2,1)}, bf16[2048,256]{1,0:T(8,128)(2,1)}, u32[]{:S(2)}, u32[]{:S(2)}) collective-permute-start(bf16[2048,256]{1,0:T(8,128)(2,1)} %collective-permute-done.5.refs_5_.refs_2_), channel_id=1, source_target_pairs={{0,16},{23,3}} | collective-permute-start | bytes 3145736 | tf_op jit(solution)/shard_map/ppermute | solution.py:502
  81.6 10.2 %collective-permute-start.13 = (f32[2048]{0:T(1024)S(1)}, f32[2048]{0:T(1024)S(1)}, u32[]{:S(2)}, u32[]{:S(2)}) collective-permute-start(f32[2048]{0:T(1024)S(1)} %multiply_reduce_fusion), channel_id=1, source_target_pairs={{0,1},{1,0},{2,3},{3,2},{4,5},{5,4},{6,7},{7,6},{8,9},{9,8},{10,11... | collective-permute-start | bytes 24584 | tf_op jit(solution)/shard_map/ppermute | solution.py:493
  82.6 1.0 copy-start.5
  83.6 30.3 %collective-permute-start.8 = (bf16[2048,256]{1,0:T(8,128)(2,1)}, bf16[2048,256]{1,0:T(8,128)(2,1)}, u32[]{:S(2)}, u32[]{:S(2)}) collective-permute-start(bf16[2048,256]{1,0:T(8,128)(2,1)} %collective-permute-done.5.refs_5_.refs_2_), channel_id=1, source_target_pairs={{6,7},{17,16},{22,23},{25,24},{30,31}} | collective-permute-start | bytes 3145736 | tf_op jit(solution)/shard_map/ppermute | solution.py:522
  84.9 29.0 %collective-permute-start.9 = (bf16[2048,256]{1,0:T(8,128)(2,1)}, bf16[2048,256]{1,0:T(8,128)(2,1)}, u32[]{:S(2)}, u32[]{:S(2)}) collective-permute-start(bf16[2048,256]{1,0:T(8,128)(2,1)} %collective-permute-done.6.refs_6_.refs_3_), channel_id=1, source_target_pairs={{2,3},{10,11},{13,12},{21,20},{26,27}} | collective-permute-start | bytes 3145736 | tf_op jit(solution)/shard_map/ppermute | solution.py:522
  87.0 1.2 %copy-start.7 = (bf16[256,2048]{1,0:T(8,128)(2,1)S(1)}, bf16[256,2048]{1,0:T(8,128)(2,1)}, u32[]{:S(2)}) copy-start(bf16[256,2048]{1,0:T(8,128)(2,1)} %refs_0_.1) | copy-start | bytes 3145732
  88.2 13.2 %copy-start.2 = (bf16[2048,256]{1,0:T(8,128)(2,1)S(1)}, bf16[2048,256]{1,0:T(8,128)(2,1)}, u32[]{:S(2)}) copy-start(bf16[2048,256]{1,0:T(8,128)(2,1)} %copy-done.1) | copy-start | bytes 3145732
  88.2 13.3 %copy-start.4 = (bf16[2048,256]{1,0:T(8,128)(2,1)S(1)}, bf16[2048,256]{1,0:T(8,128)(2,1)}, u32[]{:S(2)}) copy-start(bf16[2048,256]{1,0:T(8,128)(2,1)} %copy-done.3) | copy-start | bytes 3145732
  88.2 13.3 %copy-start.6 = (bf16[2048,256]{1,0:T(8,128)(2,1)S(1)}, bf16[2048,256]{1,0:T(8,128)(2,1)}, u32[]{:S(2)}) copy-start(bf16[2048,256]{1,0:T(8,128)(2,1)} %copy-done.5) | copy-start | bytes 3145732
  91.8 21.4 %collective-permute-start.15 = (f32[2048]{0:T(1024)S(1)}, f32[2048]{0:T(1024)S(1)}, u32[]{:S(2)}, u32[]{:S(2)}) collective-permute-start(f32[2048]{0:T(1024)S(1)} %add.39), channel_id=1, source_target_pairs={{0,2},{1,3},{2,0},{3,1},{4,6},{5,7},{6,4},{7,5},{8,10},{9,11},{10,... | collective-permute-start | bytes 24584 | tf_op jit(solution)/shard_map/ppermute | solution.py:493

commit v19 on v18

--- a/solution.py
+++ b/solution.py
@@ -467,9 +467,6 @@
         return jnp.sum(jnp.square(zx.astype(jnp.float32)), axis=1)
 
     back = [(i, (i - 1) % rows) for i in range(rows)]
-    window = [y]
-    while len(window) < STEPS:
-        window.append(lax.ppermute(window[-1], "row", back))
     squares = own_squares()
 
     starts = {}
@@ -494,7 +491,17 @@
         value, other = lax.optimization_barrier((value, other))
         return value, squares + other
 
-    buffers, crossed = {}, {}
+    crossed = {}
+    for k, crossing in enumerate(crossings):
+        pairs = [(number(*rc), number(*to)) for rc, (to, _) in crossing.items()]
+        crossed[k] = lax.ppermute(starts["cross", k], both, pairs)
+    window = [y]
+    if crossed:
+        window[0], crossed[0] = lax.optimization_barrier((y, crossed[0]))
+    while len(window) < STEPS:
+        window.append(lax.ppermute(window[-1], "row", back))
+
+    buffers = {}
 
     def bring_back(key):
         if key in returns:
@@ -520,10 +527,6 @@
             if name in buffers:
                 held, buffers[name] = lax.optimization_barrier((held, buffers[name]))
             buffers[key] = lax.ppermute(held, both, pairs_of[key])
-        if key == (0, 1):
-            for k, crossing in enumerate(crossings):
-                pairs = [(number(*rc), number(*to)) for rc, (to, _) in crossing.items()]
-                crossed[k] = lax.ppermute(starts["cross", k], both, pairs)
         bring_back(key)
     zy = standardized_window(rank_at, table, window, wide(window_factor), wide(window_twice), male_cols[None, :])
     zy, squares = sum_beside(zy, squares)

time: 122 us -> 111 us (0.910)
  the two profiles are of different devices: /device:TPU:6 before, /device:TPU:0 now
where the time goes in v19:
time: 111 us; the launch traced here: 110 us
  waiting for transfers between devices  36 us (32%)
  starting transfers between devices  32.5 us (29%)
  Pallas kernels  25.2 us (23%)
  local copies, waits for them, and re-layouts  13.7 us (12%)
  other arithmetic  1.73 us (2%)
    ppermute x8, waiting for transfers between devices, local(): buffers[key] = lax.ppermute(held, both, pairs_of[key])  35.9 us
    ppermute x8, starting transfers between devices, local(): buffers[key] = lax.ppermute(held, both, pairs_of[key])  20.7 us
    pallas_call x1, Pallas kernels, early_product(): pl.pallas_call(functools.partial(early_kernel, at, candidates, len(buffer...  11.7 us
    pallas_call x1, Pallas kernels, last_product(): pl.pallas_call(functools.partial(last_kernel, at, candidates, scale, len(...  7.4 us
    unnamed x28, local copies, waits for them, and re-layouts  6.41 us
    ppermute x2, starting transfers between devices, sum_beside(): other = lax.ppermute(squares, 'col', [(i, i ^ bit) for i in range(cols)])  6.29 us
    dynamic_slice x3, local copies, waits for them, and re-layouts, own_chunk(): lax.dynamic_slice(x, (piece * piece_rows, group * group_size), (piece_row...  5.69 us
    pallas_call x1, Pallas kernels, standardized_window(): pl.pallas_call(functools.partial(window_kernel, at), out_shape=pltpu.VMEM...  3.23 us
  transfers between devices with their start and end apart: 16, of which 5 were waited for; matrix products, arithmetic and copies ran while one was open for 6% of the time, Pallas kernels for 16%

profile of v19, /device:TPU:0, one launch (start us, length us, event | category | flops | bytes accessed | tf_op | source)
XLA Modules:
  0.0 110.1 jit_solution(16088585615425807489)
XLA Ops:
  0.6 0.0 copy-start
  0.6 0.0 copy-start.13
  0.7 0.0 copy-start.12
  0.7 2.4 %constant_dynamic-slice_fusion.1 = bf16[2048,256]{1,0:T(8,128)(2,1)} fusion(bf16[2048,512]{1,0:T(8,128)(2,1)} %x.9, s32[]{:T(128)S(6)} %select_n.35), kind=kLoop, calls=%fused_computation.14 | loop fusion | bytes 2097156 | tf_op jit(solution)/shard_map/dynamic_slice | solution.py:448
  3.1 1.3 %collective-permute-start.1 = (bf16[2048,256]{1,0:T(8,128)(2,1)}, bf16[2048,256]{1,0:T(8,128)(2,1)}, u32[]{:S(2)}, u32[]{:S(2)}) collective-permute-start(bf16[2048,256]{1,0:T(8,128)(2,1)} %constant_dynamic-slice_fusion.1), channel_id=1, source_target_pairs={{1,0},{5,6},{6,7},{9,8},{10,9},{14,15},{18,17},{19,18},{22,23},{27... | collective-permute-start | bytes 3145736 | tf_op jit(solution)/shard_map/ppermute | solution.py:529
  4.4 2.3 %dynamic_slice.32 = bf16[2048,256]{1,0:T(8,128)(2,1)} slice(bf16[2048,512]{1,0:T(8,128)(2,1)} %x.9), slice={[0:2048], [256:512]} | slice | bytes 2097152 | tf_op jit(solution)/shard_map/dynamic_slice | solution.py:448
  6.6 1.6 %collective-permute-start = (bf16[2048,256]{1,0:T(8,128)(2,1)}, bf16[2048,256]{1,0:T(8,128)(2,1)}, u32[]{:S(2)}, u32[]{:S(2)}) collective-permute-start(bf16[2048,256]{1,0:T(8,128)(2,1)} %dynamic_slice.32), channel_id=1, source_target_pairs={{18,2},{9,25},{1,21}} | collective-permute-start | bytes 3145736 | tf_op jit(solution)/shard_map/ppermute | solution.py:497
  8.3 0.0 copy-done.13
  8.3 0.1 dynamic_slice.27
  8.4 0.1 dynamic_slice.28
  8.5 0.0 copy-done
  8.5 1.0 multiply_reduce_fusion
  9.5 1.0 constant_dynamic-slice_fusion
  10.5 7.5 %collective-permute-start.3 = (bf16[2048,256]{1,0:T(8,128)(2,1)}, bf16[2048,256]{1,0:T(8,128)(2,1)S(1)}, u32[]{:S(2)}, u32[]{:S(2)}) collective-permute-start(bf16[2048,256]{1,0:T(8,128)(2,1)} %constant_dynamic-slice_fusion), channel_id=1, source_target_pairs={{0,1},{1,2},{5,4},{10,11},{13,12},{14,13},{18,19},{22,21},{23,22},... | collective-permute-start | bytes 3145736 | tf_op jit(solution)/shard_map/ppermute | solution.py:529
  18.1 0.0 collective-permute-done.refs_0_
  18.1 0.1 collective-permute-start.10
  18.2 0.7 fusion.2.table
  18.9 3.3 %collective-permute-done.1.refs_1_.refs_0_ = bf16[2048,256]{1,0:T(8,128)(2,1)} collective-permute-done((bf16[2048,256]{1,0:T(8,128)(2,1)}, bf16[2048,256]{1,0:T(8,128)(2,1)}, u32[]{:S(2)}, u32[]{:S(2)}) %collective-permute-start.1) | collective-permute-done | bytes 1048608 | tf_op jit(solution)/shard_map/ppermute | solution.py:529
  22.1 1.6 %relay.3 = bf16[2048,256]{1,0:T(8,128)(2,1)S(1)} custom-call(s32[21]{0:T(128)S(1)} %fusion.2.table, bf16[2048,512]{1,0:T(8,128)(2,1)S(1)} %copy-done, bf16[2048,256]{1,0:T(8,128)(2,1)} %collective-permute-done.refs_0_, bf16[2048,256]{1,0:T(8,128)(2,1)} %collective-permute-done.1.refs_1_.refs_0_), custom_call_target="tpu_custom_call" | custom-call | tf_op jit(solution)/shard_map/relay/pallas_call | solution.py:167
  23.8 0.0 copy-start.11
  23.8 1.3 %collective-permute-start.2 = (bf16[2048,256]{1,0:T(8,128)(2,1)S(1)}, bf16[2048,256]{1,0:T(8,128)(2,1)S(1)}, u32[]{:S(2)}, u32[]{:S(2)}) collective-permute-start(bf16[2048,256]{1,0:T(8,128)(2,1)S(1)} %relay.3), channel_id=1, source_target_pairs={{1,0},{2,1},{4,5},{5,6},{6,7},{9,8},{10,9},{13,14},{14,15},{17,16}... | collective-permute-start | bytes 3145736 | tf_op jit(solution)/shard_map/ppermute | solution.py:529
  25.1 5.6 %collective-permute-done.3.refs_0_.refs_1_ = bf16[2048,256]{1,0:T(8,128)(2,1)S(1)} collective-permute-done((bf16[2048,256]{1,0:T(8,128)(2,1)}, bf16[2048,256]{1,0:T(8,128)(2,1)S(1)}, u32[]{:S(2)}, u32[]{:S(2)}) %collective-permute-start.3) | collective-permute-done | bytes 1048608 | tf_op jit(solution)/shard_map/ppermute | solution.py:529
  30.7 0.6 relay.4
  31.4 0.9 copy-done.1
  32.3 4.3 %collective-permute-start.4 = (bf16[2048,256]{1,0:T(8,128)(2,1)S(1)}, bf16[2048,256]{1,0:T(8,128)(2,1)S(1)}, u32[]{:S(2)}, u32[]{:S(2)}) collective-permute-start(bf16[2048,256]{1,0:T(8,128)(2,1)S(1)} %relay.4), channel_id=1, source_target_pairs={{0,1},{1,2},{2,3},{5,4},{6,5},{9,10},{10,11},{13,12},{14,13},{15,1... | collective-permute-start | bytes 3145736 | tf_op jit(solution)/shard_map/ppermute | solution.py:529
  36.7 0.0 collective-permute-done.10.refs_1_
  36.7 0.1 collective-permute-start.11
  36.7 1.0 copy-done.8
  37.8 9.8 %collective-permute-done.2.refs_2_.refs_0_ = bf16[2048,256]{1,0:T(8,128)(2,1)S(1)} collective-permute-done((bf16[2048,256]{1,0:T(8,128)(2,1)S(1)}, bf16[2048,256]{1,0:T(8,128)(2,1)S(1)}, u32[]{:S(2)}, u32[]{:S(2)}) %collective-permute-start.2) | collective-permute-done | bytes 1048608 | tf_op jit(solution)/shard_map/ppermute | solution.py:529
  47.6 1.3 %collective-permute-start.5 = (bf16[2048,256]{1,0:T(8,128)(2,1)S(1)}, bf16[2048,256]{1,0:T(8,128)(2,1)}, u32[]{:S(2)}, u32[]{:S(2)}) collective-permute-start(bf16[2048,256]{1,0:T(8,128)(2,1)S(1)} %collective-permute-done.2.refs_2_.refs_0_), channel_id=1, source_target_pairs={{1,0},{5,6},{6,7},{9,8},{14,15},{17,16},{18,17},{21,22},{22,23},{2... | collective-permute-start | bytes 3145736 | tf_op jit(solution)/shard_map/ppermute | solution.py:529
  48.9 0.7 collective-permute-start.7
  49.6 0.0 copy-start.3
  49.6 1.0 copy-done.3
  50.6 2.4 %collective-permute-done.4.refs_0_.refs_3_.refs_1_ = bf16[2048,256]{1,0:T(8,128)(2,1)S(1)} collective-permute-done((bf16[2048,256]{1,0:T(8,128)(2,1)S(1)}, bf16[2048,256]{1,0:T(8,128)(2,1)S(1)}, u32[]{:S(2)}, u32[]{:S(2)}) %collective-permute-start.4) | collective-permute-done | bytes 1048608 | tf_op jit(solution)/shard_map/ppermute | solution.py:529
  53.0 0.6 relay.5
  53.6 1.7 %collective-permute-start.6 = (bf16[2048,256]{1,0:T(8,128)(2,1)S(1)}, bf16[2048,256]{1,0:T(8,128)(2,1)}, u32[]{:S(2)}, u32[]{:S(2)}) collective-permute-start(bf16[2048,256]{1,0:T(8,128)(2,1)S(1)} %relay.5), channel_id=1, source_target_pairs={{1,2},{2,3},{5,4},{9,10},{10,11},{13,12},{14,13},{21,20},{22,21},{... | collective-permute-start | bytes 3145736 | tf_op jit(solution)/shard_map/ppermute | solution.py:529
  55.3 0.0 collective-permute-done.11.refs_2_
  55.3 0.7 collective-permute-start.12
  56.0 14.8 %collective-permute-done.5.refs_5_.refs_2_ = bf16[2048,256]{1,0:T(8,128)(2,1)} collective-permute-done((bf16[2048,256]{1,0:T(8,128)(2,1)S(1)}, bf16[2048,256]{1,0:T(8,128)(2,1)}, u32[]{:S(2)}, u32[]{:S(2)}) %collective-permute-start.5) | collective-permute-done | bytes 1048608 | tf_op jit(solution)/shard_map/ppermute | solution.py:529
  70.8 2.4 %collective-permute-start.14 = (bf16[2048,256]{1,0:T(8,128)(2,1)}, bf16[2048,256]{1,0:T(8,128)(2,1)}, u32[]{:S(2)}, u32[]{:S(2)}) collective-permute-start(bf16[2048,256]{1,0:T(8,128)(2,1)} %collective-permute-done.5.refs_5_.refs_2_), channel_id=1, source_target_pairs={{0,16},{23,3}} | collective-permute-start | bytes 3145736 | tf_op jit(solution)/shard_map/ppermute | solution.py:509
  73.2 0.0 collective-permute-start.13
  73.2 0.0 collective-permute-done.7.refs_4_
  73.2 1.0 copy-done.5
  74.2 1.7 %collective-permute-start.8 = (bf16[2048,256]{1,0:T(8,128)(2,1)}, bf16[2048,256]{1,0:T(8,128)(2,1)}, u32[]{:S(2)}, u32[]{:S(2)}) collective-permute-start(bf16[2048,256]{1,0:T(8,128)(2,1)} %collective-permute-done.5.refs_5_.refs_2_), channel_id=1, source_target_pairs={{6,7},{17,16},{22,23},{25,24},{30,31}} | collective-permute-start | bytes 3145736 | tf_op jit(solution)/shard_map/ppermute | solution.py:529
  75.8 0.0 collective-permute-done.6.refs_6_.refs_3_
  75.8 1.6 %collective-permute-start.9 = (bf16[2048,256]{1,0:T(8,128)(2,1)}, bf16[2048,256]{1,0:T(8,128)(2,1)}, u32[]{:S(2)}, u32[]{:S(2)}) collective-permute-start(bf16[2048,256]{1,0:T(8,128)(2,1)} %collective-permute-done.6.refs_6_.refs_3_), channel_id=1, source_target_pairs={{2,3},{10,11},{13,12},{21,20},{26,27}} | collective-permute-start | bytes 3145736 | tf_op jit(solution)/shard_map/ppermute | solution.py:529
  77.5 0.1 fusion
  77.6 0.0 collective-permute-done.12.refs_3_
  77.6 0.2 broadcast_in_dim.42.refs_4_
  77.8 0.2 broadcast_in_dim.43.refs_5_
  78.0 0.0 copy-start.7
  78.0 1.2 %copy-done.7 = bf16[256,2048]{1,0:T(8,128)(2,1)S(1)} copy-done((bf16[256,2048]{1,0:T(8,128)(2,1)S(1)}, bf16[256,2048]{1,0:T(8,128)(2,1)}, u32[]{:S(2)}) %copy-start.7) | copy-done | bytes 1048600
  79.2 1.2 %copy-done.9 = bf16[256,2048]{1,0:T(8,128)(2,1)S(1)} copy-done((bf16[256,2048]{1,0:T(8,128)(2,1)S(1)}, bf16[256,2048]{1,0:T(8,128)(2,1)}, u32[]{:S(2)}) %copy-start.9) | copy-done | bytes 1048600
  80.4 3.2 %window.1.refs_11_.refs_9_ = bf16[1024,2048]{1,0:T(8,128)(2,1)S(1)} custom-call(s32[21]{0:T(128)S(1)} %fusion.2.table, bf16[256,2048]{1,0:T(8,128)(2,1)S(1)} %copy-done.7, bf16[256,2048]{1,0:T(8,128)(2,1)S(1)} %copy-done.9, bf16[256,2048]{1,0:T(8,128)(2,1)} %collective-permute-done.11.refs_2_, bf16[256,2048]{1,0:T(8,128)(2,1)} %collective-permute-done.12.refs_3_, ...), custom_call_target="tpu_custom_call" | custom-call | flops 8388608 | bytes 8388608 | tf_op jit(solution)/shard_map/window/pallas_call | solution.py:205
  83.7 0.0 collective-permute-done.13
  83.7 6.3 %collective-permute-start.15 = (f32[2048]{0:T(1024)S(1)}, f32[2048]{0:T(1024)S(1)}, u32[]{:S(2)}, u32[]{:S(2)}) collective-permute-start(f32[2048]{0:T(1024)S(1)} %add.39), channel_id=1, source_target_pairs={{0,2},{1,3},{2,0},{3,1},{4,6},{5,7},{6,4},{7,5},{8,10},{9,11},{10,... | collective-permute-start | bytes 24584 | tf_op jit(solution)/shard_map/ppermute | solution.py:490
  90.0 0.0 collective-permute-done.14.refs_7_
  90.0 0.3 broadcast_in_dim.41.refs_10_.refs_8_
  90.3 11.7 %early.1.refs_10_ = f32[2048,2048]{1,0:T(8,128)S(1)} custom-call(s32[21]{0:T(128)S(1)} %fusion.2.table, bf16[2048,512]{1,0:T(8,128)(2,1)S(1)} %copy-done, bf16[2048,256]{1,0:T(8,128)(2,1)} %collective-permute-done.1.refs_1_.refs_0_, bf16[2048,256]{1,0:T(8,128)(2,1)S(1)} %copy-done.2, bf16[2048,256]{1,0:T(8,128)(2,1)S(1)} %copy-done.4, ...), custom_call_target="tpu_custom_call" | custom-call | flops 6442450944 | tf_op jit(solution)/shard_map/early/pallas_call | solution.py:266
  102.1 0.0 collective-permute-done.15
  102.1 0.6 multiply_add_fusion
  102.7 0.0 collective-permute-done.8.refs_4_
  102.7 0.0 collective-permute-done.9.refs_5_
  102.7 7.4 %last.1 = bf16[2048,2048]{1,0:T(8,128)(2,1)} custom-call(s32[21]{0:T(128)S(1)} %fusion.2.table, bf16[2048,512]{1,0:T(8,128)(2,1)S(1)} %copy-done, bf16[2048,256]{1,0:T(8,128)(2,1)S(1)} %copy-done.4, bf16[2048,256]{1,0:T(8,128)(2,1)S(1)} %collective-permute-done.4.refs_0_.refs_3_.refs_1_, bf16[2048,256]{1,0:T(8,128)(2,1)} %collective-permute-done.5.refs_5_.refs_2_, ...), custom_call_target="tpu_custom_call" | custom-call | flops 2147483648 | bytes 8388608 | tf_op jit(solution)/shard_map/last/pallas_call | solution.py:310
  (18 shorter events, 0.0 us)
Async XLA Ops:
  0.6 7.8 %copy-start = (bf16[2048,512]{1,0:T(8,128)(2,1)S(1)}, bf16[2048,512]{1,0:T(8,128)(2,1)}, u32[]{:S(2)}) copy-start(bf16[2048,512]{1,0:T(8,128)(2,1)} %x.9) | copy-start | bytes 6291460
  0.6 7.6 %copy-start.13 = (f32[2048]{0:T(1024)S(1)}, f32[2048]{0:T(1024)}, u32[]{:S(2)}) copy-start(f32[2048]{0:T(1024)} %param.10) | copy-start | bytes 24580
  0.7 7.6 %copy-start.12 = (f32[2048]{0:T(1024)S(1)}, f32[2048]{0:T(1024)}, u32[]{:S(2)}) copy-start(f32[2048]{0:T(1024)} %param.9) | copy-start | bytes 24580
  0.7 7.8 %copy-start.10 = (s32[2048]{0:T(1024)S(1)}, s32[2048]{0:T(1024)}, u32[]{:S(2)}) copy-start(s32[2048]{0:T(1024)} %param.11) | copy-start | bytes 24580
  3.1 19.1 %collective-permute-start.1 = (bf16[2048,256]{1,0:T(8,128)(2,1)}, bf16[2048,256]{1,0:T(8,128)(2,1)}, u32[]{:S(2)}, u32[]{:S(2)}) collective-permute-start(bf16[2048,256]{1,0:T(8,128)(2,1)} %constant_dynamic-slice_fusion.1), channel_id=1, source_target_pairs={{1,0},{5,6},{6,7},{9,8},{10,9},{14,15},{18,17},{19,18},{22,23},{27... | collective-permute-start | bytes 3145736 | tf_op jit(solution)/shard_map/ppermute | solution.py:529
  6.6 11.5 %collective-permute-start = (bf16[2048,256]{1,0:T(8,128)(2,1)}, bf16[2048,256]{1,0:T(8,128)(2,1)}, u32[]{:S(2)}, u32[]{:S(2)}) collective-permute-start(bf16[2048,256]{1,0:T(8,128)(2,1)} %dynamic_slice.32), channel_id=1, source_target_pairs={{18,2},{9,25},{1,21}} | collective-permute-start | bytes 3145736 | tf_op jit(solution)/shard_map/ppermute | solution.py:497
  10.5 20.2 %collective-permute-start.3 = (bf16[2048,256]{1,0:T(8,128)(2,1)}, bf16[2048,256]{1,0:T(8,128)(2,1)S(1)}, u32[]{:S(2)}, u32[]{:S(2)}) collective-permute-start(bf16[2048,256]{1,0:T(8,128)(2,1)} %constant_dynamic-slice_fusion), channel_id=1, source_target_pairs={{0,1},{1,2},{5,4},{10,11},{13,12},{14,13},{18,19},{22,21},{23,22},... | collective-permute-start | bytes 3145736 | tf_op jit(solution)/shard_map/ppermute | solution.py:529
  18.1 18.6 %collective-permute-start.10 = (bf16[256,2048]{1,0:T(8,128)(2,1)}, bf16[256,2048]{1,0:T(8,128)(2,1)S(1)}, u32[]{:S(2)}, u32[]{:S(2)}) collective-permute-start(bf16[256,2048]{1,0:T(8,128)(2,1)} %refs_0_), channel_id=1, source_target_pairs={{0,28},{4,0},{8,4},{12,8},{16,12},{20,16},{24,20},{28,24},{1,29},{... | collective-permute-start | bytes 3145736 | tf_op jit(solution)/shard_map/ppermute | solution.py:502
  23.8 53.7 %copy-start.11 = (s32[2048]{0:T(1024)S(1)}, s32[2048]{0:T(1024)}, u32[]{:S(2)}) copy-start(s32[2048]{0:T(1024)} %param.12) | copy-start | bytes 24580
  23.8 23.8 %collective-permute-start.2 = (bf16[2048,256]{1,0:T(8,128)(2,1)S(1)}, bf16[2048,256]{1,0:T(8,128)(2,1)S(1)}, u32[]{:S(2)}, u32[]{:S(2)}) collective-permute-start(bf16[2048,256]{1,0:T(8,128)(2,1)S(1)} %relay.3), channel_id=1, source_target_pairs={{1,0},{2,1},{4,5},{5,6},{6,7},{9,8},{10,9},{13,14},{14,15},{17,16}... | collective-permute-start | bytes 3145736 | tf_op jit(solution)/shard_map/ppermute | solution.py:529
  31.4 1.0 copy-start.1
  32.3 20.7 %collective-permute-start.4 = (bf16[2048,256]{1,0:T(8,128)(2,1)S(1)}, bf16[2048,256]{1,0:T(8,128)(2,1)S(1)}, u32[]{:S(2)}, u32[]{:S(2)}) collective-permute-start(bf16[2048,256]{1,0:T(8,128)(2,1)S(1)} %relay.4), channel_id=1, source_target_pairs={{0,1},{1,2},{2,3},{5,4},{6,5},{9,10},{10,11},{13,12},{14,13},{15,1... | collective-permute-start | bytes 3145736 | tf_op jit(solution)/shard_map/ppermute | solution.py:529
  36.7 18.6 %collective-permute-start.11 = (bf16[256,2048]{1,0:T(8,128)(2,1)S(1)}, bf16[256,2048]{1,0:T(8,128)(2,1)}, u32[]{:S(2)}, u32[]{:S(2)}) collective-permute-start(bf16[256,2048]{1,0:T(8,128)(2,1)S(1)} %collective-permute-done.10.refs_1_), channel_id=1, source_target_pairs={{0,28},{4,0},{8,4},{12,8},{16,12},{20,16},{24,20},{28,24},{1,29},{... | collective-permute-start | bytes 3145736 | tf_op jit(solution)/shard_map/ppermute | solution.py:502
  36.7 1.1 copy-start.8
  47.6 23.2 %collective-permute-start.5 = (bf16[2048,256]{1,0:T(8,128)(2,1)S(1)}, bf16[2048,256]{1,0:T(8,128)(2,1)}, u32[]{:S(2)}, u32[]{:S(2)}) collective-permute-start(bf16[2048,256]{1,0:T(8,128)(2,1)S(1)} %collective-permute-done.2.refs_2_.refs_0_), channel_id=1, source_target_pairs={{1,0},{5,6},{6,7},{9,8},{14,15},{17,16},{18,17},{21,22},{22,23},{2... | collective-permute-start | bytes 3145736 | tf_op jit(solution)/shard_map/ppermute | solution.py:529
  48.9 24.3 %collective-permute-start.7 = (bf16[2048,256]{1,0:T(8,128)(2,1)S(1)}, bf16[2048,256]{1,0:T(8,128)(2,1)S(1)}, u32[]{:S(2)}, u32[]{:S(2)}) collective-permute-start(bf16[2048,256]{1,0:T(8,128)(2,1)S(1)} %collective-permute-done.2.refs_2_.refs_0_), channel_id=1, source_target_pairs={{1,17},{24,8},{22,2}} | collective-permute-start | bytes 3145736 | tf_op jit(solution)/shard_map/ppermute | solution.py:509
  49.6 1.0 copy-start.3
  53.6 22.2 %collective-permute-start.6 = (bf16[2048,256]{1,0:T(8,128)(2,1)S(1)}, bf16[2048,256]{1,0:T(8,128)(2,1)}, u32[]{:S(2)}, u32[]{:S(2)}) collective-permute-start(bf16[2048,256]{1,0:T(8,128)(2,1)S(1)} %relay.5), channel_id=1, source_target_pairs={{1,2},{2,3},{5,4},{9,10},{10,11},{13,12},{14,13},{21,20},{22,21},{... | collective-permute-start | bytes 3145736 | tf_op jit(solution)/shard_map/ppermute | solution.py:529
  55.3 22.3 %collective-permute-start.12 = (bf16[256,2048]{1,0:T(8,128)(2,1)}, bf16[256,2048]{1,0:T(8,128)(2,1)}, u32[]{:S(2)}, u32[]{:S(2)}) collective-permute-start(bf16[256,2048]{1,0:T(8,128)(2,1)} %collective-permute-done.11.refs_2_), channel_id=1, source_target_pairs={{0,28},{4,0},{8,4},{12,8},{16,12},{20,16},{24,20},{28,24},{1,29},{... | collective-permute-start | bytes 3145736 | tf_op jit(solution)/shard_map/ppermute | solution.py:502
  70.8 19.2 %collective-permute-start.14 = (bf16[2048,256]{1,0:T(8,128)(2,1)}, bf16[2048,256]{1,0:T(8,128)(2,1)}, u32[]{:S(2)}, u32[]{:S(2)}) collective-permute-start(bf16[2048,256]{1,0:T(8,128)(2,1)} %collective-permute-done.5.refs_5_.refs_2_), channel_id=1, source_target_pairs={{0,16},{23,3}} | collective-permute-start | bytes 3145736 | tf_op jit(solution)/shard_map/ppermute | solution.py:509
  73.2 10.5 %collective-permute-start.13 = (f32[2048]{0:T(1024)S(1)}, f32[2048]{0:T(1024)S(1)}, u32[]{:S(2)}, u32[]{:S(2)}) collective-permute-start(f32[2048]{0:T(1024)S(1)} %multiply_reduce_fusion), channel_id=1, source_target_pairs={{0,1},{1,0},{2,3},{3,2},{4,5},{5,4},{6,7},{7,6},{8,9},{9,8},{10,11... | collective-permute-start | bytes 24584 | tf_op jit(solution)/shard_map/ppermute | solution.py:490
  73.2 1.0 copy-start.5
  74.2 28.5 %collective-permute-start.8 = (bf16[2048,256]{1,0:T(8,128)(2,1)}, bf16[2048,256]{1,0:T(8,128)(2,1)}, u32[]{:S(2)}, u32[]{:S(2)}) collective-permute-start(bf16[2048,256]{1,0:T(8,128)(2,1)} %collective-permute-done.5.refs_5_.refs_2_), channel_id=1, source_target_pairs={{6,7},{17,16},{22,23},{25,24},{30,31}} | collective-permute-start | bytes 3145736 | tf_op jit(solution)/shard_map/ppermute | solution.py:529
  75.8 26.9 %collective-permute-start.9 = (bf16[2048,256]{1,0:T(8,128)(2,1)}, bf16[2048,256]{1,0:T(8,128)(2,1)}, u32[]{:S(2)}, u32[]{:S(2)}) collective-permute-start(bf16[2048,256]{1,0:T(8,128)(2,1)} %collective-permute-done.6.refs_6_.refs_3_), channel_id=1, source_target_pairs={{2,3},{10,11},{13,12},{21,20},{26,27}} | collective-permute-start | bytes 3145736 | tf_op jit(solution)/shard_map/ppermute | solution.py:529
  78.0 1.2 %copy-start.7 = (bf16[256,2048]{1,0:T(8,128)(2,1)S(1)}, bf16[256,2048]{1,0:T(8,128)(2,1)}, u32[]{:S(2)}) copy-start(bf16[256,2048]{1,0:T(8,128)(2,1)} %refs_0_) | copy-start | bytes 3145732
  79.2 1.2 %copy-start.9 = (bf16[256,2048]{1,0:T(8,128)(2,1)S(1)}, bf16[256,2048]{1,0:T(8,128)(2,1)}, u32[]{:S(2)}) copy-start(bf16[256,2048]{1,0:T(8,128)(2,1)} %copy-done.8) | copy-start | bytes 3145732
  80.4 9.9 %copy-start.2 = (bf16[2048,256]{1,0:T(8,128)(2,1)S(1)}, bf16[2048,256]{1,0:T(8,128)(2,1)}, u32[]{:S(2)}) copy-start(bf16[2048,256]{1,0:T(8,128)(2,1)} %copy-done.1) | copy-start | bytes 3145732
  80.4 9.9 %copy-start.4 = (bf16[2048,256]{1,0:T(8,128)(2,1)S(1)}, bf16[2048,256]{1,0:T(8,128)(2,1)}, u32[]{:S(2)}) copy-start(bf16[2048,256]{1,0:T(8,128)(2,1)} %copy-done.3) | copy-start | bytes 3145732
  80.4 9.9 %copy-start.6 = (bf16[2048,256]{1,0:T(8,128)(2,1)S(1)}, bf16[2048,256]{1,0:T(8,128)(2,1)}, u32[]{:S(2)}) copy-start(bf16[2048,256]{1,0:T(8,128)(2,1)} %copy-done.5) | copy-start | bytes 3145732
  83.7 18.4 %collective-permute-start.15 = (f32[2048]{0:T(1024)S(1)}, f32[2048]{0:T(1024)S(1)}, u32[]{:S(2)}, u32[]{:S(2)}) collective-permute-start(f32[2048]{0:T(1024)S(1)} %add.39), channel_id=1, source_target_pairs={{0,2},{1,3},{2,0},{3,1},{4,6},{5,7},{6,4},{7,5},{8,10},{9,11},{10,... | collective-permute-start | bytes 24584 | tf_op jit(solution)/shard_map/ppermute | solution.py:490

commit v20 on v19

--- a/solution.py
+++ b/solution.py
@@ -16,6 +16,7 @@
 COL_TILE = 512
 ROW_BLOCK = 512
 ROW_TILE = 32
+TALL_TILE = 128
 LANES = 128
 VMEM_LIMIT = 10 * 2**20
 RELAY_LIMIT = 2 * 2**20
@@ -218,10 +219,10 @@
     place, step = table[at], table[at + 1]
 
     def from_source(source, col):
-        @pl.loop(0, count // ROW_TILE)
+        @pl.loop(0, count // TALL_TILE)
         def _(i):
-            here = pl.ds(pl.multiple_of(first + i * ROW_TILE, ROW_TILE), ROW_TILE)
-            to = pl.ds(pl.multiple_of(i * ROW_TILE, ROW_TILE), ROW_TILE)
+            here = pl.ds(pl.multiple_of(first + i * TALL_TILE, TALL_TILE), TALL_TILE)
+            to = pl.ds(pl.multiple_of(i * TALL_TILE, TALL_TILE), TALL_TILE)
             for k in range(0, width, LANES):
                 lanes = pl.ds(pl.multiple_of(step * width + k, LANES), LANES)
                 value = source[here, pl.ds(pl.multiple_of(col + k, LANES), LANES)].astype(jnp.float32)

time: 111 us -> 110 us (level)
  no operation moved by 1% of the time
where the time goes in v20:
time: 110 us; the launch traced here: 109 us
  waiting for transfers between devices  36 us (33%)
  starting transfers between devices  32.5 us (30%)
  Pallas kernels  24.2 us (22%)
  local copies, waits for them, and re-layouts  13.7 us (12%)
  other arithmetic  1.73 us (2%)
    ppermute x8, waiting for transfers between devices, local(): buffers[key] = lax.ppermute(held, both, pairs_of[key])  35.9 us
    ppermute x8, starting transfers between devices, local(): buffers[key] = lax.ppermute(held, both, pairs_of[key])  20.7 us
    pallas_call x1, Pallas kernels, early_product(): pl.pallas_call(functools.partial(early_kernel, at, candidates, len(buffer...  10.8 us
    pallas_call x1, Pallas kernels, last_product(): pl.pallas_call(functools.partial(last_kernel, at, candidates, scale, len(...  7.28 us
    unnamed x28, local copies, waits for them, and re-layouts  6.41 us
    ppermute x2, starting transfers between devices, sum_beside(): other = lax.ppermute(squares, 'col', [(i, i ^ bit) for i in range(cols)])  6.29 us
    dynamic_slice x3, local copies, waits for them, and re-layouts, own_chunk(): lax.dynamic_slice(x, (piece * piece_rows, group * group_size), (piece_row...  5.69 us
    pallas_call x1, Pallas kernels, standardized_window(): pl.pallas_call(functools.partial(window_kernel, at), out_shape=pltpu.VMEM...  3.23 us
  transfers between devices with their start and end apart: 16, of which 5 were waited for; matrix products, arithmetic and copies ran while one was open for 6% of the time, Pallas kernels for 16%

profile of v20, /device:TPU:0, one launch (start us, length us, event | category | flops | bytes accessed | tf_op | source)
XLA Modules:
  0.0 109.1 jit_solution(17410993907597358929)
XLA Ops:
  0.6 0.0 copy-start
  0.6 0.0 copy-start.13
  0.7 2.4 %constant_dynamic-slice_fusion.1 = bf16[2048,256]{1,0:T(8,128)(2,1)} fusion(bf16[2048,512]{1,0:T(8,128)(2,1)} %x.9, s32[]{:T(128)S(6)} %select_n.35), kind=kLoop, calls=%fused_computation.14 | loop fusion | bytes 2097156 | tf_op jit(solution)/shard_map/dynamic_slice | solution.py:449
  3.1 1.3 %collective-permute-start.1 = (bf16[2048,256]{1,0:T(8,128)(2,1)}, bf16[2048,256]{1,0:T(8,128)(2,1)}, u32[]{:S(2)}, u32[]{:S(2)}) collective-permute-start(bf16[2048,256]{1,0:T(8,128)(2,1)} %constant_dynamic-slice_fusion.1), channel_id=1, source_target_pairs={{1,0},{5,6},{6,7},{9,8},{10,9},{14,15},{18,17},{19,18},{22,23},{27... | collective-permute-start | bytes 3145736 | tf_op jit(solution)/shard_map/ppermute | solution.py:530
  4.4 2.3 %dynamic_slice.32 = bf16[2048,256]{1,0:T(8,128)(2,1)} slice(bf16[2048,512]{1,0:T(8,128)(2,1)} %x.9), slice={[0:2048], [256:512]} | slice | bytes 2097152 | tf_op jit(solution)/shard_map/dynamic_slice | solution.py:449
  6.6 1.6 %collective-permute-start = (bf16[2048,256]{1,0:T(8,128)(2,1)}, bf16[2048,256]{1,0:T(8,128)(2,1)}, u32[]{:S(2)}, u32[]{:S(2)}) collective-permute-start(bf16[2048,256]{1,0:T(8,128)(2,1)} %dynamic_slice.32), channel_id=1, source_target_pairs={{18,2},{9,25},{1,21}} | collective-permute-start | bytes 3145736 | tf_op jit(solution)/shard_map/ppermute | solution.py:498
  8.3 0.0 copy-done.13
  8.3 0.1 dynamic_slice.27
  8.4 0.1 dynamic_slice.28
  8.5 0.0 copy-done
  8.5 1.0 multiply_reduce_fusion
  9.5 1.0 constant_dynamic-slice_fusion
  10.5 7.5 %collective-permute-start.3 = (bf16[2048,256]{1,0:T(8,128)(2,1)}, bf16[2048,256]{1,0:T(8,128)(2,1)S(1)}, u32[]{:S(2)}, u32[]{:S(2)}) collective-permute-start(bf16[2048,256]{1,0:T(8,128)(2,1)} %constant_dynamic-slice_fusion), channel_id=1, source_target_pairs={{0,1},{1,2},{5,4},{10,11},{13,12},{14,13},{18,19},{22,21},{23,22},... | collective-permute-start | bytes 3145736 | tf_op jit(solution)/shard_map/ppermute | solution.py:530
  18.1 0.0 collective-permute-done.refs_0_
  18.1 0.1 collective-permute-start.10
  18.2 0.7 fusion.2.table
  18.9 3.3 %collective-permute-done.1.refs_1_.refs_0_ = bf16[2048,256]{1,0:T(8,128)(2,1)} collective-permute-done((bf16[2048,256]{1,0:T(8,128)(2,1)}, bf16[2048,256]{1,0:T(8,128)(2,1)}, u32[]{:S(2)}, u32[]{:S(2)}) %collective-permute-start.1) | collective-permute-done | bytes 1048608 | tf_op jit(solution)/shard_map/ppermute | solution.py:530
  22.1 1.6 %relay.3 = bf16[2048,256]{1,0:T(8,128)(2,1)S(1)} custom-call(s32[21]{0:T(128)S(1)} %fusion.2.table, bf16[2048,512]{1,0:T(8,128)(2,1)S(1)} %copy-done, bf16[2048,256]{1,0:T(8,128)(2,1)} %collective-permute-done.refs_0_, bf16[2048,256]{1,0:T(8,128)(2,1)} %collective-permute-done.1.refs_1_.refs_0_), custom_call_target="tpu_custom_call" | custom-call | tf_op jit(solution)/shard_map/relay/pallas_call | solution.py:168
  23.8 0.0 copy-start.11
  23.8 1.3 %collective-permute-start.2 = (bf16[2048,256]{1,0:T(8,128)(2,1)S(1)}, bf16[2048,256]{1,0:T(8,128)(2,1)S(1)}, u32[]{:S(2)}, u32[]{:S(2)}) collective-permute-start(bf16[2048,256]{1,0:T(8,128)(2,1)S(1)} %relay.3), channel_id=1, source_target_pairs={{1,0},{2,1},{4,5},{5,6},{6,7},{9,8},{10,9},{13,14},{14,15},{17,16}... | collective-permute-start | bytes 3145736 | tf_op jit(solution)/shard_map/ppermute | solution.py:530
  25.1 5.6 %collective-permute-done.3.refs_0_.refs_1_ = bf16[2048,256]{1,0:T(8,128)(2,1)S(1)} collective-permute-done((bf16[2048,256]{1,0:T(8,128)(2,1)}, bf16[2048,256]{1,0:T(8,128)(2,1)S(1)}, u32[]{:S(2)}, u32[]{:S(2)}) %collective-permute-start.3) | collective-permute-done | bytes 1048608 | tf_op jit(solution)/shard_map/ppermute | solution.py:530
  30.7 0.6 relay.4
  31.4 0.9 copy-done.1
  32.3 4.3 %collective-permute-start.4 = (bf16[2048,256]{1,0:T(8,128)(2,1)S(1)}, bf16[2048,256]{1,0:T(8,128)(2,1)S(1)}, u32[]{:S(2)}, u32[]{:S(2)}) collective-permute-start(bf16[2048,256]{1,0:T(8,128)(2,1)S(1)} %relay.4), channel_id=1, source_target_pairs={{0,1},{1,2},{2,3},{5,4},{6,5},{9,10},{10,11},{13,12},{14,13},{15,1... | collective-permute-start | bytes 3145736 | tf_op jit(solution)/shard_map/ppermute | solution.py:530
  36.7 0.0 collective-permute-done.10.refs_1_
  36.7 0.1 collective-permute-start.11
  36.7 0.0 copy-start.8
  36.7 1.0 copy-done.8
  37.8 9.8 %collective-permute-done.2.refs_2_.refs_0_ = bf16[2048,256]{1,0:T(8,128)(2,1)S(1)} collective-permute-done((bf16[2048,256]{1,0:T(8,128)(2,1)S(1)}, bf16[2048,256]{1,0:T(8,128)(2,1)S(1)}, u32[]{:S(2)}, u32[]{:S(2)}) %collective-permute-start.2) | collective-permute-done | bytes 1048608 | tf_op jit(solution)/shard_map/ppermute | solution.py:530
  47.6 1.3 %collective-permute-start.5 = (bf16[2048,256]{1,0:T(8,128)(2,1)S(1)}, bf16[2048,256]{1,0:T(8,128)(2,1)}, u32[]{:S(2)}, u32[]{:S(2)}) collective-permute-start(bf16[2048,256]{1,0:T(8,128)(2,1)S(1)} %collective-permute-done.2.refs_2_.refs_0_), channel_id=1, source_target_pairs={{1,0},{5,6},{6,7},{9,8},{14,15},{17,16},{18,17},{21,22},{22,23},{2... | collective-permute-start | bytes 3145736 | tf_op jit(solution)/shard_map/ppermute | solution.py:530
  48.9 0.7 collective-permute-start.7
  49.6 0.0 copy-start.3
  49.6 1.0 copy-done.3
  50.6 2.4 %collective-permute-done.4.refs_0_.refs_3_.refs_1_ = bf16[2048,256]{1,0:T(8,128)(2,1)S(1)} collective-permute-done((bf16[2048,256]{1,0:T(8,128)(2,1)S(1)}, bf16[2048,256]{1,0:T(8,128)(2,1)S(1)}, u32[]{:S(2)}, u32[]{:S(2)}) %collective-permute-start.4) | collective-permute-done | bytes 1048608 | tf_op jit(solution)/shard_map/ppermute | solution.py:530
  53.0 0.6 relay.5
  53.6 1.7 %collective-permute-start.6 = (bf16[2048,256]{1,0:T(8,128)(2,1)S(1)}, bf16[2048,256]{1,0:T(8,128)(2,1)}, u32[]{:S(2)}, u32[]{:S(2)}) collective-permute-start(bf16[2048,256]{1,0:T(8,128)(2,1)S(1)} %relay.5), channel_id=1, source_target_pairs={{1,2},{2,3},{5,4},{9,10},{10,11},{13,12},{14,13},{21,20},{22,21},{... | collective-permute-start | bytes 3145736 | tf_op jit(solution)/shard_map/ppermute | solution.py:530
  55.3 0.0 collective-permute-done.11.refs_2_
  55.3 0.7 collective-permute-start.12
  56.0 14.8 %collective-permute-done.5.refs_5_.refs_2_ = bf16[2048,256]{1,0:T(8,128)(2,1)} collective-permute-done((bf16[2048,256]{1,0:T(8,128)(2,1)S(1)}, bf16[2048,256]{1,0:T(8,128)(2,1)}, u32[]{:S(2)}, u32[]{:S(2)}) %collective-permute-start.5) | collective-permute-done | bytes 1048608 | tf_op jit(solution)/shard_map/ppermute | solution.py:530
  70.8 2.4 %collective-permute-start.14 = (bf16[2048,256]{1,0:T(8,128)(2,1)}, bf16[2048,256]{1,0:T(8,128)(2,1)}, u32[]{:S(2)}, u32[]{:S(2)}) collective-permute-start(bf16[2048,256]{1,0:T(8,128)(2,1)} %collective-permute-done.5.refs_5_.refs_2_), channel_id=1, source_target_pairs={{0,16},{23,3}} | collective-permute-start | bytes 3145736 | tf_op jit(solution)/shard_map/ppermute | solution.py:510
  73.2 0.0 collective-permute-start.13
  73.2 0.0 collective-permute-done.7.refs_4_
  73.2 1.0 copy-done.5
  74.2 1.7 %collective-permute-start.8 = (bf16[2048,256]{1,0:T(8,128)(2,1)}, bf16[2048,256]{1,0:T(8,128)(2,1)}, u32[]{:S(2)}, u32[]{:S(2)}) collective-permute-start(bf16[2048,256]{1,0:T(8,128)(2,1)} %collective-permute-done.5.refs_5_.refs_2_), channel_id=1, source_target_pairs={{6,7},{17,16},{22,23},{25,24},{30,31}} | collective-permute-start | bytes 3145736 | tf_op jit(solution)/shard_map/ppermute | solution.py:530
  75.8 0.0 collective-permute-done.6.refs_6_.refs_3_
  75.8 1.6 %collective-permute-start.9 = (bf16[2048,256]{1,0:T(8,128)(2,1)}, bf16[2048,256]{1,0:T(8,128)(2,1)}, u32[]{:S(2)}, u32[]{:S(2)}) collective-permute-start(bf16[2048,256]{1,0:T(8,128)(2,1)} %collective-permute-done.6.refs_6_.refs_3_), channel_id=1, source_target_pairs={{2,3},{10,11},{13,12},{21,20},{26,27}} | collective-permute-start | bytes 3145736 | tf_op jit(solution)/shard_map/ppermute | solution.py:530
  77.5 0.1 fusion
  77.6 0.0 collective-permute-done.12.refs_3_
  77.6 0.2 broadcast_in_dim.42.refs_4_
  77.8 0.2 broadcast_in_dim.43.refs_5_
  78.0 0.0 copy-start.7
  78.0 1.2 %copy-done.7 = bf16[256,2048]{1,0:T(8,128)(2,1)S(1)} copy-done((bf16[256,2048]{1,0:T(8,128)(2,1)S(1)}, bf16[256,2048]{1,0:T(8,128)(2,1)}, u32[]{:S(2)}) %copy-start.7) | copy-done | bytes 1048600
  79.2 1.2 %copy-done.9 = bf16[256,2048]{1,0:T(8,128)(2,1)S(1)} copy-done((bf16[256,2048]{1,0:T(8,128)(2,1)S(1)}, bf16[256,2048]{1,0:T(8,128)(2,1)}, u32[]{:S(2)}) %copy-start.9) | copy-done | bytes 1048600
  80.4 3.2 %window.1.refs_11_.refs_9_ = bf16[1024,2048]{1,0:T(8,128)(2,1)S(1)} custom-call(s32[21]{0:T(128)S(1)} %fusion.2.table, bf16[256,2048]{1,0:T(8,128)(2,1)S(1)} %copy-done.7, bf16[256,2048]{1,0:T(8,128)(2,1)S(1)} %copy-done.9, bf16[256,2048]{1,0:T(8,128)(2,1)} %collective-permute-done.11.refs_2_, bf16[256,2048]{1,0:T(8,128)(2,1)} %collective-permute-done.12.refs_3_, ...), custom_call_target="tpu_custom_call" | custom-call | flops 8388608 | bytes 8388608 | tf_op jit(solution)/shard_map/window/pallas_call | solution.py:206
  83.7 0.0 collective-permute-done.13
  83.7 6.3 %collective-permute-start.15 = (f32[2048]{0:T(1024)S(1)}, f32[2048]{0:T(1024)S(1)}, u32[]{:S(2)}, u32[]{:S(2)}) collective-permute-start(f32[2048]{0:T(1024)S(1)} %add.39), channel_id=1, source_target_pairs={{0,2},{1,3},{2,0},{3,1},{4,6},{5,7},{6,4},{7,5},{8,10},{9,11},{10,... | collective-permute-start | bytes 24584 | tf_op jit(solution)/shard_map/ppermute | solution.py:491
  90.0 0.0 collective-permute-done.14.refs_7_
  90.0 0.3 broadcast_in_dim.41.refs_10_.refs_8_
  90.3 10.8 %early.1.refs_10_ = f32[2048,2048]{1,0:T(8,128)S(1)} custom-call(s32[21]{0:T(128)S(1)} %fusion.2.table, bf16[2048,512]{1,0:T(8,128)(2,1)S(1)} %copy-done, bf16[2048,256]{1,0:T(8,128)(2,1)} %collective-permute-done.1.refs_1_.refs_0_, bf16[2048,256]{1,0:T(8,128)(2,1)S(1)} %copy-done.2, bf16[2048,256]{1,0:T(8,128)(2,1)S(1)} %copy-done.4, ...), custom_call_target="tpu_custom_call" | custom-call | flops 6442450944 | tf_op jit(solution)/shard_map/early/pallas_call | solution.py:267
  101.2 0.0 collective-permute-done.15
  101.2 0.6 multiply_add_fusion
  101.8 0.0 collective-permute-done.8.refs_4_
  101.8 0.0 collective-permute-done.9.refs_5_
  101.8 7.3 %last.1 = bf16[2048,2048]{1,0:T(8,128)(2,1)} custom-call(s32[21]{0:T(128)S(1)} %fusion.2.table, bf16[2048,512]{1,0:T(8,128)(2,1)S(1)} %copy-done, bf16[2048,256]{1,0:T(8,128)(2,1)S(1)} %copy-done.4, bf16[2048,256]{1,0:T(8,128)(2,1)S(1)} %collective-permute-done.4.refs_0_.refs_3_.refs_1_, bf16[2048,256]{1,0:T(8,128)(2,1)} %collective-permute-done.5.refs_5_.refs_2_, ...), custom_call_target="tpu_custom_call" | custom-call | flops 2147483648 | bytes 8388608 | tf_op jit(solution)/shard_map/last/pallas_call | solution.py:311
  (18 shorter events, 0.0 us)
Async XLA Ops:
  0.6 7.8 %copy-start = (bf16[2048,512]{1,0:T(8,128)(2,1)S(1)}, bf16[2048,512]{1,0:T(8,128)(2,1)}, u32[]{:S(2)}) copy-start(bf16[2048,512]{1,0:T(8,128)(2,1)} %x.9) | copy-start | bytes 6291460
  0.6 7.6 %copy-start.13 = (f32[2048]{0:T(1024)S(1)}, f32[2048]{0:T(1024)}, u32[]{:S(2)}) copy-start(f32[2048]{0:T(1024)} %param.10) | copy-start | bytes 24580
  0.7 7.6 %copy-start.12 = (f32[2048]{0:T(1024)S(1)}, f32[2048]{0:T(1024)}, u32[]{:S(2)}) copy-start(f32[2048]{0:T(1024)} %param.9) | copy-start | bytes 24580
  0.7 7.8 %copy-start.10 = (s32[2048]{0:T(1024)S(1)}, s32[2048]{0:T(1024)}, u32[]{:S(2)}) copy-start(s32[2048]{0:T(1024)} %param.11) | copy-start | bytes 24580
  3.1 19.1 %collective-permute-start.1 = (bf16[2048,256]{1,0:T(8,128)(2,1)}, bf16[2048,256]{1,0:T(8,128)(2,1)}, u32[]{:S(2)}, u32[]{:S(2)}) collective-permute-start(bf16[2048,256]{1,0:T(8,128)(2,1)} %constant_dynamic-slice_fusion.1), channel_id=1, source_target_pairs={{1,0},{5,6},{6,7},{9,8},{10,9},{14,15},{18,17},{19,18},{22,23},{27... | collective-permute-start | bytes 3145736 | tf_op jit(solution)/shard_map/ppermute | solution.py:530
  6.6 11.5 %collective-permute-start = (bf16[2048,256]{1,0:T(8,128)(2,1)}, bf16[2048,256]{1,0:T(8,128)(2,1)}, u32[]{:S(2)}, u32[]{:S(2)}) collective-permute-start(bf16[2048,256]{1,0:T(8,128)(2,1)} %dynamic_slice.32), channel_id=1, source_target_pairs={{18,2},{9,25},{1,21}} | collective-permute-start | bytes 3145736 | tf_op jit(solution)/shard_map/ppermute | solution.py:498
  10.5 20.2 %collective-permute-start.3 = (bf16[2048,256]{1,0:T(8,128)(2,1)}, bf16[2048,256]{1,0:T(8,128)(2,1)S(1)}, u32[]{:S(2)}, u32[]{:S(2)}) collective-permute-start(bf16[2048,256]{1,0:T(8,128)(2,1)} %constant_dynamic-slice_fusion), channel_id=1, source_target_pairs={{0,1},{1,2},{5,4},{10,11},{13,12},{14,13},{18,19},{22,21},{23,22},... | collective-permute-start | bytes 3145736 | tf_op jit(solution)/shard_map/ppermute | solution.py:530
  18.1 18.6 %collective-permute-start.10 = (bf16[256,2048]{1,0:T(8,128)(2,1)}, bf16[256,2048]{1,0:T(8,128)(2,1)S(1)}, u32[]{:S(2)}, u32[]{:S(2)}) collective-permute-start(bf16[256,2048]{1,0:T(8,128)(2,1)} %refs_0_), channel_id=1, source_target_pairs={{0,28},{4,0},{8,4},{12,8},{16,12},{20,16},{24,20},{28,24},{1,29},{... | collective-permute-start | bytes 3145736 | tf_op jit(solution)/shard_map/ppermute | solution.py:503
  23.8 53.7 %copy-start.11 = (s32[2048]{0:T(1024)S(1)}, s32[2048]{0:T(1024)}, u32[]{:S(2)}) copy-start(s32[2048]{0:T(1024)} %param.12) | copy-start | bytes 24580
  23.8 23.8 %collective-permute-start.2 = (bf16[2048,256]{1,0:T(8,128)(2,1)S(1)}, bf16[2048,256]{1,0:T(8,128)(2,1)S(1)}, u32[]{:S(2)}, u32[]{:S(2)}) collective-permute-start(bf16[2048,256]{1,0:T(8,128)(2,1)S(1)} %relay.3), channel_id=1, source_target_pairs={{1,0},{2,1},{4,5},{5,6},{6,7},{9,8},{10,9},{13,14},{14,15},{17,16}... | collective-permute-start | bytes 3145736 | tf_op jit(solution)/shard_map/ppermute | solution.py:530
  31.4 1.0 copy-start.1
  32.3 20.7 %collective-permute-start.4 = (bf16[2048,256]{1,0:T(8,128)(2,1)S(1)}, bf16[2048,256]{1,0:T(8,128)(2,1)S(1)}, u32[]{:S(2)}, u32[]{:S(2)}) collective-permute-start(bf16[2048,256]{1,0:T(8,128)(2,1)S(1)} %relay.4), channel_id=1, source_target_pairs={{0,1},{1,2},{2,3},{5,4},{6,5},{9,10},{10,11},{13,12},{14,13},{15,1... | collective-permute-start | bytes 3145736 | tf_op jit(solution)/shard_map/ppermute | solution.py:530
  36.7 18.6 %collective-permute-start.11 = (bf16[256,2048]{1,0:T(8,128)(2,1)S(1)}, bf16[256,2048]{1,0:T(8,128)(2,1)}, u32[]{:S(2)}, u32[]{:S(2)}) collective-permute-start(bf16[256,2048]{1,0:T(8,128)(2,1)S(1)} %collective-permute-done.10.refs_1_), channel_id=1, source_target_pairs={{0,28},{4,0},{8,4},{12,8},{16,12},{20,16},{24,20},{28,24},{1,29},{... | collective-permute-start | bytes 3145736 | tf_op jit(solution)/shard_map/ppermute | solution.py:503
  36.7 1.1 copy-start.8
  47.6 23.2 %collective-permute-start.5 = (bf16[2048,256]{1,0:T(8,128)(2,1)S(1)}, bf16[2048,256]{1,0:T(8,128)(2,1)}, u32[]{:S(2)}, u32[]{:S(2)}) collective-permute-start(bf16[2048,256]{1,0:T(8,128)(2,1)S(1)} %collective-permute-done.2.refs_2_.refs_0_), channel_id=1, source_target_pairs={{1,0},{5,6},{6,7},{9,8},{14,15},{17,16},{18,17},{21,22},{22,23},{2... | collective-permute-start | bytes 3145736 | tf_op jit(solution)/shard_map/ppermute | solution.py:530
  48.9 24.3 %collective-permute-start.7 = (bf16[2048,256]{1,0:T(8,128)(2,1)S(1)}, bf16[2048,256]{1,0:T(8,128)(2,1)S(1)}, u32[]{:S(2)}, u32[]{:S(2)}) collective-permute-start(bf16[2048,256]{1,0:T(8,128)(2,1)S(1)} %collective-permute-done.2.refs_2_.refs_0_), channel_id=1, source_target_pairs={{1,17},{24,8},{22,2}} | collective-permute-start | bytes 3145736 | tf_op jit(solution)/shard_map/ppermute | solution.py:510
  49.6 1.0 copy-start.3
  53.6 22.2 %collective-permute-start.6 = (bf16[2048,256]{1,0:T(8,128)(2,1)S(1)}, bf16[2048,256]{1,0:T(8,128)(2,1)}, u32[]{:S(2)}, u32[]{:S(2)}) collective-permute-start(bf16[2048,256]{1,0:T(8,128)(2,1)S(1)} %relay.5), channel_id=1, source_target_pairs={{1,2},{2,3},{5,4},{9,10},{10,11},{13,12},{14,13},{21,20},{22,21},{... | collective-permute-start | bytes 3145736 | tf_op jit(solution)/shard_map/ppermute | solution.py:530
  55.3 22.3 %collective-permute-start.12 = (bf16[256,2048]{1,0:T(8,128)(2,1)}, bf16[256,2048]{1,0:T(8,128)(2,1)}, u32[]{:S(2)}, u32[]{:S(2)}) collective-permute-start(bf16[256,2048]{1,0:T(8,128)(2,1)} %collective-permute-done.11.refs_2_), channel_id=1, source_target_pairs={{0,28},{4,0},{8,4},{12,8},{16,12},{20,16},{24,20},{28,24},{1,29},{... | collective-permute-start | bytes 3145736 | tf_op jit(solution)/shard_map/ppermute | solution.py:503
  70.8 19.2 %collective-permute-start.14 = (bf16[2048,256]{1,0:T(8,128)(2,1)}, bf16[2048,256]{1,0:T(8,128)(2,1)}, u32[]{:S(2)}, u32[]{:S(2)}) collective-permute-start(bf16[2048,256]{1,0:T(8,128)(2,1)} %collective-permute-done.5.refs_5_.refs_2_), channel_id=1, source_target_pairs={{0,16},{23,3}} | collective-permute-start | bytes 3145736 | tf_op jit(solution)/shard_map/ppermute | solution.py:510
  73.2 10.5 %collective-permute-start.13 = (f32[2048]{0:T(1024)S(1)}, f32[2048]{0:T(1024)S(1)}, u32[]{:S(2)}, u32[]{:S(2)}) collective-permute-start(f32[2048]{0:T(1024)S(1)} %multiply_reduce_fusion), channel_id=1, source_target_pairs={{0,1},{1,0},{2,3},{3,2},{4,5},{5,4},{6,7},{7,6},{8,9},{9,8},{10,11... | collective-permute-start | bytes 24584 | tf_op jit(solution)/shard_map/ppermute | solution.py:491
  73.2 1.0 copy-start.5
  74.2 27.6 %collective-permute-start.8 = (bf16[2048,256]{1,0:T(8,128)(2,1)}, bf16[2048,256]{1,0:T(8,128)(2,1)}, u32[]{:S(2)}, u32[]{:S(2)}) collective-permute-start(bf16[2048,256]{1,0:T(8,128)(2,1)} %collective-permute-done.5.refs_5_.refs_2_), channel_id=1, source_target_pairs={{6,7},{17,16},{22,23},{25,24},{30,31}} | collective-permute-start | bytes 3145736 | tf_op jit(solution)/shard_map/ppermute | solution.py:530
  75.8 26.0 %collective-permute-start.9 = (bf16[2048,256]{1,0:T(8,128)(2,1)}, bf16[2048,256]{1,0:T(8,128)(2,1)}, u32[]{:S(2)}, u32[]{:S(2)}) collective-permute-start(bf16[2048,256]{1,0:T(8,128)(2,1)} %collective-permute-done.6.refs_6_.refs_3_), channel_id=1, source_target_pairs={{2,3},{10,11},{13,12},{21,20},{26,27}} | collective-permute-start | bytes 3145736 | tf_op jit(solution)/shard_map/ppermute | solution.py:530
  78.0 1.2 %copy-start.7 = (bf16[256,2048]{1,0:T(8,128)(2,1)S(1)}, bf16[256,2048]{1,0:T(8,128)(2,1)}, u32[]{:S(2)}) copy-start(bf16[256,2048]{1,0:T(8,128)(2,1)} %refs_0_) | copy-start | bytes 3145732
  79.2 1.2 %copy-start.9 = (bf16[256,2048]{1,0:T(8,128)(2,1)S(1)}, bf16[256,2048]{1,0:T(8,128)(2,1)}, u32[]{:S(2)}) copy-start(bf16[256,2048]{1,0:T(8,128)(2,1)} %copy-done.8) | copy-start | bytes 3145732
  80.4 9.9 %copy-start.2 = (bf16[2048,256]{1,0:T(8,128)(2,1)S(1)}, bf16[2048,256]{1,0:T(8,128)(2,1)}, u32[]{:S(2)}) copy-start(bf16[2048,256]{1,0:T(8,128)(2,1)} %copy-done.1) | copy-start | bytes 3145732
  80.4 9.9 %copy-start.4 = (bf16[2048,256]{1,0:T(8,128)(2,1)S(1)}, bf16[2048,256]{1,0:T(8,128)(2,1)}, u32[]{:S(2)}) copy-start(bf16[2048,256]{1,0:T(8,128)(2,1)} %copy-done.3) | copy-start | bytes 3145732
  80.4 9.9 %copy-start.6 = (bf16[2048,256]{1,0:T(8,128)(2,1)S(1)}, bf16[2048,256]{1,0:T(8,128)(2,1)}, u32[]{:S(2)}) copy-start(bf16[2048,256]{1,0:T(8,128)(2,1)} %copy-done.5) | copy-start | bytes 3145732
  83.7 17.5 %collective-permute-start.15 = (f32[2048]{0:T(1024)S(1)}, f32[2048]{0:T(1024)S(1)}, u32[]{:S(2)}, u32[]{:S(2)}) collective-permute-start(f32[2048]{0:T(1024)S(1)} %add.39), channel_id=1, source_target_pairs={{0,2},{1,3},{2,0},{3,1},{4,6},{5,7},{6,4},{7,5},{8,10},{9,11},{10,... | collective-permute-start | bytes 24584 | tf_op jit(solution)/shard_map/ppermute | solution.py:491

commit v21 on v20

--- a/solution.py
+++ b/solution.py
@@ -15,6 +15,7 @@
 HOP = 1
 COL_TILE = 512
 ROW_BLOCK = 512
+EARLY_BLOCK = 1024
 ROW_TILE = 32
 TALL_TILE = 128
 LANES = 128
@@ -252,9 +253,9 @@
         columns = slice(rank * width, (rank + 1) * width)
         standardize(table, at + 2 * rank, candidates[rank], x, buffers, factor, twice, male, zx, columns, 0, rows)
 
-    @pl.loop(0, rows // ROW_BLOCK)
+    @pl.loop(0, rows // EARLY_BLOCK)
     def _(i):
-        block = pl.ds(pl.multiple_of(i * ROW_BLOCK, ROW_BLOCK), ROW_BLOCK)
+        block = pl.ds(pl.multiple_of(i * EARLY_BLOCK, EARLY_BLOCK), EARLY_BLOCK)
         for j in range(0, total.shape[1], COL_TILE):
             right = zy[:depth, j : j + COL_TILE]
             total[block, j : j + COL_TILE] = jnp.dot(zx[block, :], right, preferred_element_type=jnp.float32)

time: 110 us -> 109 us (level)
  transfers between devices with their start and end apart: 16 -> 16, of which waited for: 5 -> 5; matrix products, arithmetic and copies ran while one was open for 6% -> 6% of each run, Pallas kernels for 16% -> 15%
where the time goes in v21:
time: 109 us
  waiting for transfers between devices  36 us (33%)
  starting transfers between devices  32.5 us (30%)
  Pallas kernels  23.9 us (22%)
  local copies, waits for them, and re-layouts  13.7 us (13%)
  other arithmetic  1.73 us (2%)
    ppermute x8, waiting for transfers between devices, local(): buffers[key] = lax.ppermute(held, both, pairs_of[key])  35.9 us
    ppermute x8, starting transfers between devices, local(): buffers[key] = lax.ppermute(held, both, pairs_of[key])  20.7 us
    pallas_call x1, Pallas kernels, early_product(): pl.pallas_call(functools.partial(early_kernel, at, candidates, len(buffer...  10.5 us
    pallas_call x1, Pallas kernels, last_product(): pl.pallas_call(functools.partial(last_kernel, at, candidates, scale, len(...  7.28 us
    unnamed x28, local copies, waits for them, and re-layouts  6.41 us
    ppermute x2, starting transfers between devices, sum_beside(): other = lax.ppermute(squares, 'col', [(i, i ^ bit) for i in range(cols)])  6.29 us
    dynamic_slice x3, local copies, waits for them, and re-layouts, own_chunk(): lax.dynamic_slice(x, (piece * piece_rows, group * group_size), (piece_row...  5.69 us
    pallas_call x1, Pallas kernels, standardized_window(): pl.pallas_call(functools.partial(window_kernel, at), out_shape=pltpu.VMEM...  3.23 us
  transfers between devices with their start and end apart: 16, of which 5 were waited for; matrix products, arithmetic and copies ran while one was open for 6% of the time, Pallas kernels for 15%

profile of v21, /device:TPU:0, one launch (start us, length us, event | category | flops | bytes accessed | tf_op | source)
XLA Modules:
  0.0 108.7 jit_solution(4678357923747699675)
XLA Ops:
  0.6 0.0 copy-start
  0.7 2.4 %constant_dynamic-slice_fusion.1 = bf16[2048,256]{1,0:T(8,128)(2,1)} fusion(bf16[2048,512]{1,0:T(8,128)(2,1)} %x.9, s32[]{:T(128)S(6)} %select_n.35), kind=kLoop, calls=%fused_computation.14 | loop fusion | bytes 2097156 | tf_op jit(solution)/shard_map/dynamic_slice | solution.py:450
  3.1 1.3 %collective-permute-start.1 = (bf16[2048,256]{1,0:T(8,128)(2,1)}, bf16[2048,256]{1,0:T(8,128)(2,1)}, u32[]{:S(2)}, u32[]{:S(2)}) collective-permute-start(bf16[2048,256]{1,0:T(8,128)(2,1)} %constant_dynamic-slice_fusion.1), channel_id=1, source_target_pairs={{1,0},{5,6},{6,7},{9,8},{10,9},{14,15},{18,17},{19,18},{22,23},{27... | collective-permute-start | bytes 3145736 | tf_op jit(solution)/shard_map/ppermute | solution.py:531
  4.4 2.3 %dynamic_slice.32 = bf16[2048,256]{1,0:T(8,128)(2,1)} slice(bf16[2048,512]{1,0:T(8,128)(2,1)} %x.9), slice={[0:2048], [256:512]} | slice | bytes 2097152 | tf_op jit(solution)/shard_map/dynamic_slice | solution.py:450
  6.6 1.6 %collective-permute-start = (bf16[2048,256]{1,0:T(8,128)(2,1)}, bf16[2048,256]{1,0:T(8,128)(2,1)}, u32[]{:S(2)}, u32[]{:S(2)}) collective-permute-start(bf16[2048,256]{1,0:T(8,128)(2,1)} %dynamic_slice.32), channel_id=1, source_target_pairs={{18,2},{9,25},{1,21}} | collective-permute-start | bytes 3145736 | tf_op jit(solution)/shard_map/ppermute | solution.py:499
  8.3 0.1 dynamic_slice.27
  8.4 0.1 dynamic_slice.28
  8.5 0.0 copy-done.10
  8.5 1.0 multiply_reduce_fusion
  9.5 1.0 constant_dynamic-slice_fusion
  10.5 7.5 %collective-permute-start.3 = (bf16[2048,256]{1,0:T(8,128)(2,1)}, bf16[2048,256]{1,0:T(8,128)(2,1)S(1)}, u32[]{:S(2)}, u32[]{:S(2)}) collective-permute-start(bf16[2048,256]{1,0:T(8,128)(2,1)} %constant_dynamic-slice_fusion), channel_id=1, source_target_pairs={{0,1},{1,2},{5,4},{10,11},{13,12},{14,13},{18,19},{22,21},{23,22},... | collective-permute-start | bytes 3145736 | tf_op jit(solution)/shard_map/ppermute | solution.py:531
  18.1 0.0 collective-permute-done.refs_0_
  18.1 0.1 collective-permute-start.10
  18.2 0.7 fusion.2.table
  18.9 3.3 %collective-permute-done.1.refs_1_.refs_0_ = bf16[2048,256]{1,0:T(8,128)(2,1)} collective-permute-done((bf16[2048,256]{1,0:T(8,128)(2,1)}, bf16[2048,256]{1,0:T(8,128)(2,1)}, u32[]{:S(2)}, u32[]{:S(2)}) %collective-permute-start.1) | collective-permute-done | bytes 1048608 | tf_op jit(solution)/shard_map/ppermute | solution.py:531
  22.1 1.6 %relay.3 = bf16[2048,256]{1,0:T(8,128)(2,1)S(1)} custom-call(s32[21]{0:T(128)S(1)} %fusion.2.table, bf16[2048,512]{1,0:T(8,128)(2,1)S(1)} %copy-done, bf16[2048,256]{1,0:T(8,128)(2,1)} %collective-permute-done.refs_0_, bf16[2048,256]{1,0:T(8,128)(2,1)} %collective-permute-done.1.refs_1_.refs_0_), custom_call_target="tpu_custom_call" | custom-call | tf_op jit(solution)/shard_map/relay/pallas_call | solution.py:169
  23.8 0.0 copy-start.11
  23.8 1.3 %collective-permute-start.2 = (bf16[2048,256]{1,0:T(8,128)(2,1)S(1)}, bf16[2048,256]{1,0:T(8,128)(2,1)S(1)}, u32[]{:S(2)}, u32[]{:S(2)}) collective-permute-start(bf16[2048,256]{1,0:T(8,128)(2,1)S(1)} %relay.3), channel_id=1, source_target_pairs={{1,0},{2,1},{4,5},{5,6},{6,7},{9,8},{10,9},{13,14},{14,15},{17,16}... | collective-permute-start | bytes 3145736 | tf_op jit(solution)/shard_map/ppermute | solution.py:531
  25.1 5.6 %collective-permute-done.3.refs_0_.refs_1_ = bf16[2048,256]{1,0:T(8,128)(2,1)S(1)} collective-permute-done((bf16[2048,256]{1,0:T(8,128)(2,1)}, bf16[2048,256]{1,0:T(8,128)(2,1)S(1)}, u32[]{:S(2)}, u32[]{:S(2)}) %collective-permute-start.3) | collective-permute-done | bytes 1048608 | tf_op jit(solution)/shard_map/ppermute | solution.py:531
  30.7 0.6 relay.4
  31.4 0.9 copy-done.1
  32.3 4.3 %collective-permute-start.4 = (bf16[2048,256]{1,0:T(8,128)(2,1)S(1)}, bf16[2048,256]{1,0:T(8,128)(2,1)S(1)}, u32[]{:S(2)}, u32[]{:S(2)}) collective-permute-start(bf16[2048,256]{1,0:T(8,128)(2,1)S(1)} %relay.4), channel_id=1, source_target_pairs={{0,1},{1,2},{2,3},{5,4},{6,5},{9,10},{10,11},{13,12},{14,13},{15,1... | collective-permute-start | bytes 3145736 | tf_op jit(solution)/shard_map/ppermute | solution.py:531
  36.7 0.0 collective-permute-done.10.refs_1_
  36.7 0.1 collective-permute-start.11
  36.7 1.0 copy-done.8
  37.8 9.8 %collective-permute-done.2.refs_2_.refs_0_ = bf16[2048,256]{1,0:T(8,128)(2,1)S(1)} collective-permute-done((bf16[2048,256]{1,0:T(8,128)(2,1)S(1)}, bf16[2048,256]{1,0:T(8,128)(2,1)S(1)}, u32[]{:S(2)}, u32[]{:S(2)}) %collective-permute-start.2) | collective-permute-done | bytes 1048608 | tf_op jit(solution)/shard_map/ppermute | solution.py:531
  47.6 1.3 %collective-permute-start.5 = (bf16[2048,256]{1,0:T(8,128)(2,1)S(1)}, bf16[2048,256]{1,0:T(8,128)(2,1)}, u32[]{:S(2)}, u32[]{:S(2)}) collective-permute-start(bf16[2048,256]{1,0:T(8,128)(2,1)S(1)} %collective-permute-done.2.refs_2_.refs_0_), channel_id=1, source_target_pairs={{1,0},{5,6},{6,7},{9,8},{14,15},{17,16},{18,17},{21,22},{22,23},{2... | collective-permute-start | bytes 3145736 | tf_op jit(solution)/shard_map/ppermute | solution.py:531
  48.9 0.7 collective-permute-start.7
  49.6 0.0 copy-start.3
  49.6 1.0 copy-done.3
  50.6 2.4 %collective-permute-done.4.refs_0_.refs_3_.refs_1_ = bf16[2048,256]{1,0:T(8,128)(2,1)S(1)} collective-permute-done((bf16[2048,256]{1,0:T(8,128)(2,1)S(1)}, bf16[2048,256]{1,0:T(8,128)(2,1)S(1)}, u32[]{:S(2)}, u32[]{:S(2)}) %collective-permute-start.4) | collective-permute-done | bytes 1048608 | tf_op jit(solution)/shard_map/ppermute | solution.py:531
  53.0 0.6 relay.5
  53.6 1.7 %collective-permute-start.6 = (bf16[2048,256]{1,0:T(8,128)(2,1)S(1)}, bf16[2048,256]{1,0:T(8,128)(2,1)}, u32[]{:S(2)}, u32[]{:S(2)}) collective-permute-start(bf16[2048,256]{1,0:T(8,128)(2,1)S(1)} %relay.5), channel_id=1, source_target_pairs={{1,2},{2,3},{5,4},{9,10},{10,11},{13,12},{14,13},{21,20},{22,21},{... | collective-permute-start | bytes 3145736 | tf_op jit(solution)/shard_map/ppermute | solution.py:531
  55.3 0.0 collective-permute-done.11.refs_2_
  55.3 0.7 collective-permute-start.12
  56.0 14.8 %collective-permute-done.5.refs_5_.refs_2_ = bf16[2048,256]{1,0:T(8,128)(2,1)} collective-permute-done((bf16[2048,256]{1,0:T(8,128)(2,1)S(1)}, bf16[2048,256]{1,0:T(8,128)(2,1)}, u32[]{:S(2)}, u32[]{:S(2)}) %collective-permute-start.5) | collective-permute-done | bytes 1048608 | tf_op jit(solution)/shard_map/ppermute | solution.py:531
  70.8 2.4 %collective-permute-start.14 = (bf16[2048,256]{1,0:T(8,128)(2,1)}, bf16[2048,256]{1,0:T(8,128)(2,1)}, u32[]{:S(2)}, u32[]{:S(2)}) collective-permute-start(bf16[2048,256]{1,0:T(8,128)(2,1)} %collective-permute-done.5.refs_5_.refs_2_), channel_id=1, source_target_pairs={{0,16},{23,3}} | collective-permute-start | bytes 3145736 | tf_op jit(solution)/shard_map/ppermute | solution.py:511
  73.2 0.0 collective-permute-start.13
  73.2 0.0 collective-permute-done.7.refs_4_
  73.2 1.0 copy-done.5
  74.2 1.7 %collective-permute-start.8 = (bf16[2048,256]{1,0:T(8,128)(2,1)}, bf16[2048,256]{1,0:T(8,128)(2,1)}, u32[]{:S(2)}, u32[]{:S(2)}) collective-permute-start(bf16[2048,256]{1,0:T(8,128)(2,1)} %collective-permute-done.5.refs_5_.refs_2_), channel_id=1, source_target_pairs={{6,7},{17,16},{22,23},{25,24},{30,31}} | collective-permute-start | bytes 3145736 | tf_op jit(solution)/shard_map/ppermute | solution.py:531
  75.8 0.0 collective-permute-done.6.refs_6_.refs_3_
  75.8 1.6 %collective-permute-start.9 = (bf16[2048,256]{1,0:T(8,128)(2,1)}, bf16[2048,256]{1,0:T(8,128)(2,1)}, u32[]{:S(2)}, u32[]{:S(2)}) collective-permute-start(bf16[2048,256]{1,0:T(8,128)(2,1)} %collective-permute-done.6.refs_6_.refs_3_), channel_id=1, source_target_pairs={{2,3},{10,11},{13,12},{21,20},{26,27}} | collective-permute-start | bytes 3145736 | tf_op jit(solution)/shard_map/ppermute | solution.py:531
  77.5 0.1 fusion
  77.6 0.0 collective-permute-done.12.refs_3_
  77.6 0.2 broadcast_in_dim.42.refs_4_
  77.8 0.2 broadcast_in_dim.43.refs_5_
  78.0 0.0 copy-start.7
  78.0 1.2 %copy-done.7 = bf16[256,2048]{1,0:T(8,128)(2,1)S(1)} copy-done((bf16[256,2048]{1,0:T(8,128)(2,1)S(1)}, bf16[256,2048]{1,0:T(8,128)(2,1)}, u32[]{:S(2)}) %copy-start.7) | copy-done | bytes 1048600
  79.2 1.2 %copy-done.9 = bf16[256,2048]{1,0:T(8,128)(2,1)S(1)} copy-done((bf16[256,2048]{1,0:T(8,128)(2,1)S(1)}, bf16[256,2048]{1,0:T(8,128)(2,1)}, u32[]{:S(2)}) %copy-start.9) | copy-done | bytes 1048600
  80.4 3.2 %window.1.refs_11_.refs_9_ = bf16[1024,2048]{1,0:T(8,128)(2,1)S(1)} custom-call(s32[21]{0:T(128)S(1)} %fusion.2.table, bf16[256,2048]{1,0:T(8,128)(2,1)S(1)} %copy-done.7, bf16[256,2048]{1,0:T(8,128)(2,1)S(1)} %copy-done.9, bf16[256,2048]{1,0:T(8,128)(2,1)} %collective-permute-done.11.refs_2_, bf16[256,2048]{1,0:T(8,128)(2,1)} %collective-permute-done.12.refs_3_, ...), custom_call_target="tpu_custom_call" | custom-call | flops 8388608 | bytes 8388608 | tf_op jit(solution)/shard_map/window/pallas_call | solution.py:207
  83.7 0.0 collective-permute-done.13
  83.7 6.3 %collective-permute-start.15 = (f32[2048]{0:T(1024)S(1)}, f32[2048]{0:T(1024)S(1)}, u32[]{:S(2)}, u32[]{:S(2)}) collective-permute-start(f32[2048]{0:T(1024)S(1)} %add.39), channel_id=1, source_target_pairs={{0,2},{1,3},{2,0},{3,1},{4,6},{5,7},{6,4},{7,5},{8,10},{9,11},{10,... | collective-permute-start | bytes 24584 | tf_op jit(solution)/shard_map/ppermute | solution.py:492
  90.0 0.0 collective-permute-done.14.refs_7_
  90.0 0.3 broadcast_in_dim.41.refs_10_.refs_8_
  90.3 0.0 copy-done.2
  90.3 0.0 copy-done.4
  90.3 0.0 copy-done.6
  90.3 10.5 %early.1.refs_10_ = f32[2048,2048]{1,0:T(8,128)S(1)} custom-call(s32[21]{0:T(128)S(1)} %fusion.2.table, bf16[2048,512]{1,0:T(8,128)(2,1)S(1)} %copy-done, bf16[2048,256]{1,0:T(8,128)(2,1)} %collective-permute-done.1.refs_1_.refs_0_, bf16[2048,256]{1,0:T(8,128)(2,1)S(1)} %copy-done.2, bf16[2048,256]{1,0:T(8,128)(2,1)S(1)} %copy-done.4, ...), custom_call_target="tpu_custom_call" | custom-call | flops 6442450944 | tf_op jit(solution)/shard_map/early/pallas_call | solution.py:268
  100.8 0.0 collective-permute-done.15
  100.8 0.6 multiply_add_fusion
  101.4 0.0 collective-permute-done.8.refs_4_
  101.4 0.0 collective-permute-done.9.refs_5_
  101.4 7.3 %last.1 = bf16[2048,2048]{1,0:T(8,128)(2,1)} custom-call(s32[21]{0:T(128)S(1)} %fusion.2.table, bf16[2048,512]{1,0:T(8,128)(2,1)S(1)} %copy-done, bf16[2048,256]{1,0:T(8,128)(2,1)S(1)} %copy-done.4, bf16[2048,256]{1,0:T(8,128)(2,1)S(1)} %collective-permute-done.4.refs_0_.refs_3_.refs_1_, bf16[2048,256]{1,0:T(8,128)(2,1)} %collective-permute-done.5.refs_5_.refs_2_, ...), custom_call_target="tpu_custom_call" | custom-call | flops 2147483648 | bytes 8388608 | tf_op jit(solution)/shard_map/last/pallas_call | solution.py:312
  (18 shorter events, 0.0 us)
Async XLA Ops:
  0.6 7.8 %copy-start = (bf16[2048,512]{1,0:T(8,128)(2,1)S(1)}, bf16[2048,512]{1,0:T(8,128)(2,1)}, u32[]{:S(2)}) copy-start(bf16[2048,512]{1,0:T(8,128)(2,1)} %x.9) | copy-start | bytes 6291460
  0.6 7.6 %copy-start.13 = (f32[2048]{0:T(1024)S(1)}, f32[2048]{0:T(1024)}, u32[]{:S(2)}) copy-start(f32[2048]{0:T(1024)} %param.10) | copy-start | bytes 24580
  0.7 7.6 %copy-start.12 = (f32[2048]{0:T(1024)S(1)}, f32[2048]{0:T(1024)}, u32[]{:S(2)}) copy-start(f32[2048]{0:T(1024)} %param.9) | copy-start | bytes 24580
  0.7 7.8 %copy-start.10 = (s32[2048]{0:T(1024)S(1)}, s32[2048]{0:T(1024)}, u32[]{:S(2)}) copy-start(s32[2048]{0:T(1024)} %param.11) | copy-start | bytes 24580
  3.1 19.1 %collective-permute-start.1 = (bf16[2048,256]{1,0:T(8,128)(2,1)}, bf16[2048,256]{1,0:T(8,128)(2,1)}, u32[]{:S(2)}, u32[]{:S(2)}) collective-permute-start(bf16[2048,256]{1,0:T(8,128)(2,1)} %constant_dynamic-slice_fusion.1), channel_id=1, source_target_pairs={{1,0},{5,6},{6,7},{9,8},{10,9},{14,15},{18,17},{19,18},{22,23},{27... | collective-permute-start | bytes 3145736 | tf_op jit(solution)/shard_map/ppermute | solution.py:531
  6.6 11.5 %collective-permute-start = (bf16[2048,256]{1,0:T(8,128)(2,1)}, bf16[2048,256]{1,0:T(8,128)(2,1)}, u32[]{:S(2)}, u32[]{:S(2)}) collective-permute-start(bf16[2048,256]{1,0:T(8,128)(2,1)} %dynamic_slice.32), channel_id=1, source_target_pairs={{18,2},{9,25},{1,21}} | collective-permute-start | bytes 3145736 | tf_op jit(solution)/shard_map/ppermute | solution.py:499
  10.5 20.2 %collective-permute-start.3 = (bf16[2048,256]{1,0:T(8,128)(2,1)}, bf16[2048,256]{1,0:T(8,128)(2,1)S(1)}, u32[]{:S(2)}, u32[]{:S(2)}) collective-permute-start(bf16[2048,256]{1,0:T(8,128)(2,1)} %constant_dynamic-slice_fusion), channel_id=1, source_target_pairs={{0,1},{1,2},{5,4},{10,11},{13,12},{14,13},{18,19},{22,21},{23,22},... | collective-permute-start | bytes 3145736 | tf_op jit(solution)/shard_map/ppermute | solution.py:531
  18.1 18.6 %collective-permute-start.10 = (bf16[256,2048]{1,0:T(8,128)(2,1)}, bf16[256,2048]{1,0:T(8,128)(2,1)S(1)}, u32[]{:S(2)}, u32[]{:S(2)}) collective-permute-start(bf16[256,2048]{1,0:T(8,128)(2,1)} %refs_0_), channel_id=1, source_target_pairs={{0,28},{4,0},{8,4},{12,8},{16,12},{20,16},{24,20},{28,24},{1,29},{... | collective-permute-start | bytes 3145736 | tf_op jit(solution)/shard_map/ppermute | solution.py:504
  23.8 53.7 %copy-start.11 = (s32[2048]{0:T(1024)S(1)}, s32[2048]{0:T(1024)}, u32[]{:S(2)}) copy-start(s32[2048]{0:T(1024)} %param.12) | copy-start | bytes 24580
  23.8 23.8 %collective-permute-start.2 = (bf16[2048,256]{1,0:T(8,128)(2,1)S(1)}, bf16[2048,256]{1,0:T(8,128)(2,1)S(1)}, u32[]{:S(2)}, u32[]{:S(2)}) collective-permute-start(bf16[2048,256]{1,0:T(8,128)(2,1)S(1)} %relay.3), channel_id=1, source_target_pairs={{1,0},{2,1},{4,5},{5,6},{6,7},{9,8},{10,9},{13,14},{14,15},{17,16}... | collective-permute-start | bytes 3145736 | tf_op jit(solution)/shard_map/ppermute | solution.py:531
  31.4 1.0 copy-start.1
  32.3 20.7 %collective-permute-start.4 = (bf16[2048,256]{1,0:T(8,128)(2,1)S(1)}, bf16[2048,256]{1,0:T(8,128)(2,1)S(1)}, u32[]{:S(2)}, u32[]{:S(2)}) collective-permute-start(bf16[2048,256]{1,0:T(8,128)(2,1)S(1)} %relay.4), channel_id=1, source_target_pairs={{0,1},{1,2},{2,3},{5,4},{6,5},{9,10},{10,11},{13,12},{14,13},{15,1... | collective-permute-start | bytes 3145736 | tf_op jit(solution)/shard_map/ppermute | solution.py:531
  36.7 18.6 %collective-permute-start.11 = (bf16[256,2048]{1,0:T(8,128)(2,1)S(1)}, bf16[256,2048]{1,0:T(8,128)(2,1)}, u32[]{:S(2)}, u32[]{:S(2)}) collective-permute-start(bf16[256,2048]{1,0:T(8,128)(2,1)S(1)} %collective-permute-done.10.refs_1_), channel_id=1, source_target_pairs={{0,28},{4,0},{8,4},{12,8},{16,12},{20,16},{24,20},{28,24},{1,29},{... | collective-permute-start | bytes 3145736 | tf_op jit(solution)/shard_map/ppermute | solution.py:504
  36.7 1.1 copy-start.8
  47.6 23.2 %collective-permute-start.5 = (bf16[2048,256]{1,0:T(8,128)(2,1)S(1)}, bf16[2048,256]{1,0:T(8,128)(2,1)}, u32[]{:S(2)}, u32[]{:S(2)}) collective-permute-start(bf16[2048,256]{1,0:T(8,128)(2,1)S(1)} %collective-permute-done.2.refs_2_.refs_0_), channel_id=1, source_target_pairs={{1,0},{5,6},{6,7},{9,8},{14,15},{17,16},{18,17},{21,22},{22,23},{2... | collective-permute-start | bytes 3145736 | tf_op jit(solution)/shard_map/ppermute | solution.py:531
  48.9 24.3 %collective-permute-start.7 = (bf16[2048,256]{1,0:T(8,128)(2,1)S(1)}, bf16[2048,256]{1,0:T(8,128)(2,1)S(1)}, u32[]{:S(2)}, u32[]{:S(2)}) collective-permute-start(bf16[2048,256]{1,0:T(8,128)(2,1)S(1)} %collective-permute-done.2.refs_2_.refs_0_), channel_id=1, source_target_pairs={{1,17},{24,8},{22,2}} | collective-permute-start | bytes 3145736 | tf_op jit(solution)/shard_map/ppermute | solution.py:511
  49.6 1.0 copy-start.3
  53.6 22.2 %collective-permute-start.6 = (bf16[2048,256]{1,0:T(8,128)(2,1)S(1)}, bf16[2048,256]{1,0:T(8,128)(2,1)}, u32[]{:S(2)}, u32[]{:S(2)}) collective-permute-start(bf16[2048,256]{1,0:T(8,128)(2,1)S(1)} %relay.5), channel_id=1, source_target_pairs={{1,2},{2,3},{5,4},{9,10},{10,11},{13,12},{14,13},{21,20},{22,21},{... | collective-permute-start | bytes 3145736 | tf_op jit(solution)/shard_map/ppermute | solution.py:531
  55.3 22.3 %collective-permute-start.12 = (bf16[256,2048]{1,0:T(8,128)(2,1)}, bf16[256,2048]{1,0:T(8,128)(2,1)}, u32[]{:S(2)}, u32[]{:S(2)}) collective-permute-start(bf16[256,2048]{1,0:T(8,128)(2,1)} %collective-permute-done.11.refs_2_), channel_id=1, source_target_pairs={{0,28},{4,0},{8,4},{12,8},{16,12},{20,16},{24,20},{28,24},{1,29},{... | collective-permute-start | bytes 3145736 | tf_op jit(solution)/shard_map/ppermute | solution.py:504
  70.8 19.2 %collective-permute-start.14 = (bf16[2048,256]{1,0:T(8,128)(2,1)}, bf16[2048,256]{1,0:T(8,128)(2,1)}, u32[]{:S(2)}, u32[]{:S(2)}) collective-permute-start(bf16[2048,256]{1,0:T(8,128)(2,1)} %collective-permute-done.5.refs_5_.refs_2_), channel_id=1, source_target_pairs={{0,16},{23,3}} | collective-permute-start | bytes 3145736 | tf_op jit(solution)/shard_map/ppermute | solution.py:511
  73.2 10.5 %collective-permute-start.13 = (f32[2048]{0:T(1024)S(1)}, f32[2048]{0:T(1024)S(1)}, u32[]{:S(2)}, u32[]{:S(2)}) collective-permute-start(f32[2048]{0:T(1024)S(1)} %multiply_reduce_fusion), channel_id=1, source_target_pairs={{0,1},{1,0},{2,3},{3,2},{4,5},{5,4},{6,7},{7,6},{8,9},{9,8},{10,11... | collective-permute-start | bytes 24584 | tf_op jit(solution)/shard_map/ppermute | solution.py:492
  73.2 1.0 copy-start.5
  74.2 27.3 %collective-permute-start.8 = (bf16[2048,256]{1,0:T(8,128)(2,1)}, bf16[2048,256]{1,0:T(8,128)(2,1)}, u32[]{:S(2)}, u32[]{:S(2)}) collective-permute-start(bf16[2048,256]{1,0:T(8,128)(2,1)} %collective-permute-done.5.refs_5_.refs_2_), channel_id=1, source_target_pairs={{6,7},{17,16},{22,23},{25,24},{30,31}} | collective-permute-start | bytes 3145736 | tf_op jit(solution)/shard_map/ppermute | solution.py:531
  75.8 25.6 %collective-permute-start.9 = (bf16[2048,256]{1,0:T(8,128)(2,1)}, bf16[2048,256]{1,0:T(8,128)(2,1)}, u32[]{:S(2)}, u32[]{:S(2)}) collective-permute-start(bf16[2048,256]{1,0:T(8,128)(2,1)} %collective-permute-done.6.refs_6_.refs_3_), channel_id=1, source_target_pairs={{2,3},{10,11},{13,12},{21,20},{26,27}} | collective-permute-start | bytes 3145736 | tf_op jit(solution)/shard_map/ppermute | solution.py:531
  78.0 1.2 %copy-start.7 = (bf16[256,2048]{1,0:T(8,128)(2,1)S(1)}, bf16[256,2048]{1,0:T(8,128)(2,1)}, u32[]{:S(2)}) copy-start(bf16[256,2048]{1,0:T(8,128)(2,1)} %refs_0_) | copy-start | bytes 3145732
  79.2 1.2 %copy-start.9 = (bf16[256,2048]{1,0:T(8,128)(2,1)S(1)}, bf16[256,2048]{1,0:T(8,128)(2,1)}, u32[]{:S(2)}) copy-start(bf16[256,2048]{1,0:T(8,128)(2,1)} %copy-done.8) | copy-start | bytes 3145732
  80.4 9.9 %copy-start.2 = (bf16[2048,256]{1,0:T(8,128)(2,1)S(1)}, bf16[2048,256]{1,0:T(8,128)(2,1)}, u32[]{:S(2)}) copy-start(bf16[2048,256]{1,0:T(8,128)(2,1)} %copy-done.1) | copy-start | bytes 3145732
  80.4 9.9 %copy-start.4 = (bf16[2048,256]{1,0:T(8,128)(2,1)S(1)}, bf16[2048,256]{1,0:T(8,128)(2,1)}, u32[]{:S(2)}) copy-start(bf16[2048,256]{1,0:T(8,128)(2,1)} %copy-done.3) | copy-start | bytes 3145732
  80.4 9.9 %copy-start.6 = (bf16[2048,256]{1,0:T(8,128)(2,1)S(1)}, bf16[2048,256]{1,0:T(8,128)(2,1)}, u32[]{:S(2)}) copy-start(bf16[2048,256]{1,0:T(8,128)(2,1)} %copy-done.5) | copy-start | bytes 3145732
  83.7 17.1 %collective-permute-start.15 = (f32[2048]{0:T(1024)S(1)}, f32[2048]{0:T(1024)S(1)}, u32[]{:S(2)}, u32[]{:S(2)}) collective-permute-start(f32[2048]{0:T(1024)S(1)} %add.39), channel_id=1, source_target_pairs={{0,2},{1,3},{2,0},{3,1},{4,6},{5,7},{6,4},{7,5},{8,10},{9,11},{10,... | collective-permute-start | bytes 24584 | tf_op jit(solution)/shard_map/ppermute | solution.py:492

commit v22 on v21

--- a/solution.py
+++ b/solution.py
@@ -13,7 +13,7 @@
 PIECES = 1
 DEPTH = 1
 HOP = 1
-COL_TILE = 512
+COL_TILE = 1024
 ROW_BLOCK = 512
 EARLY_BLOCK = 1024
 ROW_TILE = 32

time: 109 us -> 109 us (level)
  no operation moved by 1% of the time
where the time goes in v22:
time: 109 us
  waiting for transfers between devices  36 us (33%)
  starting transfers between devices  32.5 us (30%)
  Pallas kernels  23.9 us (22%)
  local copies, waits for them, and re-layouts  13.7 us (13%)
  other arithmetic  1.73 us (2%)
    ppermute x8, waiting for transfers between devices, local(): buffers[key] = lax.ppermute(held, both, pairs_of[key])  35.9 us
    ppermute x8, starting transfers between devices, local(): buffers[key] = lax.ppermute(held, both, pairs_of[key])  20.7 us
    pallas_call x1, Pallas kernels, early_product(): pl.pallas_call(functools.partial(early_kernel, at, candidates, len(buffer...  10.5 us
    pallas_call x1, Pallas kernels, last_product(): pl.pallas_call(functools.partial(last_kernel, at, candidates, scale, len(...  7.3 us
    unnamed x28, local copies, waits for them, and re-layouts  6.41 us
    ppermute x2, starting transfers between devices, sum_beside(): other = lax.ppermute(squares, 'col', [(i, i ^ bit) for i in range(cols)])  6.29 us
    dynamic_slice x3, local copies, waits for them, and re-layouts, own_chunk(): lax.dynamic_slice(x, (piece * piece_rows, group * group_size), (piece_row...  5.69 us
    pallas_call x1, Pallas kernels, standardized_window(): pl.pallas_call(functools.partial(window_kernel, at), out_shape=pltpu.VMEM...  3.23 us
  transfers between devices with their start and end apart: 16, of which 5 were waited for; matrix products, arithmetic and copies ran while one was open for 6% of the time, Pallas kernels for 15%

profile of v22, /device:TPU:0, one launch (start us, length us, event | category | flops | bytes accessed | tf_op | source)
XLA Modules:
  0.0 108.7 jit_solution(13228874729552641093)
XLA Ops:
  0.6 0.0 copy-start
  0.6 0.0 copy-start.13
  0.7 0.0 copy-start.12
  0.7 2.4 %constant_dynamic-slice_fusion.1 = bf16[2048,256]{1,0:T(8,128)(2,1)} fusion(bf16[2048,512]{1,0:T(8,128)(2,1)} %x.9, s32[]{:T(128)S(6)} %select_n.35), kind=kLoop, calls=%fused_computation.14 | loop fusion | bytes 2097156 | tf_op jit(solution)/shard_map/dynamic_slice | solution.py:450
  3.1 1.3 %collective-permute-start.1 = (bf16[2048,256]{1,0:T(8,128)(2,1)}, bf16[2048,256]{1,0:T(8,128)(2,1)}, u32[]{:S(2)}, u32[]{:S(2)}) collective-permute-start(bf16[2048,256]{1,0:T(8,128)(2,1)} %constant_dynamic-slice_fusion.1), channel_id=1, source_target_pairs={{1,0},{5,6},{6,7},{9,8},{10,9},{14,15},{18,17},{19,18},{22,23},{27... | collective-permute-start | bytes 3145736 | tf_op jit(solution)/shard_map/ppermute | solution.py:531
  4.4 2.3 %dynamic_slice.32 = bf16[2048,256]{1,0:T(8,128)(2,1)} slice(bf16[2048,512]{1,0:T(8,128)(2,1)} %x.9), slice={[0:2048], [256:512]} | slice | bytes 2097152 | tf_op jit(solution)/shard_map/dynamic_slice | solution.py:450
  6.6 1.6 %collective-permute-start = (bf16[2048,256]{1,0:T(8,128)(2,1)}, bf16[2048,256]{1,0:T(8,128)(2,1)}, u32[]{:S(2)}, u32[]{:S(2)}) collective-permute-start(bf16[2048,256]{1,0:T(8,128)(2,1)} %dynamic_slice.32), channel_id=1, source_target_pairs={{18,2},{9,25},{1,21}} | collective-permute-start | bytes 3145736 | tf_op jit(solution)/shard_map/ppermute | solution.py:499
  8.3 0.0 copy-done.13
  8.3 0.1 dynamic_slice.27
  8.4 0.1 dynamic_slice.28
  8.5 0.0 copy-done
  8.5 1.0 multiply_reduce_fusion
  9.5 1.0 constant_dynamic-slice_fusion
  10.5 7.5 %collective-permute-start.3 = (bf16[2048,256]{1,0:T(8,128)(2,1)}, bf16[2048,256]{1,0:T(8,128)(2,1)S(1)}, u32[]{:S(2)}, u32[]{:S(2)}) collective-permute-start(bf16[2048,256]{1,0:T(8,128)(2,1)} %constant_dynamic-slice_fusion), channel_id=1, source_target_pairs={{0,1},{1,2},{5,4},{10,11},{13,12},{14,13},{18,19},{22,21},{23,22},... | collective-permute-start | bytes 3145736 | tf_op jit(solution)/shard_map/ppermute | solution.py:531
  18.1 0.0 collective-permute-done.refs_0_
  18.1 0.1 collective-permute-start.10
  18.2 0.7 fusion.2.table
  18.9 3.3 %collective-permute-done.1.refs_1_.refs_0_ = bf16[2048,256]{1,0:T(8,128)(2,1)} collective-permute-done((bf16[2048,256]{1,0:T(8,128)(2,1)}, bf16[2048,256]{1,0:T(8,128)(2,1)}, u32[]{:S(2)}, u32[]{:S(2)}) %collective-permute-start.1) | collective-permute-done | bytes 1048608 | tf_op jit(solution)/shard_map/ppermute | solution.py:531
  22.1 1.6 %relay.3 = bf16[2048,256]{1,0:T(8,128)(2,1)S(1)} custom-call(s32[21]{0:T(128)S(1)} %fusion.2.table, bf16[2048,512]{1,0:T(8,128)(2,1)S(1)} %copy-done, bf16[2048,256]{1,0:T(8,128)(2,1)} %collective-permute-done.refs_0_, bf16[2048,256]{1,0:T(8,128)(2,1)} %collective-permute-done.1.refs_1_.refs_0_), custom_call_target="tpu_custom_call" | custom-call | tf_op jit(solution)/shard_map/relay/pallas_call | solution.py:169
  23.8 0.0 copy-start.11
  23.8 1.3 %collective-permute-start.2 = (bf16[2048,256]{1,0:T(8,128)(2,1)S(1)}, bf16[2048,256]{1,0:T(8,128)(2,1)S(1)}, u32[]{:S(2)}, u32[]{:S(2)}) collective-permute-start(bf16[2048,256]{1,0:T(8,128)(2,1)S(1)} %relay.3), channel_id=1, source_target_pairs={{1,0},{2,1},{4,5},{5,6},{6,7},{9,8},{10,9},{13,14},{14,15},{17,16}... | collective-permute-start | bytes 3145736 | tf_op jit(solution)/shard_map/ppermute | solution.py:531
  25.1 5.6 %collective-permute-done.3.refs_0_.refs_1_ = bf16[2048,256]{1,0:T(8,128)(2,1)S(1)} collective-permute-done((bf16[2048,256]{1,0:T(8,128)(2,1)}, bf16[2048,256]{1,0:T(8,128)(2,1)S(1)}, u32[]{:S(2)}, u32[]{:S(2)}) %collective-permute-start.3) | collective-permute-done | bytes 1048608 | tf_op jit(solution)/shard_map/ppermute | solution.py:531
  30.7 0.6 relay.4
  31.4 0.9 copy-done.1
  32.3 4.3 %collective-permute-start.4 = (bf16[2048,256]{1,0:T(8,128)(2,1)S(1)}, bf16[2048,256]{1,0:T(8,128)(2,1)S(1)}, u32[]{:S(2)}, u32[]{:S(2)}) collective-permute-start(bf16[2048,256]{1,0:T(8,128)(2,1)S(1)} %relay.4), channel_id=1, source_target_pairs={{0,1},{1,2},{2,3},{5,4},{6,5},{9,10},{10,11},{13,12},{14,13},{15,1... | collective-permute-start | bytes 3145736 | tf_op jit(solution)/shard_map/ppermute | solution.py:531
  36.7 0.0 collective-permute-done.10.refs_1_
  36.7 0.1 collective-permute-start.11
  36.7 1.0 copy-done.8
  37.8 9.8 %collective-permute-done.2.refs_2_.refs_0_ = bf16[2048,256]{1,0:T(8,128)(2,1)S(1)} collective-permute-done((bf16[2048,256]{1,0:T(8,128)(2,1)S(1)}, bf16[2048,256]{1,0:T(8,128)(2,1)S(1)}, u32[]{:S(2)}, u32[]{:S(2)}) %collective-permute-start.2) | collective-permute-done | bytes 1048608 | tf_op jit(solution)/shard_map/ppermute | solution.py:531
  47.6 1.3 %collective-permute-start.5 = (bf16[2048,256]{1,0:T(8,128)(2,1)S(1)}, bf16[2048,256]{1,0:T(8,128)(2,1)}, u32[]{:S(2)}, u32[]{:S(2)}) collective-permute-start(bf16[2048,256]{1,0:T(8,128)(2,1)S(1)} %collective-permute-done.2.refs_2_.refs_0_), channel_id=1, source_target_pairs={{1,0},{5,6},{6,7},{9,8},{14,15},{17,16},{18,17},{21,22},{22,23},{2... | collective-permute-start | bytes 3145736 | tf_op jit(solution)/shard_map/ppermute | solution.py:531
  48.9 0.7 collective-permute-start.7
  49.6 0.0 copy-start.3
  49.6 1.0 copy-done.3
  50.6 2.4 %collective-permute-done.4.refs_0_.refs_3_.refs_1_ = bf16[2048,256]{1,0:T(8,128)(2,1)S(1)} collective-permute-done((bf16[2048,256]{1,0:T(8,128)(2,1)S(1)}, bf16[2048,256]{1,0:T(8,128)(2,1)S(1)}, u32[]{:S(2)}, u32[]{:S(2)}) %collective-permute-start.4) | collective-permute-done | bytes 1048608 | tf_op jit(solution)/shard_map/ppermute | solution.py:531
  53.0 0.6 relay.5
  53.6 1.7 %collective-permute-start.6 = (bf16[2048,256]{1,0:T(8,128)(2,1)S(1)}, bf16[2048,256]{1,0:T(8,128)(2,1)}, u32[]{:S(2)}, u32[]{:S(2)}) collective-permute-start(bf16[2048,256]{1,0:T(8,128)(2,1)S(1)} %relay.5), channel_id=1, source_target_pairs={{1,2},{2,3},{5,4},{9,10},{10,11},{13,12},{14,13},{21,20},{22,21},{... | collective-permute-start | bytes 3145736 | tf_op jit(solution)/shard_map/ppermute | solution.py:531
  55.3 0.0 collective-permute-done.11.refs_2_
  55.3 0.7 collective-permute-start.12
  56.0 14.8 %collective-permute-done.5.refs_5_.refs_2_ = bf16[2048,256]{1,0:T(8,128)(2,1)} collective-permute-done((bf16[2048,256]{1,0:T(8,128)(2,1)S(1)}, bf16[2048,256]{1,0:T(8,128)(2,1)}, u32[]{:S(2)}, u32[]{:S(2)}) %collective-permute-start.5) | collective-permute-done | bytes 1048608 | tf_op jit(solution)/shard_map/ppermute | solution.py:531
  70.8 2.4 %collective-permute-start.14 = (bf16[2048,256]{1,0:T(8,128)(2,1)}, bf16[2048,256]{1,0:T(8,128)(2,1)}, u32[]{:S(2)}, u32[]{:S(2)}) collective-permute-start(bf16[2048,256]{1,0:T(8,128)(2,1)} %collective-permute-done.5.refs_5_.refs_2_), channel_id=1, source_target_pairs={{0,16},{23,3}} | collective-permute-start | bytes 3145736 | tf_op jit(solution)/shard_map/ppermute | solution.py:511
  73.2 0.0 collective-permute-start.13
  73.2 0.0 collective-permute-done.7.refs_4_
  73.2 1.0 copy-done.5
  74.2 1.7 %collective-permute-start.8 = (bf16[2048,256]{1,0:T(8,128)(2,1)}, bf16[2048,256]{1,0:T(8,128)(2,1)}, u32[]{:S(2)}, u32[]{:S(2)}) collective-permute-start(bf16[2048,256]{1,0:T(8,128)(2,1)} %collective-permute-done.5.refs_5_.refs_2_), channel_id=1, source_target_pairs={{6,7},{17,16},{22,23},{25,24},{30,31}} | collective-permute-start | bytes 3145736 | tf_op jit(solution)/shard_map/ppermute | solution.py:531
  75.8 0.0 collective-permute-done.6.refs_6_.refs_3_
  75.8 1.6 %collective-permute-start.9 = (bf16[2048,256]{1,0:T(8,128)(2,1)}, bf16[2048,256]{1,0:T(8,128)(2,1)}, u32[]{:S(2)}, u32[]{:S(2)}) collective-permute-start(bf16[2048,256]{1,0:T(8,128)(2,1)} %collective-permute-done.6.refs_6_.refs_3_), channel_id=1, source_target_pairs={{2,3},{10,11},{13,12},{21,20},{26,27}} | collective-permute-start | bytes 3145736 | tf_op jit(solution)/shard_map/ppermute | solution.py:531
  77.5 0.1 fusion
  77.6 0.0 collective-permute-done.12.refs_3_
  77.6 0.2 broadcast_in_dim.42.refs_4_
  77.8 0.2 broadcast_in_dim.43.refs_5_
  78.0 0.0 copy-start.7
  78.0 1.2 %copy-done.7 = bf16[256,2048]{1,0:T(8,128)(2,1)S(1)} copy-done((bf16[256,2048]{1,0:T(8,128)(2,1)S(1)}, bf16[256,2048]{1,0:T(8,128)(2,1)}, u32[]{:S(2)}) %copy-start.7) | copy-done | bytes 1048600
  79.2 1.2 %copy-done.9 = bf16[256,2048]{1,0:T(8,128)(2,1)S(1)} copy-done((bf16[256,2048]{1,0:T(8,128)(2,1)S(1)}, bf16[256,2048]{1,0:T(8,128)(2,1)}, u32[]{:S(2)}) %copy-start.9) | copy-done | bytes 1048600
  80.4 3.2 %window.1.refs_11_.refs_9_ = bf16[1024,2048]{1,0:T(8,128)(2,1)S(1)} custom-call(s32[21]{0:T(128)S(1)} %fusion.2.table, bf16[256,2048]{1,0:T(8,128)(2,1)S(1)} %copy-done.7, bf16[256,2048]{1,0:T(8,128)(2,1)S(1)} %copy-done.9, bf16[256,2048]{1,0:T(8,128)(2,1)} %collective-permute-done.11.refs_2_, bf16[256,2048]{1,0:T(8,128)(2,1)} %collective-permute-done.12.refs_3_, ...), custom_call_target="tpu_custom_call" | custom-call | flops 8388608 | bytes 8388608 | tf_op jit(solution)/shard_map/window/pallas_call | solution.py:207
  83.7 0.0 collective-permute-done.13
  83.7 6.3 %collective-permute-start.15 = (f32[2048]{0:T(1024)S(1)}, f32[2048]{0:T(1024)S(1)}, u32[]{:S(2)}, u32[]{:S(2)}) collective-permute-start(f32[2048]{0:T(1024)S(1)} %add.39), channel_id=1, source_target_pairs={{0,2},{1,3},{2,0},{3,1},{4,6},{5,7},{6,4},{7,5},{8,10},{9,11},{10,... | collective-permute-start | bytes 24584 | tf_op jit(solution)/shard_map/ppermute | solution.py:492
  90.0 0.0 collective-permute-done.14.refs_7_
  90.0 0.3 broadcast_in_dim.41.refs_10_.refs_8_
  90.3 10.5 %early.1.refs_10_ = f32[2048,2048]{1,0:T(8,128)S(1)} custom-call(s32[21]{0:T(128)S(1)} %fusion.2.table, bf16[2048,512]{1,0:T(8,128)(2,1)S(1)} %copy-done, bf16[2048,256]{1,0:T(8,128)(2,1)} %collective-permute-done.1.refs_1_.refs_0_, bf16[2048,256]{1,0:T(8,128)(2,1)S(1)} %copy-done.2, bf16[2048,256]{1,0:T(8,128)(2,1)S(1)} %copy-done.4, ...), custom_call_target="tpu_custom_call" | custom-call | flops 6442450944 | tf_op jit(solution)/shard_map/early/pallas_call | solution.py:268
  100.8 0.0 collective-permute-done.15
  100.8 0.6 multiply_add_fusion
  101.4 0.0 collective-permute-done.8.refs_4_
  101.4 0.0 collective-permute-done.9.refs_5_
  101.4 7.3 %last.1 = bf16[2048,2048]{1,0:T(8,128)(2,1)} custom-call(s32[21]{0:T(128)S(1)} %fusion.2.table, bf16[2048,512]{1,0:T(8,128)(2,1)S(1)} %copy-done, bf16[2048,256]{1,0:T(8,128)(2,1)S(1)} %copy-done.4, bf16[2048,256]{1,0:T(8,128)(2,1)S(1)} %collective-permute-done.4.refs_0_.refs_3_.refs_1_, bf16[2048,256]{1,0:T(8,128)(2,1)} %collective-permute-done.5.refs_5_.refs_2_, ...), custom_call_target="tpu_custom_call" | custom-call | flops 2147483648 | bytes 8388608 | tf_op jit(solution)/shard_map/last/pallas_call | solution.py:312
  (18 shorter events, 0.0 us)
Async XLA Ops:
  0.6 7.8 %copy-start = (bf16[2048,512]{1,0:T(8,128)(2,1)S(1)}, bf16[2048,512]{1,0:T(8,128)(2,1)}, u32[]{:S(2)}) copy-start(bf16[2048,512]{1,0:T(8,128)(2,1)} %x.9) | copy-start | bytes 6291460
  0.6 7.6 %copy-start.13 = (f32[2048]{0:T(1024)S(1)}, f32[2048]{0:T(1024)}, u32[]{:S(2)}) copy-start(f32[2048]{0:T(1024)} %param.10) | copy-start | bytes 24580
  0.7 7.6 %copy-start.12 = (f32[2048]{0:T(1024)S(1)}, f32[2048]{0:T(1024)}, u32[]{:S(2)}) copy-start(f32[2048]{0:T(1024)} %param.9) | copy-start | bytes 24580
  0.7 7.8 %copy-start.10 = (s32[2048]{0:T(1024)S(1)}, s32[2048]{0:T(1024)}, u32[]{:S(2)}) copy-start(s32[2048]{0:T(1024)} %param.11) | copy-start | bytes 24580
  3.1 19.1 %collective-permute-start.1 = (bf16[2048,256]{1,0:T(8,128)(2,1)}, bf16[2048,256]{1,0:T(8,128)(2,1)}, u32[]{:S(2)}, u32[]{:S(2)}) collective-permute-start(bf16[2048,256]{1,0:T(8,128)(2,1)} %constant_dynamic-slice_fusion.1), channel_id=1, source_target_pairs={{1,0},{5,6},{6,7},{9,8},{10,9},{14,15},{18,17},{19,18},{22,23},{27... | collective-permute-start | bytes 3145736 | tf_op jit(solution)/shard_map/ppermute | solution.py:531
  6.6 11.5 %collective-permute-start = (bf16[2048,256]{1,0:T(8,128)(2,1)}, bf16[2048,256]{1,0:T(8,128)(2,1)}, u32[]{:S(2)}, u32[]{:S(2)}) collective-permute-start(bf16[2048,256]{1,0:T(8,128)(2,1)} %dynamic_slice.32), channel_id=1, source_target_pairs={{18,2},{9,25},{1,21}} | collective-permute-start | bytes 3145736 | tf_op jit(solution)/shard_map/ppermute | solution.py:499
  10.5 20.2 %collective-permute-start.3 = (bf16[2048,256]{1,0:T(8,128)(2,1)}, bf16[2048,256]{1,0:T(8,128)(2,1)S(1)}, u32[]{:S(2)}, u32[]{:S(2)}) collective-permute-start(bf16[2048,256]{1,0:T(8,128)(2,1)} %constant_dynamic-slice_fusion), channel_id=1, source_target_pairs={{0,1},{1,2},{5,4},{10,11},{13,12},{14,13},{18,19},{22,21},{23,22},... | collective-permute-start | bytes 3145736 | tf_op jit(solution)/shard_map/ppermute | solution.py:531
  18.1 18.6 %collective-permute-start.10 = (bf16[256,2048]{1,0:T(8,128)(2,1)}, bf16[256,2048]{1,0:T(8,128)(2,1)S(1)}, u32[]{:S(2)}, u32[]{:S(2)}) collective-permute-start(bf16[256,2048]{1,0:T(8,128)(2,1)} %refs_0_), channel_id=1, source_target_pairs={{0,28},{4,0},{8,4},{12,8},{16,12},{20,16},{24,20},{28,24},{1,29},{... | collective-permute-start | bytes 3145736 | tf_op jit(solution)/shard_map/ppermute | solution.py:504
  23.8 53.7 %copy-start.11 = (s32[2048]{0:T(1024)S(1)}, s32[2048]{0:T(1024)}, u32[]{:S(2)}) copy-start(s32[2048]{0:T(1024)} %param.12) | copy-start | bytes 24580
  23.8 23.8 %collective-permute-start.2 = (bf16[2048,256]{1,0:T(8,128)(2,1)S(1)}, bf16[2048,256]{1,0:T(8,128)(2,1)S(1)}, u32[]{:S(2)}, u32[]{:S(2)}) collective-permute-start(bf16[2048,256]{1,0:T(8,128)(2,1)S(1)} %relay.3), channel_id=1, source_target_pairs={{1,0},{2,1},{4,5},{5,6},{6,7},{9,8},{10,9},{13,14},{14,15},{17,16}... | collective-permute-start | bytes 3145736 | tf_op jit(solution)/shard_map/ppermute | solution.py:531
  31.4 1.0 copy-start.1
  32.3 20.7 %collective-permute-start.4 = (bf16[2048,256]{1,0:T(8,128)(2,1)S(1)}, bf16[2048,256]{1,0:T(8,128)(2,1)S(1)}, u32[]{:S(2)}, u32[]{:S(2)}) collective-permute-start(bf16[2048,256]{1,0:T(8,128)(2,1)S(1)} %relay.4), channel_id=1, source_target_pairs={{0,1},{1,2},{2,3},{5,4},{6,5},{9,10},{10,11},{13,12},{14,13},{15,1... | collective-permute-start | bytes 3145736 | tf_op jit(solution)/shard_map/ppermute | solution.py:531
  36.7 18.6 %collective-permute-start.11 = (bf16[256,2048]{1,0:T(8,128)(2,1)S(1)}, bf16[256,2048]{1,0:T(8,128)(2,1)}, u32[]{:S(2)}, u32[]{:S(2)}) collective-permute-start(bf16[256,2048]{1,0:T(8,128)(2,1)S(1)} %collective-permute-done.10.refs_1_), channel_id=1, source_target_pairs={{0,28},{4,0},{8,4},{12,8},{16,12},{20,16},{24,20},{28,24},{1,29},{... | collective-permute-start | bytes 3145736 | tf_op jit(solution)/shard_map/ppermute | solution.py:504
  36.7 1.1 copy-start.8
  47.6 23.2 %collective-permute-start.5 = (bf16[2048,256]{1,0:T(8,128)(2,1)S(1)}, bf16[2048,256]{1,0:T(8,128)(2,1)}, u32[]{:S(2)}, u32[]{:S(2)}) collective-permute-start(bf16[2048,256]{1,0:T(8,128)(2,1)S(1)} %collective-permute-done.2.refs_2_.refs_0_), channel_id=1, source_target_pairs={{1,0},{5,6},{6,7},{9,8},{14,15},{17,16},{18,17},{21,22},{22,23},{2... | collective-permute-start | bytes 3145736 | tf_op jit(solution)/shard_map/ppermute | solution.py:531
  48.9 24.3 %collective-permute-start.7 = (bf16[2048,256]{1,0:T(8,128)(2,1)S(1)}, bf16[2048,256]{1,0:T(8,128)(2,1)S(1)}, u32[]{:S(2)}, u32[]{:S(2)}) collective-permute-start(bf16[2048,256]{1,0:T(8,128)(2,1)S(1)} %collective-permute-done.2.refs_2_.refs_0_), channel_id=1, source_target_pairs={{1,17},{24,8},{22,2}} | collective-permute-start | bytes 3145736 | tf_op jit(solution)/shard_map/ppermute | solution.py:511
  49.6 1.0 copy-start.3
  53.6 22.2 %collective-permute-start.6 = (bf16[2048,256]{1,0:T(8,128)(2,1)S(1)}, bf16[2048,256]{1,0:T(8,128)(2,1)}, u32[]{:S(2)}, u32[]{:S(2)}) collective-permute-start(bf16[2048,256]{1,0:T(8,128)(2,1)S(1)} %relay.5), channel_id=1, source_target_pairs={{1,2},{2,3},{5,4},{9,10},{10,11},{13,12},{14,13},{21,20},{22,21},{... | collective-permute-start | bytes 3145736 | tf_op jit(solution)/shard_map/ppermute | solution.py:531
  55.3 22.3 %collective-permute-start.12 = (bf16[256,2048]{1,0:T(8,128)(2,1)}, bf16[256,2048]{1,0:T(8,128)(2,1)}, u32[]{:S(2)}, u32[]{:S(2)}) collective-permute-start(bf16[256,2048]{1,0:T(8,128)(2,1)} %collective-permute-done.11.refs_2_), channel_id=1, source_target_pairs={{0,28},{4,0},{8,4},{12,8},{16,12},{20,16},{24,20},{28,24},{1,29},{... | collective-permute-start | bytes 3145736 | tf_op jit(solution)/shard_map/ppermute | solution.py:504
  70.8 19.2 %collective-permute-start.14 = (bf16[2048,256]{1,0:T(8,128)(2,1)}, bf16[2048,256]{1,0:T(8,128)(2,1)}, u32[]{:S(2)}, u32[]{:S(2)}) collective-permute-start(bf16[2048,256]{1,0:T(8,128)(2,1)} %collective-permute-done.5.refs_5_.refs_2_), channel_id=1, source_target_pairs={{0,16},{23,3}} | collective-permute-start | bytes 3145736 | tf_op jit(solution)/shard_map/ppermute | solution.py:511
  73.2 10.5 %collective-permute-start.13 = (f32[2048]{0:T(1024)S(1)}, f32[2048]{0:T(1024)S(1)}, u32[]{:S(2)}, u32[]{:S(2)}) collective-permute-start(f32[2048]{0:T(1024)S(1)} %multiply_reduce_fusion), channel_id=1, source_target_pairs={{0,1},{1,0},{2,3},{3,2},{4,5},{5,4},{6,7},{7,6},{8,9},{9,8},{10,11... | collective-permute-start | bytes 24584 | tf_op jit(solution)/shard_map/ppermute | solution.py:492
  73.2 1.0 copy-start.5
  74.2 27.3 %collective-permute-start.8 = (bf16[2048,256]{1,0:T(8,128)(2,1)}, bf16[2048,256]{1,0:T(8,128)(2,1)}, u32[]{:S(2)}, u32[]{:S(2)}) collective-permute-start(bf16[2048,256]{1,0:T(8,128)(2,1)} %collective-permute-done.5.refs_5_.refs_2_), channel_id=1, source_target_pairs={{6,7},{17,16},{22,23},{25,24},{30,31}} | collective-permute-start | bytes 3145736 | tf_op jit(solution)/shard_map/ppermute | solution.py:531
  75.8 25.6 %collective-permute-start.9 = (bf16[2048,256]{1,0:T(8,128)(2,1)}, bf16[2048,256]{1,0:T(8,128)(2,1)}, u32[]{:S(2)}, u32[]{:S(2)}) collective-permute-start(bf16[2048,256]{1,0:T(8,128)(2,1)} %collective-permute-done.6.refs_6_.refs_3_), channel_id=1, source_target_pairs={{2,3},{10,11},{13,12},{21,20},{26,27}} | collective-permute-start | bytes 3145736 | tf_op jit(solution)/shard_map/ppermute | solution.py:531
  78.0 1.2 %copy-start.7 = (bf16[256,2048]{1,0:T(8,128)(2,1)S(1)}, bf16[256,2048]{1,0:T(8,128)(2,1)}, u32[]{:S(2)}) copy-start(bf16[256,2048]{1,0:T(8,128)(2,1)} %refs_0_) | copy-start | bytes 3145732
  79.2 1.2 %copy-start.9 = (bf16[256,2048]{1,0:T(8,128)(2,1)S(1)}, bf16[256,2048]{1,0:T(8,128)(2,1)}, u32[]{:S(2)}) copy-start(bf16[256,2048]{1,0:T(8,128)(2,1)} %copy-done.8) | copy-start | bytes 3145732
  80.4 9.9 %copy-start.2 = (bf16[2048,256]{1,0:T(8,128)(2,1)S(1)}, bf16[2048,256]{1,0:T(8,128)(2,1)}, u32[]{:S(2)}) copy-start(bf16[2048,256]{1,0:T(8,128)(2,1)} %copy-done.1) | copy-start | bytes 3145732
  80.4 9.9 %copy-start.4 = (bf16[2048,256]{1,0:T(8,128)(2,1)S(1)}, bf16[2048,256]{1,0:T(8,128)(2,1)}, u32[]{:S(2)}) copy-start(bf16[2048,256]{1,0:T(8,128)(2,1)} %copy-done.3) | copy-start | bytes 3145732
  80.4 9.9 %copy-start.6 = (bf16[2048,256]{1,0:T(8,128)(2,1)S(1)}, bf16[2048,256]{1,0:T(8,128)(2,1)}, u32[]{:S(2)}) copy-start(bf16[2048,256]{1,0:T(8,128)(2,1)} %copy-done.5) | copy-start | bytes 3145732
  83.7 17.2 %collective-permute-start.15 = (f32[2048]{0:T(1024)S(1)}, f32[2048]{0:T(1024)S(1)}, u32[]{:S(2)}, u32[]{:S(2)}) collective-permute-start(f32[2048]{0:T(1024)S(1)} %add.39), channel_id=1, source_target_pairs={{0,2},{1,3},{2,0},{3,1},{4,6},{5,7},{6,4},{7,5},{8,10},{9,11},{10,... | collective-permute-start | bytes 24584 | tf_op jit(solution)/shard_map/ppermute | solution.py:492
